TPU v7x, 32 devices: a whole 2x2x4 slice. The times are simulated.
32 devices in a mesh: slab: 4 (over z), front: 8 (over y, x, core).
Axes of the slice: x: 2, y: 2, z: 4, core: 2. Of those that a mesh axis runs over, the one named last changes fastest.
Arguments:
- leaf_rhs: bfloat16 [4, 2, 128, 128, 512], P('slab', None, 'front'), may hold values from -6 to 6
- leaf_inv: bfloat16 [4, 128, 2, 128, 128], P('slab', 'front'), may hold values from -0.375 to 0.375
- leaf_off: bfloat16 [4, 128, 2, 128, 128], P('slab', 'front'), may hold values from -0.125 to 0.125
- parent: int32 [4, 128, 1], P('slab', 'front'), may hold values from 0 to 7; in each aligned block of 16 rows (0 to 15, 16 to 31, ..., all dimensions but the last counted through in order) at most 2 rows name the same one
- ancestors: int32 [4, 128, 128], P('slab', 'front'), may hold values from 0 to 255
- root_rhs: bfloat16 [4, 2, 2048, 512], P('slab', None, 'front'), may hold values from -6 to 6
- root_inv: float32 [4, 16, 2, 128, 128], P('slab', 'front'), may hold values from -2 to 2.5
- coupling: float32 [4, 2048], P('slab', 'front'), may hold values from 0.6 to 1.3
Outputs:
- leaf_sol: bfloat16 [4, 2, 128, 128, 512], P('slab', None, 'front')
- root_sol: float32 [4, 2, 2048, 512], P('slab', None, 'front')
Inputs may be any that keep to these rules, and one draw needn't show every extreme that they name: Each front index's 16 leaf blocks of a slab name any one parent at most 2 times. `ancestors`: rows may repeat within a block.
All inputs are finite; a program needn't handle non-finite values.
Results may differ from a plain program's by a relative error of at most 0.0057.
Values may be sent and summed in bfloat16 or wider, within the bound.
No kernel may reach another device: no remote copies, remote signals or barrier semaphores. Data moves between devices by JAX's collectives and lax.ppermute only.
A program may use at most 128 MiB of HBM per device.

v0:
```python
import jax
import jax.numpy as jnp
from jax import lax
from jax.sharding import PartitionSpec as P


def passed_along(x, axis, by):
    count = lax.axis_size(axis)
    pairs = [(i, i + by) for i in range(count) if 0 <= i + by < count]
    return lax.ppermute(x, axis, pairs)


def planes_apply(real_mat, imag_mat, real_vec, imag_vec, form):
    real = jnp.einsum(form, real_mat, real_vec, preferred_element_type=jnp.float32) - jnp.einsum(
        form, imag_mat, imag_vec, preferred_element_type=jnp.float32
    )
    imag = jnp.einsum(form, real_mat, imag_vec, preferred_element_type=jnp.float32) + jnp.einsum(
        form, imag_mat, real_vec, preferred_element_type=jnp.float32
    )
    return jnp.stack([real, imag])


def block_solve(blocks, field):
    highest = lax.Precision.HIGHEST
    shaped = field.reshape(2, blocks.shape[0], blocks.shape[2], field.shape[-1])
    real = jnp.einsum("kij,kjc->kic", blocks[:, 0], shaped[0], precision=highest) - jnp.einsum(
        "kij,kjc->kic", blocks[:, 1], shaped[1], precision=highest
    )
    imag = jnp.einsum("kij,kjc->kic", blocks[:, 0], shaped[1], precision=highest) + jnp.einsum(
        "kij,kjc->kic", blocks[:, 1], shaped[0], precision=highest
    )
    return jnp.stack([real, imag]).reshape(field.shape)


def body(leaf_rhs, leaf_inv, leaf_off, parent, ancestors, root_rhs, root_inv, coupling):
    forward_form = "lij,ljc->lic"
    back_form = "lji,ljc->lic"
    rhs = leaf_rhs[0]
    inverse = leaf_inv[0]
    offdiag = leaf_off[0]
    owners = parent[0, :, 0]
    anc_rows = ancestors[0]
    fronts = lax.axis_size("front")
    count = owners.shape[0]
    per_owner = (count + fronts - 1) // fronts
    blk = rhs.shape[2]
    width = rhs.shape[3]
    root_rows = root_rhs.shape[2]
    slot_total = fronts * per_owner
    hits = (owners[:, None] == jnp.arange(fronts, dtype=jnp.int32)[None, :]).astype(jnp.int32)
    rank = jnp.sum((jnp.cumsum(hits, axis=0) - hits) * hits, axis=1)
    slot = owners * per_owner + rank
    place_int = (slot[:, None] == jnp.arange(slot_total, dtype=jnp.int32)[None, :]).astype(
        jnp.int32
    )
    place = place_int.astype(jnp.bfloat16)
    slot_ids = jnp.sum(place_int[:, :, None] * anc_rows[:, None, :], axis=0).reshape(
        1, fronts, per_owner, blk
    )
    forward = planes_apply(inverse[:, 0], inverse[:, 1], rhs[0], rhs[1], forward_form).astype(
        jnp.bfloat16
    )
    partial_value = planes_apply(
        offdiag[:, 0], offdiag[:, 1], forward[0], forward[1], forward_form
    ).astype(jnp.bfloat16)
    placed = jnp.einsum(
        "ks,pkbc->psbc", place, partial_value, preferred_element_type=jnp.float32
    ).astype(jnp.bfloat16)
    placed = placed.reshape(2, fronts, per_owner, blk, width)
    arrived, arrived_ids = (
        lax.all_to_all(placed, "front", split_axis=1, concat_axis=1, tiled=True),
        lax.all_to_all(slot_ids, "front", split_axis=1, concat_axis=1, tiled=True),
    )
    slot_parts = arrived.reshape(2, slot_total * blk, width)
    flat_ids = arrived_ids.reshape(-1)
    row_table = (flat_ids[:, None] == jnp.arange(root_rows, dtype=jnp.int32)[None, :]).astype(
        jnp.bfloat16
    )
    summed = jnp.einsum("sr,psc->prc", row_table, slot_parts, preferred_element_type=jnp.float32)
    reduced = root_rhs[0].astype(jnp.float32) - summed
    blocks = root_inv[0]
    cpl = coupling[0]
    first = block_solve(blocks, reduced)

    def relay(step, state):
        previous = passed_along(state, "slab", 1)
        return block_solve(blocks, reduced - cpl[None, :, None] * previous)

    state = lax.fori_loop(0, lax.axis_size("slab") - 1, relay, first)
    root_half = state.astype(jnp.bfloat16)
    slot_rows = jnp.einsum(
        "sr,prc->psc", row_table, root_half, preferred_element_type=jnp.float32
    ).astype(jnp.bfloat16)
    slot_rows = slot_rows.reshape(2, fronts, per_owner, blk, width)
    returned = lax.all_to_all(slot_rows, "front", split_axis=1, concat_axis=1, tiled=True)
    picked = jnp.einsum(
        "ks,psbc->pkbc",
        place,
        returned.reshape(2, slot_total, blk, width),
        preferred_element_type=jnp.float32,
    ).astype(jnp.bfloat16)
    back = planes_apply(offdiag[:, 0], offdiag[:, 1], picked[0], picked[1], back_form).astype(
        jnp.bfloat16
    )
    solved = forward.astype(jnp.float32) - planes_apply(
        inverse[:, 0], inverse[:, 1], back[0], back[1], forward_form
    )
    return (solved.astype(jnp.bfloat16)[None], state[None])


def solution(mesh):
    in_specs = (
        P("slab", None, "front", None, None),
        P("slab", "front", None, None, None),
        P("slab", "front", None, None, None),
        P("slab", "front", None),
        P("slab", "front", None),
        P("slab", None, "front", None),
        P("slab", "front", None, None, None),
        P("slab", "front"),
    )
    out_specs = (P("slab", None, "front", None, None), P("slab", None, "front", None))
    return jax.shard_map(body, mesh=mesh, in_specs=in_specs, out_specs=out_specs, check_vma=False)
```

profile of v0, /device:TPU:0, one launch (start us, length us, event | category | flops | bytes accessed | tf_op | source)
XLA Modules:
  0.0 338.2 jit_solution(13666879650317722661)
XLA Ops:
  0.6 1.4 copy.96
  2.1 4.8 %fusion.11 = f32[16,128,512]{2,1,0:T(8,128)} fusion(bf16[1,2,16,128,512]{4,3,2,1,0:T(8,128)(2,1)} %param.10, bf16[16,2,128,128]{3,2,0,1:T(8,128)(2,1)S(1)} %bitcast.217), kind=kOutput, calls=%fused_computation.30 | convolution fusion | flops 268435456 | bytes 6815744 | tf_op jit(solution)/shard_map/lij,ljc->lic/dot_general | solution.py:17
  6.9 2.7 fusion.15
  10.0 3.9 %add_convert_fusion.2 = bf16[16,128,512]{2,1,0:T(8,128)(2,1)S(1)} fusion(f32[16,128,512]{2,1,0:T(8,128)} %fusion.11, bf16[1,2,16,128,512]{4,3,2,1,0:T(8,128)(2,1)} %param.10, bf16[16,2,128,128]{3,2,0,1:T(8,128)(2,1)S(1)} %bitcast.219), kind=kOutput, calls=%fused_computation.26 | convolution fusion | flops 270532608 | bytes 8912896 | tf_op jit(solution)/shard_map/lij,ljc->lic/dot_general | solution.py:17
  14.4 1.3 copy-done.10
  15.6 0.7 subtract_convert_fusion.2
  16.3 0.8 fusion.40
  17.1 0.8 fusion.41
  17.9 0.9 fusion.26
  18.9 0.9 fusion.25
  19.8 2.4 pad_maximum_fusion.1
  22.2 7.9 %copy.60 = bf16[2,16,128,512]{3,1,2,0:T(8,128)(2,1)} copy(bf16[2,16,128,512]{2,3,1,0:T(8,128)(2,1)} %pad_maximum_fusion.1) | data formatting | bytes 8388608 | tf_op jit(solution)/shard_map/stack | solution.py:20
  30.1 5.6 %convert_bitcast_fusion.2 = bf16[2,16,128,512]{3,1,2,0:T(8,128)(2,1)} fusion(bf16[2,16,128,512]{3,1,2,0:T(8,128)(2,1)} %copy.60, s32[16]{0:T(128)S(1)} %multiply_add_fusion), kind=kOutput, calls=%fused_computation.23 | convolution fusion | flops 69206784 | bytes 8388672 | tf_op jit(solution)/shard_map/ks,pkbc->psbc/dot_general | solution.py:66
  35.7 7.2 %reshape.152 = bf16[2,8,2,128,512]{4,2,1,3,0:T(2,128)(2,1)} reshape(bf16[2,16,128,512]{3,1,2,0:T(8,128)(2,1)} %convert_bitcast_fusion.2) | data formatting | bytes 8388608 | tf_op jit(solution)/shard_map/reshape | solution.py:69
  42.9 8.1 %copy.62 = bf16[2,8,2,128,512]{4,2,3,0,1:T(2,128)(2,1)} copy(bf16[2,8,2,128,512]{4,2,1,3,0:T(2,128)(2,1)} %reshape.152) | data formatting | bytes 8388608 | tf_op jit(solution)/shard_map/reshape | solution.py:69
  50.9 5.3 %all-to-all-start = ((bf16[2,8,2,128,512]{4,2,3,0,1:T(2,128)(2,1)}), bf16[2,8,2,128,512]{4,2,3,0,1:T(2,128)(2,1)}, u32[]{:S(2)}, u32[]{:S(2)}) async-start(bf16[2,8,2,128,512]{4,2,3,0,1:T(2,128)(2,1)} %copy.62), calls=%async_computation | async-start | bytes 8388608 | tf_op jit(solution)/shard_map/all_to_all | solution.py:71
  57.0 48.4 %all-to-all-done = bf16[2,8,2,128,512]{4,2,3,0,1:T(2,128)(2,1)} async-done(((bf16[2,8,2,128,512]{4,2,3,0,1:T(2,128)(2,1)}), bf16[2,8,2,128,512]{4,2,3,0,1:T(2,128)(2,1)}, u32[]{:S(2)}, u32[]{:S(2)}) %all-to-all-start) | async-done | bytes 4194336 | tf_op jit(solution)/shard_map/all_to_all | solution.py:71
  105.5 3.5 %all-to-all-start.1 = ((s32[1,8,2,128]{3,2,0,1:T(2,128)}), s32[1,8,2,128]{3,2,0,1:T(2,128)S(1)}, u32[]{:S(2)}, u32[]{:S(2)}) async-start(s32[1,8,2,128]{3,2,0,1:T(2,128)} %bitcast.30), calls=%async_computation.1 | async-start | bytes 16384 | tf_op jit(solution)/shard_map/all_to_all | solution.py:72
  109.0 5.1 %copy.63 = bf16[2,8,2,128,512]{4,3,2,1,0:T(8,128)(2,1)} copy(bf16[2,8,2,128,512]{4,2,3,0,1:T(2,128)(2,1)} %all-to-all-done) | data formatting | bytes 8388608 | tf_op jit(solution)/shard_map/all_to_all | solution.py:71
  114.2 4.0 %fusion.30 = f32[2,256,512]{2,1,0:T(8,128)S(1)} fusion(bf16[2,2048,512]{2,1,0:T(8,128)(2,1)} %bitcast.230, s32[2048]{0:T(1024)S(1)} %bitcast.233, bf16[1,2,256,512]{3,2,1,0:T(8,128)(2,1)} %param.15), kind=kOutput, calls=%fused_computation.46 | convolution fusion | flops 1074790400 | bytes 5775360 | tf_op jit(solution)/shard_map/sr,psc->prc/dot_general | solution.py:79
  120.7 1.0 pad_maximum_fusion.2
  121.8 95.1 %while.10 = (s32[]{:T(128)}, f32[2,256,512]{2,1,0:T(8,128)}, f32[1,256]{1,0:T(1,128)S(1)}, f32[2,256,512]{2,1,0:T(8,128)S(1)}, f32[2,2,128,128]{3,2,0,1:T(8,128)S(1)}, /*index=5*/s32[]{:T(128)}) while((s32[]{:T(128)}, f32[2,256,512]{2,1,0:T(8,128)}, f32[1,256]{1,0:T(1,128)S(1)}, f32[2,256,512]{2,1,0:T(8,128)S(1)}, ...), condition=%wide.region_4.5_spmd, body=%wide.region_3.4_spmd.sunk | while | flops 806354944 | bytes 17302636 | solution.py:89
  121.8 5.2 %collective-permute-start = (f32[2,256,512]{2,1,0:T(8,128)}, f32[2,256,512]{2,1,0:T(8,128)}, u32[]{:S(2)}, u32[]{:S(2)}) collective-permute-start(f32[2,256,512]{2,1,0:T(8,128)} %get-tuple-element.88), channel_id=1, source_target_pairs={{0,8},{8,16},{16,24},{1,9},{9,17},{17,25},{2,10},{10,18},{18,26},{... | collective-permute-start | bytes 3145736 | tf_op jit(solution)/shard_map/while/body/eval_jaxpr/ppermute | solution.py:10
  127.0 22.3 %collective-permute-done = f32[2,256,512]{2,1,0:T(8,128)} collective-permute-done((f32[2,256,512]{2,1,0:T(8,128)}, f32[2,256,512]{2,1,0:T(8,128)}, u32[]{:S(2)}, u32[]{:S(2)}) %collective-permute-start) | collective-permute-done | bytes 1048608 | tf_op jit(solution)/shard_map/while/body/eval_jaxpr/ppermute | solution.py:10
  149.2 1.4 multiply_subtract_fusion.2
  153.2 1.0 pad_maximum_fusion.4
  154.2 5.4 %collective-permute-start = (f32[2,256,512]{2,1,0:T(8,128)}, f32[2,256,512]{2,1,0:T(8,128)}, u32[]{:S(2)}, u32[]{:S(2)}) collective-permute-start(f32[2,256,512]{2,1,0:T(8,128)} %get-tuple-element.88), channel_id=1, source_target_pairs={{0,8},{8,16},{16,24},{1,9},{9,17},{17,25},{2,10},{10,18},{18,26},{... | collective-permute-start | bytes 3145736 | tf_op jit(solution)/shard_map/while/body/eval_jaxpr/ppermute | solution.py:10
  159.6 21.5 %collective-permute-done = f32[2,256,512]{2,1,0:T(8,128)} collective-permute-done((f32[2,256,512]{2,1,0:T(8,128)}, f32[2,256,512]{2,1,0:T(8,128)}, u32[]{:S(2)}, u32[]{:S(2)}) %collective-permute-start) | collective-permute-done | bytes 1048608 | tf_op jit(solution)/shard_map/while/body/eval_jaxpr/ppermute | solution.py:10
  181.0 1.4 multiply_subtract_fusion.2
  185.0 1.0 pad_maximum_fusion.4
  186.0 5.4 %collective-permute-start = (f32[2,256,512]{2,1,0:T(8,128)}, f32[2,256,512]{2,1,0:T(8,128)}, u32[]{:S(2)}, u32[]{:S(2)}) collective-permute-start(f32[2,256,512]{2,1,0:T(8,128)} %get-tuple-element.88), channel_id=1, source_target_pairs={{0,8},{8,16},{16,24},{1,9},{9,17},{17,25},{2,10},{10,18},{18,26},{... | collective-permute-start | bytes 3145736 | tf_op jit(solution)/shard_map/while/body/eval_jaxpr/ppermute | solution.py:10
  191.4 20.6 %collective-permute-done = f32[2,256,512]{2,1,0:T(8,128)} collective-permute-done((f32[2,256,512]{2,1,0:T(8,128)}, f32[2,256,512]{2,1,0:T(8,128)}, u32[]{:S(2)}, u32[]{:S(2)}) %collective-permute-start) | collective-permute-done | bytes 1048608 | tf_op jit(solution)/shard_map/while/body/eval_jaxpr/ppermute | solution.py:10
  211.9 1.4 multiply_subtract_fusion.2
  215.8 1.0 pad_maximum_fusion.4
  216.9 4.4 %convert_bitcast_fusion.1 = bf16[2,2048,512]{1,2,0:T(8,128)(2,1)} fusion(s32[2048]{0:T(1024)S(1)} %bitcast.234, f32[2,256,512]{2,1,0:T(8,128)} %get-tuple-element.29), kind=kOutput, calls=%fused_computation.22 | convolution fusion | flops 1076625408 | bytes 5251072 | tf_op jit(solution)/shard_map/sr,prc->psc/dot_general | solution.py:91
  221.3 7.7 %reshape.155 = bf16[2,8,2,128,512]{3,2,1,4,0:T(2,128)(2,1)} reshape(bf16[2,2048,512]{1,2,0:T(8,128)(2,1)} %convert_bitcast_fusion.1) | data formatting | bytes 8388608 | tf_op jit(solution)/shard_map/reshape | solution.py:94
  229.0 6.0 %copy.68 = bf16[2,8,2,128,512]{3,2,4,0,1:T(2,128)(2,1)S(1)} copy(bf16[2,8,2,128,512]{3,2,1,4,0:T(2,128)(2,1)} %reshape.155) | data formatting | bytes 8388608 | tf_op jit(solution)/shard_map/reshape | solution.py:94
  235.0 52.5 %all_to_all.15 = bf16[2,8,2,128,512]{3,2,4,0,1:T(2,128)(2,1)} all-to-all(bf16[2,8,2,128,512]{3,2,4,0,1:T(2,128)(2,1)S(1)} %copy.68), channel_id=1, replica_groups=mesh['slab'=4,'front'=8] {'front'}, dimensions={1} | all-to-all | bytes 8388608 | tf_op jit(solution)/shard_map/all_to_all | solution.py:95
  287.6 15.7 %copy.69 = bf16[2,8,2,128,512]{4,2,1,3,0:T(2,128)(2,1)} copy(bf16[2,8,2,128,512]{3,2,4,0,1:T(2,128)(2,1)} %all_to_all.15) | data formatting | bytes 8388608 | tf_op jit(solution)/shard_map/all_to_all | solution.py:95
  303.3 7.2 %reshape.156 = bf16[2,16,128,512]{3,1,2,0:T(8,128)(2,1)} reshape(bf16[2,8,2,128,512]{4,2,1,3,0:T(2,128)(2,1)} %copy.69) | data formatting | bytes 8388608 | tf_op jit(solution)/shard_map/reshape | solution.py:99
  310.5 3.5 %convert_bitcast_fusion = bf16[2,16,128,512]{3,1,2,0:T(8,128)(2,1)S(1)} fusion(bf16[2,16,128,512]{3,1,2,0:T(8,128)(2,1)} %reshape.156, s32[16]{0:T(128)S(1)} %multiply_add_fusion), kind=kOutput, calls=%fused_computation.21 | convolution fusion | flops 69206784 | bytes 8388672 | tf_op jit(solution)/shard_map/ks,psbc->pkbc/dot_general | solution.py:96
  314.0 2.5 slice_bitcast_fusion.1
  316.5 4.7 %copy.70 = bf16[16,128,512]{1,2,0:T(8,128)(2,1)} copy(bf16[16,128,512]{2,0,1:T(8,128)(2,1)} %get-tuple-element.42) | data formatting | bytes 4194304 | tf_op jit(solution)/shard_map/squeeze | solution.py:102
  321.1 4.5 %copy.71 = bf16[16,128,512]{1,2,0:T(8,128)(2,1)} copy(bf16[16,128,512]{2,0,1:T(8,128)(2,1)} %get-tuple-element.43) | data formatting | bytes 4194304 | tf_op jit(solution)/shard_map/squeeze | solution.py:102
  325.6 2.4 fusion.38
  329.5 0.9 copy-done.6
  334.5 0.9 copy-done.1
  335.3 2.8 fusion.10
  (65 shorter events, 17.1 us)
Async XLA Ops:
  0.6 6.3 %copy-start.8 = (bf16[1,2,16,128,512]{4,3,2,1,0:T(8,128)(2,1)S(1)}, bf16[1,2,16,128,512]{4,3,2,1,0:T(8,128)(2,1)}, u32[]{:S(2)}) copy-start(bf16[1,2,16,128,512]{4,3,2,1,0:T(8,128)(2,1)} %param.10) | copy-start | bytes 12582916
  2.1 11.8 %copy-start.4 = (bf16[1,16,2,128,128]{4,3,1,2,0:T(8,128)(2,1)}, bf16[1,16,2,128,128]{4,3,1,2,0:T(8,128)(2,1)S(1)}, u32[]{:S(2)}) copy-start(bf16[1,16,2,128,128]{4,3,1,2,0:T(8,128)(2,1)S(1)} %copy.96) | copy-start | bytes 3145732
  6.9 2.7 copy-start.15
  6.9 3.0 copy-start.11
  9.9 8.9 %copy-start.2 = (bf16[1,16,2,128,128]{4,3,1,2,0:T(8,128)(2,1)}, bf16[1,16,2,128,128]{4,3,1,2,0:T(8,128)(2,1)S(1)}, u32[]{:S(2)}) copy-start(bf16[1,16,2,128,128]{4,3,1,2,0:T(8,128)(2,1)S(1)} %copy.95) | copy-start | bytes 3145732
  9.9 4.4 %copy-start.9 = (bf16[1,2,16,128,512]{4,3,2,1,0:T(8,128)(2,1)S(1)}, bf16[1,2,16,128,512]{4,3,2,1,0:T(8,128)(2,1)}, u32[]{:S(2)}) copy-start(bf16[1,2,16,128,512]{4,3,2,1,0:T(8,128)(2,1)} %param.10) | copy-start | bytes 12582916
  10.0 5.7 %copy-start.10 = (f32[16,128,512]{2,1,0:T(8,128)S(1)}, f32[16,128,512]{2,1,0:T(8,128)}, u32[]{:S(2)}) copy-start(f32[16,128,512]{2,1,0:T(8,128)} %fusion.15) | copy-start | bytes 12582916
  16.3 1.6 copy-start
  50.9 5.4 %copy-start.14 = (s32[1,16,128]{2,1,0:T(8,128)S(1)}, s32[1,16,128]{2,1,0:T(8,128)}, u32[]{:S(2)}) copy-start(s32[1,16,128]{2,1,0:T(8,128)} %param.14) | copy-start | bytes 24580
  50.9 58.1 %copy-start.12 = (f32[1,2,2,128,128]{4,3,2,1,0:T(8,128)S(1)}, f32[1,2,2,128,128]{4,3,2,1,0:T(8,128)}, u32[]{:S(2)}) copy-start(f32[1,2,2,128,128]{4,3,2,1,0:T(8,128)} %param.16) | copy-start | bytes 786436
  50.9 54.5 %all-to-all-start = ((bf16[2,8,2,128,512]{4,2,3,0,1:T(2,128)(2,1)}), bf16[2,8,2,128,512]{4,2,3,0,1:T(2,128)(2,1)}, u32[]{:S(2)}, u32[]{:S(2)}) async-start(bf16[2,8,2,128,512]{4,2,3,0,1:T(2,128)(2,1)} %copy.62), calls=%async_computation | async-start | bytes 8388608 | tf_op jit(solution)/shard_map/all_to_all | solution.py:71
  105.5 8.7 %all-to-all-start.1 = ((s32[1,8,2,128]{3,2,0,1:T(2,128)}), s32[1,8,2,128]{3,2,0,1:T(2,128)S(1)}, u32[]{:S(2)}, u32[]{:S(2)}) async-start(s32[1,8,2,128]{3,2,0,1:T(2,128)} %bitcast.30), calls=%async_computation.1 | async-start | bytes 16384 | tf_op jit(solution)/shard_map/all_to_all | solution.py:72
  118.3 3.5 %copy-start.13 = (f32[1,256]{1,0:T(1,128)S(1)}, f32[1,256]{1,0:T(1,128)}, u32[]{:S(2)}) copy-start(f32[1,256]{1,0:T(1,128)} %param.17) | copy-start | bytes 3076
  121.8 27.5 %collective-permute-start = (f32[2,256,512]{2,1,0:T(8,128)}, f32[2,256,512]{2,1,0:T(8,128)}, u32[]{:S(2)}, u32[]{:S(2)}) collective-permute-start(f32[2,256,512]{2,1,0:T(8,128)} %get-tuple-element.88), channel_id=1, source_target_pairs={{0,8},{8,16},{16,24},{1,9},{9,17},{17,25},{2,10},{10,18},{18,26},{... | collective-permute-start | bytes 3145736 | tf_op jit(solution)/shard_map/while/body/eval_jaxpr/ppermute | solution.py:10
  154.2 26.8 %collective-permute-start = (f32[2,256,512]{2,1,0:T(8,128)}, f32[2,256,512]{2,1,0:T(8,128)}, u32[]{:S(2)}, u32[]{:S(2)}) collective-permute-start(f32[2,256,512]{2,1,0:T(8,128)} %get-tuple-element.88), channel_id=1, source_target_pairs={{0,8},{8,16},{16,24},{1,9},{9,17},{17,25},{2,10},{10,18},{18,26},{... | collective-permute-start | bytes 3145736 | tf_op jit(solution)/shard_map/while/body/eval_jaxpr/ppermute | solution.py:10
  186.0 25.9 %collective-permute-start = (f32[2,256,512]{2,1,0:T(8,128)}, f32[2,256,512]{2,1,0:T(8,128)}, u32[]{:S(2)}, u32[]{:S(2)}) collective-permute-start(f32[2,256,512]{2,1,0:T(8,128)} %get-tuple-element.88), channel_id=1, source_target_pairs={{0,8},{8,16},{16,24},{1,9},{9,17},{17,25},{2,10},{10,18},{18,26},{... | collective-permute-start | bytes 3145736 | tf_op jit(solution)/shard_map/while/body/eval_jaxpr/ppermute | solution.py:10
  316.5 9.2 %copy-start.3 = (bf16[1,16,2,128,128]{4,3,1,2,0:T(8,128)(2,1)S(1)}, bf16[1,16,2,128,128]{4,3,1,2,0:T(8,128)(2,1)}, u32[]{:S(2)}) copy-start(bf16[1,16,2,128,128]{4,3,1,2,0:T(8,128)(2,1)} %copy-done.2) | copy-start | bytes 3145732
  325.6 2.4 copy-start.7
  328.8 1.6 copy-start.6
  330.4 1.2 copy-start.5
  333.7 1.6 copy-start.1
where the time goes:
time: 340 us; the launch traced here: 338 us
  waiting for transfers between devices  113 us (33%)
  local copies, waits for them, and re-layouts  82.5 us (24%)
  blocking collectives  52.5 us (15%)
  matrix products  49.9 us (15%)
  starting transfers between devices  24.7 us (7%)
  other arithmetic  14.6 us (4%)
    ppermute x3, waiting for transfers between devices, passed_along(): return lax.ppermute(x, axis, pairs)  64.3 us
    all_to_all x1, blocking collectives, body(): lax.all_to_all(slot_rows, 'front', split_axis=1, concat_axis=1, tiled=True)  52.5 us
    all_to_all x1, waiting for transfers between devices, body(): lax.all_to_all(placed, 'front', split_axis=1, concat_axis=1, tiled=True)  48.4 us
    ppermute x3, starting transfers between devices, passed_along(): return lax.ppermute(x, axis, pairs)  15.9 us
    all_to_all x1, local copies, waits for them, and re-layouts, body(): lax.all_to_all(slot_rows, 'front', split_axis=1, concat_axis=1, tiled=True)  15.7 us
    reshape x2, local copies, waits for them, and re-layouts, body(): placed = placed.reshape(2, fronts, per_owner, blk, width)  15.3 us
    reshape x2, local copies, waits for them, and re-layouts, body(): slot_rows = slot_rows.reshape(2, fronts, per_owner, blk, width)  13.7 us
    dot_general x4, matrix products, planes_apply(): jnp.einsum(form, real_mat, imag_vec, preferred_element_type=jnp.float32)  8.7 us
  transfers between devices with their start and end apart: 5, of which 4 were waited for; matrix products, arithmetic and copies ran while one was open for 2% of the time, Pallas kernels for 0%

commit v1 on v0

v1 whole, which is shorter than its diff:
```python
import functools

import jax
import jax.numpy as jnp
from jax import lax
from jax.experimental import pallas as pl
from jax.experimental.pallas import tpu as pltpu
from jax.sharding import PartitionSpec as P

HALVES = 2
BF = jnp.bfloat16
F32 = jnp.float32
VMEM = pl.BlockSpec(memory_space=pltpu.VMEM)


def params():
    return pltpu.CompilerParams(vmem_limit_bytes=40 * 1024 * 1024)


def crossed(x, axis, mask):
    return lax.ppermute(x, axis, [(i, i ^ mask) for i in range(lax.axis_size(axis))])


def spread(vec):
    half = vec.shape[1] // 2
    return jnp.concatenate([vec, jnp.concatenate([-vec[:, half:], vec[:, :half]], axis=1)], axis=0)


def dot(a, b, dims=((1,), (0,)), precision=None):
    return lax.dot_general(a, b, (dims, ((), ())), precision=precision, preferred_element_type=F32)


def table_of(anc_row, rows):
    ids = lax.broadcasted_iota(jnp.int32, (rows, anc_row.shape[1]), 0)
    return (ids == anc_row).astype(F32).astype(BF)


def forward_kernel(group, cap, fronts, rows, owners, place, rhs, inv, off, anc, fwd, keep, send, part, ids, seen):
    step = pl.program_id(0)
    me = place[1]
    blk = rhs.shape[3]

    @pl.when(step == 0)
    def _():
        ids[...] = jnp.full(ids.shape, -1, jnp.int32)

        def clear(i, carry):
            seen[i] = 0
            return carry

        lax.fori_loop(0, fronts, clear, 0)

    for j in range(group):
        leaf = step * group + j
        dist = owners[leaf] ^ me
        rank = seen[dist]
        seen[dist] = rank + 1
        mat = jnp.concatenate([inv[0, j, 0], inv[0, j, 1]], axis=1)
        vec = jnp.concatenate([rhs[0, 0, j], rhs[0, 1, j]], axis=1)
        value = dot(mat, spread(vec)).astype(BF)
        fwd[j] = value
        mat = jnp.concatenate([off[0, j, 0], off[0, j, 1]], axis=1)
        part[dist, rank] = dot(mat, spread(value)).astype(BF)
        ids[pl.ds(dist * cap + rank, 1), :] = anc[0, pl.ds(leaf, 1), :]

    @pl.when(step == pl.num_programs(0) - 1)
    def _():
        for dist in range(fronts):
            for rank in range(cap):

                @pl.when(seen[dist] <= rank)
                def _():
                    part[dist, rank] = jnp.zeros(part.shape[2:], BF)

            row = jnp.concatenate([ids[dist * cap + rank : dist * cap + rank + 1, :] for rank in range(cap)], axis=1)
            total = dot(table_of(row, rows), part[dist].reshape(cap * blk, part.shape[3]))
            if dist % 2:
                send[dist // 2] = total.astype(BF)
            else:
                keep[dist // 2] = total.astype(BF)


def forward(h, owners, place, leaf_rhs, leaf_inv, leaf_off, ancestors, fronts, rows):
    _, _, leaves, blk, width = leaf_rhs.shape
    cols = width // HALVES
    cap = -(-leaves // fronts)
    group = 4
    spec = pltpu.PrefetchScalarGridSpec(
        num_scalar_prefetch=2,
        grid=(leaves // group,),
        in_specs=[
            pl.BlockSpec((1, 2, group, blk, cols), lambda i, o, p: (0, 0, i, 0, h)),
            pl.BlockSpec((1, group, 2, blk, blk), lambda i, o, p: (0, i, 0, 0, 0)),
            pl.BlockSpec((1, group, 2, blk, blk), lambda i, o, p: (0, i, 0, 0, 0)),
            pl.BlockSpec((1, leaves, blk), lambda i, o, p: (0, 0, 0)),
        ],
        out_specs=[pl.BlockSpec((group, blk, 2 * cols), lambda i, o, p: (i, 0, 0)), VMEM, VMEM],
        scratch_shapes=[
            pltpu.VMEM((fronts, cap, blk, 2 * cols), BF),
            pltpu.VMEM((fronts * cap, blk), jnp.int32),
            pltpu.SMEM((fronts,), jnp.int32),
        ],
    )
    block = jax.ShapeDtypeStruct((fronts // 2, rows, 2 * cols), BF)
    return pl.pallas_call(
        functools.partial(forward_kernel, group, cap, fronts, rows),
        grid_spec=spec,
        out_shape=[jax.ShapeDtypeStruct((leaves, blk, 2 * cols), BF), block, block],
        compiler_params=params(),
        cost_estimate=pl.CostEstimate(flops=6 * leaves * blk * 2 * blk * 2 * cols, bytes_accessed=6 << 20, transcendentals=0),
        name="leaf_forward",
    )(owners, place, leaf_rhs, leaf_inv, leaf_off, ancestors)


def fold_kernel(group, rows, inv, off, anc, out):
    step = pl.program_id(0)
    for j in range(group):
        leaf = step * group + j
        mat = jnp.concatenate([inv[0, j, 0], inv[0, j, 1]], axis=1)
        real, imag = off[0, j, 0], off[0, j, 1]
        other = jnp.concatenate([jnp.concatenate([real, -imag], axis=1), jnp.concatenate([imag, real], axis=1)], axis=0)
        both = dot(mat, other, ((1,), (1,))).astype(BF)
        blk = real.shape[0]
        table = table_of(anc[0, pl.ds(leaf, 1), :], rows)
        out[j, :, :rows] = dot(both[:, :blk], table, ((1,), (1,))).astype(BF)
        out[j, :, rows:] = dot(both[:, blk:], table, ((1,), (1,))).astype(BF)


def fold(leaf_inv, leaf_off, ancestors, rows):
    _, leaves, _, blk, _ = leaf_inv.shape
    group = 4
    return pl.pallas_call(
        functools.partial(fold_kernel, group, rows),
        grid=(leaves // group,),
        in_specs=[
            pl.BlockSpec((1, group, 2, blk, blk), lambda i: (0, i, 0, 0, 0)),
            pl.BlockSpec((1, group, 2, blk, blk), lambda i: (0, i, 0, 0, 0)),
            pl.BlockSpec((1, leaves, blk), lambda i: (0, 0, 0)),
        ],
        out_specs=pl.BlockSpec((group, blk, 2 * rows), lambda i: (i, 0, 0)),
        out_shape=jax.ShapeDtypeStruct((leaves, blk, 2 * rows), BF),
        compiler_params=params(),
        cost_estimate=pl.CostEstimate(flops=2 * leaves * blk * 2 * blk * 4 * blk, bytes_accessed=4 << 20, transcendentals=0),
        name="leaf_fold",
    )(leaf_inv, leaf_off, ancestors)


def pack_kernel(place, inv, cpl, same, other):
    blocks = inv.shape[1]
    blk = inv.shape[3]
    mine = place[0] % blocks
    for kind, out in enumerate((same, other)):
        block = mine ^ kind
        out[:blk, :] = inv[0, block, 0]
        out[blk : 2 * blk, :] = inv[0, block, 1]
        out[2 * blk :, :] = jnp.broadcast_to(cpl[0, pl.ds(block, 1), :], (8, blk))


def pack(place, root_inv, coupling):
    _, blocks, _, blk, _ = root_inv.shape
    shape = jax.ShapeDtypeStruct((2 * blk + 8, blk), F32)
    return pl.pallas_call(
        pack_kernel,
        in_specs=[pl.BlockSpec(memory_space=pltpu.SMEM), VMEM, VMEM],
        out_specs=[VMEM, VMEM],
        out_shape=[shape, shape],
        compiler_params=params(),
        name="solve_pack",
    )(place, root_inv, coupling.reshape(1, blocks, blk))


def piece_of(index, blk, blocks, part):
    low, left = (index % blocks) * blk, (index // blocks) * part
    return slice(low, low + blk), left


def reduce_kernel(slabs, blk, part, terms, place, rhs, keep, near, *refs):
    cols = rhs.shape[3]
    blocks = rhs.shape[2] // blk
    total = keep[0].astype(F32) + near[0].astype(F32)
    for ref in refs[:terms]:
        total = total + ref[...].astype(F32)
    real = (rhs[0, 0].astype(F32) - total[:, :cols]).astype(BF)
    imag = (rhs[0, 1].astype(F32) - total[:, cols:]).astype(BF)
    outs = refs[terms:]
    for index in range(slabs):
        rows, left = piece_of(index, blk, blocks, part)
        piece = jnp.concatenate([real[rows, left : left + part], imag[rows, left : left + part]], axis=1)
        for mask, out in enumerate(outs):

            @pl.when(place[0] ^ mask == index)
            def _(piece=piece, out=out):
                out[...] = piece


def reduce(h, place, root_rhs, keep, near, far, slabs, blk):
    _, _, rows, width = root_rhs.shape
    cols = width // HALVES
    part = cols * (rows // blk) // slabs
    spec = pltpu.PrefetchScalarGridSpec(
        num_scalar_prefetch=1,
        grid=(1,),
        in_specs=[
            pl.BlockSpec((1, 2, rows, cols), lambda i, p: (0, 0, 0, h)),
            pl.BlockSpec((1, rows, 2 * cols), lambda i, p: (0, 0, 0)),
            pl.BlockSpec((1, rows, 2 * cols), lambda i, p: (0, 0, 0)),
        ]
        + [VMEM] * len(far),
        out_specs=[VMEM] * slabs,
    )
    return pl.pallas_call(
        functools.partial(reduce_kernel, slabs, blk, part, len(far)),
        grid_spec=spec,
        out_shape=[jax.ShapeDtypeStruct((blk, 2 * part), BF)] * slabs,
        compiler_params=params(),
        name="interface_reduce",
    )(place, root_rhs, keep, near, *far)


def chain_kernel(slabs, place, *refs):
    pieces, mats = refs[:slabs], refs[slabs : 2 * slabs]
    outs = refs[2 * slabs : 3 * slabs]
    held, solver = refs[3 * slabs :]
    me = place[0]
    for mask in range(slabs):
        held[mask] = pieces[mask][...]
        solver[mask] = mats[mask][...]
    blk = held.shape[1]
    part = held.shape[2] // 2
    state = None
    for slab in range(slabs):
        at = me ^ slab
        field = held[at].astype(F32)
        packed = solver[at]
        if state is not None:
            scale = jnp.broadcast_to(packed[2 * blk : 2 * blk + 1, :], (blk, blk)).T
            field = field - scale[:, :1] * state
        mat = jnp.concatenate([packed[:blk], packed[blk : 2 * blk]], axis=1)
        state = dot(mat, spread(field), precision=lax.Precision.HIGHEST)
        half = state.astype(BF)
        for mask, out in enumerate(outs):

            @pl.when(at == mask)
            def _(half=half, out=out):
                out[...] = half


def chain(place, pieces, mats):
    slabs = len(pieces)
    return pl.pallas_call(
        functools.partial(chain_kernel, slabs),
        in_specs=[pl.BlockSpec(memory_space=pltpu.SMEM)] + [VMEM] * (2 * slabs),
        out_specs=[VMEM] * slabs,
        out_shape=[jax.ShapeDtypeStruct(pieces[0].shape, BF)] * slabs,
        scratch_shapes=[
            pltpu.VMEM((slabs,) + pieces[0].shape, BF),
            pltpu.VMEM((slabs,) + mats[0].shape, F32),
        ],
        compiler_params=params(),
        name="sweep_chain",
    )(place, *pieces, *mats)


def collect_kernel(slabs, blk, part, blocks, aliased, place, *refs):
    pieces = refs[:slabs]
    own, root = refs[slabs + aliased :]
    cols = own.shape[1] // 2
    for mask, piece in enumerate(pieces):
        for index in range(slabs):
            rows, left = piece_of(index, blk, blocks, part)

            @pl.when(place[0] ^ mask == index)
            def _(piece=piece, rows=rows, left=left):
                real, imag = piece[:, :part], piece[:, part:]
                own[rows, left : left + part] = real
                own[rows, cols + left : cols + left + part] = imag
                root[0, 0, rows, left : left + part] = real.astype(F32)
                root[0, 1, rows, left : left + part] = imag.astype(F32)


def collect(h, place, pieces, before, rows, width):
    slabs = len(pieces)
    blk, part = pieces[0].shape[0], pieces[0].shape[1] // 2
    cols = width // HALVES
    aliased = [] if before is None else [before]
    spec = pltpu.PrefetchScalarGridSpec(
        num_scalar_prefetch=1,
        grid=(1,),
        in_specs=[VMEM] * slabs + [pl.BlockSpec(memory_space=pl.ANY)] * len(aliased),
        out_specs=[VMEM, pl.BlockSpec((1, 2, rows, cols), lambda i, p: (0, 0, 0, h))],
    )
    return pl.pallas_call(
        functools.partial(collect_kernel, slabs, blk, part, rows // blk, len(aliased)),
        grid_spec=spec,
        out_shape=[
            jax.ShapeDtypeStruct((rows, 2 * cols), BF),
            jax.ShapeDtypeStruct((1, 2, rows, width), F32),
        ],
        input_output_aliases={1 + slabs: 1} if aliased else {},
        compiler_params=params(),
        name="interface_collect",
    )(place, *pieces, *aliased)


def backward_kernel(group, fronts, aliased, owners, place, fwd, mats, *refs):
    fields = refs[:fronts]
    out, wide = refs[fronts + aliased :]
    step = pl.program_id(0)
    cols = fwd.shape[2] // 2

    @pl.when(step == 0)
    def _():
        for dist in range(fronts):
            wide[dist] = spread(fields[dist][...])

    for j in range(group):
        dist = owners[step * group + j] ^ place[1]
        value = fwd[j].astype(F32) - dot(mats[j], wide[dist])
        out[0, 0, j] = value[:, :cols].astype(BF)
        out[0, 1, j] = value[:, cols:].astype(BF)


def backward(h, owners, place, fwd, mats, fields, before, width):
    leaves, blk, wide = fwd.shape
    cols = wide // 2
    rows = fields[0].shape[0]
    fronts = len(fields)
    group = 4
    aliased = [] if before is None else [before]
    spec = pltpu.PrefetchScalarGridSpec(
        num_scalar_prefetch=2,
        grid=(leaves // group,),
        in_specs=[
            pl.BlockSpec((group, blk, wide), lambda i, o, p: (i, 0, 0)),
            pl.BlockSpec((group, blk, 2 * rows), lambda i, o, p: (i, 0, 0)),
        ]
        + [VMEM] * fronts
        + [pl.BlockSpec(memory_space=pl.ANY)] * len(aliased),
        out_specs=pl.BlockSpec((1, 2, group, blk, cols), lambda i, o, p: (0, 0, i, 0, h)),
        scratch_shapes=[pltpu.VMEM((fronts, 2 * rows, wide), BF)],
    )
    return pl.pallas_call(
        functools.partial(backward_kernel, group, fronts, len(aliased)),
        grid_spec=spec,
        out_shape=jax.ShapeDtypeStruct((1, 2, leaves, blk, width), BF),
        input_output_aliases={4 + fronts: 0} if aliased else {},
        compiler_params=params(),
        cost_estimate=pl.CostEstimate(flops=2 * leaves * blk * 2 * rows * wide, bytes_accessed=8 << 20, transcendentals=0),
        name="leaf_backward",
    )(owners, place, fwd, mats, *fields, *aliased)


def body(leaf_rhs, leaf_inv, leaf_off, parent, ancestors, root_rhs, root_inv, coupling):
    fronts, slabs = lax.axis_size("front"), lax.axis_size("slab")
    rows, width = root_rhs.shape[2], root_rhs.shape[3]
    blk = leaf_rhs.shape[3]
    owners = parent.reshape(-1)
    place = jnp.stack([lax.axis_index("slab"), lax.axis_index("front")]).astype(jnp.int32)
    pairs = fronts // 2

    same, other = pack(place, root_inv, coupling)
    mats = [same] + [crossed((same, other)[mask % 2], "slab", mask) for mask in range(1, slabs)]

    leaf_fwd, fields = [], []
    for h in range(HALVES):
        fwd, keep, send = forward(h, owners, place, leaf_rhs, leaf_inv, leaf_off, ancestors, fronts, rows)
        leaf_fwd.append(fwd)
        near = crossed(send, "front", 1)
        far = []
        for j in range(1, pairs):
            total = (keep[j].astype(F32) + near[j].astype(F32)).astype(BF)
            far.append(crossed(total, "front", 2 * j))
        fields.append((keep, near, far))
    folded = fold(leaf_inv, leaf_off, ancestors, rows)

    root_sol, leaf_sol = None, None
    for h in range(HALVES):
        keep, near, far = fields[h]
        pieces = reduce(h, place, root_rhs, keep, near, far, slabs, blk)
        pieces = [pieces[0]] + [crossed(pieces[mask], "slab", mask) for mask in range(1, slabs)]
        solved = chain(place, pieces, mats)
        solved = [solved[0]] + [crossed(solved[mask], "slab", mask) for mask in range(1, slabs)]
        own, root_sol = collect(h, place, solved, root_sol, rows, width)
        mine = [own] + [crossed(own, "front", 2 * j) for j in range(1, pairs)]
        theirs = [crossed(value, "front", 1) for value in mine]
        every = [value for pair in zip(mine, theirs) for value in pair]
        leaf_sol = backward(h, owners, place, leaf_fwd[h], folded, every, leaf_sol, width)
    return leaf_sol, root_sol


def solution(mesh):
    in_specs = (
        P("slab", None, "front", None, None),
        P("slab", "front", None, None, None),
        P("slab", "front", None, None, None),
        P("slab", "front", None),
        P("slab", "front", None),
        P("slab", None, "front", None),
        P("slab", "front", None, None, None),
        P("slab", "front"),
    )
    out_specs = (P("slab", None, "front", None, None), P("slab", None, "front", None))
    return jax.shard_map(body, mesh=mesh, in_specs=in_specs, out_specs=out_specs, check_vma=False)
```

time: 340 us -> 117 us (0.34)
  waiting for transfers between devices: 113 us -> 36.2 us
  local copies, waits for them, and re-layouts: 82.5 us -> 6.01 us
  blocking collectives: 52.5 us -> 0 us
  matrix products: 49.9 us -> 0 us
  Pallas kernels: 0 us -> 34.3 us
  starting transfers between devices: 24.7 us -> 39.4 us
  other arithmetic: 14.6 us -> 0.49 us
    all_to_all x1 -> x0, blocking collectives: 52.5 us -> none  [body(): lax.all_to_all(slot_rows, 'front', split_axis=1, concat_axis=1, tiled=True)]
    dot_general x36 -> x0, matrix products: 49.9 us -> none  [the longest x4 8.7 us: planes_apply(): jnp.einsum(form, real_mat, imag_vec, preferred_element_type=jnp.float32)]
    all_to_all x2 -> x0, waiting for transfers between devices: 48.4 us -> none  [the longest x1 48.4 us: body(): lax.all_to_all(placed, 'front', split_axis=1, concat_axis=1, tiled=True)]
    reshape x5 -> x0, local copies, waits for them, and re-layouts: 36.2 us -> none  [the longest x2 15.3 us: body(): placed = placed.reshape(2, fronts, per_owner, blk, width)]
    pallas_call x0 -> x12, Pallas kernels: none -> 34.3 us  [the longest x2 13.6 us: forward(): pl.pallas_call(functools.partial(forward_kernel, group, cap, fronts, rows...]
    ppermute x3 -> x37, waiting for transfers between devices: 64.3 us -> 36.2 us  [crossed(): lax.ppermute(x, axis, [(i, i ^ mask) for i in range(lax.axis_size(axis))])]
    ppermute x3 -> x37, starting transfers between devices: 15.9 us -> 39.4 us  [crossed(): lax.ppermute(x, axis, [(i, i ^ mask) for i in range(lax.axis_size(axis))])]
    all_to_all x2 -> x0, local copies, waits for them, and re-layouts: 20.9 us -> none  [the longest x1 15.7 us: body(): lax.all_to_all(slot_rows, 'front', split_axis=1, concat_axis=1, tiled=True)]
  transfers between devices with their start and end apart: 5 -> 37, of which waited for: 4 -> 11; matrix products, arithmetic and copies ran while one was open for 2% -> 0% of each run, Pallas kernels for 0% -> 20%
where the time goes in v1:
time: 117 us
  starting transfers between devices  39.4 us (34%)
  waiting for transfers between devices  36.2 us (31%)
  Pallas kernels  34.3 us (29%)
  local copies, waits for them, and re-layouts  6.01 us (5%)
    ppermute x37, starting transfers between devices, crossed(): lax.ppermute(x, axis, [(i, i ^ mask) for i in range(lax.axis_size(axis))])  39.4 us
    ppermute x37, waiting for transfers between devices, crossed(): lax.ppermute(x, axis, [(i, i ^ mask) for i in range(lax.axis_size(axis))])  36.2 us
    pallas_call x2, Pallas kernels, forward(): pl.pallas_call(functools.partial(forward_kernel, group, cap, fronts, rows...  13.6 us
    pallas_call x2, Pallas kernels, backward(): pl.pallas_call(functools.partial(backward_kernel, group, fronts, len(alia...  7.62 us
    unnamed x18, local copies, waits for them, and re-layouts  6.01 us
    pallas_call x2, Pallas kernels, chain(): pl.pallas_call(functools.partial(chain_kernel, slabs), in_specs=[pl.Block...  4.99 us
    pallas_call x2, Pallas kernels, collect(): pl.pallas_call(functools.partial(collect_kernel, slabs, blk, part, rows /...  3.22 us
    pallas_call x1, Pallas kernels, fold(): pl.pallas_call(functools.partial(fold_kernel, group, rows), grid=(leaves...  2.34 us
  transfers between devices with their start and end apart: 37, of which 11 were waited for; matrix products, arithmetic and copies ran while one was open for 0% of the time, Pallas kernels for 20%

profile of v1, /device:TPU:0, one launch (start us, length us, event | category | flops | bytes accessed | tf_op | source)
XLA Modules:
  0.0 117.2 jit_solution(11199672376164446439)
XLA Ops:
  0.7 2.2 %copy-done = bf16[1,2,16,128,512]{4,3,2,1,0:T(8,128)(2,1)S(1)} copy-done((bf16[1,2,16,128,512]{4,3,2,1,0:T(8,128)(2,1)S(1)}, bf16[1,2,16,128,512]{4,3,2,1,0:T(8,128)(2,1)}, u32[]{:S(2)}) %copy-start) | copy-done | bytes 4194328
  2.9 1.2 %copy-done.1 = bf16[1,16,2,128,128]{4,3,2,1,0:T(8,128)(2,1)S(1)} copy-done((bf16[1,16,2,128,128]{4,3,2,1,0:T(8,128)(2,1)S(1)}, bf16[1,16,2,128,128]{4,3,2,1,0:T(8,128)(2,1)}, u32[]{:S(2)}) %copy-start.1) | copy-done | bytes 1048600
  4.1 1.2 %copy-done.2 = bf16[1,16,2,128,128]{4,3,2,1,0:T(8,128)(2,1)S(1)} copy-done((bf16[1,16,2,128,128]{4,3,2,1,0:T(8,128)(2,1)S(1)}, bf16[1,16,2,128,128]{4,3,2,1,0:T(8,128)(2,1)}, u32[]{:S(2)}) %copy-start.2) | copy-done | bytes 1048600
  5.4 0.7 copy-done.5
  6.1 0.7 copy-done.7
  6.7 6.8 %leaf_forward.3 = (bf16[16,128,512]{2,1,0:T(8,128)(2,1)S(1)}, bf16[4,256,512]{2,1,0:T(8,128)(2,1)S(1)}, bf16[4,256,512]{2,1,0:T(8,128)(2,1)S(1)}) custom-call(s32[16]{0:T(128)S(1)} %bitcast.16, s32[2]{0:T(128)S(1)} %pad_add_fusion.place, bf16[1,2,16,128,512]{4,3,2,1,0:T(8,128)(2,1)S(1)} %copy-done, bf16[1,16,2,128,128]{4,3,2,1,0:T(8,128)(2,1)S(1)} %copy-done.1, ...), custom_call_target="tpu_custom_call" | custom-call | flops 1610612736 | bytes 6291456 | tf_op jit(solution)/shard_map/leaf_forward/pallas_call | solution.py:105
  13.6 0.5 collective-permute-start.13
  14.1 6.8 %leaf_forward.2 = (bf16[16,128,512]{2,1,0:T(8,128)(2,1)S(1)}, bf16[4,256,512]{2,1,0:T(8,128)(2,1)S(1)}, bf16[4,256,512]{2,1,0:T(8,128)(2,1)S(1)}) custom-call(s32[16]{0:T(128)S(1)} %bitcast.17, s32[2]{0:T(128)S(1)} %pad_add_fusion.place, bf16[1,2,16,128,512]{4,3,2,1,0:T(8,128)(2,1)S(1)} %copy-done, bf16[1,16,2,128,128]{4,3,2,1,0:T(8,128)(2,1)S(1)} %copy-done.1, ...), custom_call_target="tpu_custom_call" | custom-call | flops 1610612736 | bytes 6291456 | tf_op jit(solution)/shard_map/leaf_forward/pallas_call | solution.py:105
  21.0 0.6 solve_pack.1
  21.6 5.1 %collective-permute-start.9 = (f32[264,128]{1,0:T(8,128)S(1)}, f32[264,128]{1,0:T(8,128)S(1)}, u32[]{:S(2)}, u32[]{:S(2)}) collective-permute-start(f32[264,128]{1,0:T(8,128)S(1)} %get-tuple-element.38), channel_id=1, source_target_pairs={{0,24},{8,16},{16,8},{24,0},{1,25},{9,17},{17,9},{25,1},{2,26},{10... | collective-permute-start | bytes 405512 | tf_op jit(solution)/shard_map/ppermute | solution.py:21
  26.9 2.5 %collective-permute-start.16 = (bf16[256,512]{1,0:T(8,128)(2,1)S(1)}, bf16[256,512]{1,0:T(8,128)(2,1)S(1)}, u32[]{:S(2)}, u32[]{:S(2)}) collective-permute-start(bf16[256,512]{1,0:T(8,128)(2,1)S(1)} %get-tuple-element.58), channel_id=1, source_target_pairs={{0,6},{1,7},{2,4},{3,5},{4,2},{5,3},{6,0},{7,1},{8,14},{9,15},{10,... | collective-permute-start | bytes 786440 | tf_op jit(solution)/shard_map/ppermute | solution.py:21
  29.9 0.5 collective-permute-start.14
  30.7 2.5 %collective-permute-start.3 = (bf16[256,512]{1,0:T(8,128)(2,1)S(1)}, bf16[256,512]{1,0:T(8,128)(2,1)S(1)}, u32[]{:S(2)}, u32[]{:S(2)}) collective-permute-start(bf16[256,512]{1,0:T(8,128)(2,1)S(1)} %get-tuple-element.61), channel_id=1, source_target_pairs={{0,6},{1,7},{2,4},{3,5},{4,2},{5,3},{6,0},{7,1},{8,14},{9,15},{10,... | collective-permute-start | bytes 786440 | tf_op jit(solution)/shard_map/ppermute | solution.py:21
  33.7 3.4 %collective-permute-done.16.refs_2_ = bf16[256,512]{1,0:T(8,128)(2,1)S(1)} collective-permute-done((bf16[256,512]{1,0:T(8,128)(2,1)S(1)}, bf16[256,512]{1,0:T(8,128)(2,1)S(1)}, u32[]{:S(2)}, u32[]{:S(2)}) %collective-permute-start.16) | collective-permute-done | bytes 262176 | tf_op jit(solution)/shard_map/ppermute | solution.py:21
  37.1 1.5 %collective-permute-start.1 = (bf16[256,512]{1,0:T(8,128)(2,1)S(1)}, bf16[256,512]{1,0:T(8,128)(2,1)S(1)}, u32[]{:S(2)}, u32[]{:S(2)}) collective-permute-start(bf16[256,512]{1,0:T(8,128)(2,1)S(1)} %get-tuple-element.63), channel_id=1, source_target_pairs={{0,2},{1,3},{2,0},{3,1},{4,6},{5,7},{6,4},{7,5},{8,10},{9,11},{10,... | collective-permute-start | bytes 786440 | tf_op jit(solution)/shard_map/ppermute | solution.py:21
  38.6 4.2 %collective-permute-done.15.refs_1_ = bf16[256,512]{1,0:T(8,128)(2,1)S(1)} collective-permute-done((bf16[256,512]{1,0:T(8,128)(2,1)S(1)}, bf16[256,512]{1,0:T(8,128)(2,1)S(1)}, u32[]{:S(2)}, u32[]{:S(2)}) %collective-permute-start.15) | collective-permute-done | bytes 262176 | tf_op jit(solution)/shard_map/ppermute | solution.py:21
  42.8 0.5 collective-permute-start.8
  43.4 1.0 interface_reduce.3
  44.3 4.1 %collective-permute-done.3.refs_2_ = bf16[256,512]{1,0:T(8,128)(2,1)S(1)} collective-permute-done((bf16[256,512]{1,0:T(8,128)(2,1)S(1)}, bf16[256,512]{1,0:T(8,128)(2,1)S(1)}, u32[]{:S(2)}, u32[]{:S(2)}) %collective-permute-start.3) | collective-permute-done | bytes 262176 | tf_op jit(solution)/shard_map/ppermute | solution.py:21
  48.4 4.3 %collective-permute-done.2.refs_1_ = bf16[256,512]{1,0:T(8,128)(2,1)S(1)} collective-permute-done((bf16[256,512]{1,0:T(8,128)(2,1)S(1)}, bf16[256,512]{1,0:T(8,128)(2,1)S(1)}, u32[]{:S(2)}, u32[]{:S(2)}) %collective-permute-start.2) | collective-permute-done | bytes 262176 | tf_op jit(solution)/shard_map/ppermute | solution.py:21
  52.8 1.8 %collective-permute-start.19 = (bf16[128,256]{1,0:T(8,128)(2,1)S(1)}, bf16[128,256]{1,0:T(8,128)(2,1)S(1)}, u32[]{:S(2)}, u32[]{:S(2)}) collective-permute-start(bf16[128,256]{1,0:T(8,128)(2,1)S(1)} %get-tuple-element.48), channel_id=1, source_target_pairs={{0,24},{8,16},{16,8},{24,0},{1,25},{9,17},{17,9},{25,1},{2,26},{10... | collective-permute-start | bytes 196616 | tf_op jit(solution)/shard_map/ppermute | solution.py:21
  54.6 1.0 interface_reduce.2
  55.6 1.6 %collective-permute-start.4 = (bf16[128,256]{1,0:T(8,128)(2,1)S(1)}, bf16[128,256]{1,0:T(8,128)(2,1)S(1)}, u32[]{:S(2)}, u32[]{:S(2)}) collective-permute-start(bf16[128,256]{1,0:T(8,128)(2,1)S(1)} %get-tuple-element.34), channel_id=1, source_target_pairs={{0,8},{8,0},{16,24},{24,16},{1,9},{9,1},{17,25},{25,17},{2,10},{10... | collective-permute-start | bytes 196616 | tf_op jit(solution)/shard_map/ppermute | solution.py:21
  57.2 1.0 collective-permute-start.5
  58.3 1.8 %collective-permute-start.6 = (bf16[128,256]{1,0:T(8,128)(2,1)S(1)}, bf16[128,256]{1,0:T(8,128)(2,1)S(1)}, u32[]{:S(2)}, u32[]{:S(2)}) collective-permute-start(bf16[128,256]{1,0:T(8,128)(2,1)S(1)} %get-tuple-element.36), channel_id=1, source_target_pairs={{0,24},{8,16},{16,8},{24,0},{1,25},{9,17},{17,9},{25,1},{2,26},{10... | collective-permute-start | bytes 196616 | tf_op jit(solution)/shard_map/ppermute | solution.py:21
  60.1 2.5 %sweep_chain.3 = (bf16[128,256]{1,0:T(8,128)(2,1)S(1)}, bf16[128,256]{1,0:T(8,128)(2,1)S(1)}, bf16[128,256]{1,0:T(8,128)(2,1)S(1)}, bf16[128,256]{1,0:T(8,128)(2,1)S(1)}) custom-call(s32[2]{0:T(128)S(1)} %pad_add_fusion.place, bf16[128,256]{1,0:T(8,128)(2,1)S(1)} %get-tuple-element.45.refs_0_, bf16[128,256]{1,0:T(8,128)(2,1)S(1)} %collective-permute-done.17.refs_1_, ...), custom_call_target="tpu_custom_call" | custom-call | tf_op jit(solution)/shard_map/sweep_chain/pallas_call | solution.py:250
  62.6 4.0 %collective-permute-start.20 = (bf16[128,256]{1,0:T(8,128)(2,1)S(1)}, bf16[128,256]{1,0:T(8,128)(2,1)S(1)}, u32[]{:S(2)}, u32[]{:S(2)}) collective-permute-start(bf16[128,256]{1,0:T(8,128)(2,1)S(1)} %get-tuple-element.50), channel_id=1, source_target_pairs={{0,8},{8,0},{16,24},{24,16},{1,9},{9,1},{17,25},{25,17},{2,10},{10... | collective-permute-start | bytes 196616 | tf_op jit(solution)/shard_map/ppermute | solution.py:21
  66.8 2.3 %collective-permute-start.22 = (bf16[128,256]{1,0:T(8,128)(2,1)S(1)}, bf16[128,256]{1,0:T(8,128)(2,1)S(1)}, u32[]{:S(2)}, u32[]{:S(2)}) collective-permute-start(bf16[128,256]{1,0:T(8,128)(2,1)S(1)} %get-tuple-element.52), channel_id=1, source_target_pairs={{0,24},{8,16},{16,8},{24,0},{1,25},{9,17},{17,9},{25,1},{2,26},{10... | collective-permute-start | bytes 196616 | tf_op jit(solution)/shard_map/ppermute | solution.py:21
  69.0 2.5 %sweep_chain.2 = (bf16[128,256]{1,0:T(8,128)(2,1)S(1)}, bf16[128,256]{1,0:T(8,128)(2,1)S(1)}, bf16[128,256]{1,0:T(8,128)(2,1)S(1)}, bf16[128,256]{1,0:T(8,128)(2,1)S(1)}) custom-call(s32[2]{0:T(128)S(1)} %pad_add_fusion.place, bf16[128,256]{1,0:T(8,128)(2,1)S(1)} %get-tuple-element.33.refs_0_, bf16[128,256]{1,0:T(8,128)(2,1)S(1)} %collective-permute-done.4.refs_1_, ...), custom_call_target="tpu_custom_call" | custom-call | tf_op jit(solution)/shard_map/sweep_chain/pallas_call | solution.py:250
  71.5 1.1 collective-permute-start.10
  72.6 0.5 collective-permute-done.22.refs_3_
  73.2 1.5 %interface_collect.2 = (bf16[256,512]{1,0:T(8,128)(2,1)S(1)}, f32[1,2,256,512]{3,2,1,0:T(8,128)}) custom-call(s32[2]{0:T(128)S(1)} %pad_add_fusion.place, bf16[128,256]{1,0:T(8,128)(2,1)S(1)} %get-tuple-element.49.refs_0_, bf16[128,256]{1,0:T(8,128)(2,1)S(1)} %collective-permute-done.20.refs_1_, bf16[128,256]{1,0:T(8,128)(2,1)S(1)} %collective-permute-done.21.refs_2_, ...), custom_call_target="tpu_custom_call" | custom-call | tf_op jit(solution)/shard_map/interface_collect/pallas_call | solution.py:292
  74.7 1.3 %collective-permute-start.35 = (bf16[256,512]{1,0:T(8,128)(2,1)S(1)}, bf16[256,512]{1,0:T(8,128)(2,1)S(1)}, u32[]{:S(2)}, u32[]{:S(2)}) collective-permute-start(bf16[256,512]{1,0:T(8,128)(2,1)S(1)} %get-tuple-element.56.refs_0_), channel_id=1, source_target_pairs={{0,6},{1,7},{2,4},{3,5},{4,2},{5,3},{6,0},{7,1},{8,14},{9,15},{10,... | collective-permute-start | bytes 786440 | tf_op jit(solution)/shard_map/ppermute | solution.py:21
  76.0 1.7 %collective-permute-start.33 = (bf16[256,512]{1,0:T(8,128)(2,1)S(1)}, bf16[256,512]{1,0:T(8,128)(2,1)S(1)}, u32[]{:S(2)}, u32[]{:S(2)}) collective-permute-start(bf16[256,512]{1,0:T(8,128)(2,1)S(1)} %get-tuple-element.56.refs_0_), channel_id=1, source_target_pairs={{0,4},{1,5},{2,6},{3,7},{4,0},{5,1},{6,2},{7,3},{8,12},{9,13},{10,... | collective-permute-start | bytes 786440 | tf_op jit(solution)/shard_map/ppermute | solution.py:21
  77.7 0.5 collective-permute-start.31
  78.2 1.0 collective-permute-start.11
  79.1 5.9 %collective-permute-done.11.refs_2_ = bf16[128,256]{1,0:T(8,128)(2,1)S(1)} collective-permute-done((bf16[128,256]{1,0:T(8,128)(2,1)S(1)}, bf16[128,256]{1,0:T(8,128)(2,1)S(1)}, u32[]{:S(2)}, u32[]{:S(2)}) %collective-permute-start.11) | collective-permute-done | bytes 65568 | tf_op jit(solution)/shard_map/ppermute | solution.py:21
  85.0 1.8 %collective-permute-start.12 = (bf16[128,256]{1,0:T(8,128)(2,1)S(1)}, bf16[128,256]{1,0:T(8,128)(2,1)S(1)}, u32[]{:S(2)}, u32[]{:S(2)}) collective-permute-start(bf16[128,256]{1,0:T(8,128)(2,1)S(1)} %get-tuple-element.42), channel_id=1, source_target_pairs={{0,24},{8,16},{16,8},{24,0},{1,25},{9,17},{17,9},{25,1},{2,26},{10... | collective-permute-start | bytes 196616 | tf_op jit(solution)/shard_map/ppermute | solution.py:21
  86.9 4.2 %collective-permute-done.12.refs_3_ = bf16[128,256]{1,0:T(8,128)(2,1)S(1)} collective-permute-done((bf16[128,256]{1,0:T(8,128)(2,1)S(1)}, bf16[128,256]{1,0:T(8,128)(2,1)S(1)}, u32[]{:S(2)}, u32[]{:S(2)}) %collective-permute-start.12) | collective-permute-done | bytes 65568 | tf_op jit(solution)/shard_map/ppermute | solution.py:21
  91.1 1.7 %interface_collect.3 = (bf16[256,512]{1,0:T(8,128)(2,1)S(1)}, f32[1,2,256,512]{3,2,1,0:T(8,128)}) custom-call(s32[2]{0:T(128)S(1)} %pad_add_fusion.place, bf16[128,256]{1,0:T(8,128)(2,1)S(1)} %get-tuple-element.39.refs_0_, bf16[128,256]{1,0:T(8,128)(2,1)S(1)} %collective-permute-done.10.refs_1_, ...), custom_call_target="tpu_custom_call", output_to_operand_aliasing={{1}: (5, {})} | custom-call | tf_op jit(solution)/shard_map/interface_collect/pallas_call | solution.py:292
  92.8 1.3 %collective-permute-start.28 = (bf16[256,512]{1,0:T(8,128)(2,1)S(1)}, bf16[256,512]{1,0:T(8,128)(2,1)S(1)}, u32[]{:S(2)}, u32[]{:S(2)}) collective-permute-start(bf16[256,512]{1,0:T(8,128)(2,1)S(1)} %get-tuple-element.54.refs_0_), channel_id=1, source_target_pairs={{0,6},{1,7},{2,4},{3,5},{4,2},{5,3},{6,0},{7,1},{8,14},{9,15},{10,... | collective-permute-start | bytes 786440 | tf_op jit(solution)/shard_map/ppermute | solution.py:21
  94.1 1.7 %collective-permute-start.26 = (bf16[256,512]{1,0:T(8,128)(2,1)S(1)}, bf16[256,512]{1,0:T(8,128)(2,1)S(1)}, u32[]{:S(2)}, u32[]{:S(2)}) collective-permute-start(bf16[256,512]{1,0:T(8,128)(2,1)S(1)} %get-tuple-element.54.refs_0_), channel_id=1, source_target_pairs={{0,4},{1,5},{2,6},{3,7},{4,0},{5,1},{6,2},{7,3},{8,12},{9,13},{10,... | collective-permute-start | bytes 786440 | tf_op jit(solution)/shard_map/ppermute | solution.py:21
  95.7 0.5 collective-permute-start.24
  96.8 6.1 %collective-permute-done.28.refs_6_ = bf16[256,512]{1,0:T(8,128)(2,1)S(1)} collective-permute-done((bf16[256,512]{1,0:T(8,128)(2,1)S(1)}, bf16[256,512]{1,0:T(8,128)(2,1)S(1)}, u32[]{:S(2)}, u32[]{:S(2)}) %collective-permute-start.28) | collective-permute-done | bytes 262176 | tf_op jit(solution)/shard_map/ppermute | solution.py:21
  102.9 3.2 %collective-permute-done.26.refs_4_ = bf16[256,512]{1,0:T(8,128)(2,1)S(1)} collective-permute-done((bf16[256,512]{1,0:T(8,128)(2,1)S(1)}, bf16[256,512]{1,0:T(8,128)(2,1)S(1)}, u32[]{:S(2)}, u32[]{:S(2)}) %collective-permute-start.26) | collective-permute-done | bytes 262176 | tf_op jit(solution)/shard_map/ppermute | solution.py:21
  107.2 2.3 %leaf_fold.1.mats = bf16[16,128,512]{2,1,0:T(8,128)(2,1)S(1)} custom-call(bf16[1,16,2,128,128]{4,3,2,1,0:T(8,128)(2,1)S(1)} %copy-done.1, bf16[1,16,2,128,128]{4,3,2,1,0:T(8,128)(2,1)S(1)} %copy-done.2, s32[1,16,128]{2,1,0:T(8,128)S(1)} %copy-done.6), custom_call_target="tpu_custom_call" | custom-call | flops 536870912 | bytes 4194304 | tf_op jit(solution)/shard_map/leaf_fold/pallas_call | solution.py:132
  109.5 3.8 %leaf_backward.2.refs_8_ = bf16[1,2,16,128,512]{4,3,2,1,0:T(8,128)(2,1)} custom-call(s32[16]{0:T(128)S(1)} %bitcast.18, s32[2]{0:T(128)S(1)} %pad_add_fusion.place, bf16[16,128,512]{2,1,0:T(8,128)(2,1)S(1)} %get-tuple-element.55.fwd, bf16[16,128,512]{2,1,0:T(8,128)(2,1)S(1)} %leaf_fold.1.mats, bf16[256,512]{1,0:T(8,128)(2,1)S(1)} %get-tuple-element.56.refs_0_, ...), custom_call_target="tpu_custom_call" | custom-call | flops 1073741824 | bytes 8388608 | tf_op jit(solution)/shard_map/leaf_backward/pallas_call | solution.py:342
  113.3 3.8 %leaf_backward.3 = bf16[1,2,16,128,512]{4,3,2,1,0:T(8,128)(2,1)} custom-call(s32[16]{0:T(128)S(1)} %bitcast.19, s32[2]{0:T(128)S(1)} %pad_add_fusion.place, bf16[16,128,512]{2,1,0:T(8,128)(2,1)S(1)} %get-tuple-element.30.fwd, bf16[16,128,512]{2,1,0:T(8,128)(2,1)S(1)} %leaf_fold.1.mats, ...), custom_call_target="tpu_custom_call", output_to_operand_aliasing={{}: (12, {})} | custom-call | flops 1073741824 | bytes 8388608 | tf_op jit(solution)/shard_map/leaf_backward/pallas_call | solution.py:342
  (59 shorter events, 3.6 us)
Async XLA Ops:
  0.6 13.4 %copy-start.6 = (s32[1,16,128]{2,1,0:T(8,128)S(1)}, s32[1,16,128]{2,1,0:T(8,128)}, u32[]{:S(2)}) copy-start(s32[1,16,128]{2,1,0:T(8,128)} %anc.5) | copy-start | bytes 24580
  0.7 2.2 %copy-start = (bf16[1,2,16,128,512]{4,3,2,1,0:T(8,128)(2,1)S(1)}, bf16[1,2,16,128,512]{4,3,2,1,0:T(8,128)(2,1)}, u32[]{:S(2)}) copy-start(bf16[1,2,16,128,512]{4,3,2,1,0:T(8,128)(2,1)} %rhs.6) | copy-start | bytes 12582916
  2.9 1.2 %copy-start.1 = (bf16[1,16,2,128,128]{4,3,2,1,0:T(8,128)(2,1)S(1)}, bf16[1,16,2,128,128]{4,3,2,1,0:T(8,128)(2,1)}, u32[]{:S(2)}) copy-start(bf16[1,16,2,128,128]{4,3,2,1,0:T(8,128)(2,1)} %inv.7) | copy-start | bytes 3145732
  4.1 1.2 %copy-start.2 = (bf16[1,16,2,128,128]{4,3,2,1,0:T(8,128)(2,1)S(1)}, bf16[1,16,2,128,128]{4,3,2,1,0:T(8,128)(2,1)}, u32[]{:S(2)}) copy-start(bf16[1,16,2,128,128]{4,3,2,1,0:T(8,128)(2,1)} %off.5) | copy-start | bytes 3145732
  5.4 0.7 copy-start.5
  6.1 0.7 copy-start.7
  13.5 7.5 %copy-start.4 = (f32[1,2,2,128,128]{4,3,2,1,0:T(8,128)S(1)}, f32[1,2,2,128,128]{4,3,2,1,0:T(8,128)}, u32[]{:S(2)}) copy-start(f32[1,2,2,128,128]{4,3,2,1,0:T(8,128)} %inv.6) | copy-start | bytes 786436
  13.5 7.5 %copy-start.8 = (f32[1,256]{1,0:T(1,128)S(1)}, f32[1,256]{1,0:T(1,128)}, u32[]{:S(2)}) copy-start(f32[1,256]{1,0:T(1,128)} %param.15) | copy-start | bytes 3076
  13.5 29.8 %copy-start.3 = (bf16[1,2,256,512]{3,2,1,0:T(8,128)(2,1)S(1)}, bf16[1,2,256,512]{3,2,1,0:T(8,128)(2,1)}, u32[]{:S(2)}) copy-start(bf16[1,2,256,512]{3,2,1,0:T(8,128)(2,1)} %rhs.7) | copy-start | bytes 1572868
  13.6 13.1 %collective-permute-start.13 = (bf16[4,256,512]{2,1,0:T(8,128)(2,1)S(1)}, bf16[4,256,512]{2,1,0:T(8,128)(2,1)S(1)}, u32[]{:S(2)}, u32[]{:S(2)}) collective-permute-start(bf16[4,256,512]{2,1,0:T(8,128)(2,1)S(1)} %get-tuple-element.44), channel_id=1, source_target_pairs={{0,1},{1,0},{2,3},{3,2},{4,5},{5,4},{6,7},{7,6},{8,9},{9,8},{10,11... | collective-permute-start | bytes 3145736 | tf_op jit(solution)/shard_map/ppermute | solution.py:21
  20.9 9.6 %collective-permute-start = (bf16[4,256,512]{2,1,0:T(8,128)(2,1)S(1)}, bf16[4,256,512]{2,1,0:T(8,128)(2,1)S(1)}, u32[]{:S(2)}, u32[]{:S(2)}) collective-permute-start(bf16[4,256,512]{2,1,0:T(8,128)(2,1)S(1)} %get-tuple-element.32), channel_id=1, source_target_pairs={{0,1},{1,0},{2,3},{3,2},{4,5},{5,4},{6,7},{7,6},{8,9},{9,8},{10,11... | collective-permute-start | bytes 3145736 | tf_op jit(solution)/shard_map/ppermute | solution.py:21
  21.6 11.6 %collective-permute-start.9 = (f32[264,128]{1,0:T(8,128)S(1)}, f32[264,128]{1,0:T(8,128)S(1)}, u32[]{:S(2)}, u32[]{:S(2)}) collective-permute-start(f32[264,128]{1,0:T(8,128)S(1)} %get-tuple-element.38), channel_id=1, source_target_pairs={{0,24},{8,16},{16,8},{24,0},{1,25},{9,17},{17,9},{25,1},{2,26},{10... | collective-permute-start | bytes 405512 | tf_op jit(solution)/shard_map/ppermute | solution.py:21
  26.9 10.2 %collective-permute-start.16 = (bf16[256,512]{1,0:T(8,128)(2,1)S(1)}, bf16[256,512]{1,0:T(8,128)(2,1)S(1)}, u32[]{:S(2)}, u32[]{:S(2)}) collective-permute-start(bf16[256,512]{1,0:T(8,128)(2,1)S(1)} %get-tuple-element.58), channel_id=1, source_target_pairs={{0,6},{1,7},{2,4},{3,5},{4,2},{5,3},{6,0},{7,1},{8,14},{9,15},{10,... | collective-permute-start | bytes 786440 | tf_op jit(solution)/shard_map/ppermute | solution.py:21
  29.4 13.4 %collective-permute-start.15 = (bf16[256,512]{1,0:T(8,128)(2,1)S(1)}, bf16[256,512]{1,0:T(8,128)(2,1)S(1)}, u32[]{:S(2)}, u32[]{:S(2)}) collective-permute-start(bf16[256,512]{1,0:T(8,128)(2,1)S(1)} %get-tuple-element.59), channel_id=1, source_target_pairs={{0,4},{1,5},{2,6},{3,7},{4,0},{5,1},{6,2},{7,3},{8,12},{9,13},{10,... | collective-permute-start | bytes 786440 | tf_op jit(solution)/shard_map/ppermute | solution.py:21
  29.9 12.9 %collective-permute-start.14 = (bf16[256,512]{1,0:T(8,128)(2,1)S(1)}, bf16[256,512]{1,0:T(8,128)(2,1)S(1)}, u32[]{:S(2)}, u32[]{:S(2)}) collective-permute-start(bf16[256,512]{1,0:T(8,128)(2,1)S(1)} %get-tuple-element.60), channel_id=1, source_target_pairs={{0,2},{1,3},{2,0},{3,1},{4,6},{5,7},{6,4},{7,5},{8,10},{9,11},{10,... | collective-permute-start | bytes 786440 | tf_op jit(solution)/shard_map/ppermute | solution.py:21
  30.7 17.7 %collective-permute-start.3 = (bf16[256,512]{1,0:T(8,128)(2,1)S(1)}, bf16[256,512]{1,0:T(8,128)(2,1)S(1)}, u32[]{:S(2)}, u32[]{:S(2)}) collective-permute-start(bf16[256,512]{1,0:T(8,128)(2,1)S(1)} %get-tuple-element.61), channel_id=1, source_target_pairs={{0,6},{1,7},{2,4},{3,5},{4,2},{5,3},{6,0},{7,1},{8,14},{9,15},{10,... | collective-permute-start | bytes 786440 | tf_op jit(solution)/shard_map/ppermute | solution.py:21
  33.2 19.5 %collective-permute-start.2 = (bf16[256,512]{1,0:T(8,128)(2,1)S(1)}, bf16[256,512]{1,0:T(8,128)(2,1)S(1)}, u32[]{:S(2)}, u32[]{:S(2)}) collective-permute-start(bf16[256,512]{1,0:T(8,128)(2,1)S(1)} %get-tuple-element.62), channel_id=1, source_target_pairs={{0,4},{1,5},{2,6},{3,7},{4,0},{5,1},{6,2},{7,3},{8,12},{9,13},{10,... | collective-permute-start | bytes 786440 | tf_op jit(solution)/shard_map/ppermute | solution.py:21
  37.1 15.7 %collective-permute-start.1 = (bf16[256,512]{1,0:T(8,128)(2,1)S(1)}, bf16[256,512]{1,0:T(8,128)(2,1)S(1)}, u32[]{:S(2)}, u32[]{:S(2)}) collective-permute-start(bf16[256,512]{1,0:T(8,128)(2,1)S(1)} %get-tuple-element.63), channel_id=1, source_target_pairs={{0,2},{1,3},{2,0},{3,1},{4,6},{5,7},{6,4},{7,5},{8,10},{9,11},{10,... | collective-permute-start | bytes 786440 | tf_op jit(solution)/shard_map/ppermute | solution.py:21
  42.8 12.8 %collective-permute-start.7 = (f32[264,128]{1,0:T(8,128)S(1)}, f32[264,128]{1,0:T(8,128)S(1)}, u32[]{:S(2)}, u32[]{:S(2)}) collective-permute-start(f32[264,128]{1,0:T(8,128)S(1)} %get-tuple-element.38), channel_id=1, source_target_pairs={{0,8},{8,0},{16,24},{24,16},{1,9},{9,1},{17,25},{25,17},{2,10},{10... | collective-permute-start | bytes 405512 | tf_op jit(solution)/shard_map/ppermute | solution.py:21
  42.8 14.4 %collective-permute-start.8 = (f32[264,128]{1,0:T(8,128)S(1)}, f32[264,128]{1,0:T(8,128)S(1)}, u32[]{:S(2)}, u32[]{:S(2)}) collective-permute-start(f32[264,128]{1,0:T(8,128)S(1)} %get-tuple-element.37.refs_4_), channel_id=1, source_target_pairs={{0,16},{8,24},{16,0},{24,8},{1,17},{9,25},{17,1},{25,9},{2,18},{10... | collective-permute-start | bytes 405512 | tf_op jit(solution)/shard_map/ppermute | solution.py:21
  48.4 9.9 %collective-permute-start.17 = (bf16[128,256]{1,0:T(8,128)(2,1)S(1)}, bf16[128,256]{1,0:T(8,128)(2,1)S(1)}, u32[]{:S(2)}, u32[]{:S(2)}) collective-permute-start(bf16[128,256]{1,0:T(8,128)(2,1)S(1)} %get-tuple-element.46), channel_id=1, source_target_pairs={{0,8},{8,0},{16,24},{24,16},{1,9},{9,1},{17,25},{25,17},{2,10},{10... | collective-permute-start | bytes 196616 | tf_op jit(solution)/shard_map/ppermute | solution.py:21
  52.7 7.4 %collective-permute-start.18 = (bf16[128,256]{1,0:T(8,128)(2,1)S(1)}, bf16[128,256]{1,0:T(8,128)(2,1)S(1)}, u32[]{:S(2)}, u32[]{:S(2)}) collective-permute-start(bf16[128,256]{1,0:T(8,128)(2,1)S(1)} %get-tuple-element.47), channel_id=1, source_target_pairs={{0,16},{8,24},{16,0},{24,8},{1,17},{9,25},{17,1},{25,9},{2,18},{10... | collective-permute-start | bytes 196616 | tf_op jit(solution)/shard_map/ppermute | solution.py:21
  52.8 7.2 %collective-permute-start.19 = (bf16[128,256]{1,0:T(8,128)(2,1)S(1)}, bf16[128,256]{1,0:T(8,128)(2,1)S(1)}, u32[]{:S(2)}, u32[]{:S(2)}) collective-permute-start(bf16[128,256]{1,0:T(8,128)(2,1)S(1)} %get-tuple-element.48), channel_id=1, source_target_pairs={{0,24},{8,16},{16,8},{24,0},{1,25},{9,17},{17,9},{25,1},{2,26},{10... | collective-permute-start | bytes 196616 | tf_op jit(solution)/shard_map/ppermute | solution.py:21
  55.6 11.2 %collective-permute-start.4 = (bf16[128,256]{1,0:T(8,128)(2,1)S(1)}, bf16[128,256]{1,0:T(8,128)(2,1)S(1)}, u32[]{:S(2)}, u32[]{:S(2)}) collective-permute-start(bf16[128,256]{1,0:T(8,128)(2,1)S(1)} %get-tuple-element.34), channel_id=1, source_target_pairs={{0,8},{8,0},{16,24},{24,16},{1,9},{9,1},{17,25},{25,17},{2,10},{10... | collective-permute-start | bytes 196616 | tf_op jit(solution)/shard_map/ppermute | solution.py:21
  57.2 11.8 %collective-permute-start.5 = (bf16[128,256]{1,0:T(8,128)(2,1)S(1)}, bf16[128,256]{1,0:T(8,128)(2,1)S(1)}, u32[]{:S(2)}, u32[]{:S(2)}) collective-permute-start(bf16[128,256]{1,0:T(8,128)(2,1)S(1)} %get-tuple-element.35), channel_id=1, source_target_pairs={{0,16},{8,24},{16,0},{24,8},{1,17},{9,25},{17,1},{25,9},{2,18},{10... | collective-permute-start | bytes 196616 | tf_op jit(solution)/shard_map/ppermute | solution.py:21
  58.3 10.7 %collective-permute-start.6 = (bf16[128,256]{1,0:T(8,128)(2,1)S(1)}, bf16[128,256]{1,0:T(8,128)(2,1)S(1)}, u32[]{:S(2)}, u32[]{:S(2)}) collective-permute-start(bf16[128,256]{1,0:T(8,128)(2,1)S(1)} %get-tuple-element.36), channel_id=1, source_target_pairs={{0,24},{8,16},{16,8},{24,0},{1,25},{9,17},{17,9},{25,1},{2,26},{10... | collective-permute-start | bytes 196616 | tf_op jit(solution)/shard_map/ppermute | solution.py:21
  62.6 10.1 %collective-permute-start.20 = (bf16[128,256]{1,0:T(8,128)(2,1)S(1)}, bf16[128,256]{1,0:T(8,128)(2,1)S(1)}, u32[]{:S(2)}, u32[]{:S(2)}) collective-permute-start(bf16[128,256]{1,0:T(8,128)(2,1)S(1)} %get-tuple-element.50), channel_id=1, source_target_pairs={{0,8},{8,0},{16,24},{24,16},{1,9},{9,1},{17,25},{25,17},{2,10},{10... | collective-permute-start | bytes 196616 | tf_op jit(solution)/shard_map/ppermute | solution.py:21
  66.6 6.1 %collective-permute-start.21 = (bf16[128,256]{1,0:T(8,128)(2,1)S(1)}, bf16[128,256]{1,0:T(8,128)(2,1)S(1)}, u32[]{:S(2)}, u32[]{:S(2)}) collective-permute-start(bf16[128,256]{1,0:T(8,128)(2,1)S(1)} %get-tuple-element.51), channel_id=1, source_target_pairs={{0,16},{8,24},{16,0},{24,8},{1,17},{9,25},{17,1},{25,9},{2,18},{10... | collective-permute-start | bytes 196616 | tf_op jit(solution)/shard_map/ppermute | solution.py:21
  66.8 6.4 %collective-permute-start.22 = (bf16[128,256]{1,0:T(8,128)(2,1)S(1)}, bf16[128,256]{1,0:T(8,128)(2,1)S(1)}, u32[]{:S(2)}, u32[]{:S(2)}) collective-permute-start(bf16[128,256]{1,0:T(8,128)(2,1)S(1)} %get-tuple-element.52), channel_id=1, source_target_pairs={{0,24},{8,16},{16,8},{24,0},{1,25},{9,17},{17,9},{25,1},{2,26},{10... | collective-permute-start | bytes 196616 | tf_op jit(solution)/shard_map/ppermute | solution.py:21
  71.5 6.7 %collective-permute-start.10 = (bf16[128,256]{1,0:T(8,128)(2,1)S(1)}, bf16[128,256]{1,0:T(8,128)(2,1)S(1)}, u32[]{:S(2)}, u32[]{:S(2)}) collective-permute-start(bf16[128,256]{1,0:T(8,128)(2,1)S(1)} %get-tuple-element.40), channel_id=1, source_target_pairs={{0,8},{8,0},{16,24},{24,16},{1,9},{9,1},{17,25},{25,17},{2,10},{10... | collective-permute-start | bytes 196616 | tf_op jit(solution)/shard_map/ppermute | solution.py:21
  74.7 19.4 %collective-permute-start.35 = (bf16[256,512]{1,0:T(8,128)(2,1)S(1)}, bf16[256,512]{1,0:T(8,128)(2,1)S(1)}, u32[]{:S(2)}, u32[]{:S(2)}) collective-permute-start(bf16[256,512]{1,0:T(8,128)(2,1)S(1)} %get-tuple-element.56.refs_0_), channel_id=1, source_target_pairs={{0,6},{1,7},{2,4},{3,5},{4,2},{5,3},{6,0},{7,1},{8,14},{9,15},{10,... | collective-permute-start | bytes 786440 | tf_op jit(solution)/shard_map/ppermute | solution.py:21
  76.0 19.7 %collective-permute-start.33 = (bf16[256,512]{1,0:T(8,128)(2,1)S(1)}, bf16[256,512]{1,0:T(8,128)(2,1)S(1)}, u32[]{:S(2)}, u32[]{:S(2)}) collective-permute-start(bf16[256,512]{1,0:T(8,128)(2,1)S(1)} %get-tuple-element.56.refs_0_), channel_id=1, source_target_pairs={{0,4},{1,5},{2,6},{3,7},{4,0},{5,1},{6,2},{7,3},{8,12},{9,13},{10,... | collective-permute-start | bytes 786440 | tf_op jit(solution)/shard_map/ppermute | solution.py:21
  77.7 18.6 %collective-permute-start.31 = (bf16[256,512]{1,0:T(8,128)(2,1)S(1)}, bf16[256,512]{1,0:T(8,128)(2,1)S(1)}, u32[]{:S(2)}, u32[]{:S(2)}) collective-permute-start(bf16[256,512]{1,0:T(8,128)(2,1)S(1)} %get-tuple-element.56.refs_0_), channel_id=1, source_target_pairs={{0,2},{1,3},{2,0},{3,1},{4,6},{5,7},{6,4},{7,5},{8,10},{9,11},{10,... | collective-permute-start | bytes 786440 | tf_op jit(solution)/shard_map/ppermute | solution.py:21
  78.2 18.1 %collective-permute-start.30 = (bf16[256,512]{1,0:T(8,128)(2,1)S(1)}, bf16[256,512]{1,0:T(8,128)(2,1)S(1)}, u32[]{:S(2)}, u32[]{:S(2)}) collective-permute-start(bf16[256,512]{1,0:T(8,128)(2,1)S(1)} %get-tuple-element.56.refs_0_), channel_id=1, source_target_pairs={{0,1},{1,0},{2,3},{3,2},{4,5},{5,4},{6,7},{7,6},{8,9},{9,8},{10,11... | collective-permute-start | bytes 786440 | tf_op jit(solution)/shard_map/ppermute | solution.py:21
  78.2 6.8 %collective-permute-start.11 = (bf16[128,256]{1,0:T(8,128)(2,1)S(1)}, bf16[128,256]{1,0:T(8,128)(2,1)S(1)}, u32[]{:S(2)}, u32[]{:S(2)}) collective-permute-start(bf16[128,256]{1,0:T(8,128)(2,1)S(1)} %get-tuple-element.41), channel_id=1, source_target_pairs={{0,16},{8,24},{16,0},{24,8},{1,17},{9,25},{17,1},{25,9},{2,18},{10... | collective-permute-start | bytes 196616 | tf_op jit(solution)/shard_map/ppermute | solution.py:21
  85.0 6.1 %collective-permute-start.12 = (bf16[128,256]{1,0:T(8,128)(2,1)S(1)}, bf16[128,256]{1,0:T(8,128)(2,1)S(1)}, u32[]{:S(2)}, u32[]{:S(2)}) collective-permute-start(bf16[128,256]{1,0:T(8,128)(2,1)S(1)} %get-tuple-element.42), channel_id=1, source_target_pairs={{0,24},{8,16},{16,8},{24,0},{1,25},{9,17},{17,9},{25,1},{2,26},{10... | collective-permute-start | bytes 196616 | tf_op jit(solution)/shard_map/ppermute | solution.py:21
  92.8 10.1 %collective-permute-start.28 = (bf16[256,512]{1,0:T(8,128)(2,1)S(1)}, bf16[256,512]{1,0:T(8,128)(2,1)S(1)}, u32[]{:S(2)}, u32[]{:S(2)}) collective-permute-start(bf16[256,512]{1,0:T(8,128)(2,1)S(1)} %get-tuple-element.54.refs_0_), channel_id=1, source_target_pairs={{0,6},{1,7},{2,4},{3,5},{4,2},{5,3},{6,0},{7,1},{8,14},{9,15},{10,... | collective-permute-start | bytes 786440 | tf_op jit(solution)/shard_map/ppermute | solution.py:21
  94.1 12.0 %collective-permute-start.26 = (bf16[256,512]{1,0:T(8,128)(2,1)S(1)}, bf16[256,512]{1,0:T(8,128)(2,1)S(1)}, u32[]{:S(2)}, u32[]{:S(2)}) collective-permute-start(bf16[256,512]{1,0:T(8,128)(2,1)S(1)} %get-tuple-element.54.refs_0_), channel_id=1, source_target_pairs={{0,4},{1,5},{2,6},{3,7},{4,0},{5,1},{6,2},{7,3},{8,12},{9,13},{10,... | collective-permute-start | bytes 786440 | tf_op jit(solution)/shard_map/ppermute | solution.py:21
  95.7 10.5 %collective-permute-start.24 = (bf16[256,512]{1,0:T(8,128)(2,1)S(1)}, bf16[256,512]{1,0:T(8,128)(2,1)S(1)}, u32[]{:S(2)}, u32[]{:S(2)}) collective-permute-start(bf16[256,512]{1,0:T(8,128)(2,1)S(1)} %get-tuple-element.54.refs_0_), channel_id=1, source_target_pairs={{0,2},{1,3},{2,0},{3,1},{4,6},{5,7},{6,4},{7,5},{8,10},{9,11},{10,... | collective-permute-start | bytes 786440 | tf_op jit(solution)/shard_map/ppermute | solution.py:21
  96.3 10.4 %collective-permute-start.36 = (bf16[256,512]{1,0:T(8,128)(2,1)S(1)}, bf16[256,512]{1,0:T(8,128)(2,1)S(1)}, u32[]{:S(2)}, u32[]{:S(2)}) collective-permute-start(bf16[256,512]{1,0:T(8,128)(2,1)S(1)} %collective-permute-done.35.refs_6_), channel_id=1, source_target_pairs={{0,1},{1,0},{2,3},{3,2},{4,5},{5,4},{6,7},{7,6},{8,9},{9,8},{10,11... | collective-permute-start | bytes 786440 | tf_op jit(solution)/shard_map/ppermute | solution.py:21
  96.3 10.5 %collective-permute-start.34 = (bf16[256,512]{1,0:T(8,128)(2,1)S(1)}, bf16[256,512]{1,0:T(8,128)(2,1)S(1)}, u32[]{:S(2)}, u32[]{:S(2)}) collective-permute-start(bf16[256,512]{1,0:T(8,128)(2,1)S(1)} %collective-permute-done.33.refs_4_), channel_id=1, source_target_pairs={{0,1},{1,0},{2,3},{3,2},{4,5},{5,4},{6,7},{7,6},{8,9},{9,8},{10,11... | collective-permute-start | bytes 786440 | tf_op jit(solution)/shard_map/ppermute | solution.py:21
  102.9 6.6 %collective-permute-start.32 = (bf16[256,512]{1,0:T(8,128)(2,1)S(1)}, bf16[256,512]{1,0:T(8,128)(2,1)S(1)}, u32[]{:S(2)}, u32[]{:S(2)}) collective-permute-start(bf16[256,512]{1,0:T(8,128)(2,1)S(1)} %collective-permute-done.31.refs_2_), channel_id=1, source_target_pairs={{0,1},{1,0},{2,3},{3,2},{4,5},{5,4},{6,7},{7,6},{8,9},{9,8},{10,11... | collective-permute-start | bytes 786440 | tf_op jit(solution)/shard_map/ppermute | solution.py:21
  106.1 7.2 %collective-permute-start.23 = (bf16[256,512]{1,0:T(8,128)(2,1)S(1)}, bf16[256,512]{1,0:T(8,128)(2,1)S(1)}, u32[]{:S(2)}, u32[]{:S(2)}) collective-permute-start(bf16[256,512]{1,0:T(8,128)(2,1)S(1)} %get-tuple-element.54.refs_0_), channel_id=1, source_target_pairs={{0,1},{1,0},{2,3},{3,2},{4,5},{5,4},{6,7},{7,6},{8,9},{9,8},{10,11... | collective-permute-start | bytes 786440 | tf_op jit(solution)/shard_map/ppermute | solution.py:21
  106.2 7.1 %collective-permute-start.29 = (bf16[256,512]{1,0:T(8,128)(2,1)S(1)}, bf16[256,512]{1,0:T(8,128)(2,1)S(1)}, u32[]{:S(2)}, u32[]{:S(2)}) collective-permute-start(bf16[256,512]{1,0:T(8,128)(2,1)S(1)} %collective-permute-done.28.refs_6_), channel_id=1, source_target_pairs={{0,1},{1,0},{2,3},{3,2},{4,5},{5,4},{6,7},{7,6},{8,9},{9,8},{10,11... | collective-permute-start | bytes 786440 | tf_op jit(solution)/shard_map/ppermute | solution.py:21
  106.6 6.7 %collective-permute-start.27 = (bf16[256,512]{1,0:T(8,128)(2,1)S(1)}, bf16[256,512]{1,0:T(8,128)(2,1)S(1)}, u32[]{:S(2)}, u32[]{:S(2)}) collective-permute-start(bf16[256,512]{1,0:T(8,128)(2,1)S(1)} %collective-permute-done.26.refs_4_), channel_id=1, source_target_pairs={{0,1},{1,0},{2,3},{3,2},{4,5},{5,4},{6,7},{7,6},{8,9},{9,8},{10,11... | collective-permute-start | bytes 786440 | tf_op jit(solution)/shard_map/ppermute | solution.py:21
  106.7 6.6 %collective-permute-start.25 = (bf16[256,512]{1,0:T(8,128)(2,1)S(1)}, bf16[256,512]{1,0:T(8,128)(2,1)S(1)}, u32[]{:S(2)}, u32[]{:S(2)}) collective-permute-start(bf16[256,512]{1,0:T(8,128)(2,1)S(1)} %collective-permute-done.24.refs_2_), channel_id=1, source_target_pairs={{0,1},{1,0},{2,3},{3,2},{4,5},{5,4},{6,7},{7,6},{8,9},{9,8},{10,11... | collective-permute-start | bytes 786440 | tf_op jit(solution)/shard_map/ppermute | solution.py:21

commit v2 on v0

v2 whole, which is shorter than its diff:
```python
import functools

import jax
import jax.numpy as jnp
from jax import lax
from jax.experimental import pallas as pl
from jax.experimental.pallas import tpu as pltpu
from jax.sharding import PartitionSpec as P

HALVES = 2
BF = jnp.bfloat16
F32 = jnp.float32
VMEM = pl.BlockSpec(memory_space=pltpu.VMEM)
SMEM = pl.BlockSpec(memory_space=pltpu.SMEM)
HBM = pl.BlockSpec(memory_space=pltpu.HBM)
ANY = pl.BlockSpec(memory_space=pl.ANY)


def shape_of(shape, dtype=BF):
    return jax.ShapeDtypeStruct(shape, dtype)


def call(kernel, name, ins, in_specs, outs, out_specs, after=(), scratch=(), aliases=None):
    count, extra = len(ins), len(after)

    def wrapped(*refs):
        kernel(*refs[:count], *refs[count + extra :])

    return pl.pallas_call(
        wrapped,
        in_specs=list(in_specs) + [ANY] * extra,
        out_specs=out_specs,
        out_shape=outs,
        scratch_shapes=list(scratch),
        input_output_aliases=aliases or {},
        compiler_params=pltpu.CompilerParams(vmem_limit_bytes=24 * 1024 * 1024),
        cost_estimate=pl.CostEstimate(flops=1, bytes_accessed=1, transcendentals=0),
        name=name,
    )(*ins, *after)


def crossed(x, axis, mask):
    return lax.ppermute(x, axis, [(i, i ^ mask) for i in range(lax.axis_size(axis))])


def stacked(real, imag):
    return jnp.concatenate(
        [jnp.concatenate([real, -imag], axis=1), jnp.concatenate([imag, real], axis=1)], axis=0
    )


def dot(a, b, dims=((1,), (0,)), precision=None):
    return lax.dot_general(a, b, (dims, ((), ())), precision=precision, preferred_element_type=F32)


def table_of(anc_row, rows):
    ids = lax.broadcasted_iota(jnp.int32, (rows, anc_row.shape[1]), 0)
    return (ids == anc_row).astype(F32).astype(BF)


def forward_kernel(h, group, cap, owners, place, rhs, inv, off, anc, fwd, keep, send,
                   vecs, invs, offs, ancs, part, ids, seen, sems):
    leaves, blk, cols = vecs.shape[1], vecs.shape[2], vecs.shape[3]
    fronts, rows = part.shape[0], keep.shape[2]
    me = place[1]
    small = pltpu.make_async_copy(anc.at[0], ancs, sems.at[leaves // group, 0])
    small.start()

    def copies(at):
        span = pl.ds(at * group, group)
        return (
            pltpu.make_async_copy(inv.at[0, span], invs.at[span], sems.at[at, 0]),
            pltpu.make_async_copy(rhs.at[0, :, span, :, pl.ds(h * cols, cols)], vecs.at[:, span], sems.at[at, 1]),
            pltpu.make_async_copy(off.at[0, span], offs.at[span], sems.at[at, 2]),
        )

    for at in range(leaves // group):
        for copy in copies(at):
            copy.start()
    ids[...] = jnp.full(ids.shape, -1, jnp.int32)
    for dist in range(fronts):
        seen[dist] = 0
    small.wait()

    def some(at, carry):
        for copy in copies(at):
            copy.wait()
        for j in range(group):
            leaf = at * group + j
            dist = owners[leaf] ^ me
            rank = seen[dist]
            seen[dist] = rank + 1
            vec = jnp.concatenate([vecs[0, leaf], vecs[1, leaf]], axis=0)
            value = dot(stacked(invs[leaf, 0], invs[leaf, 1]), vec).astype(BF)
            fwd[leaf] = value
            moved = dot(stacked(offs[leaf, 0], offs[leaf, 1]), value).astype(BF)
            part[dist, 0, rank] = moved[:blk]
            part[dist, 1, rank] = moved[blk:]
            ids[pl.ds(dist * cap + rank, 1), :] = ancs[pl.ds(leaf, 1), :]
        return carry

    lax.fori_loop(0, leaves // group, some, 0)
    for dist in range(fronts):
        for rank in range(cap):

            @pl.when(seen[dist] <= rank)
            def _(dist=dist, rank=rank):
                part[dist, 0, rank] = jnp.zeros((blk, cols), BF)
                part[dist, 1, rank] = jnp.zeros((blk, cols), BF)

        row = jnp.concatenate([ids[dist * cap + rank : dist * cap + rank + 1, :] for rank in range(cap)], axis=1)
        table = table_of(row, rows)
        out = send if dist % 2 else keep
        for plane in range(2):
            out[dist // 2, plane] = dot(table, part[dist, plane].reshape(cap * blk, cols)).astype(BF)


def forward(h, owners, place, leaf_rhs, leaf_inv, leaf_off, ancestors, fronts, rows, after):
    _, _, leaves, blk, width = leaf_rhs.shape
    cols = width // HALVES
    cap = -(-leaves // fronts)
    group = 4
    block = shape_of((fronts // 2, 2, rows, cols))
    return call(
        functools.partial(forward_kernel, h, group, cap),
        "leaf_forward",
        [owners, place, leaf_rhs, leaf_inv, leaf_off, ancestors],
        [SMEM, SMEM, HBM, HBM, HBM, HBM],
        [shape_of((leaves, 2 * blk, cols)), block, block],
        [VMEM, VMEM, VMEM],
        after,
        [
            pltpu.VMEM((2, leaves, blk, cols), BF),
            pltpu.VMEM((leaves, 2, blk, blk), BF),
            pltpu.VMEM((leaves, 2, blk, blk), BF),
            pltpu.VMEM((leaves, blk), jnp.int32),
            pltpu.VMEM((fronts, 2, cap, blk, cols), BF),
            pltpu.VMEM((fronts * cap, blk), jnp.int32),
            pltpu.SMEM((fronts,), jnp.int32),
            pltpu.SemaphoreType.DMA((leaves // group + 1, 3)),
        ],
    )


def fold_kernel(inv, off, anc, out):
    leaves, _, blk, _ = inv.shape[1:]
    rows = out.shape[2] // 2

    def one(leaf, carry):
        mat = jnp.concatenate([inv[0, leaf, 0], inv[0, leaf, 1]], axis=1)
        real, imag = off[0, leaf, 0], off[0, leaf, 1]
        other = jnp.concatenate([jnp.concatenate([real, -imag], axis=1), jnp.concatenate([imag, real], axis=1)], axis=0)
        both = dot(mat, other, ((1,), (1,))).astype(BF)
        table = table_of(anc[0, pl.ds(leaf, 1), :], rows)
        out[leaf, :, :rows] = dot(both[:, :blk], table, ((1,), (1,))).astype(BF)
        out[leaf, :, rows:] = dot(both[:, blk:], table, ((1,), (1,))).astype(BF)
        return carry

    lax.fori_loop(0, leaves, one, 0, unroll=2)


def fold(leaf_inv, leaf_off, ancestors, rows, after):
    _, leaves, _, blk, _ = leaf_inv.shape
    return call(
        fold_kernel, "leaf_fold", [leaf_inv, leaf_off, ancestors], [VMEM] * 3,
        shape_of((leaves, blk, 2 * rows)), VMEM, after,
    )


def pack_kernel(place, inv, cpl, same, other, sems):
    blocks, blk = inv.shape[1], inv.shape[3]
    mine = place[0] % blocks
    copies = []
    for kind, out in enumerate((same, other)):
        block = mine ^ kind
        for plane in range(2):
            copies.append(pltpu.make_async_copy(inv.at[0, block, plane], out.at[pl.ds(plane * blk, blk)], sems.at[kind, plane]))
            copies[-1].start()
    for kind, out in enumerate((same, other)):
        out[2 * blk :, :] = jnp.broadcast_to(cpl[0, pl.ds(mine ^ kind, 1), :], (8, blk))
    for copy in copies:
        copy.wait()


def pack(place, root_inv, coupling, after):
    _, blocks, _, blk, _ = root_inv.shape
    shape = shape_of((2 * blk + 8, blk), F32)
    return call(
        pack_kernel, "solve_pack", [place, root_inv, coupling.reshape(1, blocks, blk)], [SMEM, HBM, VMEM],
        [shape, shape], [VMEM, VMEM], after, [pltpu.SemaphoreType.DMA((2, 2))],
    )


def total_kernel(keep, near, *outs):
    for j, out in enumerate(outs):
        out[...] = (keep[j + 1].astype(F32) + near[j + 1].astype(F32)).astype(BF)


def total(keep, near, after):
    pairs = keep.shape[0]
    return call(
        total_kernel, "interface_total", [keep, near], [VMEM, VMEM],
        [shape_of(keep.shape[1:])] * (pairs - 1), [VMEM] * (pairs - 1), after,
    )


def piece_of(index, blk, blocks, part):
    low, left = (index % blocks) * blk, (index // blocks) * part
    return slice(low, low + blk), slice(left, left + part)


def reduce_kernel(h, slabs, blk, part, terms, place, rhs, keep, near, *refs):
    rows, cols = keep.shape[2], keep.shape[3]
    outs = refs[terms:]
    field = []
    for plane in range(2):
        value = keep[0, plane].astype(F32) + near[0, plane].astype(F32)
        for ref in refs[:terms]:
            value = value + ref[plane].astype(F32)
        field.append((rhs[0, plane, :, h * cols : (h + 1) * cols].astype(F32) - value).astype(BF))
    for index in range(slabs):
        at = piece_of(index, blk, rows // blk, part)
        for mask, out in enumerate(outs):

            @pl.when(place[0] ^ mask == index)
            def _(at=at, out=out):
                out[0] = field[0][at]
                out[1] = field[1][at]


def reduce(h, place, root_rhs, keep, near, far, slabs, blk, after):
    _, _, rows, width = root_rhs.shape
    cols = width // HALVES
    part = cols * (rows // blk) // slabs
    return call(
        functools.partial(reduce_kernel, h, slabs, blk, part, len(far)), "interface_reduce",
        [place, root_rhs, keep, near, *far], [SMEM] + [VMEM] * (3 + len(far)),
        [shape_of((2, blk, part))] * slabs, [VMEM] * slabs, after,
    )


def chain_kernel(slabs, place, *refs):
    pieces, mats, outs = refs[:slabs], refs[slabs : 2 * slabs], refs[2 * slabs : 3 * slabs]
    held, solver = refs[3 * slabs :]
    me = place[0]
    for mask in range(slabs):
        held[mask] = pieces[mask][...]
        solver[mask] = mats[mask][...]
    _, _, blk, part = held.shape
    state = None
    for slab in range(slabs):
        at = me ^ slab
        field = held[at].reshape(2 * blk, part).astype(F32)
        packed = solver[at]
        if state is not None:
            scale = jnp.broadcast_to(packed[2 * blk : 2 * blk + 1, :], (blk, blk)).T[:, :1]
            field = field - jnp.concatenate([scale, scale], axis=0) * state
        mat = stacked(packed[:blk], packed[blk : 2 * blk])
        state = dot(mat, field, precision=lax.Precision.HIGHEST)
        half = state.astype(BF)
        for mask, out in enumerate(outs):

            @pl.when(at == mask)
            def _(half=half, out=out):
                out[0] = half[:blk]
                out[1] = half[blk:]


def chain(place, pieces, mats, after):
    slabs = len(pieces)
    return call(
        functools.partial(chain_kernel, slabs), "sweep_chain", [place, *pieces, *mats], [SMEM] + [VMEM] * (2 * slabs),
        [shape_of(pieces[0].shape)] * slabs, [VMEM] * slabs, after,
        [pltpu.VMEM((slabs,) + pieces[0].shape, BF), pltpu.VMEM((slabs,) + mats[0].shape, F32)],
    )


def collect_kernel(h, slabs, aliased, place, *refs):
    pieces = refs[:slabs]
    own, root, full, sem = refs[slabs + aliased :]
    _, blk, part = pieces[0].shape
    rows, cols = own.shape[1], own.shape[2]
    for mask, piece in enumerate(pieces):
        for index in range(slabs):
            at = piece_of(index, blk, rows // blk, part)

            @pl.when(place[0] ^ mask == index)
            def _(piece=piece, at=at):
                for plane in range(2):
                    own[(plane,) + at] = piece[plane]
                    full[(plane,) + at] = piece[plane].astype(F32)

    copy = pltpu.make_async_copy(full, root.at[0, :, :, pl.ds(h * cols, cols)], sem)
    copy.start()
    copy.wait()


def collect(h, place, pieces, before, rows, width, after):
    slabs = len(pieces)
    cols = width // HALVES
    aliased = [] if before is None else [before]
    return call(
        functools.partial(collect_kernel, h, slabs, len(aliased)), "interface_collect",
        [place, *pieces, *aliased], [SMEM] + [VMEM] * slabs + [HBM] * len(aliased),
        [shape_of((2, rows, cols)), shape_of((1, 2, rows, width), F32)], [VMEM, HBM], after,
        [pltpu.VMEM((2, rows, cols), F32), pltpu.SemaphoreType.DMA],
        {1 + slabs: 1} if aliased else None,
    )


def backward_kernel(h, fronts, cap, aliased, owners, place, fwd, mats, *refs):
    fields = refs[:fronts]
    out, held, slots, sems = refs[fronts + aliased :]
    leaves, wide, cols = fwd.shape
    blk = wide // 2
    rows = mats.shape[2] // 2
    for dist in range(fronts):
        for rank in range(cap):
            slots[dist * cap + rank] = -1
    for leaf in range(leaves):
        first = (owners[leaf] ^ place[1]) * cap
        place_at = first
        for rank in range(cap - 1):
            place_at = jnp.where(slots[first + rank] >= 0, first + rank + 1, place_at)
        slots[place_at] = leaf

    def copy_of(leaf):
        return pltpu.make_async_copy(held.at[leaf], out.at[0, :, leaf, :, pl.ds(h * cols, cols)], sems.at[leaf])

    for dist in range(fronts):
        field = fields[dist][...].reshape(2 * rows, cols)
        names = [slots[dist * cap + rank] for rank in range(cap)]
        parts = []
        for name in names:
            leaf = jnp.maximum(name, 0)
            real, imag = mats[leaf, :, :rows], mats[leaf, :, rows:]
            parts += [jnp.concatenate([real, -imag], axis=1), jnp.concatenate([imag, real], axis=1)]
        value = dot(jnp.concatenate(parts, axis=0), field)
        for rank, name in enumerate(names):

            @pl.when(name >= 0)
            def _(rank=rank, name=name):
                result = fwd[name].astype(F32) - value[rank * wide : (rank + 1) * wide]
                held[name, 0] = result[:blk].astype(BF)
                held[name, 1] = result[blk:].astype(BF)
                copy_of(name).start()

    for leaf in range(leaves):
        copy_of(leaf).wait()


def backward(h, owners, place, fwd, mats, fields, before, width, after):
    leaves, wide, cols = fwd.shape
    blk, rows, fronts = wide // 2, mats.shape[2] // 2, len(fields)
    cap = -(-leaves // fronts)
    aliased = [] if before is None else [before]
    return call(
        functools.partial(backward_kernel, h, fronts, cap, len(aliased)), "leaf_backward",
        [owners, place, fwd, mats, *fields, *aliased], [SMEM, SMEM] + [VMEM] * (2 + fronts) + [HBM] * len(aliased),
        shape_of((1, 2, leaves, blk, width)), HBM, after,
        [
            pltpu.VMEM((leaves, 2, blk, cols), BF),
            pltpu.SMEM((fronts * cap,), jnp.int32),
            pltpu.SemaphoreType.DMA((leaves,)),
        ],
        {4 + fronts: 0} if aliased else None,
    )


def body(leaf_rhs, leaf_inv, leaf_off, parent, ancestors, root_rhs, root_inv, coupling):
    fronts, slabs = lax.axis_size("front"), lax.axis_size("slab")
    rows, width = root_rhs.shape[2], root_rhs.shape[3]
    blk = leaf_rhs.shape[3]
    owners = parent.reshape(-1)
    place = jnp.stack([lax.axis_index("slab"), lax.axis_index("front")]).astype(jnp.int32)
    pairs = fronts // 2
    masks = range(1, slabs)

    def start_forward(h, after):
        fwd, keep, send = forward(h, owners, place, leaf_rhs, leaf_inv, leaf_off, ancestors, fronts, rows, after)
        return fwd, keep, crossed(send, "front", 1)

    def send_far(keep, near, after):
        sums = total(keep, near, after)
        return sums, [crossed(value, "front", 2 * (j + 1)) for j, value in enumerate(sums)]

    def over_slabs(values):
        return [values[0]] + [crossed(values[mask], "slab", mask) for mask in masks]

    def share(own):
        mine = [own] + [crossed(own, "front", 2 * j) for j in range(1, pairs)]
        return [value for field in mine for value in (field, crossed(field, "front", 1))]

    fwd0, keep0, near0 = start_forward(0, ())
    sums0, far0 = send_far(keep0, near0, ())
    same, other = pack(place, root_inv, coupling, [sums0[0]])
    mats = [same] + [crossed((same, other)[mask % 2], "slab", mask) for mask in masks]
    fwd1, keep1, near1 = start_forward(1, [same])
    folded = fold(leaf_inv, leaf_off, ancestors, rows, [fwd1])
    sums1, far1 = send_far(keep1, near1, [folded])
    pieces0 = reduce(0, place, root_rhs, keep0, near0, far0, slabs, blk, [sums1[0]])
    solved0 = chain(place, over_slabs(pieces0), mats, ())
    pieces1 = reduce(1, place, root_rhs, keep1, near1, far1, slabs, blk, [solved0[0]])
    own0, root_sol = collect(0, place, over_slabs(solved0), None, rows, width, [pieces1[0]])
    solved1 = chain(place, over_slabs(pieces1), mats, [own0])
    fields0 = share(own0)
    own1, root_sol = collect(1, place, over_slabs(solved1), root_sol, rows, width, ())
    fields1 = share(own1)
    leaf_sol = backward(0, owners, place, fwd0, folded, fields0, None, width, [own1])
    leaf_sol = backward(1, owners, place, fwd1, folded, fields1, leaf_sol, width, ())
    return leaf_sol, root_sol


def solution(mesh):
    in_specs = (
        P("slab", None, "front", None, None),
        P("slab", "front", None, None, None),
        P("slab", "front", None, None, None),
        P("slab", "front", None),
        P("slab", "front", None),
        P("slab", None, "front", None),
        P("slab", "front", None, None, None),
        P("slab", "front"),
    )
    out_specs = (P("slab", None, "front", None, None), P("slab", None, "front", None))
    return jax.shard_map(body, mesh=mesh, in_specs=in_specs, out_specs=out_specs, check_vma=False)
```

time: 340 us -> 120 us (0.35)
  waiting for transfers between devices: 113 us -> 27.8 us
  local copies, waits for them, and re-layouts: 82.5 us -> 6.01 us
  blocking collectives: 52.5 us -> 0 us
  matrix products: 49.9 us -> 0 us
  Pallas kernels: 0 us -> 37.6 us
  starting transfers between devices: 24.7 us -> 47.5 us
  other arithmetic: 14.6 us -> 0.08 us
    all_to_all x1 -> x0, blocking collectives: 52.5 us -> none  [body(): lax.all_to_all(slot_rows, 'front', split_axis=1, concat_axis=1, tiled=True)]
    dot_general x36 -> x0, matrix products: 49.9 us -> none  [the longest x4 8.7 us: planes_apply(): jnp.einsum(form, real_mat, imag_vec, preferred_element_type=jnp.float32)]
    all_to_all x2 -> x0, waiting for transfers between devices: 48.4 us -> none  [the longest x1 48.4 us: body(): lax.all_to_all(placed, 'front', split_axis=1, concat_axis=1, tiled=True)]
    pallas_call x0 -> x14, Pallas kernels: none -> 37.6 us  [call(): pl.pallas_call(wrapped, in_specs=list(in_specs) + [ANY] * extra, out_spec...]
    ppermute x3 -> x37, waiting for transfers between devices: 64.3 us -> 27.8 us  [crossed(): lax.ppermute(x, axis, [(i, i ^ mask) for i in range(lax.axis_size(axis))])]
    reshape x5 -> x0, local copies, waits for them, and re-layouts: 36.2 us -> none  [the longest x2 15.3 us: body(): placed = placed.reshape(2, fronts, per_owner, blk, width)]
    ppermute x3 -> x37, starting transfers between devices: 15.9 us -> 47.5 us  [crossed(): lax.ppermute(x, axis, [(i, i ^ mask) for i in range(lax.axis_size(axis))])]
    all_to_all x2 -> x0, local copies, waits for them, and re-layouts: 20.9 us -> none  [the longest x1 15.7 us: body(): lax.all_to_all(slot_rows, 'front', split_axis=1, concat_axis=1, tiled=True)]
  transfers between devices with their start and end apart: 5 -> 37, of which waited for: 4 -> 12; matrix products, arithmetic and copies ran while one was open for 2% -> 0% of each run, Pallas kernels for 0% -> 17%
where the time goes in v2:
time: 120 us
  starting transfers between devices  47.5 us (40%)
  Pallas kernels  37.6 us (31%)
  waiting for transfers between devices  27.8 us (23%)
  local copies, waits for them, and re-layouts  6.01 us (5%)
    ppermute x37, starting transfers between devices, crossed(): lax.ppermute(x, axis, [(i, i ^ mask) for i in range(lax.axis_size(axis))])  47.5 us
    pallas_call x14, Pallas kernels, call(): pl.pallas_call(wrapped, in_specs=list(in_specs) + [ANY] * extra, out_spec...  37.6 us
    ppermute x37, waiting for transfers between devices, crossed(): lax.ppermute(x, axis, [(i, i ^ mask) for i in range(lax.axis_size(axis))])  27.8 us
    unnamed x20, local copies, waits for them, and re-layouts  6.01 us
  transfers between devices with their start and end apart: 37, of which 12 were waited for; matrix products, arithmetic and copies ran while one was open for 0% of the time, Pallas kernels for 17%

profile of v2, /device:TPU:0, one launch (start us, length us, event | category | flops | bytes accessed | tf_op | source)
XLA Modules:
  0.0 120.0 jit_solution(9609725748436980578)
XLA Ops:
  0.7 2.2 %copy-done = bf16[1,2,16,128,512]{4,3,2,1,0:T(8,128)(2,1)S(1)} copy-done((bf16[1,2,16,128,512]{4,3,2,1,0:T(8,128)(2,1)S(1)}, bf16[1,2,16,128,512]{4,3,2,1,0:T(8,128)(2,1)}, u32[]{:S(2)}) %copy-start) | copy-done | bytes 4194328
  2.9 1.2 %copy-done.2 = bf16[1,16,2,128,128]{4,3,2,1,0:T(8,128)(2,1)S(1)} copy-done((bf16[1,16,2,128,128]{4,3,2,1,0:T(8,128)(2,1)S(1)}, bf16[1,16,2,128,128]{4,3,2,1,0:T(8,128)(2,1)}, u32[]{:S(2)}) %copy-start.2) | copy-done | bytes 1048600
  4.1 1.2 %copy-done.3 = bf16[1,16,2,128,128]{4,3,2,1,0:T(8,128)(2,1)S(1)} copy-done((bf16[1,16,2,128,128]{4,3,2,1,0:T(8,128)(2,1)S(1)}, bf16[1,16,2,128,128]{4,3,2,1,0:T(8,128)(2,1)}, u32[]{:S(2)}) %copy-start.3) | copy-done | bytes 1048600
  6.7 5.3 %leaf_forward.2 = (bf16[16,256,256]{2,1,0:T(8,128)(2,1)S(1)}, bf16[4,2,256,256]{3,2,1,0:T(8,128)(2,1)S(1)}, bf16[4,2,256,256]{3,2,1,0:T(8,128)(2,1)S(1)}) custom-call(s32[16]{0:T(128)S(1)} %bitcast.4, s32[2]{0:T(128)S(1)} %pad_add_fusion.refs_1_.refs_0_, bf16[1,2,16,128,512]{4,3,2,1,0:T(8,128)(2,1)S(1)} %copy-done, ...), custom_call_target="tpu_custom_call" | custom-call | flops 1 | bytes 1 | tf_op jit(solution)/shard_map/leaf_forward/pallas_call | solution.py:29
  12.6 2.3 %collective-permute-done.refs_1_.refs_3_ = bf16[4,2,256,256]{3,2,1,0:T(8,128)(2,1)S(1)} collective-permute-done((bf16[4,2,256,256]{3,2,1,0:T(8,128)(2,1)S(1)}, bf16[4,2,256,256]{3,2,1,0:T(8,128)(2,1)S(1)}, u32[]{:S(2)}, u32[]{:S(2)}) %collective-permute-start) | collective-permute-done | bytes 1048608 | tf_op jit(solution)/shard_map/ppermute | solution.py:43
  15.1 0.9 solve_pack.1
  16.0 5.3 %leaf_forward.3 = (bf16[16,256,256]{2,1,0:T(8,128)(2,1)S(1)}, bf16[4,2,256,256]{3,2,1,0:T(8,128)(2,1)S(1)}, bf16[4,2,256,256]{3,2,1,0:T(8,128)(2,1)S(1)}) custom-call(s32[16]{0:T(128)S(1)} %bitcast.5, s32[2]{0:T(128)S(1)} %pad_add_fusion.refs_1_.refs_0_, bf16[1,2,16,128,512]{4,3,2,1,0:T(8,128)(2,1)S(1)} %copy-done.1, ...), custom_call_target="tpu_custom_call" | custom-call | flops 1 | bytes 1 | tf_op jit(solution)/shard_map/leaf_forward/pallas_call | solution.py:29
  21.8 2.7 %collective-permute-start.6 = (bf16[2,256,256]{2,1,0:T(8,128)(2,1)S(1)}, bf16[2,256,256]{2,1,0:T(8,128)(2,1)S(1)}, u32[]{:S(2)}, u32[]{:S(2)}) collective-permute-start(bf16[2,256,256]{2,1,0:T(8,128)(2,1)S(1)} %get-tuple-element.46), channel_id=1, source_target_pairs={{0,4},{1,5},{2,6},{3,7},{4,0},{5,1},{6,2},{7,3},{8,12},{9,13},{10,... | collective-permute-start | bytes 786440 | tf_op jit(solution)/shard_map/ppermute | solution.py:43
  24.4 1.4 %collective-permute-start.7 = (bf16[2,256,256]{2,1,0:T(8,128)(2,1)S(1)}, bf16[2,256,256]{2,1,0:T(8,128)(2,1)S(1)}, u32[]{:S(2)}, u32[]{:S(2)}) collective-permute-start(bf16[2,256,256]{2,1,0:T(8,128)(2,1)S(1)} %get-tuple-element.47), channel_id=1, source_target_pairs={{0,6},{1,7},{2,4},{3,5},{4,2},{5,3},{6,0},{7,1},{8,14},{9,15},{10,... | collective-permute-start | bytes 786440 | tf_op jit(solution)/shard_map/ppermute | solution.py:43
  25.9 4.1 %collective-permute-start.13 = (f32[264,128]{1,0:T(8,128)S(1)}, f32[264,128]{1,0:T(8,128)S(1)}, u32[]{:S(2)}, u32[]{:S(2)}) collective-permute-start(f32[264,128]{1,0:T(8,128)S(1)} %get-tuple-element.52), channel_id=1, source_target_pairs={{0,24},{8,16},{16,8},{24,0},{1,25},{9,17},{17,9},{25,1},{2,26},{10... | collective-permute-start | bytes 405512 | tf_op jit(solution)/shard_map/ppermute | solution.py:43
  30.0 3.5 %leaf_fold.1.refs_2_.refs_3_ = bf16[16,128,512]{2,1,0:T(8,128)(2,1)S(1)} custom-call(bf16[1,16,2,128,128]{4,3,2,1,0:T(8,128)(2,1)S(1)} %copy-done.2, bf16[1,16,2,128,128]{4,3,2,1,0:T(8,128)(2,1)S(1)} %copy-done.3, s32[1,16,128]{2,1,0:T(8,128)S(1)} %copy-done.7, bf16[16,256,256]{2,1,0:T(8,128)(2,1)S(1)} %get-tuple-element.40.refs_3_.refs_2_), custom_call_target="tpu_custom_call" | custom-call | flops 1 | bytes 1 | tf_op jit(solution)/shard_map/leaf_fold/pallas_call | solution.py:29
  33.7 0.7 collective-permute-done.13.refs_8_
  34.5 1.8 %collective-permute-start.3 = (bf16[2,256,256]{2,1,0:T(8,128)(2,1)S(1)}, bf16[2,256,256]{2,1,0:T(8,128)(2,1)S(1)}, u32[]{:S(2)}, u32[]{:S(2)}) collective-permute-start(bf16[2,256,256]{2,1,0:T(8,128)(2,1)S(1)} %get-tuple-element.44), channel_id=1, source_target_pairs={{0,4},{1,5},{2,6},{3,7},{4,0},{5,1},{6,2},{7,3},{8,12},{9,13},{10,... | collective-permute-start | bytes 786440 | tf_op jit(solution)/shard_map/ppermute | solution.py:43
  36.3 1.0 collective-permute-done.6.refs_5_
  37.2 2.9 %collective-permute-start.4 = (bf16[2,256,256]{2,1,0:T(8,128)(2,1)S(1)}, bf16[2,256,256]{2,1,0:T(8,128)(2,1)S(1)}, u32[]{:S(2)}, u32[]{:S(2)}) collective-permute-start(bf16[2,256,256]{2,1,0:T(8,128)(2,1)S(1)} %get-tuple-element.45), channel_id=1, source_target_pairs={{0,6},{1,7},{2,4},{3,5},{4,2},{5,3},{6,0},{7,1},{8,14},{9,15},{10,... | collective-permute-start | bytes 786440 | tf_op jit(solution)/shard_map/ppermute | solution.py:43
  40.7 2.6 %collective-permute-start.12 = (f32[264,128]{1,0:T(8,128)S(1)}, f32[264,128]{1,0:T(8,128)S(1)}, u32[]{:S(2)}, u32[]{:S(2)}) collective-permute-start(f32[264,128]{1,0:T(8,128)S(1)} %get-tuple-element.39.refs_6_.refs_5_), channel_id=1, source_target_pairs={{0,16},{8,24},{16,0},{24,8},{1,17},{9,25},{17,1},{25,9},{2,18},{10... | collective-permute-start | bytes 405512 | tf_op jit(solution)/shard_map/ppermute | solution.py:43
  43.2 0.9 interface_reduce.2
  44.2 1.6 %collective-permute-start.8 = (bf16[2,128,128]{2,1,0:T(8,128)(2,1)S(1)}, bf16[2,128,128]{2,1,0:T(8,128)(2,1)S(1)}, u32[]{:S(2)}, u32[]{:S(2)}) collective-permute-start(bf16[2,128,128]{2,1,0:T(8,128)(2,1)S(1)} %get-tuple-element.49), channel_id=1, source_target_pairs={{0,8},{8,0},{16,24},{24,16},{1,9},{9,1},{17,25},{25,17},{2,10},{10... | collective-permute-start | bytes 196616 | tf_op jit(solution)/shard_map/ppermute | solution.py:43
  45.8 2.6 %collective-permute-done.12.refs_7_ = f32[264,128]{1,0:T(8,128)S(1)} collective-permute-done((f32[264,128]{1,0:T(8,128)S(1)}, f32[264,128]{1,0:T(8,128)S(1)}, u32[]{:S(2)}, u32[]{:S(2)}) %collective-permute-start.12) | collective-permute-done | bytes 135200 | tf_op jit(solution)/shard_map/ppermute | solution.py:43
  48.5 1.3 %collective-permute-start.9 = (bf16[2,128,128]{2,1,0:T(8,128)(2,1)S(1)}, bf16[2,128,128]{2,1,0:T(8,128)(2,1)S(1)}, u32[]{:S(2)}, u32[]{:S(2)}) collective-permute-start(bf16[2,128,128]{2,1,0:T(8,128)(2,1)S(1)} %get-tuple-element.50), channel_id=1, source_target_pairs={{0,16},{8,24},{16,0},{24,8},{1,17},{9,25},{17,1},{25,9},{2,18},{10... | collective-permute-start | bytes 196616 | tf_op jit(solution)/shard_map/ppermute | solution.py:43
  49.8 2.8 %collective-permute-start.10 = (bf16[2,128,128]{2,1,0:T(8,128)(2,1)S(1)}, bf16[2,128,128]{2,1,0:T(8,128)(2,1)S(1)}, u32[]{:S(2)}, u32[]{:S(2)}) collective-permute-start(bf16[2,128,128]{2,1,0:T(8,128)(2,1)S(1)} %get-tuple-element.51), channel_id=1, source_target_pairs={{0,24},{8,16},{16,8},{24,0},{1,25},{9,17},{17,9},{25,1},{2,26},{10... | collective-permute-start | bytes 196616 | tf_op jit(solution)/shard_map/ppermute | solution.py:43
  52.6 2.5 %collective-permute-done.9.refs_3_ = bf16[2,128,128]{2,1,0:T(8,128)(2,1)S(1)} collective-permute-done((bf16[2,128,128]{2,1,0:T(8,128)(2,1)S(1)}, bf16[2,128,128]{2,1,0:T(8,128)(2,1)S(1)}, u32[]{:S(2)}, u32[]{:S(2)}) %collective-permute-start.9) | collective-permute-done | bytes 65568 | tf_op jit(solution)/shard_map/ppermute | solution.py:43
  55.1 0.8 collective-permute-done.10.refs_4_
  55.9 3.3 %sweep_chain.2 = (bf16[2,128,128]{2,1,0:T(8,128)(2,1)S(1)}, bf16[2,128,128]{2,1,0:T(8,128)(2,1)S(1)}, bf16[2,128,128]{2,1,0:T(8,128)(2,1)S(1)}, bf16[2,128,128]{2,1,0:T(8,128)(2,1)S(1)}) custom-call(s32[2]{0:T(128)S(1)} %pad_add_fusion.refs_1_.refs_0_, bf16[2,128,128]{2,1,0:T(8,128)(2,1)S(1)} %get-tuple-element.48.refs_1_, ...), custom_call_target="tpu_custom_call" | custom-call | flops 1 | bytes 1 | tf_op jit(solution)/shard_map/sweep_chain/pallas_call | solution.py:29
  59.1 1.6 %collective-permute-start.17 = (bf16[2,128,128]{2,1,0:T(8,128)(2,1)S(1)}, bf16[2,128,128]{2,1,0:T(8,128)(2,1)S(1)}, u32[]{:S(2)}, u32[]{:S(2)}) collective-permute-start(bf16[2,128,128]{2,1,0:T(8,128)(2,1)S(1)} %get-tuple-element.58), channel_id=1, source_target_pairs={{0,8},{8,0},{16,24},{24,16},{1,9},{9,1},{17,25},{25,17},{2,10},{10... | collective-permute-start | bytes 196616 | tf_op jit(solution)/shard_map/ppermute | solution.py:43
  60.8 1.9 %collective-permute-start.18 = (bf16[2,128,128]{2,1,0:T(8,128)(2,1)S(1)}, bf16[2,128,128]{2,1,0:T(8,128)(2,1)S(1)}, u32[]{:S(2)}, u32[]{:S(2)}) collective-permute-start(bf16[2,128,128]{2,1,0:T(8,128)(2,1)S(1)} %get-tuple-element.59), channel_id=1, source_target_pairs={{0,16},{8,24},{16,0},{24,8},{1,17},{9,25},{17,1},{25,9},{2,18},{10... | collective-permute-start | bytes 196616 | tf_op jit(solution)/shard_map/ppermute | solution.py:43
  62.7 0.9 collective-permute-start.19
  63.6 0.9 interface_reduce.3
  64.5 0.7 collective-permute-start.14
  65.3 2.8 %collective-permute-start.15 = (bf16[2,128,128]{2,1,0:T(8,128)(2,1)S(1)}, bf16[2,128,128]{2,1,0:T(8,128)(2,1)S(1)}, u32[]{:S(2)}, u32[]{:S(2)}) collective-permute-start(bf16[2,128,128]{2,1,0:T(8,128)(2,1)S(1)} %get-tuple-element.56), channel_id=1, source_target_pairs={{0,16},{8,24},{16,0},{24,8},{1,17},{9,25},{17,1},{25,9},{2,18},{10... | collective-permute-start | bytes 196616 | tf_op jit(solution)/shard_map/ppermute | solution.py:43
  68.1 0.9 collective-permute-start.16
  69.0 1.5 %interface_collect.2 = (bf16[2,256,256]{2,1,0:T(8,128)(2,1)S(1)}, f32[1,2,256,512]{3,2,1,0:T(8,128)}) custom-call(s32[2]{0:T(128)S(1)} %pad_add_fusion.refs_1_.refs_0_, bf16[2,128,128]{2,1,0:T(8,128)(2,1)S(1)} %get-tuple-element.53.refs_7_.refs_1_, bf16[2,128,128]{2,1,0:T(8,128)(2,1)S(1)} %collective-permute-done.17.refs_2_, ...), custom_call_target="tpu_custom_call" | custom-call | flops 1 | bytes 1 | tf_op jit(solution)/shard_map/interface_collect/pallas_call | solution.py:29
  70.6 1.5 %collective-permute-start.35 = (bf16[2,256,256]{2,1,0:T(8,128)(2,1)S(1)}, bf16[2,256,256]{2,1,0:T(8,128)(2,1)S(1)}, u32[]{:S(2)}, u32[]{:S(2)}) collective-permute-start(bf16[2,256,256]{2,1,0:T(8,128)(2,1)S(1)} %get-tuple-element.61.refs_9_.refs_4_), channel_id=1, source_target_pairs={{0,6},{1,7},{2,4},{3,5},{4,2},{5,3},{6,0},{7,1},{8,14},{9,15},{10,... | collective-permute-start | bytes 786440 | tf_op jit(solution)/shard_map/ppermute | solution.py:43
  72.1 1.5 %collective-permute-start.33 = (bf16[2,256,256]{2,1,0:T(8,128)(2,1)S(1)}, bf16[2,256,256]{2,1,0:T(8,128)(2,1)S(1)}, u32[]{:S(2)}, u32[]{:S(2)}) collective-permute-start(bf16[2,256,256]{2,1,0:T(8,128)(2,1)S(1)} %get-tuple-element.61.refs_9_.refs_4_), channel_id=1, source_target_pairs={{0,4},{1,5},{2,6},{3,7},{4,0},{5,1},{6,2},{7,3},{8,12},{9,13},{10,... | collective-permute-start | bytes 786440 | tf_op jit(solution)/shard_map/ppermute | solution.py:43
  74.1 3.5 %sweep_chain.3 = (bf16[2,128,128]{2,1,0:T(8,128)(2,1)S(1)}, bf16[2,128,128]{2,1,0:T(8,128)(2,1)S(1)}, bf16[2,128,128]{2,1,0:T(8,128)(2,1)S(1)}, bf16[2,128,128]{2,1,0:T(8,128)(2,1)S(1)}) custom-call(s32[2]{0:T(128)S(1)} %pad_add_fusion.refs_1_.refs_0_, bf16[2,128,128]{2,1,0:T(8,128)(2,1)S(1)} %get-tuple-element.54.refs_5_.refs_1_, ...), custom_call_target="tpu_custom_call" | custom-call | flops 1 | bytes 1 | tf_op jit(solution)/shard_map/sweep_chain/pallas_call | solution.py:29
  77.6 2.2 %collective-permute-start.20 = (bf16[2,128,128]{2,1,0:T(8,128)(2,1)S(1)}, bf16[2,128,128]{2,1,0:T(8,128)(2,1)S(1)}, u32[]{:S(2)}, u32[]{:S(2)}) collective-permute-start(bf16[2,128,128]{2,1,0:T(8,128)(2,1)S(1)} %get-tuple-element.63), channel_id=1, source_target_pairs={{0,8},{8,0},{16,24},{24,16},{1,9},{9,1},{17,25},{25,17},{2,10},{10... | collective-permute-start | bytes 196616 | tf_op jit(solution)/shard_map/ppermute | solution.py:43
  79.8 2.8 %collective-permute-done.20.refs_2_ = bf16[2,128,128]{2,1,0:T(8,128)(2,1)S(1)} collective-permute-done((bf16[2,128,128]{2,1,0:T(8,128)(2,1)S(1)}, bf16[2,128,128]{2,1,0:T(8,128)(2,1)S(1)}, u32[]{:S(2)}, u32[]{:S(2)}) %collective-permute-start.20) | collective-permute-done | bytes 65568 | tf_op jit(solution)/shard_map/ppermute | solution.py:43
  82.5 2.6 %collective-permute-start.21 = (bf16[2,128,128]{2,1,0:T(8,128)(2,1)S(1)}, bf16[2,128,128]{2,1,0:T(8,128)(2,1)S(1)}, u32[]{:S(2)}, u32[]{:S(2)}) collective-permute-start(bf16[2,128,128]{2,1,0:T(8,128)(2,1)S(1)} %get-tuple-element.64), channel_id=1, source_target_pairs={{0,16},{8,24},{16,0},{24,8},{1,17},{9,25},{17,1},{25,9},{2,18},{10... | collective-permute-start | bytes 196616 | tf_op jit(solution)/shard_map/ppermute | solution.py:43
  85.2 3.9 %collective-permute-done.21.refs_3_ = bf16[2,128,128]{2,1,0:T(8,128)(2,1)S(1)} collective-permute-done((bf16[2,128,128]{2,1,0:T(8,128)(2,1)S(1)}, bf16[2,128,128]{2,1,0:T(8,128)(2,1)S(1)}, u32[]{:S(2)}, u32[]{:S(2)}) %collective-permute-start.21) | collective-permute-done | bytes 65568 | tf_op jit(solution)/shard_map/ppermute | solution.py:43
  89.0 2.4 %collective-permute-start.22 = (bf16[2,128,128]{2,1,0:T(8,128)(2,1)S(1)}, bf16[2,128,128]{2,1,0:T(8,128)(2,1)S(1)}, u32[]{:S(2)}, u32[]{:S(2)}) collective-permute-start(bf16[2,128,128]{2,1,0:T(8,128)(2,1)S(1)} %get-tuple-element.65), channel_id=1, source_target_pairs={{0,24},{8,16},{16,8},{24,0},{1,25},{9,17},{17,9},{25,1},{2,26},{10... | collective-permute-start | bytes 196616 | tf_op jit(solution)/shard_map/ppermute | solution.py:43
  91.4 3.7 %collective-permute-done.22.refs_4_ = bf16[2,128,128]{2,1,0:T(8,128)(2,1)S(1)} collective-permute-done((bf16[2,128,128]{2,1,0:T(8,128)(2,1)S(1)}, bf16[2,128,128]{2,1,0:T(8,128)(2,1)S(1)}, u32[]{:S(2)}, u32[]{:S(2)}) %collective-permute-start.22) | collective-permute-done | bytes 65568 | tf_op jit(solution)/shard_map/ppermute | solution.py:43
  95.1 1.5 %interface_collect.3 = (bf16[2,256,256]{2,1,0:T(8,128)(2,1)S(1)}, f32[1,2,256,512]{3,2,1,0:T(8,128)}) custom-call(s32[2]{0:T(128)S(1)} %pad_add_fusion.refs_1_.refs_0_, bf16[2,128,128]{2,1,0:T(8,128)(2,1)S(1)} %get-tuple-element.62.refs_1_, bf16[2,128,128]{2,1,0:T(8,128)(2,1)S(1)} %collective-permute-done.20.refs_2_, ...), custom_call_target="tpu_custom_call", output_to_operand_aliasing={{1}: (5, {})} | custom-call | flops 1 | bytes 1 | tf_op jit(solution)/shard_map/interface_collect/pallas_call | solution.py:29
  96.6 1.5 %collective-permute-start.28 = (bf16[2,256,256]{2,1,0:T(8,128)(2,1)S(1)}, bf16[2,256,256]{2,1,0:T(8,128)(2,1)S(1)}, u32[]{:S(2)}, u32[]{:S(2)}) collective-permute-start(bf16[2,256,256]{2,1,0:T(8,128)(2,1)S(1)} %get-tuple-element.67.refs_12_.refs_4_), channel_id=1, source_target_pairs={{0,6},{1,7},{2,4},{3,5},{4,2},{5,3},{6,0},{7,1},{8,14},{9,15},{10,... | collective-permute-start | bytes 786440 | tf_op jit(solution)/shard_map/ppermute | solution.py:43
  98.2 1.5 %collective-permute-start.26 = (bf16[2,256,256]{2,1,0:T(8,128)(2,1)S(1)}, bf16[2,256,256]{2,1,0:T(8,128)(2,1)S(1)}, u32[]{:S(2)}, u32[]{:S(2)}) collective-permute-start(bf16[2,256,256]{2,1,0:T(8,128)(2,1)S(1)} %get-tuple-element.67.refs_12_.refs_4_), channel_id=1, source_target_pairs={{0,4},{1,5},{2,6},{3,7},{4,0},{5,1},{6,2},{7,3},{8,12},{9,13},{10,... | collective-permute-start | bytes 786440 | tf_op jit(solution)/shard_map/ppermute | solution.py:43
  100.7 4.3 %collective-permute-done.28.refs_10_ = bf16[2,256,256]{2,1,0:T(8,128)(2,1)S(1)} collective-permute-done((bf16[2,256,256]{2,1,0:T(8,128)(2,1)S(1)}, bf16[2,256,256]{2,1,0:T(8,128)(2,1)S(1)}, u32[]{:S(2)}, u32[]{:S(2)}) %collective-permute-start.28) | collective-permute-done | bytes 262176 | tf_op jit(solution)/shard_map/ppermute | solution.py:43
  105.1 2.7 %collective-permute-done.26.refs_8_ = bf16[2,256,256]{2,1,0:T(8,128)(2,1)S(1)} collective-permute-done((bf16[2,256,256]{2,1,0:T(8,128)(2,1)S(1)}, bf16[2,256,256]{2,1,0:T(8,128)(2,1)S(1)}, u32[]{:S(2)}, u32[]{:S(2)}) %collective-permute-start.26) | collective-permute-done | bytes 262176 | tf_op jit(solution)/shard_map/ppermute | solution.py:43
  109.3 5.2 %leaf_backward.2.refs_12_ = bf16[1,2,16,128,512]{4,3,2,1,0:T(8,128)(2,1)} custom-call(s32[16]{0:T(128)S(1)} %bitcast.6, s32[2]{0:T(128)S(1)} %pad_add_fusion.refs_1_.refs_0_, bf16[16,256,256]{2,1,0:T(8,128)(2,1)S(1)} %get-tuple-element.68.refs_2_, bf16[16,128,512]{2,1,0:T(8,128)(2,1)S(1)} %leaf_fold.1.refs_2_.refs_3_, ...), custom_call_target="tpu_custom_call" | custom-call | flops 1 | bytes 1 | tf_op jit(solution)/shard_map/leaf_backward/pallas_call | solution.py:29
  114.6 5.3 %leaf_backward.3 = bf16[1,2,16,128,512]{4,3,2,1,0:T(8,128)(2,1)} custom-call(s32[16]{0:T(128)S(1)} %bitcast.7, s32[2]{0:T(128)S(1)} %pad_add_fusion.refs_1_.refs_0_, bf16[16,256,256]{2,1,0:T(8,128)(2,1)S(1)} %get-tuple-element.40.refs_3_.refs_2_, bf16[16,128,512]{2,1,0:T(8,128)(2,1)S(1)} %leaf_fold.1.refs_2_.refs_3_, ...), custom_call_target="tpu_custom_call", output_to_operand_aliasing={{}: (12, {})} | custom-call | flops 1 | bytes 1 | tf_op jit(solution)/shard_map/leaf_backward/pallas_call | solution.py:29
  (61 shorter events, 6.6 us)
Async XLA Ops:
  0.7 2.2 %copy-start = (bf16[1,2,16,128,512]{4,3,2,1,0:T(8,128)(2,1)S(1)}, bf16[1,2,16,128,512]{4,3,2,1,0:T(8,128)(2,1)}, u32[]{:S(2)}) copy-start(bf16[1,2,16,128,512]{4,3,2,1,0:T(8,128)(2,1)} %refs_2_.4) | copy-start | bytes 12582916
  2.9 1.2 %copy-start.2 = (bf16[1,16,2,128,128]{4,3,2,1,0:T(8,128)(2,1)S(1)}, bf16[1,16,2,128,128]{4,3,2,1,0:T(8,128)(2,1)}, u32[]{:S(2)}) copy-start(bf16[1,16,2,128,128]{4,3,2,1,0:T(8,128)(2,1)} %refs_0_.1) | copy-start | bytes 3145732
  4.1 1.2 %copy-start.3 = (bf16[1,16,2,128,128]{4,3,2,1,0:T(8,128)(2,1)S(1)}, bf16[1,16,2,128,128]{4,3,2,1,0:T(8,128)(2,1)}, u32[]{:S(2)}) copy-start(bf16[1,16,2,128,128]{4,3,2,1,0:T(8,128)(2,1)} %refs_1_.5) | copy-start | bytes 3145732
  5.3 0.7 copy-start.6
  6.0 0.7 copy-start.8
  6.7 8.3 %copy-start.5 = (f32[1,2,2,128,128]{4,3,2,1,0:T(8,128)S(1)}, f32[1,2,2,128,128]{4,3,2,1,0:T(8,128)}, u32[]{:S(2)}) copy-start(f32[1,2,2,128,128]{4,3,2,1,0:T(8,128)} %refs_1_.4) | copy-start | bytes 786436
  6.7 8.3 %copy-start.9 = (f32[1,256]{1,0:T(1,128)S(1)}, f32[1,256]{1,0:T(1,128)}, u32[]{:S(2)}) copy-start(f32[1,256]{1,0:T(1,128)} %param.15) | copy-start | bytes 3076
  6.7 9.3 %copy-start.1 = (bf16[1,2,16,128,512]{4,3,2,1,0:T(8,128)(2,1)S(1)}, bf16[1,2,16,128,512]{4,3,2,1,0:T(8,128)(2,1)}, u32[]{:S(2)}) copy-start(bf16[1,2,16,128,512]{4,3,2,1,0:T(8,128)(2,1)} %refs_2_.4) | copy-start | bytes 12582916
  6.7 9.3 %copy-start.7 = (s32[1,16,128]{2,1,0:T(8,128)S(1)}, s32[1,16,128]{2,1,0:T(8,128)}, u32[]{:S(2)}) copy-start(s32[1,16,128]{2,1,0:T(8,128)} %refs_2_.5) | copy-start | bytes 24580
  12.0 2.8 %collective-permute-start = (bf16[4,2,256,256]{3,2,1,0:T(8,128)(2,1)S(1)}, bf16[4,2,256,256]{3,2,1,0:T(8,128)(2,1)S(1)}, u32[]{:S(2)}, u32[]{:S(2)}) collective-permute-start(bf16[4,2,256,256]{3,2,1,0:T(8,128)(2,1)S(1)} %get-tuple-element.37), channel_id=1, source_target_pairs={{0,1},{1,0},{2,3},{3,2},{4,5},{5,4},{6,7},{7,6},{8,9},{9,8},{10,11... | collective-permute-start | bytes 3145736 | tf_op jit(solution)/shard_map/ppermute | solution.py:43
  21.3 8.7 %collective-permute-start.1 = (bf16[4,2,256,256]{3,2,1,0:T(8,128)(2,1)S(1)}, bf16[4,2,256,256]{3,2,1,0:T(8,128)(2,1)S(1)}, u32[]{:S(2)}, u32[]{:S(2)}) collective-permute-start(bf16[4,2,256,256]{3,2,1,0:T(8,128)(2,1)S(1)} %get-tuple-element.42), channel_id=1, source_target_pairs={{0,1},{1,0},{2,3},{3,2},{4,5},{5,4},{6,7},{7,6},{8,9},{9,8},{10,11... | collective-permute-start | bytes 3145736 | tf_op jit(solution)/shard_map/ppermute | solution.py:43
  21.8 15.4 %collective-permute-start.6 = (bf16[2,256,256]{2,1,0:T(8,128)(2,1)S(1)}, bf16[2,256,256]{2,1,0:T(8,128)(2,1)S(1)}, u32[]{:S(2)}, u32[]{:S(2)}) collective-permute-start(bf16[2,256,256]{2,1,0:T(8,128)(2,1)S(1)} %get-tuple-element.46), channel_id=1, source_target_pairs={{0,4},{1,5},{2,6},{3,7},{4,0},{5,1},{6,2},{7,3},{8,12},{9,13},{10,... | collective-permute-start | bytes 786440 | tf_op jit(solution)/shard_map/ppermute | solution.py:43
  24.4 15.7 %collective-permute-start.7 = (bf16[2,256,256]{2,1,0:T(8,128)(2,1)S(1)}, bf16[2,256,256]{2,1,0:T(8,128)(2,1)S(1)}, u32[]{:S(2)}, u32[]{:S(2)}) collective-permute-start(bf16[2,256,256]{2,1,0:T(8,128)(2,1)S(1)} %get-tuple-element.47), channel_id=1, source_target_pairs={{0,6},{1,7},{2,4},{3,5},{4,2},{5,3},{6,0},{7,1},{8,14},{9,15},{10,... | collective-permute-start | bytes 786440 | tf_op jit(solution)/shard_map/ppermute | solution.py:43
  25.9 14.8 %collective-permute-start.5 = (bf16[2,256,256]{2,1,0:T(8,128)(2,1)S(1)}, bf16[2,256,256]{2,1,0:T(8,128)(2,1)S(1)}, u32[]{:S(2)}, u32[]{:S(2)}) collective-permute-start(bf16[2,256,256]{2,1,0:T(8,128)(2,1)S(1)} %get-tuple-element.38.refs_3_), channel_id=1, source_target_pairs={{0,2},{1,3},{2,0},{3,1},{4,6},{5,7},{6,4},{7,5},{8,10},{9,11},{10,... | collective-permute-start | bytes 786440 | tf_op jit(solution)/shard_map/ppermute | solution.py:43
  25.9 8.5 %collective-permute-start.13 = (f32[264,128]{1,0:T(8,128)S(1)}, f32[264,128]{1,0:T(8,128)S(1)}, u32[]{:S(2)}, u32[]{:S(2)}) collective-permute-start(f32[264,128]{1,0:T(8,128)S(1)} %get-tuple-element.52), channel_id=1, source_target_pairs={{0,24},{8,16},{16,8},{24,0},{1,25},{9,17},{17,9},{25,1},{2,26},{10... | collective-permute-start | bytes 405512 | tf_op jit(solution)/shard_map/ppermute | solution.py:43
  30.0 14.2 %collective-permute-start.11 = (f32[264,128]{1,0:T(8,128)S(1)}, f32[264,128]{1,0:T(8,128)S(1)}, u32[]{:S(2)}, u32[]{:S(2)}) collective-permute-start(f32[264,128]{1,0:T(8,128)S(1)} %get-tuple-element.52), channel_id=1, source_target_pairs={{0,8},{8,0},{16,24},{24,16},{1,9},{9,1},{17,25},{25,17},{2,10},{10... | collective-permute-start | bytes 405512 | tf_op jit(solution)/shard_map/ppermute | solution.py:43
  30.0 13.2 %copy-start.4 = (bf16[1,2,256,512]{3,2,1,0:T(8,128)(2,1)S(1)}, bf16[1,2,256,512]{3,2,1,0:T(8,128)(2,1)}, u32[]{:S(2)}) copy-start(bf16[1,2,256,512]{3,2,1,0:T(8,128)(2,1)} %refs_1_.7) | copy-start | bytes 1572868
  34.5 28.2 %collective-permute-start.3 = (bf16[2,256,256]{2,1,0:T(8,128)(2,1)S(1)}, bf16[2,256,256]{2,1,0:T(8,128)(2,1)S(1)}, u32[]{:S(2)}, u32[]{:S(2)}) collective-permute-start(bf16[2,256,256]{2,1,0:T(8,128)(2,1)S(1)} %get-tuple-element.44), channel_id=1, source_target_pairs={{0,4},{1,5},{2,6},{3,7},{4,0},{5,1},{6,2},{7,3},{8,12},{9,13},{10,... | collective-permute-start | bytes 786440 | tf_op jit(solution)/shard_map/ppermute | solution.py:43
  37.2 26.4 %collective-permute-start.4 = (bf16[2,256,256]{2,1,0:T(8,128)(2,1)S(1)}, bf16[2,256,256]{2,1,0:T(8,128)(2,1)S(1)}, u32[]{:S(2)}, u32[]{:S(2)}) collective-permute-start(bf16[2,256,256]{2,1,0:T(8,128)(2,1)S(1)} %get-tuple-element.45), channel_id=1, source_target_pairs={{0,6},{1,7},{2,4},{3,5},{4,2},{5,3},{6,0},{7,1},{8,14},{9,15},{10,... | collective-permute-start | bytes 786440 | tf_op jit(solution)/shard_map/ppermute | solution.py:43
  40.1 23.5 %collective-permute-start.2 = (bf16[2,256,256]{2,1,0:T(8,128)(2,1)S(1)}, bf16[2,256,256]{2,1,0:T(8,128)(2,1)S(1)}, u32[]{:S(2)}, u32[]{:S(2)}) collective-permute-start(bf16[2,256,256]{2,1,0:T(8,128)(2,1)S(1)} %get-tuple-element.43.refs_7_), channel_id=1, source_target_pairs={{0,2},{1,3},{2,0},{3,1},{4,6},{5,7},{6,4},{7,5},{8,10},{9,11},{10,... | collective-permute-start | bytes 786440 | tf_op jit(solution)/shard_map/ppermute | solution.py:43
  40.7 7.8 %collective-permute-start.12 = (f32[264,128]{1,0:T(8,128)S(1)}, f32[264,128]{1,0:T(8,128)S(1)}, u32[]{:S(2)}, u32[]{:S(2)}) collective-permute-start(f32[264,128]{1,0:T(8,128)S(1)} %get-tuple-element.39.refs_6_.refs_5_), channel_id=1, source_target_pairs={{0,16},{8,24},{16,0},{24,8},{1,17},{9,25},{17,1},{25,9},{2,18},{10... | collective-permute-start | bytes 405512 | tf_op jit(solution)/shard_map/ppermute | solution.py:43
  44.2 5.6 %collective-permute-start.8 = (bf16[2,128,128]{2,1,0:T(8,128)(2,1)S(1)}, bf16[2,128,128]{2,1,0:T(8,128)(2,1)S(1)}, u32[]{:S(2)}, u32[]{:S(2)}) collective-permute-start(bf16[2,128,128]{2,1,0:T(8,128)(2,1)S(1)} %get-tuple-element.49), channel_id=1, source_target_pairs={{0,8},{8,0},{16,24},{24,16},{1,9},{9,1},{17,25},{25,17},{2,10},{10... | collective-permute-start | bytes 196616 | tf_op jit(solution)/shard_map/ppermute | solution.py:43
  48.5 6.6 %collective-permute-start.9 = (bf16[2,128,128]{2,1,0:T(8,128)(2,1)S(1)}, bf16[2,128,128]{2,1,0:T(8,128)(2,1)S(1)}, u32[]{:S(2)}, u32[]{:S(2)}) collective-permute-start(bf16[2,128,128]{2,1,0:T(8,128)(2,1)S(1)} %get-tuple-element.50), channel_id=1, source_target_pairs={{0,16},{8,24},{16,0},{24,8},{1,17},{9,25},{17,1},{25,9},{2,18},{10... | collective-permute-start | bytes 196616 | tf_op jit(solution)/shard_map/ppermute | solution.py:43
  49.8 6.1 %collective-permute-start.10 = (bf16[2,128,128]{2,1,0:T(8,128)(2,1)S(1)}, bf16[2,128,128]{2,1,0:T(8,128)(2,1)S(1)}, u32[]{:S(2)}, u32[]{:S(2)}) collective-permute-start(bf16[2,128,128]{2,1,0:T(8,128)(2,1)S(1)} %get-tuple-element.51), channel_id=1, source_target_pairs={{0,24},{8,16},{16,8},{24,0},{1,25},{9,17},{17,9},{25,1},{2,26},{10... | collective-permute-start | bytes 196616 | tf_op jit(solution)/shard_map/ppermute | solution.py:43
  59.1 8.9 %collective-permute-start.17 = (bf16[2,128,128]{2,1,0:T(8,128)(2,1)S(1)}, bf16[2,128,128]{2,1,0:T(8,128)(2,1)S(1)}, u32[]{:S(2)}, u32[]{:S(2)}) collective-permute-start(bf16[2,128,128]{2,1,0:T(8,128)(2,1)S(1)} %get-tuple-element.58), channel_id=1, source_target_pairs={{0,8},{8,0},{16,24},{24,16},{1,9},{9,1},{17,25},{25,17},{2,10},{10... | collective-permute-start | bytes 196616 | tf_op jit(solution)/shard_map/ppermute | solution.py:43
  60.8 8.2 %collective-permute-start.18 = (bf16[2,128,128]{2,1,0:T(8,128)(2,1)S(1)}, bf16[2,128,128]{2,1,0:T(8,128)(2,1)S(1)}, u32[]{:S(2)}, u32[]{:S(2)}) collective-permute-start(bf16[2,128,128]{2,1,0:T(8,128)(2,1)S(1)} %get-tuple-element.59), channel_id=1, source_target_pairs={{0,16},{8,24},{16,0},{24,8},{1,17},{9,25},{17,1},{25,9},{2,18},{10... | collective-permute-start | bytes 196616 | tf_op jit(solution)/shard_map/ppermute | solution.py:43
  62.7 6.3 %collective-permute-start.19 = (bf16[2,128,128]{2,1,0:T(8,128)(2,1)S(1)}, bf16[2,128,128]{2,1,0:T(8,128)(2,1)S(1)}, u32[]{:S(2)}, u32[]{:S(2)}) collective-permute-start(bf16[2,128,128]{2,1,0:T(8,128)(2,1)S(1)} %get-tuple-element.60), channel_id=1, source_target_pairs={{0,24},{8,16},{16,8},{24,0},{1,25},{9,17},{17,9},{25,1},{2,26},{10... | collective-permute-start | bytes 196616 | tf_op jit(solution)/shard_map/ppermute | solution.py:43
  64.5 9.0 %collective-permute-start.14 = (bf16[2,128,128]{2,1,0:T(8,128)(2,1)S(1)}, bf16[2,128,128]{2,1,0:T(8,128)(2,1)S(1)}, u32[]{:S(2)}, u32[]{:S(2)}) collective-permute-start(bf16[2,128,128]{2,1,0:T(8,128)(2,1)S(1)} %get-tuple-element.55), channel_id=1, source_target_pairs={{0,8},{8,0},{16,24},{24,16},{1,9},{9,1},{17,25},{25,17},{2,10},{10... | collective-permute-start | bytes 196616 | tf_op jit(solution)/shard_map/ppermute | solution.py:43
  65.3 8.9 %collective-permute-start.15 = (bf16[2,128,128]{2,1,0:T(8,128)(2,1)S(1)}, bf16[2,128,128]{2,1,0:T(8,128)(2,1)S(1)}, u32[]{:S(2)}, u32[]{:S(2)}) collective-permute-start(bf16[2,128,128]{2,1,0:T(8,128)(2,1)S(1)} %get-tuple-element.56), channel_id=1, source_target_pairs={{0,16},{8,24},{16,0},{24,8},{1,17},{9,25},{17,1},{25,9},{2,18},{10... | collective-permute-start | bytes 196616 | tf_op jit(solution)/shard_map/ppermute | solution.py:43
  68.1 6.1 %collective-permute-start.16 = (bf16[2,128,128]{2,1,0:T(8,128)(2,1)S(1)}, bf16[2,128,128]{2,1,0:T(8,128)(2,1)S(1)}, u32[]{:S(2)}, u32[]{:S(2)}) collective-permute-start(bf16[2,128,128]{2,1,0:T(8,128)(2,1)S(1)} %get-tuple-element.57), channel_id=1, source_target_pairs={{0,24},{8,16},{16,8},{24,0},{1,25},{9,17},{17,9},{25,1},{2,26},{10... | collective-permute-start | bytes 196616 | tf_op jit(solution)/shard_map/ppermute | solution.py:43
  70.6 27.6 %collective-permute-start.35 = (bf16[2,256,256]{2,1,0:T(8,128)(2,1)S(1)}, bf16[2,256,256]{2,1,0:T(8,128)(2,1)S(1)}, u32[]{:S(2)}, u32[]{:S(2)}) collective-permute-start(bf16[2,256,256]{2,1,0:T(8,128)(2,1)S(1)} %get-tuple-element.61.refs_9_.refs_4_), channel_id=1, source_target_pairs={{0,6},{1,7},{2,4},{3,5},{4,2},{5,3},{6,0},{7,1},{8,14},{9,15},{10,... | collective-permute-start | bytes 786440 | tf_op jit(solution)/shard_map/ppermute | solution.py:43
  72.1 27.6 %collective-permute-start.33 = (bf16[2,256,256]{2,1,0:T(8,128)(2,1)S(1)}, bf16[2,256,256]{2,1,0:T(8,128)(2,1)S(1)}, u32[]{:S(2)}, u32[]{:S(2)}) collective-permute-start(bf16[2,256,256]{2,1,0:T(8,128)(2,1)S(1)} %get-tuple-element.61.refs_9_.refs_4_), channel_id=1, source_target_pairs={{0,4},{1,5},{2,6},{3,7},{4,0},{5,1},{6,2},{7,3},{8,12},{9,13},{10,... | collective-permute-start | bytes 786440 | tf_op jit(solution)/shard_map/ppermute | solution.py:43
  73.6 26.6 %collective-permute-start.31 = (bf16[2,256,256]{2,1,0:T(8,128)(2,1)S(1)}, bf16[2,256,256]{2,1,0:T(8,128)(2,1)S(1)}, u32[]{:S(2)}, u32[]{:S(2)}) collective-permute-start(bf16[2,256,256]{2,1,0:T(8,128)(2,1)S(1)} %get-tuple-element.61.refs_9_.refs_4_), channel_id=1, source_target_pairs={{0,2},{1,3},{2,0},{3,1},{4,6},{5,7},{6,4},{7,5},{8,10},{9,11},{10,... | collective-permute-start | bytes 786440 | tf_op jit(solution)/shard_map/ppermute | solution.py:43
  74.1 26.1 %collective-permute-start.30 = (bf16[2,256,256]{2,1,0:T(8,128)(2,1)S(1)}, bf16[2,256,256]{2,1,0:T(8,128)(2,1)S(1)}, u32[]{:S(2)}, u32[]{:S(2)}) collective-permute-start(bf16[2,256,256]{2,1,0:T(8,128)(2,1)S(1)} %get-tuple-element.61.refs_9_.refs_4_), channel_id=1, source_target_pairs={{0,1},{1,0},{2,3},{3,2},{4,5},{5,4},{6,7},{7,6},{8,9},{9,8},{10,11... | collective-permute-start | bytes 786440 | tf_op jit(solution)/shard_map/ppermute | solution.py:43
  77.6 4.9 %collective-permute-start.20 = (bf16[2,128,128]{2,1,0:T(8,128)(2,1)S(1)}, bf16[2,128,128]{2,1,0:T(8,128)(2,1)S(1)}, u32[]{:S(2)}, u32[]{:S(2)}) collective-permute-start(bf16[2,128,128]{2,1,0:T(8,128)(2,1)S(1)} %get-tuple-element.63), channel_id=1, source_target_pairs={{0,8},{8,0},{16,24},{24,16},{1,9},{9,1},{17,25},{25,17},{2,10},{10... | collective-permute-start | bytes 196616 | tf_op jit(solution)/shard_map/ppermute | solution.py:43
  82.5 6.5 %collective-permute-start.21 = (bf16[2,128,128]{2,1,0:T(8,128)(2,1)S(1)}, bf16[2,128,128]{2,1,0:T(8,128)(2,1)S(1)}, u32[]{:S(2)}, u32[]{:S(2)}) collective-permute-start(bf16[2,128,128]{2,1,0:T(8,128)(2,1)S(1)} %get-tuple-element.64), channel_id=1, source_target_pairs={{0,16},{8,24},{16,0},{24,8},{1,17},{9,25},{17,1},{25,9},{2,18},{10... | collective-permute-start | bytes 196616 | tf_op jit(solution)/shard_map/ppermute | solution.py:43
  89.0 6.1 %collective-permute-start.22 = (bf16[2,128,128]{2,1,0:T(8,128)(2,1)S(1)}, bf16[2,128,128]{2,1,0:T(8,128)(2,1)S(1)}, u32[]{:S(2)}, u32[]{:S(2)}) collective-permute-start(bf16[2,128,128]{2,1,0:T(8,128)(2,1)S(1)} %get-tuple-element.65), channel_id=1, source_target_pairs={{0,24},{8,16},{16,8},{24,0},{1,25},{9,17},{17,9},{25,1},{2,26},{10... | collective-permute-start | bytes 196616 | tf_op jit(solution)/shard_map/ppermute | solution.py:43
  96.6 8.4 %collective-permute-start.28 = (bf16[2,256,256]{2,1,0:T(8,128)(2,1)S(1)}, bf16[2,256,256]{2,1,0:T(8,128)(2,1)S(1)}, u32[]{:S(2)}, u32[]{:S(2)}) collective-permute-start(bf16[2,256,256]{2,1,0:T(8,128)(2,1)S(1)} %get-tuple-element.67.refs_12_.refs_4_), channel_id=1, source_target_pairs={{0,6},{1,7},{2,4},{3,5},{4,2},{5,3},{6,0},{7,1},{8,14},{9,15},{10,... | collective-permute-start | bytes 786440 | tf_op jit(solution)/shard_map/ppermute | solution.py:43
  98.2 9.6 %collective-permute-start.26 = (bf16[2,256,256]{2,1,0:T(8,128)(2,1)S(1)}, bf16[2,256,256]{2,1,0:T(8,128)(2,1)S(1)}, u32[]{:S(2)}, u32[]{:S(2)}) collective-permute-start(bf16[2,256,256]{2,1,0:T(8,128)(2,1)S(1)} %get-tuple-element.67.refs_12_.refs_4_), channel_id=1, source_target_pairs={{0,4},{1,5},{2,6},{3,7},{4,0},{5,1},{6,2},{7,3},{8,12},{9,13},{10,... | collective-permute-start | bytes 786440 | tf_op jit(solution)/shard_map/ppermute | solution.py:43
  99.7 8.1 %collective-permute-start.24 = (bf16[2,256,256]{2,1,0:T(8,128)(2,1)S(1)}, bf16[2,256,256]{2,1,0:T(8,128)(2,1)S(1)}, u32[]{:S(2)}, u32[]{:S(2)}) collective-permute-start(bf16[2,256,256]{2,1,0:T(8,128)(2,1)S(1)} %get-tuple-element.67.refs_12_.refs_4_), channel_id=1, source_target_pairs={{0,2},{1,3},{2,0},{3,1},{4,6},{5,7},{6,4},{7,5},{8,10},{9,11},{10,... | collective-permute-start | bytes 786440 | tf_op jit(solution)/shard_map/ppermute | solution.py:43
  100.2 8.0 %collective-permute-start.36 = (bf16[2,256,256]{2,1,0:T(8,128)(2,1)S(1)}, bf16[2,256,256]{2,1,0:T(8,128)(2,1)S(1)}, u32[]{:S(2)}, u32[]{:S(2)}) collective-permute-start(bf16[2,256,256]{2,1,0:T(8,128)(2,1)S(1)} %collective-permute-done.35.refs_10_), channel_id=1, source_target_pairs={{0,1},{1,0},{2,3},{3,2},{4,5},{5,4},{6,7},{7,6},{8,9},{9,8},{10,11... | collective-permute-start | bytes 786440 | tf_op jit(solution)/shard_map/ppermute | solution.py:43
  100.2 8.1 %collective-permute-start.34 = (bf16[2,256,256]{2,1,0:T(8,128)(2,1)S(1)}, bf16[2,256,256]{2,1,0:T(8,128)(2,1)S(1)}, u32[]{:S(2)}, u32[]{:S(2)}) collective-permute-start(bf16[2,256,256]{2,1,0:T(8,128)(2,1)S(1)} %collective-permute-done.33.refs_8_), channel_id=1, source_target_pairs={{0,1},{1,0},{2,3},{3,2},{4,5},{5,4},{6,7},{7,6},{8,9},{9,8},{10,11... | collective-permute-start | bytes 786440 | tf_op jit(solution)/shard_map/ppermute | solution.py:43
  105.1 9.5 %collective-permute-start.23 = (bf16[2,256,256]{2,1,0:T(8,128)(2,1)S(1)}, bf16[2,256,256]{2,1,0:T(8,128)(2,1)S(1)}, u32[]{:S(2)}, u32[]{:S(2)}) collective-permute-start(bf16[2,256,256]{2,1,0:T(8,128)(2,1)S(1)} %get-tuple-element.67.refs_12_.refs_4_), channel_id=1, source_target_pairs={{0,1},{1,0},{2,3},{3,2},{4,5},{5,4},{6,7},{7,6},{8,9},{9,8},{10,11... | collective-permute-start | bytes 786440 | tf_op jit(solution)/shard_map/ppermute | solution.py:43
  107.7 1.5 %collective-permute-start.32 = (bf16[2,256,256]{2,1,0:T(8,128)(2,1)S(1)}, bf16[2,256,256]{2,1,0:T(8,128)(2,1)S(1)}, u32[]{:S(2)}, u32[]{:S(2)}) collective-permute-start(bf16[2,256,256]{2,1,0:T(8,128)(2,1)S(1)} %collective-permute-done.31.refs_6_), channel_id=1, source_target_pairs={{0,1},{1,0},{2,3},{3,2},{4,5},{5,4},{6,7},{7,6},{8,9},{9,8},{10,11... | collective-permute-start | bytes 786440 | tf_op jit(solution)/shard_map/ppermute | solution.py:43
  107.7 6.8 %collective-permute-start.29 = (bf16[2,256,256]{2,1,0:T(8,128)(2,1)S(1)}, bf16[2,256,256]{2,1,0:T(8,128)(2,1)S(1)}, u32[]{:S(2)}, u32[]{:S(2)}) collective-permute-start(bf16[2,256,256]{2,1,0:T(8,128)(2,1)S(1)} %collective-permute-done.28.refs_10_), channel_id=1, source_target_pairs={{0,1},{1,0},{2,3},{3,2},{4,5},{5,4},{6,7},{7,6},{8,9},{9,8},{10,11... | collective-permute-start | bytes 786440 | tf_op jit(solution)/shard_map/ppermute | solution.py:43
  108.3 6.3 %collective-permute-start.27 = (bf16[2,256,256]{2,1,0:T(8,128)(2,1)S(1)}, bf16[2,256,256]{2,1,0:T(8,128)(2,1)S(1)}, u32[]{:S(2)}, u32[]{:S(2)}) collective-permute-start(bf16[2,256,256]{2,1,0:T(8,128)(2,1)S(1)} %collective-permute-done.26.refs_8_), channel_id=1, source_target_pairs={{0,1},{1,0},{2,3},{3,2},{4,5},{5,4},{6,7},{7,6},{8,9},{9,8},{10,11... | collective-permute-start | bytes 786440 | tf_op jit(solution)/shard_map/ppermute | solution.py:43
  108.3 6.2 %collective-permute-start.25 = (bf16[2,256,256]{2,1,0:T(8,128)(2,1)S(1)}, bf16[2,256,256]{2,1,0:T(8,128)(2,1)S(1)}, u32[]{:S(2)}, u32[]{:S(2)}) collective-permute-start(bf16[2,256,256]{2,1,0:T(8,128)(2,1)S(1)} %collective-permute-done.24.refs_6_), channel_id=1, source_target_pairs={{0,1},{1,0},{2,3},{3,2},{4,5},{5,4},{6,7},{7,6},{8,9},{9,8},{10,11... | collective-permute-start | bytes 786440 | tf_op jit(solution)/shard_map/ppermute | solution.py:43

commit v3 on v2

v3 whole, which is shorter than its diff:
```python
import functools

import jax
import jax.numpy as jnp
from jax import lax
from jax.experimental import pallas as pl
from jax.experimental.pallas import tpu as pltpu
from jax.sharding import PartitionSpec as P

HALVES = 2
BF = jnp.bfloat16
F32 = jnp.float32
VMEM = pl.BlockSpec(memory_space=pltpu.VMEM)
SMEM = pl.BlockSpec(memory_space=pltpu.SMEM)
HBM = pl.BlockSpec(memory_space=pltpu.HBM)
ANY = pl.BlockSpec(memory_space=pl.ANY)


def shape_of(shape, dtype=BF):
    return jax.ShapeDtypeStruct(shape, dtype)


def call(kernel, name, ins, in_specs, outs, out_specs, after=(), scratch=(), aliases=None, room=24):
    count, extra = len(ins), len(after)

    def wrapped(*refs):
        kernel(*refs[:count], *refs[count + extra :])

    return pl.pallas_call(
        wrapped,
        in_specs=list(in_specs) + [ANY] * extra,
        out_specs=out_specs,
        out_shape=outs,
        scratch_shapes=list(scratch),
        input_output_aliases=aliases or {},
        compiler_params=pltpu.CompilerParams(vmem_limit_bytes=room * 1024 * 1024),
        cost_estimate=pl.CostEstimate(flops=1, bytes_accessed=1, transcendentals=0),
        name=name,
    )(*ins, *after)


def crossed(x, axis, mask):
    return lax.ppermute(x, axis, [(i, i ^ mask) for i in range(lax.axis_size(axis))])


def stacked(real, imag):
    return jnp.concatenate(
        [jnp.concatenate([real, -imag], axis=1), jnp.concatenate([imag, real], axis=1)], axis=0
    )


def dot(a, b, dims=((1,), (0,)), precision=None):
    return lax.dot_general(a, b, (dims, ((), ())), precision=precision, preferred_element_type=F32)


def table_of(anc_row, rows):
    ids = lax.broadcasted_iota(jnp.int32, (rows, anc_row.shape[1]), 0)
    return (ids == anc_row).astype(F32).astype(BF)


def forward_kernel(h, group, cap, owners, place, rhs, inv, off, anc, fwd, keep, send,
                   vecs, invs, offs, ancs, part, ids, seen, sems):
    leaves, blk, cols = vecs.shape[1], vecs.shape[2], vecs.shape[3]
    fronts, rows, width = part.shape[0], keep.shape[3], keep.shape[4]
    me = place[1]
    small = pltpu.make_async_copy(anc.at[0], ancs, sems.at[leaves // group, 0])

    def copies(at):
        span = pl.ds(at * group, group)
        return (
            pltpu.make_async_copy(inv.at[0, span], invs.at[span], sems.at[at, 0]),
            pltpu.make_async_copy(rhs.at[0, :, span, :, pl.ds(h * cols, cols)], vecs.at[:, span], sems.at[at, 1]),
            pltpu.make_async_copy(off.at[0, span], offs.at[span], sems.at[at, 2]),
        )

    for at in range(leaves // group):
        for copy in copies(at):
            copy.start()
    small.start()
    ids[...] = jnp.full(ids.shape, -1, jnp.int32)
    for dist in range(fronts):
        seen[dist] = 0
    small.wait()

    def some(at, carry):
        for copy in copies(at):
            copy.wait()
        names = [at * group + j for j in range(group)]
        values = []
        for leaf in names:
            vec = jnp.concatenate([vecs[0, leaf], vecs[1, leaf]], axis=0)
            values.append(dot(stacked(invs[leaf, 0], invs[leaf, 1]), vec).astype(BF))
        moved = [dot(stacked(offs[leaf, 0], offs[leaf, 1]), value).astype(BF) for leaf, value in zip(names, values)]
        for leaf, value, shift in zip(names, values, moved):
            fwd[leaf] = value
            dist = owners[leaf] ^ me
            rank = seen[dist]
            seen[dist] = rank + 1
            part[dist, 0, rank] = shift[:blk]
            part[dist, 1, rank] = shift[blk:]
            ids[pl.ds(dist * cap + rank, 1), :] = ancs[pl.ds(leaf, 1), :]
        return carry

    lax.fori_loop(0, leaves // group, some, 0)
    for dist in range(fronts):
        for rank in range(cap):

            @pl.when(seen[dist] <= rank)
            def _(dist=dist, rank=rank):
                part[dist, 0, rank] = jnp.zeros((blk, cols), BF)
                part[dist, 1, rank] = jnp.zeros((blk, cols), BF)

    for dist in range(fronts):
        row = jnp.concatenate([ids[dist * cap + rank : dist * cap + rank + 1, :] for rank in range(cap)], axis=1)
        table = table_of(row, rows)
        out = send if dist % 2 else keep
        for plane in range(2):
            value = dot(table, part[dist, plane].reshape(cap * blk, cols)).astype(BF)
            for q in range(cols // width):
                out[dist // 2, q, plane] = value[:, q * width : (q + 1) * width]


def forward(h, owners, place, leaf_rhs, leaf_inv, leaf_off, ancestors, fronts, rows, part, after):
    _, _, leaves, blk, width = leaf_rhs.shape
    cols = width // HALVES
    cap = -(-leaves // fronts)
    group = 4
    block = shape_of((fronts // 2, cols // part, 2, rows, part))
    return call(
        functools.partial(forward_kernel, h, group, cap),
        "leaf_forward",
        [owners, place, leaf_rhs, leaf_inv, leaf_off, ancestors],
        [SMEM, SMEM, HBM, HBM, HBM, HBM],
        [shape_of((leaves, 2 * blk, cols)), block, block],
        [VMEM, VMEM, VMEM],
        after,
        [
            pltpu.VMEM((2, leaves, blk, cols), BF),
            pltpu.VMEM((leaves, 2, blk, blk), BF),
            pltpu.VMEM((leaves, 2, blk, blk), BF),
            pltpu.VMEM((leaves, blk), jnp.int32),
            pltpu.VMEM((fronts, 2, cap, blk, cols), BF),
            pltpu.VMEM((fronts * cap, blk), jnp.int32),
            pltpu.SMEM((fronts,), jnp.int32),
            pltpu.SemaphoreType.DMA((leaves // group + 1, 3)),
        ],
        room=50,
    )


def fold_kernel(inv, off, anc, out):
    leaves, _, blk, _ = inv.shape[1:]
    rows = out.shape[2] // 2

    def one(leaf, carry):
        mat = jnp.concatenate([inv[0, leaf, 0], inv[0, leaf, 1]], axis=1)
        real, imag = off[0, leaf, 0], off[0, leaf, 1]
        other = jnp.concatenate([jnp.concatenate([real, -imag], axis=1), jnp.concatenate([imag, real], axis=1)], axis=0)
        both = dot(mat, other, ((1,), (1,))).astype(BF)
        table = table_of(anc[0, pl.ds(leaf, 1), :], rows)
        real = dot(both[:, :blk], table, ((1,), (1,))).astype(BF)
        imag = dot(both[:, blk:], table, ((1,), (1,))).astype(BF)
        out[leaf, :blk, :rows] = real
        out[leaf, :blk, rows:] = -imag
        out[leaf, blk:, :rows] = imag
        out[leaf, blk:, rows:] = real
        return carry

    lax.fori_loop(0, leaves, one, 0, unroll=2)


def fold(leaf_inv, leaf_off, ancestors, rows, after):
    _, leaves, _, blk, _ = leaf_inv.shape
    return call(
        fold_kernel, "leaf_fold", [leaf_inv, leaf_off, ancestors], [VMEM] * 3,
        shape_of((leaves, 2 * blk, 2 * rows)), VMEM, after,
    )


def pack_kernel(place, inv, cpl, same, other):
    blocks, blk = inv.shape[1], inv.shape[3]
    for kind, out in enumerate((same, other)):
        block = (place[0] % blocks) ^ kind
        out[:blk] = inv[0, block, 0].astype(BF)
        out[blk : 2 * blk] = inv[0, block, 1].astype(BF)
        rest = jnp.broadcast_to(cpl[0, pl.ds(block, 1), :], (16, blk))
        row = lax.broadcasted_iota(jnp.int32, (16, blk), 0)
        value = jnp.zeros((16, blk), F32)
        for term in range(3):
            piece = rest.astype(BF).astype(F32)
            value = jnp.where(row == term, piece, value)
            rest = rest - piece
        out[2 * blk :] = value.astype(BF)


def pack(place, root_inv, coupling, after):
    _, blocks, _, blk, _ = root_inv.shape
    shape = shape_of((2 * blk + 16, blk))
    return call(
        pack_kernel, "solve_pack", [place, root_inv, coupling.reshape(1, blocks, blk)], [SMEM, VMEM, VMEM],
        [shape, shape], [VMEM, VMEM], after,
    )


def join_kernel(*refs):
    *parts, out = refs
    at = 0
    for ref in parts:
        out[at : at + ref.shape[0]] = ref[...]
        at += ref.shape[0]


def join(parts, after):
    rows = sum(part.shape[0] for part in parts)
    return call(
        join_kernel, "solve_join", parts, [VMEM] * len(parts), shape_of((rows,) + parts[0].shape[1:]), VMEM, after
    )


def first_kernel(names, keep, near, *outs):
    for (j, first, last), out in zip(names, outs):
        out[...] = (keep[j, first:last].astype(F32) + near[j, first:last].astype(F32)).astype(BF)


def first_sums(names, keep, near, after):
    return call(
        functools.partial(first_kernel, names), "interface_first", [keep, near], [VMEM, VMEM],
        [shape_of((last - first,) + keep.shape[2:]) for _, first, last in names], [VMEM] * len(names), after,
    )


def second_kernel(half, keep, near, by_x, by_y, out_x, out_y):
    parts = keep.shape[1]
    for j, out, extra, first, last in ((1, out_x, by_y, half, parts), (2, out_y, by_x, 0, half)):
        for q in range(parts):
            value = keep[j, q].astype(F32) + near[j, q].astype(F32)
            if first <= q < last:
                value = value + extra[q - first].astype(F32)
            out[q] = value.astype(BF)


def second_sums(half, keep, near, by_x, by_y, after):
    shape = shape_of(keep.shape[1:])
    return call(
        functools.partial(second_kernel, half), "interface_second", [keep, near, by_x, by_y], [VMEM] * 4,
        [shape, shape], [VMEM] * 2, after,
    )


def piece_of(index, blk, blocks):
    low = (index % blocks) * blk
    return index // blocks, slice(low, low + blk)


def reduce_kernel(h, slabs, blk, terms, place, rhs, keep, near, *refs):
    _, parts, _, rows, part = keep.shape
    outs = refs[terms:]
    for index in range(slabs):
        q, span = piece_of(index, blk, rows // blk)
        left = h * parts * part + q * part
        field = []
        for plane in range(2):
            value = keep[0, q, plane, span].astype(F32) + near[0, q, plane, span].astype(F32)
            for ref in refs[:terms]:
                value = value + ref[q, plane, span].astype(F32)
            field.append((rhs[0, plane, span, left : left + part].astype(F32) - value).astype(BF))
        for mask, out in enumerate(outs):

            @pl.when(place[0] ^ mask == index)
            def _(field=field, out=out):
                out[0] = field[0]
                out[1] = field[1]


def reduce(h, place, root_rhs, keep, near, far, slabs, blk, after):
    part = keep.shape[4]
    return call(
        functools.partial(reduce_kernel, h, slabs, blk, len(far)), "interface_reduce",
        [place, root_rhs, keep, near, *far], [SMEM] + [VMEM] * (3 + len(far)),
        [shape_of((2, blk, part))] * slabs, [VMEM] * slabs, after,
    )


def chain_kernel(slabs, count, place, *refs):
    pieces, mats, outs = refs[:slabs], refs[slabs : slabs + count], refs[slabs + count : 2 * slabs + count]
    held, solver = refs[2 * slabs + count :]
    me = place[0]
    for mask in range(slabs):
        held[mask] = pieces[mask][...]
    _, _, blk, part = held.shape
    tall = solver.shape[1]
    at = 0
    for mat in mats:
        for k in range(mat.shape[0] // tall):
            solver[at] = mat[k * tall : (k + 1) * tall]
            at += 1
    state = None
    for slab in range(slabs):
        at = me ^ slab
        field = held[at].reshape(2 * blk, part).astype(F32)
        packed = solver[at]
        if state is not None:
            terms = packed[2 * blk :].astype(F32)
            row = terms[0:1] + terms[1:2] + terms[2:3]
            scale = jnp.broadcast_to(row, (blk, blk)).T[:, :1]
            field = field - jnp.concatenate([scale, scale], axis=0) * state
        mat = stacked(packed[:blk], packed[blk : 2 * blk])
        high = field.astype(BF)
        state = dot(mat, high)
        if slab:
            state = state + dot(mat, (field - high.astype(F32)).astype(BF))
        half = state.astype(BF)
        for mask, out in enumerate(outs):

            @pl.when(at == mask)
            def _(half=half, out=out):
                out[0] = half[:blk]
                out[1] = half[blk:]


def chain(place, pieces, mats, after):
    slabs = len(pieces)
    tall = mats[0].shape
    return call(
        functools.partial(chain_kernel, slabs, len(mats)), "sweep_chain", [place, *pieces, *mats],
        [SMEM] + [VMEM] * (slabs + len(mats)),
        [shape_of(pieces[0].shape)] * slabs, [VMEM] * slabs, after,
        [pltpu.VMEM((slabs,) + pieces[0].shape, BF), pltpu.VMEM((slabs,) + tall, BF)],
    )


def collect_kernel(h, slabs, aliased, place, *refs):
    pieces = refs[:slabs]
    own, root, full, sem = refs[slabs + aliased :]
    _, blk, part = pieces[0].shape
    parts, _, rows, _ = own.shape
    cols = parts * part
    for mask, piece in enumerate(pieces):
        for index in range(slabs):
            q, span = piece_of(index, blk, rows // blk)

            @pl.when(place[0] ^ mask == index)
            def _(piece=piece, q=q, span=span):
                for plane in range(2):
                    own[q, plane, span] = piece[plane]
                    full[plane, span, q * part : (q + 1) * part] = piece[plane].astype(F32)

    copy = pltpu.make_async_copy(full, root.at[0, :, :, pl.ds(h * cols, cols)], sem)
    copy.start()
    copy.wait()


def collect(h, place, pieces, before, rows, width, after):
    slabs = len(pieces)
    cols = width // HALVES
    part = pieces[0].shape[2]
    aliased = [] if before is None else [before]
    return call(
        functools.partial(collect_kernel, h, slabs, len(aliased)), "interface_collect",
        [place, *pieces, *aliased], [SMEM] + [VMEM] * slabs + [HBM] * len(aliased),
        [shape_of((cols // part, 2, rows, part)), shape_of((1, 2, rows, width), F32)], [VMEM, HBM], after,
        [pltpu.VMEM((2, rows, cols), F32), pltpu.SemaphoreType.DMA],
        {1 + slabs: 1} if aliased else None,
    )


def backward_kernel(h, counts, cap, aliased, owners, place, fwd, mats, *refs):
    fronts = len(counts)
    fields = refs[: sum(counts)]
    out, held, slots, sems = refs[sum(counts) + aliased :]
    leaves, wide, cols = fwd.shape
    blk = wide // 2
    tall = mats.shape[2]
    for dist in range(fronts):
        for rank in range(cap):
            slots[dist * cap + rank] = -1
    for leaf in range(leaves):
        first = (owners[leaf] ^ place[1]) * cap
        spot = first
        for rank in range(cap - 1):
            spot = jnp.where(slots[first + rank] >= 0, first + rank + 1, spot)
        slots[spot] = leaf

    def copy_of(leaf):
        return pltpu.make_async_copy(held.at[leaf], out.at[0, :, leaf, :, pl.ds(h * cols, cols)], sems.at[leaf])

    for dist in range(fronts):
        mine, fields = fields[: counts[dist]], fields[counts[dist] :]
        columns = [ref[q].reshape(tall, ref.shape[3]) for ref in mine for q in range(ref.shape[0])]
        field = jnp.concatenate(columns, axis=1)
        for rank in range(cap):
            name = slots[dist * cap + rank]

            @pl.when(name >= 0)
            def _(name=name, field=field):
                result = fwd[name].astype(F32) - dot(mats[name], field)
                held[name, 0] = result[:blk].astype(BF)
                held[name, 1] = result[blk:].astype(BF)
                copy_of(name).start()

    for leaf in range(leaves):
        copy_of(leaf).wait()


def backward(h, owners, place, fwd, mats, fields, before, width, after):
    leaves, wide, cols = fwd.shape
    blk, fronts = wide // 2, len(fields)
    cap = -(-leaves // fronts)
    counts = [len(field) for field in fields]
    flat = [part for field in fields for part in field]
    aliased = [] if before is None else [before]
    return call(
        functools.partial(backward_kernel, h, counts, cap, len(aliased)), "leaf_backward",
        [owners, place, fwd, mats, *flat, *aliased], [SMEM, SMEM] + [VMEM] * (2 + len(flat)) + [HBM] * len(aliased),
        shape_of((1, 2, leaves, blk, width)), HBM, after,
        [
            pltpu.VMEM((leaves, 2, blk, cols), BF),
            pltpu.SMEM((fronts * cap,), jnp.int32),
            pltpu.SemaphoreType.DMA((leaves,)),
        ],
        {4 + len(flat): 0} if aliased else None,
    )


def body(leaf_rhs, leaf_inv, leaf_off, parent, ancestors, root_rhs, root_inv, coupling):
    fronts, slabs = lax.axis_size("front"), lax.axis_size("slab")
    rows, width = root_rhs.shape[2], root_rhs.shape[3]
    blk = leaf_rhs.shape[3]
    owners = parent.reshape(-1)
    place = jnp.stack([lax.axis_index("slab"), lax.axis_index("front")]).astype(jnp.int32)
    pairs = fronts // 2
    parts = slabs // (rows // blk)
    part = width // HALVES // parts
    square = pairs == 4

    def start_forward(h, after):
        fwd, keep, send = forward(
            h, owners, place, leaf_rhs, leaf_inv, leaf_off, ancestors, fronts, rows, part, after
        )
        return fwd, keep, crossed(send, "front", 1)

    def send_first(keep, near, after):
        if not square:
            sums = first_sums([(j, 0, parts) for j in range(1, pairs)], keep, near, after)
            return sums[0], [crossed(value, "front", 2 * (j + 1)) for j, value in enumerate(sums)]
        to_x, to_y = first_sums([(3, 0, parts // 2), (3, parts // 2, parts)], keep, near, after)
        return to_x, [crossed(to_x, "front", 2), crossed(to_y, "front", 4)]

    def send_second(keep, near, got, after):
        if not square:
            return got[0], got
        to_x, to_y = second_sums(parts // 2, keep, near, *got, after)
        return to_x, [crossed(to_x, "front", 2), crossed(to_y, "front", 4)]

    def over_slabs(values):
        return [values[0]] + [crossed(values[mask], "slab", mask) for mask in range(1, slabs)]

    def share(own):
        if square:
            by_x, by_y = crossed(own, "front", 2), crossed(own, "front", 4)
            far = [crossed(by_x[: parts // 2], "front", 4), crossed(by_y[parts // 2 :], "front", 2)]
            mine = [[own], [by_x], [by_y], far]
        else:
            mine = [[own]] + [[crossed(own, "front", 2 * j)] for j in range(1, pairs)]
        return [field for group in mine for field in (group, [crossed(value, "front", 1) for value in group])]

    fwd0, keep0, near0 = start_forward(0, ())
    same, other = pack(place, root_inv, coupling, [fwd0])
    have = [same, crossed(other, "slab", 1)]
    token, got0 = send_first(keep0, near0, [same])
    fwd1, keep1, near1 = start_forward(1, [token])
    token, far0 = send_second(keep0, near0, got0, [fwd1])
    step = 2
    while step < slabs:
        joined = join(have, [token])
        have = have + [crossed(joined, "slab", step)]
        step *= 2
        token = joined
    token, got1 = send_first(keep1, near1, [token])
    folded = fold(leaf_inv, leaf_off, ancestors, rows, [token])
    pieces0 = reduce(0, place, root_rhs, keep0, near0, far0, slabs, blk, [folded])
    token, far1 = send_second(keep1, near1, got1, [pieces0[0]])
    solved0 = chain(place, over_slabs(pieces0), have, [token])
    pieces1 = reduce(1, place, root_rhs, keep1, near1, far1, slabs, blk, [solved0[0]])
    own0, root_sol = collect(0, place, over_slabs(solved0), None, rows, width, [pieces1[0]])
    solved1 = chain(place, over_slabs(pieces1), have, [own0])
    fields0 = share(own0)
    own1, root_sol = collect(1, place, over_slabs(solved1), root_sol, rows, width, ())
    fields1 = share(own1)
    leaf_sol = backward(0, owners, place, fwd0, folded, fields0, None, width, [own1])
    leaf_sol = backward(1, owners, place, fwd1, folded, fields1, leaf_sol, width, ())
    return leaf_sol, root_sol


def solution(mesh):
    in_specs = (
        P("slab", None, "front", None, None),
        P("slab", "front", None, None, None),
        P("slab", "front", None, None, None),
        P("slab", "front", None),
        P("slab", "front", None),
        P("slab", None, "front", None),
        P("slab", "front", None, None, None),
        P("slab", "front"),
    )
    out_specs = (P("slab", None, "front", None, None), P("slab", None, "front", None))
    return jax.shard_map(body, mesh=mesh, in_specs=in_specs, out_specs=out_specs, check_vma=False)
```

time: 120 us -> 111 us (0.925)
  starting transfers between devices: 47.5 us -> 41.4 us
  Pallas kernels: 37.6 us -> 34.2 us
    ppermute x37 -> x42, starting transfers between devices: 47.5 us -> 41.4 us  [crossed(): lax.ppermute(x, axis, [(i, i ^ mask) for i in range(lax.axis_size(axis))])]
    pallas_call x14 -> x17, Pallas kernels: 37.6 us -> 34.2 us  [call(): pl.pallas_call(wrapped, in_specs=list(in_specs) + [ANY] * extra, out_spec...]
    ppermute x37 -> x42, waiting for transfers between devices: 27.8 us -> 28.4 us  [crossed(): lax.ppermute(x, axis, [(i, i ^ mask) for i in range(lax.axis_size(axis))])]
    unnamed x20 -> x24, local copies, waits for them, and re-layouts: 6.01 us -> 5.8 us
  transfers between devices with their start and end apart: 37 -> 42, of which waited for: 12 -> 15; matrix products, arithmetic and copies ran while one was open for 0% -> 0% of each run, Pallas kernels for 17% -> 15%
where the time goes in v3:
time: 111 us
  starting transfers between devices  41.4 us (37%)
  Pallas kernels  34.2 us (31%)
  waiting for transfers between devices  28.4 us (26%)
  local copies, waits for them, and re-layouts  5.83 us (5%)
    ppermute x42, starting transfers between devices, crossed(): lax.ppermute(x, axis, [(i, i ^ mask) for i in range(lax.axis_size(axis))])  41.4 us
    pallas_call x17, Pallas kernels, call(): pl.pallas_call(wrapped, in_specs=list(in_specs) + [ANY] * extra, out_spec...  34.2 us
    ppermute x42, waiting for transfers between devices, crossed(): lax.ppermute(x, axis, [(i, i ^ mask) for i in range(lax.axis_size(axis))])  28.4 us
    unnamed x24, local copies, waits for them, and re-layouts  5.8 us
  transfers between devices with their start and end apart: 42, of which 15 were waited for; matrix products, arithmetic and copies ran while one was open for 0% of the time, Pallas kernels for 15%

profile of v3, /device:TPU:0, one launch (start us, length us, event | category | flops | bytes accessed | tf_op | source)
XLA Modules:
  0.0 111.0 jit_solution(14290749593031100152)
XLA Ops:
  0.7 1.2 %copy-done = bf16[1,16,2,128,128]{4,3,2,1,0:T(8,128)(2,1)S(1)} copy-done((bf16[1,16,2,128,128]{4,3,2,1,0:T(8,128)(2,1)S(1)}, bf16[1,16,2,128,128]{4,3,2,1,0:T(8,128)(2,1)}, u32[]{:S(2)}) %copy-start) | copy-done | bytes 1048600
  1.9 0.7 copy-done.8
  2.6 0.7 copy-done.10
  3.3 5.4 %leaf_forward.2 = (bf16[16,256,256]{2,1,0:T(8,128)(2,1)}, bf16[4,2,2,256,128]{4,3,2,1,0:T(8,128)(2,1)S(1)}, bf16[4,2,2,256,128]{4,3,2,1,0:T(8,128)(2,1)S(1)}) custom-call(s32[16]{0:T(128)S(1)} %bitcast.4, s32[2]{0:T(128)S(1)} %pad_add_fusion.refs_1_.refs_0_, bf16[1,2,16,128,512]{4,3,2,1,0:T(8,128)(2,1)} %refs_2_.4, ...), custom_call_target="tpu_custom_call" | custom-call | flops 1 | bytes 1 | tf_op jit(solution)/shard_map/leaf_forward/pallas_call | solution.py:29
  9.2 1.6 %copy-done.4 = bf16[16,256,256]{2,1,0:T(8,128)(2,1)S(1)} copy-done((bf16[16,256,256]{2,1,0:T(8,128)(2,1)S(1)}, bf16[16,256,256]{2,1,0:T(8,128)(2,1)}, u32[]{:S(2)}) %copy-start.4) | copy-done | bytes 2097176
  11.6 5.4 %leaf_forward.3 = (bf16[16,256,256]{2,1,0:T(8,128)(2,1)}, bf16[4,2,2,256,128]{4,3,2,1,0:T(8,128)(2,1)S(1)}, bf16[4,2,2,256,128]{4,3,2,1,0:T(8,128)(2,1)S(1)}) custom-call(s32[16]{0:T(128)S(1)} %bitcast.5, s32[2]{0:T(128)S(1)} %pad_add_fusion.refs_1_.refs_0_, bf16[1,2,16,128,512]{4,3,2,1,0:T(8,128)(2,1)} %refs_2_.4, ...), custom_call_target="tpu_custom_call" | custom-call | flops 1 | bytes 1 | tf_op jit(solution)/shard_map/leaf_forward/pallas_call | solution.py:29
  17.4 2.7 %collective-permute-start.4 = (bf16[1,2,256,128]{3,2,1,0:T(8,128)(2,1)S(1)}, bf16[1,2,256,128]{3,2,1,0:T(8,128)(2,1)S(1)}, u32[]{:S(2)}, u32[]{:S(2)}) collective-permute-start(bf16[1,2,256,128]{3,2,1,0:T(8,128)(2,1)S(1)} %get-tuple-element.47), channel_id=1, source_target_pairs={{0,4},{1,5},{2,6},{3,7},{4,0},{5,1},{6,2},{7,3},{8,12},{9,13},{10,... | collective-permute-start | bytes 393224 | tf_op jit(solution)/shard_map/ppermute | solution.py:43
  20.1 1.5 %collective-permute-start.3 = (bf16[1,2,256,128]{3,2,1,0:T(8,128)(2,1)S(1)}, bf16[1,2,256,128]{3,2,1,0:T(8,128)(2,1)S(1)}, u32[]{:S(2)}, u32[]{:S(2)}) collective-permute-start(bf16[1,2,256,128]{3,2,1,0:T(8,128)(2,1)S(1)} %get-tuple-element.42.refs_6_), channel_id=1, source_target_pairs={{0,2},{1,3},{2,0},{3,1},{4,6},{5,7},{6,4},{7,5},{8,10},{9,11},{10,... | collective-permute-start | bytes 393224 | tf_op jit(solution)/shard_map/ppermute | solution.py:43
  21.6 2.5 %collective-permute-done.4.refs_3_ = bf16[1,2,256,128]{3,2,1,0:T(8,128)(2,1)S(1)} collective-permute-done((bf16[1,2,256,128]{3,2,1,0:T(8,128)(2,1)S(1)}, bf16[1,2,256,128]{3,2,1,0:T(8,128)(2,1)S(1)}, u32[]{:S(2)}, u32[]{:S(2)}) %collective-permute-start.4) | collective-permute-done | bytes 131104 | tf_op jit(solution)/shard_map/ppermute | solution.py:43
  24.1 1.5 %collective-permute-done.3.refs_2_ = bf16[1,2,256,128]{3,2,1,0:T(8,128)(2,1)S(1)} collective-permute-done((bf16[1,2,256,128]{3,2,1,0:T(8,128)(2,1)S(1)}, bf16[1,2,256,128]{3,2,1,0:T(8,128)(2,1)S(1)}, u32[]{:S(2)}, u32[]{:S(2)}) %collective-permute-start.3) | collective-permute-done | bytes 131104 | tf_op jit(solution)/shard_map/ppermute | solution.py:43
  25.6 1.6 %copy-done.2 = bf16[16,256,256]{2,1,0:T(8,128)(2,1)S(1)} copy-done((bf16[16,256,256]{2,1,0:T(8,128)(2,1)S(1)}, bf16[16,256,256]{2,1,0:T(8,128)(2,1)}, u32[]{:S(2)}) %copy-start.2) | copy-done | bytes 2097176
  27.7 1.7 %collective-permute-start.7 = (bf16[2,2,256,128]{3,2,1,0:T(8,128)(2,1)S(1)}, bf16[2,2,256,128]{3,2,1,0:T(8,128)(2,1)S(1)}, u32[]{:S(2)}, u32[]{:S(2)}) collective-permute-start(bf16[2,2,256,128]{3,2,1,0:T(8,128)(2,1)S(1)} %get-tuple-element.48.refs_2_), channel_id=1, source_target_pairs={{0,2},{1,3},{2,0},{3,1},{4,6},{5,7},{6,4},{7,5},{8,10},{9,11},{10,... | collective-permute-start | bytes 786440 | tf_op jit(solution)/shard_map/ppermute | solution.py:43
  29.4 1.6 %collective-permute-start.2 = (bf16[272,128]{1,0:T(8,128)(2,1)S(1)}, bf16[272,128]{1,0:T(8,128)(2,1)S(1)}, u32[]{:S(2)}, u32[]{:S(2)}) collective-permute-start(bf16[272,128]{1,0:T(8,128)(2,1)S(1)} %get-tuple-element.46), channel_id=1, source_target_pairs={{0,8},{8,0},{16,24},{24,16},{1,9},{9,1},{17,25},{25,17},{2,10},{10... | collective-permute-start | bytes 208904 | tf_op jit(solution)/shard_map/ppermute | solution.py:43
  30.9 2.7 %collective-permute-done.2.refs_1_.refs_6_ = bf16[272,128]{1,0:T(8,128)(2,1)S(1)} collective-permute-done((bf16[272,128]{1,0:T(8,128)(2,1)S(1)}, bf16[272,128]{1,0:T(8,128)(2,1)S(1)}, u32[]{:S(2)}, u32[]{:S(2)}) %collective-permute-start.2) | collective-permute-done | bytes 69664 | tf_op jit(solution)/shard_map/ppermute | solution.py:43
  33.8 1.6 %collective-permute-start.6 = (bf16[1,2,256,128]{3,2,1,0:T(8,128)(2,1)S(1)}, bf16[1,2,256,128]{3,2,1,0:T(8,128)(2,1)S(1)}, u32[]{:S(2)}, u32[]{:S(2)}) collective-permute-start(bf16[1,2,256,128]{3,2,1,0:T(8,128)(2,1)S(1)} %get-tuple-element.50), channel_id=1, source_target_pairs={{0,4},{1,5},{2,6},{3,7},{4,0},{5,1},{6,2},{7,3},{8,12},{9,13},{10,... | collective-permute-start | bytes 393224 | tf_op jit(solution)/shard_map/ppermute | solution.py:43
  35.9 2.6 %collective-permute-start.14 = (bf16[544,128]{1,0:T(8,128)(2,1)S(1)}, bf16[544,128]{1,0:T(8,128)(2,1)S(1)}, u32[]{:S(2)}, u32[]{:S(2)}) collective-permute-start(bf16[544,128]{1,0:T(8,128)(2,1)S(1)} %solve_join.1.refs_2_), channel_id=1, source_target_pairs={{0,16},{8,24},{16,0},{24,8},{1,17},{9,25},{17,1},{25,9},{2,18},{10... | collective-permute-start | bytes 417800 | tf_op jit(solution)/shard_map/ppermute | solution.py:43
  38.5 3.5 %leaf_fold.1.refs_6_.refs_3_ = bf16[16,256,512]{2,1,0:T(8,128)(2,1)S(1)} custom-call(bf16[1,16,2,128,128]{4,3,2,1,0:T(8,128)(2,1)S(1)} %copy-done, bf16[1,16,2,128,128]{4,3,2,1,0:T(8,128)(2,1)S(1)} %copy-done.1, s32[1,16,128]{2,1,0:T(8,128)S(1)} %copy-done.9, bf16[1,2,256,128]{3,2,1,0:T(8,128)(2,1)S(1)} %get-tuple-element.49.refs_3_), custom_call_target="tpu_custom_call" | custom-call | flops 1 | bytes 1 | tf_op jit(solution)/shard_map/leaf_fold/pallas_call | solution.py:29
  42.1 0.8 interface_reduce.2
  43.7 1.5 %collective-permute-start.9 = (bf16[2,2,256,128]{3,2,1,0:T(8,128)(2,1)S(1)}, bf16[2,2,256,128]{3,2,1,0:T(8,128)(2,1)S(1)}, u32[]{:S(2)}, u32[]{:S(2)}) collective-permute-start(bf16[2,2,256,128]{3,2,1,0:T(8,128)(2,1)S(1)} %get-tuple-element.53.refs_8_), channel_id=1, source_target_pairs={{0,2},{1,3},{2,0},{3,1},{4,6},{5,7},{6,4},{7,5},{8,10},{9,11},{10,... | collective-permute-start | bytes 786440 | tf_op jit(solution)/shard_map/ppermute | solution.py:43
  45.2 1.6 %collective-permute-start.11 = (bf16[2,128,128]{2,1,0:T(8,128)(2,1)S(1)}, bf16[2,128,128]{2,1,0:T(8,128)(2,1)S(1)}, u32[]{:S(2)}, u32[]{:S(2)}) collective-permute-start(bf16[2,128,128]{2,1,0:T(8,128)(2,1)S(1)} %get-tuple-element.55), channel_id=1, source_target_pairs={{0,8},{8,0},{16,24},{24,16},{1,9},{9,1},{17,25},{25,17},{2,10},{10... | collective-permute-start | bytes 196616 | tf_op jit(solution)/shard_map/ppermute | solution.py:43
  47.1 2.5 %collective-permute-start.13 = (bf16[2,128,128]{2,1,0:T(8,128)(2,1)S(1)}, bf16[2,128,128]{2,1,0:T(8,128)(2,1)S(1)}, u32[]{:S(2)}, u32[]{:S(2)}) collective-permute-start(bf16[2,128,128]{2,1,0:T(8,128)(2,1)S(1)} %get-tuple-element.57), channel_id=1, source_target_pairs={{0,24},{8,16},{16,8},{24,0},{1,25},{9,17},{17,9},{25,1},{2,26},{10... | collective-permute-start | bytes 196616 | tf_op jit(solution)/shard_map/ppermute | solution.py:43
  49.5 2.9 %collective-permute-done.12.refs_3_ = bf16[2,128,128]{2,1,0:T(8,128)(2,1)S(1)} collective-permute-done((bf16[2,128,128]{2,1,0:T(8,128)(2,1)S(1)}, bf16[2,128,128]{2,1,0:T(8,128)(2,1)S(1)}, u32[]{:S(2)}, u32[]{:S(2)}) %collective-permute-start.12) | collective-permute-done | bytes 65568 | tf_op jit(solution)/shard_map/ppermute | solution.py:43
  52.5 0.8 collective-permute-done.13.refs_4_
  53.3 1.9 %sweep_chain.2 = (bf16[2,128,128]{2,1,0:T(8,128)(2,1)S(1)}, bf16[2,128,128]{2,1,0:T(8,128)(2,1)S(1)}, bf16[2,128,128]{2,1,0:T(8,128)(2,1)S(1)}, bf16[2,128,128]{2,1,0:T(8,128)(2,1)S(1)}) custom-call(s32[2]{0:T(128)S(1)} %pad_add_fusion.refs_1_.refs_0_, bf16[2,128,128]{2,1,0:T(8,128)(2,1)S(1)} %get-tuple-element.52.refs_4_.refs_1_, ...), custom_call_target="tpu_custom_call" | custom-call | flops 1 | bytes 1 | tf_op jit(solution)/shard_map/sweep_chain/pallas_call | solution.py:29
  55.2 1.3 %collective-permute-start.18 = (bf16[2,128,128]{2,1,0:T(8,128)(2,1)S(1)}, bf16[2,128,128]{2,1,0:T(8,128)(2,1)S(1)}, u32[]{:S(2)}, u32[]{:S(2)}) collective-permute-start(bf16[2,128,128]{2,1,0:T(8,128)(2,1)S(1)} %get-tuple-element.63), channel_id=1, source_target_pairs={{0,8},{8,0},{16,24},{24,16},{1,9},{9,1},{17,25},{25,17},{2,10},{10... | collective-permute-start | bytes 196616 | tf_op jit(solution)/shard_map/ppermute | solution.py:43
  56.4 1.8 %collective-permute-start.19 = (bf16[2,128,128]{2,1,0:T(8,128)(2,1)S(1)}, bf16[2,128,128]{2,1,0:T(8,128)(2,1)S(1)}, u32[]{:S(2)}, u32[]{:S(2)}) collective-permute-start(bf16[2,128,128]{2,1,0:T(8,128)(2,1)S(1)} %get-tuple-element.64), channel_id=1, source_target_pairs={{0,16},{8,24},{16,0},{24,8},{1,17},{9,25},{17,1},{25,9},{2,18},{10... | collective-permute-start | bytes 196616 | tf_op jit(solution)/shard_map/ppermute | solution.py:43
  58.2 1.4 %collective-permute-start.20 = (bf16[2,128,128]{2,1,0:T(8,128)(2,1)S(1)}, bf16[2,128,128]{2,1,0:T(8,128)(2,1)S(1)}, u32[]{:S(2)}, u32[]{:S(2)}) collective-permute-start(bf16[2,128,128]{2,1,0:T(8,128)(2,1)S(1)} %get-tuple-element.65), channel_id=1, source_target_pairs={{0,24},{8,16},{16,8},{24,0},{1,25},{9,17},{17,9},{25,1},{2,26},{10... | collective-permute-start | bytes 196616 | tf_op jit(solution)/shard_map/ppermute | solution.py:43
  59.6 0.8 interface_reduce.3
  60.8 2.7 %collective-permute-start.16 = (bf16[2,128,128]{2,1,0:T(8,128)(2,1)S(1)}, bf16[2,128,128]{2,1,0:T(8,128)(2,1)S(1)}, u32[]{:S(2)}, u32[]{:S(2)}) collective-permute-start(bf16[2,128,128]{2,1,0:T(8,128)(2,1)S(1)} %get-tuple-element.61), channel_id=1, source_target_pairs={{0,16},{8,24},{16,0},{24,8},{1,17},{9,25},{17,1},{25,9},{2,18},{10... | collective-permute-start | bytes 196616 | tf_op jit(solution)/shard_map/ppermute | solution.py:43
  63.5 1.4 %collective-permute-start.17 = (bf16[2,128,128]{2,1,0:T(8,128)(2,1)S(1)}, bf16[2,128,128]{2,1,0:T(8,128)(2,1)S(1)}, u32[]{:S(2)}, u32[]{:S(2)}) collective-permute-start(bf16[2,128,128]{2,1,0:T(8,128)(2,1)S(1)} %get-tuple-element.62), channel_id=1, source_target_pairs={{0,24},{8,16},{16,8},{24,0},{1,25},{9,17},{17,9},{25,1},{2,26},{10... | collective-permute-start | bytes 196616 | tf_op jit(solution)/shard_map/ppermute | solution.py:43
  64.9 1.5 %interface_collect.2 = (bf16[2,2,256,128]{3,2,1,0:T(8,128)(2,1)S(1)}, f32[1,2,256,512]{3,2,1,0:T(8,128)}) custom-call(s32[2]{0:T(128)S(1)} %pad_add_fusion.refs_1_.refs_0_, bf16[2,128,128]{2,1,0:T(8,128)(2,1)S(1)} %get-tuple-element.58.refs_6_.refs_1_, bf16[2,128,128]{2,1,0:T(8,128)(2,1)S(1)} %collective-permute-done.18.refs_2_, ...), custom_call_target="tpu_custom_call" | custom-call | flops 1 | bytes 1 | tf_op jit(solution)/shard_map/interface_collect/pallas_call | solution.py:29
  66.5 3.6 %collective-permute-done.17.refs_4_ = bf16[2,128,128]{2,1,0:T(8,128)(2,1)S(1)} collective-permute-done((bf16[2,128,128]{2,1,0:T(8,128)(2,1)S(1)}, bf16[2,128,128]{2,1,0:T(8,128)(2,1)S(1)}, u32[]{:S(2)}, u32[]{:S(2)}) %collective-permute-start.17) | collective-permute-done | bytes 65568 | tf_op jit(solution)/shard_map/ppermute | solution.py:43
  70.1 1.9 %sweep_chain.3 = (bf16[2,128,128]{2,1,0:T(8,128)(2,1)S(1)}, bf16[2,128,128]{2,1,0:T(8,128)(2,1)S(1)}, bf16[2,128,128]{2,1,0:T(8,128)(2,1)S(1)}, bf16[2,128,128]{2,1,0:T(8,128)(2,1)S(1)}) custom-call(s32[2]{0:T(128)S(1)} %pad_add_fusion.refs_1_.refs_0_, bf16[2,128,128]{2,1,0:T(8,128)(2,1)S(1)} %get-tuple-element.59.refs_5_.refs_1_, ...), custom_call_target="tpu_custom_call" | custom-call | flops 1 | bytes 1 | tf_op jit(solution)/shard_map/sweep_chain/pallas_call | solution.py:29
  72.1 2.2 %collective-permute-start.22 = (bf16[2,128,128]{2,1,0:T(8,128)(2,1)S(1)}, bf16[2,128,128]{2,1,0:T(8,128)(2,1)S(1)}, u32[]{:S(2)}, u32[]{:S(2)}) collective-permute-start(bf16[2,128,128]{2,1,0:T(8,128)(2,1)S(1)} %get-tuple-element.69), channel_id=1, source_target_pairs={{0,16},{8,24},{16,0},{24,8},{1,17},{9,25},{17,1},{25,9},{2,18},{10... | collective-permute-start | bytes 196616 | tf_op jit(solution)/shard_map/ppermute | solution.py:43
  74.2 2.2 %collective-permute-start.23 = (bf16[2,128,128]{2,1,0:T(8,128)(2,1)S(1)}, bf16[2,128,128]{2,1,0:T(8,128)(2,1)S(1)}, u32[]{:S(2)}, u32[]{:S(2)}) collective-permute-start(bf16[2,128,128]{2,1,0:T(8,128)(2,1)S(1)} %get-tuple-element.70), channel_id=1, source_target_pairs={{0,24},{8,16},{16,8},{24,0},{1,25},{9,17},{17,9},{25,1},{2,26},{10... | collective-permute-start | bytes 196616 | tf_op jit(solution)/shard_map/ppermute | solution.py:43
  76.4 1.5 %collective-permute-start.36 = (bf16[2,2,256,128]{3,2,1,0:T(8,128)(2,1)S(1)}, bf16[2,2,256,128]{3,2,1,0:T(8,128)(2,1)S(1)}, u32[]{:S(2)}, u32[]{:S(2)}) collective-permute-start(bf16[2,2,256,128]{3,2,1,0:T(8,128)(2,1)S(1)} %get-tuple-element.66.refs_8_.refs_4_), channel_id=1, source_target_pairs={{0,4},{1,5},{2,6},{3,7},{4,0},{5,1},{6,2},{7,3},{8,12},{9,13},{10,... | collective-permute-start | bytes 786440 | tf_op jit(solution)/shard_map/ppermute | solution.py:43
  78.5 1.8 %collective-permute-done.23.refs_4_ = bf16[2,128,128]{2,1,0:T(8,128)(2,1)S(1)} collective-permute-done((bf16[2,128,128]{2,1,0:T(8,128)(2,1)S(1)}, bf16[2,128,128]{2,1,0:T(8,128)(2,1)S(1)}, u32[]{:S(2)}, u32[]{:S(2)}) %collective-permute-start.23) | collective-permute-done | bytes 65568 | tf_op jit(solution)/shard_map/ppermute | solution.py:43
  80.3 1.5 %interface_collect.3 = (bf16[2,2,256,128]{3,2,1,0:T(8,128)(2,1)S(1)}, f32[1,2,256,512]{3,2,1,0:T(8,128)}) custom-call(s32[2]{0:T(128)S(1)} %pad_add_fusion.refs_1_.refs_0_, bf16[2,128,128]{2,1,0:T(8,128)(2,1)S(1)} %get-tuple-element.67.refs_1_, bf16[2,128,128]{2,1,0:T(8,128)(2,1)S(1)} %collective-permute-done.21.refs_2_, ...), custom_call_target="tpu_custom_call", output_to_operand_aliasing={{1}: (5, {})} | custom-call | flops 1 | bytes 1 | tf_op jit(solution)/shard_map/interface_collect/pallas_call | solution.py:29
  81.8 1.6 %collective-permute-start.27 = (bf16[2,2,256,128]{3,2,1,0:T(8,128)(2,1)S(1)}, bf16[2,2,256,128]{3,2,1,0:T(8,128)(2,1)S(1)}, u32[]{:S(2)}, u32[]{:S(2)}) collective-permute-start(bf16[2,2,256,128]{3,2,1,0:T(8,128)(2,1)S(1)} %get-tuple-element.72.refs_14_.refs_4_), channel_id=1, source_target_pairs={{0,4},{1,5},{2,6},{3,7},{4,0},{5,1},{6,2},{7,3},{8,12},{9,13},{10,... | collective-permute-start | bytes 786440 | tf_op jit(solution)/shard_map/ppermute | solution.py:43
  84.5 3.7 %collective-permute-done.27.refs_8_ = bf16[2,2,256,128]{3,2,1,0:T(8,128)(2,1)S(1)} collective-permute-done((bf16[2,2,256,128]{3,2,1,0:T(8,128)(2,1)S(1)}, bf16[2,2,256,128]{3,2,1,0:T(8,128)(2,1)S(1)}, u32[]{:S(2)}, u32[]{:S(2)}) %collective-permute-start.27) | collective-permute-done | bytes 262176 | tf_op jit(solution)/shard_map/ppermute | solution.py:43
  88.8 3.1 %collective-permute-done.25.refs_6_ = bf16[2,2,256,128]{3,2,1,0:T(8,128)(2,1)S(1)} collective-permute-done((bf16[2,2,256,128]{3,2,1,0:T(8,128)(2,1)S(1)}, bf16[2,2,256,128]{3,2,1,0:T(8,128)(2,1)S(1)}, u32[]{:S(2)}, u32[]{:S(2)}) %collective-permute-start.25) | collective-permute-done | bytes 262176 | tf_op jit(solution)/shard_map/ppermute | solution.py:43
  92.5 1.5 %collective-permute-done.39.refs_11_ = bf16[1,2,256,128]{3,2,1,0:T(8,128)(2,1)S(1)} collective-permute-done((bf16[1,2,256,128]{3,2,1,0:T(8,128)(2,1)S(1)}, bf16[1,2,256,128]{3,2,1,0:T(8,128)(2,1)S(1)}, u32[]{:S(2)}, u32[]{:S(2)}) %collective-permute-start.39) | collective-permute-done | bytes 131104 | tf_op jit(solution)/shard_map/ppermute | solution.py:43
  94.0 1.0 collective-permute-start.29
  95.0 1.9 %collective-permute-done.38.refs_10_ = bf16[1,2,256,128]{3,2,1,0:T(8,128)(2,1)S(1)} collective-permute-done((bf16[1,2,256,128]{3,2,1,0:T(8,128)(2,1)S(1)}, bf16[1,2,256,128]{3,2,1,0:T(8,128)(2,1)S(1)}, u32[]{:S(2)}, u32[]{:S(2)}) %collective-permute-start.38) | collective-permute-done | bytes 131104 | tf_op jit(solution)/shard_map/ppermute | solution.py:43
  98.0 1.0 collective-permute-done.29.refs_10_
  99.5 0.8 collective-permute-done.40.refs_12_
  100.5 5.2 %leaf_backward.2.refs_14_ = bf16[1,2,16,128,512]{4,3,2,1,0:T(8,128)(2,1)} custom-call(s32[16]{0:T(128)S(1)} %bitcast.6, s32[2]{0:T(128)S(1)} %pad_add_fusion.refs_1_.refs_0_, bf16[16,256,256]{2,1,0:T(8,128)(2,1)S(1)} %copy-done.5, bf16[16,256,512]{2,1,0:T(8,128)(2,1)S(1)} %leaf_fold.1.refs_6_.refs_3_, ...), custom_call_target="tpu_custom_call" | custom-call | flops 1 | bytes 1 | tf_op jit(solution)/shard_map/leaf_backward/pallas_call | solution.py:29
  105.7 5.2 %leaf_backward.3 = bf16[1,2,16,128,512]{4,3,2,1,0:T(8,128)(2,1)} custom-call(s32[16]{0:T(128)S(1)} %bitcast.7, s32[2]{0:T(128)S(1)} %pad_add_fusion.refs_1_.refs_0_, bf16[16,256,256]{2,1,0:T(8,128)(2,1)S(1)} %copy-done.3, bf16[16,256,512]{2,1,0:T(8,128)(2,1)S(1)} %leaf_fold.1.refs_6_.refs_3_, ...), custom_call_target="tpu_custom_call", output_to_operand_aliasing={{}: (14, {})} | custom-call | flops 1 | bytes 1 | tf_op jit(solution)/shard_map/leaf_backward/pallas_call | solution.py:29
  (82 shorter events, 9.0 us)
Async XLA Ops:
  0.6 8.6 %copy-start.11 = (f32[1,256]{1,0:T(1,128)S(1)}, f32[1,256]{1,0:T(1,128)}, u32[]{:S(2)}) copy-start(f32[1,256]{1,0:T(1,128)} %param.15) | copy-start | bytes 3076
  8.7 2.8 %collective-permute-start = (bf16[4,2,2,256,128]{4,3,2,1,0:T(8,128)(2,1)S(1)}, bf16[4,2,2,256,128]{4,3,2,1,0:T(8,128)(2,1)S(1)}, u32[]{:S(2)}, u32[]{:S(2)}) collective-permute-start(bf16[4,2,2,256,128]{4,3,2,1,0:T(8,128)(2,1)S(1)} %get-tuple-element.39), channel_id=1, source_target_pairs={{0,1},{1,0},{2,3},{3,2},{4,5},{5,4},{6,7},{7,6},{8,9},{9,8},{10,11... | collective-permute-start | bytes 3145736 | tf_op jit(solution)/shard_map/ppermute | solution.py:43
  11.5 27.0 %copy-start.9 = (s32[1,16,128]{2,1,0:T(8,128)S(1)}, s32[1,16,128]{2,1,0:T(8,128)}, u32[]{:S(2)}) copy-start(s32[1,16,128]{2,1,0:T(8,128)} %refs_2_.5) | copy-start | bytes 24580
  17.0 21.5 %copy-start.1 = (bf16[1,16,2,128,128]{4,3,2,1,0:T(8,128)(2,1)S(1)}, bf16[1,16,2,128,128]{4,3,2,1,0:T(8,128)(2,1)}, u32[]{:S(2)}) copy-start(bf16[1,16,2,128,128]{4,3,2,1,0:T(8,128)(2,1)} %refs_1_.5) | copy-start | bytes 3145732
  17.0 16.7 %collective-permute-start.1 = (bf16[4,2,2,256,128]{4,3,2,1,0:T(8,128)(2,1)S(1)}, bf16[4,2,2,256,128]{4,3,2,1,0:T(8,128)(2,1)S(1)}, u32[]{:S(2)}, u32[]{:S(2)}) collective-permute-start(bf16[4,2,2,256,128]{4,3,2,1,0:T(8,128)(2,1)S(1)} %get-tuple-element.45), channel_id=1, source_target_pairs={{0,1},{1,0},{2,3},{3,2},{4,5},{5,4},{6,7},{7,6},{8,9},{9,8},{10,11... | collective-permute-start | bytes 3145736 | tf_op jit(solution)/shard_map/ppermute | solution.py:43
  17.4 6.7 %collective-permute-start.4 = (bf16[1,2,256,128]{3,2,1,0:T(8,128)(2,1)S(1)}, bf16[1,2,256,128]{3,2,1,0:T(8,128)(2,1)S(1)}, u32[]{:S(2)}, u32[]{:S(2)}) collective-permute-start(bf16[1,2,256,128]{3,2,1,0:T(8,128)(2,1)S(1)} %get-tuple-element.47), channel_id=1, source_target_pairs={{0,4},{1,5},{2,6},{3,7},{4,0},{5,1},{6,2},{7,3},{8,12},{9,13},{10,... | collective-permute-start | bytes 393224 | tf_op jit(solution)/shard_map/ppermute | solution.py:43
  20.1 5.5 %collective-permute-start.3 = (bf16[1,2,256,128]{3,2,1,0:T(8,128)(2,1)S(1)}, bf16[1,2,256,128]{3,2,1,0:T(8,128)(2,1)S(1)}, u32[]{:S(2)}, u32[]{:S(2)}) collective-permute-start(bf16[1,2,256,128]{3,2,1,0:T(8,128)(2,1)S(1)} %get-tuple-element.42.refs_6_), channel_id=1, source_target_pairs={{0,2},{1,3},{2,0},{3,1},{4,6},{5,7},{6,4},{7,5},{8,10},{9,11},{10,... | collective-permute-start | bytes 393224 | tf_op jit(solution)/shard_map/ppermute | solution.py:43
  27.3 14.7 %collective-permute-start.8 = (bf16[2,2,256,128]{3,2,1,0:T(8,128)(2,1)S(1)}, bf16[2,2,256,128]{3,2,1,0:T(8,128)(2,1)S(1)}, u32[]{:S(2)}, u32[]{:S(2)}) collective-permute-start(bf16[2,2,256,128]{3,2,1,0:T(8,128)(2,1)S(1)} %get-tuple-element.51), channel_id=1, source_target_pairs={{0,4},{1,5},{2,6},{3,7},{4,0},{5,1},{6,2},{7,3},{8,12},{9,13},{10,... | collective-permute-start | bytes 786440 | tf_op jit(solution)/shard_map/ppermute | solution.py:43
  27.7 14.4 %collective-permute-start.7 = (bf16[2,2,256,128]{3,2,1,0:T(8,128)(2,1)S(1)}, bf16[2,2,256,128]{3,2,1,0:T(8,128)(2,1)S(1)}, u32[]{:S(2)}, u32[]{:S(2)}) collective-permute-start(bf16[2,2,256,128]{3,2,1,0:T(8,128)(2,1)S(1)} %get-tuple-element.48.refs_2_), channel_id=1, source_target_pairs={{0,2},{1,3},{2,0},{3,1},{4,6},{5,7},{6,4},{7,5},{8,10},{9,11},{10,... | collective-permute-start | bytes 786440 | tf_op jit(solution)/shard_map/ppermute | solution.py:43
  29.4 4.3 %collective-permute-start.2 = (bf16[272,128]{1,0:T(8,128)(2,1)S(1)}, bf16[272,128]{1,0:T(8,128)(2,1)S(1)}, u32[]{:S(2)}, u32[]{:S(2)}) collective-permute-start(bf16[272,128]{1,0:T(8,128)(2,1)S(1)} %get-tuple-element.46), channel_id=1, source_target_pairs={{0,8},{8,0},{16,24},{24,16},{1,9},{9,1},{17,25},{25,17},{2,10},{10... | collective-permute-start | bytes 208904 | tf_op jit(solution)/shard_map/ppermute | solution.py:43
  33.7 8.4 %copy-start.6 = (bf16[1,2,256,512]{3,2,1,0:T(8,128)(2,1)S(1)}, bf16[1,2,256,512]{3,2,1,0:T(8,128)(2,1)}, u32[]{:S(2)}) copy-start(bf16[1,2,256,512]{3,2,1,0:T(8,128)(2,1)} %refs_1_.7) | copy-start | bytes 1572868
  33.8 9.1 %collective-permute-start.6 = (bf16[1,2,256,128]{3,2,1,0:T(8,128)(2,1)S(1)}, bf16[1,2,256,128]{3,2,1,0:T(8,128)(2,1)S(1)}, u32[]{:S(2)}, u32[]{:S(2)}) collective-permute-start(bf16[1,2,256,128]{3,2,1,0:T(8,128)(2,1)S(1)} %get-tuple-element.50), channel_id=1, source_target_pairs={{0,4},{1,5},{2,6},{3,7},{4,0},{5,1},{6,2},{7,3},{8,12},{9,13},{10,... | collective-permute-start | bytes 393224 | tf_op jit(solution)/shard_map/ppermute | solution.py:43
  35.4 7.5 %collective-permute-start.5 = (bf16[1,2,256,128]{3,2,1,0:T(8,128)(2,1)S(1)}, bf16[1,2,256,128]{3,2,1,0:T(8,128)(2,1)S(1)}, u32[]{:S(2)}, u32[]{:S(2)}) collective-permute-start(bf16[1,2,256,128]{3,2,1,0:T(8,128)(2,1)S(1)} %get-tuple-element.49.refs_3_), channel_id=1, source_target_pairs={{0,2},{1,3},{2,0},{3,1},{4,6},{5,7},{6,4},{7,5},{8,10},{9,11},{10,... | collective-permute-start | bytes 393224 | tf_op jit(solution)/shard_map/ppermute | solution.py:43
  35.9 11.2 %collective-permute-start.14 = (bf16[544,128]{1,0:T(8,128)(2,1)S(1)}, bf16[544,128]{1,0:T(8,128)(2,1)S(1)}, u32[]{:S(2)}, u32[]{:S(2)}) collective-permute-start(bf16[544,128]{1,0:T(8,128)(2,1)S(1)} %solve_join.1.refs_2_), channel_id=1, source_target_pairs={{0,16},{8,24},{16,0},{24,8},{1,17},{9,25},{17,1},{25,9},{2,18},{10... | collective-permute-start | bytes 417800 | tf_op jit(solution)/shard_map/ppermute | solution.py:43
  43.1 57.4 %copy-start.5 = (bf16[16,256,256]{2,1,0:T(8,128)(2,1)S(1)}, bf16[16,256,256]{2,1,0:T(8,128)(2,1)}, u32[]{:S(2)}) copy-start(bf16[16,256,256]{2,1,0:T(8,128)(2,1)} %get-tuple-element.40.refs_3_.refs_2_) | copy-start | bytes 6291460
  43.1 16.6 %collective-permute-start.10 = (bf16[2,2,256,128]{3,2,1,0:T(8,128)(2,1)S(1)}, bf16[2,2,256,128]{3,2,1,0:T(8,128)(2,1)S(1)}, u32[]{:S(2)}, u32[]{:S(2)}) collective-permute-start(bf16[2,2,256,128]{3,2,1,0:T(8,128)(2,1)S(1)} %get-tuple-element.54), channel_id=1, source_target_pairs={{0,4},{1,5},{2,6},{3,7},{4,0},{5,1},{6,2},{7,3},{8,12},{9,13},{10,... | collective-permute-start | bytes 786440 | tf_op jit(solution)/shard_map/ppermute | solution.py:43
  43.7 16.0 %collective-permute-start.9 = (bf16[2,2,256,128]{3,2,1,0:T(8,128)(2,1)S(1)}, bf16[2,2,256,128]{3,2,1,0:T(8,128)(2,1)S(1)}, u32[]{:S(2)}, u32[]{:S(2)}) collective-permute-start(bf16[2,2,256,128]{3,2,1,0:T(8,128)(2,1)S(1)} %get-tuple-element.53.refs_8_), channel_id=1, source_target_pairs={{0,2},{1,3},{2,0},{3,1},{4,6},{5,7},{6,4},{7,5},{8,10},{9,11},{10,... | collective-permute-start | bytes 786440 | tf_op jit(solution)/shard_map/ppermute | solution.py:43
  45.2 4.4 %collective-permute-start.11 = (bf16[2,128,128]{2,1,0:T(8,128)(2,1)S(1)}, bf16[2,128,128]{2,1,0:T(8,128)(2,1)S(1)}, u32[]{:S(2)}, u32[]{:S(2)}) collective-permute-start(bf16[2,128,128]{2,1,0:T(8,128)(2,1)S(1)} %get-tuple-element.55), channel_id=1, source_target_pairs={{0,8},{8,0},{16,24},{24,16},{1,9},{9,1},{17,25},{25,17},{2,10},{10... | collective-permute-start | bytes 196616 | tf_op jit(solution)/shard_map/ppermute | solution.py:43
  46.7 5.8 %collective-permute-start.12 = (bf16[2,128,128]{2,1,0:T(8,128)(2,1)S(1)}, bf16[2,128,128]{2,1,0:T(8,128)(2,1)S(1)}, u32[]{:S(2)}, u32[]{:S(2)}) collective-permute-start(bf16[2,128,128]{2,1,0:T(8,128)(2,1)S(1)} %get-tuple-element.56), channel_id=1, source_target_pairs={{0,16},{8,24},{16,0},{24,8},{1,17},{9,25},{17,1},{25,9},{2,18},{10... | collective-permute-start | bytes 196616 | tf_op jit(solution)/shard_map/ppermute | solution.py:43
  47.1 6.2 %collective-permute-start.13 = (bf16[2,128,128]{2,1,0:T(8,128)(2,1)S(1)}, bf16[2,128,128]{2,1,0:T(8,128)(2,1)S(1)}, u32[]{:S(2)}, u32[]{:S(2)}) collective-permute-start(bf16[2,128,128]{2,1,0:T(8,128)(2,1)S(1)} %get-tuple-element.57), channel_id=1, source_target_pairs={{0,24},{8,16},{16,8},{24,0},{1,25},{9,17},{17,9},{25,1},{2,26},{10... | collective-permute-start | bytes 196616 | tf_op jit(solution)/shard_map/ppermute | solution.py:43
  55.2 8.3 %collective-permute-start.18 = (bf16[2,128,128]{2,1,0:T(8,128)(2,1)S(1)}, bf16[2,128,128]{2,1,0:T(8,128)(2,1)S(1)}, u32[]{:S(2)}, u32[]{:S(2)}) collective-permute-start(bf16[2,128,128]{2,1,0:T(8,128)(2,1)S(1)} %get-tuple-element.63), channel_id=1, source_target_pairs={{0,8},{8,0},{16,24},{24,16},{1,9},{9,1},{17,25},{25,17},{2,10},{10... | collective-permute-start | bytes 196616 | tf_op jit(solution)/shard_map/ppermute | solution.py:43
  56.4 8.5 %collective-permute-start.19 = (bf16[2,128,128]{2,1,0:T(8,128)(2,1)S(1)}, bf16[2,128,128]{2,1,0:T(8,128)(2,1)S(1)}, u32[]{:S(2)}, u32[]{:S(2)}) collective-permute-start(bf16[2,128,128]{2,1,0:T(8,128)(2,1)S(1)} %get-tuple-element.64), channel_id=1, source_target_pairs={{0,16},{8,24},{16,0},{24,8},{1,17},{9,25},{17,1},{25,9},{2,18},{10... | collective-permute-start | bytes 196616 | tf_op jit(solution)/shard_map/ppermute | solution.py:43
  58.2 6.7 %collective-permute-start.20 = (bf16[2,128,128]{2,1,0:T(8,128)(2,1)S(1)}, bf16[2,128,128]{2,1,0:T(8,128)(2,1)S(1)}, u32[]{:S(2)}, u32[]{:S(2)}) collective-permute-start(bf16[2,128,128]{2,1,0:T(8,128)(2,1)S(1)} %get-tuple-element.65), channel_id=1, source_target_pairs={{0,24},{8,16},{16,8},{24,0},{1,25},{9,17},{17,9},{25,1},{2,26},{10... | collective-permute-start | bytes 196616 | tf_op jit(solution)/shard_map/ppermute | solution.py:43
  60.5 6.0 %collective-permute-start.15 = (bf16[2,128,128]{2,1,0:T(8,128)(2,1)S(1)}, bf16[2,128,128]{2,1,0:T(8,128)(2,1)S(1)}, u32[]{:S(2)}, u32[]{:S(2)}) collective-permute-start(bf16[2,128,128]{2,1,0:T(8,128)(2,1)S(1)} %get-tuple-element.60), channel_id=1, source_target_pairs={{0,8},{8,0},{16,24},{24,16},{1,9},{9,1},{17,25},{25,17},{2,10},{10... | collective-permute-start | bytes 196616 | tf_op jit(solution)/shard_map/ppermute | solution.py:43
  60.8 5.6 %collective-permute-start.16 = (bf16[2,128,128]{2,1,0:T(8,128)(2,1)S(1)}, bf16[2,128,128]{2,1,0:T(8,128)(2,1)S(1)}, u32[]{:S(2)}, u32[]{:S(2)}) collective-permute-start(bf16[2,128,128]{2,1,0:T(8,128)(2,1)S(1)} %get-tuple-element.61), channel_id=1, source_target_pairs={{0,16},{8,24},{16,0},{24,8},{1,17},{9,25},{17,1},{25,9},{2,18},{10... | collective-permute-start | bytes 196616 | tf_op jit(solution)/shard_map/ppermute | solution.py:43
  63.5 6.6 %collective-permute-start.17 = (bf16[2,128,128]{2,1,0:T(8,128)(2,1)S(1)}, bf16[2,128,128]{2,1,0:T(8,128)(2,1)S(1)}, u32[]{:S(2)}, u32[]{:S(2)}) collective-permute-start(bf16[2,128,128]{2,1,0:T(8,128)(2,1)S(1)} %get-tuple-element.62), channel_id=1, source_target_pairs={{0,24},{8,16},{16,8},{24,0},{1,25},{9,17},{17,9},{25,1},{2,26},{10... | collective-permute-start | bytes 196616 | tf_op jit(solution)/shard_map/ppermute | solution.py:43
  72.0 6.5 %collective-permute-start.21 = (bf16[2,128,128]{2,1,0:T(8,128)(2,1)S(1)}, bf16[2,128,128]{2,1,0:T(8,128)(2,1)S(1)}, u32[]{:S(2)}, u32[]{:S(2)}) collective-permute-start(bf16[2,128,128]{2,1,0:T(8,128)(2,1)S(1)} %get-tuple-element.68), channel_id=1, source_target_pairs={{0,8},{8,0},{16,24},{24,16},{1,9},{9,1},{17,25},{25,17},{2,10},{10... | collective-permute-start | bytes 196616 | tf_op jit(solution)/shard_map/ppermute | solution.py:43
  72.1 6.4 %collective-permute-start.22 = (bf16[2,128,128]{2,1,0:T(8,128)(2,1)S(1)}, bf16[2,128,128]{2,1,0:T(8,128)(2,1)S(1)}, u32[]{:S(2)}, u32[]{:S(2)}) collective-permute-start(bf16[2,128,128]{2,1,0:T(8,128)(2,1)S(1)} %get-tuple-element.69), channel_id=1, source_target_pairs={{0,16},{8,24},{16,0},{24,8},{1,17},{9,25},{17,1},{25,9},{2,18},{10... | collective-permute-start | bytes 196616 | tf_op jit(solution)/shard_map/ppermute | solution.py:43
  74.2 6.1 %collective-permute-start.23 = (bf16[2,128,128]{2,1,0:T(8,128)(2,1)S(1)}, bf16[2,128,128]{2,1,0:T(8,128)(2,1)S(1)}, u32[]{:S(2)}, u32[]{:S(2)}) collective-permute-start(bf16[2,128,128]{2,1,0:T(8,128)(2,1)S(1)} %get-tuple-element.70), channel_id=1, source_target_pairs={{0,24},{8,16},{16,8},{24,0},{1,25},{9,17},{17,9},{25,1},{2,26},{10... | collective-permute-start | bytes 196616 | tf_op jit(solution)/shard_map/ppermute | solution.py:43
  76.4 7.5 %collective-permute-start.36 = (bf16[2,2,256,128]{3,2,1,0:T(8,128)(2,1)S(1)}, bf16[2,2,256,128]{3,2,1,0:T(8,128)(2,1)S(1)}, u32[]{:S(2)}, u32[]{:S(2)}) collective-permute-start(bf16[2,2,256,128]{3,2,1,0:T(8,128)(2,1)S(1)} %get-tuple-element.66.refs_8_.refs_4_), channel_id=1, source_target_pairs={{0,4},{1,5},{2,6},{3,7},{4,0},{5,1},{6,2},{7,3},{8,12},{9,13},{10,... | collective-permute-start | bytes 786440 | tf_op jit(solution)/shard_map/ppermute | solution.py:43
  78.0 6.5 %collective-permute-start.34 = (bf16[2,2,256,128]{3,2,1,0:T(8,128)(2,1)S(1)}, bf16[2,2,256,128]{3,2,1,0:T(8,128)(2,1)S(1)}, u32[]{:S(2)}, u32[]{:S(2)}) collective-permute-start(bf16[2,2,256,128]{3,2,1,0:T(8,128)(2,1)S(1)} %get-tuple-element.66.refs_8_.refs_4_), channel_id=1, source_target_pairs={{0,2},{1,3},{2,0},{3,1},{4,6},{5,7},{6,4},{7,5},{8,10},{9,11},{10,... | collective-permute-start | bytes 786440 | tf_op jit(solution)/shard_map/ppermute | solution.py:43
  81.8 6.4 %collective-permute-start.27 = (bf16[2,2,256,128]{3,2,1,0:T(8,128)(2,1)S(1)}, bf16[2,2,256,128]{3,2,1,0:T(8,128)(2,1)S(1)}, u32[]{:S(2)}, u32[]{:S(2)}) collective-permute-start(bf16[2,2,256,128]{3,2,1,0:T(8,128)(2,1)S(1)} %get-tuple-element.72.refs_14_.refs_4_), channel_id=1, source_target_pairs={{0,4},{1,5},{2,6},{3,7},{4,0},{5,1},{6,2},{7,3},{8,12},{9,13},{10,... | collective-permute-start | bytes 786440 | tf_op jit(solution)/shard_map/ppermute | solution.py:43
  83.4 8.6 %collective-permute-start.25 = (bf16[2,2,256,128]{3,2,1,0:T(8,128)(2,1)S(1)}, bf16[2,2,256,128]{3,2,1,0:T(8,128)(2,1)S(1)}, u32[]{:S(2)}, u32[]{:S(2)}) collective-permute-start(bf16[2,2,256,128]{3,2,1,0:T(8,128)(2,1)S(1)} %get-tuple-element.72.refs_14_.refs_4_), channel_id=1, source_target_pairs={{0,2},{1,3},{2,0},{3,1},{4,6},{5,7},{6,4},{7,5},{8,10},{9,11},{10,... | collective-permute-start | bytes 786440 | tf_op jit(solution)/shard_map/ppermute | solution.py:43
  83.9 8.5 %collective-permute-start.33 = (bf16[2,2,256,128]{3,2,1,0:T(8,128)(2,1)S(1)}, bf16[2,2,256,128]{3,2,1,0:T(8,128)(2,1)S(1)}, u32[]{:S(2)}, u32[]{:S(2)}) collective-permute-start(bf16[2,2,256,128]{3,2,1,0:T(8,128)(2,1)S(1)} %get-tuple-element.66.refs_8_.refs_4_), channel_id=1, source_target_pairs={{0,1},{1,0},{2,3},{3,2},{4,5},{5,4},{6,7},{7,6},{8,9},{9,8},{10,11... | collective-permute-start | bytes 786440 | tf_op jit(solution)/shard_map/ppermute | solution.py:43
  83.9 13.0 %collective-permute-start.37 = (bf16[2,2,256,128]{3,2,1,0:T(8,128)(2,1)S(1)}, bf16[2,2,256,128]{3,2,1,0:T(8,128)(2,1)S(1)}, u32[]{:S(2)}, u32[]{:S(2)}) collective-permute-start(bf16[2,2,256,128]{3,2,1,0:T(8,128)(2,1)S(1)} %collective-permute-done.36.refs_8_), channel_id=1, source_target_pairs={{0,1},{1,0},{2,3},{3,2},{4,5},{5,4},{6,7},{7,6},{8,9},{9,8},{10,11... | collective-permute-start | bytes 786440 | tf_op jit(solution)/shard_map/ppermute | solution.py:43
  84.5 13.0 %collective-permute-start.35 = (bf16[2,2,256,128]{3,2,1,0:T(8,128)(2,1)S(1)}, bf16[2,2,256,128]{3,2,1,0:T(8,128)(2,1)S(1)}, u32[]{:S(2)}, u32[]{:S(2)}) collective-permute-start(bf16[2,2,256,128]{3,2,1,0:T(8,128)(2,1)S(1)} %collective-permute-done.34.refs_6_), channel_id=1, source_target_pairs={{0,1},{1,0},{2,3},{3,2},{4,5},{5,4},{6,7},{7,6},{8,9},{9,8},{10,11... | collective-permute-start | bytes 786440 | tf_op jit(solution)/shard_map/ppermute | solution.py:43
  88.3 5.7 %collective-permute-start.39 = (bf16[1,2,256,128]{3,2,1,0:T(8,128)(2,1)S(1)}, bf16[1,2,256,128]{3,2,1,0:T(8,128)(2,1)S(1)}, u32[]{:S(2)}, u32[]{:S(2)}) collective-permute-start(bf16[1,2,256,128]{3,2,1,0:T(8,128)(2,1)S(1)} %slice.19), channel_id=1, source_target_pairs={{0,2},{1,3},{2,0},{3,1},{4,6},{5,7},{6,4},{7,5},{8,10},{9,11},{10,... | collective-permute-start | bytes 393224 | tf_op jit(solution)/shard_map/ppermute | solution.py:43
  92.0 5.0 %collective-permute-start.38 = (bf16[1,2,256,128]{3,2,1,0:T(8,128)(2,1)S(1)}, bf16[1,2,256,128]{3,2,1,0:T(8,128)(2,1)S(1)}, u32[]{:S(2)}, u32[]{:S(2)}) collective-permute-start(bf16[1,2,256,128]{3,2,1,0:T(8,128)(2,1)S(1)} %slice.18), channel_id=1, source_target_pairs={{0,4},{1,5},{2,6},{3,7},{4,0},{5,1},{6,2},{7,3},{8,12},{9,13},{10,... | collective-permute-start | bytes 393224 | tf_op jit(solution)/shard_map/ppermute | solution.py:43
  92.4 13.3 %copy-start.3 = (bf16[16,256,256]{2,1,0:T(8,128)(2,1)S(1)}, bf16[16,256,256]{2,1,0:T(8,128)(2,1)}, u32[]{:S(2)}) copy-start(bf16[16,256,256]{2,1,0:T(8,128)(2,1)} %get-tuple-element.43.refs_4_.refs_2_) | copy-start | bytes 6291460
  92.4 5.1 %collective-permute-start.30 = (bf16[1,2,256,128]{3,2,1,0:T(8,128)(2,1)S(1)}, bf16[1,2,256,128]{3,2,1,0:T(8,128)(2,1)S(1)}, u32[]{:S(2)}, u32[]{:S(2)}) collective-permute-start(bf16[1,2,256,128]{3,2,1,0:T(8,128)(2,1)S(1)} %slice.17), channel_id=1, source_target_pairs={{0,2},{1,3},{2,0},{3,1},{4,6},{5,7},{6,4},{7,5},{8,10},{9,11},{10,... | collective-permute-start | bytes 393224 | tf_op jit(solution)/shard_map/ppermute | solution.py:43
  94.0 5.0 %collective-permute-start.29 = (bf16[1,2,256,128]{3,2,1,0:T(8,128)(2,1)S(1)}, bf16[1,2,256,128]{3,2,1,0:T(8,128)(2,1)S(1)}, u32[]{:S(2)}, u32[]{:S(2)}) collective-permute-start(bf16[1,2,256,128]{3,2,1,0:T(8,128)(2,1)S(1)} %slice.16), channel_id=1, source_target_pairs={{0,4},{1,5},{2,6},{3,7},{4,0},{5,1},{6,2},{7,3},{8,12},{9,13},{10,... | collective-permute-start | bytes 393224 | tf_op jit(solution)/shard_map/ppermute | solution.py:43
  96.9 8.8 %collective-permute-start.24 = (bf16[2,2,256,128]{3,2,1,0:T(8,128)(2,1)S(1)}, bf16[2,2,256,128]{3,2,1,0:T(8,128)(2,1)S(1)}, u32[]{:S(2)}, u32[]{:S(2)}) collective-permute-start(bf16[2,2,256,128]{3,2,1,0:T(8,128)(2,1)S(1)} %get-tuple-element.72.refs_14_.refs_4_), channel_id=1, source_target_pairs={{0,1},{1,0},{2,3},{3,2},{4,5},{5,4},{6,7},{7,6},{8,9},{9,8},{10,11... | collective-permute-start | bytes 786440 | tf_op jit(solution)/shard_map/ppermute | solution.py:43
  96.9 8.8 %collective-permute-start.28 = (bf16[2,2,256,128]{3,2,1,0:T(8,128)(2,1)S(1)}, bf16[2,2,256,128]{3,2,1,0:T(8,128)(2,1)S(1)}, u32[]{:S(2)}, u32[]{:S(2)}) collective-permute-start(bf16[2,2,256,128]{3,2,1,0:T(8,128)(2,1)S(1)} %collective-permute-done.27.refs_8_), channel_id=1, source_target_pairs={{0,1},{1,0},{2,3},{3,2},{4,5},{5,4},{6,7},{7,6},{8,9},{9,8},{10,11... | collective-permute-start | bytes 786440 | tf_op jit(solution)/shard_map/ppermute | solution.py:43
  97.4 8.3 %collective-permute-start.26 = (bf16[2,2,256,128]{3,2,1,0:T(8,128)(2,1)S(1)}, bf16[2,2,256,128]{3,2,1,0:T(8,128)(2,1)S(1)}, u32[]{:S(2)}, u32[]{:S(2)}) collective-permute-start(bf16[2,2,256,128]{3,2,1,0:T(8,128)(2,1)S(1)} %collective-permute-done.25.refs_6_), channel_id=1, source_target_pairs={{0,1},{1,0},{2,3},{3,2},{4,5},{5,4},{6,7},{7,6},{8,9},{9,8},{10,11... | collective-permute-start | bytes 786440 | tf_op jit(solution)/shard_map/ppermute | solution.py:43
  97.5 1.9 %collective-permute-start.41 = (bf16[1,2,256,128]{3,2,1,0:T(8,128)(2,1)S(1)}, bf16[1,2,256,128]{3,2,1,0:T(8,128)(2,1)S(1)}, u32[]{:S(2)}, u32[]{:S(2)}) collective-permute-start(bf16[1,2,256,128]{3,2,1,0:T(8,128)(2,1)S(1)} %collective-permute-done.39.refs_11_), channel_id=1, source_target_pairs={{0,1},{1,0},{2,3},{3,2},{4,5},{5,4},{6,7},{7,6},{8,9},{9,8},{10,11... | collective-permute-start | bytes 393224 | tf_op jit(solution)/shard_map/ppermute | solution.py:43
  99.0 1.3 %collective-permute-start.40 = (bf16[1,2,256,128]{3,2,1,0:T(8,128)(2,1)S(1)}, bf16[1,2,256,128]{3,2,1,0:T(8,128)(2,1)S(1)}, u32[]{:S(2)}, u32[]{:S(2)}) collective-permute-start(bf16[1,2,256,128]{3,2,1,0:T(8,128)(2,1)S(1)} %collective-permute-done.38.refs_10_), channel_id=1, source_target_pairs={{0,1},{1,0},{2,3},{3,2},{4,5},{5,4},{6,7},{7,6},{8,9},{9,8},{10,11... | collective-permute-start | bytes 393224 | tf_op jit(solution)/shard_map/ppermute | solution.py:43
  99.4 6.3 %collective-permute-start.32 = (bf16[1,2,256,128]{3,2,1,0:T(8,128)(2,1)S(1)}, bf16[1,2,256,128]{3,2,1,0:T(8,128)(2,1)S(1)}, u32[]{:S(2)}, u32[]{:S(2)}) collective-permute-start(bf16[1,2,256,128]{3,2,1,0:T(8,128)(2,1)S(1)} %collective-permute-done.30.refs_11_), channel_id=1, source_target_pairs={{0,1},{1,0},{2,3},{3,2},{4,5},{5,4},{6,7},{7,6},{8,9},{9,8},{10,11... | collective-permute-start | bytes 393224 | tf_op jit(solution)/shard_map/ppermute | solution.py:43
  100.3 5.4 %collective-permute-start.31 = (bf16[1,2,256,128]{3,2,1,0:T(8,128)(2,1)S(1)}, bf16[1,2,256,128]{3,2,1,0:T(8,128)(2,1)S(1)}, u32[]{:S(2)}, u32[]{:S(2)}) collective-permute-start(bf16[1,2,256,128]{3,2,1,0:T(8,128)(2,1)S(1)} %collective-permute-done.29.refs_10_), channel_id=1, source_target_pairs={{0,1},{1,0},{2,3},{3,2},{4,5},{5,4},{6,7},{7,6},{8,9},{9,8},{10,11... | collective-permute-start | bytes 393224 | tf_op jit(solution)/shard_map/ppermute | solution.py:43
  (6 other events, 11.7 us)

commit v4 on v3

--- a/solution.py
+++ b/solution.py
@@ -34,7 +34,7 @@
         scratch_shapes=list(scratch),
         input_output_aliases=aliases or {},
         compiler_params=pltpu.CompilerParams(vmem_limit_bytes=room * 1024 * 1024),
-        cost_estimate=pl.CostEstimate(flops=1, bytes_accessed=1, transcendentals=0),
+        cost_estimate=pl.CostEstimate(flops=10**10, bytes_accessed=1, transcendentals=0),
         name=name,
     )(*ins, *after)
 

time: 111 us -> 102 us (0.919)
  waiting for transfers between devices: 28.4 us -> 18 us
    ppermute x42, waiting for transfers between devices: 28.4 us -> 18 us  [crossed(): lax.ppermute(x, axis, [(i, i ^ mask) for i in range(lax.axis_size(axis))])]
  transfers between devices with their start and end apart: 42 -> 42, of which waited for: 15 -> 14; matrix products, arithmetic and copies ran while one was open for 0% -> 0% of each run, Pallas kernels for 15% -> 21%
where the time goes in v4:
time: 102 us; the launch traced here: 101 us
  starting transfers between devices  42.3 us (41%)
  Pallas kernels  34.2 us (34%)
  waiting for transfers between devices  18 us (18%)
  local copies, waits for them, and re-layouts  5.82 us (6%)
    ppermute x42, starting transfers between devices, crossed(): lax.ppermute(x, axis, [(i, i ^ mask) for i in range(lax.axis_size(axis))])  42.3 us
    pallas_call x17, Pallas kernels, call(): pl.pallas_call(wrapped, in_specs=list(in_specs) + [ANY] * extra, out_spec...  34.2 us
    ppermute x42, waiting for transfers between devices, crossed(): lax.ppermute(x, axis, [(i, i ^ mask) for i in range(lax.axis_size(axis))])  18 us
    unnamed x24, local copies, waits for them, and re-layouts  5.78 us
  transfers between devices with their start and end apart: 42, of which 14 were waited for; matrix products, arithmetic and copies ran while one was open for 0% of the time, Pallas kernels for 21%

profile of v4, /device:TPU:0, one launch (start us, length us, event | category | flops | bytes accessed | tf_op | source)
XLA Modules:
  0.0 101.3 jit_solution(12322908431897279002)
XLA Ops:
  0.7 1.2 %copy-done = bf16[1,16,2,128,128]{4,3,2,1,0:T(8,128)(2,1)S(1)} copy-done((bf16[1,16,2,128,128]{4,3,2,1,0:T(8,128)(2,1)S(1)}, bf16[1,16,2,128,128]{4,3,2,1,0:T(8,128)(2,1)}, u32[]{:S(2)}) %copy-start) | copy-done | bytes 1048600
  1.9 0.7 copy-done.4
  2.6 0.7 copy-done.7
  3.3 5.4 %leaf_forward.2 = (bf16[16,256,256]{2,1,0:T(8,128)(2,1)}, bf16[4,2,2,256,128]{4,3,2,1,0:T(8,128)(2,1)S(1)}, bf16[4,2,2,256,128]{4,3,2,1,0:T(8,128)(2,1)S(1)}) custom-call(s32[16]{0:T(128)S(1)} %bitcast.5, s32[2]{0:T(128)S(1)} %pad_add_fusion.refs_1_.refs_0_, bf16[1,2,16,128,512]{4,3,2,1,0:T(8,128)(2,1)} %refs_2_.4, ...), custom_call_target="tpu_custom_call" | custom-call | flops 10000000000 | bytes 1 | tf_op jit(solution)/shard_map/leaf_forward/pallas_call | solution.py:29
  9.2 1.6 %copy-done.10 = bf16[16,256,256]{2,1,0:T(8,128)(2,1)S(1)} copy-done((bf16[16,256,256]{2,1,0:T(8,128)(2,1)S(1)}, bf16[16,256,256]{2,1,0:T(8,128)(2,1)}, u32[]{:S(2)}) %copy-start.10) | copy-done | bytes 2097176
  11.4 2.7 %collective-permute-start.2 = (bf16[272,128]{1,0:T(8,128)(2,1)S(1)}, bf16[272,128]{1,0:T(8,128)(2,1)S(1)}, u32[]{:S(2)}, u32[]{:S(2)}) collective-permute-start(bf16[272,128]{1,0:T(8,128)(2,1)S(1)} %get-tuple-element.46), channel_id=1, source_target_pairs={{0,8},{8,0},{16,24},{24,16},{1,9},{9,1},{17,25},{25,17},{2,10},{10... | collective-permute-start | bytes 208904 | tf_op jit(solution)/shard_map/ppermute | solution.py:43
  14.1 1.6 %collective-permute-start.4 = (bf16[1,2,256,128]{3,2,1,0:T(8,128)(2,1)S(1)}, bf16[1,2,256,128]{3,2,1,0:T(8,128)(2,1)S(1)}, u32[]{:S(2)}, u32[]{:S(2)}) collective-permute-start(bf16[1,2,256,128]{3,2,1,0:T(8,128)(2,1)S(1)} %get-tuple-element.47), channel_id=1, source_target_pairs={{0,4},{1,5},{2,6},{3,7},{4,0},{5,1},{6,2},{7,3},{8,12},{9,13},{10,... | collective-permute-start | bytes 393224 | tf_op jit(solution)/shard_map/ppermute | solution.py:43
  15.7 1.5 %collective-permute-start.3 = (bf16[1,2,256,128]{3,2,1,0:T(8,128)(2,1)S(1)}, bf16[1,2,256,128]{3,2,1,0:T(8,128)(2,1)S(1)}, u32[]{:S(2)}, u32[]{:S(2)}) collective-permute-start(bf16[1,2,256,128]{3,2,1,0:T(8,128)(2,1)S(1)} %get-tuple-element.42.refs_6_), channel_id=1, source_target_pairs={{0,2},{1,3},{2,0},{3,1},{4,6},{5,7},{6,4},{7,5},{8,10},{9,11},{10,... | collective-permute-start | bytes 393224 | tf_op jit(solution)/shard_map/ppermute | solution.py:43
  17.2 5.4 %leaf_forward.3 = (bf16[16,256,256]{2,1,0:T(8,128)(2,1)}, bf16[4,2,2,256,128]{4,3,2,1,0:T(8,128)(2,1)S(1)}, bf16[4,2,2,256,128]{4,3,2,1,0:T(8,128)(2,1)S(1)}) custom-call(s32[16]{0:T(128)S(1)} %bitcast.6, s32[2]{0:T(128)S(1)} %pad_add_fusion.refs_1_.refs_0_, bf16[1,2,16,128,512]{4,3,2,1,0:T(8,128)(2,1)} %refs_2_.4, ...), custom_call_target="tpu_custom_call" | custom-call | flops 10000000000 | bytes 1 | tf_op jit(solution)/shard_map/leaf_forward/pallas_call | solution.py:29
  22.7 1.6 %copy-done.8 = bf16[16,256,256]{2,1,0:T(8,128)(2,1)S(1)} copy-done((bf16[16,256,256]{2,1,0:T(8,128)(2,1)S(1)}, bf16[16,256,256]{2,1,0:T(8,128)(2,1)}, u32[]{:S(2)}) %copy-start.8) | copy-done | bytes 2097176
  24.4 0.6 collective-permute-start.7
  25.1 2.7 %collective-permute-start.14 = (bf16[544,128]{1,0:T(8,128)(2,1)S(1)}, bf16[544,128]{1,0:T(8,128)(2,1)S(1)}, u32[]{:S(2)}, u32[]{:S(2)}) collective-permute-start(bf16[544,128]{1,0:T(8,128)(2,1)S(1)} %solve_join.1.refs_2_), channel_id=1, source_target_pairs={{0,16},{8,24},{16,0},{24,8},{1,17},{9,25},{17,1},{25,9},{2,18},{10... | collective-permute-start | bytes 417800 | tf_op jit(solution)/shard_map/ppermute | solution.py:43
  28.3 1.5 %collective-permute-start.5 = (bf16[1,2,256,128]{3,2,1,0:T(8,128)(2,1)S(1)}, bf16[1,2,256,128]{3,2,1,0:T(8,128)(2,1)S(1)}, u32[]{:S(2)}, u32[]{:S(2)}) collective-permute-start(bf16[1,2,256,128]{3,2,1,0:T(8,128)(2,1)S(1)} %get-tuple-element.49.refs_3_), channel_id=1, source_target_pairs={{0,2},{1,3},{2,0},{3,1},{4,6},{5,7},{6,4},{7,5},{8,10},{9,11},{10,... | collective-permute-start | bytes 393224 | tf_op jit(solution)/shard_map/ppermute | solution.py:43
  29.9 3.5 %leaf_fold.1.refs_6_.refs_3_ = bf16[16,256,512]{2,1,0:T(8,128)(2,1)S(1)} custom-call(bf16[1,16,2,128,128]{4,3,2,1,0:T(8,128)(2,1)S(1)} %copy-done, bf16[1,16,2,128,128]{4,3,2,1,0:T(8,128)(2,1)S(1)} %copy-done.1, s32[1,16,128]{2,1,0:T(8,128)S(1)} %copy-done.5, bf16[1,2,256,128]{3,2,1,0:T(8,128)(2,1)S(1)} %get-tuple-element.49.refs_3_), custom_call_target="tpu_custom_call" | custom-call | flops 10000000000 | bytes 1 | tf_op jit(solution)/shard_map/leaf_fold/pallas_call | solution.py:29
  33.4 1.6 %collective-permute-start.6 = (bf16[1,2,256,128]{3,2,1,0:T(8,128)(2,1)S(1)}, bf16[1,2,256,128]{3,2,1,0:T(8,128)(2,1)S(1)}, u32[]{:S(2)}, u32[]{:S(2)}) collective-permute-start(bf16[1,2,256,128]{3,2,1,0:T(8,128)(2,1)S(1)} %get-tuple-element.50), channel_id=1, source_target_pairs={{0,4},{1,5},{2,6},{3,7},{4,0},{5,1},{6,2},{7,3},{8,12},{9,13},{10,... | collective-permute-start | bytes 393224 | tf_op jit(solution)/shard_map/ppermute | solution.py:43
  35.0 1.2 %collective-permute-done.8.refs_5_ = bf16[2,2,256,128]{3,2,1,0:T(8,128)(2,1)S(1)} collective-permute-done((bf16[2,2,256,128]{3,2,1,0:T(8,128)(2,1)S(1)}, bf16[2,2,256,128]{3,2,1,0:T(8,128)(2,1)S(1)}, u32[]{:S(2)}, u32[]{:S(2)}) %collective-permute-start.8) | collective-permute-done | bytes 262176 | tf_op jit(solution)/shard_map/ppermute | solution.py:43
  36.2 0.8 interface_reduce.2
  37.9 0.8 collective-permute-done.6.refs_3_
  38.7 2.8 %collective-permute-start.13 = (bf16[2,128,128]{2,1,0:T(8,128)(2,1)S(1)}, bf16[2,128,128]{2,1,0:T(8,128)(2,1)S(1)}, u32[]{:S(2)}, u32[]{:S(2)}) collective-permute-start(bf16[2,128,128]{2,1,0:T(8,128)(2,1)S(1)} %get-tuple-element.57), channel_id=1, source_target_pairs={{0,24},{8,16},{16,8},{24,0},{1,25},{9,17},{17,9},{25,1},{2,26},{10... | collective-permute-start | bytes 196616 | tf_op jit(solution)/shard_map/ppermute | solution.py:43
  41.9 1.6 %collective-permute-start.9 = (bf16[2,2,256,128]{3,2,1,0:T(8,128)(2,1)S(1)}, bf16[2,2,256,128]{3,2,1,0:T(8,128)(2,1)S(1)}, u32[]{:S(2)}, u32[]{:S(2)}) collective-permute-start(bf16[2,2,256,128]{3,2,1,0:T(8,128)(2,1)S(1)} %get-tuple-element.53.refs_8_), channel_id=1, source_target_pairs={{0,2},{1,3},{2,0},{3,1},{4,6},{5,7},{6,4},{7,5},{8,10},{9,11},{10,... | collective-permute-start | bytes 786440 | tf_op jit(solution)/shard_map/ppermute | solution.py:43
  43.4 1.3 %collective-permute-done.12.refs_3_ = bf16[2,128,128]{2,1,0:T(8,128)(2,1)S(1)} collective-permute-done((bf16[2,128,128]{2,1,0:T(8,128)(2,1)S(1)}, bf16[2,128,128]{2,1,0:T(8,128)(2,1)S(1)}, u32[]{:S(2)}, u32[]{:S(2)}) %collective-permute-start.12) | collective-permute-done | bytes 65568 | tf_op jit(solution)/shard_map/ppermute | solution.py:43
  44.7 1.9 %sweep_chain.2 = (bf16[2,128,128]{2,1,0:T(8,128)(2,1)S(1)}, bf16[2,128,128]{2,1,0:T(8,128)(2,1)S(1)}, bf16[2,128,128]{2,1,0:T(8,128)(2,1)S(1)}, bf16[2,128,128]{2,1,0:T(8,128)(2,1)S(1)}) custom-call(s32[2]{0:T(128)S(1)} %pad_add_fusion.refs_1_.refs_0_, bf16[2,128,128]{2,1,0:T(8,128)(2,1)S(1)} %get-tuple-element.52.refs_4_.refs_1_, ...), custom_call_target="tpu_custom_call" | custom-call | flops 10000000000 | bytes 1 | tf_op jit(solution)/shard_map/sweep_chain/pallas_call | solution.py:29
  46.7 1.3 %collective-permute-start.18 = (bf16[2,128,128]{2,1,0:T(8,128)(2,1)S(1)}, bf16[2,128,128]{2,1,0:T(8,128)(2,1)S(1)}, u32[]{:S(2)}, u32[]{:S(2)}) collective-permute-start(bf16[2,128,128]{2,1,0:T(8,128)(2,1)S(1)} %get-tuple-element.63), channel_id=1, source_target_pairs={{0,8},{8,0},{16,24},{24,16},{1,9},{9,1},{17,25},{25,17},{2,10},{10... | collective-permute-start | bytes 196616 | tf_op jit(solution)/shard_map/ppermute | solution.py:43
  48.0 2.1 %collective-permute-start.19 = (bf16[2,128,128]{2,1,0:T(8,128)(2,1)S(1)}, bf16[2,128,128]{2,1,0:T(8,128)(2,1)S(1)}, u32[]{:S(2)}, u32[]{:S(2)}) collective-permute-start(bf16[2,128,128]{2,1,0:T(8,128)(2,1)S(1)} %get-tuple-element.64), channel_id=1, source_target_pairs={{0,16},{8,24},{16,0},{24,8},{1,17},{9,25},{17,1},{25,9},{2,18},{10... | collective-permute-start | bytes 196616 | tf_op jit(solution)/shard_map/ppermute | solution.py:43
  50.1 1.0 collective-permute-start.20
  51.1 0.8 interface_reduce.3
  52.4 3.0 %collective-permute-start.16 = (bf16[2,128,128]{2,1,0:T(8,128)(2,1)S(1)}, bf16[2,128,128]{2,1,0:T(8,128)(2,1)S(1)}, u32[]{:S(2)}, u32[]{:S(2)}) collective-permute-start(bf16[2,128,128]{2,1,0:T(8,128)(2,1)S(1)} %get-tuple-element.61), channel_id=1, source_target_pairs={{0,16},{8,24},{16,0},{24,8},{1,17},{9,25},{17,1},{25,9},{2,18},{10... | collective-permute-start | bytes 196616 | tf_op jit(solution)/shard_map/ppermute | solution.py:43
  55.4 1.0 collective-permute-start.17
  56.8 1.5 %interface_collect.2 = (bf16[2,2,256,128]{3,2,1,0:T(8,128)(2,1)S(1)}, f32[1,2,256,512]{3,2,1,0:T(8,128)}) custom-call(s32[2]{0:T(128)S(1)} %pad_add_fusion.refs_1_.refs_0_, bf16[2,128,128]{2,1,0:T(8,128)(2,1)S(1)} %get-tuple-element.58.refs_6_.refs_1_, bf16[2,128,128]{2,1,0:T(8,128)(2,1)S(1)} %collective-permute-done.18.refs_2_, ...), custom_call_target="tpu_custom_call" | custom-call | flops 10000000000 | bytes 1 | tf_op jit(solution)/shard_map/interface_collect/pallas_call | solution.py:29
  58.3 1.2 %collective-permute-done.16.refs_3_ = bf16[2,128,128]{2,1,0:T(8,128)(2,1)S(1)} collective-permute-done((bf16[2,128,128]{2,1,0:T(8,128)(2,1)S(1)}, bf16[2,128,128]{2,1,0:T(8,128)(2,1)S(1)}, u32[]{:S(2)}, u32[]{:S(2)}) %collective-permute-start.16) | collective-permute-done | bytes 65568 | tf_op jit(solution)/shard_map/ppermute | solution.py:43
  59.5 1.9 %collective-permute-done.17.refs_4_ = bf16[2,128,128]{2,1,0:T(8,128)(2,1)S(1)} collective-permute-done((bf16[2,128,128]{2,1,0:T(8,128)(2,1)S(1)}, bf16[2,128,128]{2,1,0:T(8,128)(2,1)S(1)}, u32[]{:S(2)}, u32[]{:S(2)}) %collective-permute-start.17) | collective-permute-done | bytes 65568 | tf_op jit(solution)/shard_map/ppermute | solution.py:43
  61.5 1.9 %sweep_chain.3 = (bf16[2,128,128]{2,1,0:T(8,128)(2,1)S(1)}, bf16[2,128,128]{2,1,0:T(8,128)(2,1)S(1)}, bf16[2,128,128]{2,1,0:T(8,128)(2,1)S(1)}, bf16[2,128,128]{2,1,0:T(8,128)(2,1)S(1)}) custom-call(s32[2]{0:T(128)S(1)} %pad_add_fusion.refs_1_.refs_0_, bf16[2,128,128]{2,1,0:T(8,128)(2,1)S(1)} %get-tuple-element.59.refs_5_.refs_1_, ...), custom_call_target="tpu_custom_call" | custom-call | flops 10000000000 | bytes 1 | tf_op jit(solution)/shard_map/sweep_chain/pallas_call | solution.py:29
  63.5 1.6 %collective-permute-start.22 = (bf16[2,128,128]{2,1,0:T(8,128)(2,1)S(1)}, bf16[2,128,128]{2,1,0:T(8,128)(2,1)S(1)}, u32[]{:S(2)}, u32[]{:S(2)}) collective-permute-start(bf16[2,128,128]{2,1,0:T(8,128)(2,1)S(1)} %get-tuple-element.69), channel_id=1, source_target_pairs={{0,16},{8,24},{16,0},{24,8},{1,17},{9,25},{17,1},{25,9},{2,18},{10... | collective-permute-start | bytes 196616 | tf_op jit(solution)/shard_map/ppermute | solution.py:43
  65.1 2.8 %collective-permute-start.23 = (bf16[2,128,128]{2,1,0:T(8,128)(2,1)S(1)}, bf16[2,128,128]{2,1,0:T(8,128)(2,1)S(1)}, u32[]{:S(2)}, u32[]{:S(2)}) collective-permute-start(bf16[2,128,128]{2,1,0:T(8,128)(2,1)S(1)} %get-tuple-element.70), channel_id=1, source_target_pairs={{0,24},{8,16},{16,8},{24,0},{1,25},{9,17},{17,9},{25,1},{2,26},{10... | collective-permute-start | bytes 196616 | tf_op jit(solution)/shard_map/ppermute | solution.py:43
  68.0 1.5 %collective-permute-start.34 = (bf16[2,2,256,128]{3,2,1,0:T(8,128)(2,1)S(1)}, bf16[2,2,256,128]{3,2,1,0:T(8,128)(2,1)S(1)}, u32[]{:S(2)}, u32[]{:S(2)}) collective-permute-start(bf16[2,2,256,128]{3,2,1,0:T(8,128)(2,1)S(1)} %get-tuple-element.66.refs_8_.refs_4_), channel_id=1, source_target_pairs={{0,2},{1,3},{2,0},{3,1},{4,6},{5,7},{6,4},{7,5},{8,10},{9,11},{10,... | collective-permute-start | bytes 786440 | tf_op jit(solution)/shard_map/ppermute | solution.py:43
  69.5 1.7 %collective-permute-done.23.refs_4_ = bf16[2,128,128]{2,1,0:T(8,128)(2,1)S(1)} collective-permute-done((bf16[2,128,128]{2,1,0:T(8,128)(2,1)S(1)}, bf16[2,128,128]{2,1,0:T(8,128)(2,1)S(1)}, u32[]{:S(2)}, u32[]{:S(2)}) %collective-permute-start.23) | collective-permute-done | bytes 65568 | tf_op jit(solution)/shard_map/ppermute | solution.py:43
  71.1 1.5 %interface_collect.3 = (bf16[2,2,256,128]{3,2,1,0:T(8,128)(2,1)S(1)}, f32[1,2,256,512]{3,2,1,0:T(8,128)}) custom-call(s32[2]{0:T(128)S(1)} %pad_add_fusion.refs_1_.refs_0_, bf16[2,128,128]{2,1,0:T(8,128)(2,1)S(1)} %get-tuple-element.67.refs_1_, bf16[2,128,128]{2,1,0:T(8,128)(2,1)S(1)} %collective-permute-done.21.refs_2_, ...), custom_call_target="tpu_custom_call", output_to_operand_aliasing={{1}: (5, {})} | custom-call | flops 10000000000 | bytes 1 | tf_op jit(solution)/shard_map/interface_collect/pallas_call | solution.py:29
  72.7 1.3 %collective-permute-start.27 = (bf16[2,2,256,128]{3,2,1,0:T(8,128)(2,1)S(1)}, bf16[2,2,256,128]{3,2,1,0:T(8,128)(2,1)S(1)}, u32[]{:S(2)}, u32[]{:S(2)}) collective-permute-start(bf16[2,2,256,128]{3,2,1,0:T(8,128)(2,1)S(1)} %get-tuple-element.72.refs_14_.refs_4_), channel_id=1, source_target_pairs={{0,4},{1,5},{2,6},{3,7},{4,0},{5,1},{6,2},{7,3},{8,12},{9,13},{10,... | collective-permute-start | bytes 786440 | tf_op jit(solution)/shard_map/ppermute | solution.py:43
  73.9 1.2 %collective-permute-start.25 = (bf16[2,2,256,128]{3,2,1,0:T(8,128)(2,1)S(1)}, bf16[2,2,256,128]{3,2,1,0:T(8,128)(2,1)S(1)}, u32[]{:S(2)}, u32[]{:S(2)}) collective-permute-start(bf16[2,2,256,128]{3,2,1,0:T(8,128)(2,1)S(1)} %get-tuple-element.72.refs_14_.refs_4_), channel_id=1, source_target_pairs={{0,2},{1,3},{2,0},{3,1},{4,6},{5,7},{6,4},{7,5},{8,10},{9,11},{10,... | collective-permute-start | bytes 786440 | tf_op jit(solution)/shard_map/ppermute | solution.py:43
  75.2 1.0 %collective-permute-done.36.refs_8_ = bf16[2,2,256,128]{3,2,1,0:T(8,128)(2,1)S(1)} collective-permute-done((bf16[2,2,256,128]{3,2,1,0:T(8,128)(2,1)S(1)}, bf16[2,2,256,128]{3,2,1,0:T(8,128)(2,1)S(1)}, u32[]{:S(2)}, u32[]{:S(2)}) %collective-permute-start.36) | collective-permute-done | bytes 262176 | tf_op jit(solution)/shard_map/ppermute | solution.py:43
  76.8 2.3 %collective-permute-done.27.refs_8_ = bf16[2,2,256,128]{3,2,1,0:T(8,128)(2,1)S(1)} collective-permute-done((bf16[2,2,256,128]{3,2,1,0:T(8,128)(2,1)S(1)}, bf16[2,2,256,128]{3,2,1,0:T(8,128)(2,1)S(1)}, u32[]{:S(2)}, u32[]{:S(2)}) %collective-permute-start.27) | collective-permute-done | bytes 262176 | tf_op jit(solution)/shard_map/ppermute | solution.py:43
  79.1 1.7 %collective-permute-start.39 = (bf16[1,2,256,128]{3,2,1,0:T(8,128)(2,1)S(1)}, bf16[1,2,256,128]{3,2,1,0:T(8,128)(2,1)S(1)}, u32[]{:S(2)}, u32[]{:S(2)}) collective-permute-start(bf16[1,2,256,128]{3,2,1,0:T(8,128)(2,1)S(1)} %slice.19), channel_id=1, source_target_pairs={{0,2},{1,3},{2,0},{3,1},{4,6},{5,7},{6,4},{7,5},{8,10},{9,11},{10,... | collective-permute-start | bytes 393224 | tf_op jit(solution)/shard_map/ppermute | solution.py:43
  81.6 1.4 %collective-permute-start.30 = (bf16[1,2,256,128]{3,2,1,0:T(8,128)(2,1)S(1)}, bf16[1,2,256,128]{3,2,1,0:T(8,128)(2,1)S(1)}, u32[]{:S(2)}, u32[]{:S(2)}) collective-permute-start(bf16[1,2,256,128]{3,2,1,0:T(8,128)(2,1)S(1)} %slice.17), channel_id=1, source_target_pairs={{0,2},{1,3},{2,0},{3,1},{4,6},{5,7},{6,4},{7,5},{8,10},{9,11},{10,... | collective-permute-start | bytes 393224 | tf_op jit(solution)/shard_map/ppermute | solution.py:43
  83.0 2.2 %collective-permute-done.39.refs_11_ = bf16[1,2,256,128]{3,2,1,0:T(8,128)(2,1)S(1)} collective-permute-done((bf16[1,2,256,128]{3,2,1,0:T(8,128)(2,1)S(1)}, bf16[1,2,256,128]{3,2,1,0:T(8,128)(2,1)S(1)}, u32[]{:S(2)}, u32[]{:S(2)}) %collective-permute-start.39) | collective-permute-done | bytes 131104 | tf_op jit(solution)/shard_map/ppermute | solution.py:43
  85.6 1.4 %collective-permute-done.38.refs_10_ = bf16[1,2,256,128]{3,2,1,0:T(8,128)(2,1)S(1)} collective-permute-done((bf16[1,2,256,128]{3,2,1,0:T(8,128)(2,1)S(1)}, bf16[1,2,256,128]{3,2,1,0:T(8,128)(2,1)S(1)}, u32[]{:S(2)}, u32[]{:S(2)}) %collective-permute-start.38) | collective-permute-done | bytes 131104 | tf_op jit(solution)/shard_map/ppermute | solution.py:43
  88.0 2.2 %collective-permute-done.29.refs_10_ = bf16[1,2,256,128]{3,2,1,0:T(8,128)(2,1)S(1)} collective-permute-done((bf16[1,2,256,128]{3,2,1,0:T(8,128)(2,1)S(1)}, bf16[1,2,256,128]{3,2,1,0:T(8,128)(2,1)S(1)}, u32[]{:S(2)}, u32[]{:S(2)}) %collective-permute-start.29) | collective-permute-done | bytes 131104 | tf_op jit(solution)/shard_map/ppermute | solution.py:43
  90.7 5.2 %leaf_backward.2.refs_14_ = bf16[1,2,16,128,512]{4,3,2,1,0:T(8,128)(2,1)} custom-call(s32[16]{0:T(128)S(1)} %bitcast.7, s32[2]{0:T(128)S(1)} %pad_add_fusion.refs_1_.refs_0_, bf16[16,256,256]{2,1,0:T(8,128)(2,1)S(1)} %copy-done.11, bf16[16,256,512]{2,1,0:T(8,128)(2,1)S(1)} %leaf_fold.1.refs_6_.refs_3_, ...), custom_call_target="tpu_custom_call" | custom-call | flops 10000000000 | bytes 1 | tf_op jit(solution)/shard_map/leaf_backward/pallas_call | solution.py:29
  96.0 5.2 %leaf_backward.3 = bf16[1,2,16,128,512]{4,3,2,1,0:T(8,128)(2,1)} custom-call(s32[16]{0:T(128)S(1)} %bitcast.8, s32[2]{0:T(128)S(1)} %pad_add_fusion.refs_1_.refs_0_, bf16[16,256,256]{2,1,0:T(8,128)(2,1)S(1)} %copy-done.9, bf16[16,256,512]{2,1,0:T(8,128)(2,1)S(1)} %leaf_fold.1.refs_6_.refs_3_, ...), custom_call_target="tpu_custom_call", output_to_operand_aliasing={{}: (14, {})} | custom-call | flops 10000000000 | bytes 1 | tf_op jit(solution)/shard_map/leaf_backward/pallas_call | solution.py:29
  (82 shorter events, 7.8 us)
Async XLA Ops:
  3.3 5.9 %copy-start.3 = (f32[1,2,2,128,128]{4,3,2,1,0:T(8,128)S(1)}, f32[1,2,2,128,128]{4,3,2,1,0:T(8,128)}, u32[]{:S(2)}) copy-start(f32[1,2,2,128,128]{4,3,2,1,0:T(8,128)} %refs_1_.4) | copy-start | bytes 786436
  3.3 5.9 %copy-start.6 = (f32[1,256]{1,0:T(1,128)S(1)}, f32[1,256]{1,0:T(1,128)}, u32[]{:S(2)}) copy-start(f32[1,256]{1,0:T(1,128)} %param.15) | copy-start | bytes 3076
  8.7 5.4 %collective-permute-start = (bf16[4,2,2,256,128]{4,3,2,1,0:T(8,128)(2,1)S(1)}, bf16[4,2,2,256,128]{4,3,2,1,0:T(8,128)(2,1)S(1)}, u32[]{:S(2)}, u32[]{:S(2)}) collective-permute-start(bf16[4,2,2,256,128]{4,3,2,1,0:T(8,128)(2,1)S(1)} %get-tuple-element.39), channel_id=1, source_target_pairs={{0,1},{1,0},{2,3},{3,2},{4,5},{5,4},{6,7},{7,6},{8,9},{9,8},{10,11... | collective-permute-start | bytes 3145736 | tf_op jit(solution)/shard_map/ppermute | solution.py:43
  11.4 13.7 %collective-permute-start.2 = (bf16[272,128]{1,0:T(8,128)(2,1)S(1)}, bf16[272,128]{1,0:T(8,128)(2,1)S(1)}, u32[]{:S(2)}, u32[]{:S(2)}) collective-permute-start(bf16[272,128]{1,0:T(8,128)(2,1)S(1)} %get-tuple-element.46), channel_id=1, source_target_pairs={{0,8},{8,0},{16,24},{24,16},{1,9},{9,1},{17,25},{25,17},{2,10},{10... | collective-permute-start | bytes 208904 | tf_op jit(solution)/shard_map/ppermute | solution.py:43
  14.1 8.6 %collective-permute-start.4 = (bf16[1,2,256,128]{3,2,1,0:T(8,128)(2,1)S(1)}, bf16[1,2,256,128]{3,2,1,0:T(8,128)(2,1)S(1)}, u32[]{:S(2)}, u32[]{:S(2)}) collective-permute-start(bf16[1,2,256,128]{3,2,1,0:T(8,128)(2,1)S(1)} %get-tuple-element.47), channel_id=1, source_target_pairs={{0,4},{1,5},{2,6},{3,7},{4,0},{5,1},{6,2},{7,3},{8,12},{9,13},{10,... | collective-permute-start | bytes 393224 | tf_op jit(solution)/shard_map/ppermute | solution.py:43
  15.7 7.0 %collective-permute-start.3 = (bf16[1,2,256,128]{3,2,1,0:T(8,128)(2,1)S(1)}, bf16[1,2,256,128]{3,2,1,0:T(8,128)(2,1)S(1)}, u32[]{:S(2)}, u32[]{:S(2)}) collective-permute-start(bf16[1,2,256,128]{3,2,1,0:T(8,128)(2,1)S(1)} %get-tuple-element.42.refs_6_), channel_id=1, source_target_pairs={{0,2},{1,3},{2,0},{3,1},{4,6},{5,7},{6,4},{7,5},{8,10},{9,11},{10,... | collective-permute-start | bytes 393224 | tf_op jit(solution)/shard_map/ppermute | solution.py:43
  22.6 5.7 %collective-permute-start.1 = (bf16[4,2,2,256,128]{4,3,2,1,0:T(8,128)(2,1)S(1)}, bf16[4,2,2,256,128]{4,3,2,1,0:T(8,128)(2,1)S(1)}, u32[]{:S(2)}, u32[]{:S(2)}) collective-permute-start(bf16[4,2,2,256,128]{4,3,2,1,0:T(8,128)(2,1)S(1)} %get-tuple-element.45), channel_id=1, source_target_pairs={{0,1},{1,0},{2,3},{3,2},{4,5},{5,4},{6,7},{7,6},{8,9},{9,8},{10,11... | collective-permute-start | bytes 3145736 | tf_op jit(solution)/shard_map/ppermute | solution.py:43
  24.4 11.8 %collective-permute-start.7 = (bf16[2,2,256,128]{3,2,1,0:T(8,128)(2,1)S(1)}, bf16[2,2,256,128]{3,2,1,0:T(8,128)(2,1)S(1)}, u32[]{:S(2)}, u32[]{:S(2)}) collective-permute-start(bf16[2,2,256,128]{3,2,1,0:T(8,128)(2,1)S(1)} %get-tuple-element.48.refs_2_), channel_id=1, source_target_pairs={{0,2},{1,3},{2,0},{3,1},{4,6},{5,7},{6,4},{7,5},{8,10},{9,11},{10,... | collective-permute-start | bytes 786440 | tf_op jit(solution)/shard_map/ppermute | solution.py:43
  25.1 16.8 %collective-permute-start.14 = (bf16[544,128]{1,0:T(8,128)(2,1)S(1)}, bf16[544,128]{1,0:T(8,128)(2,1)S(1)}, u32[]{:S(2)}, u32[]{:S(2)}) collective-permute-start(bf16[544,128]{1,0:T(8,128)(2,1)S(1)} %solve_join.1.refs_2_), channel_id=1, source_target_pairs={{0,16},{8,24},{16,0},{24,8},{1,17},{9,25},{17,1},{25,9},{2,18},{10... | collective-permute-start | bytes 417800 | tf_op jit(solution)/shard_map/ppermute | solution.py:43
  27.7 8.5 %collective-permute-start.8 = (bf16[2,2,256,128]{3,2,1,0:T(8,128)(2,1)S(1)}, bf16[2,2,256,128]{3,2,1,0:T(8,128)(2,1)S(1)}, u32[]{:S(2)}, u32[]{:S(2)}) collective-permute-start(bf16[2,2,256,128]{3,2,1,0:T(8,128)(2,1)S(1)} %get-tuple-element.51), channel_id=1, source_target_pairs={{0,4},{1,5},{2,6},{3,7},{4,0},{5,1},{6,2},{7,3},{8,12},{9,13},{10,... | collective-permute-start | bytes 786440 | tf_op jit(solution)/shard_map/ppermute | solution.py:43
  28.2 1.6 %copy-start.5 = (s32[1,16,128]{2,1,0:T(8,128)S(1)}, s32[1,16,128]{2,1,0:T(8,128)}, u32[]{:S(2)}) copy-start(s32[1,16,128]{2,1,0:T(8,128)} %refs_2_.5) | copy-start | bytes 24580
  28.3 7.9 %copy-start.2 = (bf16[1,2,256,512]{3,2,1,0:T(8,128)(2,1)S(1)}, bf16[1,2,256,512]{3,2,1,0:T(8,128)(2,1)}, u32[]{:S(2)}) copy-start(bf16[1,2,256,512]{3,2,1,0:T(8,128)(2,1)} %refs_1_.7) | copy-start | bytes 1572868
  28.3 13.2 %collective-permute-start.5 = (bf16[1,2,256,128]{3,2,1,0:T(8,128)(2,1)S(1)}, bf16[1,2,256,128]{3,2,1,0:T(8,128)(2,1)S(1)}, u32[]{:S(2)}, u32[]{:S(2)}) collective-permute-start(bf16[1,2,256,128]{3,2,1,0:T(8,128)(2,1)S(1)} %get-tuple-element.49.refs_3_), channel_id=1, source_target_pairs={{0,2},{1,3},{2,0},{3,1},{4,6},{5,7},{6,4},{7,5},{8,10},{9,11},{10,... | collective-permute-start | bytes 393224 | tf_op jit(solution)/shard_map/ppermute | solution.py:43
  33.4 5.3 %collective-permute-start.6 = (bf16[1,2,256,128]{3,2,1,0:T(8,128)(2,1)S(1)}, bf16[1,2,256,128]{3,2,1,0:T(8,128)(2,1)S(1)}, u32[]{:S(2)}, u32[]{:S(2)}) collective-permute-start(bf16[1,2,256,128]{3,2,1,0:T(8,128)(2,1)S(1)} %get-tuple-element.50), channel_id=1, source_target_pairs={{0,4},{1,5},{2,6},{3,7},{4,0},{5,1},{6,2},{7,3},{8,12},{9,13},{10,... | collective-permute-start | bytes 393224 | tf_op jit(solution)/shard_map/ppermute | solution.py:43
  37.0 6.4 %collective-permute-start.11 = (bf16[2,128,128]{2,1,0:T(8,128)(2,1)S(1)}, bf16[2,128,128]{2,1,0:T(8,128)(2,1)S(1)}, u32[]{:S(2)}, u32[]{:S(2)}) collective-permute-start(bf16[2,128,128]{2,1,0:T(8,128)(2,1)S(1)} %get-tuple-element.55), channel_id=1, source_target_pairs={{0,8},{8,0},{16,24},{24,16},{1,9},{9,1},{17,25},{25,17},{2,10},{10... | collective-permute-start | bytes 196616 | tf_op jit(solution)/shard_map/ppermute | solution.py:43
  37.5 7.2 %collective-permute-start.12 = (bf16[2,128,128]{2,1,0:T(8,128)(2,1)S(1)}, bf16[2,128,128]{2,1,0:T(8,128)(2,1)S(1)}, u32[]{:S(2)}, u32[]{:S(2)}) collective-permute-start(bf16[2,128,128]{2,1,0:T(8,128)(2,1)S(1)} %get-tuple-element.56), channel_id=1, source_target_pairs={{0,16},{8,24},{16,0},{24,8},{1,17},{9,25},{17,1},{25,9},{2,18},{10... | collective-permute-start | bytes 196616 | tf_op jit(solution)/shard_map/ppermute | solution.py:43
  38.7 6.1 %collective-permute-start.13 = (bf16[2,128,128]{2,1,0:T(8,128)(2,1)S(1)}, bf16[2,128,128]{2,1,0:T(8,128)(2,1)S(1)}, u32[]{:S(2)}, u32[]{:S(2)}) collective-permute-start(bf16[2,128,128]{2,1,0:T(8,128)(2,1)S(1)} %get-tuple-element.57), channel_id=1, source_target_pairs={{0,24},{8,16},{16,8},{24,0},{1,25},{9,17},{17,9},{25,1},{2,26},{10... | collective-permute-start | bytes 196616 | tf_op jit(solution)/shard_map/ppermute | solution.py:43
  41.7 9.5 %collective-permute-start.10 = (bf16[2,2,256,128]{3,2,1,0:T(8,128)(2,1)S(1)}, bf16[2,2,256,128]{3,2,1,0:T(8,128)(2,1)S(1)}, u32[]{:S(2)}, u32[]{:S(2)}) collective-permute-start(bf16[2,2,256,128]{3,2,1,0:T(8,128)(2,1)S(1)} %get-tuple-element.54), channel_id=1, source_target_pairs={{0,4},{1,5},{2,6},{3,7},{4,0},{5,1},{6,2},{7,3},{8,12},{9,13},{10,... | collective-permute-start | bytes 786440 | tf_op jit(solution)/shard_map/ppermute | solution.py:43
  41.9 9.3 %collective-permute-start.9 = (bf16[2,2,256,128]{3,2,1,0:T(8,128)(2,1)S(1)}, bf16[2,2,256,128]{3,2,1,0:T(8,128)(2,1)S(1)}, u32[]{:S(2)}, u32[]{:S(2)}) collective-permute-start(bf16[2,2,256,128]{3,2,1,0:T(8,128)(2,1)S(1)} %get-tuple-element.53.refs_8_), channel_id=1, source_target_pairs={{0,2},{1,3},{2,0},{3,1},{4,6},{5,7},{6,4},{7,5},{8,10},{9,11},{10,... | collective-permute-start | bytes 786440 | tf_op jit(solution)/shard_map/ppermute | solution.py:43
  46.7 8.7 %collective-permute-start.18 = (bf16[2,128,128]{2,1,0:T(8,128)(2,1)S(1)}, bf16[2,128,128]{2,1,0:T(8,128)(2,1)S(1)}, u32[]{:S(2)}, u32[]{:S(2)}) collective-permute-start(bf16[2,128,128]{2,1,0:T(8,128)(2,1)S(1)} %get-tuple-element.63), channel_id=1, source_target_pairs={{0,8},{8,0},{16,24},{24,16},{1,9},{9,1},{17,25},{25,17},{2,10},{10... | collective-permute-start | bytes 196616 | tf_op jit(solution)/shard_map/ppermute | solution.py:43
  48.0 8.4 %collective-permute-start.19 = (bf16[2,128,128]{2,1,0:T(8,128)(2,1)S(1)}, bf16[2,128,128]{2,1,0:T(8,128)(2,1)S(1)}, u32[]{:S(2)}, u32[]{:S(2)}) collective-permute-start(bf16[2,128,128]{2,1,0:T(8,128)(2,1)S(1)} %get-tuple-element.64), channel_id=1, source_target_pairs={{0,16},{8,24},{16,0},{24,8},{1,17},{9,25},{17,1},{25,9},{2,18},{10... | collective-permute-start | bytes 196616 | tf_op jit(solution)/shard_map/ppermute | solution.py:43
  50.1 6.7 %collective-permute-start.20 = (bf16[2,128,128]{2,1,0:T(8,128)(2,1)S(1)}, bf16[2,128,128]{2,1,0:T(8,128)(2,1)S(1)}, u32[]{:S(2)}, u32[]{:S(2)}) collective-permute-start(bf16[2,128,128]{2,1,0:T(8,128)(2,1)S(1)} %get-tuple-element.65), channel_id=1, source_target_pairs={{0,24},{8,16},{16,8},{24,0},{1,25},{9,17},{17,9},{25,1},{2,26},{10... | collective-permute-start | bytes 196616 | tf_op jit(solution)/shard_map/ppermute | solution.py:43
  51.9 6.4 %collective-permute-start.15 = (bf16[2,128,128]{2,1,0:T(8,128)(2,1)S(1)}, bf16[2,128,128]{2,1,0:T(8,128)(2,1)S(1)}, u32[]{:S(2)}, u32[]{:S(2)}) collective-permute-start(bf16[2,128,128]{2,1,0:T(8,128)(2,1)S(1)} %get-tuple-element.60), channel_id=1, source_target_pairs={{0,8},{8,0},{16,24},{24,16},{1,9},{9,1},{17,25},{25,17},{2,10},{10... | collective-permute-start | bytes 196616 | tf_op jit(solution)/shard_map/ppermute | solution.py:43
  52.4 7.2 %collective-permute-start.16 = (bf16[2,128,128]{2,1,0:T(8,128)(2,1)S(1)}, bf16[2,128,128]{2,1,0:T(8,128)(2,1)S(1)}, u32[]{:S(2)}, u32[]{:S(2)}) collective-permute-start(bf16[2,128,128]{2,1,0:T(8,128)(2,1)S(1)} %get-tuple-element.61), channel_id=1, source_target_pairs={{0,16},{8,24},{16,0},{24,8},{1,17},{9,25},{17,1},{25,9},{2,18},{10... | collective-permute-start | bytes 196616 | tf_op jit(solution)/shard_map/ppermute | solution.py:43
  55.4 6.1 %collective-permute-start.17 = (bf16[2,128,128]{2,1,0:T(8,128)(2,1)S(1)}, bf16[2,128,128]{2,1,0:T(8,128)(2,1)S(1)}, u32[]{:S(2)}, u32[]{:S(2)}) collective-permute-start(bf16[2,128,128]{2,1,0:T(8,128)(2,1)S(1)} %get-tuple-element.62), channel_id=1, source_target_pairs={{0,24},{8,16},{16,8},{24,0},{1,25},{9,17},{17,9},{25,1},{2,26},{10... | collective-permute-start | bytes 196616 | tf_op jit(solution)/shard_map/ppermute | solution.py:43
  63.4 6.1 %collective-permute-start.21 = (bf16[2,128,128]{2,1,0:T(8,128)(2,1)S(1)}, bf16[2,128,128]{2,1,0:T(8,128)(2,1)S(1)}, u32[]{:S(2)}, u32[]{:S(2)}) collective-permute-start(bf16[2,128,128]{2,1,0:T(8,128)(2,1)S(1)} %get-tuple-element.68), channel_id=1, source_target_pairs={{0,8},{8,0},{16,24},{24,16},{1,9},{9,1},{17,25},{25,17},{2,10},{10... | collective-permute-start | bytes 196616 | tf_op jit(solution)/shard_map/ppermute | solution.py:43
  63.5 6.0 %collective-permute-start.22 = (bf16[2,128,128]{2,1,0:T(8,128)(2,1)S(1)}, bf16[2,128,128]{2,1,0:T(8,128)(2,1)S(1)}, u32[]{:S(2)}, u32[]{:S(2)}) collective-permute-start(bf16[2,128,128]{2,1,0:T(8,128)(2,1)S(1)} %get-tuple-element.69), channel_id=1, source_target_pairs={{0,16},{8,24},{16,0},{24,8},{1,17},{9,25},{17,1},{25,9},{2,18},{10... | collective-permute-start | bytes 196616 | tf_op jit(solution)/shard_map/ppermute | solution.py:43
  65.1 6.1 %collective-permute-start.23 = (bf16[2,128,128]{2,1,0:T(8,128)(2,1)S(1)}, bf16[2,128,128]{2,1,0:T(8,128)(2,1)S(1)}, u32[]{:S(2)}, u32[]{:S(2)}) collective-permute-start(bf16[2,128,128]{2,1,0:T(8,128)(2,1)S(1)} %get-tuple-element.70), channel_id=1, source_target_pairs={{0,24},{8,16},{16,8},{24,0},{1,25},{9,17},{17,9},{25,1},{2,26},{10... | collective-permute-start | bytes 196616 | tf_op jit(solution)/shard_map/ppermute | solution.py:43
  67.8 8.4 %collective-permute-start.36 = (bf16[2,2,256,128]{3,2,1,0:T(8,128)(2,1)S(1)}, bf16[2,2,256,128]{3,2,1,0:T(8,128)(2,1)S(1)}, u32[]{:S(2)}, u32[]{:S(2)}) collective-permute-start(bf16[2,2,256,128]{3,2,1,0:T(8,128)(2,1)S(1)} %get-tuple-element.66.refs_8_.refs_4_), channel_id=1, source_target_pairs={{0,4},{1,5},{2,6},{3,7},{4,0},{5,1},{6,2},{7,3},{8,12},{9,13},{10,... | collective-permute-start | bytes 786440 | tf_op jit(solution)/shard_map/ppermute | solution.py:43
  68.0 8.3 %collective-permute-start.34 = (bf16[2,2,256,128]{3,2,1,0:T(8,128)(2,1)S(1)}, bf16[2,2,256,128]{3,2,1,0:T(8,128)(2,1)S(1)}, u32[]{:S(2)}, u32[]{:S(2)}) collective-permute-start(bf16[2,2,256,128]{3,2,1,0:T(8,128)(2,1)S(1)} %get-tuple-element.66.refs_8_.refs_4_), channel_id=1, source_target_pairs={{0,2},{1,3},{2,0},{3,1},{4,6},{5,7},{6,4},{7,5},{8,10},{9,11},{10,... | collective-permute-start | bytes 786440 | tf_op jit(solution)/shard_map/ppermute | solution.py:43
  71.1 19.6 %copy-start.11 = (bf16[16,256,256]{2,1,0:T(8,128)(2,1)S(1)}, bf16[16,256,256]{2,1,0:T(8,128)(2,1)}, u32[]{:S(2)}) copy-start(bf16[16,256,256]{2,1,0:T(8,128)(2,1)} %get-tuple-element.40.refs_3_.refs_2_) | copy-start | bytes 6291460
  72.7 6.4 %collective-permute-start.27 = (bf16[2,2,256,128]{3,2,1,0:T(8,128)(2,1)S(1)}, bf16[2,2,256,128]{3,2,1,0:T(8,128)(2,1)S(1)}, u32[]{:S(2)}, u32[]{:S(2)}) collective-permute-start(bf16[2,2,256,128]{3,2,1,0:T(8,128)(2,1)S(1)} %get-tuple-element.72.refs_14_.refs_4_), channel_id=1, source_target_pairs={{0,4},{1,5},{2,6},{3,7},{4,0},{5,1},{6,2},{7,3},{8,12},{9,13},{10,... | collective-permute-start | bytes 786440 | tf_op jit(solution)/shard_map/ppermute | solution.py:43
  73.9 7.1 %collective-permute-start.25 = (bf16[2,2,256,128]{3,2,1,0:T(8,128)(2,1)S(1)}, bf16[2,2,256,128]{3,2,1,0:T(8,128)(2,1)S(1)}, u32[]{:S(2)}, u32[]{:S(2)}) collective-permute-start(bf16[2,2,256,128]{3,2,1,0:T(8,128)(2,1)S(1)} %get-tuple-element.72.refs_14_.refs_4_), channel_id=1, source_target_pairs={{0,2},{1,3},{2,0},{3,1},{4,6},{5,7},{6,4},{7,5},{8,10},{9,11},{10,... | collective-permute-start | bytes 786440 | tf_op jit(solution)/shard_map/ppermute | solution.py:43
  75.2 6.4 %collective-permute-start.33 = (bf16[2,2,256,128]{3,2,1,0:T(8,128)(2,1)S(1)}, bf16[2,2,256,128]{3,2,1,0:T(8,128)(2,1)S(1)}, u32[]{:S(2)}, u32[]{:S(2)}) collective-permute-start(bf16[2,2,256,128]{3,2,1,0:T(8,128)(2,1)S(1)} %get-tuple-element.66.refs_8_.refs_4_), channel_id=1, source_target_pairs={{0,1},{1,0},{2,3},{3,2},{4,5},{5,4},{6,7},{7,6},{8,9},{9,8},{10,11... | collective-permute-start | bytes 786440 | tf_op jit(solution)/shard_map/ppermute | solution.py:43
  76.2 10.7 %collective-permute-start.37 = (bf16[2,2,256,128]{3,2,1,0:T(8,128)(2,1)S(1)}, bf16[2,2,256,128]{3,2,1,0:T(8,128)(2,1)S(1)}, u32[]{:S(2)}, u32[]{:S(2)}) collective-permute-start(bf16[2,2,256,128]{3,2,1,0:T(8,128)(2,1)S(1)} %collective-permute-done.36.refs_8_), channel_id=1, source_target_pairs={{0,1},{1,0},{2,3},{3,2},{4,5},{5,4},{6,7},{7,6},{8,9},{9,8},{10,11... | collective-permute-start | bytes 786440 | tf_op jit(solution)/shard_map/ppermute | solution.py:43
  76.3 11.2 %collective-permute-start.35 = (bf16[2,2,256,128]{3,2,1,0:T(8,128)(2,1)S(1)}, bf16[2,2,256,128]{3,2,1,0:T(8,128)(2,1)S(1)}, u32[]{:S(2)}, u32[]{:S(2)}) collective-permute-start(bf16[2,2,256,128]{3,2,1,0:T(8,128)(2,1)S(1)} %collective-permute-done.34.refs_6_), channel_id=1, source_target_pairs={{0,1},{1,0},{2,3},{3,2},{4,5},{5,4},{6,7},{7,6},{8,9},{9,8},{10,11... | collective-permute-start | bytes 786440 | tf_op jit(solution)/shard_map/ppermute | solution.py:43
  79.1 6.1 %collective-permute-start.39 = (bf16[1,2,256,128]{3,2,1,0:T(8,128)(2,1)S(1)}, bf16[1,2,256,128]{3,2,1,0:T(8,128)(2,1)S(1)}, u32[]{:S(2)}, u32[]{:S(2)}) collective-permute-start(bf16[1,2,256,128]{3,2,1,0:T(8,128)(2,1)S(1)} %slice.19), channel_id=1, source_target_pairs={{0,2},{1,3},{2,0},{3,1},{4,6},{5,7},{6,4},{7,5},{8,10},{9,11},{10,... | collective-permute-start | bytes 393224 | tf_op jit(solution)/shard_map/ppermute | solution.py:43
  81.0 5.9 %collective-permute-start.38 = (bf16[1,2,256,128]{3,2,1,0:T(8,128)(2,1)S(1)}, bf16[1,2,256,128]{3,2,1,0:T(8,128)(2,1)S(1)}, u32[]{:S(2)}, u32[]{:S(2)}) collective-permute-start(bf16[1,2,256,128]{3,2,1,0:T(8,128)(2,1)S(1)} %slice.18), channel_id=1, source_target_pairs={{0,4},{1,5},{2,6},{3,7},{4,0},{5,1},{6,2},{7,3},{8,12},{9,13},{10,... | collective-permute-start | bytes 393224 | tf_op jit(solution)/shard_map/ppermute | solution.py:43
  81.6 14.5 %copy-start.9 = (bf16[16,256,256]{2,1,0:T(8,128)(2,1)S(1)}, bf16[16,256,256]{2,1,0:T(8,128)(2,1)}, u32[]{:S(2)}) copy-start(bf16[16,256,256]{2,1,0:T(8,128)(2,1)} %get-tuple-element.43.refs_4_.refs_2_) | copy-start | bytes 6291460
  81.6 5.9 %collective-permute-start.30 = (bf16[1,2,256,128]{3,2,1,0:T(8,128)(2,1)S(1)}, bf16[1,2,256,128]{3,2,1,0:T(8,128)(2,1)S(1)}, u32[]{:S(2)}, u32[]{:S(2)}) collective-permute-start(bf16[1,2,256,128]{3,2,1,0:T(8,128)(2,1)S(1)} %slice.17), channel_id=1, source_target_pairs={{0,2},{1,3},{2,0},{3,1},{4,6},{5,7},{6,4},{7,5},{8,10},{9,11},{10,... | collective-permute-start | bytes 393224 | tf_op jit(solution)/shard_map/ppermute | solution.py:43
  85.2 5.0 %collective-permute-start.29 = (bf16[1,2,256,128]{3,2,1,0:T(8,128)(2,1)S(1)}, bf16[1,2,256,128]{3,2,1,0:T(8,128)(2,1)S(1)}, u32[]{:S(2)}, u32[]{:S(2)}) collective-permute-start(bf16[1,2,256,128]{3,2,1,0:T(8,128)(2,1)S(1)} %slice.16), channel_id=1, source_target_pairs={{0,4},{1,5},{2,6},{3,7},{4,0},{5,1},{6,2},{7,3},{8,12},{9,13},{10,... | collective-permute-start | bytes 393224 | tf_op jit(solution)/shard_map/ppermute | solution.py:43
  86.9 3.2 %collective-permute-start.41 = (bf16[1,2,256,128]{3,2,1,0:T(8,128)(2,1)S(1)}, bf16[1,2,256,128]{3,2,1,0:T(8,128)(2,1)S(1)}, u32[]{:S(2)}, u32[]{:S(2)}) collective-permute-start(bf16[1,2,256,128]{3,2,1,0:T(8,128)(2,1)S(1)} %collective-permute-done.39.refs_11_), channel_id=1, source_target_pairs={{0,1},{1,0},{2,3},{3,2},{4,5},{5,4},{6,7},{7,6},{8,9},{9,8},{10,11... | collective-permute-start | bytes 393224 | tf_op jit(solution)/shard_map/ppermute | solution.py:43
  86.9 3.7 %collective-permute-start.40 = (bf16[1,2,256,128]{3,2,1,0:T(8,128)(2,1)S(1)}, bf16[1,2,256,128]{3,2,1,0:T(8,128)(2,1)S(1)}, u32[]{:S(2)}, u32[]{:S(2)}) collective-permute-start(bf16[1,2,256,128]{3,2,1,0:T(8,128)(2,1)S(1)} %collective-permute-done.38.refs_10_), channel_id=1, source_target_pairs={{0,1},{1,0},{2,3},{3,2},{4,5},{5,4},{6,7},{7,6},{8,9},{9,8},{10,11... | collective-permute-start | bytes 393224 | tf_op jit(solution)/shard_map/ppermute | solution.py:43
  87.5 8.5 %collective-permute-start.24 = (bf16[2,2,256,128]{3,2,1,0:T(8,128)(2,1)S(1)}, bf16[2,2,256,128]{3,2,1,0:T(8,128)(2,1)S(1)}, u32[]{:S(2)}, u32[]{:S(2)}) collective-permute-start(bf16[2,2,256,128]{3,2,1,0:T(8,128)(2,1)S(1)} %get-tuple-element.72.refs_14_.refs_4_), channel_id=1, source_target_pairs={{0,1},{1,0},{2,3},{3,2},{4,5},{5,4},{6,7},{7,6},{8,9},{9,8},{10,11... | collective-permute-start | bytes 786440 | tf_op jit(solution)/shard_map/ppermute | solution.py:43
  87.5 8.5 %collective-permute-start.28 = (bf16[2,2,256,128]{3,2,1,0:T(8,128)(2,1)S(1)}, bf16[2,2,256,128]{3,2,1,0:T(8,128)(2,1)S(1)}, u32[]{:S(2)}, u32[]{:S(2)}) collective-permute-start(bf16[2,2,256,128]{3,2,1,0:T(8,128)(2,1)S(1)} %collective-permute-done.27.refs_8_), channel_id=1, source_target_pairs={{0,1},{1,0},{2,3},{3,2},{4,5},{5,4},{6,7},{7,6},{8,9},{9,8},{10,11... | collective-permute-start | bytes 786440 | tf_op jit(solution)/shard_map/ppermute | solution.py:43
  90.1 5.9 %collective-permute-start.26 = (bf16[2,2,256,128]{3,2,1,0:T(8,128)(2,1)S(1)}, bf16[2,2,256,128]{3,2,1,0:T(8,128)(2,1)S(1)}, u32[]{:S(2)}, u32[]{:S(2)}) collective-permute-start(bf16[2,2,256,128]{3,2,1,0:T(8,128)(2,1)S(1)} %collective-permute-done.25.refs_6_), channel_id=1, source_target_pairs={{0,1},{1,0},{2,3},{3,2},{4,5},{5,4},{6,7},{7,6},{8,9},{9,8},{10,11... | collective-permute-start | bytes 786440 | tf_op jit(solution)/shard_map/ppermute | solution.py:43
  90.1 5.9 %collective-permute-start.32 = (bf16[1,2,256,128]{3,2,1,0:T(8,128)(2,1)S(1)}, bf16[1,2,256,128]{3,2,1,0:T(8,128)(2,1)S(1)}, u32[]{:S(2)}, u32[]{:S(2)}) collective-permute-start(bf16[1,2,256,128]{3,2,1,0:T(8,128)(2,1)S(1)} %collective-permute-done.30.refs_11_), channel_id=1, source_target_pairs={{0,1},{1,0},{2,3},{3,2},{4,5},{5,4},{6,7},{7,6},{8,9},{9,8},{10,11... | collective-permute-start | bytes 393224 | tf_op jit(solution)/shard_map/ppermute | solution.py:43
  90.7 5.4 %collective-permute-start.31 = (bf16[1,2,256,128]{3,2,1,0:T(8,128)(2,1)S(1)}, bf16[1,2,256,128]{3,2,1,0:T(8,128)(2,1)S(1)}, u32[]{:S(2)}, u32[]{:S(2)}) collective-permute-start(bf16[1,2,256,128]{3,2,1,0:T(8,128)(2,1)S(1)} %collective-permute-done.29.refs_10_), channel_id=1, source_target_pairs={{0,1},{1,0},{2,3},{3,2},{4,5},{5,4},{6,7},{7,6},{8,9},{9,8},{10,11... | collective-permute-start | bytes 393224 | tf_op jit(solution)/shard_map/ppermute | solution.py:43
  (6 other events, 7.4 us)

commit v5 on v4

--- a/solution.py
+++ b/solution.py
@@ -8,6 +8,7 @@
 from jax.sharding import PartitionSpec as P
 
 HALVES = 2
+FORWARD_ROOM = (52, 24)
 BF = jnp.bfloat16
 F32 = jnp.float32
 VMEM = pl.BlockSpec(memory_space=pltpu.VMEM)
@@ -82,7 +83,7 @@
         seen[dist] = 0
     small.wait()
 
-    def some(at, carry):
+    for at in range(leaves // group):
         for copy in copies(at):
             copy.wait()
         names = [at * group + j for j in range(group)]
@@ -99,10 +100,8 @@
             part[dist, 0, rank] = shift[:blk]
             part[dist, 1, rank] = shift[blk:]
             ids[pl.ds(dist * cap + rank, 1), :] = ancs[pl.ds(leaf, 1), :]
-        return carry
-
-    lax.fori_loop(0, leaves // group, some, 0)
-    for dist in range(fronts):
+
+    for dist in range(fronts if fronts * cap > leaves else 0):
         for rank in range(cap):
 
             @pl.when(seen[dist] <= rank)
@@ -144,7 +143,7 @@
             pltpu.SMEM((fronts,), jnp.int32),
             pltpu.SemaphoreType.DMA((leaves // group + 1, 3)),
         ],
-        room=50,
+        room=FORWARD_ROOM[h],
     )
 
 
@@ -254,22 +253,17 @@
 
 def reduce_kernel(h, slabs, blk, terms, place, rhs, keep, near, *refs):
     _, parts, _, rows, part = keep.shape
-    outs = refs[terms:]
+    outs, held = refs[terms:-1], refs[-1]
     for index in range(slabs):
         q, span = piece_of(index, blk, rows // blk)
         left = h * parts * part + q * part
-        field = []
         for plane in range(2):
             value = keep[0, q, plane, span].astype(F32) + near[0, q, plane, span].astype(F32)
             for ref in refs[:terms]:
                 value = value + ref[q, plane, span].astype(F32)
-            field.append((rhs[0, plane, span, left : left + part].astype(F32) - value).astype(BF))
-        for mask, out in enumerate(outs):
-
-            @pl.when(place[0] ^ mask == index)
-            def _(field=field, out=out):
-                out[0] = field[0]
-                out[1] = field[1]
+            held[index, plane] = (rhs[0, plane, span, left : left + part].astype(F32) - value).astype(BF)
+    for mask, out in enumerate(outs):
+        out[...] = held[place[0] ^ mask]
 
 
 def reduce(h, place, root_rhs, keep, near, far, slabs, blk, after):
@@ -277,7 +271,7 @@
     return call(
         functools.partial(reduce_kernel, h, slabs, blk, len(far)), "interface_reduce",
         [place, root_rhs, keep, near, *far], [SMEM] + [VMEM] * (3 + len(far)),
-        [shape_of((2, blk, part))] * slabs, [VMEM] * slabs, after,
+        [shape_of((2, blk, part))] * slabs, [VMEM] * slabs, after, [pltpu.VMEM((slabs, 2, blk, part), BF)],
     )
 
 
@@ -306,16 +300,15 @@
             field = field - jnp.concatenate([scale, scale], axis=0) * state
         mat = stacked(packed[:blk], packed[blk : 2 * blk])
         high = field.astype(BF)
-        state = dot(mat, high)
         if slab:
-            state = state + dot(mat, (field - high.astype(F32)).astype(BF))
-        half = state.astype(BF)
-        for mask, out in enumerate(outs):
-
-            @pl.when(at == mask)
-            def _(half=half, out=out):
-                out[0] = half[:blk]
-                out[1] = half[blk:]
+            low = (field - high.astype(F32)).astype(BF)
+            both = dot(mat, jnp.concatenate([high, low], axis=1))
+            state = both[:, :part] + both[:, part:]
+        else:
+            state = dot(mat, high)
+        held[at] = state.astype(BF).reshape(2, blk, part)
+    for mask, out in enumerate(outs):
+        out[...] = held[mask]
 
 
 def chain(place, pieces, mats, after):
@@ -329,51 +322,70 @@
     )
 
 
-def collect_kernel(h, slabs, aliased, place, *refs):
+def collect_kernel(slabs, place, *refs):
     pieces = refs[:slabs]
-    own, root, full, sem = refs[slabs + aliased :]
+    own, held = refs[slabs:]
+    _, blk, _ = pieces[0].shape
+    rows = own.shape[2]
+    for mask, piece in enumerate(pieces):
+        held[mask] = piece[...]
+    for index in range(slabs):
+        q, span = piece_of(index, blk, rows // blk)
+        piece = held[place[0] ^ index]
+        own[q, 0, span] = piece[0]
+        own[q, 1, span] = piece[1]
+
+
+def collect(place, pieces, rows, after):
+    slabs = len(pieces)
     _, blk, part = pieces[0].shape
-    parts, _, rows, _ = own.shape
-    cols = parts * part
-    for mask, piece in enumerate(pieces):
-        for index in range(slabs):
-            q, span = piece_of(index, blk, rows // blk)
-
-            @pl.when(place[0] ^ mask == index)
-            def _(piece=piece, q=q, span=span):
-                for plane in range(2):
-                    own[q, plane, span] = piece[plane]
-                    full[plane, span, q * part : (q + 1) * part] = piece[plane].astype(F32)
-
-    copy = pltpu.make_async_copy(full, root.at[0, :, :, pl.ds(h * cols, cols)], sem)
-    copy.start()
-    copy.wait()
-
-
-def collect(h, place, pieces, before, rows, width, after):
-    slabs = len(pieces)
-    cols = width // HALVES
-    part = pieces[0].shape[2]
-    aliased = [] if before is None else [before]
-    return call(
-        functools.partial(collect_kernel, h, slabs, len(aliased)), "interface_collect",
-        [place, *pieces, *aliased], [SMEM] + [VMEM] * slabs + [HBM] * len(aliased),
-        [shape_of((cols // part, 2, rows, part)), shape_of((1, 2, rows, width), F32)], [VMEM, HBM], after,
-        [pltpu.VMEM((2, rows, cols), F32), pltpu.SemaphoreType.DMA],
-        {1 + slabs: 1} if aliased else None,
-    )
-
-
-def backward_kernel(h, counts, cap, aliased, owners, place, fwd, mats, *refs):
-    fronts = len(counts)
-    fields = refs[: sum(counts)]
-    out, held, slots, sems = refs[sum(counts) + aliased :]
+    return call(
+        functools.partial(collect_kernel, slabs), "interface_collect", [place, *pieces], [SMEM] + [VMEM] * slabs,
+        shape_of((slabs // (rows // blk), 2, rows, part)), VMEM, after, [pltpu.VMEM((slabs, 2, blk, part), BF)],
+    )
+
+
+def relay_kernel(half, own, by_x, by_y, to_y, to_x, near):
+    to_y[...] = by_x[:half]
+    to_x[...] = by_y[half:]
+    for at, ref in enumerate((own, by_x, by_y)):
+        near[at] = ref[...]
+
+
+def relay(own, by_x, by_y, after):
+    parts = own.shape[0]
+    half = parts // 2
+    return call(
+        functools.partial(relay_kernel, half), "interface_relay", [own, by_x, by_y], [VMEM] * 3,
+        [shape_of((half,) + own.shape[1:]), shape_of((parts - half,) + own.shape[1:]), shape_of((3,) + own.shape)],
+        [VMEM] * 3, after,
+    )
+
+
+def backward_kernel(h, named, count, cap, owns, aliased, owners, place, fwd, mats, *refs):
+    fronts = len(named)
+    fields, refs = refs[:count], refs[count:]
+    roots, refs = refs[:owns], refs[owns + aliased :]
+    out, refs = refs[0], refs[1:]
+    held, slots, sems = refs[-3:]
     leaves, wide, cols = fwd.shape
     blk = wide // 2
     tall = mats.shape[2]
-    for dist in range(fronts):
-        for rank in range(cap):
-            slots[dist * cap + rank] = -1
+    full = fronts * cap == leaves
+    copies = []
+    if owns:
+        root, token, wider, root_sem = refs[:4]
+        token[...] = jnp.zeros(token.shape, F32)
+        parts, _, _, part = roots[0].shape
+        for at, ref in enumerate(roots):
+            for q in range(parts):
+                left = (at * parts + q) * part
+                for plane in range(2):
+                    wider[plane, :, left : left + part] = ref[q, plane].astype(F32)
+        copies.append(pltpu.make_async_copy(wider, root.at[0], root_sem))
+        copies[0].start()
+    for slot in range(fronts * cap):
+        slots[slot] = -1
     for leaf in range(leaves):
         first = (owners[leaf] ^ place[1]) * cap
         spot = first
@@ -384,36 +396,56 @@
     def copy_of(leaf):
         return pltpu.make_async_copy(held.at[leaf], out.at[0, :, leaf, :, pl.ds(h * cols, cols)], sems.at[leaf])
 
+    def solve(name, field):
+        result = fwd[name].astype(F32) - dot(mats[name], field)
+        held[name, 0] = result[:blk].astype(BF)
+        held[name, 1] = result[blk:].astype(BF)
+        copy_of(name).start()
+
     for dist in range(fronts):
-        mine, fields = fields[: counts[dist]], fields[counts[dist] :]
+        mine = [fields[at] if lead is None else fields[at].at[lead] for at, lead in named[dist]]
         columns = [ref[q].reshape(tall, ref.shape[3]) for ref in mine for q in range(ref.shape[0])]
         field = jnp.concatenate(columns, axis=1)
         for rank in range(cap):
             name = slots[dist * cap + rank]
-
-            @pl.when(name >= 0)
-            def _(name=name, field=field):
-                result = fwd[name].astype(F32) - dot(mats[name], field)
-                held[name, 0] = result[:blk].astype(BF)
-                held[name, 1] = result[blk:].astype(BF)
-                copy_of(name).start()
+            if full:
+                solve(name, field)
+            else:
+                pl.when(name >= 0)(functools.partial(solve, name, field))
 
     for leaf in range(leaves):
-        copy_of(leaf).wait()
-
-
-def backward(h, owners, place, fwd, mats, fields, before, width, after):
+        copies.append(copy_of(leaf))
+    for copy in copies:
+        copy.wait()
+
+
+def backward(h, owners, place, fwd, mats, fields, roots, before, width, after):
     leaves, wide, cols = fwd.shape
     blk, fronts = wide // 2, len(fields)
     cap = -(-leaves // fronts)
-    counts = [len(field) for field in fields]
-    flat = [part for field in fields for part in field]
+    flat, named = [], []
+    for field in fields:
+        named.append([])
+        for value in field:
+            value, lead = value if isinstance(value, tuple) else (value, None)
+            known = [at for at, other in enumerate(flat) if other is value]
+            if not known:
+                flat.append(value)
+            named[-1].append((known[0] if known else len(flat) - 1, lead))
+    count = len(flat)
+    flat = flat + roots
     aliased = [] if before is None else [before]
-    return call(
-        functools.partial(backward_kernel, h, counts, cap, len(aliased)), "leaf_backward",
+    outs, specs, scratch = [shape_of((1, 2, leaves, blk, width))], [HBM], []
+    if roots:
+        rows = roots[0].shape[2]
+        outs, specs = outs + [shape_of((1, 2, rows, width), F32), shape_of((8, 128), F32)], [HBM, HBM, VMEM]
+        scratch = [pltpu.VMEM((2, rows, width), F32), pltpu.SemaphoreType.DMA]
+    return call(
+        functools.partial(backward_kernel, h, named, count, cap, len(roots), len(aliased)), "leaf_backward",
         [owners, place, fwd, mats, *flat, *aliased], [SMEM, SMEM] + [VMEM] * (2 + len(flat)) + [HBM] * len(aliased),
-        shape_of((1, 2, leaves, blk, width)), HBM, after,
-        [
+        outs, specs, after,
+        scratch
+        + [
             pltpu.VMEM((leaves, 2, blk, cols), BF),
             pltpu.SMEM((fronts * cap,), jnp.int32),
             pltpu.SemaphoreType.DMA((leaves,)),
@@ -455,40 +487,50 @@
     def over_slabs(values):
         return [values[0]] + [crossed(values[mask], "slab", mask) for mask in range(1, slabs)]
 
-    def share(own):
-        if square:
-            by_x, by_y = crossed(own, "front", 2), crossed(own, "front", 4)
-            far = [crossed(by_x[: parts // 2], "front", 4), crossed(by_y[parts // 2 :], "front", 2)]
-            mine = [[own], [by_x], [by_y], far]
-        else:
-            mine = [[own]] + [[crossed(own, "front", 2 * j)] for j in range(1, pairs)]
-        return [field for group in mine for field in (group, [crossed(value, "front", 1) for value in group])]
+    def near_of(values):
+        return [crossed(value, "front", 1) for value in values]
+
+    def share_first(own):
+        return [crossed(own, "front", mask) for mask in ((2, 4) if square else range(2, fronts, 2))]
+
+    def share_second(own, got, after):
+        if not square:
+            mine = [own] + got
+            return [[value] for pair in zip(mine, near_of(mine)) for value in pair], got[0]
+        to_y, to_x, held = relay(own, *got, after)
+        far = [crossed(to_y, "front", 4), crossed(to_x, "front", 2)]
+        there = crossed(held, "front", 1)
+        fields = []
+        for at, value in enumerate([own] + got):
+            fields += [[value], [(there, at)]]
+        return fields + [far, near_of(far)], to_y
 
     fwd0, keep0, near0 = start_forward(0, ())
-    same, other = pack(place, root_inv, coupling, [fwd0])
-    have = [same, crossed(other, "slab", 1)]
-    token, got0 = send_first(keep0, near0, [same])
+    token, got0 = send_first(keep0, near0, ())
     fwd1, keep1, near1 = start_forward(1, [token])
     token, far0 = send_second(keep0, near0, got0, [fwd1])
+    same, other = pack(place, root_inv, coupling, [token])
+    have = [same, crossed(other, "slab", 1)]
+    token, got1 = send_first(keep1, near1, [same])
     step = 2
     while step < slabs:
-        joined = join(have, [token])
-        have = have + [crossed(joined, "slab", step)]
+        token = join(have, [token])
+        have = have + [crossed(token, "slab", step)]
         step *= 2
-        token = joined
-    token, got1 = send_first(keep1, near1, [token])
     folded = fold(leaf_inv, leaf_off, ancestors, rows, [token])
     pieces0 = reduce(0, place, root_rhs, keep0, near0, far0, slabs, blk, [folded])
     token, far1 = send_second(keep1, near1, got1, [pieces0[0]])
     solved0 = chain(place, over_slabs(pieces0), have, [token])
     pieces1 = reduce(1, place, root_rhs, keep1, near1, far1, slabs, blk, [solved0[0]])
-    own0, root_sol = collect(0, place, over_slabs(solved0), None, rows, width, [pieces1[0]])
+    own0 = collect(place, over_slabs(solved0), rows, [pieces1[0]])
+    got0 = share_first(own0)
     solved1 = chain(place, over_slabs(pieces1), have, [own0])
-    fields0 = share(own0)
-    own1, root_sol = collect(1, place, over_slabs(solved1), root_sol, rows, width, ())
-    fields1 = share(own1)
-    leaf_sol = backward(0, owners, place, fwd0, folded, fields0, None, width, [own1])
-    leaf_sol = backward(1, owners, place, fwd1, folded, fields1, leaf_sol, width, ())
+    fields0, token = share_second(own0, got0, [solved1[0]])
+    own1 = collect(place, over_slabs(solved1), rows, [token])
+    got1 = share_first(own1)
+    leaf_sol, root_sol, token = backward(0, owners, place, fwd0, folded, fields0, [own0, own1], None, width, ())
+    fields1, _ = share_second(own1, got1, [token])
+    (leaf_sol,) = backward(1, owners, place, fwd1, folded, fields1, [], leaf_sol, width, ())
     return leaf_sol, root_sol
 
 

time: 102 us -> 97.1 us (0.952)
  local copies, waits for them, and re-layouts: 5.82 us -> 1.39 us
  Pallas kernels: 34.2 us -> 31.5 us
  waiting for transfers between devices: 18 us -> 20.7 us
    unnamed x24 -> x18, local copies, waits for them, and re-layouts: 5.78 us -> 1.39 us
    pallas_call x17 -> x19, Pallas kernels: 34.2 us -> 31.5 us  [call(): pl.pallas_call(wrapped, in_specs=list(in_specs) + [ANY] * extra, out_spec...]
    ppermute x42 -> x38, waiting for transfers between devices: 18 us -> 20.7 us  [crossed(): lax.ppermute(x, axis, [(i, i ^ mask) for i in range(lax.axis_size(axis))])]
    ppermute x42 -> x38, starting transfers between devices: 42.3 us -> 42.2 us  [crossed(): lax.ppermute(x, axis, [(i, i ^ mask) for i in range(lax.axis_size(axis))])]
  transfers between devices with their start and end apart: 42 -> 38, of which waited for: 14 -> 14; matrix products, arithmetic and copies ran while one was open for 0% -> 0% of each run, Pallas kernels for 21% -> 20%
where the time goes in v5:
time: 97.1 us; the launch traced here: 96.9 us
  starting transfers between devices  42.2 us (43%)
  Pallas kernels  31.5 us (32%)
  waiting for transfers between devices  20.7 us (21%)
  local copies, waits for them, and re-layouts  1.39 us (1%)
  between operations  1.05 us (1%)
    ppermute x38, starting transfers between devices, crossed(): lax.ppermute(x, axis, [(i, i ^ mask) for i in range(lax.axis_size(axis))])  42.2 us
    pallas_call x19, Pallas kernels, call(): pl.pallas_call(wrapped, in_specs=list(in_specs) + [ANY] * extra, out_spec...  31.5 us
    ppermute x38, waiting for transfers between devices, crossed(): lax.ppermute(x, axis, [(i, i ^ mask) for i in range(lax.axis_size(axis))])  20.7 us
  transfers between devices with their start and end apart: 38, of which 14 were waited for; matrix products, arithmetic and copies ran while one was open for 0% of the time, Pallas kernels for 20%

profile of v5, /device:TPU:0, one launch (start us, length us, event | category | flops | bytes accessed | tf_op | source)
XLA Modules:
  0.0 96.9 jit_solution(16822482651006395874)
XLA Ops:
  0.7 0.7 copy-done.5
  2.1 5.7 %leaf_forward.2 = (bf16[16,256,256]{2,1,0:T(8,128)(2,1)}, bf16[4,2,2,256,128]{4,3,2,1,0:T(8,128)(2,1)S(1)}, bf16[4,2,2,256,128]{4,3,2,1,0:T(8,128)(2,1)}) custom-call(s32[16]{0:T(128)S(1)} %bitcast.5, s32[2]{0:T(128)S(1)} %pad_add_fusion.refs_1_.refs_0_, bf16[1,2,16,128,512]{4,3,2,1,0:T(8,128)(2,1)} %refs_2_.4, bf16[1,16,2,128,128]{4,3,2,1,0:T(8,128)(2,1)} %refs_0_.1, ...), custom_call_target="tpu_custom_call" | custom-call | flops 10000000000 | bytes 1 | tf_op jit(solution)/shard_map/leaf_forward/pallas_call | solution.py:30
  8.2 2.5 %collective-permute-done.refs_1_.refs_3_ = bf16[4,2,2,256,128]{4,3,2,1,0:T(8,128)(2,1)S(1)} collective-permute-done((bf16[4,2,2,256,128]{4,3,2,1,0:T(8,128)(2,1)}, bf16[4,2,2,256,128]{4,3,2,1,0:T(8,128)(2,1)S(1)}, u32[]{:S(2)}, u32[]{:S(2)}) %collective-permute-start) | collective-permute-done | bytes 1048608 | tf_op jit(solution)/shard_map/ppermute | solution.py:44
  10.8 3.0 %collective-permute-start.2 = (bf16[1,2,256,128]{3,2,1,0:T(8,128)(2,1)S(1)}, bf16[1,2,256,128]{3,2,1,0:T(8,128)(2,1)S(1)}, u32[]{:S(2)}, u32[]{:S(2)}) collective-permute-start(bf16[1,2,256,128]{3,2,1,0:T(8,128)(2,1)S(1)} %get-tuple-element.47), channel_id=1, source_target_pairs={{0,4},{1,5},{2,6},{3,7},{4,0},{5,1},{6,2},{7,3},{8,12},{9,13},{10,... | collective-permute-start | bytes 393224 | tf_op jit(solution)/shard_map/ppermute | solution.py:44
  13.8 1.5 %collective-permute-start.1 = (bf16[1,2,256,128]{3,2,1,0:T(8,128)(2,1)S(1)}, bf16[1,2,256,128]{3,2,1,0:T(8,128)(2,1)S(1)}, u32[]{:S(2)}, u32[]{:S(2)}) collective-permute-start(bf16[1,2,256,128]{3,2,1,0:T(8,128)(2,1)S(1)} %get-tuple-element.45.refs_6_), channel_id=1, source_target_pairs={{0,2},{1,3},{2,0},{3,1},{4,6},{5,7},{6,4},{7,5},{8,10},{9,11},{10,... | collective-permute-start | bytes 393224 | tf_op jit(solution)/shard_map/ppermute | solution.py:44
  15.3 3.8 %leaf_forward.3 = (bf16[16,256,256]{2,1,0:T(8,128)(2,1)S(1)}, bf16[4,2,2,256,128]{4,3,2,1,0:T(8,128)(2,1)S(1)}, bf16[4,2,2,256,128]{4,3,2,1,0:T(8,128)(2,1)S(1)}) custom-call(s32[16]{0:T(128)S(1)} %bitcast.6, s32[2]{0:T(128)S(1)} %pad_add_fusion.refs_1_.refs_0_, bf16[1,2,16,128,512]{4,3,2,1,0:T(8,128)(2,1)S(1)} %copy-done, ...), custom_call_target="tpu_custom_call" | custom-call | flops 10000000000 | bytes 1 | tf_op jit(solution)/shard_map/leaf_forward/pallas_call | solution.py:30
  19.4 1.4 %collective-permute-start.7 = (bf16[2,2,256,128]{3,2,1,0:T(8,128)(2,1)S(1)}, bf16[2,2,256,128]{3,2,1,0:T(8,128)(2,1)S(1)}, u32[]{:S(2)}, u32[]{:S(2)}) collective-permute-start(bf16[2,2,256,128]{3,2,1,0:T(8,128)(2,1)S(1)} %get-tuple-element.48.refs_3_), channel_id=1, source_target_pairs={{0,2},{1,3},{2,0},{3,1},{4,6},{5,7},{6,4},{7,5},{8,10},{9,11},{10,... | collective-permute-start | bytes 786440 | tf_op jit(solution)/shard_map/ppermute | solution.py:44
  21.3 1.6 %collective-permute-start.3 = (bf16[272,128]{1,0:T(8,128)(2,1)S(1)}, bf16[272,128]{1,0:T(8,128)(2,1)S(1)}, u32[]{:S(2)}, u32[]{:S(2)}) collective-permute-start(bf16[272,128]{1,0:T(8,128)(2,1)S(1)} %get-tuple-element.50), channel_id=1, source_target_pairs={{0,8},{8,0},{16,24},{24,16},{1,9},{9,1},{17,25},{25,17},{2,10},{10... | collective-permute-start | bytes 208904 | tf_op jit(solution)/shard_map/ppermute | solution.py:44
  23.0 1.5 %collective-permute-start.8 = (bf16[2,2,256,128]{3,2,1,0:T(8,128)(2,1)S(1)}, bf16[2,2,256,128]{3,2,1,0:T(8,128)(2,1)S(1)}, u32[]{:S(2)}, u32[]{:S(2)}) collective-permute-start(bf16[2,2,256,128]{3,2,1,0:T(8,128)(2,1)S(1)} %get-tuple-element.55), channel_id=1, source_target_pairs={{0,4},{1,5},{2,6},{3,7},{4,0},{5,1},{6,2},{7,3},{8,12},{9,13},{10,... | collective-permute-start | bytes 786440 | tf_op jit(solution)/shard_map/ppermute | solution.py:44
  24.5 0.8 collective-permute-start.5
  25.7 2.7 %collective-permute-start.14 = (bf16[544,128]{1,0:T(8,128)(2,1)S(1)}, bf16[544,128]{1,0:T(8,128)(2,1)S(1)}, u32[]{:S(2)}, u32[]{:S(2)}) collective-permute-start(bf16[544,128]{1,0:T(8,128)(2,1)S(1)} %solve_join.1.refs_3_), channel_id=1, source_target_pairs={{0,16},{8,24},{16,0},{24,8},{1,17},{9,25},{17,1},{25,9},{2,18},{10... | collective-permute-start | bytes 417800 | tf_op jit(solution)/shard_map/ppermute | solution.py:44
  28.4 3.7 %leaf_fold.1.refs_6_.refs_3_ = bf16[16,256,512]{2,1,0:T(8,128)(2,1)S(1)} custom-call(bf16[1,16,2,128,128]{4,3,2,1,0:T(8,128)(2,1)S(1)} %copy-done.1, bf16[1,16,2,128,128]{4,3,2,1,0:T(8,128)(2,1)S(1)} %copy-done.2, s32[1,16,128]{2,1,0:T(8,128)S(1)} %copy-done.5, bf16[544,128]{1,0:T(8,128)(2,1)S(1)} %solve_join.1.refs_3_), custom_call_target="tpu_custom_call" | custom-call | flops 10000000000 | bytes 1 | tf_op jit(solution)/shard_map/leaf_fold/pallas_call | solution.py:30
  32.1 1.5 %collective-permute-start.6 = (bf16[1,2,256,128]{3,2,1,0:T(8,128)(2,1)S(1)}, bf16[1,2,256,128]{3,2,1,0:T(8,128)(2,1)S(1)}, u32[]{:S(2)}, u32[]{:S(2)}) collective-permute-start(bf16[1,2,256,128]{3,2,1,0:T(8,128)(2,1)S(1)} %get-tuple-element.54), channel_id=1, source_target_pairs={{0,4},{1,5},{2,6},{3,7},{4,0},{5,1},{6,2},{7,3},{8,12},{9,13},{10,... | collective-permute-start | bytes 393224 | tf_op jit(solution)/shard_map/ppermute | solution.py:44
  33.6 0.7 interface_reduce.2
  34.4 1.6 %collective-permute-start.11 = (bf16[2,128,128]{2,1,0:T(8,128)(2,1)S(1)}, bf16[2,128,128]{2,1,0:T(8,128)(2,1)S(1)}, u32[]{:S(2)}, u32[]{:S(2)}) collective-permute-start(bf16[2,128,128]{2,1,0:T(8,128)(2,1)S(1)} %get-tuple-element.59), channel_id=1, source_target_pairs={{0,8},{8,0},{16,24},{24,16},{1,9},{9,1},{17,25},{25,17},{2,10},{10... | collective-permute-start | bytes 196616 | tf_op jit(solution)/shard_map/ppermute | solution.py:44
  36.3 0.8 collective-permute-done.6.refs_3_
  37.1 1.7 %collective-permute-start.13 = (bf16[2,128,128]{2,1,0:T(8,128)(2,1)S(1)}, bf16[2,128,128]{2,1,0:T(8,128)(2,1)S(1)}, u32[]{:S(2)}, u32[]{:S(2)}) collective-permute-start(bf16[2,128,128]{2,1,0:T(8,128)(2,1)S(1)} %get-tuple-element.61), channel_id=1, source_target_pairs={{0,24},{8,16},{16,8},{24,0},{1,25},{9,17},{17,9},{25,1},{2,26},{10... | collective-permute-start | bytes 196616 | tf_op jit(solution)/shard_map/ppermute | solution.py:44
  39.0 1.2 %collective-permute-start.10 = (bf16[2,2,256,128]{3,2,1,0:T(8,128)(2,1)S(1)}, bf16[2,2,256,128]{3,2,1,0:T(8,128)(2,1)S(1)}, u32[]{:S(2)}, u32[]{:S(2)}) collective-permute-start(bf16[2,2,256,128]{3,2,1,0:T(8,128)(2,1)S(1)} %get-tuple-element.58), channel_id=1, source_target_pairs={{0,4},{1,5},{2,6},{3,7},{4,0},{5,1},{6,2},{7,3},{8,12},{9,13},{10,... | collective-permute-start | bytes 786440 | tf_op jit(solution)/shard_map/ppermute | solution.py:44
  40.2 0.8 collective-permute-start.9
  41.0 1.0 %collective-permute-done.12.refs_3_ = bf16[2,128,128]{2,1,0:T(8,128)(2,1)S(1)} collective-permute-done((bf16[2,128,128]{2,1,0:T(8,128)(2,1)S(1)}, bf16[2,128,128]{2,1,0:T(8,128)(2,1)S(1)}, u32[]{:S(2)}, u32[]{:S(2)}) %collective-permute-start.12) | collective-permute-done | bytes 65568 | tf_op jit(solution)/shard_map/ppermute | solution.py:44
  42.0 1.3 %collective-permute-done.13.refs_4_ = bf16[2,128,128]{2,1,0:T(8,128)(2,1)S(1)} collective-permute-done((bf16[2,128,128]{2,1,0:T(8,128)(2,1)S(1)}, bf16[2,128,128]{2,1,0:T(8,128)(2,1)S(1)}, u32[]{:S(2)}, u32[]{:S(2)}) %collective-permute-start.13) | collective-permute-done | bytes 65568 | tf_op jit(solution)/shard_map/ppermute | solution.py:44
  43.3 1.5 %sweep_chain.2 = (bf16[2,128,128]{2,1,0:T(8,128)(2,1)S(1)}, bf16[2,128,128]{2,1,0:T(8,128)(2,1)S(1)}, bf16[2,128,128]{2,1,0:T(8,128)(2,1)S(1)}, bf16[2,128,128]{2,1,0:T(8,128)(2,1)S(1)}) custom-call(s32[2]{0:T(128)S(1)} %pad_add_fusion.refs_1_.refs_0_, bf16[2,128,128]{2,1,0:T(8,128)(2,1)S(1)} %get-tuple-element.56.refs_4_.refs_1_, ...), custom_call_target="tpu_custom_call" | custom-call | flops 10000000000 | bytes 1 | tf_op jit(solution)/shard_map/sweep_chain/pallas_call | solution.py:30
  44.8 0.8 collective-permute-start.18
  45.5 1.4 %collective-permute-start.19 = (bf16[2,128,128]{2,1,0:T(8,128)(2,1)S(1)}, bf16[2,128,128]{2,1,0:T(8,128)(2,1)S(1)}, u32[]{:S(2)}, u32[]{:S(2)}) collective-permute-start(bf16[2,128,128]{2,1,0:T(8,128)(2,1)S(1)} %get-tuple-element.68), channel_id=1, source_target_pairs={{0,16},{8,24},{16,0},{24,8},{1,17},{9,25},{17,1},{25,9},{2,18},{10... | collective-permute-start | bytes 196616 | tf_op jit(solution)/shard_map/ppermute | solution.py:44
  47.0 2.2 %collective-permute-start.20 = (bf16[2,128,128]{2,1,0:T(8,128)(2,1)S(1)}, bf16[2,128,128]{2,1,0:T(8,128)(2,1)S(1)}, u32[]{:S(2)}, u32[]{:S(2)}) collective-permute-start(bf16[2,128,128]{2,1,0:T(8,128)(2,1)S(1)} %get-tuple-element.69), channel_id=1, source_target_pairs={{0,24},{8,16},{16,8},{24,0},{1,25},{9,17},{17,9},{25,1},{2,26},{10... | collective-permute-start | bytes 196616 | tf_op jit(solution)/shard_map/ppermute | solution.py:44
  49.2 0.7 interface_reduce.3
  50.0 2.1 %collective-permute-start.16 = (bf16[2,128,128]{2,1,0:T(8,128)(2,1)S(1)}, bf16[2,128,128]{2,1,0:T(8,128)(2,1)S(1)}, u32[]{:S(2)}, u32[]{:S(2)}) collective-permute-start(bf16[2,128,128]{2,1,0:T(8,128)(2,1)S(1)} %get-tuple-element.65), channel_id=1, source_target_pairs={{0,16},{8,24},{16,0},{24,8},{1,17},{9,25},{17,1},{25,9},{2,18},{10... | collective-permute-start | bytes 196616 | tf_op jit(solution)/shard_map/ppermute | solution.py:44
  52.2 2.2 %collective-permute-start.17 = (bf16[2,128,128]{2,1,0:T(8,128)(2,1)S(1)}, bf16[2,128,128]{2,1,0:T(8,128)(2,1)S(1)}, u32[]{:S(2)}, u32[]{:S(2)}) collective-permute-start(bf16[2,128,128]{2,1,0:T(8,128)(2,1)S(1)} %get-tuple-element.66), channel_id=1, source_target_pairs={{0,24},{8,16},{16,8},{24,0},{1,25},{9,17},{17,9},{25,1},{2,26},{10... | collective-permute-start | bytes 196616 | tf_op jit(solution)/shard_map/ppermute | solution.py:44
  55.0 1.4 %collective-permute-start.25 = (bf16[2,2,256,128]{3,2,1,0:T(8,128)(2,1)S(1)}, bf16[2,2,256,128]{3,2,1,0:T(8,128)(2,1)S(1)}, u32[]{:S(2)}, u32[]{:S(2)}) collective-permute-start(bf16[2,2,256,128]{3,2,1,0:T(8,128)(2,1)S(1)} %interface_collect.2.refs_8_.refs_0_.refs_4_.refs_12_), channel_id=1, source_target_pairs={{0,4},{1,5},{2,6},{3,7},{4,0},{5,1},{6,2},{7,3},{8,12},{9,13},{10,... | collective-permute-start | bytes 786440 | tf_op jit(solution)/shard_map/ppermute | solution.py:44
  56.4 0.8 collective-permute-start.24
  57.3 1.1 %collective-permute-done.17.refs_4_ = bf16[2,128,128]{2,1,0:T(8,128)(2,1)S(1)} collective-permute-done((bf16[2,128,128]{2,1,0:T(8,128)(2,1)S(1)}, bf16[2,128,128]{2,1,0:T(8,128)(2,1)S(1)}, u32[]{:S(2)}, u32[]{:S(2)}) %collective-permute-start.17) | collective-permute-done | bytes 65568 | tf_op jit(solution)/shard_map/ppermute | solution.py:44
  58.4 1.5 %sweep_chain.3 = (bf16[2,128,128]{2,1,0:T(8,128)(2,1)S(1)}, bf16[2,128,128]{2,1,0:T(8,128)(2,1)S(1)}, bf16[2,128,128]{2,1,0:T(8,128)(2,1)S(1)}, bf16[2,128,128]{2,1,0:T(8,128)(2,1)S(1)}) custom-call(s32[2]{0:T(128)S(1)} %pad_add_fusion.refs_1_.refs_0_, bf16[2,128,128]{2,1,0:T(8,128)(2,1)S(1)} %get-tuple-element.63.refs_5_.refs_1_, ...), custom_call_target="tpu_custom_call" | custom-call | flops 10000000000 | bytes 1 | tf_op jit(solution)/shard_map/sweep_chain/pallas_call | solution.py:30
  59.8 2.1 %collective-permute-done.25.refs_2_.refs_7_ = bf16[2,2,256,128]{3,2,1,0:T(8,128)(2,1)S(1)} collective-permute-done((bf16[2,2,256,128]{3,2,1,0:T(8,128)(2,1)S(1)}, bf16[2,2,256,128]{3,2,1,0:T(8,128)(2,1)S(1)}, u32[]{:S(2)}, u32[]{:S(2)}) %collective-permute-start.25) | collective-permute-done | bytes 262176 | tf_op jit(solution)/shard_map/ppermute | solution.py:44
  61.9 2.2 %collective-permute-done.24.refs_1_.refs_6_ = bf16[2,2,256,128]{3,2,1,0:T(8,128)(2,1)S(1)} collective-permute-done((bf16[2,2,256,128]{3,2,1,0:T(8,128)(2,1)S(1)}, bf16[2,2,256,128]{3,2,1,0:T(8,128)(2,1)S(1)}, u32[]{:S(2)}, u32[]{:S(2)}) %collective-permute-start.24) | collective-permute-done | bytes 262176 | tf_op jit(solution)/shard_map/ppermute | solution.py:44
  64.2 1.0 %collective-permute-start.30 = (bf16[1,2,256,128]{3,2,1,0:T(8,128)(2,1)S(1)}, bf16[1,2,256,128]{3,2,1,0:T(8,128)(2,1)S(1)}, u32[]{:S(2)}, u32[]{:S(2)}) collective-permute-start(bf16[1,2,256,128]{3,2,1,0:T(8,128)(2,1)S(1)} %get-tuple-element.77), channel_id=1, source_target_pairs={{0,2},{1,3},{2,0},{3,1},{4,6},{5,7},{6,4},{7,5},{8,10},{9,11},{10,... | collective-permute-start | bytes 393224 | tf_op jit(solution)/shard_map/ppermute | solution.py:44
  65.2 0.7 collective-permute-start.29
  66.5 1.6 %collective-permute-start.22 = (bf16[2,128,128]{2,1,0:T(8,128)(2,1)S(1)}, bf16[2,128,128]{2,1,0:T(8,128)(2,1)S(1)}, u32[]{:S(2)}, u32[]{:S(2)}) collective-permute-start(bf16[2,128,128]{2,1,0:T(8,128)(2,1)S(1)} %get-tuple-element.72), channel_id=1, source_target_pairs={{0,16},{8,24},{16,0},{24,8},{1,17},{9,25},{17,1},{25,9},{2,18},{10... | collective-permute-start | bytes 196616 | tf_op jit(solution)/shard_map/ppermute | solution.py:44
  68.1 2.2 %collective-permute-start.23 = (bf16[2,128,128]{2,1,0:T(8,128)(2,1)S(1)}, bf16[2,128,128]{2,1,0:T(8,128)(2,1)S(1)}, u32[]{:S(2)}, u32[]{:S(2)}) collective-permute-start(bf16[2,128,128]{2,1,0:T(8,128)(2,1)S(1)} %get-tuple-element.73), channel_id=1, source_target_pairs={{0,24},{8,16},{16,8},{24,0},{1,25},{9,17},{17,9},{25,1},{2,26},{10... | collective-permute-start | bytes 196616 | tf_op jit(solution)/shard_map/ppermute | solution.py:44
  70.9 0.8 collective-permute-done.22.refs_3_
  71.7 2.5 %collective-permute-done.23.refs_4_ = bf16[2,128,128]{2,1,0:T(8,128)(2,1)S(1)} collective-permute-done((bf16[2,128,128]{2,1,0:T(8,128)(2,1)S(1)}, bf16[2,128,128]{2,1,0:T(8,128)(2,1)S(1)}, u32[]{:S(2)}, u32[]{:S(2)}) %collective-permute-start.23) | collective-permute-done | bytes 65568 | tf_op jit(solution)/shard_map/ppermute | solution.py:44
  74.8 1.1 %collective-permute-start.27 = (bf16[2,2,256,128]{3,2,1,0:T(8,128)(2,1)S(1)}, bf16[2,2,256,128]{3,2,1,0:T(8,128)(2,1)S(1)}, u32[]{:S(2)}, u32[]{:S(2)}) collective-permute-start(bf16[2,2,256,128]{3,2,1,0:T(8,128)(2,1)S(1)} %interface_collect.3.refs_13_.refs_0_.refs_4_), channel_id=1, source_target_pairs={{0,4},{1,5},{2,6},{3,7},{4,0},{5,1},{6,2},{7,3},{8,12},{9,13},{10,... | collective-permute-start | bytes 786440 | tf_op jit(solution)/shard_map/ppermute | solution.py:44
  75.9 1.1 %collective-permute-start.26 = (bf16[2,2,256,128]{3,2,1,0:T(8,128)(2,1)S(1)}, bf16[2,2,256,128]{3,2,1,0:T(8,128)(2,1)S(1)}, u32[]{:S(2)}, u32[]{:S(2)}) collective-permute-start(bf16[2,2,256,128]{3,2,1,0:T(8,128)(2,1)S(1)} %interface_collect.3.refs_13_.refs_0_.refs_4_), channel_id=1, source_target_pairs={{0,2},{1,3},{2,0},{3,1},{4,6},{5,7},{6,4},{7,5},{8,10},{9,11},{10,... | collective-permute-start | bytes 786440 | tf_op jit(solution)/shard_map/ppermute | solution.py:44
  77.0 5.8 %leaf_backward.2 = (bf16[1,2,16,128,512]{4,3,2,1,0:T(8,128)(2,1)}, f32[1,2,256,512]{3,2,1,0:T(8,128)}, f32[8,128]{1,0:T(8,128)S(1)}) custom-call(s32[16]{0:T(128)S(1)} %bitcast.7, s32[2]{0:T(128)S(1)} %pad_add_fusion.refs_1_.refs_0_, bf16[16,256,256]{2,1,0:T(8,128)(2,1)S(1)} %copy-done.8, bf16[16,256,512]{2,1,0:T(8,128)(2,1)S(1)} %leaf_fold.1.refs_6_.refs_3_, ...), custom_call_target="tpu_custom_call" | custom-call | flops 10000000000 | bytes 1 | tf_op jit(solution)/shard_map/leaf_backward/pallas_call | solution.py:30
  83.1 1.0 %collective-permute-start.34 = (bf16[1,2,256,128]{3,2,1,0:T(8,128)(2,1)S(1)}, bf16[1,2,256,128]{3,2,1,0:T(8,128)(2,1)S(1)}, u32[]{:S(2)}, u32[]{:S(2)}) collective-permute-start(bf16[1,2,256,128]{3,2,1,0:T(8,128)(2,1)S(1)} %get-tuple-element.80), channel_id=1, source_target_pairs={{0,4},{1,5},{2,6},{3,7},{4,0},{5,1},{6,2},{7,3},{8,12},{9,13},{10,... | collective-permute-start | bytes 393224 | tf_op jit(solution)/shard_map/ppermute | solution.py:44
  84.0 0.9 collective-permute-start.35
  85.0 4.0 %collective-permute-done.34.refs_8_ = bf16[1,2,256,128]{3,2,1,0:T(8,128)(2,1)S(1)} collective-permute-done((bf16[1,2,256,128]{3,2,1,0:T(8,128)(2,1)S(1)}, bf16[1,2,256,128]{3,2,1,0:T(8,128)(2,1)S(1)}, u32[]{:S(2)}, u32[]{:S(2)}) %collective-permute-start.34) | collective-permute-done | bytes 131104 | tf_op jit(solution)/shard_map/ppermute | solution.py:44
  89.6 0.7 collective-permute-done.36.refs_10_
  91.0 5.8 %leaf_backward.3 = bf16[1,2,16,128,512]{4,3,2,1,0:T(8,128)(2,1)} custom-call(s32[16]{0:T(128)S(1)} %bitcast.8, s32[2]{0:T(128)S(1)} %pad_add_fusion.refs_1_.refs_0_, bf16[16,256,256]{2,1,0:T(8,128)(2,1)S(1)} %get-tuple-element.46.refs_4_.refs_2_, bf16[16,256,512]{2,1,0:T(8,128)(2,1)S(1)} %leaf_fold.1.refs_6_.refs_3_, ...), custom_call_target="tpu_custom_call", output_to_operand_aliasing={{}: (12, {})} | custom-call | flops 10000000000 | bytes 1 | tf_op jit(solution)/shard_map/leaf_backward/pallas_call | solution.py:30
  (66 shorter events, 7.1 us)
Async XLA Ops:
  0.7 0.7 copy-start.5
  1.4 0.7 copy-start.7
  7.7 3.0 %collective-permute-start = (bf16[4,2,2,256,128]{4,3,2,1,0:T(8,128)(2,1)}, bf16[4,2,2,256,128]{4,3,2,1,0:T(8,128)(2,1)S(1)}, u32[]{:S(2)}, u32[]{:S(2)}) collective-permute-start(bf16[4,2,2,256,128]{4,3,2,1,0:T(8,128)(2,1)} %get-tuple-element.44), channel_id=1, source_target_pairs={{0,1},{1,0},{2,3},{3,2},{4,5},{5,4},{6,7},{7,6},{8,9},{9,8},{10,11... | collective-permute-start | bytes 3145736 | tf_op jit(solution)/shard_map/ppermute | solution.py:44
  10.7 4.5 %copy-start = (bf16[1,2,16,128,512]{4,3,2,1,0:T(8,128)(2,1)S(1)}, bf16[1,2,16,128,512]{4,3,2,1,0:T(8,128)(2,1)}, u32[]{:S(2)}) copy-start(bf16[1,2,16,128,512]{4,3,2,1,0:T(8,128)(2,1)} %refs_2_.4) | copy-start | bytes 12582916
  10.7 4.5 %copy-start.1 = (bf16[1,16,2,128,128]{4,3,2,1,0:T(8,128)(2,1)S(1)}, bf16[1,16,2,128,128]{4,3,2,1,0:T(8,128)(2,1)}, u32[]{:S(2)}) copy-start(bf16[1,16,2,128,128]{4,3,2,1,0:T(8,128)(2,1)} %refs_0_.1) | copy-start | bytes 3145732
  10.7 4.5 %copy-start.2 = (bf16[1,16,2,128,128]{4,3,2,1,0:T(8,128)(2,1)S(1)}, bf16[1,16,2,128,128]{4,3,2,1,0:T(8,128)(2,1)}, u32[]{:S(2)}) copy-start(bf16[1,16,2,128,128]{4,3,2,1,0:T(8,128)(2,1)} %refs_1_.5) | copy-start | bytes 3145732
  10.8 8.3 %collective-permute-start.2 = (bf16[1,2,256,128]{3,2,1,0:T(8,128)(2,1)S(1)}, bf16[1,2,256,128]{3,2,1,0:T(8,128)(2,1)S(1)}, u32[]{:S(2)}, u32[]{:S(2)}) collective-permute-start(bf16[1,2,256,128]{3,2,1,0:T(8,128)(2,1)S(1)} %get-tuple-element.47), channel_id=1, source_target_pairs={{0,4},{1,5},{2,6},{3,7},{4,0},{5,1},{6,2},{7,3},{8,12},{9,13},{10,... | collective-permute-start | bytes 393224 | tf_op jit(solution)/shard_map/ppermute | solution.py:44
  13.8 5.4 %collective-permute-start.1 = (bf16[1,2,256,128]{3,2,1,0:T(8,128)(2,1)S(1)}, bf16[1,2,256,128]{3,2,1,0:T(8,128)(2,1)S(1)}, u32[]{:S(2)}, u32[]{:S(2)}) collective-permute-start(bf16[1,2,256,128]{3,2,1,0:T(8,128)(2,1)S(1)} %get-tuple-element.45.refs_6_), channel_id=1, source_target_pairs={{0,2},{1,3},{2,0},{3,1},{4,6},{5,7},{6,4},{7,5},{8,10},{9,11},{10,... | collective-permute-start | bytes 393224 | tf_op jit(solution)/shard_map/ppermute | solution.py:44
  19.1 5.3 %collective-permute-start.4 = (bf16[4,2,2,256,128]{4,3,2,1,0:T(8,128)(2,1)S(1)}, bf16[4,2,2,256,128]{4,3,2,1,0:T(8,128)(2,1)S(1)}, u32[]{:S(2)}, u32[]{:S(2)}) collective-permute-start(bf16[4,2,2,256,128]{4,3,2,1,0:T(8,128)(2,1)S(1)} %get-tuple-element.52), channel_id=1, source_target_pairs={{0,1},{1,0},{2,3},{3,2},{4,5},{5,4},{6,7},{7,6},{8,9},{9,8},{10,11... | collective-permute-start | bytes 3145736 | tf_op jit(solution)/shard_map/ppermute | solution.py:44
  19.2 1.6 %copy-start.4 = (f32[1,2,2,128,128]{4,3,2,1,0:T(8,128)S(1)}, f32[1,2,2,128,128]{4,3,2,1,0:T(8,128)}, u32[]{:S(2)}) copy-start(f32[1,2,2,128,128]{4,3,2,1,0:T(8,128)} %refs_1_.4) | copy-start | bytes 786436
  19.2 1.6 %copy-start.6 = (f32[1,256]{1,0:T(1,128)S(1)}, f32[1,256]{1,0:T(1,128)}, u32[]{:S(2)}) copy-start(f32[1,256]{1,0:T(1,128)} %param.15) | copy-start | bytes 3076
  19.4 14.2 %collective-permute-start.7 = (bf16[2,2,256,128]{3,2,1,0:T(8,128)(2,1)S(1)}, bf16[2,2,256,128]{3,2,1,0:T(8,128)(2,1)S(1)}, u32[]{:S(2)}, u32[]{:S(2)}) collective-permute-start(bf16[2,2,256,128]{3,2,1,0:T(8,128)(2,1)S(1)} %get-tuple-element.48.refs_3_), channel_id=1, source_target_pairs={{0,2},{1,3},{2,0},{3,1},{4,6},{5,7},{6,4},{7,5},{8,10},{9,11},{10,... | collective-permute-start | bytes 786440 | tf_op jit(solution)/shard_map/ppermute | solution.py:44
  21.3 4.4 %collective-permute-start.3 = (bf16[272,128]{1,0:T(8,128)(2,1)S(1)}, bf16[272,128]{1,0:T(8,128)(2,1)S(1)}, u32[]{:S(2)}, u32[]{:S(2)}) collective-permute-start(bf16[272,128]{1,0:T(8,128)(2,1)S(1)} %get-tuple-element.50), channel_id=1, source_target_pairs={{0,8},{8,0},{16,24},{24,16},{1,9},{9,1},{17,25},{25,17},{2,10},{10... | collective-permute-start | bytes 208904 | tf_op jit(solution)/shard_map/ppermute | solution.py:44
  23.0 10.6 %collective-permute-start.8 = (bf16[2,2,256,128]{3,2,1,0:T(8,128)(2,1)S(1)}, bf16[2,2,256,128]{3,2,1,0:T(8,128)(2,1)S(1)}, u32[]{:S(2)}, u32[]{:S(2)}) collective-permute-start(bf16[2,2,256,128]{3,2,1,0:T(8,128)(2,1)S(1)} %get-tuple-element.55), channel_id=1, source_target_pairs={{0,4},{1,5},{2,6},{3,7},{4,0},{5,1},{6,2},{7,3},{8,12},{9,13},{10,... | collective-permute-start | bytes 786440 | tf_op jit(solution)/shard_map/ppermute | solution.py:44
  24.5 14.3 %collective-permute-start.5 = (bf16[1,2,256,128]{3,2,1,0:T(8,128)(2,1)S(1)}, bf16[1,2,256,128]{3,2,1,0:T(8,128)(2,1)S(1)}, u32[]{:S(2)}, u32[]{:S(2)}) collective-permute-start(bf16[1,2,256,128]{3,2,1,0:T(8,128)(2,1)S(1)} %get-tuple-element.53.refs_2_), channel_id=1, source_target_pairs={{0,2},{1,3},{2,0},{3,1},{4,6},{5,7},{6,4},{7,5},{8,10},{9,11},{10,... | collective-permute-start | bytes 393224 | tf_op jit(solution)/shard_map/ppermute | solution.py:44
  25.7 7.9 %copy-start.3 = (bf16[1,2,256,512]{3,2,1,0:T(8,128)(2,1)S(1)}, bf16[1,2,256,512]{3,2,1,0:T(8,128)(2,1)}, u32[]{:S(2)}) copy-start(bf16[1,2,256,512]{3,2,1,0:T(8,128)(2,1)} %refs_1_.7) | copy-start | bytes 1572868
  25.7 17.6 %collective-permute-start.14 = (bf16[544,128]{1,0:T(8,128)(2,1)S(1)}, bf16[544,128]{1,0:T(8,128)(2,1)S(1)}, u32[]{:S(2)}, u32[]{:S(2)}) collective-permute-start(bf16[544,128]{1,0:T(8,128)(2,1)S(1)} %solve_join.1.refs_3_), channel_id=1, source_target_pairs={{0,16},{8,24},{16,0},{24,8},{1,17},{9,25},{17,1},{25,9},{2,18},{10... | collective-permute-start | bytes 417800 | tf_op jit(solution)/shard_map/ppermute | solution.py:44
  32.1 5.0 %collective-permute-start.6 = (bf16[1,2,256,128]{3,2,1,0:T(8,128)(2,1)S(1)}, bf16[1,2,256,128]{3,2,1,0:T(8,128)(2,1)S(1)}, u32[]{:S(2)}, u32[]{:S(2)}) collective-permute-start(bf16[1,2,256,128]{3,2,1,0:T(8,128)(2,1)S(1)} %get-tuple-element.54), channel_id=1, source_target_pairs={{0,4},{1,5},{2,6},{3,7},{4,0},{5,1},{6,2},{7,3},{8,12},{9,13},{10,... | collective-permute-start | bytes 393224 | tf_op jit(solution)/shard_map/ppermute | solution.py:44
  34.4 5.8 %collective-permute-start.11 = (bf16[2,128,128]{2,1,0:T(8,128)(2,1)S(1)}, bf16[2,128,128]{2,1,0:T(8,128)(2,1)S(1)}, u32[]{:S(2)}, u32[]{:S(2)}) collective-permute-start(bf16[2,128,128]{2,1,0:T(8,128)(2,1)S(1)} %get-tuple-element.59), channel_id=1, source_target_pairs={{0,8},{8,0},{16,24},{24,16},{1,9},{9,1},{17,25},{25,17},{2,10},{10... | collective-permute-start | bytes 196616 | tf_op jit(solution)/shard_map/ppermute | solution.py:44
  36.0 6.0 %collective-permute-start.12 = (bf16[2,128,128]{2,1,0:T(8,128)(2,1)S(1)}, bf16[2,128,128]{2,1,0:T(8,128)(2,1)S(1)}, u32[]{:S(2)}, u32[]{:S(2)}) collective-permute-start(bf16[2,128,128]{2,1,0:T(8,128)(2,1)S(1)} %get-tuple-element.60), channel_id=1, source_target_pairs={{0,16},{8,24},{16,0},{24,8},{1,17},{9,25},{17,1},{25,9},{2,18},{10... | collective-permute-start | bytes 196616 | tf_op jit(solution)/shard_map/ppermute | solution.py:44
  37.1 6.2 %collective-permute-start.13 = (bf16[2,128,128]{2,1,0:T(8,128)(2,1)S(1)}, bf16[2,128,128]{2,1,0:T(8,128)(2,1)S(1)}, u32[]{:S(2)}, u32[]{:S(2)}) collective-permute-start(bf16[2,128,128]{2,1,0:T(8,128)(2,1)S(1)} %get-tuple-element.61), channel_id=1, source_target_pairs={{0,24},{8,16},{16,8},{24,0},{1,25},{9,17},{17,9},{25,1},{2,26},{10... | collective-permute-start | bytes 196616 | tf_op jit(solution)/shard_map/ppermute | solution.py:44
  39.0 10.2 %collective-permute-start.10 = (bf16[2,2,256,128]{3,2,1,0:T(8,128)(2,1)S(1)}, bf16[2,2,256,128]{3,2,1,0:T(8,128)(2,1)S(1)}, u32[]{:S(2)}, u32[]{:S(2)}) collective-permute-start(bf16[2,2,256,128]{3,2,1,0:T(8,128)(2,1)S(1)} %get-tuple-element.58), channel_id=1, source_target_pairs={{0,4},{1,5},{2,6},{3,7},{4,0},{5,1},{6,2},{7,3},{8,12},{9,13},{10,... | collective-permute-start | bytes 786440 | tf_op jit(solution)/shard_map/ppermute | solution.py:44
  40.2 9.1 %collective-permute-start.9 = (bf16[2,2,256,128]{3,2,1,0:T(8,128)(2,1)S(1)}, bf16[2,2,256,128]{3,2,1,0:T(8,128)(2,1)S(1)}, u32[]{:S(2)}, u32[]{:S(2)}) collective-permute-start(bf16[2,2,256,128]{3,2,1,0:T(8,128)(2,1)S(1)} %get-tuple-element.57.refs_8_), channel_id=1, source_target_pairs={{0,2},{1,3},{2,0},{3,1},{4,6},{5,7},{6,4},{7,5},{8,10},{9,11},{10,... | collective-permute-start | bytes 786440 | tf_op jit(solution)/shard_map/ppermute | solution.py:44
  44.8 7.4 %collective-permute-start.18 = (bf16[2,128,128]{2,1,0:T(8,128)(2,1)S(1)}, bf16[2,128,128]{2,1,0:T(8,128)(2,1)S(1)}, u32[]{:S(2)}, u32[]{:S(2)}) collective-permute-start(bf16[2,128,128]{2,1,0:T(8,128)(2,1)S(1)} %get-tuple-element.67), channel_id=1, source_target_pairs={{0,8},{8,0},{16,24},{24,16},{1,9},{9,1},{17,25},{25,17},{2,10},{10... | collective-permute-start | bytes 196616 | tf_op jit(solution)/shard_map/ppermute | solution.py:44
  45.5 8.9 %collective-permute-start.19 = (bf16[2,128,128]{2,1,0:T(8,128)(2,1)S(1)}, bf16[2,128,128]{2,1,0:T(8,128)(2,1)S(1)}, u32[]{:S(2)}, u32[]{:S(2)}) collective-permute-start(bf16[2,128,128]{2,1,0:T(8,128)(2,1)S(1)} %get-tuple-element.68), channel_id=1, source_target_pairs={{0,16},{8,24},{16,0},{24,8},{1,17},{9,25},{17,1},{25,9},{2,18},{10... | collective-permute-start | bytes 196616 | tf_op jit(solution)/shard_map/ppermute | solution.py:44
  47.0 7.4 %collective-permute-start.20 = (bf16[2,128,128]{2,1,0:T(8,128)(2,1)S(1)}, bf16[2,128,128]{2,1,0:T(8,128)(2,1)S(1)}, u32[]{:S(2)}, u32[]{:S(2)}) collective-permute-start(bf16[2,128,128]{2,1,0:T(8,128)(2,1)S(1)} %get-tuple-element.69), channel_id=1, source_target_pairs={{0,24},{8,16},{16,8},{24,0},{1,25},{9,17},{17,9},{25,1},{2,26},{10... | collective-permute-start | bytes 196616 | tf_op jit(solution)/shard_map/ppermute | solution.py:44
  50.0 7.3 %collective-permute-start.15 = (bf16[2,128,128]{2,1,0:T(8,128)(2,1)S(1)}, bf16[2,128,128]{2,1,0:T(8,128)(2,1)S(1)}, u32[]{:S(2)}, u32[]{:S(2)}) collective-permute-start(bf16[2,128,128]{2,1,0:T(8,128)(2,1)S(1)} %get-tuple-element.64), channel_id=1, source_target_pairs={{0,8},{8,0},{16,24},{24,16},{1,9},{9,1},{17,25},{25,17},{2,10},{10... | collective-permute-start | bytes 196616 | tf_op jit(solution)/shard_map/ppermute | solution.py:44
  50.0 7.2 %collective-permute-start.16 = (bf16[2,128,128]{2,1,0:T(8,128)(2,1)S(1)}, bf16[2,128,128]{2,1,0:T(8,128)(2,1)S(1)}, u32[]{:S(2)}, u32[]{:S(2)}) collective-permute-start(bf16[2,128,128]{2,1,0:T(8,128)(2,1)S(1)} %get-tuple-element.65), channel_id=1, source_target_pairs={{0,16},{8,24},{16,0},{24,8},{1,17},{9,25},{17,1},{25,9},{2,18},{10... | collective-permute-start | bytes 196616 | tf_op jit(solution)/shard_map/ppermute | solution.py:44
  52.2 6.2 %collective-permute-start.17 = (bf16[2,128,128]{2,1,0:T(8,128)(2,1)S(1)}, bf16[2,128,128]{2,1,0:T(8,128)(2,1)S(1)}, u32[]{:S(2)}, u32[]{:S(2)}) collective-permute-start(bf16[2,128,128]{2,1,0:T(8,128)(2,1)S(1)} %get-tuple-element.66), channel_id=1, source_target_pairs={{0,24},{8,16},{16,8},{24,0},{1,25},{9,17},{17,9},{25,1},{2,26},{10... | collective-permute-start | bytes 196616 | tf_op jit(solution)/shard_map/ppermute | solution.py:44
  55.0 6.9 %collective-permute-start.25 = (bf16[2,2,256,128]{3,2,1,0:T(8,128)(2,1)S(1)}, bf16[2,2,256,128]{3,2,1,0:T(8,128)(2,1)S(1)}, u32[]{:S(2)}, u32[]{:S(2)}) collective-permute-start(bf16[2,2,256,128]{3,2,1,0:T(8,128)(2,1)S(1)} %interface_collect.2.refs_8_.refs_0_.refs_4_.refs_12_), channel_id=1, source_target_pairs={{0,4},{1,5},{2,6},{3,7},{4,0},{5,1},{6,2},{7,3},{8,12},{9,13},{10,... | collective-permute-start | bytes 786440 | tf_op jit(solution)/shard_map/ppermute | solution.py:44
  56.4 7.7 %collective-permute-start.24 = (bf16[2,2,256,128]{3,2,1,0:T(8,128)(2,1)S(1)}, bf16[2,2,256,128]{3,2,1,0:T(8,128)(2,1)S(1)}, u32[]{:S(2)}, u32[]{:S(2)}) collective-permute-start(bf16[2,2,256,128]{3,2,1,0:T(8,128)(2,1)S(1)} %interface_collect.2.refs_8_.refs_0_.refs_4_.refs_12_), channel_id=1, source_target_pairs={{0,2},{1,3},{2,0},{3,1},{4,6},{5,7},{6,4},{7,5},{8,10},{9,11},{10,... | collective-permute-start | bytes 786440 | tf_op jit(solution)/shard_map/ppermute | solution.py:44
  64.2 6.1 %collective-permute-start.30 = (bf16[1,2,256,128]{3,2,1,0:T(8,128)(2,1)S(1)}, bf16[1,2,256,128]{3,2,1,0:T(8,128)(2,1)S(1)}, u32[]{:S(2)}, u32[]{:S(2)}) collective-permute-start(bf16[1,2,256,128]{3,2,1,0:T(8,128)(2,1)S(1)} %get-tuple-element.77), channel_id=1, source_target_pairs={{0,2},{1,3},{2,0},{3,1},{4,6},{5,7},{6,4},{7,5},{8,10},{9,11},{10,... | collective-permute-start | bytes 393224 | tf_op jit(solution)/shard_map/ppermute | solution.py:44
  65.2 5.6 %collective-permute-start.29 = (bf16[1,2,256,128]{3,2,1,0:T(8,128)(2,1)S(1)}, bf16[1,2,256,128]{3,2,1,0:T(8,128)(2,1)S(1)}, u32[]{:S(2)}, u32[]{:S(2)}) collective-permute-start(bf16[1,2,256,128]{3,2,1,0:T(8,128)(2,1)S(1)} %get-tuple-element.74.refs_5_), channel_id=1, source_target_pairs={{0,4},{1,5},{2,6},{3,7},{4,0},{5,1},{6,2},{7,3},{8,12},{9,13},{10,... | collective-permute-start | bytes 393224 | tf_op jit(solution)/shard_map/ppermute | solution.py:44
  65.9 4.4 %collective-permute-start.21 = (bf16[2,128,128]{2,1,0:T(8,128)(2,1)S(1)}, bf16[2,128,128]{2,1,0:T(8,128)(2,1)S(1)}, u32[]{:S(2)}, u32[]{:S(2)}) collective-permute-start(bf16[2,128,128]{2,1,0:T(8,128)(2,1)S(1)} %get-tuple-element.71), channel_id=1, source_target_pairs={{0,8},{8,0},{16,24},{24,16},{1,9},{9,1},{17,25},{25,17},{2,10},{10... | collective-permute-start | bytes 196616 | tf_op jit(solution)/shard_map/ppermute | solution.py:44
  66.5 5.2 %collective-permute-start.22 = (bf16[2,128,128]{2,1,0:T(8,128)(2,1)S(1)}, bf16[2,128,128]{2,1,0:T(8,128)(2,1)S(1)}, u32[]{:S(2)}, u32[]{:S(2)}) collective-permute-start(bf16[2,128,128]{2,1,0:T(8,128)(2,1)S(1)} %get-tuple-element.72), channel_id=1, source_target_pairs={{0,16},{8,24},{16,0},{24,8},{1,17},{9,25},{17,1},{25,9},{2,18},{10... | collective-permute-start | bytes 196616 | tf_op jit(solution)/shard_map/ppermute | solution.py:44
  68.1 6.1 %collective-permute-start.23 = (bf16[2,128,128]{2,1,0:T(8,128)(2,1)S(1)}, bf16[2,128,128]{2,1,0:T(8,128)(2,1)S(1)}, u32[]{:S(2)}, u32[]{:S(2)}) collective-permute-start(bf16[2,128,128]{2,1,0:T(8,128)(2,1)S(1)} %get-tuple-element.73), channel_id=1, source_target_pairs={{0,24},{8,16},{16,8},{24,0},{1,25},{9,17},{17,9},{25,1},{2,26},{10... | collective-permute-start | bytes 196616 | tf_op jit(solution)/shard_map/ppermute | solution.py:44
  70.3 6.7 %copy-start.8 = (bf16[16,256,256]{2,1,0:T(8,128)(2,1)S(1)}, bf16[16,256,256]{2,1,0:T(8,128)(2,1)}, u32[]{:S(2)}) copy-start(bf16[16,256,256]{2,1,0:T(8,128)(2,1)} %get-tuple-element.75.refs_2_) | copy-start | bytes 6291460
  70.3 6.7 %collective-permute-start.28 = (bf16[3,2,2,256,128]{4,3,2,1,0:T(8,128)(2,1)S(1)}, bf16[3,2,2,256,128]{4,3,2,1,0:T(8,128)(2,1)S(1)}, u32[]{:S(2)}, u32[]{:S(2)}) collective-permute-start(bf16[3,2,2,256,128]{4,3,2,1,0:T(8,128)(2,1)S(1)} %get-tuple-element.76), channel_id=1, source_target_pairs={{0,1},{1,0},{2,3},{3,2},{4,5},{5,4},{6,7},{7,6},{8,9},{9,8},{10,11... | collective-permute-start | bytes 2359304 | tf_op jit(solution)/shard_map/ppermute | solution.py:44
  70.3 6.7 %collective-permute-start.32 = (bf16[1,2,256,128]{3,2,1,0:T(8,128)(2,1)S(1)}, bf16[1,2,256,128]{3,2,1,0:T(8,128)(2,1)S(1)}, u32[]{:S(2)}, u32[]{:S(2)}) collective-permute-start(bf16[1,2,256,128]{3,2,1,0:T(8,128)(2,1)S(1)} %collective-permute-done.30.refs_9_), channel_id=1, source_target_pairs={{0,1},{1,0},{2,3},{3,2},{4,5},{5,4},{6,7},{7,6},{8,9},{9,8},{10,11... | collective-permute-start | bytes 393224 | tf_op jit(solution)/shard_map/ppermute | solution.py:44
  70.8 6.2 %collective-permute-start.31 = (bf16[1,2,256,128]{3,2,1,0:T(8,128)(2,1)S(1)}, bf16[1,2,256,128]{3,2,1,0:T(8,128)(2,1)S(1)}, u32[]{:S(2)}, u32[]{:S(2)}) collective-permute-start(bf16[1,2,256,128]{3,2,1,0:T(8,128)(2,1)S(1)} %collective-permute-done.29.refs_8_), channel_id=1, source_target_pairs={{0,1},{1,0},{2,3},{3,2},{4,5},{5,4},{6,7},{7,6},{8,9},{9,8},{10,11... | collective-permute-start | bytes 393224 | tf_op jit(solution)/shard_map/ppermute | solution.py:44
  74.8 8.1 %collective-permute-start.27 = (bf16[2,2,256,128]{3,2,1,0:T(8,128)(2,1)S(1)}, bf16[2,2,256,128]{3,2,1,0:T(8,128)(2,1)S(1)}, u32[]{:S(2)}, u32[]{:S(2)}) collective-permute-start(bf16[2,2,256,128]{3,2,1,0:T(8,128)(2,1)S(1)} %interface_collect.3.refs_13_.refs_0_.refs_4_), channel_id=1, source_target_pairs={{0,4},{1,5},{2,6},{3,7},{4,0},{5,1},{6,2},{7,3},{8,12},{9,13},{10,... | collective-permute-start | bytes 786440 | tf_op jit(solution)/shard_map/ppermute | solution.py:44
  75.9 7.0 %collective-permute-start.26 = (bf16[2,2,256,128]{3,2,1,0:T(8,128)(2,1)S(1)}, bf16[2,2,256,128]{3,2,1,0:T(8,128)(2,1)S(1)}, u32[]{:S(2)}, u32[]{:S(2)}) collective-permute-start(bf16[2,2,256,128]{3,2,1,0:T(8,128)(2,1)S(1)} %interface_collect.3.refs_13_.refs_0_.refs_4_), channel_id=1, source_target_pairs={{0,2},{1,3},{2,0},{3,1},{4,6},{5,7},{6,4},{7,5},{8,10},{9,11},{10,... | collective-permute-start | bytes 786440 | tf_op jit(solution)/shard_map/ppermute | solution.py:44
  83.0 8.0 %collective-permute-start.33 = (bf16[3,2,2,256,128]{4,3,2,1,0:T(8,128)(2,1)S(1)}, bf16[3,2,2,256,128]{4,3,2,1,0:T(8,128)(2,1)S(1)}, u32[]{:S(2)}, u32[]{:S(2)}) collective-permute-start(bf16[3,2,2,256,128]{4,3,2,1,0:T(8,128)(2,1)S(1)} %get-tuple-element.79), channel_id=1, source_target_pairs={{0,1},{1,0},{2,3},{3,2},{4,5},{5,4},{6,7},{7,6},{8,9},{9,8},{10,11... | collective-permute-start | bytes 2359304 | tf_op jit(solution)/shard_map/ppermute | solution.py:44
  83.1 5.9 %collective-permute-start.34 = (bf16[1,2,256,128]{3,2,1,0:T(8,128)(2,1)S(1)}, bf16[1,2,256,128]{3,2,1,0:T(8,128)(2,1)S(1)}, u32[]{:S(2)}, u32[]{:S(2)}) collective-permute-start(bf16[1,2,256,128]{3,2,1,0:T(8,128)(2,1)S(1)} %get-tuple-element.80), channel_id=1, source_target_pairs={{0,4},{1,5},{2,6},{3,7},{4,0},{5,1},{6,2},{7,3},{8,12},{9,13},{10,... | collective-permute-start | bytes 393224 | tf_op jit(solution)/shard_map/ppermute | solution.py:44
  84.0 5.6 %collective-permute-start.35 = (bf16[1,2,256,128]{3,2,1,0:T(8,128)(2,1)S(1)}, bf16[1,2,256,128]{3,2,1,0:T(8,128)(2,1)S(1)}, u32[]{:S(2)}, u32[]{:S(2)}) collective-permute-start(bf16[1,2,256,128]{3,2,1,0:T(8,128)(2,1)S(1)} %get-tuple-element.81), channel_id=1, source_target_pairs={{0,2},{1,3},{2,0},{3,1},{4,6},{5,7},{6,4},{7,5},{8,10},{9,11},{10,... | collective-permute-start | bytes 393224 | tf_op jit(solution)/shard_map/ppermute | solution.py:44
  89.0 1.3 %collective-permute-start.36 = (bf16[1,2,256,128]{3,2,1,0:T(8,128)(2,1)S(1)}, bf16[1,2,256,128]{3,2,1,0:T(8,128)(2,1)S(1)}, u32[]{:S(2)}, u32[]{:S(2)}) collective-permute-start(bf16[1,2,256,128]{3,2,1,0:T(8,128)(2,1)S(1)} %collective-permute-done.34.refs_8_), channel_id=1, source_target_pairs={{0,1},{1,0},{2,3},{3,2},{4,5},{5,4},{6,7},{7,6},{8,9},{9,8},{10,11... | collective-permute-start | bytes 393224 | tf_op jit(solution)/shard_map/ppermute | solution.py:44
  89.6 1.3 %collective-permute-start.37 = (bf16[1,2,256,128]{3,2,1,0:T(8,128)(2,1)S(1)}, bf16[1,2,256,128]{3,2,1,0:T(8,128)(2,1)S(1)}, u32[]{:S(2)}, u32[]{:S(2)}) collective-permute-start(bf16[1,2,256,128]{3,2,1,0:T(8,128)(2,1)S(1)} %collective-permute-done.35.refs_9_), channel_id=1, source_target_pairs={{0,1},{1,0},{2,3},{3,2},{4,5},{5,4},{6,7},{7,6},{8,9},{9,8},{10,11... | collective-permute-start | bytes 393224 | tf_op jit(solution)/shard_map/ppermute | solution.py:44

commit v6 on v5

--- a/solution.py
+++ b/solution.py
@@ -8,7 +8,8 @@
 from jax.sharding import PartitionSpec as P
 
 HALVES = 2
-FORWARD_ROOM = (52, 24)
+FIRST_ROOM = 52
+BRIEF = ("solve_join", "interface_first", "interface_relay", "interface_join")
 BF = jnp.bfloat16
 F32 = jnp.float32
 VMEM = pl.BlockSpec(memory_space=pltpu.VMEM)
@@ -35,7 +36,7 @@
         scratch_shapes=list(scratch),
         input_output_aliases=aliases or {},
         compiler_params=pltpu.CompilerParams(vmem_limit_bytes=room * 1024 * 1024),
-        cost_estimate=pl.CostEstimate(flops=10**10, bytes_accessed=1, transcendentals=0),
+        cost_estimate=pl.CostEstimate(flops=1 if name in BRIEF else 10**10, bytes_accessed=1, transcendentals=0),
         name=name,
     )(*ins, *after)
 
@@ -59,32 +60,36 @@
     return (ids == anc_row).astype(F32).astype(BF)
 
 
-def forward_kernel(h, group, cap, owners, place, rhs, inv, off, anc, fwd, keep, send,
-                   vecs, invs, offs, ancs, part, ids, seen, sems):
-    leaves, blk, cols = vecs.shape[1], vecs.shape[2], vecs.shape[3]
+def forward_kernel(h, group, cap, owners, place, rhs, inv, off, anc, fwd, keep, send, part, ids, seen, *rest):
+    leaves, blk, cols = rhs.shape[2], rhs.shape[3], part.shape[4]
     fronts, rows, width = part.shape[0], keep.shape[3], keep.shape[4]
     me = place[1]
-    small = pltpu.make_async_copy(anc.at[0], ancs, sems.at[leaves // group, 0])
-
-    def copies(at):
-        span = pl.ds(at * group, group)
-        return (
-            pltpu.make_async_copy(inv.at[0, span], invs.at[span], sems.at[at, 0]),
-            pltpu.make_async_copy(rhs.at[0, :, span, :, pl.ds(h * cols, cols)], vecs.at[:, span], sems.at[at, 1]),
-            pltpu.make_async_copy(off.at[0, span], offs.at[span], sems.at[at, 2]),
-        )
-
-    for at in range(leaves // group):
-        for copy in copies(at):
-            copy.start()
-    small.start()
+    if rest:
+        vecs, invs, offs, ancs, sems = rest
+        small = pltpu.make_async_copy(anc.at[0], ancs, sems.at[leaves // group, 0])
+
+        def copies(at):
+            span = pl.ds(at * group, group)
+            return (
+                pltpu.make_async_copy(inv.at[0, span], invs.at[span], sems.at[at, 0]),
+                pltpu.make_async_copy(rhs.at[0, :, span, :, pl.ds(h * cols, cols)], vecs.at[:, span], sems.at[at, 1]),
+                pltpu.make_async_copy(off.at[0, span], offs.at[span], sems.at[at, 2]),
+            )
+
+        for at in range(leaves // group):
+            for copy in copies(at):
+                copy.start()
+        small.start()
+    else:
+        vecs, invs, offs, ancs = rhs.at[0, :, :, :, pl.ds(h * cols, cols)], inv.at[0], off.at[0], anc.at[0]
     ids[...] = jnp.full(ids.shape, -1, jnp.int32)
     for dist in range(fronts):
         seen[dist] = 0
-    small.wait()
+    if rest:
+        small.wait()
 
     for at in range(leaves // group):
-        for copy in copies(at):
+        for copy in copies(at) if rest else ():
             copy.wait()
         names = [at * group + j for j in range(group)]
         values = []
@@ -123,27 +128,31 @@
     _, _, leaves, blk, width = leaf_rhs.shape
     cols = width // HALVES
     cap = -(-leaves // fronts)
-    group = 4
+    group = 8
     block = shape_of((fronts // 2, cols // part, 2, rows, part))
-    return call(
-        functools.partial(forward_kernel, h, group, cap),
-        "leaf_forward",
-        [owners, place, leaf_rhs, leaf_inv, leaf_off, ancestors],
-        [SMEM, SMEM, HBM, HBM, HBM, HBM],
-        [shape_of((leaves, 2 * blk, cols)), block, block],
-        [VMEM, VMEM, VMEM],
-        after,
-        [
+    scratch = [
+        pltpu.VMEM((fronts, 2, cap, blk, cols), BF),
+        pltpu.VMEM((fronts * cap, blk), jnp.int32),
+        pltpu.SMEM((fronts,), jnp.int32),
+    ]
+    if h == 0:
+        scratch += [
             pltpu.VMEM((2, leaves, blk, cols), BF),
             pltpu.VMEM((leaves, 2, blk, blk), BF),
             pltpu.VMEM((leaves, 2, blk, blk), BF),
             pltpu.VMEM((leaves, blk), jnp.int32),
-            pltpu.VMEM((fronts, 2, cap, blk, cols), BF),
-            pltpu.VMEM((fronts * cap, blk), jnp.int32),
-            pltpu.SMEM((fronts,), jnp.int32),
             pltpu.SemaphoreType.DMA((leaves // group + 1, 3)),
-        ],
-        room=FORWARD_ROOM[h],
+        ]
+    return call(
+        functools.partial(forward_kernel, h, group, cap),
+        "leaf_forward",
+        [owners, place, leaf_rhs, leaf_inv, leaf_off, ancestors],
+        [SMEM, SMEM] + [VMEM if h else HBM] * 4,
+        [shape_of((leaves, 2 * blk, cols)), block, block],
+        [VMEM, VMEM, VMEM],
+        after,
+        scratch,
+        room=24 if h else FIRST_ROOM,
     )
 
 
@@ -165,7 +174,7 @@
         out[leaf, blk:, rows:] = real
         return carry
 
-    lax.fori_loop(0, leaves, one, 0, unroll=2)
+    lax.fori_loop(0, leaves, one, 0, unroll=leaves)
 
 
 def fold(leaf_inv, leaf_off, ancestors, rows, after):
@@ -209,10 +218,10 @@
         at += ref.shape[0]
 
 
-def join(parts, after):
+def join(parts, after, name="solve_join"):
     rows = sum(part.shape[0] for part in parts)
     return call(
-        join_kernel, "solve_join", parts, [VMEM] * len(parts), shape_of((rows,) + parts[0].shape[1:]), VMEM, after
+        join_kernel, name, parts, [VMEM] * len(parts), shape_of((rows,) + parts[0].shape[1:]), VMEM, after
     )
 
 
@@ -400,18 +409,25 @@
         result = fwd[name].astype(F32) - dot(mats[name], field)
         held[name, 0] = result[:blk].astype(BF)
         held[name, 1] = result[blk:].astype(BF)
-        copy_of(name).start()
-
-    for dist in range(fronts):
-        mine = [fields[at] if lead is None else fields[at].at[lead] for at, lead in named[dist]]
-        columns = [ref[q].reshape(tall, ref.shape[3]) for ref in mine for q in range(ref.shape[0])]
-        field = jnp.concatenate(columns, axis=1)
-        for rank in range(cap):
-            name = slots[dist * cap + rank]
+
+    batch = 4
+    for low in range(0, fronts, batch):
+        names = []
+        for dist in range(low, min(fronts, low + batch)):
+            mine = [fields[at] if lead is None else fields[at].at[lead] for at, lead in named[dist]]
+            columns = [ref[q].reshape(tall, ref.shape[3]) for ref in mine for q in range(ref.shape[0])]
+            field = jnp.concatenate(columns, axis=1)
+            for rank in range(cap):
+                names.append(slots[dist * cap + rank])
+                if full:
+                    solve(names[-1], field)
+                else:
+                    pl.when(names[-1] >= 0)(functools.partial(solve, names[-1], field))
+        for name in names:
             if full:
-                solve(name, field)
+                copy_of(name).start()
             else:
-                pl.when(name >= 0)(functools.partial(solve, name, field))
+                pl.when(name >= 0)(copy_of(name).start)
 
     for leaf in range(leaves):
         copies.append(copy_of(leaf))
@@ -487,49 +503,52 @@
     def over_slabs(values):
         return [values[0]] + [crossed(values[mask], "slab", mask) for mask in range(1, slabs)]
 
-    def near_of(values):
-        return [crossed(value, "front", 1) for value in values]
-
     def share_first(own):
         return [crossed(own, "front", mask) for mask in ((2, 4) if square else range(2, fronts, 2))]
 
     def share_second(own, got, after):
         if not square:
+            return got[0], []
+        to_y, to_x, held = relay(own, *got, after)
+        return to_y, [crossed(to_y, "front", 4), crossed(to_x, "front", 2), crossed(held, "front", 1)]
+
+    def share_third(own, got, more, after):
+        if not square:
             mine = [own] + got
-            return [[value] for pair in zip(mine, near_of(mine)) for value in pair], got[0]
-        to_y, to_x, held = relay(own, *got, after)
-        far = [crossed(to_y, "front", 4), crossed(to_x, "front", 2)]
-        there = crossed(held, "front", 1)
+            return [[value] for field in mine for value in (field, crossed(field, "front", 1))]
+        far = join(more[:2], after, "interface_join")
         fields = []
         for at, value in enumerate([own] + got):
-            fields += [[value], [(there, at)]]
-        return fields + [far, near_of(far)], to_y
+            fields += [[value], [(more[2], at)]]
+        return fields + [[far], [crossed(far, "front", 1)]]
 
     fwd0, keep0, near0 = start_forward(0, ())
-    token, got0 = send_first(keep0, near0, ())
-    fwd1, keep1, near1 = start_forward(1, [token])
+    same, other = pack(place, root_inv, coupling, [fwd0])
+    have = [same, crossed(other, "slab", 1)]
+    token, got0 = send_first(keep0, near0, [same])
+    fwd1, keep1, near1 = start_forward(1, [token, have[1]])
     token, far0 = send_second(keep0, near0, got0, [fwd1])
-    same, other = pack(place, root_inv, coupling, [token])
-    have = [same, crossed(other, "slab", 1)]
-    token, got1 = send_first(keep1, near1, [same])
+    token, got1 = send_first(keep1, near1, [token])
     step = 2
     while step < slabs:
         token = join(have, [token])
         have = have + [crossed(token, "slab", step)]
         step *= 2
-    folded = fold(leaf_inv, leaf_off, ancestors, rows, [token])
-    pieces0 = reduce(0, place, root_rhs, keep0, near0, far0, slabs, blk, [folded])
+    pieces0 = reduce(0, place, root_rhs, keep0, near0, far0, slabs, blk, [token])
     token, far1 = send_second(keep1, near1, got1, [pieces0[0]])
     solved0 = chain(place, over_slabs(pieces0), have, [token])
     pieces1 = reduce(1, place, root_rhs, keep1, near1, far1, slabs, blk, [solved0[0]])
     own0 = collect(place, over_slabs(solved0), rows, [pieces1[0]])
     got0 = share_first(own0)
     solved1 = chain(place, over_slabs(pieces1), have, [own0])
-    fields0, token = share_second(own0, got0, [solved1[0]])
-    own1 = collect(place, over_slabs(solved1), rows, [token])
+    folded = fold(leaf_inv, leaf_off, ancestors, rows, [solved1[0]])
+    own1 = collect(place, over_slabs(solved1), rows, [folded])
     got1 = share_first(own1)
-    leaf_sol, root_sol, token = backward(0, owners, place, fwd0, folded, fields0, [own0, own1], None, width, ())
-    fields1, _ = share_second(own1, got1, [token])
+    token, more0 = share_second(own0, got0, [own1])
+    token, more1 = share_second(own1, got1, [token])
+    fields0 = share_third(own0, got0, more0, [token])
+    leaf_sol, root_sol, token = backward(0, owners, place, fwd0, folded, fields0, [own0, own1], None, width, [token])
+    fields1 = share_third(own1, got1, more1, [token])
     (leaf_sol,) = backward(1, owners, place, fwd1, folded, fields1, [], leaf_sol, width, ())
     return leaf_sol, root_sol
 

time: 97.1 us -> 90.8 us (0.935)
  Pallas kernels: 31.5 us -> 22.7 us
  local copies, waits for them, and re-layouts: 1.39 us -> 2.97 us
    pallas_call x19 -> x21, Pallas kernels: 31.5 us -> 22.7 us  [call(): pl.pallas_call(wrapped, in_specs=list(in_specs) + [ANY] * extra, out_spec...]
    unnamed x18 -> x20, local copies, waits for them, and re-layouts: 1.39 us -> 2.97 us
    ppermute x38 -> x36, starting transfers between devices: 42.2 us -> 43 us  [crossed(): lax.ppermute(x, axis, [(i, i ^ mask) for i in range(lax.axis_size(axis))])]
    ppermute x38 -> x36, waiting for transfers between devices: 20.7 us -> 20.8 us  [crossed(): lax.ppermute(x, axis, [(i, i ^ mask) for i in range(lax.axis_size(axis))])]
  transfers between devices with their start and end apart: 38 -> 36, of which waited for: 14 -> 13; matrix products, arithmetic and copies ran while one was open for 0% -> 0% of each run, Pallas kernels for 20% -> 16%
where the time goes in v6:
time: 90.8 us; the launch traced here: 90.6 us
  starting transfers between devices  43 us (47%)
  Pallas kernels  22.7 us (25%)
  waiting for transfers between devices  20.8 us (23%)
  local copies, waits for them, and re-layouts  2.97 us (3%)
    ppermute x36, starting transfers between devices, crossed(): lax.ppermute(x, axis, [(i, i ^ mask) for i in range(lax.axis_size(axis))])  43 us
    pallas_call x21, Pallas kernels, call(): pl.pallas_call(wrapped, in_specs=list(in_specs) + [ANY] * extra, out_spec...  22.7 us
    ppermute x36, waiting for transfers between devices, crossed(): lax.ppermute(x, axis, [(i, i ^ mask) for i in range(lax.axis_size(axis))])  20.8 us
    unnamed x20, local copies, waits for them, and re-layouts  2.97 us
  transfers between devices with their start and end apart: 36, of which 13 were waited for; matrix products, arithmetic and copies ran while one was open for 0% of the time, Pallas kernels for 16%

profile of v6, /device:TPU:0, one launch (start us, length us, event | category | flops | bytes accessed | tf_op | source)
XLA Modules:
  0.0 90.6 jit_solution(3206067104134948518)
XLA Ops:
  0.7 0.7 copy-done.5
  1.4 0.7 copy-done.7
  2.1 5.3 %leaf_forward.2 = (bf16[16,256,256]{2,1,0:T(8,128)(2,1)}, bf16[4,2,2,256,128]{4,3,2,1,0:T(8,128)(2,1)S(1)}, bf16[4,2,2,256,128]{4,3,2,1,0:T(8,128)(2,1)}) custom-call(s32[16]{0:T(128)S(1)} %bitcast.5, s32[2]{0:T(128)S(1)} %pad_add_fusion.refs_1_.refs_0_, bf16[1,2,16,128,512]{4,3,2,1,0:T(8,128)(2,1)} %refs_2_.4, bf16[1,16,2,128,128]{4,3,2,1,0:T(8,128)(2,1)} %refs_0_.1, ...), custom_call_target="tpu_custom_call" | custom-call | flops 10000000000 | bytes 1 | tf_op jit(solution)/shard_map/leaf_forward/pallas_call | solution.py:31
  7.9 1.6 %copy-done.8 = bf16[16,256,256]{2,1,0:T(8,128)(2,1)S(1)} copy-done((bf16[16,256,256]{2,1,0:T(8,128)(2,1)S(1)}, bf16[16,256,256]{2,1,0:T(8,128)(2,1)}, u32[]{:S(2)}) %copy-start.8) | copy-done | bytes 2097176
  10.1 2.7 %collective-permute-start.1 = (bf16[272,128]{1,0:T(8,128)(2,1)S(1)}, bf16[272,128]{1,0:T(8,128)(2,1)S(1)}, u32[]{:S(2)}, u32[]{:S(2)}) collective-permute-start(bf16[272,128]{1,0:T(8,128)(2,1)S(1)} %get-tuple-element.48), channel_id=1, source_target_pairs={{0,8},{8,0},{16,24},{24,16},{1,9},{9,1},{17,25},{25,17},{2,10},{10... | collective-permute-start | bytes 208904 | tf_op jit(solution)/shard_map/ppermute | solution.py:45
  12.8 1.6 %collective-permute-start.4 = (bf16[1,2,256,128]{3,2,1,0:T(8,128)(2,1)S(1)}, bf16[1,2,256,128]{3,2,1,0:T(8,128)(2,1)S(1)}, u32[]{:S(2)}, u32[]{:S(2)}) collective-permute-start(bf16[1,2,256,128]{3,2,1,0:T(8,128)(2,1)S(1)} %get-tuple-element.52), channel_id=1, source_target_pairs={{0,4},{1,5},{2,6},{3,7},{4,0},{5,1},{6,2},{7,3},{8,12},{9,13},{10,... | collective-permute-start | bytes 393224 | tf_op jit(solution)/shard_map/ppermute | solution.py:45
  14.4 1.5 %collective-permute-start.3 = (bf16[1,2,256,128]{3,2,1,0:T(8,128)(2,1)S(1)}, bf16[1,2,256,128]{3,2,1,0:T(8,128)(2,1)S(1)}, u32[]{:S(2)}, u32[]{:S(2)}) collective-permute-start(bf16[1,2,256,128]{3,2,1,0:T(8,128)(2,1)S(1)} %get-tuple-element.47.refs_6_), channel_id=1, source_target_pairs={{0,2},{1,3},{2,0},{3,1},{4,6},{5,7},{6,4},{7,5},{8,10},{9,11},{10,... | collective-permute-start | bytes 393224 | tf_op jit(solution)/shard_map/ppermute | solution.py:45
  15.9 2.6 %leaf_forward.3 = (bf16[16,256,256]{2,1,0:T(8,128)(2,1)S(1)}, bf16[4,2,2,256,128]{4,3,2,1,0:T(8,128)(2,1)S(1)}, bf16[4,2,2,256,128]{4,3,2,1,0:T(8,128)(2,1)S(1)}) custom-call(s32[16]{0:T(128)S(1)} %bitcast.6, s32[2]{0:T(128)S(1)} %pad_add_fusion.refs_1_.refs_0_, bf16[1,2,16,128,512]{4,3,2,1,0:T(8,128)(2,1)S(1)} %copy-done, ...), custom_call_target="tpu_custom_call" | custom-call | flops 10000000000 | bytes 1 | tf_op jit(solution)/shard_map/leaf_forward/pallas_call | solution.py:31
  18.7 1.1 %collective-permute-done.3.refs_2_ = bf16[1,2,256,128]{3,2,1,0:T(8,128)(2,1)S(1)} collective-permute-done((bf16[1,2,256,128]{3,2,1,0:T(8,128)(2,1)S(1)}, bf16[1,2,256,128]{3,2,1,0:T(8,128)(2,1)S(1)}, u32[]{:S(2)}, u32[]{:S(2)}) %collective-permute-start.3) | collective-permute-done | bytes 131104 | tf_op jit(solution)/shard_map/ppermute | solution.py:45
  20.5 1.5 %collective-permute-start.7 = (bf16[2,2,256,128]{3,2,1,0:T(8,128)(2,1)S(1)}, bf16[2,2,256,128]{3,2,1,0:T(8,128)(2,1)S(1)}, u32[]{:S(2)}, u32[]{:S(2)}) collective-permute-start(bf16[2,2,256,128]{3,2,1,0:T(8,128)(2,1)S(1)} %get-tuple-element.53.refs_2_), channel_id=1, source_target_pairs={{0,2},{1,3},{2,0},{3,1},{4,6},{5,7},{6,4},{7,5},{8,10},{9,11},{10,... | collective-permute-start | bytes 786440 | tf_op jit(solution)/shard_map/ppermute | solution.py:45
  22.1 1.6 %collective-permute-start.6 = (bf16[1,2,256,128]{3,2,1,0:T(8,128)(2,1)S(1)}, bf16[1,2,256,128]{3,2,1,0:T(8,128)(2,1)S(1)}, u32[]{:S(2)}, u32[]{:S(2)}) collective-permute-start(bf16[1,2,256,128]{3,2,1,0:T(8,128)(2,1)S(1)} %get-tuple-element.55), channel_id=1, source_target_pairs={{0,4},{1,5},{2,6},{3,7},{4,0},{5,1},{6,2},{7,3},{8,12},{9,13},{10,... | collective-permute-start | bytes 393224 | tf_op jit(solution)/shard_map/ppermute | solution.py:45
  23.6 0.6 collective-permute-start.5
  24.3 2.7 %collective-permute-start.14 = (bf16[544,128]{1,0:T(8,128)(2,1)S(1)}, bf16[544,128]{1,0:T(8,128)(2,1)S(1)}, u32[]{:S(2)}, u32[]{:S(2)}) collective-permute-start(bf16[544,128]{1,0:T(8,128)(2,1)S(1)} %solve_join.1.refs_6_), channel_id=1, source_target_pairs={{0,16},{8,24},{16,0},{24,8},{1,17},{9,25},{17,1},{25,9},{2,18},{10... | collective-permute-start | bytes 417800 | tf_op jit(solution)/shard_map/ppermute | solution.py:45
  27.0 2.1 %collective-permute-done.8.refs_5_ = bf16[2,2,256,128]{3,2,1,0:T(8,128)(2,1)S(1)} collective-permute-done((bf16[2,2,256,128]{3,2,1,0:T(8,128)(2,1)S(1)}, bf16[2,2,256,128]{3,2,1,0:T(8,128)(2,1)S(1)}, u32[]{:S(2)}, u32[]{:S(2)}) %collective-permute-start.8) | collective-permute-done | bytes 262176 | tf_op jit(solution)/shard_map/ppermute | solution.py:45
  29.7 0.7 interface_reduce.2
  30.4 1.4 %collective-permute-start.11 = (bf16[2,128,128]{2,1,0:T(8,128)(2,1)S(1)}, bf16[2,128,128]{2,1,0:T(8,128)(2,1)S(1)}, u32[]{:S(2)}, u32[]{:S(2)}) collective-permute-start(bf16[2,128,128]{2,1,0:T(8,128)(2,1)S(1)} %get-tuple-element.60), channel_id=1, source_target_pairs={{0,8},{8,0},{16,24},{24,16},{1,9},{9,1},{17,25},{25,17},{2,10},{10... | collective-permute-start | bytes 196616 | tf_op jit(solution)/shard_map/ppermute | solution.py:45
  31.8 2.6 %collective-permute-start.12 = (bf16[2,128,128]{2,1,0:T(8,128)(2,1)S(1)}, bf16[2,128,128]{2,1,0:T(8,128)(2,1)S(1)}, u32[]{:S(2)}, u32[]{:S(2)}) collective-permute-start(bf16[2,128,128]{2,1,0:T(8,128)(2,1)S(1)} %get-tuple-element.61), channel_id=1, source_target_pairs={{0,16},{8,24},{16,0},{24,8},{1,17},{9,25},{17,1},{25,9},{2,18},{10... | collective-permute-start | bytes 196616 | tf_op jit(solution)/shard_map/ppermute | solution.py:45
  35.0 1.2 %collective-permute-start.10 = (bf16[2,2,256,128]{3,2,1,0:T(8,128)(2,1)S(1)}, bf16[2,2,256,128]{3,2,1,0:T(8,128)(2,1)S(1)}, u32[]{:S(2)}, u32[]{:S(2)}) collective-permute-start(bf16[2,2,256,128]{3,2,1,0:T(8,128)(2,1)S(1)} %get-tuple-element.59), channel_id=1, source_target_pairs={{0,4},{1,5},{2,6},{3,7},{4,0},{5,1},{6,2},{7,3},{8,12},{9,13},{10,... | collective-permute-start | bytes 786440 | tf_op jit(solution)/shard_map/ppermute | solution.py:45
  36.2 1.3 %collective-permute-start.9 = (bf16[2,2,256,128]{3,2,1,0:T(8,128)(2,1)S(1)}, bf16[2,2,256,128]{3,2,1,0:T(8,128)(2,1)S(1)}, u32[]{:S(2)}, u32[]{:S(2)}) collective-permute-start(bf16[2,2,256,128]{3,2,1,0:T(8,128)(2,1)S(1)} %get-tuple-element.58.refs_8_), channel_id=1, source_target_pairs={{0,2},{1,3},{2,0},{3,1},{4,6},{5,7},{6,4},{7,5},{8,10},{9,11},{10,... | collective-permute-start | bytes 786440 | tf_op jit(solution)/shard_map/ppermute | solution.py:45
  37.5 0.9 collective-permute-done.12.refs_3_
  38.4 2.1 %collective-permute-done.13.refs_4_ = bf16[2,128,128]{2,1,0:T(8,128)(2,1)S(1)} collective-permute-done((bf16[2,128,128]{2,1,0:T(8,128)(2,1)S(1)}, bf16[2,128,128]{2,1,0:T(8,128)(2,1)S(1)}, u32[]{:S(2)}, u32[]{:S(2)}) %collective-permute-start.13) | collective-permute-done | bytes 65568 | tf_op jit(solution)/shard_map/ppermute | solution.py:45
  40.5 1.5 %sweep_chain.2 = (bf16[2,128,128]{2,1,0:T(8,128)(2,1)S(1)}, bf16[2,128,128]{2,1,0:T(8,128)(2,1)S(1)}, bf16[2,128,128]{2,1,0:T(8,128)(2,1)S(1)}, bf16[2,128,128]{2,1,0:T(8,128)(2,1)S(1)}) custom-call(s32[2]{0:T(128)S(1)} %pad_add_fusion.refs_1_.refs_0_, bf16[2,128,128]{2,1,0:T(8,128)(2,1)S(1)} %get-tuple-element.57.refs_4_.refs_1_, ...), custom_call_target="tpu_custom_call" | custom-call | flops 10000000000 | bytes 1 | tf_op jit(solution)/shard_map/sweep_chain/pallas_call | solution.py:31
  42.0 1.9 %collective-permute-start.19 = (bf16[2,128,128]{2,1,0:T(8,128)(2,1)S(1)}, bf16[2,128,128]{2,1,0:T(8,128)(2,1)S(1)}, u32[]{:S(2)}, u32[]{:S(2)}) collective-permute-start(bf16[2,128,128]{2,1,0:T(8,128)(2,1)S(1)} %get-tuple-element.69), channel_id=1, source_target_pairs={{0,16},{8,24},{16,0},{24,8},{1,17},{9,25},{17,1},{25,9},{2,18},{10... | collective-permute-start | bytes 196616 | tf_op jit(solution)/shard_map/ppermute | solution.py:45
  44.0 2.4 %collective-permute-start.20 = (bf16[2,128,128]{2,1,0:T(8,128)(2,1)S(1)}, bf16[2,128,128]{2,1,0:T(8,128)(2,1)S(1)}, u32[]{:S(2)}, u32[]{:S(2)}) collective-permute-start(bf16[2,128,128]{2,1,0:T(8,128)(2,1)S(1)} %get-tuple-element.70), channel_id=1, source_target_pairs={{0,24},{8,16},{16,8},{24,0},{1,25},{9,17},{17,9},{25,1},{2,26},{10... | collective-permute-start | bytes 196616 | tf_op jit(solution)/shard_map/ppermute | solution.py:45
  46.4 0.7 interface_reduce.3
  47.2 2.1 %collective-permute-start.16 = (bf16[2,128,128]{2,1,0:T(8,128)(2,1)S(1)}, bf16[2,128,128]{2,1,0:T(8,128)(2,1)S(1)}, u32[]{:S(2)}, u32[]{:S(2)}) collective-permute-start(bf16[2,128,128]{2,1,0:T(8,128)(2,1)S(1)} %get-tuple-element.66), channel_id=1, source_target_pairs={{0,16},{8,24},{16,0},{24,8},{1,17},{9,25},{17,1},{25,9},{2,18},{10... | collective-permute-start | bytes 196616 | tf_op jit(solution)/shard_map/ppermute | solution.py:45
  49.4 2.2 %collective-permute-start.17 = (bf16[2,128,128]{2,1,0:T(8,128)(2,1)S(1)}, bf16[2,128,128]{2,1,0:T(8,128)(2,1)S(1)}, u32[]{:S(2)}, u32[]{:S(2)}) collective-permute-start(bf16[2,128,128]{2,1,0:T(8,128)(2,1)S(1)} %get-tuple-element.67), channel_id=1, source_target_pairs={{0,24},{8,16},{16,8},{24,0},{1,25},{9,17},{17,9},{25,1},{2,26},{10... | collective-permute-start | bytes 196616 | tf_op jit(solution)/shard_map/ppermute | solution.py:45
  52.2 0.8 collective-permute-start.27
  53.0 1.5 %collective-permute-start.26 = (bf16[2,2,256,128]{3,2,1,0:T(8,128)(2,1)S(1)}, bf16[2,2,256,128]{3,2,1,0:T(8,128)(2,1)S(1)}, u32[]{:S(2)}, u32[]{:S(2)}) collective-permute-start(bf16[2,2,256,128]{3,2,1,0:T(8,128)(2,1)S(1)} %interface_collect.2.refs_8_.refs_0_.refs_4_.refs_10_), channel_id=1, source_target_pairs={{0,2},{1,3},{2,0},{3,1},{4,6},{5,7},{6,4},{7,5},{8,10},{9,11},{10,... | collective-permute-start | bytes 786440 | tf_op jit(solution)/shard_map/ppermute | solution.py:45
  54.4 1.1 %collective-permute-done.17.refs_4_ = bf16[2,128,128]{2,1,0:T(8,128)(2,1)S(1)} collective-permute-done((bf16[2,128,128]{2,1,0:T(8,128)(2,1)S(1)}, bf16[2,128,128]{2,1,0:T(8,128)(2,1)S(1)}, u32[]{:S(2)}, u32[]{:S(2)}) %collective-permute-start.17) | collective-permute-done | bytes 65568 | tf_op jit(solution)/shard_map/ppermute | solution.py:45
  55.5 1.5 %sweep_chain.3 = (bf16[2,128,128]{2,1,0:T(8,128)(2,1)S(1)}, bf16[2,128,128]{2,1,0:T(8,128)(2,1)S(1)}, bf16[2,128,128]{2,1,0:T(8,128)(2,1)S(1)}, bf16[2,128,128]{2,1,0:T(8,128)(2,1)S(1)}) custom-call(s32[2]{0:T(128)S(1)} %pad_add_fusion.refs_1_.refs_0_, bf16[2,128,128]{2,1,0:T(8,128)(2,1)S(1)} %get-tuple-element.64.refs_5_.refs_1_, ...), custom_call_target="tpu_custom_call" | custom-call | flops 10000000000 | bytes 1 | tf_op jit(solution)/shard_map/sweep_chain/pallas_call | solution.py:31
  57.0 0.8 collective-permute-start.21
  57.8 2.1 %collective-permute-start.22 = (bf16[2,128,128]{2,1,0:T(8,128)(2,1)S(1)}, bf16[2,128,128]{2,1,0:T(8,128)(2,1)S(1)}, u32[]{:S(2)}, u32[]{:S(2)}) collective-permute-start(bf16[2,128,128]{2,1,0:T(8,128)(2,1)S(1)} %get-tuple-element.73), channel_id=1, source_target_pairs={{0,16},{8,24},{16,0},{24,8},{1,17},{9,25},{17,1},{25,9},{2,18},{10... | collective-permute-start | bytes 196616 | tf_op jit(solution)/shard_map/ppermute | solution.py:45
  59.9 1.6 %collective-permute-start.23 = (bf16[2,128,128]{2,1,0:T(8,128)(2,1)S(1)}, bf16[2,128,128]{2,1,0:T(8,128)(2,1)S(1)}, u32[]{:S(2)}, u32[]{:S(2)}) collective-permute-start(bf16[2,128,128]{2,1,0:T(8,128)(2,1)S(1)} %get-tuple-element.74), channel_id=1, source_target_pairs={{0,24},{8,16},{16,8},{24,0},{1,25},{9,17},{17,9},{25,1},{2,26},{10... | collective-permute-start | bytes 196616 | tf_op jit(solution)/shard_map/ppermute | solution.py:45
  61.5 1.4 %leaf_fold.1.refs_5_.refs_3_ = bf16[16,256,512]{2,1,0:T(8,128)(2,1)S(1)} custom-call(bf16[1,16,2,128,128]{4,3,2,1,0:T(8,128)(2,1)S(1)} %copy-done.1, bf16[1,16,2,128,128]{4,3,2,1,0:T(8,128)(2,1)S(1)} %copy-done.2, s32[1,16,128]{2,1,0:T(8,128)S(1)} %copy-done.5, bf16[2,128,128]{2,1,0:T(8,128)(2,1)S(1)} %get-tuple-element.71.refs_3_.refs_1_), custom_call_target="tpu_custom_call" | custom-call | flops 10000000000 | bytes 1 | tf_op jit(solution)/shard_map/leaf_fold/pallas_call | solution.py:31
  62.9 1.1 %collective-permute-done.22.refs_3_ = bf16[2,128,128]{2,1,0:T(8,128)(2,1)S(1)} collective-permute-done((bf16[2,128,128]{2,1,0:T(8,128)(2,1)S(1)}, bf16[2,128,128]{2,1,0:T(8,128)(2,1)S(1)}, u32[]{:S(2)}, u32[]{:S(2)}) %collective-permute-start.22) | collective-permute-done | bytes 65568 | tf_op jit(solution)/shard_map/ppermute | solution.py:45
  64.1 1.9 %collective-permute-done.23.refs_4_ = bf16[2,128,128]{2,1,0:T(8,128)(2,1)S(1)} collective-permute-done((bf16[2,128,128]{2,1,0:T(8,128)(2,1)S(1)}, bf16[2,128,128]{2,1,0:T(8,128)(2,1)S(1)}, u32[]{:S(2)}, u32[]{:S(2)}) %collective-permute-start.23) | collective-permute-done | bytes 65568 | tf_op jit(solution)/shard_map/ppermute | solution.py:45
  66.7 0.7 collective-permute-start.25
  67.4 1.5 %collective-permute-start.24 = (bf16[2,2,256,128]{3,2,1,0:T(8,128)(2,1)S(1)}, bf16[2,2,256,128]{3,2,1,0:T(8,128)(2,1)S(1)}, u32[]{:S(2)}, u32[]{:S(2)}) collective-permute-start(bf16[2,2,256,128]{3,2,1,0:T(8,128)(2,1)S(1)} %interface_collect.3.refs_3_.refs_0_.refs_11_.refs_4_), channel_id=1, source_target_pairs={{0,2},{1,3},{2,0},{3,1},{4,6},{5,7},{6,4},{7,5},{8,10},{9,11},{10,... | collective-permute-start | bytes 786440 | tf_op jit(solution)/shard_map/ppermute | solution.py:45
  69.4 1.4 %collective-permute-start.32 = (bf16[1,2,256,128]{3,2,1,0:T(8,128)(2,1)S(1)}, bf16[1,2,256,128]{3,2,1,0:T(8,128)(2,1)S(1)}, u32[]{:S(2)}, u32[]{:S(2)}) collective-permute-start(bf16[1,2,256,128]{3,2,1,0:T(8,128)(2,1)S(1)} %get-tuple-element.75.refs_3_), channel_id=1, source_target_pairs={{0,4},{1,5},{2,6},{3,7},{4,0},{5,1},{6,2},{7,3},{8,12},{9,13},{10,... | collective-permute-start | bytes 393224 | tf_op jit(solution)/shard_map/ppermute | solution.py:45
  70.8 5.1 %collective-permute-done.25.refs_2_.refs_7_ = bf16[2,2,256,128]{3,2,1,0:T(8,128)(2,1)S(1)} collective-permute-done((bf16[2,2,256,128]{3,2,1,0:T(8,128)(2,1)S(1)}, bf16[2,2,256,128]{3,2,1,0:T(8,128)(2,1)S(1)}, u32[]{:S(2)}, u32[]{:S(2)}) %collective-permute-start.25) | collective-permute-done | bytes 262176 | tf_op jit(solution)/shard_map/ppermute | solution.py:45
  76.6 2.0 %collective-permute-done.33.refs_1_ = bf16[1,2,256,128]{3,2,1,0:T(8,128)(2,1)S(1)} collective-permute-done((bf16[1,2,256,128]{3,2,1,0:T(8,128)(2,1)S(1)}, bf16[1,2,256,128]{3,2,1,0:T(8,128)(2,1)S(1)}, u32[]{:S(2)}, u32[]{:S(2)}) %collective-permute-start.33) | collective-permute-done | bytes 131104 | tf_op jit(solution)/shard_map/ppermute | solution.py:45
  78.6 1.5 %collective-permute-start.29 = (bf16[1,2,256,128]{3,2,1,0:T(8,128)(2,1)S(1)}, bf16[1,2,256,128]{3,2,1,0:T(8,128)(2,1)S(1)}, u32[]{:S(2)}, u32[]{:S(2)}) collective-permute-start(bf16[1,2,256,128]{3,2,1,0:T(8,128)(2,1)S(1)} %get-tuple-element.77.refs_2_.refs_12_), channel_id=1, source_target_pairs={{0,4},{1,5},{2,6},{3,7},{4,0},{5,1},{6,2},{7,3},{8,12},{9,13},{10,... | collective-permute-start | bytes 393224 | tf_op jit(solution)/shard_map/ppermute | solution.py:45
  80.1 1.4 %collective-permute-start.30 = (bf16[1,2,256,128]{3,2,1,0:T(8,128)(2,1)S(1)}, bf16[1,2,256,128]{3,2,1,0:T(8,128)(2,1)S(1)}, u32[]{:S(2)}, u32[]{:S(2)}) collective-permute-start(bf16[1,2,256,128]{3,2,1,0:T(8,128)(2,1)S(1)} %get-tuple-element.78), channel_id=1, source_target_pairs={{0,2},{1,3},{2,0},{3,1},{4,6},{5,7},{6,4},{7,5},{8,10},{9,11},{10,... | collective-permute-start | bytes 393224 | tf_op jit(solution)/shard_map/ppermute | solution.py:45
  81.5 3.4 %leaf_backward.2 = (bf16[1,2,16,128,512]{4,3,2,1,0:T(8,128)(2,1)}, f32[1,2,256,512]{3,2,1,0:T(8,128)}, f32[8,128]{1,0:T(8,128)S(1)}) custom-call(s32[16]{0:T(128)S(1)} %bitcast.7, s32[2]{0:T(128)S(1)} %pad_add_fusion.refs_1_.refs_0_, bf16[16,256,256]{2,1,0:T(8,128)(2,1)S(1)} %copy-done.9, bf16[16,256,512]{2,1,0:T(8,128)(2,1)S(1)} %leaf_fold.1.refs_5_.refs_3_, ...), custom_call_target="tpu_custom_call" | custom-call | flops 10000000000 | bytes 1 | tf_op jit(solution)/shard_map/leaf_backward/pallas_call | solution.py:31
  84.9 0.8 collective-permute-done.30.refs_1_
  85.8 1.5 %collective-permute-done.35.refs_9_ = bf16[2,2,256,128]{3,2,1,0:T(8,128)(2,1)S(1)} collective-permute-done((bf16[2,2,256,128]{3,2,1,0:T(8,128)(2,1)S(1)}, bf16[2,2,256,128]{3,2,1,0:T(8,128)(2,1)S(1)}, u32[]{:S(2)}, u32[]{:S(2)}) %collective-permute-start.35) | collective-permute-done | bytes 262176 | tf_op jit(solution)/shard_map/ppermute | solution.py:45
  87.3 3.2 %leaf_backward.3 = bf16[1,2,16,128,512]{4,3,2,1,0:T(8,128)(2,1)} custom-call(s32[16]{0:T(128)S(1)} %bitcast.8, s32[2]{0:T(128)S(1)} %pad_add_fusion.refs_1_.refs_0_, bf16[16,256,256]{2,1,0:T(8,128)(2,1)S(1)} %get-tuple-element.49.refs_4_.refs_2_, bf16[16,256,512]{2,1,0:T(8,128)(2,1)S(1)} %leaf_fold.1.refs_5_.refs_3_, ...), custom_call_target="tpu_custom_call", output_to_operand_aliasing={{}: (10, {})} | custom-call | flops 10000000000 | bytes 1 | tf_op jit(solution)/shard_map/leaf_backward/pallas_call | solution.py:31
  (66 shorter events, 6.3 us)
Async XLA Ops:
  0.7 0.7 copy-start.5
  1.4 0.7 copy-start.7
  2.1 5.9 %copy-start.4 = (f32[1,2,2,128,128]{4,3,2,1,0:T(8,128)S(1)}, f32[1,2,2,128,128]{4,3,2,1,0:T(8,128)}, u32[]{:S(2)}) copy-start(f32[1,2,2,128,128]{4,3,2,1,0:T(8,128)} %refs_1_.4) | copy-start | bytes 786436
  2.1 5.9 %copy-start.6 = (f32[1,256]{1,0:T(1,128)S(1)}, f32[1,256]{1,0:T(1,128)}, u32[]{:S(2)}) copy-start(f32[1,256]{1,0:T(1,128)} %param.15) | copy-start | bytes 3076
  7.4 5.4 %collective-permute-start = (bf16[4,2,2,256,128]{4,3,2,1,0:T(8,128)(2,1)}, bf16[4,2,2,256,128]{4,3,2,1,0:T(8,128)(2,1)S(1)}, u32[]{:S(2)}, u32[]{:S(2)}) collective-permute-start(bf16[4,2,2,256,128]{4,3,2,1,0:T(8,128)(2,1)} %get-tuple-element.44), channel_id=1, source_target_pairs={{0,1},{1,0},{2,3},{3,2},{4,5},{5,4},{6,7},{7,6},{8,9},{9,8},{10,11... | collective-permute-start | bytes 3145736 | tf_op jit(solution)/shard_map/ppermute | solution.py:45
  7.9 1.6 %copy-start.8 = (bf16[16,256,256]{2,1,0:T(8,128)(2,1)S(1)}, bf16[16,256,256]{2,1,0:T(8,128)(2,1)}, u32[]{:S(2)}) copy-start(bf16[16,256,256]{2,1,0:T(8,128)(2,1)} %get-tuple-element.45.refs_3_.refs_2_) | copy-start | bytes 6291460
  9.5 6.4 %copy-start = (bf16[1,2,16,128,512]{4,3,2,1,0:T(8,128)(2,1)S(1)}, bf16[1,2,16,128,512]{4,3,2,1,0:T(8,128)(2,1)}, u32[]{:S(2)}) copy-start(bf16[1,2,16,128,512]{4,3,2,1,0:T(8,128)(2,1)} %refs_2_.4) | copy-start | bytes 12582916
  9.5 6.4 %copy-start.1 = (bf16[1,16,2,128,128]{4,3,2,1,0:T(8,128)(2,1)S(1)}, bf16[1,16,2,128,128]{4,3,2,1,0:T(8,128)(2,1)}, u32[]{:S(2)}) copy-start(bf16[1,16,2,128,128]{4,3,2,1,0:T(8,128)(2,1)} %refs_0_.1) | copy-start | bytes 3145732
  9.5 6.4 %copy-start.2 = (bf16[1,16,2,128,128]{4,3,2,1,0:T(8,128)(2,1)S(1)}, bf16[1,16,2,128,128]{4,3,2,1,0:T(8,128)(2,1)}, u32[]{:S(2)}) copy-start(bf16[1,16,2,128,128]{4,3,2,1,0:T(8,128)(2,1)} %refs_1_.7) | copy-start | bytes 3145732
  10.1 5.8 %collective-permute-start.1 = (bf16[272,128]{1,0:T(8,128)(2,1)S(1)}, bf16[272,128]{1,0:T(8,128)(2,1)S(1)}, u32[]{:S(2)}, u32[]{:S(2)}) collective-permute-start(bf16[272,128]{1,0:T(8,128)(2,1)S(1)} %get-tuple-element.48), channel_id=1, source_target_pairs={{0,8},{8,0},{16,24},{24,16},{1,9},{9,1},{17,25},{25,17},{2,10},{10... | collective-permute-start | bytes 208904 | tf_op jit(solution)/shard_map/ppermute | solution.py:45
  12.8 5.8 %collective-permute-start.4 = (bf16[1,2,256,128]{3,2,1,0:T(8,128)(2,1)S(1)}, bf16[1,2,256,128]{3,2,1,0:T(8,128)(2,1)S(1)}, u32[]{:S(2)}, u32[]{:S(2)}) collective-permute-start(bf16[1,2,256,128]{3,2,1,0:T(8,128)(2,1)S(1)} %get-tuple-element.52), channel_id=1, source_target_pairs={{0,4},{1,5},{2,6},{3,7},{4,0},{5,1},{6,2},{7,3},{8,12},{9,13},{10,... | collective-permute-start | bytes 393224 | tf_op jit(solution)/shard_map/ppermute | solution.py:45
  14.4 5.3 %collective-permute-start.3 = (bf16[1,2,256,128]{3,2,1,0:T(8,128)(2,1)S(1)}, bf16[1,2,256,128]{3,2,1,0:T(8,128)(2,1)S(1)}, u32[]{:S(2)}, u32[]{:S(2)}) collective-permute-start(bf16[1,2,256,128]{3,2,1,0:T(8,128)(2,1)S(1)} %get-tuple-element.47.refs_6_), channel_id=1, source_target_pairs={{0,2},{1,3},{2,0},{3,1},{4,6},{5,7},{6,4},{7,5},{8,10},{9,11},{10,... | collective-permute-start | bytes 393224 | tf_op jit(solution)/shard_map/ppermute | solution.py:45
  18.6 3.4 %collective-permute-start.2 = (bf16[4,2,2,256,128]{4,3,2,1,0:T(8,128)(2,1)S(1)}, bf16[4,2,2,256,128]{4,3,2,1,0:T(8,128)(2,1)S(1)}, u32[]{:S(2)}, u32[]{:S(2)}) collective-permute-start(bf16[4,2,2,256,128]{4,3,2,1,0:T(8,128)(2,1)S(1)} %get-tuple-element.51), channel_id=1, source_target_pairs={{0,1},{1,0},{2,3},{3,2},{4,5},{5,4},{6,7},{7,6},{8,9},{9,8},{10,11... | collective-permute-start | bytes 3145736 | tf_op jit(solution)/shard_map/ppermute | solution.py:45
  19.7 9.9 %copy-start.3 = (bf16[1,2,256,512]{3,2,1,0:T(8,128)(2,1)S(1)}, bf16[1,2,256,512]{3,2,1,0:T(8,128)(2,1)}, u32[]{:S(2)}) copy-start(bf16[1,2,256,512]{3,2,1,0:T(8,128)(2,1)} %refs_1_.6) | copy-start | bytes 1572868
  19.9 9.1 %collective-permute-start.8 = (bf16[2,2,256,128]{3,2,1,0:T(8,128)(2,1)S(1)}, bf16[2,2,256,128]{3,2,1,0:T(8,128)(2,1)S(1)}, u32[]{:S(2)}, u32[]{:S(2)}) collective-permute-start(bf16[2,2,256,128]{3,2,1,0:T(8,128)(2,1)S(1)} %get-tuple-element.56), channel_id=1, source_target_pairs={{0,4},{1,5},{2,6},{3,7},{4,0},{5,1},{6,2},{7,3},{8,12},{9,13},{10,... | collective-permute-start | bytes 786440 | tf_op jit(solution)/shard_map/ppermute | solution.py:45
  20.5 9.2 %collective-permute-start.7 = (bf16[2,2,256,128]{3,2,1,0:T(8,128)(2,1)S(1)}, bf16[2,2,256,128]{3,2,1,0:T(8,128)(2,1)S(1)}, u32[]{:S(2)}, u32[]{:S(2)}) collective-permute-start(bf16[2,2,256,128]{3,2,1,0:T(8,128)(2,1)S(1)} %get-tuple-element.53.refs_2_), channel_id=1, source_target_pairs={{0,2},{1,3},{2,0},{3,1},{4,6},{5,7},{6,4},{7,5},{8,10},{9,11},{10,... | collective-permute-start | bytes 786440 | tf_op jit(solution)/shard_map/ppermute | solution.py:45
  22.1 12.4 %collective-permute-start.6 = (bf16[1,2,256,128]{3,2,1,0:T(8,128)(2,1)S(1)}, bf16[1,2,256,128]{3,2,1,0:T(8,128)(2,1)S(1)}, u32[]{:S(2)}, u32[]{:S(2)}) collective-permute-start(bf16[1,2,256,128]{3,2,1,0:T(8,128)(2,1)S(1)} %get-tuple-element.55), channel_id=1, source_target_pairs={{0,4},{1,5},{2,6},{3,7},{4,0},{5,1},{6,2},{7,3},{8,12},{9,13},{10,... | collective-permute-start | bytes 393224 | tf_op jit(solution)/shard_map/ppermute | solution.py:45
  23.6 11.2 %collective-permute-start.5 = (bf16[1,2,256,128]{3,2,1,0:T(8,128)(2,1)S(1)}, bf16[1,2,256,128]{3,2,1,0:T(8,128)(2,1)S(1)}, u32[]{:S(2)}, u32[]{:S(2)}) collective-permute-start(bf16[1,2,256,128]{3,2,1,0:T(8,128)(2,1)S(1)} %get-tuple-element.54.refs_2_), channel_id=1, source_target_pairs={{0,2},{1,3},{2,0},{3,1},{4,6},{5,7},{6,4},{7,5},{8,10},{9,11},{10,... | collective-permute-start | bytes 393224 | tf_op jit(solution)/shard_map/ppermute | solution.py:45
  24.3 16.2 %collective-permute-start.14 = (bf16[544,128]{1,0:T(8,128)(2,1)S(1)}, bf16[544,128]{1,0:T(8,128)(2,1)S(1)}, u32[]{:S(2)}, u32[]{:S(2)}) collective-permute-start(bf16[544,128]{1,0:T(8,128)(2,1)S(1)} %solve_join.1.refs_6_), channel_id=1, source_target_pairs={{0,16},{8,24},{16,0},{24,8},{1,17},{9,25},{17,1},{25,9},{2,18},{10... | collective-permute-start | bytes 417800 | tf_op jit(solution)/shard_map/ppermute | solution.py:45
  30.4 5.8 %collective-permute-start.11 = (bf16[2,128,128]{2,1,0:T(8,128)(2,1)S(1)}, bf16[2,128,128]{2,1,0:T(8,128)(2,1)S(1)}, u32[]{:S(2)}, u32[]{:S(2)}) collective-permute-start(bf16[2,128,128]{2,1,0:T(8,128)(2,1)S(1)} %get-tuple-element.60), channel_id=1, source_target_pairs={{0,8},{8,0},{16,24},{24,16},{1,9},{9,1},{17,25},{25,17},{2,10},{10... | collective-permute-start | bytes 196616 | tf_op jit(solution)/shard_map/ppermute | solution.py:45
  31.8 6.6 %collective-permute-start.12 = (bf16[2,128,128]{2,1,0:T(8,128)(2,1)S(1)}, bf16[2,128,128]{2,1,0:T(8,128)(2,1)S(1)}, u32[]{:S(2)}, u32[]{:S(2)}) collective-permute-start(bf16[2,128,128]{2,1,0:T(8,128)(2,1)S(1)} %get-tuple-element.61), channel_id=1, source_target_pairs={{0,16},{8,24},{16,0},{24,8},{1,17},{9,25},{17,1},{25,9},{2,18},{10... | collective-permute-start | bytes 196616 | tf_op jit(solution)/shard_map/ppermute | solution.py:45
  34.4 6.1 %collective-permute-start.13 = (bf16[2,128,128]{2,1,0:T(8,128)(2,1)S(1)}, bf16[2,128,128]{2,1,0:T(8,128)(2,1)S(1)}, u32[]{:S(2)}, u32[]{:S(2)}) collective-permute-start(bf16[2,128,128]{2,1,0:T(8,128)(2,1)S(1)} %get-tuple-element.62), channel_id=1, source_target_pairs={{0,24},{8,16},{16,8},{24,0},{1,25},{9,17},{17,9},{25,1},{2,26},{10... | collective-permute-start | bytes 196616 | tf_op jit(solution)/shard_map/ppermute | solution.py:45
  35.0 11.4 %collective-permute-start.10 = (bf16[2,2,256,128]{3,2,1,0:T(8,128)(2,1)S(1)}, bf16[2,2,256,128]{3,2,1,0:T(8,128)(2,1)S(1)}, u32[]{:S(2)}, u32[]{:S(2)}) collective-permute-start(bf16[2,2,256,128]{3,2,1,0:T(8,128)(2,1)S(1)} %get-tuple-element.59), channel_id=1, source_target_pairs={{0,4},{1,5},{2,6},{3,7},{4,0},{5,1},{6,2},{7,3},{8,12},{9,13},{10,... | collective-permute-start | bytes 786440 | tf_op jit(solution)/shard_map/ppermute | solution.py:45
  36.2 10.2 %collective-permute-start.9 = (bf16[2,2,256,128]{3,2,1,0:T(8,128)(2,1)S(1)}, bf16[2,2,256,128]{3,2,1,0:T(8,128)(2,1)S(1)}, u32[]{:S(2)}, u32[]{:S(2)}) collective-permute-start(bf16[2,2,256,128]{3,2,1,0:T(8,128)(2,1)S(1)} %get-tuple-element.58.refs_8_), channel_id=1, source_target_pairs={{0,2},{1,3},{2,0},{3,1},{4,6},{5,7},{6,4},{7,5},{8,10},{9,11},{10,... | collective-permute-start | bytes 786440 | tf_op jit(solution)/shard_map/ppermute | solution.py:45
  41.9 7.4 %collective-permute-start.18 = (bf16[2,128,128]{2,1,0:T(8,128)(2,1)S(1)}, bf16[2,128,128]{2,1,0:T(8,128)(2,1)S(1)}, u32[]{:S(2)}, u32[]{:S(2)}) collective-permute-start(bf16[2,128,128]{2,1,0:T(8,128)(2,1)S(1)} %get-tuple-element.68), channel_id=1, source_target_pairs={{0,8},{8,0},{16,24},{24,16},{1,9},{9,1},{17,25},{25,17},{2,10},{10... | collective-permute-start | bytes 196616 | tf_op jit(solution)/shard_map/ppermute | solution.py:45
  42.0 9.6 %collective-permute-start.19 = (bf16[2,128,128]{2,1,0:T(8,128)(2,1)S(1)}, bf16[2,128,128]{2,1,0:T(8,128)(2,1)S(1)}, u32[]{:S(2)}, u32[]{:S(2)}) collective-permute-start(bf16[2,128,128]{2,1,0:T(8,128)(2,1)S(1)} %get-tuple-element.69), channel_id=1, source_target_pairs={{0,16},{8,24},{16,0},{24,8},{1,17},{9,25},{17,1},{25,9},{2,18},{10... | collective-permute-start | bytes 196616 | tf_op jit(solution)/shard_map/ppermute | solution.py:45
  44.0 7.6 %collective-permute-start.20 = (bf16[2,128,128]{2,1,0:T(8,128)(2,1)S(1)}, bf16[2,128,128]{2,1,0:T(8,128)(2,1)S(1)}, u32[]{:S(2)}, u32[]{:S(2)}) collective-permute-start(bf16[2,128,128]{2,1,0:T(8,128)(2,1)S(1)} %get-tuple-element.70), channel_id=1, source_target_pairs={{0,24},{8,16},{16,8},{24,0},{1,25},{9,17},{17,9},{25,1},{2,26},{10... | collective-permute-start | bytes 196616 | tf_op jit(solution)/shard_map/ppermute | solution.py:45
  47.1 7.3 %collective-permute-start.15 = (bf16[2,128,128]{2,1,0:T(8,128)(2,1)S(1)}, bf16[2,128,128]{2,1,0:T(8,128)(2,1)S(1)}, u32[]{:S(2)}, u32[]{:S(2)}) collective-permute-start(bf16[2,128,128]{2,1,0:T(8,128)(2,1)S(1)} %get-tuple-element.65), channel_id=1, source_target_pairs={{0,8},{8,0},{16,24},{24,16},{1,9},{9,1},{17,25},{25,17},{2,10},{10... | collective-permute-start | bytes 196616 | tf_op jit(solution)/shard_map/ppermute | solution.py:45
  47.2 7.2 %collective-permute-start.16 = (bf16[2,128,128]{2,1,0:T(8,128)(2,1)S(1)}, bf16[2,128,128]{2,1,0:T(8,128)(2,1)S(1)}, u32[]{:S(2)}, u32[]{:S(2)}) collective-permute-start(bf16[2,128,128]{2,1,0:T(8,128)(2,1)S(1)} %get-tuple-element.66), channel_id=1, source_target_pairs={{0,16},{8,24},{16,0},{24,8},{1,17},{9,25},{17,1},{25,9},{2,18},{10... | collective-permute-start | bytes 196616 | tf_op jit(solution)/shard_map/ppermute | solution.py:45
  49.4 6.2 %collective-permute-start.17 = (bf16[2,128,128]{2,1,0:T(8,128)(2,1)S(1)}, bf16[2,128,128]{2,1,0:T(8,128)(2,1)S(1)}, u32[]{:S(2)}, u32[]{:S(2)}) collective-permute-start(bf16[2,128,128]{2,1,0:T(8,128)(2,1)S(1)} %get-tuple-element.67), channel_id=1, source_target_pairs={{0,24},{8,16},{16,8},{24,0},{1,25},{9,17},{17,9},{25,1},{2,26},{10... | collective-permute-start | bytes 196616 | tf_op jit(solution)/shard_map/ppermute | solution.py:45
  52.2 14.3 %collective-permute-start.27 = (bf16[2,2,256,128]{3,2,1,0:T(8,128)(2,1)S(1)}, bf16[2,2,256,128]{3,2,1,0:T(8,128)(2,1)S(1)}, u32[]{:S(2)}, u32[]{:S(2)}) collective-permute-start(bf16[2,2,256,128]{3,2,1,0:T(8,128)(2,1)S(1)} %interface_collect.2.refs_8_.refs_0_.refs_4_.refs_10_), channel_id=1, source_target_pairs={{0,4},{1,5},{2,6},{3,7},{4,0},{5,1},{6,2},{7,3},{8,12},{9,13},{10,... | collective-permute-start | bytes 786440 | tf_op jit(solution)/shard_map/ppermute | solution.py:45
  53.0 13.6 %collective-permute-start.26 = (bf16[2,2,256,128]{3,2,1,0:T(8,128)(2,1)S(1)}, bf16[2,2,256,128]{3,2,1,0:T(8,128)(2,1)S(1)}, u32[]{:S(2)}, u32[]{:S(2)}) collective-permute-start(bf16[2,2,256,128]{3,2,1,0:T(8,128)(2,1)S(1)} %interface_collect.2.refs_8_.refs_0_.refs_4_.refs_10_), channel_id=1, source_target_pairs={{0,2},{1,3},{2,0},{3,1},{4,6},{5,7},{6,4},{7,5},{8,10},{9,11},{10,... | collective-permute-start | bytes 786440 | tf_op jit(solution)/shard_map/ppermute | solution.py:45
  57.0 5.9 %collective-permute-start.21 = (bf16[2,128,128]{2,1,0:T(8,128)(2,1)S(1)}, bf16[2,128,128]{2,1,0:T(8,128)(2,1)S(1)}, u32[]{:S(2)}, u32[]{:S(2)}) collective-permute-start(bf16[2,128,128]{2,1,0:T(8,128)(2,1)S(1)} %get-tuple-element.72), channel_id=1, source_target_pairs={{0,8},{8,0},{16,24},{24,16},{1,9},{9,1},{17,25},{25,17},{2,10},{10... | collective-permute-start | bytes 196616 | tf_op jit(solution)/shard_map/ppermute | solution.py:45
  57.8 6.3 %collective-permute-start.22 = (bf16[2,128,128]{2,1,0:T(8,128)(2,1)S(1)}, bf16[2,128,128]{2,1,0:T(8,128)(2,1)S(1)}, u32[]{:S(2)}, u32[]{:S(2)}) collective-permute-start(bf16[2,128,128]{2,1,0:T(8,128)(2,1)S(1)} %get-tuple-element.73), channel_id=1, source_target_pairs={{0,16},{8,24},{16,0},{24,8},{1,17},{9,25},{17,1},{25,9},{2,18},{10... | collective-permute-start | bytes 196616 | tf_op jit(solution)/shard_map/ppermute | solution.py:45
  59.9 6.1 %collective-permute-start.23 = (bf16[2,128,128]{2,1,0:T(8,128)(2,1)S(1)}, bf16[2,128,128]{2,1,0:T(8,128)(2,1)S(1)}, u32[]{:S(2)}, u32[]{:S(2)}) collective-permute-start(bf16[2,128,128]{2,1,0:T(8,128)(2,1)S(1)} %get-tuple-element.74), channel_id=1, source_target_pairs={{0,24},{8,16},{16,8},{24,0},{1,25},{9,17},{17,9},{25,1},{2,26},{10... | collective-permute-start | bytes 196616 | tf_op jit(solution)/shard_map/ppermute | solution.py:45
  62.9 18.6 %copy-start.9 = (bf16[16,256,256]{2,1,0:T(8,128)(2,1)S(1)}, bf16[16,256,256]{2,1,0:T(8,128)(2,1)}, u32[]{:S(2)}) copy-start(bf16[16,256,256]{2,1,0:T(8,128)(2,1)} %get-tuple-element.45.refs_3_.refs_2_) | copy-start | bytes 6291460
  66.6 14.9 %collective-permute-start.31 = (bf16[3,2,2,256,128]{4,3,2,1,0:T(8,128)(2,1)S(1)}, bf16[3,2,2,256,128]{4,3,2,1,0:T(8,128)(2,1)S(1)}, u32[]{:S(2)}, u32[]{:S(2)}) collective-permute-start(bf16[3,2,2,256,128]{4,3,2,1,0:T(8,128)(2,1)S(1)} %get-tuple-element.79), channel_id=1, source_target_pairs={{0,1},{1,0},{2,3},{3,2},{4,5},{5,4},{6,7},{7,6},{8,9},{9,8},{10,11... | collective-permute-start | bytes 2359304 | tf_op jit(solution)/shard_map/ppermute | solution.py:45
  66.7 9.2 %collective-permute-start.25 = (bf16[2,2,256,128]{3,2,1,0:T(8,128)(2,1)S(1)}, bf16[2,2,256,128]{3,2,1,0:T(8,128)(2,1)S(1)}, u32[]{:S(2)}, u32[]{:S(2)}) collective-permute-start(bf16[2,2,256,128]{3,2,1,0:T(8,128)(2,1)S(1)} %interface_collect.3.refs_3_.refs_0_.refs_11_.refs_4_), channel_id=1, source_target_pairs={{0,4},{1,5},{2,6},{3,7},{4,0},{5,1},{6,2},{7,3},{8,12},{9,13},{10,... | collective-permute-start | bytes 786440 | tf_op jit(solution)/shard_map/ppermute | solution.py:45
  67.4 9.2 %collective-permute-start.24 = (bf16[2,2,256,128]{3,2,1,0:T(8,128)(2,1)S(1)}, bf16[2,2,256,128]{3,2,1,0:T(8,128)(2,1)S(1)}, u32[]{:S(2)}, u32[]{:S(2)}) collective-permute-start(bf16[2,2,256,128]{3,2,1,0:T(8,128)(2,1)S(1)} %interface_collect.3.refs_3_.refs_0_.refs_11_.refs_4_), channel_id=1, source_target_pairs={{0,2},{1,3},{2,0},{3,1},{4,6},{5,7},{6,4},{7,5},{8,10},{9,11},{10,... | collective-permute-start | bytes 786440 | tf_op jit(solution)/shard_map/ppermute | solution.py:45
  68.9 9.7 %collective-permute-start.33 = (bf16[1,2,256,128]{3,2,1,0:T(8,128)(2,1)S(1)}, bf16[1,2,256,128]{3,2,1,0:T(8,128)(2,1)S(1)}, u32[]{:S(2)}, u32[]{:S(2)}) collective-permute-start(bf16[1,2,256,128]{3,2,1,0:T(8,128)(2,1)S(1)} %get-tuple-element.80), channel_id=1, source_target_pairs={{0,2},{1,3},{2,0},{3,1},{4,6},{5,7},{6,4},{7,5},{8,10},{9,11},{10,... | collective-permute-start | bytes 393224 | tf_op jit(solution)/shard_map/ppermute | solution.py:45
  69.4 9.2 %collective-permute-start.32 = (bf16[1,2,256,128]{3,2,1,0:T(8,128)(2,1)S(1)}, bf16[1,2,256,128]{3,2,1,0:T(8,128)(2,1)S(1)}, u32[]{:S(2)}, u32[]{:S(2)}) collective-permute-start(bf16[1,2,256,128]{3,2,1,0:T(8,128)(2,1)S(1)} %get-tuple-element.75.refs_3_), channel_id=1, source_target_pairs={{0,4},{1,5},{2,6},{3,7},{4,0},{5,1},{6,2},{7,3},{8,12},{9,13},{10,... | collective-permute-start | bytes 393224 | tf_op jit(solution)/shard_map/ppermute | solution.py:45
  78.6 3.0 %collective-permute-start.34 = (bf16[2,2,256,128]{3,2,1,0:T(8,128)(2,1)S(1)}, bf16[2,2,256,128]{3,2,1,0:T(8,128)(2,1)S(1)}, u32[]{:S(2)}, u32[]{:S(2)}) collective-permute-start(bf16[2,2,256,128]{3,2,1,0:T(8,128)(2,1)S(1)} %interface_join.2.refs_8_), channel_id=1, source_target_pairs={{0,1},{1,0},{2,3},{3,2},{4,5},{5,4},{6,7},{7,6},{8,9},{9,8},{10,11... | collective-permute-start | bytes 786440 | tf_op jit(solution)/shard_map/ppermute | solution.py:45
  78.6 7.1 %collective-permute-start.29 = (bf16[1,2,256,128]{3,2,1,0:T(8,128)(2,1)S(1)}, bf16[1,2,256,128]{3,2,1,0:T(8,128)(2,1)S(1)}, u32[]{:S(2)}, u32[]{:S(2)}) collective-permute-start(bf16[1,2,256,128]{3,2,1,0:T(8,128)(2,1)S(1)} %get-tuple-element.77.refs_2_.refs_12_), channel_id=1, source_target_pairs={{0,4},{1,5},{2,6},{3,7},{4,0},{5,1},{6,2},{7,3},{8,12},{9,13},{10,... | collective-permute-start | bytes 393224 | tf_op jit(solution)/shard_map/ppermute | solution.py:45
  80.1 5.6 %collective-permute-start.30 = (bf16[1,2,256,128]{3,2,1,0:T(8,128)(2,1)S(1)}, bf16[1,2,256,128]{3,2,1,0:T(8,128)(2,1)S(1)}, u32[]{:S(2)}, u32[]{:S(2)}) collective-permute-start(bf16[1,2,256,128]{3,2,1,0:T(8,128)(2,1)S(1)} %get-tuple-element.78), channel_id=1, source_target_pairs={{0,2},{1,3},{2,0},{3,1},{4,6},{5,7},{6,4},{7,5},{8,10},{9,11},{10,... | collective-permute-start | bytes 393224 | tf_op jit(solution)/shard_map/ppermute | solution.py:45
  81.5 4.3 %collective-permute-start.28 = (bf16[3,2,2,256,128]{4,3,2,1,0:T(8,128)(2,1)S(1)}, bf16[3,2,2,256,128]{4,3,2,1,0:T(8,128)(2,1)S(1)}, u32[]{:S(2)}, u32[]{:S(2)}) collective-permute-start(bf16[3,2,2,256,128]{4,3,2,1,0:T(8,128)(2,1)S(1)} %get-tuple-element.76), channel_id=1, source_target_pairs={{0,1},{1,0},{2,3},{3,2},{4,5},{5,4},{6,7},{7,6},{8,9},{9,8},{10,11... | collective-permute-start | bytes 2359304 | tf_op jit(solution)/shard_map/ppermute | solution.py:45
  85.7 1.6 %collective-permute-start.35 = (bf16[2,2,256,128]{3,2,1,0:T(8,128)(2,1)S(1)}, bf16[2,2,256,128]{3,2,1,0:T(8,128)(2,1)S(1)}, u32[]{:S(2)}, u32[]{:S(2)}) collective-permute-start(bf16[2,2,256,128]{3,2,1,0:T(8,128)(2,1)S(1)} %interface_join.3.refs_8_), channel_id=1, source_target_pairs={{0,1},{1,0},{2,3},{3,2},{4,5},{5,4},{6,7},{7,6},{8,9},{9,8},{10,11... | collective-permute-start | bytes 786440 | tf_op jit(solution)/shard_map/ppermute | solution.py:45

commit v7 on v6

--- a/solution.py
+++ b/solution.py
@@ -9,7 +9,7 @@
 
 HALVES = 2
 FIRST_ROOM = 52
-BRIEF = ("solve_join", "interface_first", "interface_relay", "interface_join")
+BRIEF = ("solve_join", "interface_first", "interface_join", "interface_second_1", "interface_relay_0")
 BF = jnp.bfloat16
 F32 = jnp.float32
 VMEM = pl.BlockSpec(memory_space=pltpu.VMEM)
@@ -60,7 +60,7 @@
     return (ids == anc_row).astype(F32).astype(BF)
 
 
-def forward_kernel(h, group, cap, owners, place, rhs, inv, off, anc, fwd, keep, send, part, ids, seen, *rest):
+def forward_kernel(h, group, cap, owners, place, rhs, inv, off, anc, keep, send, part, ids, seen, *rest):
     leaves, blk, cols = rhs.shape[2], rhs.shape[3], part.shape[4]
     fronts, rows, width = part.shape[0], keep.shape[3], keep.shape[4]
     me = place[1]
@@ -97,8 +97,7 @@
             vec = jnp.concatenate([vecs[0, leaf], vecs[1, leaf]], axis=0)
             values.append(dot(stacked(invs[leaf, 0], invs[leaf, 1]), vec).astype(BF))
         moved = [dot(stacked(offs[leaf, 0], offs[leaf, 1]), value).astype(BF) for leaf, value in zip(names, values)]
-        for leaf, value, shift in zip(names, values, moved):
-            fwd[leaf] = value
+        for leaf, shift in zip(names, moved):
             dist = owners[leaf] ^ me
             rank = seen[dist]
             seen[dist] = rank + 1
@@ -148,8 +147,8 @@
         "leaf_forward",
         [owners, place, leaf_rhs, leaf_inv, leaf_off, ancestors],
         [SMEM, SMEM] + [VMEM if h else HBM] * 4,
-        [shape_of((leaves, 2 * blk, cols)), block, block],
-        [VMEM, VMEM, VMEM],
+        [block, block],
+        [VMEM, VMEM],
         after,
         scratch,
         room=24 if h else FIRST_ROOM,
@@ -158,7 +157,8 @@
 
 def fold_kernel(inv, off, anc, out):
     leaves, _, blk, _ = inv.shape[1:]
-    rows = out.shape[2] // 2
+    wide = 2 * blk
+    rows = (out.shape[2] - wide) // 2
 
     def one(leaf, carry):
         mat = jnp.concatenate([inv[0, leaf, 0], inv[0, leaf, 1]], axis=1)
@@ -168,10 +168,11 @@
         table = table_of(anc[0, pl.ds(leaf, 1), :], rows)
         real = dot(both[:, :blk], table, ((1,), (1,))).astype(BF)
         imag = dot(both[:, blk:], table, ((1,), (1,))).astype(BF)
-        out[leaf, :blk, :rows] = real
-        out[leaf, :blk, rows:] = -imag
-        out[leaf, blk:, :rows] = imag
-        out[leaf, blk:, rows:] = real
+        out[leaf, :, :wide] = stacked(inv[0, leaf, 0], inv[0, leaf, 1])
+        out[leaf, :blk, wide : wide + rows] = -real
+        out[leaf, :blk, wide + rows :] = imag
+        out[leaf, blk:, wide : wide + rows] = -imag
+        out[leaf, blk:, wide + rows :] = -real
         return carry
 
     lax.fori_loop(0, leaves, one, 0, unroll=leaves)
@@ -181,7 +182,7 @@
     _, leaves, _, blk, _ = leaf_inv.shape
     return call(
         fold_kernel, "leaf_fold", [leaf_inv, leaf_off, ancestors], [VMEM] * 3,
-        shape_of((leaves, 2 * blk, 2 * rows)), VMEM, after,
+        shape_of((leaves, 2 * blk, 2 * blk + 2 * rows)), VMEM, after,
     )
 
 
@@ -247,10 +248,10 @@
             out[q] = value.astype(BF)
 
 
-def second_sums(half, keep, near, by_x, by_y, after):
+def second_sums(h, half, keep, near, by_x, by_y, after):
     shape = shape_of(keep.shape[1:])
     return call(
-        functools.partial(second_kernel, half), "interface_second", [keep, near, by_x, by_y], [VMEM] * 4,
+        functools.partial(second_kernel, half), f"interface_second_{h}", [keep, near, by_x, by_y], [VMEM] * 4,
         [shape, shape], [VMEM] * 2, after,
     )
 
@@ -361,25 +362,25 @@
         near[at] = ref[...]
 
 
-def relay(own, by_x, by_y, after):
+def relay(h, own, by_x, by_y, after):
     parts = own.shape[0]
     half = parts // 2
     return call(
-        functools.partial(relay_kernel, half), "interface_relay", [own, by_x, by_y], [VMEM] * 3,
+        functools.partial(relay_kernel, half), f"interface_relay_{h}", [own, by_x, by_y], [VMEM] * 3,
         [shape_of((half,) + own.shape[1:]), shape_of((parts - half,) + own.shape[1:]), shape_of((3,) + own.shape)],
         [VMEM] * 3, after,
     )
 
 
-def backward_kernel(h, named, count, cap, owns, aliased, owners, place, fwd, mats, *refs):
+def backward_kernel(h, named, count, cap, owns, aliased, owners, place, rhs, mats, *refs):
     fronts = len(named)
     fields, refs = refs[:count], refs[count:]
     roots, refs = refs[:owns], refs[owns + aliased :]
     out, refs = refs[0], refs[1:]
     held, slots, sems = refs[-3:]
-    leaves, wide, cols = fwd.shape
-    blk = wide // 2
-    tall = mats.shape[2]
+    leaves, wide, tall = mats.shape
+    blk, cols = wide // 2, rhs.shape[4] // HALVES
+    tall = tall - wide
     full = fronts * cap == leaves
     copies = []
     if owns:
@@ -406,7 +407,9 @@
         return pltpu.make_async_copy(held.at[leaf], out.at[0, :, leaf, :, pl.ds(h * cols, cols)], sems.at[leaf])
 
     def solve(name, field):
-        result = fwd[name].astype(F32) - dot(mats[name], field)
+        here = pl.ds(h * cols, cols)
+        vec = jnp.concatenate([rhs[0, 0, name, :, here], rhs[0, 1, name, :, here]], axis=0)
+        result = dot(mats[name, :, :wide], vec) + dot(mats[name, :, wide:], field)
         held[name, 0] = result[:blk].astype(BF)
         held[name, 1] = result[blk:].astype(BF)
 
@@ -435,9 +438,9 @@
         copy.wait()
 
 
-def backward(h, owners, place, fwd, mats, fields, roots, before, width, after):
-    leaves, wide, cols = fwd.shape
-    blk, fronts = wide // 2, len(fields)
+def backward(h, owners, place, leaf_rhs, mats, fields, roots, before, width, after):
+    leaves, wide, _ = mats.shape
+    blk, fronts, cols = wide // 2, len(fields), width // HALVES
     cap = -(-leaves // fronts)
     flat, named = [], []
     for field in fields:
@@ -458,7 +461,7 @@
         scratch = [pltpu.VMEM((2, rows, width), F32), pltpu.SemaphoreType.DMA]
     return call(
         functools.partial(backward_kernel, h, named, count, cap, len(roots), len(aliased)), "leaf_backward",
-        [owners, place, fwd, mats, *flat, *aliased], [SMEM, SMEM] + [VMEM] * (2 + len(flat)) + [HBM] * len(aliased),
+        [owners, place, leaf_rhs, mats, *flat, *aliased], [SMEM, SMEM] + [VMEM] * (2 + len(flat)) + [HBM] * len(aliased),
         outs, specs, after,
         scratch
         + [
@@ -482,10 +485,10 @@
     square = pairs == 4
 
     def start_forward(h, after):
-        fwd, keep, send = forward(
+        keep, send = forward(
             h, owners, place, leaf_rhs, leaf_inv, leaf_off, ancestors, fronts, rows, part, after
         )
-        return fwd, keep, crossed(send, "front", 1)
+        return keep, crossed(send, "front", 1)
 
     def send_first(keep, near, after):
         if not square:
@@ -494,10 +497,10 @@
         to_x, to_y = first_sums([(3, 0, parts // 2), (3, parts // 2, parts)], keep, near, after)
         return to_x, [crossed(to_x, "front", 2), crossed(to_y, "front", 4)]
 
-    def send_second(keep, near, got, after):
+    def send_second(h, keep, near, got, after):
         if not square:
             return got[0], got
-        to_x, to_y = second_sums(parts // 2, keep, near, *got, after)
+        to_x, to_y = second_sums(h, parts // 2, keep, near, *got, after)
         return to_x, [crossed(to_x, "front", 2), crossed(to_y, "front", 4)]
 
     def over_slabs(values):
@@ -506,10 +509,10 @@
     def share_first(own):
         return [crossed(own, "front", mask) for mask in ((2, 4) if square else range(2, fronts, 2))]
 
-    def share_second(own, got, after):
+    def share_second(h, own, got, after):
         if not square:
             return got[0], []
-        to_y, to_x, held = relay(own, *got, after)
+        to_y, to_x, held = relay(h, own, *got, after)
         return to_y, [crossed(to_y, "front", 4), crossed(to_x, "front", 2), crossed(held, "front", 1)]
 
     def share_third(own, got, more, after):
@@ -522,34 +525,36 @@
             fields += [[value], [(more[2], at)]]
         return fields + [[far], [crossed(far, "front", 1)]]
 
-    fwd0, keep0, near0 = start_forward(0, ())
-    same, other = pack(place, root_inv, coupling, [fwd0])
+    keep0, near0 = start_forward(0, ())
+    same, other = pack(place, root_inv, coupling, [keep0])
     have = [same, crossed(other, "slab", 1)]
     token, got0 = send_first(keep0, near0, [same])
-    fwd1, keep1, near1 = start_forward(1, [token, have[1]])
-    token, far0 = send_second(keep0, near0, got0, [fwd1])
+    keep1, near1 = start_forward(1, [token, have[1]])
+    token, far0 = send_second(0, keep0, near0, got0, [keep1])
     token, got1 = send_first(keep1, near1, [token])
     step = 2
     while step < slabs:
         token = join(have, [token])
         have = have + [crossed(token, "slab", step)]
         step *= 2
+    token, far1 = send_second(1, keep1, near1, got1, [token])
     pieces0 = reduce(0, place, root_rhs, keep0, near0, far0, slabs, blk, [token])
-    token, far1 = send_second(keep1, near1, got1, [pieces0[0]])
-    solved0 = chain(place, over_slabs(pieces0), have, [token])
-    pieces1 = reduce(1, place, root_rhs, keep1, near1, far1, slabs, blk, [solved0[0]])
-    own0 = collect(place, over_slabs(solved0), rows, [pieces1[0]])
+    pieces1 = reduce(1, place, root_rhs, keep1, near1, far1, slabs, blk, [pieces0[0]])
+    solved0 = chain(place, over_slabs(pieces0), have, [pieces1[0]])
+    solved1 = chain(place, over_slabs(pieces1), have, [solved0[0]])
+    own0 = collect(place, over_slabs(solved0), rows, [solved1[0]])
     got0 = share_first(own0)
-    solved1 = chain(place, over_slabs(pieces1), have, [own0])
-    folded = fold(leaf_inv, leaf_off, ancestors, rows, [solved1[0]])
-    own1 = collect(place, over_slabs(solved1), rows, [folded])
+    own1 = collect(place, over_slabs(solved1), rows, [own0])
     got1 = share_first(own1)
-    token, more0 = share_second(own0, got0, [own1])
-    token, more1 = share_second(own1, got1, [token])
+    folded = fold(leaf_inv, leaf_off, ancestors, rows, [own1])
+    token, more0 = share_second(0, own0, got0, [folded])
+    token, more1 = share_second(1, own1, got1, [token])
     fields0 = share_third(own0, got0, more0, [token])
-    leaf_sol, root_sol, token = backward(0, owners, place, fwd0, folded, fields0, [own0, own1], None, width, [token])
+    leaf_sol, root_sol, token = backward(
+        0, owners, place, leaf_rhs, folded, fields0, [own0, own1], None, width, [token]
+    )
     fields1 = share_third(own1, got1, more1, [token])
-    (leaf_sol,) = backward(1, owners, place, fwd1, folded, fields1, [], leaf_sol, width, ())
+    (leaf_sol,) = backward(1, owners, place, leaf_rhs, folded, fields1, [], leaf_sol, width, ())
     return leaf_sol, root_sol
 
 

time: 90.8 us -> 86.3 us (0.950)
  waiting for transfers between devices: 20.8 us -> 13.6 us
  starting transfers between devices: 43 us -> 46.4 us
  local copies, waits for them, and re-layouts: 2.97 us -> 1.38 us
  Pallas kernels: 22.7 us -> 23.8 us
    ppermute x36, waiting for transfers between devices: 20.8 us -> 13.6 us  [crossed(): lax.ppermute(x, axis, [(i, i ^ mask) for i in range(lax.axis_size(axis))])]
    ppermute x36, starting transfers between devices: 43 us -> 46.4 us  [crossed(): lax.ppermute(x, axis, [(i, i ^ mask) for i in range(lax.axis_size(axis))])]
    unnamed x20 -> x16, local copies, waits for them, and re-layouts: 2.97 us -> 1.38 us
    pallas_call x21, Pallas kernels: 22.7 us -> 23.8 us  [call(): pl.pallas_call(wrapped, in_specs=list(in_specs) + [ANY] * extra, out_spec...]
  transfers between devices with their start and end apart: 36 -> 36, of which waited for: 13 -> 10; matrix products, arithmetic and copies ran while one was open for 0% -> 0% of each run, Pallas kernels for 16% -> 17%
where the time goes in v7:
time: 86.3 us; the launch traced here: 86.1 us
  starting transfers between devices  46.4 us (54%)
  Pallas kernels  23.8 us (28%)
  waiting for transfers between devices  13.6 us (16%)
  local copies, waits for them, and re-layouts  1.38 us (2%)
  between operations  0.9 us (1%)
    ppermute x36, starting transfers between devices, crossed(): lax.ppermute(x, axis, [(i, i ^ mask) for i in range(lax.axis_size(axis))])  46.4 us
    pallas_call x21, Pallas kernels, call(): pl.pallas_call(wrapped, in_specs=list(in_specs) + [ANY] * extra, out_spec...  23.8 us
    ppermute x36, waiting for transfers between devices, crossed(): lax.ppermute(x, axis, [(i, i ^ mask) for i in range(lax.axis_size(axis))])  13.6 us
  transfers between devices with their start and end apart: 36, of which 10 were waited for; matrix products, arithmetic and copies ran while one was open for 0% of the time, Pallas kernels for 17%

profile of v7, /device:TPU:0, one launch (start us, length us, event | category | flops | bytes accessed | tf_op | source)
XLA Modules:
  0.0 86.1 jit_solution(3707048051598997354)
XLA Ops:
  0.7 0.7 copy-done.5
  1.4 0.7 copy-done.7
  2.1 5.3 %leaf_forward.2 = (bf16[4,2,2,256,128]{4,3,2,1,0:T(8,128)(2,1)S(1)}, bf16[4,2,2,256,128]{4,3,2,1,0:T(8,128)(2,1)}) custom-call(s32[16]{0:T(128)S(1)} %bitcast.5, s32[2]{0:T(128)S(1)} %pad_add_fusion.refs_1_.refs_0_, bf16[1,2,16,128,512]{4,3,2,1,0:T(8,128)(2,1)} %refs_2_.9, bf16[1,16,2,128,128]{4,3,2,1,0:T(8,128)(2,1)} %refs_0_.1, ...), custom_call_target="tpu_custom_call" | custom-call | flops 10000000000 | bytes 1 | tf_op jit(solution)/shard_map/leaf_forward/pallas_call | solution.py:31
  7.9 0.6 solve_pack.1
  8.5 2.7 %collective-permute-start.1 = (bf16[272,128]{1,0:T(8,128)(2,1)S(1)}, bf16[272,128]{1,0:T(8,128)(2,1)S(1)}, u32[]{:S(2)}, u32[]{:S(2)}) collective-permute-start(bf16[272,128]{1,0:T(8,128)(2,1)S(1)} %get-tuple-element.45), channel_id=1, source_target_pairs={{0,8},{8,0},{16,24},{24,16},{1,9},{9,1},{17,25},{25,17},{2,10},{10... | collective-permute-start | bytes 208904 | tf_op jit(solution)/shard_map/ppermute | solution.py:45
  11.3 2.2 %collective-permute-start.4 = (bf16[1,2,256,128]{3,2,1,0:T(8,128)(2,1)S(1)}, bf16[1,2,256,128]{3,2,1,0:T(8,128)(2,1)S(1)}, u32[]{:S(2)}, u32[]{:S(2)}) collective-permute-start(bf16[1,2,256,128]{3,2,1,0:T(8,128)(2,1)S(1)} %get-tuple-element.48), channel_id=1, source_target_pairs={{0,4},{1,5},{2,6},{3,7},{4,0},{5,1},{6,2},{7,3},{8,12},{9,13},{10,... | collective-permute-start | bytes 393224 | tf_op jit(solution)/shard_map/ppermute | solution.py:45
  13.4 1.5 %collective-permute-start.3 = (bf16[1,2,256,128]{3,2,1,0:T(8,128)(2,1)S(1)}, bf16[1,2,256,128]{3,2,1,0:T(8,128)(2,1)S(1)}, u32[]{:S(2)}, u32[]{:S(2)}) collective-permute-start(bf16[1,2,256,128]{3,2,1,0:T(8,128)(2,1)S(1)} %get-tuple-element.44.refs_6_), channel_id=1, source_target_pairs={{0,2},{1,3},{2,0},{3,1},{4,6},{5,7},{6,4},{7,5},{8,10},{9,11},{10,... | collective-permute-start | bytes 393224 | tf_op jit(solution)/shard_map/ppermute | solution.py:45
  15.0 2.6 %leaf_forward.3 = (bf16[4,2,2,256,128]{4,3,2,1,0:T(8,128)(2,1)S(1)}, bf16[4,2,2,256,128]{4,3,2,1,0:T(8,128)(2,1)S(1)}) custom-call(s32[16]{0:T(128)S(1)} %bitcast.6, s32[2]{0:T(128)S(1)} %pad_add_fusion.refs_1_.refs_0_, bf16[1,2,16,128,512]{4,3,2,1,0:T(8,128)(2,1)S(1)} %copy-done, bf16[1,16,2,128,128]{4,3,2,1,0:T(8,128)(2,1)S(1)} %copy-done.1, ...), custom_call_target="tpu_custom_call" | custom-call | flops 10000000000 | bytes 1 | tf_op jit(solution)/shard_map/leaf_forward/pallas_call | solution.py:31
  17.7 1.0 %collective-permute-done.3.refs_2_ = bf16[1,2,256,128]{3,2,1,0:T(8,128)(2,1)S(1)} collective-permute-done((bf16[1,2,256,128]{3,2,1,0:T(8,128)(2,1)S(1)}, bf16[1,2,256,128]{3,2,1,0:T(8,128)(2,1)S(1)}, u32[]{:S(2)}, u32[]{:S(2)}) %collective-permute-start.3) | collective-permute-done | bytes 131104 | tf_op jit(solution)/shard_map/ppermute | solution.py:45
  19.3 1.6 %collective-permute-start.9 = (bf16[2,2,256,128]{3,2,1,0:T(8,128)(2,1)S(1)}, bf16[2,2,256,128]{3,2,1,0:T(8,128)(2,1)S(1)}, u32[]{:S(2)}, u32[]{:S(2)}) collective-permute-start(bf16[2,2,256,128]{3,2,1,0:T(8,128)(2,1)S(1)} %get-tuple-element.49.refs_2_), channel_id=1, source_target_pairs={{0,2},{1,3},{2,0},{3,1},{4,6},{5,7},{6,4},{7,5},{8,10},{9,11},{10,... | collective-permute-start | bytes 786440 | tf_op jit(solution)/shard_map/ppermute | solution.py:45
  21.0 1.6 %collective-permute-start.6 = (bf16[1,2,256,128]{3,2,1,0:T(8,128)(2,1)S(1)}, bf16[1,2,256,128]{3,2,1,0:T(8,128)(2,1)S(1)}, u32[]{:S(2)}, u32[]{:S(2)}) collective-permute-start(bf16[1,2,256,128]{3,2,1,0:T(8,128)(2,1)S(1)} %get-tuple-element.51), channel_id=1, source_target_pairs={{0,4},{1,5},{2,6},{3,7},{4,0},{5,1},{6,2},{7,3},{8,12},{9,13},{10,... | collective-permute-start | bytes 393224 | tf_op jit(solution)/shard_map/ppermute | solution.py:45
  22.6 0.5 collective-permute-start.5
  23.1 2.7 %collective-permute-start.14 = (bf16[544,128]{1,0:T(8,128)(2,1)S(1)}, bf16[544,128]{1,0:T(8,128)(2,1)S(1)}, u32[]{:S(2)}, u32[]{:S(2)}) collective-permute-start(bf16[544,128]{1,0:T(8,128)(2,1)S(1)} %solve_join.1.refs_4_), channel_id=1, source_target_pairs={{0,16},{8,24},{16,0},{24,8},{1,17},{9,25},{17,1},{25,9},{2,18},{10... | collective-permute-start | bytes 417800 | tf_op jit(solution)/shard_map/ppermute | solution.py:45
  25.8 3.7 %collective-permute-done.6.refs_3_ = bf16[1,2,256,128]{3,2,1,0:T(8,128)(2,1)S(1)} collective-permute-done((bf16[1,2,256,128]{3,2,1,0:T(8,128)(2,1)S(1)}, bf16[1,2,256,128]{3,2,1,0:T(8,128)(2,1)S(1)}, u32[]{:S(2)}, u32[]{:S(2)}) %collective-permute-start.6) | collective-permute-done | bytes 131104 | tf_op jit(solution)/shard_map/ppermute | solution.py:45
  30.1 1.3 %collective-permute-start.8 = (bf16[2,2,256,128]{3,2,1,0:T(8,128)(2,1)S(1)}, bf16[2,2,256,128]{3,2,1,0:T(8,128)(2,1)S(1)}, u32[]{:S(2)}, u32[]{:S(2)}) collective-permute-start(bf16[2,2,256,128]{3,2,1,0:T(8,128)(2,1)S(1)} %get-tuple-element.53), channel_id=1, source_target_pairs={{0,4},{1,5},{2,6},{3,7},{4,0},{5,1},{6,2},{7,3},{8,12},{9,13},{10,... | collective-permute-start | bytes 786440 | tf_op jit(solution)/shard_map/ppermute | solution.py:45
  31.4 1.0 %collective-permute-start.7 = (bf16[2,2,256,128]{3,2,1,0:T(8,128)(2,1)S(1)}, bf16[2,2,256,128]{3,2,1,0:T(8,128)(2,1)S(1)}, u32[]{:S(2)}, u32[]{:S(2)}) collective-permute-start(bf16[2,2,256,128]{3,2,1,0:T(8,128)(2,1)S(1)} %get-tuple-element.52.refs_6_), channel_id=1, source_target_pairs={{0,2},{1,3},{2,0},{3,1},{4,6},{5,7},{6,4},{7,5},{8,10},{9,11},{10,... | collective-permute-start | bytes 786440 | tf_op jit(solution)/shard_map/ppermute | solution.py:45
  32.4 0.7 interface_reduce.2
  33.2 1.6 %collective-permute-start.15 = (bf16[2,128,128]{2,1,0:T(8,128)(2,1)S(1)}, bf16[2,128,128]{2,1,0:T(8,128)(2,1)S(1)}, u32[]{:S(2)}, u32[]{:S(2)}) collective-permute-start(bf16[2,128,128]{2,1,0:T(8,128)(2,1)S(1)} %get-tuple-element.60), channel_id=1, source_target_pairs={{0,8},{8,0},{16,24},{24,16},{1,9},{9,1},{17,25},{25,17},{2,10},{10... | collective-permute-start | bytes 196616 | tf_op jit(solution)/shard_map/ppermute | solution.py:45
  34.8 2.6 %collective-permute-start.16 = (bf16[2,128,128]{2,1,0:T(8,128)(2,1)S(1)}, bf16[2,128,128]{2,1,0:T(8,128)(2,1)S(1)}, u32[]{:S(2)}, u32[]{:S(2)}) collective-permute-start(bf16[2,128,128]{2,1,0:T(8,128)(2,1)S(1)} %get-tuple-element.61), channel_id=1, source_target_pairs={{0,16},{8,24},{16,0},{24,8},{1,17},{9,25},{17,1},{25,9},{2,18},{10... | collective-permute-start | bytes 196616 | tf_op jit(solution)/shard_map/ppermute | solution.py:45
  37.4 3.1 %collective-permute-start.17 = (bf16[2,128,128]{2,1,0:T(8,128)(2,1)S(1)}, bf16[2,128,128]{2,1,0:T(8,128)(2,1)S(1)}, u32[]{:S(2)}, u32[]{:S(2)}) collective-permute-start(bf16[2,128,128]{2,1,0:T(8,128)(2,1)S(1)} %get-tuple-element.62), channel_id=1, source_target_pairs={{0,24},{8,16},{16,8},{24,0},{1,25},{9,17},{17,9},{25,1},{2,26},{10... | collective-permute-start | bytes 196616 | tf_op jit(solution)/shard_map/ppermute | solution.py:45
  40.5 0.7 interface_reduce.3
  41.3 1.4 %collective-permute-start.12 = (bf16[2,128,128]{2,1,0:T(8,128)(2,1)S(1)}, bf16[2,128,128]{2,1,0:T(8,128)(2,1)S(1)}, u32[]{:S(2)}, u32[]{:S(2)}) collective-permute-start(bf16[2,128,128]{2,1,0:T(8,128)(2,1)S(1)} %get-tuple-element.58), channel_id=1, source_target_pairs={{0,16},{8,24},{16,0},{24,8},{1,17},{9,25},{17,1},{25,9},{2,18},{10... | collective-permute-start | bytes 196616 | tf_op jit(solution)/shard_map/ppermute | solution.py:45
  42.8 2.9 %collective-permute-start.13 = (bf16[2,128,128]{2,1,0:T(8,128)(2,1)S(1)}, bf16[2,128,128]{2,1,0:T(8,128)(2,1)S(1)}, u32[]{:S(2)}, u32[]{:S(2)}) collective-permute-start(bf16[2,128,128]{2,1,0:T(8,128)(2,1)S(1)} %get-tuple-element.59), channel_id=1, source_target_pairs={{0,24},{8,16},{16,8},{24,0},{1,25},{9,17},{17,9},{25,1},{2,26},{10... | collective-permute-start | bytes 196616 | tf_op jit(solution)/shard_map/ppermute | solution.py:45
  45.7 1.5 %sweep_chain.2 = (bf16[2,128,128]{2,1,0:T(8,128)(2,1)S(1)}, bf16[2,128,128]{2,1,0:T(8,128)(2,1)S(1)}, bf16[2,128,128]{2,1,0:T(8,128)(2,1)S(1)}, bf16[2,128,128]{2,1,0:T(8,128)(2,1)S(1)}) custom-call(s32[2]{0:T(128)S(1)} %pad_add_fusion.refs_1_.refs_0_, bf16[2,128,128]{2,1,0:T(8,128)(2,1)S(1)} %get-tuple-element.55.refs_6_.refs_1_, ...), custom_call_target="tpu_custom_call" | custom-call | flops 10000000000 | bytes 1 | tf_op jit(solution)/shard_map/sweep_chain/pallas_call | solution.py:31
  47.3 1.6 %collective-permute-start.22 = (bf16[2,128,128]{2,1,0:T(8,128)(2,1)S(1)}, bf16[2,128,128]{2,1,0:T(8,128)(2,1)S(1)}, u32[]{:S(2)}, u32[]{:S(2)}) collective-permute-start(bf16[2,128,128]{2,1,0:T(8,128)(2,1)S(1)} %get-tuple-element.69), channel_id=1, source_target_pairs={{0,16},{8,24},{16,0},{24,8},{1,17},{9,25},{17,1},{25,9},{2,18},{10... | collective-permute-start | bytes 196616 | tf_op jit(solution)/shard_map/ppermute | solution.py:45
  48.8 2.8 %collective-permute-start.23 = (bf16[2,128,128]{2,1,0:T(8,128)(2,1)S(1)}, bf16[2,128,128]{2,1,0:T(8,128)(2,1)S(1)}, u32[]{:S(2)}, u32[]{:S(2)}) collective-permute-start(bf16[2,128,128]{2,1,0:T(8,128)(2,1)S(1)} %get-tuple-element.70), channel_id=1, source_target_pairs={{0,24},{8,16},{16,8},{24,0},{1,25},{9,17},{17,9},{25,1},{2,26},{10... | collective-permute-start | bytes 196616 | tf_op jit(solution)/shard_map/ppermute | solution.py:45
  51.6 1.5 %sweep_chain.3 = (bf16[2,128,128]{2,1,0:T(8,128)(2,1)S(1)}, bf16[2,128,128]{2,1,0:T(8,128)(2,1)S(1)}, bf16[2,128,128]{2,1,0:T(8,128)(2,1)S(1)}, bf16[2,128,128]{2,1,0:T(8,128)(2,1)S(1)}) custom-call(s32[2]{0:T(128)S(1)} %pad_add_fusion.refs_1_.refs_0_, bf16[2,128,128]{2,1,0:T(8,128)(2,1)S(1)} %get-tuple-element.56.refs_8_.refs_1_, ...), custom_call_target="tpu_custom_call" | custom-call | flops 10000000000 | bytes 1 | tf_op jit(solution)/shard_map/sweep_chain/pallas_call | solution.py:31
  53.2 1.6 %collective-permute-start.19 = (bf16[2,128,128]{2,1,0:T(8,128)(2,1)S(1)}, bf16[2,128,128]{2,1,0:T(8,128)(2,1)S(1)}, u32[]{:S(2)}, u32[]{:S(2)}) collective-permute-start(bf16[2,128,128]{2,1,0:T(8,128)(2,1)S(1)} %get-tuple-element.66), channel_id=1, source_target_pairs={{0,16},{8,24},{16,0},{24,8},{1,17},{9,25},{17,1},{25,9},{2,18},{10... | collective-permute-start | bytes 196616 | tf_op jit(solution)/shard_map/ppermute | solution.py:45
  54.8 2.8 %collective-permute-start.20 = (bf16[2,128,128]{2,1,0:T(8,128)(2,1)S(1)}, bf16[2,128,128]{2,1,0:T(8,128)(2,1)S(1)}, u32[]{:S(2)}, u32[]{:S(2)}) collective-permute-start(bf16[2,128,128]{2,1,0:T(8,128)(2,1)S(1)} %get-tuple-element.67), channel_id=1, source_target_pairs={{0,24},{8,16},{16,8},{24,0},{1,25},{9,17},{17,9},{25,1},{2,26},{10... | collective-permute-start | bytes 196616 | tf_op jit(solution)/shard_map/ppermute | solution.py:45
  57.6 0.6 interface_collect.2.refs_5_.refs_0_.refs_4_.refs_10_
  58.2 1.1 %collective-permute-start.27 = (bf16[2,2,256,128]{3,2,1,0:T(8,128)(2,1)S(1)}, bf16[2,2,256,128]{3,2,1,0:T(8,128)(2,1)S(1)}, u32[]{:S(2)}, u32[]{:S(2)}) collective-permute-start(bf16[2,2,256,128]{3,2,1,0:T(8,128)(2,1)S(1)} %interface_collect.2.refs_5_.refs_0_.refs_4_.refs_10_), channel_id=1, source_target_pairs={{0,4},{1,5},{2,6},{3,7},{4,0},{5,1},{6,2},{7,3},{8,12},{9,13},{10,... | collective-permute-start | bytes 786440 | tf_op jit(solution)/shard_map/ppermute | solution.py:45
  59.2 1.1 %collective-permute-start.26 = (bf16[2,2,256,128]{3,2,1,0:T(8,128)(2,1)S(1)}, bf16[2,2,256,128]{3,2,1,0:T(8,128)(2,1)S(1)}, u32[]{:S(2)}, u32[]{:S(2)}) collective-permute-start(bf16[2,2,256,128]{3,2,1,0:T(8,128)(2,1)S(1)} %interface_collect.2.refs_5_.refs_0_.refs_4_.refs_10_), channel_id=1, source_target_pairs={{0,2},{1,3},{2,0},{3,1},{4,6},{5,7},{6,4},{7,5},{8,10},{9,11},{10,... | collective-permute-start | bytes 786440 | tf_op jit(solution)/shard_map/ppermute | solution.py:45
  60.3 0.6 collective-permute-done.20.refs_4_
  60.9 0.6 interface_collect.3.refs_3_.refs_0_.refs_11_.refs_4_
  61.5 1.1 %collective-permute-start.25 = (bf16[2,2,256,128]{3,2,1,0:T(8,128)(2,1)S(1)}, bf16[2,2,256,128]{3,2,1,0:T(8,128)(2,1)S(1)}, u32[]{:S(2)}, u32[]{:S(2)}) collective-permute-start(bf16[2,2,256,128]{3,2,1,0:T(8,128)(2,1)S(1)} %interface_collect.3.refs_3_.refs_0_.refs_11_.refs_4_), channel_id=1, source_target_pairs={{0,4},{1,5},{2,6},{3,7},{4,0},{5,1},{6,2},{7,3},{8,12},{9,13},{10,... | collective-permute-start | bytes 786440 | tf_op jit(solution)/shard_map/ppermute | solution.py:45
  62.6 1.1 %collective-permute-start.24 = (bf16[2,2,256,128]{3,2,1,0:T(8,128)(2,1)S(1)}, bf16[2,2,256,128]{3,2,1,0:T(8,128)(2,1)S(1)}, u32[]{:S(2)}, u32[]{:S(2)}) collective-permute-start(bf16[2,2,256,128]{3,2,1,0:T(8,128)(2,1)S(1)} %interface_collect.3.refs_3_.refs_0_.refs_11_.refs_4_), channel_id=1, source_target_pairs={{0,2},{1,3},{2,0},{3,1},{4,6},{5,7},{6,4},{7,5},{8,10},{9,11},{10,... | collective-permute-start | bytes 786440 | tf_op jit(solution)/shard_map/ppermute | solution.py:45
  63.7 1.5 %leaf_fold.1.refs_3_ = bf16[16,256,768]{2,1,0:T(8,128)(2,1)S(1)} custom-call(bf16[1,16,2,128,128]{4,3,2,1,0:T(8,128)(2,1)S(1)} %copy-done.1, bf16[1,16,2,128,128]{4,3,2,1,0:T(8,128)(2,1)S(1)} %copy-done.2, s32[1,16,128]{2,1,0:T(8,128)S(1)} %copy-done.5, bf16[2,2,256,128]{3,2,1,0:T(8,128)(2,1)S(1)} %interface_collect.3.refs_3_.refs_0_.refs_11_.refs_4_), custom_call_target="tpu_custom_call" | custom-call | flops 10000000000 | bytes 1 | tf_op jit(solution)/shard_map/leaf_fold/pallas_call | solution.py:31
  65.2 1.5 %collective-permute-done.27.refs_2_.refs_7_ = bf16[2,2,256,128]{3,2,1,0:T(8,128)(2,1)S(1)} collective-permute-done((bf16[2,2,256,128]{3,2,1,0:T(8,128)(2,1)S(1)}, bf16[2,2,256,128]{3,2,1,0:T(8,128)(2,1)S(1)}, u32[]{:S(2)}, u32[]{:S(2)}) %collective-permute-start.27) | collective-permute-done | bytes 262176 | tf_op jit(solution)/shard_map/ppermute | solution.py:45
  67.1 1.3 %collective-permute-start.33 = (bf16[1,2,256,128]{3,2,1,0:T(8,128)(2,1)S(1)}, bf16[1,2,256,128]{3,2,1,0:T(8,128)(2,1)S(1)}, u32[]{:S(2)}, u32[]{:S(2)}) collective-permute-start(bf16[1,2,256,128]{3,2,1,0:T(8,128)(2,1)S(1)} %get-tuple-element.76), channel_id=1, source_target_pairs={{0,2},{1,3},{2,0},{3,1},{4,6},{5,7},{6,4},{7,5},{8,10},{9,11},{10,... | collective-permute-start | bytes 393224 | tf_op jit(solution)/shard_map/ppermute | solution.py:45
  68.4 1.6 %collective-permute-start.32 = (bf16[1,2,256,128]{3,2,1,0:T(8,128)(2,1)S(1)}, bf16[1,2,256,128]{3,2,1,0:T(8,128)(2,1)S(1)}, u32[]{:S(2)}, u32[]{:S(2)}) collective-permute-start(bf16[1,2,256,128]{3,2,1,0:T(8,128)(2,1)S(1)} %get-tuple-element.71.refs_3_), channel_id=1, source_target_pairs={{0,4},{1,5},{2,6},{3,7},{4,0},{5,1},{6,2},{7,3},{8,12},{9,13},{10,... | collective-permute-start | bytes 393224 | tf_op jit(solution)/shard_map/ppermute | solution.py:45
  70.1 2.1 %collective-permute-done.33.refs_1_ = bf16[1,2,256,128]{3,2,1,0:T(8,128)(2,1)S(1)} collective-permute-done((bf16[1,2,256,128]{3,2,1,0:T(8,128)(2,1)S(1)}, bf16[1,2,256,128]{3,2,1,0:T(8,128)(2,1)S(1)}, u32[]{:S(2)}, u32[]{:S(2)}) %collective-permute-start.33) | collective-permute-done | bytes 131104 | tf_op jit(solution)/shard_map/ppermute | solution.py:45
  72.2 1.2 %collective-permute-done.32.refs_0_ = bf16[1,2,256,128]{3,2,1,0:T(8,128)(2,1)S(1)} collective-permute-done((bf16[1,2,256,128]{3,2,1,0:T(8,128)(2,1)S(1)}, bf16[1,2,256,128]{3,2,1,0:T(8,128)(2,1)S(1)}, u32[]{:S(2)}, u32[]{:S(2)}) %collective-permute-start.32) | collective-permute-done | bytes 131104 | tf_op jit(solution)/shard_map/ppermute | solution.py:45
  73.5 1.7 %collective-permute-start.29 = (bf16[1,2,256,128]{3,2,1,0:T(8,128)(2,1)S(1)}, bf16[1,2,256,128]{3,2,1,0:T(8,128)(2,1)S(1)}, u32[]{:S(2)}, u32[]{:S(2)}) collective-permute-start(bf16[1,2,256,128]{3,2,1,0:T(8,128)(2,1)S(1)} %get-tuple-element.73.refs_2_.refs_12_), channel_id=1, source_target_pairs={{0,4},{1,5},{2,6},{3,7},{4,0},{5,1},{6,2},{7,3},{8,12},{9,13},{10,... | collective-permute-start | bytes 393224 | tf_op jit(solution)/shard_map/ppermute | solution.py:45
  75.1 0.5 collective-permute-start.30
  75.7 3.8 %leaf_backward.2 = (bf16[1,2,16,128,512]{4,3,2,1,0:T(8,128)(2,1)}, f32[1,2,256,512]{3,2,1,0:T(8,128)}, f32[8,128]{1,0:T(8,128)S(1)}) custom-call(s32[16]{0:T(128)S(1)} %bitcast.7, s32[2]{0:T(128)S(1)} %pad_add_fusion.refs_1_.refs_0_, bf16[1,2,16,128,512]{4,3,2,1,0:T(8,128)(2,1)S(1)} %copy-done, bf16[16,256,768]{2,1,0:T(8,128)(2,1)S(1)} %leaf_fold.1.refs_3_, ...), custom_call_target="tpu_custom_call" | custom-call | flops 10000000000 | bytes 1 | tf_op jit(solution)/shard_map/leaf_backward/pallas_call | solution.py:31
  79.5 1.2 %collective-permute-done.30.refs_1_ = bf16[1,2,256,128]{3,2,1,0:T(8,128)(2,1)S(1)} collective-permute-done((bf16[1,2,256,128]{3,2,1,0:T(8,128)(2,1)S(1)}, bf16[1,2,256,128]{3,2,1,0:T(8,128)(2,1)S(1)}, u32[]{:S(2)}, u32[]{:S(2)}) %collective-permute-start.30) | collective-permute-done | bytes 131104 | tf_op jit(solution)/shard_map/ppermute | solution.py:45
  80.8 1.5 %collective-permute-done.35.refs_9_ = bf16[2,2,256,128]{3,2,1,0:T(8,128)(2,1)S(1)} collective-permute-done((bf16[2,2,256,128]{3,2,1,0:T(8,128)(2,1)S(1)}, bf16[2,2,256,128]{3,2,1,0:T(8,128)(2,1)S(1)}, u32[]{:S(2)}, u32[]{:S(2)}) %collective-permute-start.35) | collective-permute-done | bytes 262176 | tf_op jit(solution)/shard_map/ppermute | solution.py:45
  82.3 3.8 %leaf_backward.3 = bf16[1,2,16,128,512]{4,3,2,1,0:T(8,128)(2,1)} custom-call(s32[16]{0:T(128)S(1)} %bitcast.8, s32[2]{0:T(128)S(1)} %pad_add_fusion.refs_1_.refs_0_, bf16[1,2,16,128,512]{4,3,2,1,0:T(8,128)(2,1)S(1)} %copy-done, bf16[16,256,768]{2,1,0:T(8,128)(2,1)S(1)} %leaf_fold.1.refs_3_, ...), custom_call_target="tpu_custom_call", output_to_operand_aliasing={{}: (10, {})} | custom-call | flops 10000000000 | bytes 1 | tf_op jit(solution)/shard_map/leaf_backward/pallas_call | solution.py:31
  (62 shorter events, 3.1 us)
Async XLA Ops:
  0.7 0.7 copy-start.5
  1.4 0.7 copy-start.7
  2.1 5.9 %copy-start.4 = (f32[1,2,2,128,128]{4,3,2,1,0:T(8,128)S(1)}, f32[1,2,2,128,128]{4,3,2,1,0:T(8,128)}, u32[]{:S(2)}) copy-start(f32[1,2,2,128,128]{4,3,2,1,0:T(8,128)} %refs_1_.4) | copy-start | bytes 786436
  2.1 5.9 %copy-start.6 = (f32[1,256]{1,0:T(1,128)S(1)}, f32[1,256]{1,0:T(1,128)}, u32[]{:S(2)}) copy-start(f32[1,256]{1,0:T(1,128)} %param.15) | copy-start | bytes 3076
  7.4 3.8 %collective-permute-start = (bf16[4,2,2,256,128]{4,3,2,1,0:T(8,128)(2,1)}, bf16[4,2,2,256,128]{4,3,2,1,0:T(8,128)(2,1)S(1)}, u32[]{:S(2)}, u32[]{:S(2)}) collective-permute-start(bf16[4,2,2,256,128]{4,3,2,1,0:T(8,128)(2,1)} %get-tuple-element.42), channel_id=1, source_target_pairs={{0,1},{1,0},{2,3},{3,2},{4,5},{5,4},{6,7},{7,6},{8,9},{9,8},{10,11... | collective-permute-start | bytes 3145736 | tf_op jit(solution)/shard_map/ppermute | solution.py:45
  7.9 7.0 %copy-start = (bf16[1,2,16,128,512]{4,3,2,1,0:T(8,128)(2,1)S(1)}, bf16[1,2,16,128,512]{4,3,2,1,0:T(8,128)(2,1)}, u32[]{:S(2)}) copy-start(bf16[1,2,16,128,512]{4,3,2,1,0:T(8,128)(2,1)} %refs_2_.9) | copy-start | bytes 12582916
  7.9 7.0 %copy-start.1 = (bf16[1,16,2,128,128]{4,3,2,1,0:T(8,128)(2,1)S(1)}, bf16[1,16,2,128,128]{4,3,2,1,0:T(8,128)(2,1)}, u32[]{:S(2)}) copy-start(bf16[1,16,2,128,128]{4,3,2,1,0:T(8,128)(2,1)} %refs_0_.1) | copy-start | bytes 3145732
  7.9 7.0 %copy-start.2 = (bf16[1,16,2,128,128]{4,3,2,1,0:T(8,128)(2,1)S(1)}, bf16[1,16,2,128,128]{4,3,2,1,0:T(8,128)(2,1)}, u32[]{:S(2)}) copy-start(bf16[1,16,2,128,128]{4,3,2,1,0:T(8,128)(2,1)} %refs_1_.7) | copy-start | bytes 3145732
  8.5 6.4 %collective-permute-start.1 = (bf16[272,128]{1,0:T(8,128)(2,1)S(1)}, bf16[272,128]{1,0:T(8,128)(2,1)S(1)}, u32[]{:S(2)}, u32[]{:S(2)}) collective-permute-start(bf16[272,128]{1,0:T(8,128)(2,1)S(1)} %get-tuple-element.45), channel_id=1, source_target_pairs={{0,8},{8,0},{16,24},{24,16},{1,9},{9,1},{17,25},{25,17},{2,10},{10... | collective-permute-start | bytes 208904 | tf_op jit(solution)/shard_map/ppermute | solution.py:45
  11.3 6.4 %collective-permute-start.4 = (bf16[1,2,256,128]{3,2,1,0:T(8,128)(2,1)S(1)}, bf16[1,2,256,128]{3,2,1,0:T(8,128)(2,1)S(1)}, u32[]{:S(2)}, u32[]{:S(2)}) collective-permute-start(bf16[1,2,256,128]{3,2,1,0:T(8,128)(2,1)S(1)} %get-tuple-element.48), channel_id=1, source_target_pairs={{0,4},{1,5},{2,6},{3,7},{4,0},{5,1},{6,2},{7,3},{8,12},{9,13},{10,... | collective-permute-start | bytes 393224 | tf_op jit(solution)/shard_map/ppermute | solution.py:45
  13.4 5.3 %collective-permute-start.3 = (bf16[1,2,256,128]{3,2,1,0:T(8,128)(2,1)S(1)}, bf16[1,2,256,128]{3,2,1,0:T(8,128)(2,1)S(1)}, u32[]{:S(2)}, u32[]{:S(2)}) collective-permute-start(bf16[1,2,256,128]{3,2,1,0:T(8,128)(2,1)S(1)} %get-tuple-element.44.refs_6_), channel_id=1, source_target_pairs={{0,2},{1,3},{2,0},{3,1},{4,6},{5,7},{6,4},{7,5},{8,10},{9,11},{10,... | collective-permute-start | bytes 393224 | tf_op jit(solution)/shard_map/ppermute | solution.py:45
  17.6 3.3 %collective-permute-start.2 = (bf16[4,2,2,256,128]{4,3,2,1,0:T(8,128)(2,1)S(1)}, bf16[4,2,2,256,128]{4,3,2,1,0:T(8,128)(2,1)S(1)}, u32[]{:S(2)}, u32[]{:S(2)}) collective-permute-start(bf16[4,2,2,256,128]{4,3,2,1,0:T(8,128)(2,1)S(1)} %get-tuple-element.47), channel_id=1, source_target_pairs={{0,1},{1,0},{2,3},{3,2},{4,5},{5,4},{6,7},{7,6},{8,9},{9,8},{10,11... | collective-permute-start | bytes 3145736 | tf_op jit(solution)/shard_map/ppermute | solution.py:45
  18.9 13.6 %copy-start.3 = (bf16[1,2,256,512]{3,2,1,0:T(8,128)(2,1)S(1)}, bf16[1,2,256,512]{3,2,1,0:T(8,128)(2,1)}, u32[]{:S(2)}) copy-start(bf16[1,2,256,512]{3,2,1,0:T(8,128)(2,1)} %refs_1_.6) | copy-start | bytes 1572868
  18.9 13.5 %collective-permute-start.10 = (bf16[2,2,256,128]{3,2,1,0:T(8,128)(2,1)S(1)}, bf16[2,2,256,128]{3,2,1,0:T(8,128)(2,1)S(1)}, u32[]{:S(2)}, u32[]{:S(2)}) collective-permute-start(bf16[2,2,256,128]{3,2,1,0:T(8,128)(2,1)S(1)} %get-tuple-element.54), channel_id=1, source_target_pairs={{0,4},{1,5},{2,6},{3,7},{4,0},{5,1},{6,2},{7,3},{8,12},{9,13},{10,... | collective-permute-start | bytes 786440 | tf_op jit(solution)/shard_map/ppermute | solution.py:45
  19.3 13.1 %collective-permute-start.9 = (bf16[2,2,256,128]{3,2,1,0:T(8,128)(2,1)S(1)}, bf16[2,2,256,128]{3,2,1,0:T(8,128)(2,1)S(1)}, u32[]{:S(2)}, u32[]{:S(2)}) collective-permute-start(bf16[2,2,256,128]{3,2,1,0:T(8,128)(2,1)S(1)} %get-tuple-element.49.refs_2_), channel_id=1, source_target_pairs={{0,2},{1,3},{2,0},{3,1},{4,6},{5,7},{6,4},{7,5},{8,10},{9,11},{10,... | collective-permute-start | bytes 786440 | tf_op jit(solution)/shard_map/ppermute | solution.py:45
  21.0 8.4 %collective-permute-start.6 = (bf16[1,2,256,128]{3,2,1,0:T(8,128)(2,1)S(1)}, bf16[1,2,256,128]{3,2,1,0:T(8,128)(2,1)S(1)}, u32[]{:S(2)}, u32[]{:S(2)}) collective-permute-start(bf16[1,2,256,128]{3,2,1,0:T(8,128)(2,1)S(1)} %get-tuple-element.51), channel_id=1, source_target_pairs={{0,4},{1,5},{2,6},{3,7},{4,0},{5,1},{6,2},{7,3},{8,12},{9,13},{10,... | collective-permute-start | bytes 393224 | tf_op jit(solution)/shard_map/ppermute | solution.py:45
  22.6 7.3 %collective-permute-start.5 = (bf16[1,2,256,128]{3,2,1,0:T(8,128)(2,1)S(1)}, bf16[1,2,256,128]{3,2,1,0:T(8,128)(2,1)S(1)}, u32[]{:S(2)}, u32[]{:S(2)}) collective-permute-start(bf16[1,2,256,128]{3,2,1,0:T(8,128)(2,1)S(1)} %get-tuple-element.50.refs_2_), channel_id=1, source_target_pairs={{0,2},{1,3},{2,0},{3,1},{4,6},{5,7},{6,4},{7,5},{8,10},{9,11},{10,... | collective-permute-start | bytes 393224 | tf_op jit(solution)/shard_map/ppermute | solution.py:45
  23.1 18.2 %collective-permute-start.14 = (bf16[544,128]{1,0:T(8,128)(2,1)S(1)}, bf16[544,128]{1,0:T(8,128)(2,1)S(1)}, u32[]{:S(2)}, u32[]{:S(2)}) collective-permute-start(bf16[544,128]{1,0:T(8,128)(2,1)S(1)} %solve_join.1.refs_4_), channel_id=1, source_target_pairs={{0,16},{8,24},{16,0},{24,8},{1,17},{9,25},{17,1},{25,9},{2,18},{10... | collective-permute-start | bytes 417800 | tf_op jit(solution)/shard_map/ppermute | solution.py:45
  30.1 7.3 %collective-permute-start.8 = (bf16[2,2,256,128]{3,2,1,0:T(8,128)(2,1)S(1)}, bf16[2,2,256,128]{3,2,1,0:T(8,128)(2,1)S(1)}, u32[]{:S(2)}, u32[]{:S(2)}) collective-permute-start(bf16[2,2,256,128]{3,2,1,0:T(8,128)(2,1)S(1)} %get-tuple-element.53), channel_id=1, source_target_pairs={{0,4},{1,5},{2,6},{3,7},{4,0},{5,1},{6,2},{7,3},{8,12},{9,13},{10,... | collective-permute-start | bytes 786440 | tf_op jit(solution)/shard_map/ppermute | solution.py:45
  31.4 9.1 %collective-permute-start.7 = (bf16[2,2,256,128]{3,2,1,0:T(8,128)(2,1)S(1)}, bf16[2,2,256,128]{3,2,1,0:T(8,128)(2,1)S(1)}, u32[]{:S(2)}, u32[]{:S(2)}) collective-permute-start(bf16[2,2,256,128]{3,2,1,0:T(8,128)(2,1)S(1)} %get-tuple-element.52.refs_6_), channel_id=1, source_target_pairs={{0,2},{1,3},{2,0},{3,1},{4,6},{5,7},{6,4},{7,5},{8,10},{9,11},{10,... | collective-permute-start | bytes 786440 | tf_op jit(solution)/shard_map/ppermute | solution.py:45
  33.2 9.6 %collective-permute-start.15 = (bf16[2,128,128]{2,1,0:T(8,128)(2,1)S(1)}, bf16[2,128,128]{2,1,0:T(8,128)(2,1)S(1)}, u32[]{:S(2)}, u32[]{:S(2)}) collective-permute-start(bf16[2,128,128]{2,1,0:T(8,128)(2,1)S(1)} %get-tuple-element.60), channel_id=1, source_target_pairs={{0,8},{8,0},{16,24},{24,16},{1,9},{9,1},{17,25},{25,17},{2,10},{10... | collective-permute-start | bytes 196616 | tf_op jit(solution)/shard_map/ppermute | solution.py:45
  34.8 10.9 %collective-permute-start.16 = (bf16[2,128,128]{2,1,0:T(8,128)(2,1)S(1)}, bf16[2,128,128]{2,1,0:T(8,128)(2,1)S(1)}, u32[]{:S(2)}, u32[]{:S(2)}) collective-permute-start(bf16[2,128,128]{2,1,0:T(8,128)(2,1)S(1)} %get-tuple-element.61), channel_id=1, source_target_pairs={{0,16},{8,24},{16,0},{24,8},{1,17},{9,25},{17,1},{25,9},{2,18},{10... | collective-permute-start | bytes 196616 | tf_op jit(solution)/shard_map/ppermute | solution.py:45
  37.4 8.3 %collective-permute-start.17 = (bf16[2,128,128]{2,1,0:T(8,128)(2,1)S(1)}, bf16[2,128,128]{2,1,0:T(8,128)(2,1)S(1)}, u32[]{:S(2)}, u32[]{:S(2)}) collective-permute-start(bf16[2,128,128]{2,1,0:T(8,128)(2,1)S(1)} %get-tuple-element.62), channel_id=1, source_target_pairs={{0,24},{8,16},{16,8},{24,0},{1,25},{9,17},{17,9},{25,1},{2,26},{10... | collective-permute-start | bytes 196616 | tf_op jit(solution)/shard_map/ppermute | solution.py:45
  41.2 7.6 %collective-permute-start.11 = (bf16[2,128,128]{2,1,0:T(8,128)(2,1)S(1)}, bf16[2,128,128]{2,1,0:T(8,128)(2,1)S(1)}, u32[]{:S(2)}, u32[]{:S(2)}) collective-permute-start(bf16[2,128,128]{2,1,0:T(8,128)(2,1)S(1)} %get-tuple-element.57), channel_id=1, source_target_pairs={{0,8},{8,0},{16,24},{24,16},{1,9},{9,1},{17,25},{25,17},{2,10},{10... | collective-permute-start | bytes 196616 | tf_op jit(solution)/shard_map/ppermute | solution.py:45
  41.3 10.3 %collective-permute-start.12 = (bf16[2,128,128]{2,1,0:T(8,128)(2,1)S(1)}, bf16[2,128,128]{2,1,0:T(8,128)(2,1)S(1)}, u32[]{:S(2)}, u32[]{:S(2)}) collective-permute-start(bf16[2,128,128]{2,1,0:T(8,128)(2,1)S(1)} %get-tuple-element.58), channel_id=1, source_target_pairs={{0,16},{8,24},{16,0},{24,8},{1,17},{9,25},{17,1},{25,9},{2,18},{10... | collective-permute-start | bytes 196616 | tf_op jit(solution)/shard_map/ppermute | solution.py:45
  42.8 8.9 %collective-permute-start.13 = (bf16[2,128,128]{2,1,0:T(8,128)(2,1)S(1)}, bf16[2,128,128]{2,1,0:T(8,128)(2,1)S(1)}, u32[]{:S(2)}, u32[]{:S(2)}) collective-permute-start(bf16[2,128,128]{2,1,0:T(8,128)(2,1)S(1)} %get-tuple-element.59), channel_id=1, source_target_pairs={{0,24},{8,16},{16,8},{24,0},{1,25},{9,17},{17,9},{25,1},{2,26},{10... | collective-permute-start | bytes 196616 | tf_op jit(solution)/shard_map/ppermute | solution.py:45
  47.2 7.6 %collective-permute-start.21 = (bf16[2,128,128]{2,1,0:T(8,128)(2,1)S(1)}, bf16[2,128,128]{2,1,0:T(8,128)(2,1)S(1)}, u32[]{:S(2)}, u32[]{:S(2)}) collective-permute-start(bf16[2,128,128]{2,1,0:T(8,128)(2,1)S(1)} %get-tuple-element.68), channel_id=1, source_target_pairs={{0,8},{8,0},{16,24},{24,16},{1,9},{9,1},{17,25},{25,17},{2,10},{10... | collective-permute-start | bytes 196616 | tf_op jit(solution)/shard_map/ppermute | solution.py:45
  47.3 10.3 %collective-permute-start.22 = (bf16[2,128,128]{2,1,0:T(8,128)(2,1)S(1)}, bf16[2,128,128]{2,1,0:T(8,128)(2,1)S(1)}, u32[]{:S(2)}, u32[]{:S(2)}) collective-permute-start(bf16[2,128,128]{2,1,0:T(8,128)(2,1)S(1)} %get-tuple-element.69), channel_id=1, source_target_pairs={{0,16},{8,24},{16,0},{24,8},{1,17},{9,25},{17,1},{25,9},{2,18},{10... | collective-permute-start | bytes 196616 | tf_op jit(solution)/shard_map/ppermute | solution.py:45
  48.8 8.8 %collective-permute-start.23 = (bf16[2,128,128]{2,1,0:T(8,128)(2,1)S(1)}, bf16[2,128,128]{2,1,0:T(8,128)(2,1)S(1)}, u32[]{:S(2)}, u32[]{:S(2)}) collective-permute-start(bf16[2,128,128]{2,1,0:T(8,128)(2,1)S(1)} %get-tuple-element.70), channel_id=1, source_target_pairs={{0,24},{8,16},{16,8},{24,0},{1,25},{9,17},{17,9},{25,1},{2,26},{10... | collective-permute-start | bytes 196616 | tf_op jit(solution)/shard_map/ppermute | solution.py:45
  53.1 7.2 %collective-permute-start.18 = (bf16[2,128,128]{2,1,0:T(8,128)(2,1)S(1)}, bf16[2,128,128]{2,1,0:T(8,128)(2,1)S(1)}, u32[]{:S(2)}, u32[]{:S(2)}) collective-permute-start(bf16[2,128,128]{2,1,0:T(8,128)(2,1)S(1)} %get-tuple-element.65), channel_id=1, source_target_pairs={{0,8},{8,0},{16,24},{24,16},{1,9},{9,1},{17,25},{25,17},{2,10},{10... | collective-permute-start | bytes 196616 | tf_op jit(solution)/shard_map/ppermute | solution.py:45
  53.2 7.1 %collective-permute-start.19 = (bf16[2,128,128]{2,1,0:T(8,128)(2,1)S(1)}, bf16[2,128,128]{2,1,0:T(8,128)(2,1)S(1)}, u32[]{:S(2)}, u32[]{:S(2)}) collective-permute-start(bf16[2,128,128]{2,1,0:T(8,128)(2,1)S(1)} %get-tuple-element.66), channel_id=1, source_target_pairs={{0,16},{8,24},{16,0},{24,8},{1,17},{9,25},{17,1},{25,9},{2,18},{10... | collective-permute-start | bytes 196616 | tf_op jit(solution)/shard_map/ppermute | solution.py:45
  54.8 6.1 %collective-permute-start.20 = (bf16[2,128,128]{2,1,0:T(8,128)(2,1)S(1)}, bf16[2,128,128]{2,1,0:T(8,128)(2,1)S(1)}, u32[]{:S(2)}, u32[]{:S(2)}) collective-permute-start(bf16[2,128,128]{2,1,0:T(8,128)(2,1)S(1)} %get-tuple-element.67), channel_id=1, source_target_pairs={{0,24},{8,16},{16,8},{24,0},{1,25},{9,17},{17,9},{25,1},{2,26},{10... | collective-permute-start | bytes 196616 | tf_op jit(solution)/shard_map/ppermute | solution.py:45
  58.2 8.5 %collective-permute-start.27 = (bf16[2,2,256,128]{3,2,1,0:T(8,128)(2,1)S(1)}, bf16[2,2,256,128]{3,2,1,0:T(8,128)(2,1)S(1)}, u32[]{:S(2)}, u32[]{:S(2)}) collective-permute-start(bf16[2,2,256,128]{3,2,1,0:T(8,128)(2,1)S(1)} %interface_collect.2.refs_5_.refs_0_.refs_4_.refs_10_), channel_id=1, source_target_pairs={{0,4},{1,5},{2,6},{3,7},{4,0},{5,1},{6,2},{7,3},{8,12},{9,13},{10,... | collective-permute-start | bytes 786440 | tf_op jit(solution)/shard_map/ppermute | solution.py:45
  59.2 7.8 %collective-permute-start.26 = (bf16[2,2,256,128]{3,2,1,0:T(8,128)(2,1)S(1)}, bf16[2,2,256,128]{3,2,1,0:T(8,128)(2,1)S(1)}, u32[]{:S(2)}, u32[]{:S(2)}) collective-permute-start(bf16[2,2,256,128]{3,2,1,0:T(8,128)(2,1)S(1)} %interface_collect.2.refs_5_.refs_0_.refs_4_.refs_10_), channel_id=1, source_target_pairs={{0,2},{1,3},{2,0},{3,1},{4,6},{5,7},{6,4},{7,5},{8,10},{9,11},{10,... | collective-permute-start | bytes 786440 | tf_op jit(solution)/shard_map/ppermute | solution.py:45
  61.5 8.5 %collective-permute-start.25 = (bf16[2,2,256,128]{3,2,1,0:T(8,128)(2,1)S(1)}, bf16[2,2,256,128]{3,2,1,0:T(8,128)(2,1)S(1)}, u32[]{:S(2)}, u32[]{:S(2)}) collective-permute-start(bf16[2,2,256,128]{3,2,1,0:T(8,128)(2,1)S(1)} %interface_collect.3.refs_3_.refs_0_.refs_11_.refs_4_), channel_id=1, source_target_pairs={{0,4},{1,5},{2,6},{3,7},{4,0},{5,1},{6,2},{7,3},{8,12},{9,13},{10,... | collective-permute-start | bytes 786440 | tf_op jit(solution)/shard_map/ppermute | solution.py:45
  62.6 7.5 %collective-permute-start.24 = (bf16[2,2,256,128]{3,2,1,0:T(8,128)(2,1)S(1)}, bf16[2,2,256,128]{3,2,1,0:T(8,128)(2,1)S(1)}, u32[]{:S(2)}, u32[]{:S(2)}) collective-permute-start(bf16[2,2,256,128]{3,2,1,0:T(8,128)(2,1)S(1)} %interface_collect.3.refs_3_.refs_0_.refs_11_.refs_4_), channel_id=1, source_target_pairs={{0,2},{1,3},{2,0},{3,1},{4,6},{5,7},{6,4},{7,5},{8,10},{9,11},{10,... | collective-permute-start | bytes 786440 | tf_op jit(solution)/shard_map/ppermute | solution.py:45
  67.1 5.0 %collective-permute-start.33 = (bf16[1,2,256,128]{3,2,1,0:T(8,128)(2,1)S(1)}, bf16[1,2,256,128]{3,2,1,0:T(8,128)(2,1)S(1)}, u32[]{:S(2)}, u32[]{:S(2)}) collective-permute-start(bf16[1,2,256,128]{3,2,1,0:T(8,128)(2,1)S(1)} %get-tuple-element.76), channel_id=1, source_target_pairs={{0,2},{1,3},{2,0},{3,1},{4,6},{5,7},{6,4},{7,5},{8,10},{9,11},{10,... | collective-permute-start | bytes 393224 | tf_op jit(solution)/shard_map/ppermute | solution.py:45
  68.4 5.0 %collective-permute-start.32 = (bf16[1,2,256,128]{3,2,1,0:T(8,128)(2,1)S(1)}, bf16[1,2,256,128]{3,2,1,0:T(8,128)(2,1)S(1)}, u32[]{:S(2)}, u32[]{:S(2)}) collective-permute-start(bf16[1,2,256,128]{3,2,1,0:T(8,128)(2,1)S(1)} %get-tuple-element.71.refs_3_), channel_id=1, source_target_pairs={{0,4},{1,5},{2,6},{3,7},{4,0},{5,1},{6,2},{7,3},{8,12},{9,13},{10,... | collective-permute-start | bytes 393224 | tf_op jit(solution)/shard_map/ppermute | solution.py:45
  70.0 5.7 %collective-permute-start.31 = (bf16[3,2,2,256,128]{4,3,2,1,0:T(8,128)(2,1)S(1)}, bf16[3,2,2,256,128]{4,3,2,1,0:T(8,128)(2,1)S(1)}, u32[]{:S(2)}, u32[]{:S(2)}) collective-permute-start(bf16[3,2,2,256,128]{4,3,2,1,0:T(8,128)(2,1)S(1)} %get-tuple-element.75), channel_id=1, source_target_pairs={{0,1},{1,0},{2,3},{3,2},{4,5},{5,4},{6,7},{7,6},{8,9},{9,8},{10,11... | collective-permute-start | bytes 2359304 | tf_op jit(solution)/shard_map/ppermute | solution.py:45
  73.4 2.3 %collective-permute-start.34 = (bf16[2,2,256,128]{3,2,1,0:T(8,128)(2,1)S(1)}, bf16[2,2,256,128]{3,2,1,0:T(8,128)(2,1)S(1)}, u32[]{:S(2)}, u32[]{:S(2)}) collective-permute-start(bf16[2,2,256,128]{3,2,1,0:T(8,128)(2,1)S(1)} %interface_join.2.refs_8_), channel_id=1, source_target_pairs={{0,1},{1,0},{2,3},{3,2},{4,5},{5,4},{6,7},{7,6},{8,9},{9,8},{10,11... | collective-permute-start | bytes 786440 | tf_op jit(solution)/shard_map/ppermute | solution.py:45
  73.5 7.2 %collective-permute-start.29 = (bf16[1,2,256,128]{3,2,1,0:T(8,128)(2,1)S(1)}, bf16[1,2,256,128]{3,2,1,0:T(8,128)(2,1)S(1)}, u32[]{:S(2)}, u32[]{:S(2)}) collective-permute-start(bf16[1,2,256,128]{3,2,1,0:T(8,128)(2,1)S(1)} %get-tuple-element.73.refs_2_.refs_12_), channel_id=1, source_target_pairs={{0,4},{1,5},{2,6},{3,7},{4,0},{5,1},{6,2},{7,3},{8,12},{9,13},{10,... | collective-permute-start | bytes 393224 | tf_op jit(solution)/shard_map/ppermute | solution.py:45
  75.1 5.6 %collective-permute-start.30 = (bf16[1,2,256,128]{3,2,1,0:T(8,128)(2,1)S(1)}, bf16[1,2,256,128]{3,2,1,0:T(8,128)(2,1)S(1)}, u32[]{:S(2)}, u32[]{:S(2)}) collective-permute-start(bf16[1,2,256,128]{3,2,1,0:T(8,128)(2,1)S(1)} %get-tuple-element.74), channel_id=1, source_target_pairs={{0,2},{1,3},{2,0},{3,1},{4,6},{5,7},{6,4},{7,5},{8,10},{9,11},{10,... | collective-permute-start | bytes 393224 | tf_op jit(solution)/shard_map/ppermute | solution.py:45
  75.7 5.1 %collective-permute-start.28 = (bf16[3,2,2,256,128]{4,3,2,1,0:T(8,128)(2,1)S(1)}, bf16[3,2,2,256,128]{4,3,2,1,0:T(8,128)(2,1)S(1)}, u32[]{:S(2)}, u32[]{:S(2)}) collective-permute-start(bf16[3,2,2,256,128]{4,3,2,1,0:T(8,128)(2,1)S(1)} %get-tuple-element.72), channel_id=1, source_target_pairs={{0,1},{1,0},{2,3},{3,2},{4,5},{5,4},{6,7},{7,6},{8,9},{9,8},{10,11... | collective-permute-start | bytes 2359304 | tf_op jit(solution)/shard_map/ppermute | solution.py:45
  80.7 1.6 %collective-permute-start.35 = (bf16[2,2,256,128]{3,2,1,0:T(8,128)(2,1)S(1)}, bf16[2,2,256,128]{3,2,1,0:T(8,128)(2,1)S(1)}, u32[]{:S(2)}, u32[]{:S(2)}) collective-permute-start(bf16[2,2,256,128]{3,2,1,0:T(8,128)(2,1)S(1)} %interface_join.3.refs_8_), channel_id=1, source_target_pairs={{0,1},{1,0},{2,3},{3,2},{4,5},{5,4},{6,7},{7,6},{8,9},{9,8},{10,11... | collective-permute-start | bytes 786440 | tf_op jit(solution)/shard_map/ppermute | solution.py:45

commit v8 on v7

--- a/solution.py
+++ b/solution.py
@@ -384,8 +384,7 @@
     full = fronts * cap == leaves
     copies = []
     if owns:
-        root, token, wider, root_sem = refs[:4]
-        token[...] = jnp.zeros(token.shape, F32)
+        root, wider, root_sem = refs[:3]
         parts, _, _, part = roots[0].shape
         for at, ref in enumerate(roots):
             for q in range(parts):
@@ -457,7 +456,7 @@
     outs, specs, scratch = [shape_of((1, 2, leaves, blk, width))], [HBM], []
     if roots:
         rows = roots[0].shape[2]
-        outs, specs = outs + [shape_of((1, 2, rows, width), F32), shape_of((8, 128), F32)], [HBM, HBM, VMEM]
+        outs, specs = outs + [shape_of((1, 2, rows, width), F32)], [HBM, HBM]
         scratch = [pltpu.VMEM((2, rows, width), F32), pltpu.SemaphoreType.DMA]
     return call(
         functools.partial(backward_kernel, h, named, count, cap, len(roots), len(aliased)), "leaf_backward",
@@ -515,24 +514,26 @@
         to_y, to_x, held = relay(h, own, *got, after)
         return to_y, [crossed(to_y, "front", 4), crossed(to_x, "front", 2), crossed(held, "front", 1)]
 
-    def share_third(own, got, more, after):
+    def share_third(owns, gots, mores):
         if not square:
-            mine = [own] + got
-            return [[value] for field in mine for value in (field, crossed(field, "front", 1))]
-        far = join(more[:2], after, "interface_join")
+            whole = [[own] + got for own, got in zip(owns, gots)]
+            return [[[value] for field in mine for value in (field, crossed(field, "front", 1))] for mine in whole]
+        far = join([value for more in mores for value in more[:2]], (), "interface_join")
+        there = crossed(far, "front", 1)
         fields = []
-        for at, value in enumerate([own] + got):
-            fields += [[value], [(more[2], at)]]
-        return fields + [[far], [crossed(far, "front", 1)]]
+        for h, (own, got, more) in enumerate(zip(owns, gots, mores)):
+            span = pl.ds(h * parts, parts)
+            near = [field for at, value in enumerate([own] + got) for field in ([value], [(more[2], at)])]
+            fields.append(near + [[(far, span)], [(there, span)]])
+        return fields
 
     keep0, near0 = start_forward(0, ())
-    same, other = pack(place, root_inv, coupling, [keep0])
-    have = [same, crossed(other, "slab", 1)]
-    token, got0 = send_first(keep0, near0, [same])
-    keep1, near1 = start_forward(1, [token, have[1]])
+    token, got0 = send_first(keep0, near0, ())
+    keep1, near1 = start_forward(1, [token])
     token, far0 = send_second(0, keep0, near0, got0, [keep1])
     token, got1 = send_first(keep1, near1, [token])
-    step = 2
+    same, other = pack(place, root_inv, coupling, [token])
+    have, step = [same, crossed(other, "slab", 1)], 2
     while step < slabs:
         token = join(have, [token])
         have = have + [crossed(token, "slab", step)]
@@ -548,12 +549,11 @@
     got1 = share_first(own1)
     folded = fold(leaf_inv, leaf_off, ancestors, rows, [own1])
     token, more0 = share_second(0, own0, got0, [folded])
-    token, more1 = share_second(1, own1, got1, [token])
-    fields0 = share_third(own0, got0, more0, [token])
-    leaf_sol, root_sol, token = backward(
-        0, owners, place, leaf_rhs, folded, fields0, [own0, own1], None, width, [token]
-    )
-    fields1 = share_third(own1, got1, more1, [token])
+    _, more1 = share_second(1, own1, got1, [token])
+    fields0, fields1 = share_third((own0, own1), (got0, got1), (more0, more1))
+    leaf_sol, root_sol = backward(
+        0, owners, place, leaf_rhs, folded, fields0, [own0, own1], None, width, ()
+    )
     (leaf_sol,) = backward(1, owners, place, leaf_rhs, folded, fields1, [], leaf_sol, width, ())
     return leaf_sol, root_sol
 

time: 86.3 us -> 85.7 us (level)
  starting transfers between devices: 46.4 us -> 43.8 us
  waiting for transfers between devices: 13.6 us -> 15.6 us
    ppermute x36 -> x35, starting transfers between devices: 46.4 us -> 43.8 us  [crossed(): lax.ppermute(x, axis, [(i, i ^ mask) for i in range(lax.axis_size(axis))])]
    ppermute x36 -> x35, waiting for transfers between devices: 13.6 us -> 15.6 us  [crossed(): lax.ppermute(x, axis, [(i, i ^ mask) for i in range(lax.axis_size(axis))])]
    pallas_call x21 -> x20, Pallas kernels: 23.8 us -> 23.9 us  [call(): pl.pallas_call(wrapped, in_specs=list(in_specs) + [ANY] * extra, out_spec...]
  transfers between devices with their start and end apart: 36 -> 35, of which waited for: 10 -> 13; matrix products, arithmetic and copies ran while one was open for 0% -> 0% of each run, Pallas kernels for 17% -> 17%
where the time goes in v8:
time: 85.7 us; the launch traced here: 85.5 us
  starting transfers between devices  43.8 us (51%)
  Pallas kernels  23.9 us (28%)
  waiting for transfers between devices  15.6 us (18%)
  local copies, waits for them, and re-layouts  1.37 us (2%)
    ppermute x35, starting transfers between devices, crossed(): lax.ppermute(x, axis, [(i, i ^ mask) for i in range(lax.axis_size(axis))])  43.8 us
    pallas_call x20, Pallas kernels, call(): pl.pallas_call(wrapped, in_specs=list(in_specs) + [ANY] * extra, out_spec...  23.9 us
    ppermute x35, waiting for transfers between devices, crossed(): lax.ppermute(x, axis, [(i, i ^ mask) for i in range(lax.axis_size(axis))])  15.6 us
  transfers between devices with their start and end apart: 35, of which 13 were waited for; matrix products, arithmetic and copies ran while one was open for 0% of the time, Pallas kernels for 17%

profile of v8, /device:TPU:0, one launch (start us, length us, event | category | flops | bytes accessed | tf_op | source)
XLA Modules:
  0.0 85.5 jit_solution(16346704331767010908)
XLA Ops:
  0.7 0.7 copy-done.5
  1.4 0.7 copy-done.7
  2.1 5.6 %leaf_forward.2 = (bf16[4,2,2,256,128]{4,3,2,1,0:T(8,128)(2,1)S(1)}, bf16[4,2,2,256,128]{4,3,2,1,0:T(8,128)(2,1)}) custom-call(s32[16]{0:T(128)S(1)} %bitcast.5, s32[2]{0:T(128)S(1)} %pad_add_fusion.refs_1_.refs_0_, bf16[1,2,16,128,512]{4,3,2,1,0:T(8,128)(2,1)} %refs_2_.9, bf16[1,16,2,128,128]{4,3,2,1,0:T(8,128)(2,1)} %refs_0_.1, ...), custom_call_target="tpu_custom_call" | custom-call | flops 10000000000 | bytes 1 | tf_op jit(solution)/shard_map/leaf_forward/pallas_call | solution.py:31
  8.2 2.5 %collective-permute-done.refs_1_.refs_3_ = bf16[4,2,2,256,128]{4,3,2,1,0:T(8,128)(2,1)S(1)} collective-permute-done((bf16[4,2,2,256,128]{4,3,2,1,0:T(8,128)(2,1)}, bf16[4,2,2,256,128]{4,3,2,1,0:T(8,128)(2,1)S(1)}, u32[]{:S(2)}, u32[]{:S(2)}) %collective-permute-start) | collective-permute-done | bytes 1048608 | tf_op jit(solution)/shard_map/ppermute | solution.py:45
  10.7 3.0 %collective-permute-start.3 = (bf16[1,2,256,128]{3,2,1,0:T(8,128)(2,1)S(1)}, bf16[1,2,256,128]{3,2,1,0:T(8,128)(2,1)S(1)}, u32[]{:S(2)}, u32[]{:S(2)}) collective-permute-start(bf16[1,2,256,128]{3,2,1,0:T(8,128)(2,1)S(1)} %get-tuple-element.45), channel_id=1, source_target_pairs={{0,4},{1,5},{2,6},{3,7},{4,0},{5,1},{6,2},{7,3},{8,12},{9,13},{10,... | collective-permute-start | bytes 393224 | tf_op jit(solution)/shard_map/ppermute | solution.py:45
  13.7 1.5 %collective-permute-start.2 = (bf16[1,2,256,128]{3,2,1,0:T(8,128)(2,1)S(1)}, bf16[1,2,256,128]{3,2,1,0:T(8,128)(2,1)S(1)}, u32[]{:S(2)}, u32[]{:S(2)}) collective-permute-start(bf16[1,2,256,128]{3,2,1,0:T(8,128)(2,1)S(1)} %get-tuple-element.42.refs_6_), channel_id=1, source_target_pairs={{0,2},{1,3},{2,0},{3,1},{4,6},{5,7},{6,4},{7,5},{8,10},{9,11},{10,... | collective-permute-start | bytes 393224 | tf_op jit(solution)/shard_map/ppermute | solution.py:45
  15.2 2.6 %leaf_forward.3 = (bf16[4,2,2,256,128]{4,3,2,1,0:T(8,128)(2,1)S(1)}, bf16[4,2,2,256,128]{4,3,2,1,0:T(8,128)(2,1)S(1)}) custom-call(s32[16]{0:T(128)S(1)} %bitcast.6, s32[2]{0:T(128)S(1)} %pad_add_fusion.refs_1_.refs_0_, bf16[1,2,16,128,512]{4,3,2,1,0:T(8,128)(2,1)S(1)} %copy-done, bf16[1,16,2,128,128]{4,3,2,1,0:T(8,128)(2,1)S(1)} %copy-done.1, ...), custom_call_target="tpu_custom_call" | custom-call | flops 10000000000 | bytes 1 | tf_op jit(solution)/shard_map/leaf_forward/pallas_call | solution.py:31
  17.9 1.1 %collective-permute-done.2.refs_2_ = bf16[1,2,256,128]{3,2,1,0:T(8,128)(2,1)S(1)} collective-permute-done((bf16[1,2,256,128]{3,2,1,0:T(8,128)(2,1)S(1)}, bf16[1,2,256,128]{3,2,1,0:T(8,128)(2,1)S(1)}, u32[]{:S(2)}, u32[]{:S(2)}) %collective-permute-start.2) | collective-permute-done | bytes 131104 | tf_op jit(solution)/shard_map/ppermute | solution.py:45
  19.5 1.6 %collective-permute-start.9 = (bf16[2,2,256,128]{3,2,1,0:T(8,128)(2,1)S(1)}, bf16[2,2,256,128]{3,2,1,0:T(8,128)(2,1)S(1)}, u32[]{:S(2)}, u32[]{:S(2)}) collective-permute-start(bf16[2,2,256,128]{3,2,1,0:T(8,128)(2,1)S(1)} %get-tuple-element.46.refs_2_), channel_id=1, source_target_pairs={{0,2},{1,3},{2,0},{3,1},{4,6},{5,7},{6,4},{7,5},{8,10},{9,11},{10,... | collective-permute-start | bytes 786440 | tf_op jit(solution)/shard_map/ppermute | solution.py:45
  21.3 1.6 %collective-permute-start.5 = (bf16[1,2,256,128]{3,2,1,0:T(8,128)(2,1)S(1)}, bf16[1,2,256,128]{3,2,1,0:T(8,128)(2,1)S(1)}, u32[]{:S(2)}, u32[]{:S(2)}) collective-permute-start(bf16[1,2,256,128]{3,2,1,0:T(8,128)(2,1)S(1)} %get-tuple-element.48), channel_id=1, source_target_pairs={{0,4},{1,5},{2,6},{3,7},{4,0},{5,1},{6,2},{7,3},{8,12},{9,13},{10,... | collective-permute-start | bytes 393224 | tf_op jit(solution)/shard_map/ppermute | solution.py:45
  24.0 1.6 %collective-permute-start.6 = (bf16[272,128]{1,0:T(8,128)(2,1)S(1)}, bf16[272,128]{1,0:T(8,128)(2,1)S(1)}, u32[]{:S(2)}, u32[]{:S(2)}) collective-permute-start(bf16[272,128]{1,0:T(8,128)(2,1)S(1)} %get-tuple-element.50), channel_id=1, source_target_pairs={{0,8},{8,0},{16,24},{24,16},{1,9},{9,1},{17,25},{25,17},{2,10},{10... | collective-permute-start | bytes 208904 | tf_op jit(solution)/shard_map/ppermute | solution.py:45
  25.6 2.7 %collective-permute-done.6.refs_1_.refs_6_ = bf16[272,128]{1,0:T(8,128)(2,1)S(1)} collective-permute-done((bf16[272,128]{1,0:T(8,128)(2,1)S(1)}, bf16[272,128]{1,0:T(8,128)(2,1)S(1)}, u32[]{:S(2)}, u32[]{:S(2)}) %collective-permute-start.6) | collective-permute-done | bytes 69664 | tf_op jit(solution)/shard_map/ppermute | solution.py:45
  28.3 2.7 %collective-permute-start.14 = (bf16[544,128]{1,0:T(8,128)(2,1)S(1)}, bf16[544,128]{1,0:T(8,128)(2,1)S(1)}, u32[]{:S(2)}, u32[]{:S(2)}) collective-permute-start(bf16[544,128]{1,0:T(8,128)(2,1)S(1)} %solve_join.1.refs_4_), channel_id=1, source_target_pairs={{0,16},{8,24},{16,0},{24,8},{1,17},{9,25},{17,1},{25,9},{2,18},{10... | collective-permute-start | bytes 417800 | tf_op jit(solution)/shard_map/ppermute | solution.py:45
  31.2 0.6 collective-permute-start.8
  31.7 1.5 %collective-permute-start.7 = (bf16[2,2,256,128]{3,2,1,0:T(8,128)(2,1)S(1)}, bf16[2,2,256,128]{3,2,1,0:T(8,128)(2,1)S(1)}, u32[]{:S(2)}, u32[]{:S(2)}) collective-permute-start(bf16[2,2,256,128]{3,2,1,0:T(8,128)(2,1)S(1)} %get-tuple-element.51.refs_6_), channel_id=1, source_target_pairs={{0,2},{1,3},{2,0},{3,1},{4,6},{5,7},{6,4},{7,5},{8,10},{9,11},{10,... | collective-permute-start | bytes 786440 | tf_op jit(solution)/shard_map/ppermute | solution.py:45
  33.2 0.7 interface_reduce.2
  34.0 1.6 %collective-permute-start.15 = (bf16[2,128,128]{2,1,0:T(8,128)(2,1)S(1)}, bf16[2,128,128]{2,1,0:T(8,128)(2,1)S(1)}, u32[]{:S(2)}, u32[]{:S(2)}) collective-permute-start(bf16[2,128,128]{2,1,0:T(8,128)(2,1)S(1)} %get-tuple-element.59), channel_id=1, source_target_pairs={{0,8},{8,0},{16,24},{24,16},{1,9},{9,1},{17,25},{25,17},{2,10},{10... | collective-permute-start | bytes 196616 | tf_op jit(solution)/shard_map/ppermute | solution.py:45
  35.6 2.0 %collective-permute-start.16 = (bf16[2,128,128]{2,1,0:T(8,128)(2,1)S(1)}, bf16[2,128,128]{2,1,0:T(8,128)(2,1)S(1)}, u32[]{:S(2)}, u32[]{:S(2)}) collective-permute-start(bf16[2,128,128]{2,1,0:T(8,128)(2,1)S(1)} %get-tuple-element.60), channel_id=1, source_target_pairs={{0,16},{8,24},{16,0},{24,8},{1,17},{9,25},{17,1},{25,9},{2,18},{10... | collective-permute-start | bytes 196616 | tf_op jit(solution)/shard_map/ppermute | solution.py:45
  37.6 2.5 %collective-permute-start.17 = (bf16[2,128,128]{2,1,0:T(8,128)(2,1)S(1)}, bf16[2,128,128]{2,1,0:T(8,128)(2,1)S(1)}, u32[]{:S(2)}, u32[]{:S(2)}) collective-permute-start(bf16[2,128,128]{2,1,0:T(8,128)(2,1)S(1)} %get-tuple-element.61), channel_id=1, source_target_pairs={{0,24},{8,16},{16,8},{24,0},{1,25},{9,17},{17,9},{25,1},{2,26},{10... | collective-permute-start | bytes 196616 | tf_op jit(solution)/shard_map/ppermute | solution.py:45
  40.2 0.7 interface_reduce.3
  41.0 2.0 %collective-permute-start.12 = (bf16[2,128,128]{2,1,0:T(8,128)(2,1)S(1)}, bf16[2,128,128]{2,1,0:T(8,128)(2,1)S(1)}, u32[]{:S(2)}, u32[]{:S(2)}) collective-permute-start(bf16[2,128,128]{2,1,0:T(8,128)(2,1)S(1)} %get-tuple-element.57), channel_id=1, source_target_pairs={{0,16},{8,24},{16,0},{24,8},{1,17},{9,25},{17,1},{25,9},{2,18},{10... | collective-permute-start | bytes 196616 | tf_op jit(solution)/shard_map/ppermute | solution.py:45
  42.9 2.4 %collective-permute-start.13 = (bf16[2,128,128]{2,1,0:T(8,128)(2,1)S(1)}, bf16[2,128,128]{2,1,0:T(8,128)(2,1)S(1)}, u32[]{:S(2)}, u32[]{:S(2)}) collective-permute-start(bf16[2,128,128]{2,1,0:T(8,128)(2,1)S(1)} %get-tuple-element.58), channel_id=1, source_target_pairs={{0,24},{8,16},{16,8},{24,0},{1,25},{9,17},{17,9},{25,1},{2,26},{10... | collective-permute-start | bytes 196616 | tf_op jit(solution)/shard_map/ppermute | solution.py:45
  45.4 1.5 %sweep_chain.2 = (bf16[2,128,128]{2,1,0:T(8,128)(2,1)S(1)}, bf16[2,128,128]{2,1,0:T(8,128)(2,1)S(1)}, bf16[2,128,128]{2,1,0:T(8,128)(2,1)S(1)}, bf16[2,128,128]{2,1,0:T(8,128)(2,1)S(1)}) custom-call(s32[2]{0:T(128)S(1)} %pad_add_fusion.refs_1_.refs_0_, bf16[2,128,128]{2,1,0:T(8,128)(2,1)S(1)} %get-tuple-element.54.refs_6_.refs_1_, ...), custom_call_target="tpu_custom_call" | custom-call | flops 10000000000 | bytes 1 | tf_op jit(solution)/shard_map/sweep_chain/pallas_call | solution.py:31
  46.8 0.9 %collective-permute-start.21 = (bf16[2,128,128]{2,1,0:T(8,128)(2,1)S(1)}, bf16[2,128,128]{2,1,0:T(8,128)(2,1)S(1)}, u32[]{:S(2)}, u32[]{:S(2)}) collective-permute-start(bf16[2,128,128]{2,1,0:T(8,128)(2,1)S(1)} %get-tuple-element.67), channel_id=1, source_target_pairs={{0,8},{8,0},{16,24},{24,16},{1,9},{9,1},{17,25},{25,17},{2,10},{10... | collective-permute-start | bytes 196616 | tf_op jit(solution)/shard_map/ppermute | solution.py:45
  47.7 1.1 %collective-permute-start.22 = (bf16[2,128,128]{2,1,0:T(8,128)(2,1)S(1)}, bf16[2,128,128]{2,1,0:T(8,128)(2,1)S(1)}, u32[]{:S(2)}, u32[]{:S(2)}) collective-permute-start(bf16[2,128,128]{2,1,0:T(8,128)(2,1)S(1)} %get-tuple-element.68), channel_id=1, source_target_pairs={{0,16},{8,24},{16,0},{24,8},{1,17},{9,25},{17,1},{25,9},{2,18},{10... | collective-permute-start | bytes 196616 | tf_op jit(solution)/shard_map/ppermute | solution.py:45
  48.9 2.4 %collective-permute-start.23 = (bf16[2,128,128]{2,1,0:T(8,128)(2,1)S(1)}, bf16[2,128,128]{2,1,0:T(8,128)(2,1)S(1)}, u32[]{:S(2)}, u32[]{:S(2)}) collective-permute-start(bf16[2,128,128]{2,1,0:T(8,128)(2,1)S(1)} %get-tuple-element.69), channel_id=1, source_target_pairs={{0,24},{8,16},{16,8},{24,0},{1,25},{9,17},{17,9},{25,1},{2,26},{10... | collective-permute-start | bytes 196616 | tf_op jit(solution)/shard_map/ppermute | solution.py:45
  51.3 1.5 %sweep_chain.3 = (bf16[2,128,128]{2,1,0:T(8,128)(2,1)S(1)}, bf16[2,128,128]{2,1,0:T(8,128)(2,1)S(1)}, bf16[2,128,128]{2,1,0:T(8,128)(2,1)S(1)}, bf16[2,128,128]{2,1,0:T(8,128)(2,1)S(1)}) custom-call(s32[2]{0:T(128)S(1)} %pad_add_fusion.refs_1_.refs_0_, bf16[2,128,128]{2,1,0:T(8,128)(2,1)S(1)} %get-tuple-element.55.refs_8_.refs_1_, ...), custom_call_target="tpu_custom_call" | custom-call | flops 10000000000 | bytes 1 | tf_op jit(solution)/shard_map/sweep_chain/pallas_call | solution.py:31
  52.8 2.0 %collective-permute-start.19 = (bf16[2,128,128]{2,1,0:T(8,128)(2,1)S(1)}, bf16[2,128,128]{2,1,0:T(8,128)(2,1)S(1)}, u32[]{:S(2)}, u32[]{:S(2)}) collective-permute-start(bf16[2,128,128]{2,1,0:T(8,128)(2,1)S(1)} %get-tuple-element.65), channel_id=1, source_target_pairs={{0,16},{8,24},{16,0},{24,8},{1,17},{9,25},{17,1},{25,9},{2,18},{10... | collective-permute-start | bytes 196616 | tf_op jit(solution)/shard_map/ppermute | solution.py:45
  54.8 2.4 %collective-permute-start.20 = (bf16[2,128,128]{2,1,0:T(8,128)(2,1)S(1)}, bf16[2,128,128]{2,1,0:T(8,128)(2,1)S(1)}, u32[]{:S(2)}, u32[]{:S(2)}) collective-permute-start(bf16[2,128,128]{2,1,0:T(8,128)(2,1)S(1)} %get-tuple-element.66), channel_id=1, source_target_pairs={{0,24},{8,16},{16,8},{24,0},{1,25},{9,17},{17,9},{25,1},{2,26},{10... | collective-permute-start | bytes 196616 | tf_op jit(solution)/shard_map/ppermute | solution.py:45
  57.2 0.6 interface_collect.2.refs_5_.refs_0_.refs_4_.refs_10_
  57.8 1.5 %collective-permute-start.27 = (bf16[2,2,256,128]{3,2,1,0:T(8,128)(2,1)S(1)}, bf16[2,2,256,128]{3,2,1,0:T(8,128)(2,1)S(1)}, u32[]{:S(2)}, u32[]{:S(2)}) collective-permute-start(bf16[2,2,256,128]{3,2,1,0:T(8,128)(2,1)S(1)} %interface_collect.2.refs_5_.refs_0_.refs_4_.refs_10_), channel_id=1, source_target_pairs={{0,4},{1,5},{2,6},{3,7},{4,0},{5,1},{6,2},{7,3},{8,12},{9,13},{10,... | collective-permute-start | bytes 786440 | tf_op jit(solution)/shard_map/ppermute | solution.py:45
  59.3 1.0 %collective-permute-start.26 = (bf16[2,2,256,128]{3,2,1,0:T(8,128)(2,1)S(1)}, bf16[2,2,256,128]{3,2,1,0:T(8,128)(2,1)S(1)}, u32[]{:S(2)}, u32[]{:S(2)}) collective-permute-start(bf16[2,2,256,128]{3,2,1,0:T(8,128)(2,1)S(1)} %interface_collect.2.refs_5_.refs_0_.refs_4_.refs_10_), channel_id=1, source_target_pairs={{0,2},{1,3},{2,0},{3,1},{4,6},{5,7},{6,4},{7,5},{8,10},{9,11},{10,... | collective-permute-start | bytes 786440 | tf_op jit(solution)/shard_map/ppermute | solution.py:45
  60.9 0.6 interface_collect.3.refs_3_.refs_0_.refs_11_.refs_4_
  61.5 1.2 %collective-permute-start.25 = (bf16[2,2,256,128]{3,2,1,0:T(8,128)(2,1)S(1)}, bf16[2,2,256,128]{3,2,1,0:T(8,128)(2,1)S(1)}, u32[]{:S(2)}, u32[]{:S(2)}) collective-permute-start(bf16[2,2,256,128]{3,2,1,0:T(8,128)(2,1)S(1)} %interface_collect.3.refs_3_.refs_0_.refs_11_.refs_4_), channel_id=1, source_target_pairs={{0,4},{1,5},{2,6},{3,7},{4,0},{5,1},{6,2},{7,3},{8,12},{9,13},{10,... | collective-permute-start | bytes 786440 | tf_op jit(solution)/shard_map/ppermute | solution.py:45
  62.7 1.3 %collective-permute-start.24 = (bf16[2,2,256,128]{3,2,1,0:T(8,128)(2,1)S(1)}, bf16[2,2,256,128]{3,2,1,0:T(8,128)(2,1)S(1)}, u32[]{:S(2)}, u32[]{:S(2)}) collective-permute-start(bf16[2,2,256,128]{3,2,1,0:T(8,128)(2,1)S(1)} %interface_collect.3.refs_3_.refs_0_.refs_11_.refs_4_), channel_id=1, source_target_pairs={{0,2},{1,3},{2,0},{3,1},{4,6},{5,7},{6,4},{7,5},{8,10},{9,11},{10,... | collective-permute-start | bytes 786440 | tf_op jit(solution)/shard_map/ppermute | solution.py:45
  64.0 1.5 %leaf_fold.1.refs_3_ = bf16[16,256,768]{2,1,0:T(8,128)(2,1)S(1)} custom-call(bf16[1,16,2,128,128]{4,3,2,1,0:T(8,128)(2,1)S(1)} %copy-done.1, bf16[1,16,2,128,128]{4,3,2,1,0:T(8,128)(2,1)S(1)} %copy-done.2, s32[1,16,128]{2,1,0:T(8,128)S(1)} %copy-done.5, bf16[2,2,256,128]{3,2,1,0:T(8,128)(2,1)S(1)} %interface_collect.3.refs_3_.refs_0_.refs_11_.refs_4_), custom_call_target="tpu_custom_call" | custom-call | flops 10000000000 | bytes 1 | tf_op jit(solution)/shard_map/leaf_fold/pallas_call | solution.py:31
  65.5 0.8 collective-permute-done.27.refs_2_.refs_7_
  66.3 1.0 %collective-permute-done.26.refs_1_.refs_6_ = bf16[2,2,256,128]{3,2,1,0:T(8,128)(2,1)S(1)} collective-permute-done((bf16[2,2,256,128]{3,2,1,0:T(8,128)(2,1)S(1)}, bf16[2,2,256,128]{3,2,1,0:T(8,128)(2,1)S(1)}, u32[]{:S(2)}, u32[]{:S(2)}) %collective-permute-start.26) | collective-permute-done | bytes 262176 | tf_op jit(solution)/shard_map/ppermute | solution.py:45
  67.3 0.6 collective-permute-start.30
  68.0 0.7 collective-permute-start.29
  69.1 1.0 %collective-permute-done.24.refs_1_.refs_6_ = bf16[2,2,256,128]{3,2,1,0:T(8,128)(2,1)S(1)} collective-permute-done((bf16[2,2,256,128]{3,2,1,0:T(8,128)(2,1)S(1)}, bf16[2,2,256,128]{3,2,1,0:T(8,128)(2,1)S(1)}, u32[]{:S(2)}, u32[]{:S(2)}) %collective-permute-start.24) | collective-permute-done | bytes 262176 | tf_op jit(solution)/shard_map/ppermute | solution.py:45
  70.2 0.8 collective-permute-start.31
  71.0 0.9 %collective-permute-start.32 = (bf16[1,2,256,128]{3,2,1,0:T(8,128)(2,1)S(1)}, bf16[1,2,256,128]{3,2,1,0:T(8,128)(2,1)S(1)}, u32[]{:S(2)}, u32[]{:S(2)}) collective-permute-start(bf16[1,2,256,128]{3,2,1,0:T(8,128)(2,1)S(1)} %get-tuple-element.74), channel_id=1, source_target_pairs={{0,2},{1,3},{2,0},{3,1},{4,6},{5,7},{6,4},{7,5},{8,10},{9,11},{10,... | collective-permute-start | bytes 393224 | tf_op jit(solution)/shard_map/ppermute | solution.py:45
  72.4 1.6 %collective-permute-done.29.refs_0_ = bf16[1,2,256,128]{3,2,1,0:T(8,128)(2,1)S(1)} collective-permute-done((bf16[1,2,256,128]{3,2,1,0:T(8,128)(2,1)S(1)}, bf16[1,2,256,128]{3,2,1,0:T(8,128)(2,1)S(1)}, u32[]{:S(2)}, u32[]{:S(2)}) %collective-permute-start.29) | collective-permute-done | bytes 131104 | tf_op jit(solution)/shard_map/ppermute | solution.py:45
  74.0 1.8 %collective-permute-done.31.refs_2_ = bf16[1,2,256,128]{3,2,1,0:T(8,128)(2,1)S(1)} collective-permute-done((bf16[1,2,256,128]{3,2,1,0:T(8,128)(2,1)S(1)}, bf16[1,2,256,128]{3,2,1,0:T(8,128)(2,1)S(1)}, u32[]{:S(2)}, u32[]{:S(2)}) %collective-permute-start.31) | collective-permute-done | bytes 131104 | tf_op jit(solution)/shard_map/ppermute | solution.py:45
  76.6 1.4 %collective-permute-done.33.refs_9_ = bf16[4,2,256,128]{3,2,1,0:T(8,128)(2,1)S(1)} collective-permute-done((bf16[4,2,256,128]{3,2,1,0:T(8,128)(2,1)S(1)}, bf16[4,2,256,128]{3,2,1,0:T(8,128)(2,1)S(1)}, u32[]{:S(2)}, u32[]{:S(2)}) %collective-permute-start.33) | collective-permute-done | bytes 524320 | tf_op jit(solution)/shard_map/ppermute | solution.py:45
  78.0 3.8 %leaf_backward.2 = (bf16[1,2,16,128,512]{4,3,2,1,0:T(8,128)(2,1)}, f32[1,2,256,512]{3,2,1,0:T(8,128)}) custom-call(s32[16]{0:T(128)S(1)} %bitcast.7, s32[2]{0:T(128)S(1)} %pad_add_fusion.refs_1_.refs_0_, bf16[1,2,16,128,512]{4,3,2,1,0:T(8,128)(2,1)S(1)} %copy-done, bf16[16,256,768]{2,1,0:T(8,128)(2,1)S(1)} %leaf_fold.1.refs_3_, ...), custom_call_target="tpu_custom_call" | custom-call | flops 10000000000 | bytes 1 | tf_op jit(solution)/shard_map/leaf_backward/pallas_call | solution.py:31
  81.8 3.7 %leaf_backward.3 = bf16[1,2,16,128,512]{4,3,2,1,0:T(8,128)(2,1)} custom-call(s32[16]{0:T(128)S(1)} %bitcast.8, s32[2]{0:T(128)S(1)} %pad_add_fusion.refs_1_.refs_0_, bf16[1,2,16,128,512]{4,3,2,1,0:T(8,128)(2,1)S(1)} %copy-done, bf16[16,256,768]{2,1,0:T(8,128)(2,1)S(1)} %leaf_fold.1.refs_3_, ...), custom_call_target="tpu_custom_call", output_to_operand_aliasing={{}: (10, {})} | custom-call | flops 10000000000 | bytes 1 | tf_op jit(solution)/shard_map/leaf_backward/pallas_call | solution.py:31
  (59 shorter events, 5.2 us)
Async XLA Ops:
  0.7 0.7 copy-start.5
  1.4 0.7 copy-start.7
  2.1 13.1 %copy-start = (bf16[1,2,16,128,512]{4,3,2,1,0:T(8,128)(2,1)S(1)}, bf16[1,2,16,128,512]{4,3,2,1,0:T(8,128)(2,1)}, u32[]{:S(2)}) copy-start(bf16[1,2,16,128,512]{4,3,2,1,0:T(8,128)(2,1)} %refs_2_.9) | copy-start | bytes 12582916
  2.1 13.1 %copy-start.1 = (bf16[1,16,2,128,128]{4,3,2,1,0:T(8,128)(2,1)S(1)}, bf16[1,16,2,128,128]{4,3,2,1,0:T(8,128)(2,1)}, u32[]{:S(2)}) copy-start(bf16[1,16,2,128,128]{4,3,2,1,0:T(8,128)(2,1)} %refs_0_.1) | copy-start | bytes 3145732
  2.1 13.1 %copy-start.2 = (bf16[1,16,2,128,128]{4,3,2,1,0:T(8,128)(2,1)S(1)}, bf16[1,16,2,128,128]{4,3,2,1,0:T(8,128)(2,1)}, u32[]{:S(2)}) copy-start(bf16[1,16,2,128,128]{4,3,2,1,0:T(8,128)(2,1)} %refs_1_.7) | copy-start | bytes 3145732
  7.7 3.0 %collective-permute-start = (bf16[4,2,2,256,128]{4,3,2,1,0:T(8,128)(2,1)}, bf16[4,2,2,256,128]{4,3,2,1,0:T(8,128)(2,1)S(1)}, u32[]{:S(2)}, u32[]{:S(2)}) collective-permute-start(bf16[4,2,2,256,128]{4,3,2,1,0:T(8,128)(2,1)} %get-tuple-element.41), channel_id=1, source_target_pairs={{0,1},{1,0},{2,3},{3,2},{4,5},{5,4},{6,7},{7,6},{8,9},{9,8},{10,11... | collective-permute-start | bytes 3145736 | tf_op jit(solution)/shard_map/ppermute | solution.py:45
  10.7 7.1 %collective-permute-start.3 = (bf16[1,2,256,128]{3,2,1,0:T(8,128)(2,1)S(1)}, bf16[1,2,256,128]{3,2,1,0:T(8,128)(2,1)S(1)}, u32[]{:S(2)}, u32[]{:S(2)}) collective-permute-start(bf16[1,2,256,128]{3,2,1,0:T(8,128)(2,1)S(1)} %get-tuple-element.45), channel_id=1, source_target_pairs={{0,4},{1,5},{2,6},{3,7},{4,0},{5,1},{6,2},{7,3},{8,12},{9,13},{10,... | collective-permute-start | bytes 393224 | tf_op jit(solution)/shard_map/ppermute | solution.py:45
  13.7 5.3 %collective-permute-start.2 = (bf16[1,2,256,128]{3,2,1,0:T(8,128)(2,1)S(1)}, bf16[1,2,256,128]{3,2,1,0:T(8,128)(2,1)S(1)}, u32[]{:S(2)}, u32[]{:S(2)}) collective-permute-start(bf16[1,2,256,128]{3,2,1,0:T(8,128)(2,1)S(1)} %get-tuple-element.42.refs_6_), channel_id=1, source_target_pairs={{0,2},{1,3},{2,0},{3,1},{4,6},{5,7},{6,4},{7,5},{8,10},{9,11},{10,... | collective-permute-start | bytes 393224 | tf_op jit(solution)/shard_map/ppermute | solution.py:45
  17.8 3.4 %collective-permute-start.1 = (bf16[4,2,2,256,128]{4,3,2,1,0:T(8,128)(2,1)S(1)}, bf16[4,2,2,256,128]{4,3,2,1,0:T(8,128)(2,1)S(1)}, u32[]{:S(2)}, u32[]{:S(2)}) collective-permute-start(bf16[4,2,2,256,128]{4,3,2,1,0:T(8,128)(2,1)S(1)} %get-tuple-element.44), channel_id=1, source_target_pairs={{0,1},{1,0},{2,3},{3,2},{4,5},{5,4},{6,7},{7,6},{8,9},{9,8},{10,11... | collective-permute-start | bytes 3145736 | tf_op jit(solution)/shard_map/ppermute | solution.py:45
  19.0 4.4 %copy-start.4 = (f32[1,2,2,128,128]{4,3,2,1,0:T(8,128)S(1)}, f32[1,2,2,128,128]{4,3,2,1,0:T(8,128)}, u32[]{:S(2)}) copy-start(f32[1,2,2,128,128]{4,3,2,1,0:T(8,128)} %refs_1_.4) | copy-start | bytes 786436
  19.0 4.4 %copy-start.6 = (f32[1,256]{1,0:T(1,128)S(1)}, f32[1,256]{1,0:T(1,128)}, u32[]{:S(2)}) copy-start(f32[1,256]{1,0:T(1,128)} %param.15) | copy-start | bytes 3076
  19.1 14.1 %collective-permute-start.10 = (bf16[2,2,256,128]{3,2,1,0:T(8,128)(2,1)S(1)}, bf16[2,2,256,128]{3,2,1,0:T(8,128)(2,1)S(1)}, u32[]{:S(2)}, u32[]{:S(2)}) collective-permute-start(bf16[2,2,256,128]{3,2,1,0:T(8,128)(2,1)S(1)} %get-tuple-element.53), channel_id=1, source_target_pairs={{0,4},{1,5},{2,6},{3,7},{4,0},{5,1},{6,2},{7,3},{8,12},{9,13},{10,... | collective-permute-start | bytes 786440 | tf_op jit(solution)/shard_map/ppermute | solution.py:45
  19.5 13.7 %collective-permute-start.9 = (bf16[2,2,256,128]{3,2,1,0:T(8,128)(2,1)S(1)}, bf16[2,2,256,128]{3,2,1,0:T(8,128)(2,1)S(1)}, u32[]{:S(2)}, u32[]{:S(2)}) collective-permute-start(bf16[2,2,256,128]{3,2,1,0:T(8,128)(2,1)S(1)} %get-tuple-element.46.refs_2_), channel_id=1, source_target_pairs={{0,2},{1,3},{2,0},{3,1},{4,6},{5,7},{6,4},{7,5},{8,10},{9,11},{10,... | collective-permute-start | bytes 786440 | tf_op jit(solution)/shard_map/ppermute | solution.py:45
  21.3 9.7 %collective-permute-start.5 = (bf16[1,2,256,128]{3,2,1,0:T(8,128)(2,1)S(1)}, bf16[1,2,256,128]{3,2,1,0:T(8,128)(2,1)S(1)}, u32[]{:S(2)}, u32[]{:S(2)}) collective-permute-start(bf16[1,2,256,128]{3,2,1,0:T(8,128)(2,1)S(1)} %get-tuple-element.48), channel_id=1, source_target_pairs={{0,4},{1,5},{2,6},{3,7},{4,0},{5,1},{6,2},{7,3},{8,12},{9,13},{10,... | collective-permute-start | bytes 393224 | tf_op jit(solution)/shard_map/ppermute | solution.py:45
  22.8 8.2 %collective-permute-start.4 = (bf16[1,2,256,128]{3,2,1,0:T(8,128)(2,1)S(1)}, bf16[1,2,256,128]{3,2,1,0:T(8,128)(2,1)S(1)}, u32[]{:S(2)}, u32[]{:S(2)}) collective-permute-start(bf16[1,2,256,128]{3,2,1,0:T(8,128)(2,1)S(1)} %get-tuple-element.47.refs_3_.refs_2_), channel_id=1, source_target_pairs={{0,2},{1,3},{2,0},{3,1},{4,6},{5,7},{6,4},{7,5},{8,10},{9,11},{10,... | collective-permute-start | bytes 393224 | tf_op jit(solution)/shard_map/ppermute | solution.py:45
  23.4 9.9 %copy-start.3 = (bf16[1,2,256,512]{3,2,1,0:T(8,128)(2,1)S(1)}, bf16[1,2,256,512]{3,2,1,0:T(8,128)(2,1)}, u32[]{:S(2)}) copy-start(bf16[1,2,256,512]{3,2,1,0:T(8,128)(2,1)} %refs_1_.6) | copy-start | bytes 1572868
  24.0 4.4 %collective-permute-start.6 = (bf16[272,128]{1,0:T(8,128)(2,1)S(1)}, bf16[272,128]{1,0:T(8,128)(2,1)S(1)}, u32[]{:S(2)}, u32[]{:S(2)}) collective-permute-start(bf16[272,128]{1,0:T(8,128)(2,1)S(1)} %get-tuple-element.50), channel_id=1, source_target_pairs={{0,8},{8,0},{16,24},{24,16},{1,9},{9,1},{17,25},{25,17},{2,10},{10... | collective-permute-start | bytes 208904 | tf_op jit(solution)/shard_map/ppermute | solution.py:45
  28.3 17.0 %collective-permute-start.14 = (bf16[544,128]{1,0:T(8,128)(2,1)S(1)}, bf16[544,128]{1,0:T(8,128)(2,1)S(1)}, u32[]{:S(2)}, u32[]{:S(2)}) collective-permute-start(bf16[544,128]{1,0:T(8,128)(2,1)S(1)} %solve_join.1.refs_4_), channel_id=1, source_target_pairs={{0,16},{8,24},{16,0},{24,8},{1,17},{9,25},{17,1},{25,9},{2,18},{10... | collective-permute-start | bytes 417800 | tf_op jit(solution)/shard_map/ppermute | solution.py:45
  31.2 6.5 %collective-permute-start.8 = (bf16[2,2,256,128]{3,2,1,0:T(8,128)(2,1)S(1)}, bf16[2,2,256,128]{3,2,1,0:T(8,128)(2,1)S(1)}, u32[]{:S(2)}, u32[]{:S(2)}) collective-permute-start(bf16[2,2,256,128]{3,2,1,0:T(8,128)(2,1)S(1)} %get-tuple-element.52), channel_id=1, source_target_pairs={{0,4},{1,5},{2,6},{3,7},{4,0},{5,1},{6,2},{7,3},{8,12},{9,13},{10,... | collective-permute-start | bytes 786440 | tf_op jit(solution)/shard_map/ppermute | solution.py:45
  31.7 8.4 %collective-permute-start.7 = (bf16[2,2,256,128]{3,2,1,0:T(8,128)(2,1)S(1)}, bf16[2,2,256,128]{3,2,1,0:T(8,128)(2,1)S(1)}, u32[]{:S(2)}, u32[]{:S(2)}) collective-permute-start(bf16[2,2,256,128]{3,2,1,0:T(8,128)(2,1)S(1)} %get-tuple-element.51.refs_6_), channel_id=1, source_target_pairs={{0,2},{1,3},{2,0},{3,1},{4,6},{5,7},{6,4},{7,5},{8,10},{9,11},{10,... | collective-permute-start | bytes 786440 | tf_op jit(solution)/shard_map/ppermute | solution.py:45
  34.0 7.0 %collective-permute-start.15 = (bf16[2,128,128]{2,1,0:T(8,128)(2,1)S(1)}, bf16[2,128,128]{2,1,0:T(8,128)(2,1)S(1)}, u32[]{:S(2)}, u32[]{:S(2)}) collective-permute-start(bf16[2,128,128]{2,1,0:T(8,128)(2,1)S(1)} %get-tuple-element.59), channel_id=1, source_target_pairs={{0,8},{8,0},{16,24},{24,16},{1,9},{9,1},{17,25},{25,17},{2,10},{10... | collective-permute-start | bytes 196616 | tf_op jit(solution)/shard_map/ppermute | solution.py:45
  35.6 7.3 %collective-permute-start.16 = (bf16[2,128,128]{2,1,0:T(8,128)(2,1)S(1)}, bf16[2,128,128]{2,1,0:T(8,128)(2,1)S(1)}, u32[]{:S(2)}, u32[]{:S(2)}) collective-permute-start(bf16[2,128,128]{2,1,0:T(8,128)(2,1)S(1)} %get-tuple-element.60), channel_id=1, source_target_pairs={{0,16},{8,24},{16,0},{24,8},{1,17},{9,25},{17,1},{25,9},{2,18},{10... | collective-permute-start | bytes 196616 | tf_op jit(solution)/shard_map/ppermute | solution.py:45
  37.6 7.7 %collective-permute-start.17 = (bf16[2,128,128]{2,1,0:T(8,128)(2,1)S(1)}, bf16[2,128,128]{2,1,0:T(8,128)(2,1)S(1)}, u32[]{:S(2)}, u32[]{:S(2)}) collective-permute-start(bf16[2,128,128]{2,1,0:T(8,128)(2,1)S(1)} %get-tuple-element.61), channel_id=1, source_target_pairs={{0,24},{8,16},{16,8},{24,0},{1,25},{9,17},{17,9},{25,1},{2,26},{10... | collective-permute-start | bytes 196616 | tf_op jit(solution)/shard_map/ppermute | solution.py:45
  40.9 8.0 %collective-permute-start.11 = (bf16[2,128,128]{2,1,0:T(8,128)(2,1)S(1)}, bf16[2,128,128]{2,1,0:T(8,128)(2,1)S(1)}, u32[]{:S(2)}, u32[]{:S(2)}) collective-permute-start(bf16[2,128,128]{2,1,0:T(8,128)(2,1)S(1)} %get-tuple-element.56), channel_id=1, source_target_pairs={{0,8},{8,0},{16,24},{24,16},{1,9},{9,1},{17,25},{25,17},{2,10},{10... | collective-permute-start | bytes 196616 | tf_op jit(solution)/shard_map/ppermute | solution.py:45
  41.0 10.3 %collective-permute-start.12 = (bf16[2,128,128]{2,1,0:T(8,128)(2,1)S(1)}, bf16[2,128,128]{2,1,0:T(8,128)(2,1)S(1)}, u32[]{:S(2)}, u32[]{:S(2)}) collective-permute-start(bf16[2,128,128]{2,1,0:T(8,128)(2,1)S(1)} %get-tuple-element.57), channel_id=1, source_target_pairs={{0,16},{8,24},{16,0},{24,8},{1,17},{9,25},{17,1},{25,9},{2,18},{10... | collective-permute-start | bytes 196616 | tf_op jit(solution)/shard_map/ppermute | solution.py:45
  42.9 8.4 %collective-permute-start.13 = (bf16[2,128,128]{2,1,0:T(8,128)(2,1)S(1)}, bf16[2,128,128]{2,1,0:T(8,128)(2,1)S(1)}, u32[]{:S(2)}, u32[]{:S(2)}) collective-permute-start(bf16[2,128,128]{2,1,0:T(8,128)(2,1)S(1)} %get-tuple-element.58), channel_id=1, source_target_pairs={{0,24},{8,16},{16,8},{24,0},{1,25},{9,17},{17,9},{25,1},{2,26},{10... | collective-permute-start | bytes 196616 | tf_op jit(solution)/shard_map/ppermute | solution.py:45
  46.8 8.0 %collective-permute-start.21 = (bf16[2,128,128]{2,1,0:T(8,128)(2,1)S(1)}, bf16[2,128,128]{2,1,0:T(8,128)(2,1)S(1)}, u32[]{:S(2)}, u32[]{:S(2)}) collective-permute-start(bf16[2,128,128]{2,1,0:T(8,128)(2,1)S(1)} %get-tuple-element.67), channel_id=1, source_target_pairs={{0,8},{8,0},{16,24},{24,16},{1,9},{9,1},{17,25},{25,17},{2,10},{10... | collective-permute-start | bytes 196616 | tf_op jit(solution)/shard_map/ppermute | solution.py:45
  47.7 9.5 %collective-permute-start.22 = (bf16[2,128,128]{2,1,0:T(8,128)(2,1)S(1)}, bf16[2,128,128]{2,1,0:T(8,128)(2,1)S(1)}, u32[]{:S(2)}, u32[]{:S(2)}) collective-permute-start(bf16[2,128,128]{2,1,0:T(8,128)(2,1)S(1)} %get-tuple-element.68), channel_id=1, source_target_pairs={{0,16},{8,24},{16,0},{24,8},{1,17},{9,25},{17,1},{25,9},{2,18},{10... | collective-permute-start | bytes 196616 | tf_op jit(solution)/shard_map/ppermute | solution.py:45
  48.9 8.4 %collective-permute-start.23 = (bf16[2,128,128]{2,1,0:T(8,128)(2,1)S(1)}, bf16[2,128,128]{2,1,0:T(8,128)(2,1)S(1)}, u32[]{:S(2)}, u32[]{:S(2)}) collective-permute-start(bf16[2,128,128]{2,1,0:T(8,128)(2,1)S(1)} %get-tuple-element.69), channel_id=1, source_target_pairs={{0,24},{8,16},{16,8},{24,0},{1,25},{9,17},{17,9},{25,1},{2,26},{10... | collective-permute-start | bytes 196616 | tf_op jit(solution)/shard_map/ppermute | solution.py:45
  52.8 7.6 %collective-permute-start.18 = (bf16[2,128,128]{2,1,0:T(8,128)(2,1)S(1)}, bf16[2,128,128]{2,1,0:T(8,128)(2,1)S(1)}, u32[]{:S(2)}, u32[]{:S(2)}) collective-permute-start(bf16[2,128,128]{2,1,0:T(8,128)(2,1)S(1)} %get-tuple-element.64), channel_id=1, source_target_pairs={{0,8},{8,0},{16,24},{24,16},{1,9},{9,1},{17,25},{25,17},{2,10},{10... | collective-permute-start | bytes 196616 | tf_op jit(solution)/shard_map/ppermute | solution.py:45
  52.8 7.5 %collective-permute-start.19 = (bf16[2,128,128]{2,1,0:T(8,128)(2,1)S(1)}, bf16[2,128,128]{2,1,0:T(8,128)(2,1)S(1)}, u32[]{:S(2)}, u32[]{:S(2)}) collective-permute-start(bf16[2,128,128]{2,1,0:T(8,128)(2,1)S(1)} %get-tuple-element.65), channel_id=1, source_target_pairs={{0,16},{8,24},{16,0},{24,8},{1,17},{9,25},{17,1},{25,9},{2,18},{10... | collective-permute-start | bytes 196616 | tf_op jit(solution)/shard_map/ppermute | solution.py:45
  54.8 6.1 %collective-permute-start.20 = (bf16[2,128,128]{2,1,0:T(8,128)(2,1)S(1)}, bf16[2,128,128]{2,1,0:T(8,128)(2,1)S(1)}, u32[]{:S(2)}, u32[]{:S(2)}) collective-permute-start(bf16[2,128,128]{2,1,0:T(8,128)(2,1)S(1)} %get-tuple-element.66), channel_id=1, source_target_pairs={{0,24},{8,16},{16,8},{24,0},{1,25},{9,17},{17,9},{25,1},{2,26},{10... | collective-permute-start | bytes 196616 | tf_op jit(solution)/shard_map/ppermute | solution.py:45
  57.8 8.5 %collective-permute-start.27 = (bf16[2,2,256,128]{3,2,1,0:T(8,128)(2,1)S(1)}, bf16[2,2,256,128]{3,2,1,0:T(8,128)(2,1)S(1)}, u32[]{:S(2)}, u32[]{:S(2)}) collective-permute-start(bf16[2,2,256,128]{3,2,1,0:T(8,128)(2,1)S(1)} %interface_collect.2.refs_5_.refs_0_.refs_4_.refs_10_), channel_id=1, source_target_pairs={{0,4},{1,5},{2,6},{3,7},{4,0},{5,1},{6,2},{7,3},{8,12},{9,13},{10,... | collective-permute-start | bytes 786440 | tf_op jit(solution)/shard_map/ppermute | solution.py:45
  59.3 7.9 %collective-permute-start.26 = (bf16[2,2,256,128]{3,2,1,0:T(8,128)(2,1)S(1)}, bf16[2,2,256,128]{3,2,1,0:T(8,128)(2,1)S(1)}, u32[]{:S(2)}, u32[]{:S(2)}) collective-permute-start(bf16[2,2,256,128]{3,2,1,0:T(8,128)(2,1)S(1)} %interface_collect.2.refs_5_.refs_0_.refs_4_.refs_10_), channel_id=1, source_target_pairs={{0,2},{1,3},{2,0},{3,1},{4,6},{5,7},{6,4},{7,5},{8,10},{9,11},{10,... | collective-permute-start | bytes 786440 | tf_op jit(solution)/shard_map/ppermute | solution.py:45
  61.5 7.6 %collective-permute-start.25 = (bf16[2,2,256,128]{3,2,1,0:T(8,128)(2,1)S(1)}, bf16[2,2,256,128]{3,2,1,0:T(8,128)(2,1)S(1)}, u32[]{:S(2)}, u32[]{:S(2)}) collective-permute-start(bf16[2,2,256,128]{3,2,1,0:T(8,128)(2,1)S(1)} %interface_collect.3.refs_3_.refs_0_.refs_11_.refs_4_), channel_id=1, source_target_pairs={{0,4},{1,5},{2,6},{3,7},{4,0},{5,1},{6,2},{7,3},{8,12},{9,13},{10,... | collective-permute-start | bytes 786440 | tf_op jit(solution)/shard_map/ppermute | solution.py:45
  62.7 7.4 %collective-permute-start.24 = (bf16[2,2,256,128]{3,2,1,0:T(8,128)(2,1)S(1)}, bf16[2,2,256,128]{3,2,1,0:T(8,128)(2,1)S(1)}, u32[]{:S(2)}, u32[]{:S(2)}) collective-permute-start(bf16[2,2,256,128]{3,2,1,0:T(8,128)(2,1)S(1)} %interface_collect.3.refs_3_.refs_0_.refs_11_.refs_4_), channel_id=1, source_target_pairs={{0,2},{1,3},{2,0},{3,1},{4,6},{5,7},{6,4},{7,5},{8,10},{9,11},{10,... | collective-permute-start | bytes 786440 | tf_op jit(solution)/shard_map/ppermute | solution.py:45
  67.3 5.0 %collective-permute-start.30 = (bf16[1,2,256,128]{3,2,1,0:T(8,128)(2,1)S(1)}, bf16[1,2,256,128]{3,2,1,0:T(8,128)(2,1)S(1)}, u32[]{:S(2)}, u32[]{:S(2)}) collective-permute-start(bf16[1,2,256,128]{3,2,1,0:T(8,128)(2,1)S(1)} %get-tuple-element.72), channel_id=1, source_target_pairs={{0,2},{1,3},{2,0},{3,1},{4,6},{5,7},{6,4},{7,5},{8,10},{9,11},{10,... | collective-permute-start | bytes 393224 | tf_op jit(solution)/shard_map/ppermute | solution.py:45
  68.0 6.0 %collective-permute-start.29 = (bf16[1,2,256,128]{3,2,1,0:T(8,128)(2,1)S(1)}, bf16[1,2,256,128]{3,2,1,0:T(8,128)(2,1)S(1)}, u32[]{:S(2)}, u32[]{:S(2)}) collective-permute-start(bf16[1,2,256,128]{3,2,1,0:T(8,128)(2,1)S(1)} %get-tuple-element.70.refs_3_), channel_id=1, source_target_pairs={{0,4},{1,5},{2,6},{3,7},{4,0},{5,1},{6,2},{7,3},{8,12},{9,13},{10,... | collective-permute-start | bytes 393224 | tf_op jit(solution)/shard_map/ppermute | solution.py:45
  68.7 9.2 %collective-permute-start.34 = (bf16[3,2,2,256,128]{4,3,2,1,0:T(8,128)(2,1)S(1)}, bf16[3,2,2,256,128]{4,3,2,1,0:T(8,128)(2,1)S(1)}, u32[]{:S(2)}, u32[]{:S(2)}) collective-permute-start(bf16[3,2,2,256,128]{4,3,2,1,0:T(8,128)(2,1)S(1)} %get-tuple-element.75), channel_id=1, source_target_pairs={{0,1},{1,0},{2,3},{3,2},{4,5},{5,4},{6,7},{7,6},{8,9},{9,8},{10,11... | collective-permute-start | bytes 2359304 | tf_op jit(solution)/shard_map/ppermute | solution.py:45
  70.2 5.6 %collective-permute-start.31 = (bf16[1,2,256,128]{3,2,1,0:T(8,128)(2,1)S(1)}, bf16[1,2,256,128]{3,2,1,0:T(8,128)(2,1)S(1)}, u32[]{:S(2)}, u32[]{:S(2)}) collective-permute-start(bf16[1,2,256,128]{3,2,1,0:T(8,128)(2,1)S(1)} %get-tuple-element.73), channel_id=1, source_target_pairs={{0,4},{1,5},{2,6},{3,7},{4,0},{5,1},{6,2},{7,3},{8,12},{9,13},{10,... | collective-permute-start | bytes 393224 | tf_op jit(solution)/shard_map/ppermute | solution.py:45
  71.0 5.0 %collective-permute-start.32 = (bf16[1,2,256,128]{3,2,1,0:T(8,128)(2,1)S(1)}, bf16[1,2,256,128]{3,2,1,0:T(8,128)(2,1)S(1)}, u32[]{:S(2)}, u32[]{:S(2)}) collective-permute-start(bf16[1,2,256,128]{3,2,1,0:T(8,128)(2,1)S(1)} %get-tuple-element.74), channel_id=1, source_target_pairs={{0,2},{1,3},{2,0},{3,1},{4,6},{5,7},{6,4},{7,5},{8,10},{9,11},{10,... | collective-permute-start | bytes 393224 | tf_op jit(solution)/shard_map/ppermute | solution.py:45
  76.0 2.0 %collective-permute-start.33 = (bf16[4,2,256,128]{3,2,1,0:T(8,128)(2,1)S(1)}, bf16[4,2,256,128]{3,2,1,0:T(8,128)(2,1)S(1)}, u32[]{:S(2)}, u32[]{:S(2)}) collective-permute-start(bf16[4,2,256,128]{3,2,1,0:T(8,128)(2,1)S(1)} %interface_join.1.refs_8_), channel_id=1, source_target_pairs={{0,1},{1,0},{2,3},{3,2},{4,5},{5,4},{6,7},{7,6},{8,9},{9,8},{10,11... | collective-permute-start | bytes 1572872 | tf_op jit(solution)/shard_map/ppermute | solution.py:45
  76.1 5.7 %collective-permute-start.28 = (bf16[3,2,2,256,128]{4,3,2,1,0:T(8,128)(2,1)S(1)}, bf16[3,2,2,256,128]{4,3,2,1,0:T(8,128)(2,1)S(1)}, u32[]{:S(2)}, u32[]{:S(2)}) collective-permute-start(bf16[3,2,2,256,128]{4,3,2,1,0:T(8,128)(2,1)S(1)} %get-tuple-element.71), channel_id=1, source_target_pairs={{0,1},{1,0},{2,3},{3,2},{4,5},{5,4},{6,7},{7,6},{8,9},{9,8},{10,11... | collective-permute-start | bytes 2359304 | tf_op jit(solution)/shard_map/ppermute | solution.py:45

commit v9 on v8

--- a/solution.py
+++ b/solution.py
@@ -372,8 +372,7 @@
     )
 
 
-def backward_kernel(h, named, count, cap, owns, aliased, owners, place, rhs, mats, *refs):
-    fronts = len(named)
+def backward_kernel(jobs, count, cap, fronts, owns, aliased, owners, place, rhs, mats, *refs):
     fields, refs = refs[:count], refs[count:]
     roots, refs = refs[:owns], refs[owns + aliased :]
     out, refs = refs[0], refs[1:]
@@ -384,15 +383,16 @@
     full = fronts * cap == leaves
     copies = []
     if owns:
-        root, wider, root_sem = refs[:3]
+        root, token, wider, root_sem = refs[:4]
+        token[...] = jnp.zeros(token.shape, F32)
         parts, _, _, part = roots[0].shape
         for at, ref in enumerate(roots):
             for q in range(parts):
                 left = (at * parts + q) * part
                 for plane in range(2):
                     wider[plane, :, left : left + part] = ref[q, plane].astype(F32)
-        copies.append(pltpu.make_async_copy(wider, root.at[0], root_sem))
-        copies[0].start()
+        copies.append((True, pltpu.make_async_copy(wider, root.at[0], root_sem)))
+        copies[0][1].start()
     for slot in range(fronts * cap):
         slots[slot] = -1
     for leaf in range(leaves):
@@ -402,71 +402,74 @@
             spot = jnp.where(slots[first + rank] >= 0, first + rank + 1, spot)
         slots[spot] = leaf
 
-    def copy_of(leaf):
-        return pltpu.make_async_copy(held.at[leaf], out.at[0, :, leaf, :, pl.ds(h * cols, cols)], sems.at[leaf])
-
-    def solve(name, field):
+    def solve(at, h, name, field):
         here = pl.ds(h * cols, cols)
         vec = jnp.concatenate([rhs[0, 0, name, :, here], rhs[0, 1, name, :, here]], axis=0)
         result = dot(mats[name, :, :wide], vec) + dot(mats[name, :, wide:], field)
-        held[name, 0] = result[:blk].astype(BF)
-        held[name, 1] = result[blk:].astype(BF)
+        held[at, 0] = result[:blk].astype(BF)
+        held[at, 1] = result[blk:].astype(BF)
 
     batch = 4
-    for low in range(0, fronts, batch):
-        names = []
-        for dist in range(low, min(fronts, low + batch)):
-            mine = [fields[at] if lead is None else fields[at].at[lead] for at, lead in named[dist]]
+    for low in range(0, len(jobs), batch):
+        ready = len(copies)
+        for job in range(low, min(len(jobs), low + batch)):
+            h, dist, sources = jobs[job]
+            mine = [fields[at] if lead is None else fields[at].at[lead] for at, lead in sources]
             columns = [ref[q].reshape(tall, ref.shape[3]) for ref in mine for q in range(ref.shape[0])]
             field = jnp.concatenate(columns, axis=1)
             for rank in range(cap):
-                names.append(slots[dist * cap + rank])
+                at, name = job * cap + rank, slots[dist * cap + rank]
+                copy = pltpu.make_async_copy(
+                    held.at[at], out.at[0, :, jnp.maximum(name, 0), :, pl.ds(h * cols, cols)], sems.at[at]
+                )
+                copies.append((name >= 0, copy))
                 if full:
-                    solve(names[-1], field)
+                    solve(at, h, name, field)
                 else:
-                    pl.when(names[-1] >= 0)(functools.partial(solve, names[-1], field))
-        for name in names:
+                    pl.when(name >= 0)(functools.partial(solve, at, h, name, field))
+        for there, copy in copies[ready:]:
             if full:
-                copy_of(name).start()
+                copy.start()
             else:
-                pl.when(name >= 0)(copy_of(name).start)
-
-    for leaf in range(leaves):
-        copies.append(copy_of(leaf))
-    for copy in copies:
-        copy.wait()
-
-
-def backward(h, owners, place, leaf_rhs, mats, fields, roots, before, width, after):
-    leaves, wide, _ = mats.shape
-    blk, fronts, cols = wide // 2, len(fields), width // HALVES
-    cap = -(-leaves // fronts)
+                pl.when(there)(copy.start)
+
+    for at, (there, copy) in enumerate(copies):
+        if full or (owns and at == 0):
+            copy.wait()
+        else:
+            pl.when(there)(copy.wait)
+
+
+def backward(name, owners, place, leaf_rhs, mats, jobs, fronts, roots, before, after):
+    _, _, leaves, blk, width = leaf_rhs.shape
+    cap, cols = -(-leaves // fronts), width // HALVES
     flat, named = [], []
-    for field in fields:
-        named.append([])
+    for h, dist, field in jobs:
+        sources = []
         for value in field:
             value, lead = value if isinstance(value, tuple) else (value, None)
             known = [at for at, other in enumerate(flat) if other is value]
             if not known:
                 flat.append(value)
-            named[-1].append((known[0] if known else len(flat) - 1, lead))
+            sources.append((known[0] if known else len(flat) - 1, lead))
+        named.append((h, dist, sources))
     count = len(flat)
     flat = flat + roots
     aliased = [] if before is None else [before]
     outs, specs, scratch = [shape_of((1, 2, leaves, blk, width))], [HBM], []
     if roots:
         rows = roots[0].shape[2]
-        outs, specs = outs + [shape_of((1, 2, rows, width), F32)], [HBM, HBM]
+        outs, specs = outs + [shape_of((1, 2, rows, width), F32), shape_of((8, 128), F32)], [HBM, HBM, VMEM]
         scratch = [pltpu.VMEM((2, rows, width), F32), pltpu.SemaphoreType.DMA]
     return call(
-        functools.partial(backward_kernel, h, named, count, cap, len(roots), len(aliased)), "leaf_backward",
+        functools.partial(backward_kernel, named, count, cap, fronts, len(roots), len(aliased)), name,
         [owners, place, leaf_rhs, mats, *flat, *aliased], [SMEM, SMEM] + [VMEM] * (2 + len(flat)) + [HBM] * len(aliased),
         outs, specs, after,
         scratch
         + [
-            pltpu.VMEM((leaves, 2, blk, cols), BF),
+            pltpu.VMEM((len(jobs) * cap, 2, blk, cols), BF),
             pltpu.SMEM((fronts * cap,), jnp.int32),
-            pltpu.SemaphoreType.DMA((leaves,)),
+            pltpu.SemaphoreType.DMA((len(jobs) * cap,)),
         ],
         {4 + len(flat): 0} if aliased else None,
     )
@@ -514,18 +517,22 @@
         to_y, to_x, held = relay(h, own, *got, after)
         return to_y, [crossed(to_y, "front", 4), crossed(to_x, "front", 2), crossed(held, "front", 1)]
 
-    def share_third(owns, gots, mores):
-        if not square:
-            whole = [[own] + got for own, got in zip(owns, gots)]
-            return [[[value] for field in mine for value in (field, crossed(field, "front", 1))] for mine in whole]
-        far = join([value for more in mores for value in more[:2]], (), "interface_join")
+    def near_jobs(h, own, got, more):
+        mine = [own] + got
+        if square:
+            fields = [field for at, value in enumerate(mine) for field in ([value], [(more[2], at)])]
+        else:
+            fields = [[field] for value in mine for field in (value, crossed(value, "front", 1))]
+        return [(h, dist, field) for dist, field in enumerate(fields)]
+
+    def far_jobs(mores, after):
+        far = join([value for more in mores for value in more[:2]], after, "interface_join")
         there = crossed(far, "front", 1)
-        fields = []
-        for h, (own, got, more) in enumerate(zip(owns, gots, mores)):
+        jobs = []
+        for h in range(len(mores)):
             span = pl.ds(h * parts, parts)
-            near = [field for at, value in enumerate([own] + got) for field in ([value], [(more[2], at)])]
-            fields.append(near + [[(far, span)], [(there, span)]])
-        return fields
+            jobs += [(h, fronts - 2, [(far, span)]), (h, fronts - 1, [(there, span)])]
+        return jobs
 
     keep0, near0 = start_forward(0, ())
     token, got0 = send_first(keep0, near0, ())
@@ -549,12 +556,16 @@
     got1 = share_first(own1)
     folded = fold(leaf_inv, leaf_off, ancestors, rows, [own1])
     token, more0 = share_second(0, own0, got0, [folded])
-    _, more1 = share_second(1, own1, got1, [token])
-    fields0, fields1 = share_third((own0, own1), (got0, got1), (more0, more1))
-    leaf_sol, root_sol = backward(
-        0, owners, place, leaf_rhs, folded, fields0, [own0, own1], None, width, ()
-    )
-    (leaf_sol,) = backward(1, owners, place, leaf_rhs, folded, fields1, [], leaf_sol, width, ())
+    token, more1 = share_second(1, own1, got1, [token])
+    leaf_sol, root_sol, token = backward(
+        "leaf_backward", owners, place, leaf_rhs, folded, near_jobs(0, own0, got0, more0), fronts, [own0, own1], None, [token]
+    )
+    (leaf_sol,) = backward(
+        "leaf_backward", owners, place, leaf_rhs, folded, near_jobs(1, own1, got1, more1), fronts, [], leaf_sol, ()
+    )
+    if square:
+        jobs = far_jobs((more0, more1), [token])
+        (leaf_sol,) = backward("leaf_backward", owners, place, leaf_rhs, folded, jobs, fronts, [], leaf_sol, ())
     return leaf_sol, root_sol
 
 

time: 85.7 us -> 82.6 us (0.964)
  waiting for transfers between devices: 15.6 us -> 10.6 us
  Pallas kernels: 23.9 us -> 25.3 us
    ppermute x35, waiting for transfers between devices: 15.6 us -> 10.6 us  [crossed(): lax.ppermute(x, axis, [(i, i ^ mask) for i in range(lax.axis_size(axis))])]
    pallas_call x20 -> x21, Pallas kernels: 23.9 us -> 25.3 us  [call(): pl.pallas_call(wrapped, in_specs=list(in_specs) + [ANY] * extra, out_spec...]
  transfers between devices with their start and end apart: 35 -> 35, of which waited for: 13 -> 9; matrix products, arithmetic and copies ran while one was open for 0% -> 0% of each run, Pallas kernels for 17% -> 21%
where the time goes in v9:
time: 82.6 us; the launch traced here: 82.4 us
  starting transfers between devices  44.1 us (53%)
  Pallas kernels  25.3 us (31%)
  waiting for transfers between devices  10.6 us (13%)
  local copies, waits for them, and re-layouts  1.37 us (2%)
  between operations  0.9 us (1%)
    ppermute x35, starting transfers between devices, crossed(): lax.ppermute(x, axis, [(i, i ^ mask) for i in range(lax.axis_size(axis))])  44.1 us
    pallas_call x21, Pallas kernels, call(): pl.pallas_call(wrapped, in_specs=list(in_specs) + [ANY] * extra, out_spec...  25.3 us
    ppermute x35, waiting for transfers between devices, crossed(): lax.ppermute(x, axis, [(i, i ^ mask) for i in range(lax.axis_size(axis))])  10.6 us
  transfers between devices with their start and end apart: 35, of which 9 were waited for; matrix products, arithmetic and copies ran while one was open for 0% of the time, Pallas kernels for 21%

profile of v9, /device:TPU:0, one launch (start us, length us, event | category | flops | bytes accessed | tf_op | source)
XLA Modules:
  0.0 82.4 jit_solution(11427456078546179891)
XLA Ops:
  0.7 0.7 copy-done.5
  1.4 0.7 copy-done.7
  2.1 5.6 %leaf_forward.2 = (bf16[4,2,2,256,128]{4,3,2,1,0:T(8,128)(2,1)S(1)}, bf16[4,2,2,256,128]{4,3,2,1,0:T(8,128)(2,1)}) custom-call(s32[16]{0:T(128)S(1)} %bitcast.5, s32[2]{0:T(128)S(1)} %pad_add_fusion.refs_1_.refs_0_, bf16[1,2,16,128,512]{4,3,2,1,0:T(8,128)(2,1)} %refs_2_.11, bf16[1,16,2,128,128]{4,3,2,1,0:T(8,128)(2,1)} %refs_0_.1, ...), custom_call_target="tpu_custom_call" | custom-call | flops 10000000000 | bytes 1 | tf_op jit(solution)/shard_map/leaf_forward/pallas_call | solution.py:31
  8.2 2.5 %collective-permute-done.refs_1_.refs_3_ = bf16[4,2,2,256,128]{4,3,2,1,0:T(8,128)(2,1)S(1)} collective-permute-done((bf16[4,2,2,256,128]{4,3,2,1,0:T(8,128)(2,1)}, bf16[4,2,2,256,128]{4,3,2,1,0:T(8,128)(2,1)S(1)}, u32[]{:S(2)}, u32[]{:S(2)}) %collective-permute-start) | collective-permute-done | bytes 1048608 | tf_op jit(solution)/shard_map/ppermute | solution.py:45
  10.7 2.9 %collective-permute-start.2 = (bf16[1,2,256,128]{3,2,1,0:T(8,128)(2,1)S(1)}, bf16[1,2,256,128]{3,2,1,0:T(8,128)(2,1)S(1)}, u32[]{:S(2)}, u32[]{:S(2)}) collective-permute-start(bf16[1,2,256,128]{3,2,1,0:T(8,128)(2,1)S(1)} %get-tuple-element.43.refs_6_), channel_id=1, source_target_pairs={{0,2},{1,3},{2,0},{3,1},{4,6},{5,7},{6,4},{7,5},{8,10},{9,11},{10,... | collective-permute-start | bytes 393224 | tf_op jit(solution)/shard_map/ppermute | solution.py:45
  13.7 1.5 %collective-permute-start.3 = (bf16[1,2,256,128]{3,2,1,0:T(8,128)(2,1)S(1)}, bf16[1,2,256,128]{3,2,1,0:T(8,128)(2,1)S(1)}, u32[]{:S(2)}, u32[]{:S(2)}) collective-permute-start(bf16[1,2,256,128]{3,2,1,0:T(8,128)(2,1)S(1)} %get-tuple-element.46), channel_id=1, source_target_pairs={{0,4},{1,5},{2,6},{3,7},{4,0},{5,1},{6,2},{7,3},{8,12},{9,13},{10,... | collective-permute-start | bytes 393224 | tf_op jit(solution)/shard_map/ppermute | solution.py:45
  15.2 2.6 %leaf_forward.3 = (bf16[4,2,2,256,128]{4,3,2,1,0:T(8,128)(2,1)S(1)}, bf16[4,2,2,256,128]{4,3,2,1,0:T(8,128)(2,1)S(1)}) custom-call(s32[16]{0:T(128)S(1)} %bitcast.6, s32[2]{0:T(128)S(1)} %pad_add_fusion.refs_1_.refs_0_, bf16[1,2,16,128,512]{4,3,2,1,0:T(8,128)(2,1)S(1)} %copy-done, bf16[1,16,2,128,128]{4,3,2,1,0:T(8,128)(2,1)S(1)} %copy-done.1, ...), custom_call_target="tpu_custom_call" | custom-call | flops 10000000000 | bytes 1 | tf_op jit(solution)/shard_map/leaf_forward/pallas_call | solution.py:31
  17.9 1.1 %collective-permute-done.3.refs_3_ = bf16[1,2,256,128]{3,2,1,0:T(8,128)(2,1)S(1)} collective-permute-done((bf16[1,2,256,128]{3,2,1,0:T(8,128)(2,1)S(1)}, bf16[1,2,256,128]{3,2,1,0:T(8,128)(2,1)S(1)}, u32[]{:S(2)}, u32[]{:S(2)}) %collective-permute-start.3) | collective-permute-done | bytes 131104 | tf_op jit(solution)/shard_map/ppermute | solution.py:45
  19.1 1.6 %collective-permute-start.10 = (bf16[2,2,256,128]{3,2,1,0:T(8,128)(2,1)S(1)}, bf16[2,2,256,128]{3,2,1,0:T(8,128)(2,1)S(1)}, u32[]{:S(2)}, u32[]{:S(2)}) collective-permute-start(bf16[2,2,256,128]{3,2,1,0:T(8,128)(2,1)S(1)} %get-tuple-element.54), channel_id=1, source_target_pairs={{0,4},{1,5},{2,6},{3,7},{4,0},{5,1},{6,2},{7,3},{8,12},{9,13},{10,... | collective-permute-start | bytes 786440 | tf_op jit(solution)/shard_map/ppermute | solution.py:45
  20.7 0.5 collective-permute-start.9
  21.3 1.6 %collective-permute-start.4 = (bf16[1,2,256,128]{3,2,1,0:T(8,128)(2,1)S(1)}, bf16[1,2,256,128]{3,2,1,0:T(8,128)(2,1)S(1)}, u32[]{:S(2)}, u32[]{:S(2)}) collective-permute-start(bf16[1,2,256,128]{3,2,1,0:T(8,128)(2,1)S(1)} %get-tuple-element.48.refs_3_.refs_2_), channel_id=1, source_target_pairs={{0,2},{1,3},{2,0},{3,1},{4,6},{5,7},{6,4},{7,5},{8,10},{9,11},{10,... | collective-permute-start | bytes 393224 | tf_op jit(solution)/shard_map/ppermute | solution.py:45
  23.4 0.6 solve_pack.1
  23.9 1.6 %collective-permute-start.6 = (bf16[272,128]{1,0:T(8,128)(2,1)S(1)}, bf16[272,128]{1,0:T(8,128)(2,1)S(1)}, u32[]{:S(2)}, u32[]{:S(2)}) collective-permute-start(bf16[272,128]{1,0:T(8,128)(2,1)S(1)} %get-tuple-element.51), channel_id=1, source_target_pairs={{0,8},{8,0},{16,24},{24,16},{1,9},{9,1},{17,25},{25,17},{2,10},{10... | collective-permute-start | bytes 208904 | tf_op jit(solution)/shard_map/ppermute | solution.py:45
  25.6 2.7 %collective-permute-done.6.refs_1_.refs_6_ = bf16[272,128]{1,0:T(8,128)(2,1)S(1)} collective-permute-done((bf16[272,128]{1,0:T(8,128)(2,1)S(1)}, bf16[272,128]{1,0:T(8,128)(2,1)S(1)}, u32[]{:S(2)}, u32[]{:S(2)}) %collective-permute-start.6) | collective-permute-done | bytes 69664 | tf_op jit(solution)/shard_map/ppermute | solution.py:45
  28.3 2.7 %collective-permute-start.14 = (bf16[544,128]{1,0:T(8,128)(2,1)S(1)}, bf16[544,128]{1,0:T(8,128)(2,1)S(1)}, u32[]{:S(2)}, u32[]{:S(2)}) collective-permute-start(bf16[544,128]{1,0:T(8,128)(2,1)S(1)} %solve_join.1.refs_4_), channel_id=1, source_target_pairs={{0,16},{8,24},{16,0},{24,8},{1,17},{9,25},{17,1},{25,9},{2,18},{10... | collective-permute-start | bytes 417800 | tf_op jit(solution)/shard_map/ppermute | solution.py:45
  31.1 0.6 collective-permute-start.7
  31.7 1.5 %collective-permute-start.8 = (bf16[2,2,256,128]{3,2,1,0:T(8,128)(2,1)S(1)}, bf16[2,2,256,128]{3,2,1,0:T(8,128)(2,1)S(1)}, u32[]{:S(2)}, u32[]{:S(2)}) collective-permute-start(bf16[2,2,256,128]{3,2,1,0:T(8,128)(2,1)S(1)} %get-tuple-element.53), channel_id=1, source_target_pairs={{0,4},{1,5},{2,6},{3,7},{4,0},{5,1},{6,2},{7,3},{8,12},{9,13},{10,... | collective-permute-start | bytes 786440 | tf_op jit(solution)/shard_map/ppermute | solution.py:45
  33.3 0.7 interface_reduce.2
  34.0 1.6 %collective-permute-start.15 = (bf16[2,128,128]{2,1,0:T(8,128)(2,1)S(1)}, bf16[2,128,128]{2,1,0:T(8,128)(2,1)S(1)}, u32[]{:S(2)}, u32[]{:S(2)}) collective-permute-start(bf16[2,128,128]{2,1,0:T(8,128)(2,1)S(1)} %get-tuple-element.60), channel_id=1, source_target_pairs={{0,8},{8,0},{16,24},{24,16},{1,9},{9,1},{17,25},{25,17},{2,10},{10... | collective-permute-start | bytes 196616 | tf_op jit(solution)/shard_map/ppermute | solution.py:45
  35.6 1.5 %collective-permute-start.16 = (bf16[2,128,128]{2,1,0:T(8,128)(2,1)S(1)}, bf16[2,128,128]{2,1,0:T(8,128)(2,1)S(1)}, u32[]{:S(2)}, u32[]{:S(2)}) collective-permute-start(bf16[2,128,128]{2,1,0:T(8,128)(2,1)S(1)} %get-tuple-element.61), channel_id=1, source_target_pairs={{0,16},{8,24},{16,0},{24,8},{1,17},{9,25},{17,1},{25,9},{2,18},{10... | collective-permute-start | bytes 196616 | tf_op jit(solution)/shard_map/ppermute | solution.py:45
  37.6 3.0 %collective-permute-start.17 = (bf16[2,128,128]{2,1,0:T(8,128)(2,1)S(1)}, bf16[2,128,128]{2,1,0:T(8,128)(2,1)S(1)}, u32[]{:S(2)}, u32[]{:S(2)}) collective-permute-start(bf16[2,128,128]{2,1,0:T(8,128)(2,1)S(1)} %get-tuple-element.62), channel_id=1, source_target_pairs={{0,24},{8,16},{16,8},{24,0},{1,25},{9,17},{17,9},{25,1},{2,26},{10... | collective-permute-start | bytes 196616 | tf_op jit(solution)/shard_map/ppermute | solution.py:45
  40.6 0.7 interface_reduce.3
  41.4 1.3 %collective-permute-start.12 = (bf16[2,128,128]{2,1,0:T(8,128)(2,1)S(1)}, bf16[2,128,128]{2,1,0:T(8,128)(2,1)S(1)}, u32[]{:S(2)}, u32[]{:S(2)}) collective-permute-start(bf16[2,128,128]{2,1,0:T(8,128)(2,1)S(1)} %get-tuple-element.58), channel_id=1, source_target_pairs={{0,16},{8,24},{16,0},{24,8},{1,17},{9,25},{17,1},{25,9},{2,18},{10... | collective-permute-start | bytes 196616 | tf_op jit(solution)/shard_map/ppermute | solution.py:45
  42.8 3.0 %collective-permute-start.13 = (bf16[2,128,128]{2,1,0:T(8,128)(2,1)S(1)}, bf16[2,128,128]{2,1,0:T(8,128)(2,1)S(1)}, u32[]{:S(2)}, u32[]{:S(2)}) collective-permute-start(bf16[2,128,128]{2,1,0:T(8,128)(2,1)S(1)} %get-tuple-element.59), channel_id=1, source_target_pairs={{0,24},{8,16},{16,8},{24,0},{1,25},{9,17},{17,9},{25,1},{2,26},{10... | collective-permute-start | bytes 196616 | tf_op jit(solution)/shard_map/ppermute | solution.py:45
  45.8 1.5 %sweep_chain.2 = (bf16[2,128,128]{2,1,0:T(8,128)(2,1)S(1)}, bf16[2,128,128]{2,1,0:T(8,128)(2,1)S(1)}, bf16[2,128,128]{2,1,0:T(8,128)(2,1)S(1)}, bf16[2,128,128]{2,1,0:T(8,128)(2,1)S(1)}) custom-call(s32[2]{0:T(128)S(1)} %pad_add_fusion.refs_1_.refs_0_, bf16[2,128,128]{2,1,0:T(8,128)(2,1)S(1)} %get-tuple-element.55.refs_6_.refs_1_, ...), custom_call_target="tpu_custom_call" | custom-call | flops 10000000000 | bytes 1 | tf_op jit(solution)/shard_map/sweep_chain/pallas_call | solution.py:31
  47.7 1.6 %collective-permute-start.22 = (bf16[2,128,128]{2,1,0:T(8,128)(2,1)S(1)}, bf16[2,128,128]{2,1,0:T(8,128)(2,1)S(1)}, u32[]{:S(2)}, u32[]{:S(2)}) collective-permute-start(bf16[2,128,128]{2,1,0:T(8,128)(2,1)S(1)} %get-tuple-element.69), channel_id=1, source_target_pairs={{0,16},{8,24},{16,0},{24,8},{1,17},{9,25},{17,1},{25,9},{2,18},{10... | collective-permute-start | bytes 196616 | tf_op jit(solution)/shard_map/ppermute | solution.py:45
  49.3 2.4 %collective-permute-start.23 = (bf16[2,128,128]{2,1,0:T(8,128)(2,1)S(1)}, bf16[2,128,128]{2,1,0:T(8,128)(2,1)S(1)}, u32[]{:S(2)}, u32[]{:S(2)}) collective-permute-start(bf16[2,128,128]{2,1,0:T(8,128)(2,1)S(1)} %get-tuple-element.70), channel_id=1, source_target_pairs={{0,24},{8,16},{16,8},{24,0},{1,25},{9,17},{17,9},{25,1},{2,26},{10... | collective-permute-start | bytes 196616 | tf_op jit(solution)/shard_map/ppermute | solution.py:45
  51.7 1.5 %sweep_chain.3 = (bf16[2,128,128]{2,1,0:T(8,128)(2,1)S(1)}, bf16[2,128,128]{2,1,0:T(8,128)(2,1)S(1)}, bf16[2,128,128]{2,1,0:T(8,128)(2,1)S(1)}, bf16[2,128,128]{2,1,0:T(8,128)(2,1)S(1)}) custom-call(s32[2]{0:T(128)S(1)} %pad_add_fusion.refs_1_.refs_0_, bf16[2,128,128]{2,1,0:T(8,128)(2,1)S(1)} %get-tuple-element.56.refs_8_.refs_1_, ...), custom_call_target="tpu_custom_call" | custom-call | flops 10000000000 | bytes 1 | tf_op jit(solution)/shard_map/sweep_chain/pallas_call | solution.py:31
  53.3 2.0 %collective-permute-start.19 = (bf16[2,128,128]{2,1,0:T(8,128)(2,1)S(1)}, bf16[2,128,128]{2,1,0:T(8,128)(2,1)S(1)}, u32[]{:S(2)}, u32[]{:S(2)}) collective-permute-start(bf16[2,128,128]{2,1,0:T(8,128)(2,1)S(1)} %get-tuple-element.66), channel_id=1, source_target_pairs={{0,16},{8,24},{16,0},{24,8},{1,17},{9,25},{17,1},{25,9},{2,18},{10... | collective-permute-start | bytes 196616 | tf_op jit(solution)/shard_map/ppermute | solution.py:45
  55.3 2.4 %collective-permute-start.20 = (bf16[2,128,128]{2,1,0:T(8,128)(2,1)S(1)}, bf16[2,128,128]{2,1,0:T(8,128)(2,1)S(1)}, u32[]{:S(2)}, u32[]{:S(2)}) collective-permute-start(bf16[2,128,128]{2,1,0:T(8,128)(2,1)S(1)} %get-tuple-element.67), channel_id=1, source_target_pairs={{0,24},{8,16},{16,8},{24,0},{1,25},{9,17},{17,9},{25,1},{2,26},{10... | collective-permute-start | bytes 196616 | tf_op jit(solution)/shard_map/ppermute | solution.py:45
  57.7 0.6 interface_collect.2.refs_5_.refs_0_.refs_4_.refs_8_
  58.3 0.7 collective-permute-start.24
  58.9 1.0 %collective-permute-start.25 = (bf16[2,2,256,128]{3,2,1,0:T(8,128)(2,1)S(1)}, bf16[2,2,256,128]{3,2,1,0:T(8,128)(2,1)S(1)}, u32[]{:S(2)}, u32[]{:S(2)}) collective-permute-start(bf16[2,2,256,128]{3,2,1,0:T(8,128)(2,1)S(1)} %interface_collect.2.refs_5_.refs_0_.refs_4_.refs_8_), channel_id=1, source_target_pairs={{0,4},{1,5},{2,6},{3,7},{4,0},{5,1},{6,2},{7,3},{8,12},{9,13},{10,... | collective-permute-start | bytes 786440 | tf_op jit(solution)/shard_map/ppermute | solution.py:45
  59.9 1.4 %collective-permute-done.20.refs_4_ = bf16[2,128,128]{2,1,0:T(8,128)(2,1)S(1)} collective-permute-done((bf16[2,128,128]{2,1,0:T(8,128)(2,1)S(1)}, bf16[2,128,128]{2,1,0:T(8,128)(2,1)S(1)}, u32[]{:S(2)}, u32[]{:S(2)}) %collective-permute-start.20) | collective-permute-done | bytes 65568 | tf_op jit(solution)/shard_map/ppermute | solution.py:45
  61.4 0.6 interface_collect.3.refs_3_.refs_0_.refs_9_.refs_4_
  61.9 0.7 collective-permute-start.28
  62.6 0.9 %collective-permute-start.29 = (bf16[2,2,256,128]{3,2,1,0:T(8,128)(2,1)S(1)}, bf16[2,2,256,128]{3,2,1,0:T(8,128)(2,1)S(1)}, u32[]{:S(2)}, u32[]{:S(2)}) collective-permute-start(bf16[2,2,256,128]{3,2,1,0:T(8,128)(2,1)S(1)} %interface_collect.3.refs_3_.refs_0_.refs_9_.refs_4_), channel_id=1, source_target_pairs={{0,4},{1,5},{2,6},{3,7},{4,0},{5,1},{6,2},{7,3},{8,12},{9,13},{10,... | collective-permute-start | bytes 786440 | tf_op jit(solution)/shard_map/ppermute | solution.py:45
  63.6 1.5 %leaf_fold.1.refs_3_ = bf16[16,256,768]{2,1,0:T(8,128)(2,1)S(1)} custom-call(bf16[1,16,2,128,128]{4,3,2,1,0:T(8,128)(2,1)S(1)} %copy-done.1, bf16[1,16,2,128,128]{4,3,2,1,0:T(8,128)(2,1)S(1)} %copy-done.2, s32[1,16,128]{2,1,0:T(8,128)S(1)} %copy-done.5, bf16[2,2,256,128]{3,2,1,0:T(8,128)(2,1)S(1)} %interface_collect.3.refs_3_.refs_0_.refs_9_.refs_4_), custom_call_target="tpu_custom_call" | custom-call | flops 10000000000 | bytes 1 | tf_op jit(solution)/shard_map/leaf_fold/pallas_call | solution.py:31
  65.0 0.8 collective-permute-done.25.refs_2_.refs_7_
  65.9 0.9 %collective-permute-start.26 = (bf16[1,2,256,128]{3,2,1,0:T(8,128)(2,1)S(1)}, bf16[1,2,256,128]{3,2,1,0:T(8,128)(2,1)S(1)}, u32[]{:S(2)}, u32[]{:S(2)}) collective-permute-start(bf16[1,2,256,128]{3,2,1,0:T(8,128)(2,1)S(1)} %get-tuple-element.71.refs_3_), channel_id=1, source_target_pairs={{0,4},{1,5},{2,6},{3,7},{4,0},{5,1},{6,2},{7,3},{8,12},{9,13},{10,... | collective-permute-start | bytes 393224 | tf_op jit(solution)/shard_map/ppermute | solution.py:45
  66.9 1.1 %collective-permute-start.27 = (bf16[1,2,256,128]{3,2,1,0:T(8,128)(2,1)S(1)}, bf16[1,2,256,128]{3,2,1,0:T(8,128)(2,1)S(1)}, u32[]{:S(2)}, u32[]{:S(2)}) collective-permute-start(bf16[1,2,256,128]{3,2,1,0:T(8,128)(2,1)S(1)} %get-tuple-element.72), channel_id=1, source_target_pairs={{0,2},{1,3},{2,0},{3,1},{4,6},{5,7},{6,4},{7,5},{8,10},{9,11},{10,... | collective-permute-start | bytes 393224 | tf_op jit(solution)/shard_map/ppermute | solution.py:45
  68.4 0.6 collective-permute-done.29.refs_2_.refs_7_
  69.2 1.0 %collective-permute-start.30 = (bf16[1,2,256,128]{3,2,1,0:T(8,128)(2,1)S(1)}, bf16[1,2,256,128]{3,2,1,0:T(8,128)(2,1)S(1)}, u32[]{:S(2)}, u32[]{:S(2)}) collective-permute-start(bf16[1,2,256,128]{3,2,1,0:T(8,128)(2,1)S(1)} %get-tuple-element.73.refs_10_), channel_id=1, source_target_pairs={{0,4},{1,5},{2,6},{3,7},{4,0},{5,1},{6,2},{7,3},{8,12},{9,13},{10,... | collective-permute-start | bytes 393224 | tf_op jit(solution)/shard_map/ppermute | solution.py:45
  70.1 2.5 %collective-permute-start.31 = (bf16[1,2,256,128]{3,2,1,0:T(8,128)(2,1)S(1)}, bf16[1,2,256,128]{3,2,1,0:T(8,128)(2,1)S(1)}, u32[]{:S(2)}, u32[]{:S(2)}) collective-permute-start(bf16[1,2,256,128]{3,2,1,0:T(8,128)(2,1)S(1)} %get-tuple-element.74), channel_id=1, source_target_pairs={{0,2},{1,3},{2,0},{3,1},{4,6},{5,7},{6,4},{7,5},{8,10},{9,11},{10,... | collective-permute-start | bytes 393224 | tf_op jit(solution)/shard_map/ppermute | solution.py:45
  72.7 3.2 %leaf_backward.3 = (bf16[1,2,16,128,512]{4,3,2,1,0:T(8,128)(2,1)}, f32[1,2,256,512]{3,2,1,0:T(8,128)}, f32[8,128]{1,0:T(8,128)S(1)}) custom-call(s32[16]{0:T(128)S(1)} %bitcast.7, s32[2]{0:T(128)S(1)} %pad_add_fusion.refs_1_.refs_0_, bf16[1,2,16,128,512]{4,3,2,1,0:T(8,128)(2,1)S(1)} %copy-done, bf16[16,256,768]{2,1,0:T(8,128)(2,1)S(1)} %leaf_fold.1.refs_3_, ...), custom_call_target="tpu_custom_call" | custom-call | flops 10000000000 | bytes 1 | tf_op jit(solution)/shard_map/leaf_backward/pallas_call | solution.py:31
  75.9 0.6 collective-permute-done.31.refs_3_
  76.6 3.1 %leaf_backward.4.refs_6_ = bf16[1,2,16,128,512]{4,3,2,1,0:T(8,128)(2,1)} custom-call(s32[16]{0:T(128)S(1)} %bitcast.8, s32[2]{0:T(128)S(1)} %pad_add_fusion.refs_1_.refs_0_, bf16[1,2,16,128,512]{4,3,2,1,0:T(8,128)(2,1)S(1)} %copy-done, bf16[16,256,768]{2,1,0:T(8,128)(2,1)S(1)} %leaf_fold.1.refs_3_, ...), custom_call_target="tpu_custom_call", output_to_operand_aliasing={{}: (8, {})} | custom-call | flops 10000000000 | bytes 1 | tf_op jit(solution)/shard_map/leaf_backward/pallas_call | solution.py:31
  79.8 2.6 %leaf_backward.5 = bf16[1,2,16,128,512]{4,3,2,1,0:T(8,128)(2,1)} custom-call(s32[16]{0:T(128)S(1)} %bitcast.9, s32[2]{0:T(128)S(1)} %pad_add_fusion.refs_1_.refs_0_, bf16[1,2,16,128,512]{4,3,2,1,0:T(8,128)(2,1)S(1)} %copy-done, bf16[16,256,768]{2,1,0:T(8,128)(2,1)S(1)} %leaf_fold.1.refs_3_, ...), custom_call_target="tpu_custom_call", output_to_operand_aliasing={{}: (6, {})} | custom-call | flops 10000000000 | bytes 1 | tf_op jit(solution)/shard_map/leaf_backward/pallas_call | solution.py:31
  (60 shorter events, 3.5 us)
Async XLA Ops:
  0.7 0.7 copy-start.5
  1.4 0.7 copy-start.7
  2.1 13.1 %copy-start = (bf16[1,2,16,128,512]{4,3,2,1,0:T(8,128)(2,1)S(1)}, bf16[1,2,16,128,512]{4,3,2,1,0:T(8,128)(2,1)}, u32[]{:S(2)}) copy-start(bf16[1,2,16,128,512]{4,3,2,1,0:T(8,128)(2,1)} %refs_2_.11) | copy-start | bytes 12582916
  2.1 13.1 %copy-start.1 = (bf16[1,16,2,128,128]{4,3,2,1,0:T(8,128)(2,1)S(1)}, bf16[1,16,2,128,128]{4,3,2,1,0:T(8,128)(2,1)}, u32[]{:S(2)}) copy-start(bf16[1,16,2,128,128]{4,3,2,1,0:T(8,128)(2,1)} %refs_0_.1) | copy-start | bytes 3145732
  2.1 13.1 %copy-start.2 = (bf16[1,16,2,128,128]{4,3,2,1,0:T(8,128)(2,1)S(1)}, bf16[1,16,2,128,128]{4,3,2,1,0:T(8,128)(2,1)}, u32[]{:S(2)}) copy-start(bf16[1,16,2,128,128]{4,3,2,1,0:T(8,128)(2,1)} %refs_1_.7) | copy-start | bytes 3145732
  7.7 3.0 %collective-permute-start = (bf16[4,2,2,256,128]{4,3,2,1,0:T(8,128)(2,1)}, bf16[4,2,2,256,128]{4,3,2,1,0:T(8,128)(2,1)S(1)}, u32[]{:S(2)}, u32[]{:S(2)}) collective-permute-start(bf16[4,2,2,256,128]{4,3,2,1,0:T(8,128)(2,1)} %get-tuple-element.42), channel_id=1, source_target_pairs={{0,1},{1,0},{2,3},{3,2},{4,5},{5,4},{6,7},{7,6},{8,9},{9,8},{10,11... | collective-permute-start | bytes 3145736 | tf_op jit(solution)/shard_map/ppermute | solution.py:45
  10.7 7.1 %collective-permute-start.2 = (bf16[1,2,256,128]{3,2,1,0:T(8,128)(2,1)S(1)}, bf16[1,2,256,128]{3,2,1,0:T(8,128)(2,1)S(1)}, u32[]{:S(2)}, u32[]{:S(2)}) collective-permute-start(bf16[1,2,256,128]{3,2,1,0:T(8,128)(2,1)S(1)} %get-tuple-element.43.refs_6_), channel_id=1, source_target_pairs={{0,2},{1,3},{2,0},{3,1},{4,6},{5,7},{6,4},{7,5},{8,10},{9,11},{10,... | collective-permute-start | bytes 393224 | tf_op jit(solution)/shard_map/ppermute | solution.py:45
  13.7 5.3 %collective-permute-start.3 = (bf16[1,2,256,128]{3,2,1,0:T(8,128)(2,1)S(1)}, bf16[1,2,256,128]{3,2,1,0:T(8,128)(2,1)S(1)}, u32[]{:S(2)}, u32[]{:S(2)}) collective-permute-start(bf16[1,2,256,128]{3,2,1,0:T(8,128)(2,1)S(1)} %get-tuple-element.46), channel_id=1, source_target_pairs={{0,4},{1,5},{2,6},{3,7},{4,0},{5,1},{6,2},{7,3},{8,12},{9,13},{10,... | collective-permute-start | bytes 393224 | tf_op jit(solution)/shard_map/ppermute | solution.py:45
  17.8 3.5 %collective-permute-start.1 = (bf16[4,2,2,256,128]{4,3,2,1,0:T(8,128)(2,1)S(1)}, bf16[4,2,2,256,128]{4,3,2,1,0:T(8,128)(2,1)S(1)}, u32[]{:S(2)}, u32[]{:S(2)}) collective-permute-start(bf16[4,2,2,256,128]{4,3,2,1,0:T(8,128)(2,1)S(1)} %get-tuple-element.45), channel_id=1, source_target_pairs={{0,1},{1,0},{2,3},{3,2},{4,5},{5,4},{6,7},{7,6},{8,9},{9,8},{10,11... | collective-permute-start | bytes 3145736 | tf_op jit(solution)/shard_map/ppermute | solution.py:45
  18.9 4.4 %copy-start.4 = (f32[1,2,2,128,128]{4,3,2,1,0:T(8,128)S(1)}, f32[1,2,2,128,128]{4,3,2,1,0:T(8,128)}, u32[]{:S(2)}) copy-start(f32[1,2,2,128,128]{4,3,2,1,0:T(8,128)} %refs_1_.4) | copy-start | bytes 786436
  18.9 4.4 %copy-start.6 = (f32[1,256]{1,0:T(1,128)S(1)}, f32[1,256]{1,0:T(1,128)}, u32[]{:S(2)}) copy-start(f32[1,256]{1,0:T(1,128)} %param.15) | copy-start | bytes 3076
  19.1 14.2 %collective-permute-start.10 = (bf16[2,2,256,128]{3,2,1,0:T(8,128)(2,1)S(1)}, bf16[2,2,256,128]{3,2,1,0:T(8,128)(2,1)S(1)}, u32[]{:S(2)}, u32[]{:S(2)}) collective-permute-start(bf16[2,2,256,128]{3,2,1,0:T(8,128)(2,1)S(1)} %get-tuple-element.54), channel_id=1, source_target_pairs={{0,4},{1,5},{2,6},{3,7},{4,0},{5,1},{6,2},{7,3},{8,12},{9,13},{10,... | collective-permute-start | bytes 786440 | tf_op jit(solution)/shard_map/ppermute | solution.py:45
  20.7 12.6 %collective-permute-start.9 = (bf16[2,2,256,128]{3,2,1,0:T(8,128)(2,1)S(1)}, bf16[2,2,256,128]{3,2,1,0:T(8,128)(2,1)S(1)}, u32[]{:S(2)}, u32[]{:S(2)}) collective-permute-start(bf16[2,2,256,128]{3,2,1,0:T(8,128)(2,1)S(1)} %get-tuple-element.47.refs_2_), channel_id=1, source_target_pairs={{0,2},{1,3},{2,0},{3,1},{4,6},{5,7},{6,4},{7,5},{8,10},{9,11},{10,... | collective-permute-start | bytes 786440 | tf_op jit(solution)/shard_map/ppermute | solution.py:45
  21.3 9.7 %collective-permute-start.4 = (bf16[1,2,256,128]{3,2,1,0:T(8,128)(2,1)S(1)}, bf16[1,2,256,128]{3,2,1,0:T(8,128)(2,1)S(1)}, u32[]{:S(2)}, u32[]{:S(2)}) collective-permute-start(bf16[1,2,256,128]{3,2,1,0:T(8,128)(2,1)S(1)} %get-tuple-element.48.refs_3_.refs_2_), channel_id=1, source_target_pairs={{0,2},{1,3},{2,0},{3,1},{4,6},{5,7},{6,4},{7,5},{8,10},{9,11},{10,... | collective-permute-start | bytes 393224 | tf_op jit(solution)/shard_map/ppermute | solution.py:45
  22.8 8.1 %collective-permute-start.5 = (bf16[1,2,256,128]{3,2,1,0:T(8,128)(2,1)S(1)}, bf16[1,2,256,128]{3,2,1,0:T(8,128)(2,1)S(1)}, u32[]{:S(2)}, u32[]{:S(2)}) collective-permute-start(bf16[1,2,256,128]{3,2,1,0:T(8,128)(2,1)S(1)} %get-tuple-element.49), channel_id=1, source_target_pairs={{0,4},{1,5},{2,6},{3,7},{4,0},{5,1},{6,2},{7,3},{8,12},{9,13},{10,... | collective-permute-start | bytes 393224 | tf_op jit(solution)/shard_map/ppermute | solution.py:45
  23.3 9.9 %copy-start.3 = (bf16[1,2,256,512]{3,2,1,0:T(8,128)(2,1)S(1)}, bf16[1,2,256,512]{3,2,1,0:T(8,128)(2,1)}, u32[]{:S(2)}) copy-start(bf16[1,2,256,512]{3,2,1,0:T(8,128)(2,1)} %refs_1_.6) | copy-start | bytes 1572868
  23.9 4.4 %collective-permute-start.6 = (bf16[272,128]{1,0:T(8,128)(2,1)S(1)}, bf16[272,128]{1,0:T(8,128)(2,1)S(1)}, u32[]{:S(2)}, u32[]{:S(2)}) collective-permute-start(bf16[272,128]{1,0:T(8,128)(2,1)S(1)} %get-tuple-element.51), channel_id=1, source_target_pairs={{0,8},{8,0},{16,24},{24,16},{1,9},{9,1},{17,25},{25,17},{2,10},{10... | collective-permute-start | bytes 208904 | tf_op jit(solution)/shard_map/ppermute | solution.py:45
  28.3 17.5 %collective-permute-start.14 = (bf16[544,128]{1,0:T(8,128)(2,1)S(1)}, bf16[544,128]{1,0:T(8,128)(2,1)S(1)}, u32[]{:S(2)}, u32[]{:S(2)}) collective-permute-start(bf16[544,128]{1,0:T(8,128)(2,1)S(1)} %solve_join.1.refs_4_), channel_id=1, source_target_pairs={{0,16},{8,24},{16,0},{24,8},{1,17},{9,25},{17,1},{25,9},{2,18},{10... | collective-permute-start | bytes 417800 | tf_op jit(solution)/shard_map/ppermute | solution.py:45
  31.1 6.4 %collective-permute-start.7 = (bf16[2,2,256,128]{3,2,1,0:T(8,128)(2,1)S(1)}, bf16[2,2,256,128]{3,2,1,0:T(8,128)(2,1)S(1)}, u32[]{:S(2)}, u32[]{:S(2)}) collective-permute-start(bf16[2,2,256,128]{3,2,1,0:T(8,128)(2,1)S(1)} %get-tuple-element.52.refs_6_), channel_id=1, source_target_pairs={{0,2},{1,3},{2,0},{3,1},{4,6},{5,7},{6,4},{7,5},{8,10},{9,11},{10,... | collective-permute-start | bytes 786440 | tf_op jit(solution)/shard_map/ppermute | solution.py:45
  31.7 8.9 %collective-permute-start.8 = (bf16[2,2,256,128]{3,2,1,0:T(8,128)(2,1)S(1)}, bf16[2,2,256,128]{3,2,1,0:T(8,128)(2,1)S(1)}, u32[]{:S(2)}, u32[]{:S(2)}) collective-permute-start(bf16[2,2,256,128]{3,2,1,0:T(8,128)(2,1)S(1)} %get-tuple-element.53), channel_id=1, source_target_pairs={{0,4},{1,5},{2,6},{3,7},{4,0},{5,1},{6,2},{7,3},{8,12},{9,13},{10,... | collective-permute-start | bytes 786440 | tf_op jit(solution)/shard_map/ppermute | solution.py:45
  34.0 7.4 %collective-permute-start.15 = (bf16[2,128,128]{2,1,0:T(8,128)(2,1)S(1)}, bf16[2,128,128]{2,1,0:T(8,128)(2,1)S(1)}, u32[]{:S(2)}, u32[]{:S(2)}) collective-permute-start(bf16[2,128,128]{2,1,0:T(8,128)(2,1)S(1)} %get-tuple-element.60), channel_id=1, source_target_pairs={{0,8},{8,0},{16,24},{24,16},{1,9},{9,1},{17,25},{25,17},{2,10},{10... | collective-permute-start | bytes 196616 | tf_op jit(solution)/shard_map/ppermute | solution.py:45
  35.6 7.1 %collective-permute-start.16 = (bf16[2,128,128]{2,1,0:T(8,128)(2,1)S(1)}, bf16[2,128,128]{2,1,0:T(8,128)(2,1)S(1)}, u32[]{:S(2)}, u32[]{:S(2)}) collective-permute-start(bf16[2,128,128]{2,1,0:T(8,128)(2,1)S(1)} %get-tuple-element.61), channel_id=1, source_target_pairs={{0,16},{8,24},{16,0},{24,8},{1,17},{9,25},{17,1},{25,9},{2,18},{10... | collective-permute-start | bytes 196616 | tf_op jit(solution)/shard_map/ppermute | solution.py:45
  37.6 8.2 %collective-permute-start.17 = (bf16[2,128,128]{2,1,0:T(8,128)(2,1)S(1)}, bf16[2,128,128]{2,1,0:T(8,128)(2,1)S(1)}, u32[]{:S(2)}, u32[]{:S(2)}) collective-permute-start(bf16[2,128,128]{2,1,0:T(8,128)(2,1)S(1)} %get-tuple-element.62), channel_id=1, source_target_pairs={{0,24},{8,16},{16,8},{24,0},{1,25},{9,17},{17,9},{25,1},{2,26},{10... | collective-permute-start | bytes 196616 | tf_op jit(solution)/shard_map/ppermute | solution.py:45
  41.3 8.0 %collective-permute-start.11 = (bf16[2,128,128]{2,1,0:T(8,128)(2,1)S(1)}, bf16[2,128,128]{2,1,0:T(8,128)(2,1)S(1)}, u32[]{:S(2)}, u32[]{:S(2)}) collective-permute-start(bf16[2,128,128]{2,1,0:T(8,128)(2,1)S(1)} %get-tuple-element.57), channel_id=1, source_target_pairs={{0,8},{8,0},{16,24},{24,16},{1,9},{9,1},{17,25},{25,17},{2,10},{10... | collective-permute-start | bytes 196616 | tf_op jit(solution)/shard_map/ppermute | solution.py:45
  41.4 10.3 %collective-permute-start.12 = (bf16[2,128,128]{2,1,0:T(8,128)(2,1)S(1)}, bf16[2,128,128]{2,1,0:T(8,128)(2,1)S(1)}, u32[]{:S(2)}, u32[]{:S(2)}) collective-permute-start(bf16[2,128,128]{2,1,0:T(8,128)(2,1)S(1)} %get-tuple-element.58), channel_id=1, source_target_pairs={{0,16},{8,24},{16,0},{24,8},{1,17},{9,25},{17,1},{25,9},{2,18},{10... | collective-permute-start | bytes 196616 | tf_op jit(solution)/shard_map/ppermute | solution.py:45
  42.8 9.0 %collective-permute-start.13 = (bf16[2,128,128]{2,1,0:T(8,128)(2,1)S(1)}, bf16[2,128,128]{2,1,0:T(8,128)(2,1)S(1)}, u32[]{:S(2)}, u32[]{:S(2)}) collective-permute-start(bf16[2,128,128]{2,1,0:T(8,128)(2,1)S(1)} %get-tuple-element.59), channel_id=1, source_target_pairs={{0,24},{8,16},{16,8},{24,0},{1,25},{9,17},{17,9},{25,1},{2,26},{10... | collective-permute-start | bytes 196616 | tf_op jit(solution)/shard_map/ppermute | solution.py:45
  47.3 8.0 %collective-permute-start.21 = (bf16[2,128,128]{2,1,0:T(8,128)(2,1)S(1)}, bf16[2,128,128]{2,1,0:T(8,128)(2,1)S(1)}, u32[]{:S(2)}, u32[]{:S(2)}) collective-permute-start(bf16[2,128,128]{2,1,0:T(8,128)(2,1)S(1)} %get-tuple-element.68), channel_id=1, source_target_pairs={{0,8},{8,0},{16,24},{24,16},{1,9},{9,1},{17,25},{25,17},{2,10},{10... | collective-permute-start | bytes 196616 | tf_op jit(solution)/shard_map/ppermute | solution.py:45
  47.7 10.0 %collective-permute-start.22 = (bf16[2,128,128]{2,1,0:T(8,128)(2,1)S(1)}, bf16[2,128,128]{2,1,0:T(8,128)(2,1)S(1)}, u32[]{:S(2)}, u32[]{:S(2)}) collective-permute-start(bf16[2,128,128]{2,1,0:T(8,128)(2,1)S(1)} %get-tuple-element.69), channel_id=1, source_target_pairs={{0,16},{8,24},{16,0},{24,8},{1,17},{9,25},{17,1},{25,9},{2,18},{10... | collective-permute-start | bytes 196616 | tf_op jit(solution)/shard_map/ppermute | solution.py:45
  49.3 8.3 %collective-permute-start.23 = (bf16[2,128,128]{2,1,0:T(8,128)(2,1)S(1)}, bf16[2,128,128]{2,1,0:T(8,128)(2,1)S(1)}, u32[]{:S(2)}, u32[]{:S(2)}) collective-permute-start(bf16[2,128,128]{2,1,0:T(8,128)(2,1)S(1)} %get-tuple-element.70), channel_id=1, source_target_pairs={{0,24},{8,16},{16,8},{24,0},{1,25},{9,17},{17,9},{25,1},{2,26},{10... | collective-permute-start | bytes 196616 | tf_op jit(solution)/shard_map/ppermute | solution.py:45
  53.2 6.7 %collective-permute-start.18 = (bf16[2,128,128]{2,1,0:T(8,128)(2,1)S(1)}, bf16[2,128,128]{2,1,0:T(8,128)(2,1)S(1)}, u32[]{:S(2)}, u32[]{:S(2)}) collective-permute-start(bf16[2,128,128]{2,1,0:T(8,128)(2,1)S(1)} %get-tuple-element.65), channel_id=1, source_target_pairs={{0,8},{8,0},{16,24},{24,16},{1,9},{9,1},{17,25},{25,17},{2,10},{10... | collective-permute-start | bytes 196616 | tf_op jit(solution)/shard_map/ppermute | solution.py:45
  53.3 6.6 %collective-permute-start.19 = (bf16[2,128,128]{2,1,0:T(8,128)(2,1)S(1)}, bf16[2,128,128]{2,1,0:T(8,128)(2,1)S(1)}, u32[]{:S(2)}, u32[]{:S(2)}) collective-permute-start(bf16[2,128,128]{2,1,0:T(8,128)(2,1)S(1)} %get-tuple-element.66), channel_id=1, source_target_pairs={{0,16},{8,24},{16,0},{24,8},{1,17},{9,25},{17,1},{25,9},{2,18},{10... | collective-permute-start | bytes 196616 | tf_op jit(solution)/shard_map/ppermute | solution.py:45
  55.3 6.1 %collective-permute-start.20 = (bf16[2,128,128]{2,1,0:T(8,128)(2,1)S(1)}, bf16[2,128,128]{2,1,0:T(8,128)(2,1)S(1)}, u32[]{:S(2)}, u32[]{:S(2)}) collective-permute-start(bf16[2,128,128]{2,1,0:T(8,128)(2,1)S(1)} %get-tuple-element.67), channel_id=1, source_target_pairs={{0,24},{8,16},{16,8},{24,0},{1,25},{9,17},{17,9},{25,1},{2,26},{10... | collective-permute-start | bytes 196616 | tf_op jit(solution)/shard_map/ppermute | solution.py:45
  58.3 6.8 %collective-permute-start.24 = (bf16[2,2,256,128]{3,2,1,0:T(8,128)(2,1)S(1)}, bf16[2,2,256,128]{3,2,1,0:T(8,128)(2,1)S(1)}, u32[]{:S(2)}, u32[]{:S(2)}) collective-permute-start(bf16[2,2,256,128]{3,2,1,0:T(8,128)(2,1)S(1)} %interface_collect.2.refs_5_.refs_0_.refs_4_.refs_8_), channel_id=1, source_target_pairs={{0,2},{1,3},{2,0},{3,1},{4,6},{5,7},{6,4},{7,5},{8,10},{9,11},{10,... | collective-permute-start | bytes 786440 | tf_op jit(solution)/shard_map/ppermute | solution.py:45
  58.9 6.9 %collective-permute-start.25 = (bf16[2,2,256,128]{3,2,1,0:T(8,128)(2,1)S(1)}, bf16[2,2,256,128]{3,2,1,0:T(8,128)(2,1)S(1)}, u32[]{:S(2)}, u32[]{:S(2)}) collective-permute-start(bf16[2,2,256,128]{3,2,1,0:T(8,128)(2,1)S(1)} %interface_collect.2.refs_5_.refs_0_.refs_4_.refs_8_), channel_id=1, source_target_pairs={{0,4},{1,5},{2,6},{3,7},{4,0},{5,1},{6,2},{7,3},{8,12},{9,13},{10,... | collective-permute-start | bytes 786440 | tf_op jit(solution)/shard_map/ppermute | solution.py:45
  61.9 6.4 %collective-permute-start.28 = (bf16[2,2,256,128]{3,2,1,0:T(8,128)(2,1)S(1)}, bf16[2,2,256,128]{3,2,1,0:T(8,128)(2,1)S(1)}, u32[]{:S(2)}, u32[]{:S(2)}) collective-permute-start(bf16[2,2,256,128]{3,2,1,0:T(8,128)(2,1)S(1)} %interface_collect.3.refs_3_.refs_0_.refs_9_.refs_4_), channel_id=1, source_target_pairs={{0,2},{1,3},{2,0},{3,1},{4,6},{5,7},{6,4},{7,5},{8,10},{9,11},{10,... | collective-permute-start | bytes 786440 | tf_op jit(solution)/shard_map/ppermute | solution.py:45
  62.6 6.4 %collective-permute-start.29 = (bf16[2,2,256,128]{3,2,1,0:T(8,128)(2,1)S(1)}, bf16[2,2,256,128]{3,2,1,0:T(8,128)(2,1)S(1)}, u32[]{:S(2)}, u32[]{:S(2)}) collective-permute-start(bf16[2,2,256,128]{3,2,1,0:T(8,128)(2,1)S(1)} %interface_collect.3.refs_3_.refs_0_.refs_9_.refs_4_), channel_id=1, source_target_pairs={{0,4},{1,5},{2,6},{3,7},{4,0},{5,1},{6,2},{7,3},{8,12},{9,13},{10,... | collective-permute-start | bytes 786440 | tf_op jit(solution)/shard_map/ppermute | solution.py:45
  65.9 4.3 %collective-permute-start.32 = (bf16[3,2,2,256,128]{4,3,2,1,0:T(8,128)(2,1)S(1)}, bf16[3,2,2,256,128]{4,3,2,1,0:T(8,128)(2,1)S(1)}, u32[]{:S(2)}, u32[]{:S(2)}) collective-permute-start(bf16[3,2,2,256,128]{4,3,2,1,0:T(8,128)(2,1)S(1)} %get-tuple-element.75), channel_id=1, source_target_pairs={{0,1},{1,0},{2,3},{3,2},{4,5},{5,4},{6,7},{7,6},{8,9},{9,8},{10,11... | collective-permute-start | bytes 2359304 | tf_op jit(solution)/shard_map/ppermute | solution.py:45
  65.9 10.0 %collective-permute-start.26 = (bf16[1,2,256,128]{3,2,1,0:T(8,128)(2,1)S(1)}, bf16[1,2,256,128]{3,2,1,0:T(8,128)(2,1)S(1)}, u32[]{:S(2)}, u32[]{:S(2)}) collective-permute-start(bf16[1,2,256,128]{3,2,1,0:T(8,128)(2,1)S(1)} %get-tuple-element.71.refs_3_), channel_id=1, source_target_pairs={{0,4},{1,5},{2,6},{3,7},{4,0},{5,1},{6,2},{7,3},{8,12},{9,13},{10,... | collective-permute-start | bytes 393224 | tf_op jit(solution)/shard_map/ppermute | solution.py:45
  66.9 9.1 %collective-permute-start.27 = (bf16[1,2,256,128]{3,2,1,0:T(8,128)(2,1)S(1)}, bf16[1,2,256,128]{3,2,1,0:T(8,128)(2,1)S(1)}, u32[]{:S(2)}, u32[]{:S(2)}) collective-permute-start(bf16[1,2,256,128]{3,2,1,0:T(8,128)(2,1)S(1)} %get-tuple-element.72), channel_id=1, source_target_pairs={{0,2},{1,3},{2,0},{3,1},{4,6},{5,7},{6,4},{7,5},{8,10},{9,11},{10,... | collective-permute-start | bytes 393224 | tf_op jit(solution)/shard_map/ppermute | solution.py:45
  69.1 7.5 %collective-permute-start.34 = (bf16[3,2,2,256,128]{4,3,2,1,0:T(8,128)(2,1)S(1)}, bf16[3,2,2,256,128]{4,3,2,1,0:T(8,128)(2,1)S(1)}, u32[]{:S(2)}, u32[]{:S(2)}) collective-permute-start(bf16[3,2,2,256,128]{4,3,2,1,0:T(8,128)(2,1)S(1)} %get-tuple-element.77), channel_id=1, source_target_pairs={{0,1},{1,0},{2,3},{3,2},{4,5},{5,4},{6,7},{7,6},{8,9},{9,8},{10,11... | collective-permute-start | bytes 2359304 | tf_op jit(solution)/shard_map/ppermute | solution.py:45
  69.2 6.8 %collective-permute-start.30 = (bf16[1,2,256,128]{3,2,1,0:T(8,128)(2,1)S(1)}, bf16[1,2,256,128]{3,2,1,0:T(8,128)(2,1)S(1)}, u32[]{:S(2)}, u32[]{:S(2)}) collective-permute-start(bf16[1,2,256,128]{3,2,1,0:T(8,128)(2,1)S(1)} %get-tuple-element.73.refs_10_), channel_id=1, source_target_pairs={{0,4},{1,5},{2,6},{3,7},{4,0},{5,1},{6,2},{7,3},{8,12},{9,13},{10,... | collective-permute-start | bytes 393224 | tf_op jit(solution)/shard_map/ppermute | solution.py:45
  70.1 6.4 %collective-permute-start.31 = (bf16[1,2,256,128]{3,2,1,0:T(8,128)(2,1)S(1)}, bf16[1,2,256,128]{3,2,1,0:T(8,128)(2,1)S(1)}, u32[]{:S(2)}, u32[]{:S(2)}) collective-permute-start(bf16[1,2,256,128]{3,2,1,0:T(8,128)(2,1)S(1)} %get-tuple-element.74), channel_id=1, source_target_pairs={{0,2},{1,3},{2,0},{3,1},{4,6},{5,7},{6,4},{7,5},{8,10},{9,11},{10,... | collective-permute-start | bytes 393224 | tf_op jit(solution)/shard_map/ppermute | solution.py:45
  76.5 3.2 %collective-permute-start.33 = (bf16[4,2,256,128]{3,2,1,0:T(8,128)(2,1)S(1)}, bf16[4,2,256,128]{3,2,1,0:T(8,128)(2,1)S(1)}, u32[]{:S(2)}, u32[]{:S(2)}) collective-permute-start(bf16[4,2,256,128]{3,2,1,0:T(8,128)(2,1)S(1)} %interface_join.1.refs_4_), channel_id=1, source_target_pairs={{0,1},{1,0},{2,3},{3,2},{4,5},{5,4},{6,7},{7,6},{8,9},{9,8},{10,11... | collective-permute-start | bytes 1572872 | tf_op jit(solution)/shard_map/ppermute | solution.py:45

commit v10 on v9

--- a/solution.py
+++ b/solution.py
@@ -8,7 +8,7 @@
 from jax.sharding import PartitionSpec as P
 
 HALVES = 2
-FIRST_ROOM = 52
+FIRST_ROOM = 51
 BRIEF = ("solve_join", "interface_first", "interface_join", "interface_second_1", "interface_relay_0")
 BF = jnp.bfloat16
 F32 = jnp.float32
@@ -60,7 +60,7 @@
     return (ids == anc_row).astype(F32).astype(BF)
 
 
-def forward_kernel(h, group, cap, owners, place, rhs, inv, off, anc, keep, send, part, ids, seen, *rest):
+def forward_kernel(h, group, cap, owners, place, rhs, inv, off, anc, keep, send, last, part, ids, seen, *rest):
     leaves, blk, cols = rhs.shape[2], rhs.shape[3], part.shape[4]
     fronts, rows, width = part.shape[0], keep.shape[3], keep.shape[4]
     me = place[1]
@@ -116,11 +116,12 @@
     for dist in range(fronts):
         row = jnp.concatenate([ids[dist * cap + rank : dist * cap + rank + 1, :] for rank in range(cap)], axis=1)
         table = table_of(row, rows)
-        out = send if dist % 2 else keep
+        out = keep if dist % 2 == 0 else send if dist < fronts - 1 else last
+        spot = 0 if dist == fronts - 1 else dist // 2
         for plane in range(2):
             value = dot(table, part[dist, plane].reshape(cap * blk, cols)).astype(BF)
             for q in range(cols // width):
-                out[dist // 2, q, plane] = value[:, q * width : (q + 1) * width]
+                out[spot, q, plane] = value[:, q * width : (q + 1) * width]
 
 
 def forward(h, owners, place, leaf_rhs, leaf_inv, leaf_off, ancestors, fronts, rows, part, after):
@@ -128,7 +129,7 @@
     cols = width // HALVES
     cap = -(-leaves // fronts)
     group = 8
-    block = shape_of((fronts // 2, cols // part, 2, rows, part))
+    block = (cols // part, 2, rows, part)
     scratch = [
         pltpu.VMEM((fronts, 2, cap, blk, cols), BF),
         pltpu.VMEM((fronts * cap, blk), jnp.int32),
@@ -147,8 +148,8 @@
         "leaf_forward",
         [owners, place, leaf_rhs, leaf_inv, leaf_off, ancestors],
         [SMEM, SMEM] + [VMEM if h else HBM] * 4,
-        [block, block],
-        [VMEM, VMEM],
+        [shape_of((fronts // 2,) + block), shape_of((fronts // 2 - 1,) + block), shape_of((1,) + block)],
+        [VMEM, VMEM, VMEM],
         after,
         scratch,
         room=24 if h else FIRST_ROOM,
@@ -226,14 +227,16 @@
     )
 
 
-def first_kernel(names, keep, near, *outs):
+def first_kernel(names, keep, *refs):
+    nears, outs = refs[: -len(names)], refs[-len(names) :]
     for (j, first, last), out in zip(names, outs):
-        out[...] = (keep[j, first:last].astype(F32) + near[j, first:last].astype(F32)).astype(BF)
-
-
-def first_sums(names, keep, near, after):
-    return call(
-        functools.partial(first_kernel, names), "interface_first", [keep, near], [VMEM, VMEM],
+        near, at = (nears[-1], 0) if j == keep.shape[0] - 1 else (nears[0], j)
+        out[...] = (keep[j, first:last].astype(F32) + near[at, first:last].astype(F32)).astype(BF)
+
+
+def first_sums(names, keep, nears, after):
+    return call(
+        functools.partial(first_kernel, names), "interface_first", [keep, *nears], [VMEM] * (1 + len(nears)),
         [shape_of((last - first,) + keep.shape[2:]) for _, first, last in names], [VMEM] * len(names), after,
     )
 
@@ -487,22 +490,23 @@
     square = pairs == 4
 
     def start_forward(h, after):
-        keep, send = forward(
+        keep, send, last = forward(
             h, owners, place, leaf_rhs, leaf_inv, leaf_off, ancestors, fronts, rows, part, after
         )
-        return keep, crossed(send, "front", 1)
+        last = crossed(last, "front", 1)
+        return keep, (crossed(send, "front", 1), last)
 
     def send_first(keep, near, after):
         if not square:
             sums = first_sums([(j, 0, parts) for j in range(1, pairs)], keep, near, after)
             return sums[0], [crossed(value, "front", 2 * (j + 1)) for j, value in enumerate(sums)]
-        to_x, to_y = first_sums([(3, 0, parts // 2), (3, parts // 2, parts)], keep, near, after)
+        to_x, to_y = first_sums([(3, 0, parts // 2), (3, parts // 2, parts)], keep, near[1:], after)
         return to_x, [crossed(to_x, "front", 2), crossed(to_y, "front", 4)]
 
     def send_second(h, keep, near, got, after):
         if not square:
             return got[0], got
-        to_x, to_y = second_sums(h, parts // 2, keep, near, *got, after)
+        to_x, to_y = second_sums(h, parts // 2, keep, near[0], *got, after)
         return to_x, [crossed(to_x, "front", 2), crossed(to_y, "front", 4)]
 
     def over_slabs(values):
@@ -535,19 +539,19 @@
         return jobs
 
     keep0, near0 = start_forward(0, ())
-    token, got0 = send_first(keep0, near0, ())
-    keep1, near1 = start_forward(1, [token])
+    same, other = pack(place, root_inv, coupling, [keep0])
+    have, step = [same, crossed(other, "slab", 1)], 2
+    token, got0 = send_first(keep0, near0, [same])
+    keep1, near1 = start_forward(1, [token, have[1]])
     token, far0 = send_second(0, keep0, near0, got0, [keep1])
     token, got1 = send_first(keep1, near1, [token])
-    same, other = pack(place, root_inv, coupling, [token])
-    have, step = [same, crossed(other, "slab", 1)], 2
     while step < slabs:
         token = join(have, [token])
         have = have + [crossed(token, "slab", step)]
         step *= 2
     token, far1 = send_second(1, keep1, near1, got1, [token])
-    pieces0 = reduce(0, place, root_rhs, keep0, near0, far0, slabs, blk, [token])
-    pieces1 = reduce(1, place, root_rhs, keep1, near1, far1, slabs, blk, [pieces0[0]])
+    pieces0 = reduce(0, place, root_rhs, keep0, near0[0], far0, slabs, blk, [token])
+    pieces1 = reduce(1, place, root_rhs, keep1, near1[0], far1, slabs, blk, [pieces0[0]])
     solved0 = chain(place, over_slabs(pieces0), have, [pieces1[0]])
     solved1 = chain(place, over_slabs(pieces1), have, [solved0[0]])
     own0 = collect(place, over_slabs(solved0), rows, [solved1[0]])

time: 82.6 us -> 83.3 us (level)
  waiting for transfers between devices: 10.6 us -> 14.1 us
  starting transfers between devices: 44.1 us -> 42.4 us
  Pallas kernels: 25.3 us -> 24.2 us
    ppermute x35 -> x37, waiting for transfers between devices: 10.6 us -> 14.1 us  [crossed(): lax.ppermute(x, axis, [(i, i ^ mask) for i in range(lax.axis_size(axis))])]
    ppermute x35 -> x37, starting transfers between devices: 44.1 us -> 42.4 us  [crossed(): lax.ppermute(x, axis, [(i, i ^ mask) for i in range(lax.axis_size(axis))])]
    pallas_call x21, Pallas kernels: 25.3 us -> 24.2 us  [call(): pl.pallas_call(wrapped, in_specs=list(in_specs) + [ANY] * extra, out_spec...]
  transfers between devices with their start and end apart: 35 -> 37, of which waited for: 9 -> 9; matrix products, arithmetic and copies ran while one was open for 0% -> 0% of each run, Pallas kernels for 21% -> 21%
where the time goes in v10:
time: 83.3 us; the launch traced here: 83.1 us
  starting transfers between devices  42.4 us (51%)
  Pallas kernels  24.2 us (29%)
  waiting for transfers between devices  14.1 us (17%)
  local copies, waits for them, and re-layouts  1.38 us (2%)
  between operations  0.89 us (1%)
    ppermute x37, starting transfers between devices, crossed(): lax.ppermute(x, axis, [(i, i ^ mask) for i in range(lax.axis_size(axis))])  42.4 us
    pallas_call x21, Pallas kernels, call(): pl.pallas_call(wrapped, in_specs=list(in_specs) + [ANY] * extra, out_spec...  24.2 us
    ppermute x37, waiting for transfers between devices, crossed(): lax.ppermute(x, axis, [(i, i ^ mask) for i in range(lax.axis_size(axis))])  14.1 us
  transfers between devices with their start and end apart: 37, of which 9 were waited for; matrix products, arithmetic and copies ran while one was open for 0% of the time, Pallas kernels for 21%

profile of v10, /device:TPU:0, one launch (start us, length us, event | category | flops | bytes accessed | tf_op | source)
XLA Modules:
  0.0 83.1 jit_solution(8657265665790575543)
XLA Ops:
  0.7 0.7 copy-done.5
  1.4 0.7 copy-done.7
  2.1 4.4 %leaf_forward.2 = (bf16[4,2,2,256,128]{4,3,2,1,0:T(8,128)(2,1)S(1)}, bf16[3,2,2,256,128]{4,3,2,1,0:T(8,128)(2,1)S(1)}, bf16[1,2,2,256,128]{4,3,2,1,0:T(8,128)(2,1)S(1)}) custom-call(s32[16]{0:T(128)S(1)} %bitcast.5, s32[2]{0:T(128)S(1)} %pad_add_fusion.refs_1_.refs_0_, bf16[1,2,16,128,512]{4,3,2,1,0:T(8,128)(2,1)} %refs_2_.11, ...), custom_call_target="tpu_custom_call" | custom-call | flops 10000000000 | bytes 1 | tf_op jit(solution)/shard_map/leaf_forward/pallas_call | solution.py:31
  7.0 0.6 solve_pack.1
  7.5 2.7 %collective-permute-start.1 = (bf16[272,128]{1,0:T(8,128)(2,1)S(1)}, bf16[272,128]{1,0:T(8,128)(2,1)S(1)}, u32[]{:S(2)}, u32[]{:S(2)}) collective-permute-start(bf16[272,128]{1,0:T(8,128)(2,1)S(1)} %get-tuple-element.47), channel_id=1, source_target_pairs={{0,8},{8,0},{16,24},{24,16},{1,9},{9,1},{17,25},{25,17},{2,10},{10... | collective-permute-start | bytes 208904 | tf_op jit(solution)/shard_map/ppermute | solution.py:45
  10.5 1.6 %collective-permute-start.5 = (bf16[1,2,256,128]{3,2,1,0:T(8,128)(2,1)S(1)}, bf16[1,2,256,128]{3,2,1,0:T(8,128)(2,1)S(1)}, u32[]{:S(2)}, u32[]{:S(2)}) collective-permute-start(bf16[1,2,256,128]{3,2,1,0:T(8,128)(2,1)S(1)} %get-tuple-element.46.refs_6_), channel_id=1, source_target_pairs={{0,2},{1,3},{2,0},{3,1},{4,6},{5,7},{6,4},{7,5},{8,10},{9,11},{10,... | collective-permute-start | bytes 393224 | tf_op jit(solution)/shard_map/ppermute | solution.py:45
  12.0 1.5 %collective-permute-start.6 = (bf16[1,2,256,128]{3,2,1,0:T(8,128)(2,1)S(1)}, bf16[1,2,256,128]{3,2,1,0:T(8,128)(2,1)S(1)}, u32[]{:S(2)}, u32[]{:S(2)}) collective-permute-start(bf16[1,2,256,128]{3,2,1,0:T(8,128)(2,1)S(1)} %get-tuple-element.52), channel_id=1, source_target_pairs={{0,4},{1,5},{2,6},{3,7},{4,0},{5,1},{6,2},{7,3},{8,12},{9,13},{10,... | collective-permute-start | bytes 393224 | tf_op jit(solution)/shard_map/ppermute | solution.py:45
  13.6 2.6 %leaf_forward.3 = (bf16[4,2,2,256,128]{4,3,2,1,0:T(8,128)(2,1)S(1)}, bf16[3,2,2,256,128]{4,3,2,1,0:T(8,128)(2,1)S(1)}, bf16[1,2,2,256,128]{4,3,2,1,0:T(8,128)(2,1)S(1)}) custom-call(s32[16]{0:T(128)S(1)} %bitcast.6, s32[2]{0:T(128)S(1)} %pad_add_fusion.refs_1_.refs_0_, bf16[1,2,16,128,512]{4,3,2,1,0:T(8,128)(2,1)S(1)} %copy-done, ...), custom_call_target="tpu_custom_call" | custom-call | flops 10000000000 | bytes 1 | tf_op jit(solution)/shard_map/leaf_forward/pallas_call | solution.py:31
  16.8 0.7 collective-permute-done.6.refs_3_
  17.7 0.6 collective-permute-start.11
  18.3 1.5 %collective-permute-start.12 = (bf16[2,2,256,128]{3,2,1,0:T(8,128)(2,1)S(1)}, bf16[2,2,256,128]{3,2,1,0:T(8,128)(2,1)S(1)}, u32[]{:S(2)}, u32[]{:S(2)}) collective-permute-start(bf16[2,2,256,128]{3,2,1,0:T(8,128)(2,1)S(1)} %get-tuple-element.58), channel_id=1, source_target_pairs={{0,4},{1,5},{2,6},{3,7},{4,0},{5,1},{6,2},{7,3},{8,12},{9,13},{10,... | collective-permute-start | bytes 786440 | tf_op jit(solution)/shard_map/ppermute | solution.py:45
  19.9 1.6 %collective-permute-start.7 = (bf16[1,2,256,128]{3,2,1,0:T(8,128)(2,1)S(1)}, bf16[1,2,256,128]{3,2,1,0:T(8,128)(2,1)S(1)}, u32[]{:S(2)}, u32[]{:S(2)}) collective-permute-start(bf16[1,2,256,128]{3,2,1,0:T(8,128)(2,1)S(1)} %get-tuple-element.54.refs_2_), channel_id=1, source_target_pairs={{0,2},{1,3},{2,0},{3,1},{4,6},{5,7},{6,4},{7,5},{8,10},{9,11},{10,... | collective-permute-start | bytes 393224 | tf_op jit(solution)/shard_map/ppermute | solution.py:45
  21.9 6.2 %collective-permute-done.7.refs_2_ = bf16[1,2,256,128]{3,2,1,0:T(8,128)(2,1)S(1)} collective-permute-done((bf16[1,2,256,128]{3,2,1,0:T(8,128)(2,1)S(1)}, bf16[1,2,256,128]{3,2,1,0:T(8,128)(2,1)S(1)}, u32[]{:S(2)}, u32[]{:S(2)}) %collective-permute-start.7) | collective-permute-done | bytes 131104 | tf_op jit(solution)/shard_map/ppermute | solution.py:45
  28.2 2.6 %collective-permute-start.16 = (bf16[544,128]{1,0:T(8,128)(2,1)S(1)}, bf16[544,128]{1,0:T(8,128)(2,1)S(1)}, u32[]{:S(2)}, u32[]{:S(2)}) collective-permute-start(bf16[544,128]{1,0:T(8,128)(2,1)S(1)} %solve_join.1.refs_4_), channel_id=1, source_target_pairs={{0,16},{8,24},{16,0},{24,8},{1,17},{9,25},{17,1},{25,9},{2,18},{10... | collective-permute-start | bytes 417800 | tf_op jit(solution)/shard_map/ppermute | solution.py:45
  30.9 1.4 %collective-permute-start.10 = (bf16[2,2,256,128]{3,2,1,0:T(8,128)(2,1)S(1)}, bf16[2,2,256,128]{3,2,1,0:T(8,128)(2,1)S(1)}, u32[]{:S(2)}, u32[]{:S(2)}) collective-permute-start(bf16[2,2,256,128]{3,2,1,0:T(8,128)(2,1)S(1)} %get-tuple-element.57), channel_id=1, source_target_pairs={{0,4},{1,5},{2,6},{3,7},{4,0},{5,1},{6,2},{7,3},{8,12},{9,13},{10,... | collective-permute-start | bytes 786440 | tf_op jit(solution)/shard_map/ppermute | solution.py:45
  32.3 1.3 %collective-permute-start.9 = (bf16[2,2,256,128]{3,2,1,0:T(8,128)(2,1)S(1)}, bf16[2,2,256,128]{3,2,1,0:T(8,128)(2,1)S(1)}, u32[]{:S(2)}, u32[]{:S(2)}) collective-permute-start(bf16[2,2,256,128]{3,2,1,0:T(8,128)(2,1)S(1)} %get-tuple-element.56.refs_6_), channel_id=1, source_target_pairs={{0,2},{1,3},{2,0},{3,1},{4,6},{5,7},{6,4},{7,5},{8,10},{9,11},{10,... | collective-permute-start | bytes 786440 | tf_op jit(solution)/shard_map/ppermute | solution.py:45
  33.7 0.7 interface_reduce.2
  34.4 1.6 %collective-permute-start.17 = (bf16[2,128,128]{2,1,0:T(8,128)(2,1)S(1)}, bf16[2,128,128]{2,1,0:T(8,128)(2,1)S(1)}, u32[]{:S(2)}, u32[]{:S(2)}) collective-permute-start(bf16[2,128,128]{2,1,0:T(8,128)(2,1)S(1)} %get-tuple-element.64), channel_id=1, source_target_pairs={{0,8},{8,0},{16,24},{24,16},{1,9},{9,1},{17,25},{25,17},{2,10},{10... | collective-permute-start | bytes 196616 | tf_op jit(solution)/shard_map/ppermute | solution.py:45
  36.4 1.1 %collective-permute-done.10.refs_5_ = bf16[2,2,256,128]{3,2,1,0:T(8,128)(2,1)S(1)} collective-permute-done((bf16[2,2,256,128]{3,2,1,0:T(8,128)(2,1)S(1)}, bf16[2,2,256,128]{3,2,1,0:T(8,128)(2,1)S(1)}, u32[]{:S(2)}, u32[]{:S(2)}) %collective-permute-start.10) | collective-permute-done | bytes 262176 | tf_op jit(solution)/shard_map/ppermute | solution.py:45
  37.4 2.6 %collective-permute-start.19 = (bf16[2,128,128]{2,1,0:T(8,128)(2,1)S(1)}, bf16[2,128,128]{2,1,0:T(8,128)(2,1)S(1)}, u32[]{:S(2)}, u32[]{:S(2)}) collective-permute-start(bf16[2,128,128]{2,1,0:T(8,128)(2,1)S(1)} %get-tuple-element.66), channel_id=1, source_target_pairs={{0,24},{8,16},{16,8},{24,0},{1,25},{9,17},{17,9},{25,1},{2,26},{10... | collective-permute-start | bytes 196616 | tf_op jit(solution)/shard_map/ppermute | solution.py:45
  40.0 0.7 interface_reduce.3
  40.7 0.7 collective-permute-start.13
  41.4 1.2 %collective-permute-start.14 = (bf16[2,128,128]{2,1,0:T(8,128)(2,1)S(1)}, bf16[2,128,128]{2,1,0:T(8,128)(2,1)S(1)}, u32[]{:S(2)}, u32[]{:S(2)}) collective-permute-start(bf16[2,128,128]{2,1,0:T(8,128)(2,1)S(1)} %get-tuple-element.62), channel_id=1, source_target_pairs={{0,16},{8,24},{16,0},{24,8},{1,17},{9,25},{17,1},{25,9},{2,18},{10... | collective-permute-start | bytes 196616 | tf_op jit(solution)/shard_map/ppermute | solution.py:45
  42.6 2.6 %collective-permute-start.15 = (bf16[2,128,128]{2,1,0:T(8,128)(2,1)S(1)}, bf16[2,128,128]{2,1,0:T(8,128)(2,1)S(1)}, u32[]{:S(2)}, u32[]{:S(2)}) collective-permute-start(bf16[2,128,128]{2,1,0:T(8,128)(2,1)S(1)} %get-tuple-element.63), channel_id=1, source_target_pairs={{0,24},{8,16},{16,8},{24,0},{1,25},{9,17},{17,9},{25,1},{2,26},{10... | collective-permute-start | bytes 196616 | tf_op jit(solution)/shard_map/ppermute | solution.py:45
  45.2 1.5 %sweep_chain.2 = (bf16[2,128,128]{2,1,0:T(8,128)(2,1)S(1)}, bf16[2,128,128]{2,1,0:T(8,128)(2,1)S(1)}, bf16[2,128,128]{2,1,0:T(8,128)(2,1)S(1)}, bf16[2,128,128]{2,1,0:T(8,128)(2,1)S(1)}) custom-call(s32[2]{0:T(128)S(1)} %pad_add_fusion.refs_1_.refs_0_, bf16[2,128,128]{2,1,0:T(8,128)(2,1)S(1)} %get-tuple-element.59.refs_6_.refs_1_, ...), custom_call_target="tpu_custom_call" | custom-call | flops 10000000000 | bytes 1 | tf_op jit(solution)/shard_map/sweep_chain/pallas_call | solution.py:31
  46.7 1.3 %collective-permute-start.23 = (bf16[2,128,128]{2,1,0:T(8,128)(2,1)S(1)}, bf16[2,128,128]{2,1,0:T(8,128)(2,1)S(1)}, u32[]{:S(2)}, u32[]{:S(2)}) collective-permute-start(bf16[2,128,128]{2,1,0:T(8,128)(2,1)S(1)} %get-tuple-element.72), channel_id=1, source_target_pairs={{0,8},{8,0},{16,24},{24,16},{1,9},{9,1},{17,25},{25,17},{2,10},{10... | collective-permute-start | bytes 196616 | tf_op jit(solution)/shard_map/ppermute | solution.py:45
  48.0 0.6 collective-permute-start.24
  48.6 2.6 %collective-permute-start.25 = (bf16[2,128,128]{2,1,0:T(8,128)(2,1)S(1)}, bf16[2,128,128]{2,1,0:T(8,128)(2,1)S(1)}, u32[]{:S(2)}, u32[]{:S(2)}) collective-permute-start(bf16[2,128,128]{2,1,0:T(8,128)(2,1)S(1)} %get-tuple-element.74), channel_id=1, source_target_pairs={{0,24},{8,16},{16,8},{24,0},{1,25},{9,17},{17,9},{25,1},{2,26},{10... | collective-permute-start | bytes 196616 | tf_op jit(solution)/shard_map/ppermute | solution.py:45
  51.1 1.5 %sweep_chain.3 = (bf16[2,128,128]{2,1,0:T(8,128)(2,1)S(1)}, bf16[2,128,128]{2,1,0:T(8,128)(2,1)S(1)}, bf16[2,128,128]{2,1,0:T(8,128)(2,1)S(1)}, bf16[2,128,128]{2,1,0:T(8,128)(2,1)S(1)}) custom-call(s32[2]{0:T(128)S(1)} %pad_add_fusion.refs_1_.refs_0_, bf16[2,128,128]{2,1,0:T(8,128)(2,1)S(1)} %get-tuple-element.60.refs_8_.refs_1_, ...), custom_call_target="tpu_custom_call" | custom-call | flops 10000000000 | bytes 1 | tf_op jit(solution)/shard_map/sweep_chain/pallas_call | solution.py:31
  52.6 1.1 %collective-permute-start.20 = (bf16[2,128,128]{2,1,0:T(8,128)(2,1)S(1)}, bf16[2,128,128]{2,1,0:T(8,128)(2,1)S(1)}, u32[]{:S(2)}, u32[]{:S(2)}) collective-permute-start(bf16[2,128,128]{2,1,0:T(8,128)(2,1)S(1)} %get-tuple-element.69), channel_id=1, source_target_pairs={{0,8},{8,0},{16,24},{24,16},{1,9},{9,1},{17,25},{25,17},{2,10},{10... | collective-permute-start | bytes 196616 | tf_op jit(solution)/shard_map/ppermute | solution.py:45
  53.7 0.8 %collective-permute-start.21 = (bf16[2,128,128]{2,1,0:T(8,128)(2,1)S(1)}, bf16[2,128,128]{2,1,0:T(8,128)(2,1)S(1)}, u32[]{:S(2)}, u32[]{:S(2)}) collective-permute-start(bf16[2,128,128]{2,1,0:T(8,128)(2,1)S(1)} %get-tuple-element.70), channel_id=1, source_target_pairs={{0,16},{8,24},{16,0},{24,8},{1,17},{9,25},{17,1},{25,9},{2,18},{10... | collective-permute-start | bytes 196616 | tf_op jit(solution)/shard_map/ppermute | solution.py:45
  54.5 2.6 %collective-permute-start.22 = (bf16[2,128,128]{2,1,0:T(8,128)(2,1)S(1)}, bf16[2,128,128]{2,1,0:T(8,128)(2,1)S(1)}, u32[]{:S(2)}, u32[]{:S(2)}) collective-permute-start(bf16[2,128,128]{2,1,0:T(8,128)(2,1)S(1)} %get-tuple-element.71), channel_id=1, source_target_pairs={{0,24},{8,16},{16,8},{24,0},{1,25},{9,17},{17,9},{25,1},{2,26},{10... | collective-permute-start | bytes 196616 | tf_op jit(solution)/shard_map/ppermute | solution.py:45
  57.1 0.6 interface_collect.2.refs_5_.refs_0_.refs_4_.refs_8_
  57.6 1.6 %collective-permute-start.26 = (bf16[2,2,256,128]{3,2,1,0:T(8,128)(2,1)S(1)}, bf16[2,2,256,128]{3,2,1,0:T(8,128)(2,1)S(1)}, u32[]{:S(2)}, u32[]{:S(2)}) collective-permute-start(bf16[2,2,256,128]{3,2,1,0:T(8,128)(2,1)S(1)} %interface_collect.2.refs_5_.refs_0_.refs_4_.refs_8_), channel_id=1, source_target_pairs={{0,2},{1,3},{2,0},{3,1},{4,6},{5,7},{6,4},{7,5},{8,10},{9,11},{10,... | collective-permute-start | bytes 786440 | tf_op jit(solution)/shard_map/ppermute | solution.py:45
  59.2 0.7 collective-permute-start.27
  60.0 0.7 collective-permute-done.22.refs_4_
  60.7 0.6 interface_collect.3.refs_3_.refs_0_.refs_9_.refs_4_
  61.3 1.8 %collective-permute-start.30 = (bf16[2,2,256,128]{3,2,1,0:T(8,128)(2,1)S(1)}, bf16[2,2,256,128]{3,2,1,0:T(8,128)(2,1)S(1)}, u32[]{:S(2)}, u32[]{:S(2)}) collective-permute-start(bf16[2,2,256,128]{3,2,1,0:T(8,128)(2,1)S(1)} %interface_collect.3.refs_3_.refs_0_.refs_9_.refs_4_), channel_id=1, source_target_pairs={{0,2},{1,3},{2,0},{3,1},{4,6},{5,7},{6,4},{7,5},{8,10},{9,11},{10,... | collective-permute-start | bytes 786440 | tf_op jit(solution)/shard_map/ppermute | solution.py:45
  63.1 1.4 %collective-permute-start.31 = (bf16[2,2,256,128]{3,2,1,0:T(8,128)(2,1)S(1)}, bf16[2,2,256,128]{3,2,1,0:T(8,128)(2,1)S(1)}, u32[]{:S(2)}, u32[]{:S(2)}) collective-permute-start(bf16[2,2,256,128]{3,2,1,0:T(8,128)(2,1)S(1)} %interface_collect.3.refs_3_.refs_0_.refs_9_.refs_4_), channel_id=1, source_target_pairs={{0,4},{1,5},{2,6},{3,7},{4,0},{5,1},{6,2},{7,3},{8,12},{9,13},{10,... | collective-permute-start | bytes 786440 | tf_op jit(solution)/shard_map/ppermute | solution.py:45
  64.5 1.5 %leaf_fold.1.refs_3_ = bf16[16,256,768]{2,1,0:T(8,128)(2,1)S(1)} custom-call(bf16[1,16,2,128,128]{4,3,2,1,0:T(8,128)(2,1)S(1)} %copy-done.1, bf16[1,16,2,128,128]{4,3,2,1,0:T(8,128)(2,1)S(1)} %copy-done.2, s32[1,16,128]{2,1,0:T(8,128)S(1)} %copy-done.5, bf16[2,2,256,128]{3,2,1,0:T(8,128)(2,1)S(1)} %interface_collect.3.refs_3_.refs_0_.refs_9_.refs_4_), custom_call_target="tpu_custom_call" | custom-call | flops 10000000000 | bytes 1 | tf_op jit(solution)/shard_map/leaf_fold/pallas_call | solution.py:31
  66.0 0.8 collective-permute-done.26.refs_1_.refs_6_
  66.8 1.5 %collective-permute-done.27.refs_2_.refs_7_ = bf16[2,2,256,128]{3,2,1,0:T(8,128)(2,1)S(1)} collective-permute-done((bf16[2,2,256,128]{3,2,1,0:T(8,128)(2,1)S(1)}, bf16[2,2,256,128]{3,2,1,0:T(8,128)(2,1)S(1)}, u32[]{:S(2)}, u32[]{:S(2)}) %collective-permute-start.27) | collective-permute-done | bytes 262176 | tf_op jit(solution)/shard_map/ppermute | solution.py:45
  69.6 1.5 %collective-permute-done.31.refs_2_.refs_7_ = bf16[2,2,256,128]{3,2,1,0:T(8,128)(2,1)S(1)} collective-permute-done((bf16[2,2,256,128]{3,2,1,0:T(8,128)(2,1)S(1)}, bf16[2,2,256,128]{3,2,1,0:T(8,128)(2,1)S(1)}, u32[]{:S(2)}, u32[]{:S(2)}) %collective-permute-start.31) | collective-permute-done | bytes 262176 | tf_op jit(solution)/shard_map/ppermute | solution.py:45
  71.6 1.2 %collective-permute-start.33 = (bf16[1,2,256,128]{3,2,1,0:T(8,128)(2,1)S(1)}, bf16[1,2,256,128]{3,2,1,0:T(8,128)(2,1)S(1)}, u32[]{:S(2)}, u32[]{:S(2)}) collective-permute-start(bf16[1,2,256,128]{3,2,1,0:T(8,128)(2,1)S(1)} %get-tuple-element.78), channel_id=1, source_target_pairs={{0,2},{1,3},{2,0},{3,1},{4,6},{5,7},{6,4},{7,5},{8,10},{9,11},{10,... | collective-permute-start | bytes 393224 | tf_op jit(solution)/shard_map/ppermute | solution.py:45
  72.8 3.2 %leaf_backward.3 = (bf16[1,2,16,128,512]{4,3,2,1,0:T(8,128)(2,1)}, f32[1,2,256,512]{3,2,1,0:T(8,128)}, f32[8,128]{1,0:T(8,128)S(1)}) custom-call(s32[16]{0:T(128)S(1)} %bitcast.7, s32[2]{0:T(128)S(1)} %pad_add_fusion.refs_1_.refs_0_, bf16[1,2,16,128,512]{4,3,2,1,0:T(8,128)(2,1)S(1)} %copy-done, bf16[16,256,768]{2,1,0:T(8,128)(2,1)S(1)} %leaf_fold.1.refs_3_, ...), custom_call_target="tpu_custom_call" | custom-call | flops 10000000000 | bytes 1 | tf_op jit(solution)/shard_map/leaf_backward/pallas_call | solution.py:31
  76.0 1.1 %collective-permute-done.32.refs_2_ = bf16[1,2,256,128]{3,2,1,0:T(8,128)(2,1)S(1)} collective-permute-done((bf16[1,2,256,128]{3,2,1,0:T(8,128)(2,1)S(1)}, bf16[1,2,256,128]{3,2,1,0:T(8,128)(2,1)S(1)}, u32[]{:S(2)}, u32[]{:S(2)}) %collective-permute-start.32) | collective-permute-done | bytes 131104 | tf_op jit(solution)/shard_map/ppermute | solution.py:45
  77.3 3.1 %leaf_backward.4.refs_6_ = bf16[1,2,16,128,512]{4,3,2,1,0:T(8,128)(2,1)} custom-call(s32[16]{0:T(128)S(1)} %bitcast.8, s32[2]{0:T(128)S(1)} %pad_add_fusion.refs_1_.refs_0_, bf16[1,2,16,128,512]{4,3,2,1,0:T(8,128)(2,1)S(1)} %copy-done, bf16[16,256,768]{2,1,0:T(8,128)(2,1)S(1)} %leaf_fold.1.refs_3_, ...), custom_call_target="tpu_custom_call", output_to_operand_aliasing={{}: (8, {})} | custom-call | flops 10000000000 | bytes 1 | tf_op jit(solution)/shard_map/leaf_backward/pallas_call | solution.py:31
  80.4 2.6 %leaf_backward.5 = bf16[1,2,16,128,512]{4,3,2,1,0:T(8,128)(2,1)} custom-call(s32[16]{0:T(128)S(1)} %bitcast.9, s32[2]{0:T(128)S(1)} %pad_add_fusion.refs_1_.refs_0_, bf16[1,2,16,128,512]{4,3,2,1,0:T(8,128)(2,1)S(1)} %copy-done, bf16[16,256,768]{2,1,0:T(8,128)(2,1)S(1)} %leaf_fold.1.refs_3_, ...), custom_call_target="tpu_custom_call", output_to_operand_aliasing={{}: (6, {})} | custom-call | flops 10000000000 | bytes 1 | tf_op jit(solution)/shard_map/leaf_backward/pallas_call | solution.py:31
  (64 shorter events, 4.7 us)
Async XLA Ops:
  0.7 0.7 copy-start.5
  1.4 0.7 copy-start.7
  2.1 4.9 %copy-start.4 = (f32[1,2,2,128,128]{4,3,2,1,0:T(8,128)S(1)}, f32[1,2,2,128,128]{4,3,2,1,0:T(8,128)}, u32[]{:S(2)}) copy-start(f32[1,2,2,128,128]{4,3,2,1,0:T(8,128)} %refs_1_.4) | copy-start | bytes 786436
  2.1 4.9 %copy-start.6 = (f32[1,256]{1,0:T(1,128)S(1)}, f32[1,256]{1,0:T(1,128)}, u32[]{:S(2)}) copy-start(f32[1,256]{1,0:T(1,128)} %param.15) | copy-start | bytes 3076
  6.4 4.0 %collective-permute-start = (bf16[1,2,2,256,128]{4,3,2,1,0:T(8,128)(2,1)S(1)}, bf16[1,2,2,256,128]{4,3,2,1,0:T(8,128)(2,1)S(1)}, u32[]{:S(2)}, u32[]{:S(2)}) collective-permute-start(bf16[1,2,2,256,128]{4,3,2,1,0:T(8,128)(2,1)S(1)} %get-tuple-element.44), channel_id=1, source_target_pairs={{0,1},{1,0},{2,3},{3,2},{4,5},{5,4},{6,7},{7,6},{8,9},{9,8},{10,11... | collective-permute-start | bytes 786440 | tf_op jit(solution)/shard_map/ppermute | solution.py:45
  6.9 6.6 %copy-start = (bf16[1,2,16,128,512]{4,3,2,1,0:T(8,128)(2,1)S(1)}, bf16[1,2,16,128,512]{4,3,2,1,0:T(8,128)(2,1)}, u32[]{:S(2)}) copy-start(bf16[1,2,16,128,512]{4,3,2,1,0:T(8,128)(2,1)} %refs_2_.11) | copy-start | bytes 12582916
  7.0 6.6 %copy-start.1 = (bf16[1,16,2,128,128]{4,3,2,1,0:T(8,128)(2,1)S(1)}, bf16[1,16,2,128,128]{4,3,2,1,0:T(8,128)(2,1)}, u32[]{:S(2)}) copy-start(bf16[1,16,2,128,128]{4,3,2,1,0:T(8,128)(2,1)} %refs_0_.1) | copy-start | bytes 3145732
  7.0 6.6 %copy-start.2 = (bf16[1,16,2,128,128]{4,3,2,1,0:T(8,128)(2,1)S(1)}, bf16[1,16,2,128,128]{4,3,2,1,0:T(8,128)(2,1)}, u32[]{:S(2)}) copy-start(bf16[1,16,2,128,128]{4,3,2,1,0:T(8,128)(2,1)} %refs_1_.7) | copy-start | bytes 3145732
  7.5 6.0 %collective-permute-start.1 = (bf16[272,128]{1,0:T(8,128)(2,1)S(1)}, bf16[272,128]{1,0:T(8,128)(2,1)S(1)}, u32[]{:S(2)}, u32[]{:S(2)}) collective-permute-start(bf16[272,128]{1,0:T(8,128)(2,1)S(1)} %get-tuple-element.47), channel_id=1, source_target_pairs={{0,8},{8,0},{16,24},{24,16},{1,9},{9,1},{17,25},{25,17},{2,10},{10... | collective-permute-start | bytes 208904 | tf_op jit(solution)/shard_map/ppermute | solution.py:45
  10.2 7.3 %collective-permute-start.4 = (bf16[3,2,2,256,128]{4,3,2,1,0:T(8,128)(2,1)S(1)}, bf16[3,2,2,256,128]{4,3,2,1,0:T(8,128)(2,1)S(1)}, u32[]{:S(2)}, u32[]{:S(2)}) collective-permute-start(bf16[3,2,2,256,128]{4,3,2,1,0:T(8,128)(2,1)S(1)} %get-tuple-element.51), channel_id=1, source_target_pairs={{0,1},{1,0},{2,3},{3,2},{4,5},{5,4},{6,7},{7,6},{8,9},{9,8},{10,11... | collective-permute-start | bytes 2359304 | tf_op jit(solution)/shard_map/ppermute | solution.py:45
  10.5 6.3 %collective-permute-start.5 = (bf16[1,2,256,128]{3,2,1,0:T(8,128)(2,1)S(1)}, bf16[1,2,256,128]{3,2,1,0:T(8,128)(2,1)S(1)}, u32[]{:S(2)}, u32[]{:S(2)}) collective-permute-start(bf16[1,2,256,128]{3,2,1,0:T(8,128)(2,1)S(1)} %get-tuple-element.46.refs_6_), channel_id=1, source_target_pairs={{0,2},{1,3},{2,0},{3,1},{4,6},{5,7},{6,4},{7,5},{8,10},{9,11},{10,... | collective-permute-start | bytes 393224 | tf_op jit(solution)/shard_map/ppermute | solution.py:45
  12.0 5.4 %collective-permute-start.6 = (bf16[1,2,256,128]{3,2,1,0:T(8,128)(2,1)S(1)}, bf16[1,2,256,128]{3,2,1,0:T(8,128)(2,1)S(1)}, u32[]{:S(2)}, u32[]{:S(2)}) collective-permute-start(bf16[1,2,256,128]{3,2,1,0:T(8,128)(2,1)S(1)} %get-tuple-element.52), channel_id=1, source_target_pairs={{0,4},{1,5},{2,6},{3,7},{4,0},{5,1},{6,2},{7,3},{8,12},{9,13},{10,... | collective-permute-start | bytes 393224 | tf_op jit(solution)/shard_map/ppermute | solution.py:45
  16.2 3.6 %collective-permute-start.3 = (bf16[1,2,2,256,128]{4,3,2,1,0:T(8,128)(2,1)S(1)}, bf16[1,2,2,256,128]{4,3,2,1,0:T(8,128)(2,1)S(1)}, u32[]{:S(2)}, u32[]{:S(2)}) collective-permute-start(bf16[1,2,2,256,128]{4,3,2,1,0:T(8,128)(2,1)S(1)} %get-tuple-element.50), channel_id=1, source_target_pairs={{0,1},{1,0},{2,3},{3,2},{4,5},{5,4},{6,7},{7,6},{8,9},{9,8},{10,11... | collective-permute-start | bytes 786440 | tf_op jit(solution)/shard_map/ppermute | solution.py:45
  16.3 14.5 %collective-permute-start.2 = (bf16[3,2,2,256,128]{4,3,2,1,0:T(8,128)(2,1)S(1)}, bf16[3,2,2,256,128]{4,3,2,1,0:T(8,128)(2,1)S(1)}, u32[]{:S(2)}, u32[]{:S(2)}) collective-permute-start(bf16[3,2,2,256,128]{4,3,2,1,0:T(8,128)(2,1)S(1)} %get-tuple-element.49), channel_id=1, source_target_pairs={{0,1},{1,0},{2,3},{3,2},{4,5},{5,4},{6,7},{7,6},{8,9},{9,8},{10,11... | collective-permute-start | bytes 2359304 | tf_op jit(solution)/shard_map/ppermute | solution.py:45
  17.7 16.0 %copy-start.3 = (bf16[1,2,256,512]{3,2,1,0:T(8,128)(2,1)S(1)}, bf16[1,2,256,512]{3,2,1,0:T(8,128)(2,1)}, u32[]{:S(2)}) copy-start(bf16[1,2,256,512]{3,2,1,0:T(8,128)(2,1)} %refs_1_.6) | copy-start | bytes 1572868
  17.7 16.0 %collective-permute-start.11 = (bf16[2,2,256,128]{3,2,1,0:T(8,128)(2,1)S(1)}, bf16[2,2,256,128]{3,2,1,0:T(8,128)(2,1)S(1)}, u32[]{:S(2)}, u32[]{:S(2)}) collective-permute-start(bf16[2,2,256,128]{3,2,1,0:T(8,128)(2,1)S(1)} %get-tuple-element.53.refs_2_), channel_id=1, source_target_pairs={{0,2},{1,3},{2,0},{3,1},{4,6},{5,7},{6,4},{7,5},{8,10},{9,11},{10,... | collective-permute-start | bytes 786440 | tf_op jit(solution)/shard_map/ppermute | solution.py:45
  18.3 15.4 %collective-permute-start.12 = (bf16[2,2,256,128]{3,2,1,0:T(8,128)(2,1)S(1)}, bf16[2,2,256,128]{3,2,1,0:T(8,128)(2,1)S(1)}, u32[]{:S(2)}, u32[]{:S(2)}) collective-permute-start(bf16[2,2,256,128]{3,2,1,0:T(8,128)(2,1)S(1)} %get-tuple-element.58), channel_id=1, source_target_pairs={{0,4},{1,5},{2,6},{3,7},{4,0},{5,1},{6,2},{7,3},{8,12},{9,13},{10,... | collective-permute-start | bytes 786440 | tf_op jit(solution)/shard_map/ppermute | solution.py:45
  19.9 8.3 %collective-permute-start.7 = (bf16[1,2,256,128]{3,2,1,0:T(8,128)(2,1)S(1)}, bf16[1,2,256,128]{3,2,1,0:T(8,128)(2,1)S(1)}, u32[]{:S(2)}, u32[]{:S(2)}) collective-permute-start(bf16[1,2,256,128]{3,2,1,0:T(8,128)(2,1)S(1)} %get-tuple-element.54.refs_2_), channel_id=1, source_target_pairs={{0,2},{1,3},{2,0},{3,1},{4,6},{5,7},{6,4},{7,5},{8,10},{9,11},{10,... | collective-permute-start | bytes 393224 | tf_op jit(solution)/shard_map/ppermute | solution.py:45
  21.4 9.3 %collective-permute-start.8 = (bf16[1,2,256,128]{3,2,1,0:T(8,128)(2,1)S(1)}, bf16[1,2,256,128]{3,2,1,0:T(8,128)(2,1)S(1)}, u32[]{:S(2)}, u32[]{:S(2)}) collective-permute-start(bf16[1,2,256,128]{3,2,1,0:T(8,128)(2,1)S(1)} %get-tuple-element.55), channel_id=1, source_target_pairs={{0,4},{1,5},{2,6},{3,7},{4,0},{5,1},{6,2},{7,3},{8,12},{9,13},{10,... | collective-permute-start | bytes 393224 | tf_op jit(solution)/shard_map/ppermute | solution.py:45
  28.2 13.2 %collective-permute-start.16 = (bf16[544,128]{1,0:T(8,128)(2,1)S(1)}, bf16[544,128]{1,0:T(8,128)(2,1)S(1)}, u32[]{:S(2)}, u32[]{:S(2)}) collective-permute-start(bf16[544,128]{1,0:T(8,128)(2,1)S(1)} %solve_join.1.refs_4_), channel_id=1, source_target_pairs={{0,16},{8,24},{16,0},{24,8},{1,17},{9,25},{17,1},{25,9},{2,18},{10... | collective-permute-start | bytes 417800 | tf_op jit(solution)/shard_map/ppermute | solution.py:45
  30.9 6.5 %collective-permute-start.10 = (bf16[2,2,256,128]{3,2,1,0:T(8,128)(2,1)S(1)}, bf16[2,2,256,128]{3,2,1,0:T(8,128)(2,1)S(1)}, u32[]{:S(2)}, u32[]{:S(2)}) collective-permute-start(bf16[2,2,256,128]{3,2,1,0:T(8,128)(2,1)S(1)} %get-tuple-element.57), channel_id=1, source_target_pairs={{0,4},{1,5},{2,6},{3,7},{4,0},{5,1},{6,2},{7,3},{8,12},{9,13},{10,... | collective-permute-start | bytes 786440 | tf_op jit(solution)/shard_map/ppermute | solution.py:45
  32.3 7.7 %collective-permute-start.9 = (bf16[2,2,256,128]{3,2,1,0:T(8,128)(2,1)S(1)}, bf16[2,2,256,128]{3,2,1,0:T(8,128)(2,1)S(1)}, u32[]{:S(2)}, u32[]{:S(2)}) collective-permute-start(bf16[2,2,256,128]{3,2,1,0:T(8,128)(2,1)S(1)} %get-tuple-element.56.refs_6_), channel_id=1, source_target_pairs={{0,2},{1,3},{2,0},{3,1},{4,6},{5,7},{6,4},{7,5},{8,10},{9,11},{10,... | collective-permute-start | bytes 786440 | tf_op jit(solution)/shard_map/ppermute | solution.py:45
  34.4 8.2 %collective-permute-start.17 = (bf16[2,128,128]{2,1,0:T(8,128)(2,1)S(1)}, bf16[2,128,128]{2,1,0:T(8,128)(2,1)S(1)}, u32[]{:S(2)}, u32[]{:S(2)}) collective-permute-start(bf16[2,128,128]{2,1,0:T(8,128)(2,1)S(1)} %get-tuple-element.64), channel_id=1, source_target_pairs={{0,8},{8,0},{16,24},{24,16},{1,9},{9,1},{17,25},{25,17},{2,10},{10... | collective-permute-start | bytes 196616 | tf_op jit(solution)/shard_map/ppermute | solution.py:45
  36.0 9.2 %collective-permute-start.18 = (bf16[2,128,128]{2,1,0:T(8,128)(2,1)S(1)}, bf16[2,128,128]{2,1,0:T(8,128)(2,1)S(1)}, u32[]{:S(2)}, u32[]{:S(2)}) collective-permute-start(bf16[2,128,128]{2,1,0:T(8,128)(2,1)S(1)} %get-tuple-element.65), channel_id=1, source_target_pairs={{0,16},{8,24},{16,0},{24,8},{1,17},{9,25},{17,1},{25,9},{2,18},{10... | collective-permute-start | bytes 196616 | tf_op jit(solution)/shard_map/ppermute | solution.py:45
  37.4 7.8 %collective-permute-start.19 = (bf16[2,128,128]{2,1,0:T(8,128)(2,1)S(1)}, bf16[2,128,128]{2,1,0:T(8,128)(2,1)S(1)}, u32[]{:S(2)}, u32[]{:S(2)}) collective-permute-start(bf16[2,128,128]{2,1,0:T(8,128)(2,1)S(1)} %get-tuple-element.66), channel_id=1, source_target_pairs={{0,24},{8,16},{16,8},{24,0},{1,25},{9,17},{17,9},{25,1},{2,26},{10... | collective-permute-start | bytes 196616 | tf_op jit(solution)/shard_map/ppermute | solution.py:45
  40.7 7.8 %collective-permute-start.13 = (bf16[2,128,128]{2,1,0:T(8,128)(2,1)S(1)}, bf16[2,128,128]{2,1,0:T(8,128)(2,1)S(1)}, u32[]{:S(2)}, u32[]{:S(2)}) collective-permute-start(bf16[2,128,128]{2,1,0:T(8,128)(2,1)S(1)} %get-tuple-element.61), channel_id=1, source_target_pairs={{0,8},{8,0},{16,24},{24,16},{1,9},{9,1},{17,25},{25,17},{2,10},{10... | collective-permute-start | bytes 196616 | tf_op jit(solution)/shard_map/ppermute | solution.py:45
  41.4 9.7 %collective-permute-start.14 = (bf16[2,128,128]{2,1,0:T(8,128)(2,1)S(1)}, bf16[2,128,128]{2,1,0:T(8,128)(2,1)S(1)}, u32[]{:S(2)}, u32[]{:S(2)}) collective-permute-start(bf16[2,128,128]{2,1,0:T(8,128)(2,1)S(1)} %get-tuple-element.62), channel_id=1, source_target_pairs={{0,16},{8,24},{16,0},{24,8},{1,17},{9,25},{17,1},{25,9},{2,18},{10... | collective-permute-start | bytes 196616 | tf_op jit(solution)/shard_map/ppermute | solution.py:45
  42.6 8.5 %collective-permute-start.15 = (bf16[2,128,128]{2,1,0:T(8,128)(2,1)S(1)}, bf16[2,128,128]{2,1,0:T(8,128)(2,1)S(1)}, u32[]{:S(2)}, u32[]{:S(2)}) collective-permute-start(bf16[2,128,128]{2,1,0:T(8,128)(2,1)S(1)} %get-tuple-element.63), channel_id=1, source_target_pairs={{0,24},{8,16},{16,8},{24,0},{1,25},{9,17},{17,9},{25,1},{2,26},{10... | collective-permute-start | bytes 196616 | tf_op jit(solution)/shard_map/ppermute | solution.py:45
  46.7 7.8 %collective-permute-start.23 = (bf16[2,128,128]{2,1,0:T(8,128)(2,1)S(1)}, bf16[2,128,128]{2,1,0:T(8,128)(2,1)S(1)}, u32[]{:S(2)}, u32[]{:S(2)}) collective-permute-start(bf16[2,128,128]{2,1,0:T(8,128)(2,1)S(1)} %get-tuple-element.72), channel_id=1, source_target_pairs={{0,8},{8,0},{16,24},{24,16},{1,9},{9,1},{17,25},{25,17},{2,10},{10... | collective-permute-start | bytes 196616 | tf_op jit(solution)/shard_map/ppermute | solution.py:45
  48.0 9.1 %collective-permute-start.24 = (bf16[2,128,128]{2,1,0:T(8,128)(2,1)S(1)}, bf16[2,128,128]{2,1,0:T(8,128)(2,1)S(1)}, u32[]{:S(2)}, u32[]{:S(2)}) collective-permute-start(bf16[2,128,128]{2,1,0:T(8,128)(2,1)S(1)} %get-tuple-element.73), channel_id=1, source_target_pairs={{0,16},{8,24},{16,0},{24,8},{1,17},{9,25},{17,1},{25,9},{2,18},{10... | collective-permute-start | bytes 196616 | tf_op jit(solution)/shard_map/ppermute | solution.py:45
  48.6 8.5 %collective-permute-start.25 = (bf16[2,128,128]{2,1,0:T(8,128)(2,1)S(1)}, bf16[2,128,128]{2,1,0:T(8,128)(2,1)S(1)}, u32[]{:S(2)}, u32[]{:S(2)}) collective-permute-start(bf16[2,128,128]{2,1,0:T(8,128)(2,1)S(1)} %get-tuple-element.74), channel_id=1, source_target_pairs={{0,24},{8,16},{16,8},{24,0},{1,25},{9,17},{17,9},{25,1},{2,26},{10... | collective-permute-start | bytes 196616 | tf_op jit(solution)/shard_map/ppermute | solution.py:45
  52.6 7.3 %collective-permute-start.20 = (bf16[2,128,128]{2,1,0:T(8,128)(2,1)S(1)}, bf16[2,128,128]{2,1,0:T(8,128)(2,1)S(1)}, u32[]{:S(2)}, u32[]{:S(2)}) collective-permute-start(bf16[2,128,128]{2,1,0:T(8,128)(2,1)S(1)} %get-tuple-element.69), channel_id=1, source_target_pairs={{0,8},{8,0},{16,24},{24,16},{1,9},{9,1},{17,25},{25,17},{2,10},{10... | collective-permute-start | bytes 196616 | tf_op jit(solution)/shard_map/ppermute | solution.py:45
  53.7 6.3 %collective-permute-start.21 = (bf16[2,128,128]{2,1,0:T(8,128)(2,1)S(1)}, bf16[2,128,128]{2,1,0:T(8,128)(2,1)S(1)}, u32[]{:S(2)}, u32[]{:S(2)}) collective-permute-start(bf16[2,128,128]{2,1,0:T(8,128)(2,1)S(1)} %get-tuple-element.70), channel_id=1, source_target_pairs={{0,16},{8,24},{16,0},{24,8},{1,17},{9,25},{17,1},{25,9},{2,18},{10... | collective-permute-start | bytes 196616 | tf_op jit(solution)/shard_map/ppermute | solution.py:45
  54.5 6.2 %collective-permute-start.22 = (bf16[2,128,128]{2,1,0:T(8,128)(2,1)S(1)}, bf16[2,128,128]{2,1,0:T(8,128)(2,1)S(1)}, u32[]{:S(2)}, u32[]{:S(2)}) collective-permute-start(bf16[2,128,128]{2,1,0:T(8,128)(2,1)S(1)} %get-tuple-element.71), channel_id=1, source_target_pairs={{0,24},{8,16},{16,8},{24,0},{1,25},{9,17},{17,9},{25,1},{2,26},{10... | collective-permute-start | bytes 196616 | tf_op jit(solution)/shard_map/ppermute | solution.py:45
  57.6 9.2 %collective-permute-start.26 = (bf16[2,2,256,128]{3,2,1,0:T(8,128)(2,1)S(1)}, bf16[2,2,256,128]{3,2,1,0:T(8,128)(2,1)S(1)}, u32[]{:S(2)}, u32[]{:S(2)}) collective-permute-start(bf16[2,2,256,128]{3,2,1,0:T(8,128)(2,1)S(1)} %interface_collect.2.refs_5_.refs_0_.refs_4_.refs_8_), channel_id=1, source_target_pairs={{0,2},{1,3},{2,0},{3,1},{4,6},{5,7},{6,4},{7,5},{8,10},{9,11},{10,... | collective-permute-start | bytes 786440 | tf_op jit(solution)/shard_map/ppermute | solution.py:45
  59.2 9.1 %collective-permute-start.27 = (bf16[2,2,256,128]{3,2,1,0:T(8,128)(2,1)S(1)}, bf16[2,2,256,128]{3,2,1,0:T(8,128)(2,1)S(1)}, u32[]{:S(2)}, u32[]{:S(2)}) collective-permute-start(bf16[2,2,256,128]{3,2,1,0:T(8,128)(2,1)S(1)} %interface_collect.2.refs_5_.refs_0_.refs_4_.refs_8_), channel_id=1, source_target_pairs={{0,4},{1,5},{2,6},{3,7},{4,0},{5,1},{6,2},{7,3},{8,12},{9,13},{10,... | collective-permute-start | bytes 786440 | tf_op jit(solution)/shard_map/ppermute | solution.py:45
  61.3 8.4 %collective-permute-start.30 = (bf16[2,2,256,128]{3,2,1,0:T(8,128)(2,1)S(1)}, bf16[2,2,256,128]{3,2,1,0:T(8,128)(2,1)S(1)}, u32[]{:S(2)}, u32[]{:S(2)}) collective-permute-start(bf16[2,2,256,128]{3,2,1,0:T(8,128)(2,1)S(1)} %interface_collect.3.refs_3_.refs_0_.refs_9_.refs_4_), channel_id=1, source_target_pairs={{0,2},{1,3},{2,0},{3,1},{4,6},{5,7},{6,4},{7,5},{8,10},{9,11},{10,... | collective-permute-start | bytes 786440 | tf_op jit(solution)/shard_map/ppermute | solution.py:45
  63.1 8.0 %collective-permute-start.31 = (bf16[2,2,256,128]{3,2,1,0:T(8,128)(2,1)S(1)}, bf16[2,2,256,128]{3,2,1,0:T(8,128)(2,1)S(1)}, u32[]{:S(2)}, u32[]{:S(2)}) collective-permute-start(bf16[2,2,256,128]{3,2,1,0:T(8,128)(2,1)S(1)} %interface_collect.3.refs_3_.refs_0_.refs_9_.refs_4_), channel_id=1, source_target_pairs={{0,4},{1,5},{2,6},{3,7},{4,0},{5,1},{6,2},{7,3},{8,12},{9,13},{10,... | collective-permute-start | bytes 786440 | tf_op jit(solution)/shard_map/ppermute | solution.py:45
  68.4 3.2 %collective-permute-start.34 = (bf16[3,2,2,256,128]{4,3,2,1,0:T(8,128)(2,1)S(1)}, bf16[3,2,2,256,128]{4,3,2,1,0:T(8,128)(2,1)S(1)}, u32[]{:S(2)}, u32[]{:S(2)}) collective-permute-start(bf16[3,2,2,256,128]{4,3,2,1,0:T(8,128)(2,1)S(1)} %get-tuple-element.79), channel_id=1, source_target_pairs={{0,1},{1,0},{2,3},{3,2},{4,5},{5,4},{6,7},{7,6},{8,9},{9,8},{10,11... | collective-permute-start | bytes 2359304 | tf_op jit(solution)/shard_map/ppermute | solution.py:45
  68.4 7.6 %collective-permute-start.28 = (bf16[1,2,256,128]{3,2,1,0:T(8,128)(2,1)S(1)}, bf16[1,2,256,128]{3,2,1,0:T(8,128)(2,1)S(1)}, u32[]{:S(2)}, u32[]{:S(2)}) collective-permute-start(bf16[1,2,256,128]{3,2,1,0:T(8,128)(2,1)S(1)} %get-tuple-element.75.refs_3_), channel_id=1, source_target_pairs={{0,4},{1,5},{2,6},{3,7},{4,0},{5,1},{6,2},{7,3},{8,12},{9,13},{10,... | collective-permute-start | bytes 393224 | tf_op jit(solution)/shard_map/ppermute | solution.py:45
  68.8 7.2 %collective-permute-start.29 = (bf16[1,2,256,128]{3,2,1,0:T(8,128)(2,1)S(1)}, bf16[1,2,256,128]{3,2,1,0:T(8,128)(2,1)S(1)}, u32[]{:S(2)}, u32[]{:S(2)}) collective-permute-start(bf16[1,2,256,128]{3,2,1,0:T(8,128)(2,1)S(1)} %get-tuple-element.76), channel_id=1, source_target_pairs={{0,2},{1,3},{2,0},{3,1},{4,6},{5,7},{6,4},{7,5},{8,10},{9,11},{10,... | collective-permute-start | bytes 393224 | tf_op jit(solution)/shard_map/ppermute | solution.py:45
  71.2 6.1 %collective-permute-start.36 = (bf16[3,2,2,256,128]{4,3,2,1,0:T(8,128)(2,1)S(1)}, bf16[3,2,2,256,128]{4,3,2,1,0:T(8,128)(2,1)S(1)}, u32[]{:S(2)}, u32[]{:S(2)}) collective-permute-start(bf16[3,2,2,256,128]{4,3,2,1,0:T(8,128)(2,1)S(1)} %get-tuple-element.81), channel_id=1, source_target_pairs={{0,1},{1,0},{2,3},{3,2},{4,5},{5,4},{6,7},{7,6},{8,9},{9,8},{10,11... | collective-permute-start | bytes 2359304 | tf_op jit(solution)/shard_map/ppermute | solution.py:45
  71.3 5.9 %collective-permute-start.32 = (bf16[1,2,256,128]{3,2,1,0:T(8,128)(2,1)S(1)}, bf16[1,2,256,128]{3,2,1,0:T(8,128)(2,1)S(1)}, u32[]{:S(2)}, u32[]{:S(2)}) collective-permute-start(bf16[1,2,256,128]{3,2,1,0:T(8,128)(2,1)S(1)} %get-tuple-element.77.refs_10_), channel_id=1, source_target_pairs={{0,4},{1,5},{2,6},{3,7},{4,0},{5,1},{6,2},{7,3},{8,12},{9,13},{10,... | collective-permute-start | bytes 393224 | tf_op jit(solution)/shard_map/ppermute | solution.py:45
  71.6 5.6 %collective-permute-start.33 = (bf16[1,2,256,128]{3,2,1,0:T(8,128)(2,1)S(1)}, bf16[1,2,256,128]{3,2,1,0:T(8,128)(2,1)S(1)}, u32[]{:S(2)}, u32[]{:S(2)}) collective-permute-start(bf16[1,2,256,128]{3,2,1,0:T(8,128)(2,1)S(1)} %get-tuple-element.78), channel_id=1, source_target_pairs={{0,2},{1,3},{2,0},{3,1},{4,6},{5,7},{6,4},{7,5},{8,10},{9,11},{10,... | collective-permute-start | bytes 393224 | tf_op jit(solution)/shard_map/ppermute | solution.py:45
  77.2 3.2 %collective-permute-start.35 = (bf16[4,2,256,128]{3,2,1,0:T(8,128)(2,1)S(1)}, bf16[4,2,256,128]{3,2,1,0:T(8,128)(2,1)S(1)}, u32[]{:S(2)}, u32[]{:S(2)}) collective-permute-start(bf16[4,2,256,128]{3,2,1,0:T(8,128)(2,1)S(1)} %interface_join.1.refs_4_), channel_id=1, source_target_pairs={{0,1},{1,0},{2,3},{3,2},{4,5},{5,4},{6,7},{7,6},{8,9},{9,8},{10,11... | collective-permute-start | bytes 1572872 | tf_op jit(solution)/shard_map/ppermute | solution.py:45

commit v11 on v10

--- a/solution.py
+++ b/solution.py
@@ -544,7 +544,7 @@
     token, got0 = send_first(keep0, near0, [same])
     keep1, near1 = start_forward(1, [token, have[1]])
     token, far0 = send_second(0, keep0, near0, got0, [keep1])
-    token, got1 = send_first(keep1, near1, [token])
+    token, got1 = send_first(keep1, near1, [token, near1[0]])
     while step < slabs:
         token = join(have, [token])
         have = have + [crossed(token, "slab", step)]

time: 83.3 us -> 81.4 us (0.977)
  waiting for transfers between devices: 14.1 us -> 7.77 us
  starting transfers between devices: 42.4 us -> 46.8 us
    ppermute x37, waiting for transfers between devices: 14.1 us -> 7.77 us  [crossed(): lax.ppermute(x, axis, [(i, i ^ mask) for i in range(lax.axis_size(axis))])]
    ppermute x37, starting transfers between devices: 42.4 us -> 46.8 us  [crossed(): lax.ppermute(x, axis, [(i, i ^ mask) for i in range(lax.axis_size(axis))])]
  transfers between devices with their start and end apart: 37 -> 37, of which waited for: 9 -> 8; matrix products, arithmetic and copies ran while one was open for 0% -> 0% of each run, Pallas kernels for 21% -> 21%
where the time goes in v11:
time: 81.4 us; the launch traced here: 81.2 us
  starting transfers between devices  46.8 us (57%)
  Pallas kernels  24.2 us (30%)
  waiting for transfers between devices  7.77 us (10%)
  local copies, waits for them, and re-layouts  1.38 us (2%)
  between operations  0.92 us (1%)
    ppermute x37, starting transfers between devices, crossed(): lax.ppermute(x, axis, [(i, i ^ mask) for i in range(lax.axis_size(axis))])  46.8 us
    pallas_call x21, Pallas kernels, call(): pl.pallas_call(wrapped, in_specs=list(in_specs) + [ANY] * extra, out_spec...  24.2 us
    ppermute x37, waiting for transfers between devices, crossed(): lax.ppermute(x, axis, [(i, i ^ mask) for i in range(lax.axis_size(axis))])  7.77 us
  transfers between devices with their start and end apart: 37, of which 8 were waited for; matrix products, arithmetic and copies ran while one was open for 0% of the time, Pallas kernels for 21%

profile of v11, /device:TPU:0, one launch (start us, length us, event | category | flops | bytes accessed | tf_op | source)
XLA Modules:
  0.0 81.2 jit_solution(15422364308400941648)
XLA Ops:
  0.7 0.7 copy-done.5
  1.4 0.7 copy-done.7
  2.1 4.4 %leaf_forward.2 = (bf16[4,2,2,256,128]{4,3,2,1,0:T(8,128)(2,1)S(1)}, bf16[3,2,2,256,128]{4,3,2,1,0:T(8,128)(2,1)S(1)}, bf16[1,2,2,256,128]{4,3,2,1,0:T(8,128)(2,1)S(1)}) custom-call(s32[16]{0:T(128)S(1)} %bitcast.5, s32[2]{0:T(128)S(1)} %pad_add_fusion.refs_1_.refs_0_, bf16[1,2,16,128,512]{4,3,2,1,0:T(8,128)(2,1)} %refs_2_.11, ...), custom_call_target="tpu_custom_call" | custom-call | flops 10000000000 | bytes 1 | tf_op jit(solution)/shard_map/leaf_forward/pallas_call | solution.py:31
  6.4 0.5 collective-permute-start
  7.0 0.6 solve_pack.1
  7.5 2.7 %collective-permute-start.1 = (bf16[272,128]{1,0:T(8,128)(2,1)S(1)}, bf16[272,128]{1,0:T(8,128)(2,1)S(1)}, u32[]{:S(2)}, u32[]{:S(2)}) collective-permute-start(bf16[272,128]{1,0:T(8,128)(2,1)S(1)} %get-tuple-element.47), channel_id=1, source_target_pairs={{0,8},{8,0},{16,24},{24,16},{1,9},{9,1},{17,25},{25,17},{2,10},{10... | collective-permute-start | bytes 208904 | tf_op jit(solution)/shard_map/ppermute | solution.py:45
  10.5 1.6 %collective-permute-start.5 = (bf16[1,2,256,128]{3,2,1,0:T(8,128)(2,1)S(1)}, bf16[1,2,256,128]{3,2,1,0:T(8,128)(2,1)S(1)}, u32[]{:S(2)}, u32[]{:S(2)}) collective-permute-start(bf16[1,2,256,128]{3,2,1,0:T(8,128)(2,1)S(1)} %get-tuple-element.46.refs_6_), channel_id=1, source_target_pairs={{0,2},{1,3},{2,0},{3,1},{4,6},{5,7},{6,4},{7,5},{8,10},{9,11},{10,... | collective-permute-start | bytes 393224 | tf_op jit(solution)/shard_map/ppermute | solution.py:45
  12.0 1.5 %collective-permute-start.6 = (bf16[1,2,256,128]{3,2,1,0:T(8,128)(2,1)S(1)}, bf16[1,2,256,128]{3,2,1,0:T(8,128)(2,1)S(1)}, u32[]{:S(2)}, u32[]{:S(2)}) collective-permute-start(bf16[1,2,256,128]{3,2,1,0:T(8,128)(2,1)S(1)} %get-tuple-element.52), channel_id=1, source_target_pairs={{0,4},{1,5},{2,6},{3,7},{4,0},{5,1},{6,2},{7,3},{8,12},{9,13},{10,... | collective-permute-start | bytes 393224 | tf_op jit(solution)/shard_map/ppermute | solution.py:45
  13.6 2.6 %leaf_forward.3 = (bf16[4,2,2,256,128]{4,3,2,1,0:T(8,128)(2,1)S(1)}, bf16[3,2,2,256,128]{4,3,2,1,0:T(8,128)(2,1)S(1)}, bf16[1,2,2,256,128]{4,3,2,1,0:T(8,128)(2,1)S(1)}) custom-call(s32[16]{0:T(128)S(1)} %bitcast.6, s32[2]{0:T(128)S(1)} %pad_add_fusion.refs_1_.refs_0_, bf16[1,2,16,128,512]{4,3,2,1,0:T(8,128)(2,1)S(1)} %copy-done, ...), custom_call_target="tpu_custom_call" | custom-call | flops 10000000000 | bytes 1 | tf_op jit(solution)/shard_map/leaf_forward/pallas_call | solution.py:31
  16.8 0.7 collective-permute-done.6.refs_3_
  17.7 0.6 collective-permute-start.11
  18.3 1.5 %collective-permute-start.12 = (bf16[2,2,256,128]{3,2,1,0:T(8,128)(2,1)S(1)}, bf16[2,2,256,128]{3,2,1,0:T(8,128)(2,1)S(1)}, u32[]{:S(2)}, u32[]{:S(2)}) collective-permute-start(bf16[2,2,256,128]{3,2,1,0:T(8,128)(2,1)S(1)} %get-tuple-element.58), channel_id=1, source_target_pairs={{0,4},{1,5},{2,6},{3,7},{4,0},{5,1},{6,2},{7,3},{8,12},{9,13},{10,... | collective-permute-start | bytes 786440 | tf_op jit(solution)/shard_map/ppermute | solution.py:45
  19.9 1.6 %collective-permute-start.7 = (bf16[1,2,256,128]{3,2,1,0:T(8,128)(2,1)S(1)}, bf16[1,2,256,128]{3,2,1,0:T(8,128)(2,1)S(1)}, u32[]{:S(2)}, u32[]{:S(2)}) collective-permute-start(bf16[1,2,256,128]{3,2,1,0:T(8,128)(2,1)S(1)} %get-tuple-element.54.refs_2_), channel_id=1, source_target_pairs={{0,2},{1,3},{2,0},{3,1},{4,6},{5,7},{6,4},{7,5},{8,10},{9,11},{10,... | collective-permute-start | bytes 393224 | tf_op jit(solution)/shard_map/ppermute | solution.py:45
  22.0 2.7 %collective-permute-start.16 = (bf16[544,128]{1,0:T(8,128)(2,1)S(1)}, bf16[544,128]{1,0:T(8,128)(2,1)S(1)}, u32[]{:S(2)}, u32[]{:S(2)}) collective-permute-start(bf16[544,128]{1,0:T(8,128)(2,1)S(1)} %solve_join.1.refs_4_), channel_id=1, source_target_pairs={{0,16},{8,24},{16,0},{24,8},{1,17},{9,25},{17,1},{25,9},{2,18},{10... | collective-permute-start | bytes 417800 | tf_op jit(solution)/shard_map/ppermute | solution.py:45
  24.6 3.6 %collective-permute-done.7.refs_2_ = bf16[1,2,256,128]{3,2,1,0:T(8,128)(2,1)S(1)} collective-permute-done((bf16[1,2,256,128]{3,2,1,0:T(8,128)(2,1)S(1)}, bf16[1,2,256,128]{3,2,1,0:T(8,128)(2,1)S(1)}, u32[]{:S(2)}, u32[]{:S(2)}) %collective-permute-start.7) | collective-permute-done | bytes 131104 | tf_op jit(solution)/shard_map/ppermute | solution.py:45
  28.2 0.8 %collective-permute-done.8.refs_3_ = bf16[1,2,256,128]{3,2,1,0:T(8,128)(2,1)S(1)} collective-permute-done((bf16[1,2,256,128]{3,2,1,0:T(8,128)(2,1)S(1)}, bf16[1,2,256,128]{3,2,1,0:T(8,128)(2,1)S(1)}, u32[]{:S(2)}, u32[]{:S(2)}) %collective-permute-start.8) | collective-permute-done | bytes 131104 | tf_op jit(solution)/shard_map/ppermute | solution.py:45
  29.2 1.6 %collective-permute-start.10 = (bf16[2,2,256,128]{3,2,1,0:T(8,128)(2,1)S(1)}, bf16[2,2,256,128]{3,2,1,0:T(8,128)(2,1)S(1)}, u32[]{:S(2)}, u32[]{:S(2)}) collective-permute-start(bf16[2,2,256,128]{3,2,1,0:T(8,128)(2,1)S(1)} %get-tuple-element.57), channel_id=1, source_target_pairs={{0,4},{1,5},{2,6},{3,7},{4,0},{5,1},{6,2},{7,3},{8,12},{9,13},{10,... | collective-permute-start | bytes 786440 | tf_op jit(solution)/shard_map/ppermute | solution.py:45
  30.8 0.7 collective-permute-start.9
  31.5 0.7 interface_reduce.2
  32.2 1.5 %collective-permute-start.17 = (bf16[2,128,128]{2,1,0:T(8,128)(2,1)S(1)}, bf16[2,128,128]{2,1,0:T(8,128)(2,1)S(1)}, u32[]{:S(2)}, u32[]{:S(2)}) collective-permute-start(bf16[2,128,128]{2,1,0:T(8,128)(2,1)S(1)} %get-tuple-element.64), channel_id=1, source_target_pairs={{0,8},{8,0},{16,24},{24,16},{1,9},{9,1},{17,25},{25,17},{2,10},{10... | collective-permute-start | bytes 196616 | tf_op jit(solution)/shard_map/ppermute | solution.py:45
  33.7 2.6 %collective-permute-start.18 = (bf16[2,128,128]{2,1,0:T(8,128)(2,1)S(1)}, bf16[2,128,128]{2,1,0:T(8,128)(2,1)S(1)}, u32[]{:S(2)}, u32[]{:S(2)}) collective-permute-start(bf16[2,128,128]{2,1,0:T(8,128)(2,1)S(1)} %get-tuple-element.65), channel_id=1, source_target_pairs={{0,16},{8,24},{16,0},{24,8},{1,17},{9,25},{17,1},{25,9},{2,18},{10... | collective-permute-start | bytes 196616 | tf_op jit(solution)/shard_map/ppermute | solution.py:45
  36.3 3.7 %collective-permute-start.19 = (bf16[2,128,128]{2,1,0:T(8,128)(2,1)S(1)}, bf16[2,128,128]{2,1,0:T(8,128)(2,1)S(1)}, u32[]{:S(2)}, u32[]{:S(2)}) collective-permute-start(bf16[2,128,128]{2,1,0:T(8,128)(2,1)S(1)} %get-tuple-element.66), channel_id=1, source_target_pairs={{0,24},{8,16},{16,8},{24,0},{1,25},{9,17},{17,9},{25,1},{2,26},{10... | collective-permute-start | bytes 196616 | tf_op jit(solution)/shard_map/ppermute | solution.py:45
  40.0 0.7 interface_reduce.3
  40.8 1.8 %collective-permute-start.14 = (bf16[2,128,128]{2,1,0:T(8,128)(2,1)S(1)}, bf16[2,128,128]{2,1,0:T(8,128)(2,1)S(1)}, u32[]{:S(2)}, u32[]{:S(2)}) collective-permute-start(bf16[2,128,128]{2,1,0:T(8,128)(2,1)S(1)} %get-tuple-element.62), channel_id=1, source_target_pairs={{0,16},{8,24},{16,0},{24,8},{1,17},{9,25},{17,1},{25,9},{2,18},{10... | collective-permute-start | bytes 196616 | tf_op jit(solution)/shard_map/ppermute | solution.py:45
  42.6 2.6 %collective-permute-start.15 = (bf16[2,128,128]{2,1,0:T(8,128)(2,1)S(1)}, bf16[2,128,128]{2,1,0:T(8,128)(2,1)S(1)}, u32[]{:S(2)}, u32[]{:S(2)}) collective-permute-start(bf16[2,128,128]{2,1,0:T(8,128)(2,1)S(1)} %get-tuple-element.63), channel_id=1, source_target_pairs={{0,24},{8,16},{16,8},{24,0},{1,25},{9,17},{17,9},{25,1},{2,26},{10... | collective-permute-start | bytes 196616 | tf_op jit(solution)/shard_map/ppermute | solution.py:45
  45.2 1.5 %sweep_chain.2 = (bf16[2,128,128]{2,1,0:T(8,128)(2,1)S(1)}, bf16[2,128,128]{2,1,0:T(8,128)(2,1)S(1)}, bf16[2,128,128]{2,1,0:T(8,128)(2,1)S(1)}, bf16[2,128,128]{2,1,0:T(8,128)(2,1)S(1)}) custom-call(s32[2]{0:T(128)S(1)} %pad_add_fusion.refs_1_.refs_0_, bf16[2,128,128]{2,1,0:T(8,128)(2,1)S(1)} %get-tuple-element.59.refs_6_.refs_1_, ...), custom_call_target="tpu_custom_call" | custom-call | flops 10000000000 | bytes 1 | tf_op jit(solution)/shard_map/sweep_chain/pallas_call | solution.py:31
  46.7 1.8 %collective-permute-start.24 = (bf16[2,128,128]{2,1,0:T(8,128)(2,1)S(1)}, bf16[2,128,128]{2,1,0:T(8,128)(2,1)S(1)}, u32[]{:S(2)}, u32[]{:S(2)}) collective-permute-start(bf16[2,128,128]{2,1,0:T(8,128)(2,1)S(1)} %get-tuple-element.73), channel_id=1, source_target_pairs={{0,16},{8,24},{16,0},{24,8},{1,17},{9,25},{17,1},{25,9},{2,18},{10... | collective-permute-start | bytes 196616 | tf_op jit(solution)/shard_map/ppermute | solution.py:45
  48.5 2.6 %collective-permute-start.25 = (bf16[2,128,128]{2,1,0:T(8,128)(2,1)S(1)}, bf16[2,128,128]{2,1,0:T(8,128)(2,1)S(1)}, u32[]{:S(2)}, u32[]{:S(2)}) collective-permute-start(bf16[2,128,128]{2,1,0:T(8,128)(2,1)S(1)} %get-tuple-element.74), channel_id=1, source_target_pairs={{0,24},{8,16},{16,8},{24,0},{1,25},{9,17},{17,9},{25,1},{2,26},{10... | collective-permute-start | bytes 196616 | tf_op jit(solution)/shard_map/ppermute | solution.py:45
  51.1 1.5 %sweep_chain.3 = (bf16[2,128,128]{2,1,0:T(8,128)(2,1)S(1)}, bf16[2,128,128]{2,1,0:T(8,128)(2,1)S(1)}, bf16[2,128,128]{2,1,0:T(8,128)(2,1)S(1)}, bf16[2,128,128]{2,1,0:T(8,128)(2,1)S(1)}) custom-call(s32[2]{0:T(128)S(1)} %pad_add_fusion.refs_1_.refs_0_, bf16[2,128,128]{2,1,0:T(8,128)(2,1)S(1)} %get-tuple-element.60.refs_8_.refs_1_, ...), custom_call_target="tpu_custom_call" | custom-call | flops 10000000000 | bytes 1 | tf_op jit(solution)/shard_map/sweep_chain/pallas_call | solution.py:31
  52.7 1.8 %collective-permute-start.21 = (bf16[2,128,128]{2,1,0:T(8,128)(2,1)S(1)}, bf16[2,128,128]{2,1,0:T(8,128)(2,1)S(1)}, u32[]{:S(2)}, u32[]{:S(2)}) collective-permute-start(bf16[2,128,128]{2,1,0:T(8,128)(2,1)S(1)} %get-tuple-element.70), channel_id=1, source_target_pairs={{0,16},{8,24},{16,0},{24,8},{1,17},{9,25},{17,1},{25,9},{2,18},{10... | collective-permute-start | bytes 196616 | tf_op jit(solution)/shard_map/ppermute | solution.py:45
  54.5 2.6 %collective-permute-start.22 = (bf16[2,128,128]{2,1,0:T(8,128)(2,1)S(1)}, bf16[2,128,128]{2,1,0:T(8,128)(2,1)S(1)}, u32[]{:S(2)}, u32[]{:S(2)}) collective-permute-start(bf16[2,128,128]{2,1,0:T(8,128)(2,1)S(1)} %get-tuple-element.71), channel_id=1, source_target_pairs={{0,24},{8,16},{16,8},{24,0},{1,25},{9,17},{17,9},{25,1},{2,26},{10... | collective-permute-start | bytes 196616 | tf_op jit(solution)/shard_map/ppermute | solution.py:45
  57.1 0.6 interface_collect.2.refs_5_.refs_0_.refs_4_.refs_8_
  57.6 0.7 collective-permute-start.26
  58.3 1.5 %collective-permute-start.27 = (bf16[2,2,256,128]{3,2,1,0:T(8,128)(2,1)S(1)}, bf16[2,2,256,128]{3,2,1,0:T(8,128)(2,1)S(1)}, u32[]{:S(2)}, u32[]{:S(2)}) collective-permute-start(bf16[2,2,256,128]{3,2,1,0:T(8,128)(2,1)S(1)} %interface_collect.2.refs_5_.refs_0_.refs_4_.refs_8_), channel_id=1, source_target_pairs={{0,4},{1,5},{2,6},{3,7},{4,0},{5,1},{6,2},{7,3},{8,12},{9,13},{10,... | collective-permute-start | bytes 786440 | tf_op jit(solution)/shard_map/ppermute | solution.py:45
  59.8 0.7 collective-permute-done.22.refs_4_
  60.5 0.6 interface_collect.3.refs_3_.refs_0_.refs_9_.refs_4_
  61.1 0.8 collective-permute-start.30
  61.9 1.2 %collective-permute-start.31 = (bf16[2,2,256,128]{3,2,1,0:T(8,128)(2,1)S(1)}, bf16[2,2,256,128]{3,2,1,0:T(8,128)(2,1)S(1)}, u32[]{:S(2)}, u32[]{:S(2)}) collective-permute-start(bf16[2,2,256,128]{3,2,1,0:T(8,128)(2,1)S(1)} %interface_collect.3.refs_3_.refs_0_.refs_9_.refs_4_), channel_id=1, source_target_pairs={{0,4},{1,5},{2,6},{3,7},{4,0},{5,1},{6,2},{7,3},{8,12},{9,13},{10,... | collective-permute-start | bytes 786440 | tf_op jit(solution)/shard_map/ppermute | solution.py:45
  63.1 1.5 %leaf_fold.1.refs_3_ = bf16[16,256,768]{2,1,0:T(8,128)(2,1)S(1)} custom-call(bf16[1,16,2,128,128]{4,3,2,1,0:T(8,128)(2,1)S(1)} %copy-done.1, bf16[1,16,2,128,128]{4,3,2,1,0:T(8,128)(2,1)S(1)} %copy-done.2, s32[1,16,128]{2,1,0:T(8,128)S(1)} %copy-done.5, bf16[2,2,256,128]{3,2,1,0:T(8,128)(2,1)S(1)} %interface_collect.3.refs_3_.refs_0_.refs_9_.refs_4_), custom_call_target="tpu_custom_call" | custom-call | flops 10000000000 | bytes 1 | tf_op jit(solution)/shard_map/leaf_fold/pallas_call | solution.py:31
  64.9 0.8 collective-permute-done.27.refs_2_.refs_7_
  65.8 1.1 %collective-permute-start.28 = (bf16[1,2,256,128]{3,2,1,0:T(8,128)(2,1)S(1)}, bf16[1,2,256,128]{3,2,1,0:T(8,128)(2,1)S(1)}, u32[]{:S(2)}, u32[]{:S(2)}) collective-permute-start(bf16[1,2,256,128]{3,2,1,0:T(8,128)(2,1)S(1)} %get-tuple-element.75.refs_3_), channel_id=1, source_target_pairs={{0,4},{1,5},{2,6},{3,7},{4,0},{5,1},{6,2},{7,3},{8,12},{9,13},{10,... | collective-permute-start | bytes 393224 | tf_op jit(solution)/shard_map/ppermute | solution.py:45
  66.9 1.4 %collective-permute-start.29 = (bf16[1,2,256,128]{3,2,1,0:T(8,128)(2,1)S(1)}, bf16[1,2,256,128]{3,2,1,0:T(8,128)(2,1)S(1)}, u32[]{:S(2)}, u32[]{:S(2)}) collective-permute-start(bf16[1,2,256,128]{3,2,1,0:T(8,128)(2,1)S(1)} %get-tuple-element.76), channel_id=1, source_target_pairs={{0,2},{1,3},{2,0},{3,1},{4,6},{5,7},{6,4},{7,5},{8,10},{9,11},{10,... | collective-permute-start | bytes 393224 | tf_op jit(solution)/shard_map/ppermute | solution.py:45
  68.6 1.1 %collective-permute-start.32 = (bf16[1,2,256,128]{3,2,1,0:T(8,128)(2,1)S(1)}, bf16[1,2,256,128]{3,2,1,0:T(8,128)(2,1)S(1)}, u32[]{:S(2)}, u32[]{:S(2)}) collective-permute-start(bf16[1,2,256,128]{3,2,1,0:T(8,128)(2,1)S(1)} %get-tuple-element.77.refs_10_), channel_id=1, source_target_pairs={{0,4},{1,5},{2,6},{3,7},{4,0},{5,1},{6,2},{7,3},{8,12},{9,13},{10,... | collective-permute-start | bytes 393224 | tf_op jit(solution)/shard_map/ppermute | solution.py:45
  69.7 1.5 %collective-permute-start.33 = (bf16[1,2,256,128]{3,2,1,0:T(8,128)(2,1)S(1)}, bf16[1,2,256,128]{3,2,1,0:T(8,128)(2,1)S(1)}, u32[]{:S(2)}, u32[]{:S(2)}) collective-permute-start(bf16[1,2,256,128]{3,2,1,0:T(8,128)(2,1)S(1)} %get-tuple-element.78), channel_id=1, source_target_pairs={{0,2},{1,3},{2,0},{3,1},{4,6},{5,7},{6,4},{7,5},{8,10},{9,11},{10,... | collective-permute-start | bytes 393224 | tf_op jit(solution)/shard_map/ppermute | solution.py:45
  71.2 3.2 %leaf_backward.3 = (bf16[1,2,16,128,512]{4,3,2,1,0:T(8,128)(2,1)}, f32[1,2,256,512]{3,2,1,0:T(8,128)}, f32[8,128]{1,0:T(8,128)S(1)}) custom-call(s32[16]{0:T(128)S(1)} %bitcast.7, s32[2]{0:T(128)S(1)} %pad_add_fusion.refs_1_.refs_0_, bf16[1,2,16,128,512]{4,3,2,1,0:T(8,128)(2,1)S(1)} %copy-done, bf16[16,256,768]{2,1,0:T(8,128)(2,1)S(1)} %leaf_fold.1.refs_3_, ...), custom_call_target="tpu_custom_call" | custom-call | flops 10000000000 | bytes 1 | tf_op jit(solution)/shard_map/leaf_backward/pallas_call | solution.py:31
  74.5 0.8 collective-permute-done.33.refs_3_
  75.4 3.1 %leaf_backward.4.refs_6_ = bf16[1,2,16,128,512]{4,3,2,1,0:T(8,128)(2,1)} custom-call(s32[16]{0:T(128)S(1)} %bitcast.8, s32[2]{0:T(128)S(1)} %pad_add_fusion.refs_1_.refs_0_, bf16[1,2,16,128,512]{4,3,2,1,0:T(8,128)(2,1)S(1)} %copy-done, bf16[16,256,768]{2,1,0:T(8,128)(2,1)S(1)} %leaf_fold.1.refs_3_, ...), custom_call_target="tpu_custom_call", output_to_operand_aliasing={{}: (8, {})} | custom-call | flops 10000000000 | bytes 1 | tf_op jit(solution)/shard_map/leaf_backward/pallas_call | solution.py:31
  78.6 2.6 %leaf_backward.5 = bf16[1,2,16,128,512]{4,3,2,1,0:T(8,128)(2,1)} custom-call(s32[16]{0:T(128)S(1)} %bitcast.9, s32[2]{0:T(128)S(1)} %pad_add_fusion.refs_1_.refs_0_, bf16[1,2,16,128,512]{4,3,2,1,0:T(8,128)(2,1)S(1)} %copy-done, bf16[16,256,768]{2,1,0:T(8,128)(2,1)S(1)} %leaf_fold.1.refs_3_, ...), custom_call_target="tpu_custom_call", output_to_operand_aliasing={{}: (6, {})} | custom-call | flops 10000000000 | bytes 1 | tf_op jit(solution)/shard_map/leaf_backward/pallas_call | solution.py:31
  (64 shorter events, 2.9 us)
Async XLA Ops:
  0.7 0.7 copy-start.5
  1.4 0.7 copy-start.7
  2.1 4.9 %copy-start.4 = (f32[1,2,2,128,128]{4,3,2,1,0:T(8,128)S(1)}, f32[1,2,2,128,128]{4,3,2,1,0:T(8,128)}, u32[]{:S(2)}) copy-start(f32[1,2,2,128,128]{4,3,2,1,0:T(8,128)} %refs_1_.4) | copy-start | bytes 786436
  2.1 4.9 %copy-start.6 = (f32[1,256]{1,0:T(1,128)S(1)}, f32[1,256]{1,0:T(1,128)}, u32[]{:S(2)}) copy-start(f32[1,256]{1,0:T(1,128)} %param.15) | copy-start | bytes 3076
  6.4 4.0 %collective-permute-start = (bf16[1,2,2,256,128]{4,3,2,1,0:T(8,128)(2,1)S(1)}, bf16[1,2,2,256,128]{4,3,2,1,0:T(8,128)(2,1)S(1)}, u32[]{:S(2)}, u32[]{:S(2)}) collective-permute-start(bf16[1,2,2,256,128]{4,3,2,1,0:T(8,128)(2,1)S(1)} %get-tuple-element.44), channel_id=1, source_target_pairs={{0,1},{1,0},{2,3},{3,2},{4,5},{5,4},{6,7},{7,6},{8,9},{9,8},{10,11... | collective-permute-start | bytes 786440 | tf_op jit(solution)/shard_map/ppermute | solution.py:45
  6.9 6.6 %copy-start = (bf16[1,2,16,128,512]{4,3,2,1,0:T(8,128)(2,1)S(1)}, bf16[1,2,16,128,512]{4,3,2,1,0:T(8,128)(2,1)}, u32[]{:S(2)}) copy-start(bf16[1,2,16,128,512]{4,3,2,1,0:T(8,128)(2,1)} %refs_2_.11) | copy-start | bytes 12582916
  7.0 6.6 %copy-start.1 = (bf16[1,16,2,128,128]{4,3,2,1,0:T(8,128)(2,1)S(1)}, bf16[1,16,2,128,128]{4,3,2,1,0:T(8,128)(2,1)}, u32[]{:S(2)}) copy-start(bf16[1,16,2,128,128]{4,3,2,1,0:T(8,128)(2,1)} %refs_0_.1) | copy-start | bytes 3145732
  7.0 6.6 %copy-start.2 = (bf16[1,16,2,128,128]{4,3,2,1,0:T(8,128)(2,1)S(1)}, bf16[1,16,2,128,128]{4,3,2,1,0:T(8,128)(2,1)}, u32[]{:S(2)}) copy-start(bf16[1,16,2,128,128]{4,3,2,1,0:T(8,128)(2,1)} %refs_1_.7) | copy-start | bytes 3145732
  7.5 6.0 %collective-permute-start.1 = (bf16[272,128]{1,0:T(8,128)(2,1)S(1)}, bf16[272,128]{1,0:T(8,128)(2,1)S(1)}, u32[]{:S(2)}, u32[]{:S(2)}) collective-permute-start(bf16[272,128]{1,0:T(8,128)(2,1)S(1)} %get-tuple-element.47), channel_id=1, source_target_pairs={{0,8},{8,0},{16,24},{24,16},{1,9},{9,1},{17,25},{25,17},{2,10},{10... | collective-permute-start | bytes 208904 | tf_op jit(solution)/shard_map/ppermute | solution.py:45
  10.2 7.3 %collective-permute-start.4 = (bf16[3,2,2,256,128]{4,3,2,1,0:T(8,128)(2,1)S(1)}, bf16[3,2,2,256,128]{4,3,2,1,0:T(8,128)(2,1)S(1)}, u32[]{:S(2)}, u32[]{:S(2)}) collective-permute-start(bf16[3,2,2,256,128]{4,3,2,1,0:T(8,128)(2,1)S(1)} %get-tuple-element.51), channel_id=1, source_target_pairs={{0,1},{1,0},{2,3},{3,2},{4,5},{5,4},{6,7},{7,6},{8,9},{9,8},{10,11... | collective-permute-start | bytes 2359304 | tf_op jit(solution)/shard_map/ppermute | solution.py:45
  10.5 6.3 %collective-permute-start.5 = (bf16[1,2,256,128]{3,2,1,0:T(8,128)(2,1)S(1)}, bf16[1,2,256,128]{3,2,1,0:T(8,128)(2,1)S(1)}, u32[]{:S(2)}, u32[]{:S(2)}) collective-permute-start(bf16[1,2,256,128]{3,2,1,0:T(8,128)(2,1)S(1)} %get-tuple-element.46.refs_6_), channel_id=1, source_target_pairs={{0,2},{1,3},{2,0},{3,1},{4,6},{5,7},{6,4},{7,5},{8,10},{9,11},{10,... | collective-permute-start | bytes 393224 | tf_op jit(solution)/shard_map/ppermute | solution.py:45
  12.0 5.4 %collective-permute-start.6 = (bf16[1,2,256,128]{3,2,1,0:T(8,128)(2,1)S(1)}, bf16[1,2,256,128]{3,2,1,0:T(8,128)(2,1)S(1)}, u32[]{:S(2)}, u32[]{:S(2)}) collective-permute-start(bf16[1,2,256,128]{3,2,1,0:T(8,128)(2,1)S(1)} %get-tuple-element.52), channel_id=1, source_target_pairs={{0,4},{1,5},{2,6},{3,7},{4,0},{5,1},{6,2},{7,3},{8,12},{9,13},{10,... | collective-permute-start | bytes 393224 | tf_op jit(solution)/shard_map/ppermute | solution.py:45
  16.2 3.6 %collective-permute-start.2 = (bf16[3,2,2,256,128]{4,3,2,1,0:T(8,128)(2,1)S(1)}, bf16[3,2,2,256,128]{4,3,2,1,0:T(8,128)(2,1)S(1)}, u32[]{:S(2)}, u32[]{:S(2)}) collective-permute-start(bf16[3,2,2,256,128]{4,3,2,1,0:T(8,128)(2,1)S(1)} %get-tuple-element.49), channel_id=1, source_target_pairs={{0,1},{1,0},{2,3},{3,2},{4,5},{5,4},{6,7},{7,6},{8,9},{9,8},{10,11... | collective-permute-start | bytes 2359304 | tf_op jit(solution)/shard_map/ppermute | solution.py:45
  16.3 3.5 %collective-permute-start.3 = (bf16[1,2,2,256,128]{4,3,2,1,0:T(8,128)(2,1)S(1)}, bf16[1,2,2,256,128]{4,3,2,1,0:T(8,128)(2,1)S(1)}, u32[]{:S(2)}, u32[]{:S(2)}) collective-permute-start(bf16[1,2,2,256,128]{4,3,2,1,0:T(8,128)(2,1)S(1)} %get-tuple-element.50), channel_id=1, source_target_pairs={{0,1},{1,0},{2,3},{3,2},{4,5},{5,4},{6,7},{7,6},{8,9},{9,8},{10,11... | collective-permute-start | bytes 786440 | tf_op jit(solution)/shard_map/ppermute | solution.py:45
  17.7 13.8 %copy-start.3 = (bf16[1,2,256,512]{3,2,1,0:T(8,128)(2,1)S(1)}, bf16[1,2,256,512]{3,2,1,0:T(8,128)(2,1)}, u32[]{:S(2)}) copy-start(bf16[1,2,256,512]{3,2,1,0:T(8,128)(2,1)} %refs_1_.6) | copy-start | bytes 1572868
  17.7 13.8 %collective-permute-start.11 = (bf16[2,2,256,128]{3,2,1,0:T(8,128)(2,1)S(1)}, bf16[2,2,256,128]{3,2,1,0:T(8,128)(2,1)S(1)}, u32[]{:S(2)}, u32[]{:S(2)}) collective-permute-start(bf16[2,2,256,128]{3,2,1,0:T(8,128)(2,1)S(1)} %get-tuple-element.53.refs_2_), channel_id=1, source_target_pairs={{0,2},{1,3},{2,0},{3,1},{4,6},{5,7},{6,4},{7,5},{8,10},{9,11},{10,... | collective-permute-start | bytes 786440 | tf_op jit(solution)/shard_map/ppermute | solution.py:45
  18.3 13.2 %collective-permute-start.12 = (bf16[2,2,256,128]{3,2,1,0:T(8,128)(2,1)S(1)}, bf16[2,2,256,128]{3,2,1,0:T(8,128)(2,1)S(1)}, u32[]{:S(2)}, u32[]{:S(2)}) collective-permute-start(bf16[2,2,256,128]{3,2,1,0:T(8,128)(2,1)S(1)} %get-tuple-element.58), channel_id=1, source_target_pairs={{0,4},{1,5},{2,6},{3,7},{4,0},{5,1},{6,2},{7,3},{8,12},{9,13},{10,... | collective-permute-start | bytes 786440 | tf_op jit(solution)/shard_map/ppermute | solution.py:45
  19.9 8.3 %collective-permute-start.7 = (bf16[1,2,256,128]{3,2,1,0:T(8,128)(2,1)S(1)}, bf16[1,2,256,128]{3,2,1,0:T(8,128)(2,1)S(1)}, u32[]{:S(2)}, u32[]{:S(2)}) collective-permute-start(bf16[1,2,256,128]{3,2,1,0:T(8,128)(2,1)S(1)} %get-tuple-element.54.refs_2_), channel_id=1, source_target_pairs={{0,2},{1,3},{2,0},{3,1},{4,6},{5,7},{6,4},{7,5},{8,10},{9,11},{10,... | collective-permute-start | bytes 393224 | tf_op jit(solution)/shard_map/ppermute | solution.py:45
  21.4 7.6 %collective-permute-start.8 = (bf16[1,2,256,128]{3,2,1,0:T(8,128)(2,1)S(1)}, bf16[1,2,256,128]{3,2,1,0:T(8,128)(2,1)S(1)}, u32[]{:S(2)}, u32[]{:S(2)}) collective-permute-start(bf16[1,2,256,128]{3,2,1,0:T(8,128)(2,1)S(1)} %get-tuple-element.55), channel_id=1, source_target_pairs={{0,4},{1,5},{2,6},{3,7},{4,0},{5,1},{6,2},{7,3},{8,12},{9,13},{10,... | collective-permute-start | bytes 393224 | tf_op jit(solution)/shard_map/ppermute | solution.py:45
  22.0 18.8 %collective-permute-start.16 = (bf16[544,128]{1,0:T(8,128)(2,1)S(1)}, bf16[544,128]{1,0:T(8,128)(2,1)S(1)}, u32[]{:S(2)}, u32[]{:S(2)}) collective-permute-start(bf16[544,128]{1,0:T(8,128)(2,1)S(1)} %solve_join.1.refs_4_), channel_id=1, source_target_pairs={{0,16},{8,24},{16,0},{24,8},{1,17},{9,25},{17,1},{25,9},{2,18},{10... | collective-permute-start | bytes 417800 | tf_op jit(solution)/shard_map/ppermute | solution.py:45
  29.2 7.1 %collective-permute-start.10 = (bf16[2,2,256,128]{3,2,1,0:T(8,128)(2,1)S(1)}, bf16[2,2,256,128]{3,2,1,0:T(8,128)(2,1)S(1)}, u32[]{:S(2)}, u32[]{:S(2)}) collective-permute-start(bf16[2,2,256,128]{3,2,1,0:T(8,128)(2,1)S(1)} %get-tuple-element.57), channel_id=1, source_target_pairs={{0,4},{1,5},{2,6},{3,7},{4,0},{5,1},{6,2},{7,3},{8,12},{9,13},{10,... | collective-permute-start | bytes 786440 | tf_op jit(solution)/shard_map/ppermute | solution.py:45
  30.8 9.2 %collective-permute-start.9 = (bf16[2,2,256,128]{3,2,1,0:T(8,128)(2,1)S(1)}, bf16[2,2,256,128]{3,2,1,0:T(8,128)(2,1)S(1)}, u32[]{:S(2)}, u32[]{:S(2)}) collective-permute-start(bf16[2,2,256,128]{3,2,1,0:T(8,128)(2,1)S(1)} %get-tuple-element.56.refs_6_), channel_id=1, source_target_pairs={{0,2},{1,3},{2,0},{3,1},{4,6},{5,7},{6,4},{7,5},{8,10},{9,11},{10,... | collective-permute-start | bytes 786440 | tf_op jit(solution)/shard_map/ppermute | solution.py:45
  32.2 10.4 %collective-permute-start.17 = (bf16[2,128,128]{2,1,0:T(8,128)(2,1)S(1)}, bf16[2,128,128]{2,1,0:T(8,128)(2,1)S(1)}, u32[]{:S(2)}, u32[]{:S(2)}) collective-permute-start(bf16[2,128,128]{2,1,0:T(8,128)(2,1)S(1)} %get-tuple-element.64), channel_id=1, source_target_pairs={{0,8},{8,0},{16,24},{24,16},{1,9},{9,1},{17,25},{25,17},{2,10},{10... | collective-permute-start | bytes 196616 | tf_op jit(solution)/shard_map/ppermute | solution.py:45
  33.7 11.5 %collective-permute-start.18 = (bf16[2,128,128]{2,1,0:T(8,128)(2,1)S(1)}, bf16[2,128,128]{2,1,0:T(8,128)(2,1)S(1)}, u32[]{:S(2)}, u32[]{:S(2)}) collective-permute-start(bf16[2,128,128]{2,1,0:T(8,128)(2,1)S(1)} %get-tuple-element.65), channel_id=1, source_target_pairs={{0,16},{8,24},{16,0},{24,8},{1,17},{9,25},{17,1},{25,9},{2,18},{10... | collective-permute-start | bytes 196616 | tf_op jit(solution)/shard_map/ppermute | solution.py:45
  36.3 8.9 %collective-permute-start.19 = (bf16[2,128,128]{2,1,0:T(8,128)(2,1)S(1)}, bf16[2,128,128]{2,1,0:T(8,128)(2,1)S(1)}, u32[]{:S(2)}, u32[]{:S(2)}) collective-permute-start(bf16[2,128,128]{2,1,0:T(8,128)(2,1)S(1)} %get-tuple-element.66), channel_id=1, source_target_pairs={{0,24},{8,16},{16,8},{24,0},{1,25},{9,17},{17,9},{25,1},{2,26},{10... | collective-permute-start | bytes 196616 | tf_op jit(solution)/shard_map/ppermute | solution.py:45
  40.7 7.8 %collective-permute-start.13 = (bf16[2,128,128]{2,1,0:T(8,128)(2,1)S(1)}, bf16[2,128,128]{2,1,0:T(8,128)(2,1)S(1)}, u32[]{:S(2)}, u32[]{:S(2)}) collective-permute-start(bf16[2,128,128]{2,1,0:T(8,128)(2,1)S(1)} %get-tuple-element.61), channel_id=1, source_target_pairs={{0,8},{8,0},{16,24},{24,16},{1,9},{9,1},{17,25},{25,17},{2,10},{10... | collective-permute-start | bytes 196616 | tf_op jit(solution)/shard_map/ppermute | solution.py:45
  40.8 10.3 %collective-permute-start.14 = (bf16[2,128,128]{2,1,0:T(8,128)(2,1)S(1)}, bf16[2,128,128]{2,1,0:T(8,128)(2,1)S(1)}, u32[]{:S(2)}, u32[]{:S(2)}) collective-permute-start(bf16[2,128,128]{2,1,0:T(8,128)(2,1)S(1)} %get-tuple-element.62), channel_id=1, source_target_pairs={{0,16},{8,24},{16,0},{24,8},{1,17},{9,25},{17,1},{25,9},{2,18},{10... | collective-permute-start | bytes 196616 | tf_op jit(solution)/shard_map/ppermute | solution.py:45
  42.6 8.5 %collective-permute-start.15 = (bf16[2,128,128]{2,1,0:T(8,128)(2,1)S(1)}, bf16[2,128,128]{2,1,0:T(8,128)(2,1)S(1)}, u32[]{:S(2)}, u32[]{:S(2)}) collective-permute-start(bf16[2,128,128]{2,1,0:T(8,128)(2,1)S(1)} %get-tuple-element.63), channel_id=1, source_target_pairs={{0,24},{8,16},{16,8},{24,0},{1,25},{9,17},{17,9},{25,1},{2,26},{10... | collective-permute-start | bytes 196616 | tf_op jit(solution)/shard_map/ppermute | solution.py:45
  46.7 7.8 %collective-permute-start.23 = (bf16[2,128,128]{2,1,0:T(8,128)(2,1)S(1)}, bf16[2,128,128]{2,1,0:T(8,128)(2,1)S(1)}, u32[]{:S(2)}, u32[]{:S(2)}) collective-permute-start(bf16[2,128,128]{2,1,0:T(8,128)(2,1)S(1)} %get-tuple-element.72), channel_id=1, source_target_pairs={{0,8},{8,0},{16,24},{24,16},{1,9},{9,1},{17,25},{25,17},{2,10},{10... | collective-permute-start | bytes 196616 | tf_op jit(solution)/shard_map/ppermute | solution.py:45
  46.7 10.3 %collective-permute-start.24 = (bf16[2,128,128]{2,1,0:T(8,128)(2,1)S(1)}, bf16[2,128,128]{2,1,0:T(8,128)(2,1)S(1)}, u32[]{:S(2)}, u32[]{:S(2)}) collective-permute-start(bf16[2,128,128]{2,1,0:T(8,128)(2,1)S(1)} %get-tuple-element.73), channel_id=1, source_target_pairs={{0,16},{8,24},{16,0},{24,8},{1,17},{9,25},{17,1},{25,9},{2,18},{10... | collective-permute-start | bytes 196616 | tf_op jit(solution)/shard_map/ppermute | solution.py:45
  48.5 8.5 %collective-permute-start.25 = (bf16[2,128,128]{2,1,0:T(8,128)(2,1)S(1)}, bf16[2,128,128]{2,1,0:T(8,128)(2,1)S(1)}, u32[]{:S(2)}, u32[]{:S(2)}) collective-permute-start(bf16[2,128,128]{2,1,0:T(8,128)(2,1)S(1)} %get-tuple-element.74), channel_id=1, source_target_pairs={{0,24},{8,16},{16,8},{24,0},{1,25},{9,17},{17,9},{25,1},{2,26},{10... | collective-permute-start | bytes 196616 | tf_op jit(solution)/shard_map/ppermute | solution.py:45
  52.6 7.2 %collective-permute-start.20 = (bf16[2,128,128]{2,1,0:T(8,128)(2,1)S(1)}, bf16[2,128,128]{2,1,0:T(8,128)(2,1)S(1)}, u32[]{:S(2)}, u32[]{:S(2)}) collective-permute-start(bf16[2,128,128]{2,1,0:T(8,128)(2,1)S(1)} %get-tuple-element.69), channel_id=1, source_target_pairs={{0,8},{8,0},{16,24},{24,16},{1,9},{9,1},{17,25},{25,17},{2,10},{10... | collective-permute-start | bytes 196616 | tf_op jit(solution)/shard_map/ppermute | solution.py:45
  52.7 7.2 %collective-permute-start.21 = (bf16[2,128,128]{2,1,0:T(8,128)(2,1)S(1)}, bf16[2,128,128]{2,1,0:T(8,128)(2,1)S(1)}, u32[]{:S(2)}, u32[]{:S(2)}) collective-permute-start(bf16[2,128,128]{2,1,0:T(8,128)(2,1)S(1)} %get-tuple-element.70), channel_id=1, source_target_pairs={{0,16},{8,24},{16,0},{24,8},{1,17},{9,25},{17,1},{25,9},{2,18},{10... | collective-permute-start | bytes 196616 | tf_op jit(solution)/shard_map/ppermute | solution.py:45
  54.5 6.1 %collective-permute-start.22 = (bf16[2,128,128]{2,1,0:T(8,128)(2,1)S(1)}, bf16[2,128,128]{2,1,0:T(8,128)(2,1)S(1)}, u32[]{:S(2)}, u32[]{:S(2)}) collective-permute-start(bf16[2,128,128]{2,1,0:T(8,128)(2,1)S(1)} %get-tuple-element.71), channel_id=1, source_target_pairs={{0,24},{8,16},{16,8},{24,0},{1,25},{9,17},{17,9},{25,1},{2,26},{10... | collective-permute-start | bytes 196616 | tf_op jit(solution)/shard_map/ppermute | solution.py:45
  57.6 7.2 %collective-permute-start.26 = (bf16[2,2,256,128]{3,2,1,0:T(8,128)(2,1)S(1)}, bf16[2,2,256,128]{3,2,1,0:T(8,128)(2,1)S(1)}, u32[]{:S(2)}, u32[]{:S(2)}) collective-permute-start(bf16[2,2,256,128]{3,2,1,0:T(8,128)(2,1)S(1)} %interface_collect.2.refs_5_.refs_0_.refs_4_.refs_8_), channel_id=1, source_target_pairs={{0,2},{1,3},{2,0},{3,1},{4,6},{5,7},{6,4},{7,5},{8,10},{9,11},{10,... | collective-permute-start | bytes 786440 | tf_op jit(solution)/shard_map/ppermute | solution.py:45
  58.3 7.3 %collective-permute-start.27 = (bf16[2,2,256,128]{3,2,1,0:T(8,128)(2,1)S(1)}, bf16[2,2,256,128]{3,2,1,0:T(8,128)(2,1)S(1)}, u32[]{:S(2)}, u32[]{:S(2)}) collective-permute-start(bf16[2,2,256,128]{3,2,1,0:T(8,128)(2,1)S(1)} %interface_collect.2.refs_5_.refs_0_.refs_4_.refs_8_), channel_id=1, source_target_pairs={{0,4},{1,5},{2,6},{3,7},{4,0},{5,1},{6,2},{7,3},{8,12},{9,13},{10,... | collective-permute-start | bytes 786440 | tf_op jit(solution)/shard_map/ppermute | solution.py:45
  61.1 7.2 %collective-permute-start.30 = (bf16[2,2,256,128]{3,2,1,0:T(8,128)(2,1)S(1)}, bf16[2,2,256,128]{3,2,1,0:T(8,128)(2,1)S(1)}, u32[]{:S(2)}, u32[]{:S(2)}) collective-permute-start(bf16[2,2,256,128]{3,2,1,0:T(8,128)(2,1)S(1)} %interface_collect.3.refs_3_.refs_0_.refs_9_.refs_4_), channel_id=1, source_target_pairs={{0,2},{1,3},{2,0},{3,1},{4,6},{5,7},{6,4},{7,5},{8,10},{9,11},{10,... | collective-permute-start | bytes 786440 | tf_op jit(solution)/shard_map/ppermute | solution.py:45
  61.9 6.5 %collective-permute-start.31 = (bf16[2,2,256,128]{3,2,1,0:T(8,128)(2,1)S(1)}, bf16[2,2,256,128]{3,2,1,0:T(8,128)(2,1)S(1)}, u32[]{:S(2)}, u32[]{:S(2)}) collective-permute-start(bf16[2,2,256,128]{3,2,1,0:T(8,128)(2,1)S(1)} %interface_collect.3.refs_3_.refs_0_.refs_9_.refs_4_), channel_id=1, source_target_pairs={{0,4},{1,5},{2,6},{3,7},{4,0},{5,1},{6,2},{7,3},{8,12},{9,13},{10,... | collective-permute-start | bytes 786440 | tf_op jit(solution)/shard_map/ppermute | solution.py:45
  65.7 4.0 %collective-permute-start.34 = (bf16[3,2,2,256,128]{4,3,2,1,0:T(8,128)(2,1)S(1)}, bf16[3,2,2,256,128]{4,3,2,1,0:T(8,128)(2,1)S(1)}, u32[]{:S(2)}, u32[]{:S(2)}) collective-permute-start(bf16[3,2,2,256,128]{4,3,2,1,0:T(8,128)(2,1)S(1)} %get-tuple-element.79), channel_id=1, source_target_pairs={{0,1},{1,0},{2,3},{3,2},{4,5},{5,4},{6,7},{7,6},{8,9},{9,8},{10,11... | collective-permute-start | bytes 2359304 | tf_op jit(solution)/shard_map/ppermute | solution.py:45
  65.8 8.7 %collective-permute-start.28 = (bf16[1,2,256,128]{3,2,1,0:T(8,128)(2,1)S(1)}, bf16[1,2,256,128]{3,2,1,0:T(8,128)(2,1)S(1)}, u32[]{:S(2)}, u32[]{:S(2)}) collective-permute-start(bf16[1,2,256,128]{3,2,1,0:T(8,128)(2,1)S(1)} %get-tuple-element.75.refs_3_), channel_id=1, source_target_pairs={{0,4},{1,5},{2,6},{3,7},{4,0},{5,1},{6,2},{7,3},{8,12},{9,13},{10,... | collective-permute-start | bytes 393224 | tf_op jit(solution)/shard_map/ppermute | solution.py:45
  66.9 7.5 %collective-permute-start.29 = (bf16[1,2,256,128]{3,2,1,0:T(8,128)(2,1)S(1)}, bf16[1,2,256,128]{3,2,1,0:T(8,128)(2,1)S(1)}, u32[]{:S(2)}, u32[]{:S(2)}) collective-permute-start(bf16[1,2,256,128]{3,2,1,0:T(8,128)(2,1)S(1)} %get-tuple-element.76), channel_id=1, source_target_pairs={{0,2},{1,3},{2,0},{3,1},{4,6},{5,7},{6,4},{7,5},{8,10},{9,11},{10,... | collective-permute-start | bytes 393224 | tf_op jit(solution)/shard_map/ppermute | solution.py:45
  68.5 6.9 %collective-permute-start.36 = (bf16[3,2,2,256,128]{4,3,2,1,0:T(8,128)(2,1)S(1)}, bf16[3,2,2,256,128]{4,3,2,1,0:T(8,128)(2,1)S(1)}, u32[]{:S(2)}, u32[]{:S(2)}) collective-permute-start(bf16[3,2,2,256,128]{4,3,2,1,0:T(8,128)(2,1)S(1)} %get-tuple-element.81), channel_id=1, source_target_pairs={{0,1},{1,0},{2,3},{3,2},{4,5},{5,4},{6,7},{7,6},{8,9},{9,8},{10,11... | collective-permute-start | bytes 2359304 | tf_op jit(solution)/shard_map/ppermute | solution.py:45
  68.6 5.9 %collective-permute-start.32 = (bf16[1,2,256,128]{3,2,1,0:T(8,128)(2,1)S(1)}, bf16[1,2,256,128]{3,2,1,0:T(8,128)(2,1)S(1)}, u32[]{:S(2)}, u32[]{:S(2)}) collective-permute-start(bf16[1,2,256,128]{3,2,1,0:T(8,128)(2,1)S(1)} %get-tuple-element.77.refs_10_), channel_id=1, source_target_pairs={{0,4},{1,5},{2,6},{3,7},{4,0},{5,1},{6,2},{7,3},{8,12},{9,13},{10,... | collective-permute-start | bytes 393224 | tf_op jit(solution)/shard_map/ppermute | solution.py:45
  69.7 5.6 %collective-permute-start.33 = (bf16[1,2,256,128]{3,2,1,0:T(8,128)(2,1)S(1)}, bf16[1,2,256,128]{3,2,1,0:T(8,128)(2,1)S(1)}, u32[]{:S(2)}, u32[]{:S(2)}) collective-permute-start(bf16[1,2,256,128]{3,2,1,0:T(8,128)(2,1)S(1)} %get-tuple-element.78), channel_id=1, source_target_pairs={{0,2},{1,3},{2,0},{3,1},{4,6},{5,7},{6,4},{7,5},{8,10},{9,11},{10,... | collective-permute-start | bytes 393224 | tf_op jit(solution)/shard_map/ppermute | solution.py:45
  75.3 3.2 %collective-permute-start.35 = (bf16[4,2,256,128]{3,2,1,0:T(8,128)(2,1)S(1)}, bf16[4,2,256,128]{3,2,1,0:T(8,128)(2,1)S(1)}, u32[]{:S(2)}, u32[]{:S(2)}) collective-permute-start(bf16[4,2,256,128]{3,2,1,0:T(8,128)(2,1)S(1)} %interface_join.1.refs_4_), channel_id=1, source_target_pairs={{0,1},{1,0},{2,3},{3,2},{4,5},{5,4},{6,7},{7,6},{8,9},{9,8},{10,11... | collective-permute-start | bytes 1572872 | tf_op jit(solution)/shard_map/ppermute | solution.py:45

commit v12 on v11

--- a/solution.py
+++ b/solution.py
@@ -412,7 +412,7 @@
         held[at, 0] = result[:blk].astype(BF)
         held[at, 1] = result[blk:].astype(BF)
 
-    batch = 4
+    batch = -(-len(jobs) // 2)
     for low in range(0, len(jobs), batch):
         ready = len(copies)
         for job in range(low, min(len(jobs), low + batch)):

time: 81.4 us -> 81.5 us (level)
  no operation moved by 1% of the time
where the time goes in v12:
time: 81.5 us; the launch traced here: 81.3 us
  starting transfers between devices  46.8 us (57%)
  Pallas kernels  24.3 us (30%)
  waiting for transfers between devices  7.77 us (10%)
  local copies, waits for them, and re-layouts  1.38 us (2%)
  between operations  0.92 us (1%)
    ppermute x37, starting transfers between devices, crossed(): lax.ppermute(x, axis, [(i, i ^ mask) for i in range(lax.axis_size(axis))])  46.8 us
    pallas_call x21, Pallas kernels, call(): pl.pallas_call(wrapped, in_specs=list(in_specs) + [ANY] * extra, out_spec...  24.3 us
    ppermute x37, waiting for transfers between devices, crossed(): lax.ppermute(x, axis, [(i, i ^ mask) for i in range(lax.axis_size(axis))])  7.77 us
  transfers between devices with their start and end apart: 37, of which 8 were waited for; matrix products, arithmetic and copies ran while one was open for 0% of the time, Pallas kernels for 21%

profile of v12, /device:TPU:0, one launch (start us, length us, event | category | flops | bytes accessed | tf_op | source)
XLA Modules:
  0.0 81.3 jit_solution(15108649725449441195)
XLA Ops:
  0.7 0.7 copy-done.5
  1.4 0.7 copy-done.7
  2.1 4.4 %leaf_forward.2 = (bf16[4,2,2,256,128]{4,3,2,1,0:T(8,128)(2,1)S(1)}, bf16[3,2,2,256,128]{4,3,2,1,0:T(8,128)(2,1)S(1)}, bf16[1,2,2,256,128]{4,3,2,1,0:T(8,128)(2,1)S(1)}) custom-call(s32[16]{0:T(128)S(1)} %bitcast.5, s32[2]{0:T(128)S(1)} %pad_add_fusion.refs_1_.refs_0_, bf16[1,2,16,128,512]{4,3,2,1,0:T(8,128)(2,1)} %refs_2_.11, ...), custom_call_target="tpu_custom_call" | custom-call | flops 10000000000 | bytes 1 | tf_op jit(solution)/shard_map/leaf_forward/pallas_call | solution.py:31
  6.4 0.5 collective-permute-start
  7.0 0.6 solve_pack.1
  7.5 2.7 %collective-permute-start.1 = (bf16[272,128]{1,0:T(8,128)(2,1)S(1)}, bf16[272,128]{1,0:T(8,128)(2,1)S(1)}, u32[]{:S(2)}, u32[]{:S(2)}) collective-permute-start(bf16[272,128]{1,0:T(8,128)(2,1)S(1)} %get-tuple-element.47), channel_id=1, source_target_pairs={{0,8},{8,0},{16,24},{24,16},{1,9},{9,1},{17,25},{25,17},{2,10},{10... | collective-permute-start | bytes 208904 | tf_op jit(solution)/shard_map/ppermute | solution.py:45
  10.5 1.6 %collective-permute-start.5 = (bf16[1,2,256,128]{3,2,1,0:T(8,128)(2,1)S(1)}, bf16[1,2,256,128]{3,2,1,0:T(8,128)(2,1)S(1)}, u32[]{:S(2)}, u32[]{:S(2)}) collective-permute-start(bf16[1,2,256,128]{3,2,1,0:T(8,128)(2,1)S(1)} %get-tuple-element.46.refs_6_), channel_id=1, source_target_pairs={{0,2},{1,3},{2,0},{3,1},{4,6},{5,7},{6,4},{7,5},{8,10},{9,11},{10,... | collective-permute-start | bytes 393224 | tf_op jit(solution)/shard_map/ppermute | solution.py:45
  12.0 1.5 %collective-permute-start.6 = (bf16[1,2,256,128]{3,2,1,0:T(8,128)(2,1)S(1)}, bf16[1,2,256,128]{3,2,1,0:T(8,128)(2,1)S(1)}, u32[]{:S(2)}, u32[]{:S(2)}) collective-permute-start(bf16[1,2,256,128]{3,2,1,0:T(8,128)(2,1)S(1)} %get-tuple-element.52), channel_id=1, source_target_pairs={{0,4},{1,5},{2,6},{3,7},{4,0},{5,1},{6,2},{7,3},{8,12},{9,13},{10,... | collective-permute-start | bytes 393224 | tf_op jit(solution)/shard_map/ppermute | solution.py:45
  13.6 2.6 %leaf_forward.3 = (bf16[4,2,2,256,128]{4,3,2,1,0:T(8,128)(2,1)S(1)}, bf16[3,2,2,256,128]{4,3,2,1,0:T(8,128)(2,1)S(1)}, bf16[1,2,2,256,128]{4,3,2,1,0:T(8,128)(2,1)S(1)}) custom-call(s32[16]{0:T(128)S(1)} %bitcast.6, s32[2]{0:T(128)S(1)} %pad_add_fusion.refs_1_.refs_0_, bf16[1,2,16,128,512]{4,3,2,1,0:T(8,128)(2,1)S(1)} %copy-done, ...), custom_call_target="tpu_custom_call" | custom-call | flops 10000000000 | bytes 1 | tf_op jit(solution)/shard_map/leaf_forward/pallas_call | solution.py:31
  16.8 0.7 collective-permute-done.6.refs_3_
  17.7 0.6 collective-permute-start.11
  18.3 1.5 %collective-permute-start.12 = (bf16[2,2,256,128]{3,2,1,0:T(8,128)(2,1)S(1)}, bf16[2,2,256,128]{3,2,1,0:T(8,128)(2,1)S(1)}, u32[]{:S(2)}, u32[]{:S(2)}) collective-permute-start(bf16[2,2,256,128]{3,2,1,0:T(8,128)(2,1)S(1)} %get-tuple-element.58), channel_id=1, source_target_pairs={{0,4},{1,5},{2,6},{3,7},{4,0},{5,1},{6,2},{7,3},{8,12},{9,13},{10,... | collective-permute-start | bytes 786440 | tf_op jit(solution)/shard_map/ppermute | solution.py:45
  19.9 1.6 %collective-permute-start.7 = (bf16[1,2,256,128]{3,2,1,0:T(8,128)(2,1)S(1)}, bf16[1,2,256,128]{3,2,1,0:T(8,128)(2,1)S(1)}, u32[]{:S(2)}, u32[]{:S(2)}) collective-permute-start(bf16[1,2,256,128]{3,2,1,0:T(8,128)(2,1)S(1)} %get-tuple-element.54.refs_2_), channel_id=1, source_target_pairs={{0,2},{1,3},{2,0},{3,1},{4,6},{5,7},{6,4},{7,5},{8,10},{9,11},{10,... | collective-permute-start | bytes 393224 | tf_op jit(solution)/shard_map/ppermute | solution.py:45
  22.0 2.7 %collective-permute-start.16 = (bf16[544,128]{1,0:T(8,128)(2,1)S(1)}, bf16[544,128]{1,0:T(8,128)(2,1)S(1)}, u32[]{:S(2)}, u32[]{:S(2)}) collective-permute-start(bf16[544,128]{1,0:T(8,128)(2,1)S(1)} %solve_join.1.refs_4_), channel_id=1, source_target_pairs={{0,16},{8,24},{16,0},{24,8},{1,17},{9,25},{17,1},{25,9},{2,18},{10... | collective-permute-start | bytes 417800 | tf_op jit(solution)/shard_map/ppermute | solution.py:45
  24.6 3.6 %collective-permute-done.7.refs_2_ = bf16[1,2,256,128]{3,2,1,0:T(8,128)(2,1)S(1)} collective-permute-done((bf16[1,2,256,128]{3,2,1,0:T(8,128)(2,1)S(1)}, bf16[1,2,256,128]{3,2,1,0:T(8,128)(2,1)S(1)}, u32[]{:S(2)}, u32[]{:S(2)}) %collective-permute-start.7) | collective-permute-done | bytes 131104 | tf_op jit(solution)/shard_map/ppermute | solution.py:45
  28.2 0.8 %collective-permute-done.8.refs_3_ = bf16[1,2,256,128]{3,2,1,0:T(8,128)(2,1)S(1)} collective-permute-done((bf16[1,2,256,128]{3,2,1,0:T(8,128)(2,1)S(1)}, bf16[1,2,256,128]{3,2,1,0:T(8,128)(2,1)S(1)}, u32[]{:S(2)}, u32[]{:S(2)}) %collective-permute-start.8) | collective-permute-done | bytes 131104 | tf_op jit(solution)/shard_map/ppermute | solution.py:45
  29.2 1.6 %collective-permute-start.10 = (bf16[2,2,256,128]{3,2,1,0:T(8,128)(2,1)S(1)}, bf16[2,2,256,128]{3,2,1,0:T(8,128)(2,1)S(1)}, u32[]{:S(2)}, u32[]{:S(2)}) collective-permute-start(bf16[2,2,256,128]{3,2,1,0:T(8,128)(2,1)S(1)} %get-tuple-element.57), channel_id=1, source_target_pairs={{0,4},{1,5},{2,6},{3,7},{4,0},{5,1},{6,2},{7,3},{8,12},{9,13},{10,... | collective-permute-start | bytes 786440 | tf_op jit(solution)/shard_map/ppermute | solution.py:45
  30.8 0.7 collective-permute-start.9
  31.5 0.7 interface_reduce.2
  32.2 1.5 %collective-permute-start.17 = (bf16[2,128,128]{2,1,0:T(8,128)(2,1)S(1)}, bf16[2,128,128]{2,1,0:T(8,128)(2,1)S(1)}, u32[]{:S(2)}, u32[]{:S(2)}) collective-permute-start(bf16[2,128,128]{2,1,0:T(8,128)(2,1)S(1)} %get-tuple-element.64), channel_id=1, source_target_pairs={{0,8},{8,0},{16,24},{24,16},{1,9},{9,1},{17,25},{25,17},{2,10},{10... | collective-permute-start | bytes 196616 | tf_op jit(solution)/shard_map/ppermute | solution.py:45
  33.7 2.6 %collective-permute-start.18 = (bf16[2,128,128]{2,1,0:T(8,128)(2,1)S(1)}, bf16[2,128,128]{2,1,0:T(8,128)(2,1)S(1)}, u32[]{:S(2)}, u32[]{:S(2)}) collective-permute-start(bf16[2,128,128]{2,1,0:T(8,128)(2,1)S(1)} %get-tuple-element.65), channel_id=1, source_target_pairs={{0,16},{8,24},{16,0},{24,8},{1,17},{9,25},{17,1},{25,9},{2,18},{10... | collective-permute-start | bytes 196616 | tf_op jit(solution)/shard_map/ppermute | solution.py:45
  36.3 3.7 %collective-permute-start.19 = (bf16[2,128,128]{2,1,0:T(8,128)(2,1)S(1)}, bf16[2,128,128]{2,1,0:T(8,128)(2,1)S(1)}, u32[]{:S(2)}, u32[]{:S(2)}) collective-permute-start(bf16[2,128,128]{2,1,0:T(8,128)(2,1)S(1)} %get-tuple-element.66), channel_id=1, source_target_pairs={{0,24},{8,16},{16,8},{24,0},{1,25},{9,17},{17,9},{25,1},{2,26},{10... | collective-permute-start | bytes 196616 | tf_op jit(solution)/shard_map/ppermute | solution.py:45
  40.0 0.7 interface_reduce.3
  40.8 1.8 %collective-permute-start.14 = (bf16[2,128,128]{2,1,0:T(8,128)(2,1)S(1)}, bf16[2,128,128]{2,1,0:T(8,128)(2,1)S(1)}, u32[]{:S(2)}, u32[]{:S(2)}) collective-permute-start(bf16[2,128,128]{2,1,0:T(8,128)(2,1)S(1)} %get-tuple-element.62), channel_id=1, source_target_pairs={{0,16},{8,24},{16,0},{24,8},{1,17},{9,25},{17,1},{25,9},{2,18},{10... | collective-permute-start | bytes 196616 | tf_op jit(solution)/shard_map/ppermute | solution.py:45
  42.6 2.6 %collective-permute-start.15 = (bf16[2,128,128]{2,1,0:T(8,128)(2,1)S(1)}, bf16[2,128,128]{2,1,0:T(8,128)(2,1)S(1)}, u32[]{:S(2)}, u32[]{:S(2)}) collective-permute-start(bf16[2,128,128]{2,1,0:T(8,128)(2,1)S(1)} %get-tuple-element.63), channel_id=1, source_target_pairs={{0,24},{8,16},{16,8},{24,0},{1,25},{9,17},{17,9},{25,1},{2,26},{10... | collective-permute-start | bytes 196616 | tf_op jit(solution)/shard_map/ppermute | solution.py:45
  45.2 1.5 %sweep_chain.2 = (bf16[2,128,128]{2,1,0:T(8,128)(2,1)S(1)}, bf16[2,128,128]{2,1,0:T(8,128)(2,1)S(1)}, bf16[2,128,128]{2,1,0:T(8,128)(2,1)S(1)}, bf16[2,128,128]{2,1,0:T(8,128)(2,1)S(1)}) custom-call(s32[2]{0:T(128)S(1)} %pad_add_fusion.refs_1_.refs_0_, bf16[2,128,128]{2,1,0:T(8,128)(2,1)S(1)} %get-tuple-element.59.refs_6_.refs_1_, ...), custom_call_target="tpu_custom_call" | custom-call | flops 10000000000 | bytes 1 | tf_op jit(solution)/shard_map/sweep_chain/pallas_call | solution.py:31
  46.7 1.8 %collective-permute-start.24 = (bf16[2,128,128]{2,1,0:T(8,128)(2,1)S(1)}, bf16[2,128,128]{2,1,0:T(8,128)(2,1)S(1)}, u32[]{:S(2)}, u32[]{:S(2)}) collective-permute-start(bf16[2,128,128]{2,1,0:T(8,128)(2,1)S(1)} %get-tuple-element.73), channel_id=1, source_target_pairs={{0,16},{8,24},{16,0},{24,8},{1,17},{9,25},{17,1},{25,9},{2,18},{10... | collective-permute-start | bytes 196616 | tf_op jit(solution)/shard_map/ppermute | solution.py:45
  48.5 2.6 %collective-permute-start.25 = (bf16[2,128,128]{2,1,0:T(8,128)(2,1)S(1)}, bf16[2,128,128]{2,1,0:T(8,128)(2,1)S(1)}, u32[]{:S(2)}, u32[]{:S(2)}) collective-permute-start(bf16[2,128,128]{2,1,0:T(8,128)(2,1)S(1)} %get-tuple-element.74), channel_id=1, source_target_pairs={{0,24},{8,16},{16,8},{24,0},{1,25},{9,17},{17,9},{25,1},{2,26},{10... | collective-permute-start | bytes 196616 | tf_op jit(solution)/shard_map/ppermute | solution.py:45
  51.1 1.5 %sweep_chain.3 = (bf16[2,128,128]{2,1,0:T(8,128)(2,1)S(1)}, bf16[2,128,128]{2,1,0:T(8,128)(2,1)S(1)}, bf16[2,128,128]{2,1,0:T(8,128)(2,1)S(1)}, bf16[2,128,128]{2,1,0:T(8,128)(2,1)S(1)}) custom-call(s32[2]{0:T(128)S(1)} %pad_add_fusion.refs_1_.refs_0_, bf16[2,128,128]{2,1,0:T(8,128)(2,1)S(1)} %get-tuple-element.60.refs_8_.refs_1_, ...), custom_call_target="tpu_custom_call" | custom-call | flops 10000000000 | bytes 1 | tf_op jit(solution)/shard_map/sweep_chain/pallas_call | solution.py:31
  52.7 1.8 %collective-permute-start.21 = (bf16[2,128,128]{2,1,0:T(8,128)(2,1)S(1)}, bf16[2,128,128]{2,1,0:T(8,128)(2,1)S(1)}, u32[]{:S(2)}, u32[]{:S(2)}) collective-permute-start(bf16[2,128,128]{2,1,0:T(8,128)(2,1)S(1)} %get-tuple-element.70), channel_id=1, source_target_pairs={{0,16},{8,24},{16,0},{24,8},{1,17},{9,25},{17,1},{25,9},{2,18},{10... | collective-permute-start | bytes 196616 | tf_op jit(solution)/shard_map/ppermute | solution.py:45
  54.5 2.6 %collective-permute-start.22 = (bf16[2,128,128]{2,1,0:T(8,128)(2,1)S(1)}, bf16[2,128,128]{2,1,0:T(8,128)(2,1)S(1)}, u32[]{:S(2)}, u32[]{:S(2)}) collective-permute-start(bf16[2,128,128]{2,1,0:T(8,128)(2,1)S(1)} %get-tuple-element.71), channel_id=1, source_target_pairs={{0,24},{8,16},{16,8},{24,0},{1,25},{9,17},{17,9},{25,1},{2,26},{10... | collective-permute-start | bytes 196616 | tf_op jit(solution)/shard_map/ppermute | solution.py:45
  57.1 0.6 interface_collect.2.refs_5_.refs_0_.refs_4_.refs_8_
  57.6 0.7 collective-permute-start.26
  58.3 1.5 %collective-permute-start.27 = (bf16[2,2,256,128]{3,2,1,0:T(8,128)(2,1)S(1)}, bf16[2,2,256,128]{3,2,1,0:T(8,128)(2,1)S(1)}, u32[]{:S(2)}, u32[]{:S(2)}) collective-permute-start(bf16[2,2,256,128]{3,2,1,0:T(8,128)(2,1)S(1)} %interface_collect.2.refs_5_.refs_0_.refs_4_.refs_8_), channel_id=1, source_target_pairs={{0,4},{1,5},{2,6},{3,7},{4,0},{5,1},{6,2},{7,3},{8,12},{9,13},{10,... | collective-permute-start | bytes 786440 | tf_op jit(solution)/shard_map/ppermute | solution.py:45
  59.8 0.7 collective-permute-done.22.refs_4_
  60.5 0.6 interface_collect.3.refs_3_.refs_0_.refs_9_.refs_4_
  61.1 0.8 collective-permute-start.30
  61.9 1.2 %collective-permute-start.31 = (bf16[2,2,256,128]{3,2,1,0:T(8,128)(2,1)S(1)}, bf16[2,2,256,128]{3,2,1,0:T(8,128)(2,1)S(1)}, u32[]{:S(2)}, u32[]{:S(2)}) collective-permute-start(bf16[2,2,256,128]{3,2,1,0:T(8,128)(2,1)S(1)} %interface_collect.3.refs_3_.refs_0_.refs_9_.refs_4_), channel_id=1, source_target_pairs={{0,4},{1,5},{2,6},{3,7},{4,0},{5,1},{6,2},{7,3},{8,12},{9,13},{10,... | collective-permute-start | bytes 786440 | tf_op jit(solution)/shard_map/ppermute | solution.py:45
  63.1 1.5 %leaf_fold.1.refs_3_ = bf16[16,256,768]{2,1,0:T(8,128)(2,1)S(1)} custom-call(bf16[1,16,2,128,128]{4,3,2,1,0:T(8,128)(2,1)S(1)} %copy-done.1, bf16[1,16,2,128,128]{4,3,2,1,0:T(8,128)(2,1)S(1)} %copy-done.2, s32[1,16,128]{2,1,0:T(8,128)S(1)} %copy-done.5, bf16[2,2,256,128]{3,2,1,0:T(8,128)(2,1)S(1)} %interface_collect.3.refs_3_.refs_0_.refs_9_.refs_4_), custom_call_target="tpu_custom_call" | custom-call | flops 10000000000 | bytes 1 | tf_op jit(solution)/shard_map/leaf_fold/pallas_call | solution.py:31
  64.9 0.8 collective-permute-done.27.refs_2_.refs_7_
  65.8 1.1 %collective-permute-start.28 = (bf16[1,2,256,128]{3,2,1,0:T(8,128)(2,1)S(1)}, bf16[1,2,256,128]{3,2,1,0:T(8,128)(2,1)S(1)}, u32[]{:S(2)}, u32[]{:S(2)}) collective-permute-start(bf16[1,2,256,128]{3,2,1,0:T(8,128)(2,1)S(1)} %get-tuple-element.75.refs_3_), channel_id=1, source_target_pairs={{0,4},{1,5},{2,6},{3,7},{4,0},{5,1},{6,2},{7,3},{8,12},{9,13},{10,... | collective-permute-start | bytes 393224 | tf_op jit(solution)/shard_map/ppermute | solution.py:45
  66.9 1.4 %collective-permute-start.29 = (bf16[1,2,256,128]{3,2,1,0:T(8,128)(2,1)S(1)}, bf16[1,2,256,128]{3,2,1,0:T(8,128)(2,1)S(1)}, u32[]{:S(2)}, u32[]{:S(2)}) collective-permute-start(bf16[1,2,256,128]{3,2,1,0:T(8,128)(2,1)S(1)} %get-tuple-element.76), channel_id=1, source_target_pairs={{0,2},{1,3},{2,0},{3,1},{4,6},{5,7},{6,4},{7,5},{8,10},{9,11},{10,... | collective-permute-start | bytes 393224 | tf_op jit(solution)/shard_map/ppermute | solution.py:45
  68.6 1.1 %collective-permute-start.32 = (bf16[1,2,256,128]{3,2,1,0:T(8,128)(2,1)S(1)}, bf16[1,2,256,128]{3,2,1,0:T(8,128)(2,1)S(1)}, u32[]{:S(2)}, u32[]{:S(2)}) collective-permute-start(bf16[1,2,256,128]{3,2,1,0:T(8,128)(2,1)S(1)} %get-tuple-element.77.refs_10_), channel_id=1, source_target_pairs={{0,4},{1,5},{2,6},{3,7},{4,0},{5,1},{6,2},{7,3},{8,12},{9,13},{10,... | collective-permute-start | bytes 393224 | tf_op jit(solution)/shard_map/ppermute | solution.py:45
  69.7 1.5 %collective-permute-start.33 = (bf16[1,2,256,128]{3,2,1,0:T(8,128)(2,1)S(1)}, bf16[1,2,256,128]{3,2,1,0:T(8,128)(2,1)S(1)}, u32[]{:S(2)}, u32[]{:S(2)}) collective-permute-start(bf16[1,2,256,128]{3,2,1,0:T(8,128)(2,1)S(1)} %get-tuple-element.78), channel_id=1, source_target_pairs={{0,2},{1,3},{2,0},{3,1},{4,6},{5,7},{6,4},{7,5},{8,10},{9,11},{10,... | collective-permute-start | bytes 393224 | tf_op jit(solution)/shard_map/ppermute | solution.py:45
  71.2 3.2 %leaf_backward.3 = (bf16[1,2,16,128,512]{4,3,2,1,0:T(8,128)(2,1)}, f32[1,2,256,512]{3,2,1,0:T(8,128)}, f32[8,128]{1,0:T(8,128)S(1)}) custom-call(s32[16]{0:T(128)S(1)} %bitcast.7, s32[2]{0:T(128)S(1)} %pad_add_fusion.refs_1_.refs_0_, bf16[1,2,16,128,512]{4,3,2,1,0:T(8,128)(2,1)S(1)} %copy-done, bf16[16,256,768]{2,1,0:T(8,128)(2,1)S(1)} %leaf_fold.1.refs_3_, ...), custom_call_target="tpu_custom_call" | custom-call | flops 10000000000 | bytes 1 | tf_op jit(solution)/shard_map/leaf_backward/pallas_call | solution.py:31
  74.5 0.8 collective-permute-done.33.refs_3_
  75.4 3.2 %leaf_backward.4.refs_6_ = bf16[1,2,16,128,512]{4,3,2,1,0:T(8,128)(2,1)} custom-call(s32[16]{0:T(128)S(1)} %bitcast.8, s32[2]{0:T(128)S(1)} %pad_add_fusion.refs_1_.refs_0_, bf16[1,2,16,128,512]{4,3,2,1,0:T(8,128)(2,1)S(1)} %copy-done, bf16[16,256,768]{2,1,0:T(8,128)(2,1)S(1)} %leaf_fold.1.refs_3_, ...), custom_call_target="tpu_custom_call", output_to_operand_aliasing={{}: (8, {})} | custom-call | flops 10000000000 | bytes 1 | tf_op jit(solution)/shard_map/leaf_backward/pallas_call | solution.py:31
  78.6 2.6 %leaf_backward.5 = bf16[1,2,16,128,512]{4,3,2,1,0:T(8,128)(2,1)} custom-call(s32[16]{0:T(128)S(1)} %bitcast.9, s32[2]{0:T(128)S(1)} %pad_add_fusion.refs_1_.refs_0_, bf16[1,2,16,128,512]{4,3,2,1,0:T(8,128)(2,1)S(1)} %copy-done, bf16[16,256,768]{2,1,0:T(8,128)(2,1)S(1)} %leaf_fold.1.refs_3_, ...), custom_call_target="tpu_custom_call", output_to_operand_aliasing={{}: (6, {})} | custom-call | flops 10000000000 | bytes 1 | tf_op jit(solution)/shard_map/leaf_backward/pallas_call | solution.py:31
  (64 shorter events, 2.9 us)
Async XLA Ops:
  0.7 0.7 copy-start.5
  1.4 0.7 copy-start.7
  2.1 4.9 %copy-start.4 = (f32[1,2,2,128,128]{4,3,2,1,0:T(8,128)S(1)}, f32[1,2,2,128,128]{4,3,2,1,0:T(8,128)}, u32[]{:S(2)}) copy-start(f32[1,2,2,128,128]{4,3,2,1,0:T(8,128)} %refs_1_.4) | copy-start | bytes 786436
  2.1 4.9 %copy-start.6 = (f32[1,256]{1,0:T(1,128)S(1)}, f32[1,256]{1,0:T(1,128)}, u32[]{:S(2)}) copy-start(f32[1,256]{1,0:T(1,128)} %param.15) | copy-start | bytes 3076
  6.4 4.0 %collective-permute-start = (bf16[1,2,2,256,128]{4,3,2,1,0:T(8,128)(2,1)S(1)}, bf16[1,2,2,256,128]{4,3,2,1,0:T(8,128)(2,1)S(1)}, u32[]{:S(2)}, u32[]{:S(2)}) collective-permute-start(bf16[1,2,2,256,128]{4,3,2,1,0:T(8,128)(2,1)S(1)} %get-tuple-element.44), channel_id=1, source_target_pairs={{0,1},{1,0},{2,3},{3,2},{4,5},{5,4},{6,7},{7,6},{8,9},{9,8},{10,11... | collective-permute-start | bytes 786440 | tf_op jit(solution)/shard_map/ppermute | solution.py:45
  6.9 6.6 %copy-start = (bf16[1,2,16,128,512]{4,3,2,1,0:T(8,128)(2,1)S(1)}, bf16[1,2,16,128,512]{4,3,2,1,0:T(8,128)(2,1)}, u32[]{:S(2)}) copy-start(bf16[1,2,16,128,512]{4,3,2,1,0:T(8,128)(2,1)} %refs_2_.11) | copy-start | bytes 12582916
  7.0 6.6 %copy-start.1 = (bf16[1,16,2,128,128]{4,3,2,1,0:T(8,128)(2,1)S(1)}, bf16[1,16,2,128,128]{4,3,2,1,0:T(8,128)(2,1)}, u32[]{:S(2)}) copy-start(bf16[1,16,2,128,128]{4,3,2,1,0:T(8,128)(2,1)} %refs_0_.1) | copy-start | bytes 3145732
  7.0 6.6 %copy-start.2 = (bf16[1,16,2,128,128]{4,3,2,1,0:T(8,128)(2,1)S(1)}, bf16[1,16,2,128,128]{4,3,2,1,0:T(8,128)(2,1)}, u32[]{:S(2)}) copy-start(bf16[1,16,2,128,128]{4,3,2,1,0:T(8,128)(2,1)} %refs_1_.7) | copy-start | bytes 3145732
  7.5 6.0 %collective-permute-start.1 = (bf16[272,128]{1,0:T(8,128)(2,1)S(1)}, bf16[272,128]{1,0:T(8,128)(2,1)S(1)}, u32[]{:S(2)}, u32[]{:S(2)}) collective-permute-start(bf16[272,128]{1,0:T(8,128)(2,1)S(1)} %get-tuple-element.47), channel_id=1, source_target_pairs={{0,8},{8,0},{16,24},{24,16},{1,9},{9,1},{17,25},{25,17},{2,10},{10... | collective-permute-start | bytes 208904 | tf_op jit(solution)/shard_map/ppermute | solution.py:45
  10.2 7.3 %collective-permute-start.4 = (bf16[3,2,2,256,128]{4,3,2,1,0:T(8,128)(2,1)S(1)}, bf16[3,2,2,256,128]{4,3,2,1,0:T(8,128)(2,1)S(1)}, u32[]{:S(2)}, u32[]{:S(2)}) collective-permute-start(bf16[3,2,2,256,128]{4,3,2,1,0:T(8,128)(2,1)S(1)} %get-tuple-element.51), channel_id=1, source_target_pairs={{0,1},{1,0},{2,3},{3,2},{4,5},{5,4},{6,7},{7,6},{8,9},{9,8},{10,11... | collective-permute-start | bytes 2359304 | tf_op jit(solution)/shard_map/ppermute | solution.py:45
  10.5 6.3 %collective-permute-start.5 = (bf16[1,2,256,128]{3,2,1,0:T(8,128)(2,1)S(1)}, bf16[1,2,256,128]{3,2,1,0:T(8,128)(2,1)S(1)}, u32[]{:S(2)}, u32[]{:S(2)}) collective-permute-start(bf16[1,2,256,128]{3,2,1,0:T(8,128)(2,1)S(1)} %get-tuple-element.46.refs_6_), channel_id=1, source_target_pairs={{0,2},{1,3},{2,0},{3,1},{4,6},{5,7},{6,4},{7,5},{8,10},{9,11},{10,... | collective-permute-start | bytes 393224 | tf_op jit(solution)/shard_map/ppermute | solution.py:45
  12.0 5.4 %collective-permute-start.6 = (bf16[1,2,256,128]{3,2,1,0:T(8,128)(2,1)S(1)}, bf16[1,2,256,128]{3,2,1,0:T(8,128)(2,1)S(1)}, u32[]{:S(2)}, u32[]{:S(2)}) collective-permute-start(bf16[1,2,256,128]{3,2,1,0:T(8,128)(2,1)S(1)} %get-tuple-element.52), channel_id=1, source_target_pairs={{0,4},{1,5},{2,6},{3,7},{4,0},{5,1},{6,2},{7,3},{8,12},{9,13},{10,... | collective-permute-start | bytes 393224 | tf_op jit(solution)/shard_map/ppermute | solution.py:45
  16.2 3.6 %collective-permute-start.2 = (bf16[3,2,2,256,128]{4,3,2,1,0:T(8,128)(2,1)S(1)}, bf16[3,2,2,256,128]{4,3,2,1,0:T(8,128)(2,1)S(1)}, u32[]{:S(2)}, u32[]{:S(2)}) collective-permute-start(bf16[3,2,2,256,128]{4,3,2,1,0:T(8,128)(2,1)S(1)} %get-tuple-element.49), channel_id=1, source_target_pairs={{0,1},{1,0},{2,3},{3,2},{4,5},{5,4},{6,7},{7,6},{8,9},{9,8},{10,11... | collective-permute-start | bytes 2359304 | tf_op jit(solution)/shard_map/ppermute | solution.py:45
  16.3 3.5 %collective-permute-start.3 = (bf16[1,2,2,256,128]{4,3,2,1,0:T(8,128)(2,1)S(1)}, bf16[1,2,2,256,128]{4,3,2,1,0:T(8,128)(2,1)S(1)}, u32[]{:S(2)}, u32[]{:S(2)}) collective-permute-start(bf16[1,2,2,256,128]{4,3,2,1,0:T(8,128)(2,1)S(1)} %get-tuple-element.50), channel_id=1, source_target_pairs={{0,1},{1,0},{2,3},{3,2},{4,5},{5,4},{6,7},{7,6},{8,9},{9,8},{10,11... | collective-permute-start | bytes 786440 | tf_op jit(solution)/shard_map/ppermute | solution.py:45
  17.7 13.8 %copy-start.3 = (bf16[1,2,256,512]{3,2,1,0:T(8,128)(2,1)S(1)}, bf16[1,2,256,512]{3,2,1,0:T(8,128)(2,1)}, u32[]{:S(2)}) copy-start(bf16[1,2,256,512]{3,2,1,0:T(8,128)(2,1)} %refs_1_.6) | copy-start | bytes 1572868
  17.7 13.8 %collective-permute-start.11 = (bf16[2,2,256,128]{3,2,1,0:T(8,128)(2,1)S(1)}, bf16[2,2,256,128]{3,2,1,0:T(8,128)(2,1)S(1)}, u32[]{:S(2)}, u32[]{:S(2)}) collective-permute-start(bf16[2,2,256,128]{3,2,1,0:T(8,128)(2,1)S(1)} %get-tuple-element.53.refs_2_), channel_id=1, source_target_pairs={{0,2},{1,3},{2,0},{3,1},{4,6},{5,7},{6,4},{7,5},{8,10},{9,11},{10,... | collective-permute-start | bytes 786440 | tf_op jit(solution)/shard_map/ppermute | solution.py:45
  18.3 13.2 %collective-permute-start.12 = (bf16[2,2,256,128]{3,2,1,0:T(8,128)(2,1)S(1)}, bf16[2,2,256,128]{3,2,1,0:T(8,128)(2,1)S(1)}, u32[]{:S(2)}, u32[]{:S(2)}) collective-permute-start(bf16[2,2,256,128]{3,2,1,0:T(8,128)(2,1)S(1)} %get-tuple-element.58), channel_id=1, source_target_pairs={{0,4},{1,5},{2,6},{3,7},{4,0},{5,1},{6,2},{7,3},{8,12},{9,13},{10,... | collective-permute-start | bytes 786440 | tf_op jit(solution)/shard_map/ppermute | solution.py:45
  19.9 8.3 %collective-permute-start.7 = (bf16[1,2,256,128]{3,2,1,0:T(8,128)(2,1)S(1)}, bf16[1,2,256,128]{3,2,1,0:T(8,128)(2,1)S(1)}, u32[]{:S(2)}, u32[]{:S(2)}) collective-permute-start(bf16[1,2,256,128]{3,2,1,0:T(8,128)(2,1)S(1)} %get-tuple-element.54.refs_2_), channel_id=1, source_target_pairs={{0,2},{1,3},{2,0},{3,1},{4,6},{5,7},{6,4},{7,5},{8,10},{9,11},{10,... | collective-permute-start | bytes 393224 | tf_op jit(solution)/shard_map/ppermute | solution.py:45
  21.4 7.6 %collective-permute-start.8 = (bf16[1,2,256,128]{3,2,1,0:T(8,128)(2,1)S(1)}, bf16[1,2,256,128]{3,2,1,0:T(8,128)(2,1)S(1)}, u32[]{:S(2)}, u32[]{:S(2)}) collective-permute-start(bf16[1,2,256,128]{3,2,1,0:T(8,128)(2,1)S(1)} %get-tuple-element.55), channel_id=1, source_target_pairs={{0,4},{1,5},{2,6},{3,7},{4,0},{5,1},{6,2},{7,3},{8,12},{9,13},{10,... | collective-permute-start | bytes 393224 | tf_op jit(solution)/shard_map/ppermute | solution.py:45
  22.0 18.8 %collective-permute-start.16 = (bf16[544,128]{1,0:T(8,128)(2,1)S(1)}, bf16[544,128]{1,0:T(8,128)(2,1)S(1)}, u32[]{:S(2)}, u32[]{:S(2)}) collective-permute-start(bf16[544,128]{1,0:T(8,128)(2,1)S(1)} %solve_join.1.refs_4_), channel_id=1, source_target_pairs={{0,16},{8,24},{16,0},{24,8},{1,17},{9,25},{17,1},{25,9},{2,18},{10... | collective-permute-start | bytes 417800 | tf_op jit(solution)/shard_map/ppermute | solution.py:45
  29.2 7.1 %collective-permute-start.10 = (bf16[2,2,256,128]{3,2,1,0:T(8,128)(2,1)S(1)}, bf16[2,2,256,128]{3,2,1,0:T(8,128)(2,1)S(1)}, u32[]{:S(2)}, u32[]{:S(2)}) collective-permute-start(bf16[2,2,256,128]{3,2,1,0:T(8,128)(2,1)S(1)} %get-tuple-element.57), channel_id=1, source_target_pairs={{0,4},{1,5},{2,6},{3,7},{4,0},{5,1},{6,2},{7,3},{8,12},{9,13},{10,... | collective-permute-start | bytes 786440 | tf_op jit(solution)/shard_map/ppermute | solution.py:45
  30.8 9.2 %collective-permute-start.9 = (bf16[2,2,256,128]{3,2,1,0:T(8,128)(2,1)S(1)}, bf16[2,2,256,128]{3,2,1,0:T(8,128)(2,1)S(1)}, u32[]{:S(2)}, u32[]{:S(2)}) collective-permute-start(bf16[2,2,256,128]{3,2,1,0:T(8,128)(2,1)S(1)} %get-tuple-element.56.refs_6_), channel_id=1, source_target_pairs={{0,2},{1,3},{2,0},{3,1},{4,6},{5,7},{6,4},{7,5},{8,10},{9,11},{10,... | collective-permute-start | bytes 786440 | tf_op jit(solution)/shard_map/ppermute | solution.py:45
  32.2 10.4 %collective-permute-start.17 = (bf16[2,128,128]{2,1,0:T(8,128)(2,1)S(1)}, bf16[2,128,128]{2,1,0:T(8,128)(2,1)S(1)}, u32[]{:S(2)}, u32[]{:S(2)}) collective-permute-start(bf16[2,128,128]{2,1,0:T(8,128)(2,1)S(1)} %get-tuple-element.64), channel_id=1, source_target_pairs={{0,8},{8,0},{16,24},{24,16},{1,9},{9,1},{17,25},{25,17},{2,10},{10... | collective-permute-start | bytes 196616 | tf_op jit(solution)/shard_map/ppermute | solution.py:45
  33.7 11.5 %collective-permute-start.18 = (bf16[2,128,128]{2,1,0:T(8,128)(2,1)S(1)}, bf16[2,128,128]{2,1,0:T(8,128)(2,1)S(1)}, u32[]{:S(2)}, u32[]{:S(2)}) collective-permute-start(bf16[2,128,128]{2,1,0:T(8,128)(2,1)S(1)} %get-tuple-element.65), channel_id=1, source_target_pairs={{0,16},{8,24},{16,0},{24,8},{1,17},{9,25},{17,1},{25,9},{2,18},{10... | collective-permute-start | bytes 196616 | tf_op jit(solution)/shard_map/ppermute | solution.py:45
  36.3 8.9 %collective-permute-start.19 = (bf16[2,128,128]{2,1,0:T(8,128)(2,1)S(1)}, bf16[2,128,128]{2,1,0:T(8,128)(2,1)S(1)}, u32[]{:S(2)}, u32[]{:S(2)}) collective-permute-start(bf16[2,128,128]{2,1,0:T(8,128)(2,1)S(1)} %get-tuple-element.66), channel_id=1, source_target_pairs={{0,24},{8,16},{16,8},{24,0},{1,25},{9,17},{17,9},{25,1},{2,26},{10... | collective-permute-start | bytes 196616 | tf_op jit(solution)/shard_map/ppermute | solution.py:45
  40.7 7.8 %collective-permute-start.13 = (bf16[2,128,128]{2,1,0:T(8,128)(2,1)S(1)}, bf16[2,128,128]{2,1,0:T(8,128)(2,1)S(1)}, u32[]{:S(2)}, u32[]{:S(2)}) collective-permute-start(bf16[2,128,128]{2,1,0:T(8,128)(2,1)S(1)} %get-tuple-element.61), channel_id=1, source_target_pairs={{0,8},{8,0},{16,24},{24,16},{1,9},{9,1},{17,25},{25,17},{2,10},{10... | collective-permute-start | bytes 196616 | tf_op jit(solution)/shard_map/ppermute | solution.py:45
  40.8 10.3 %collective-permute-start.14 = (bf16[2,128,128]{2,1,0:T(8,128)(2,1)S(1)}, bf16[2,128,128]{2,1,0:T(8,128)(2,1)S(1)}, u32[]{:S(2)}, u32[]{:S(2)}) collective-permute-start(bf16[2,128,128]{2,1,0:T(8,128)(2,1)S(1)} %get-tuple-element.62), channel_id=1, source_target_pairs={{0,16},{8,24},{16,0},{24,8},{1,17},{9,25},{17,1},{25,9},{2,18},{10... | collective-permute-start | bytes 196616 | tf_op jit(solution)/shard_map/ppermute | solution.py:45
  42.6 8.5 %collective-permute-start.15 = (bf16[2,128,128]{2,1,0:T(8,128)(2,1)S(1)}, bf16[2,128,128]{2,1,0:T(8,128)(2,1)S(1)}, u32[]{:S(2)}, u32[]{:S(2)}) collective-permute-start(bf16[2,128,128]{2,1,0:T(8,128)(2,1)S(1)} %get-tuple-element.63), channel_id=1, source_target_pairs={{0,24},{8,16},{16,8},{24,0},{1,25},{9,17},{17,9},{25,1},{2,26},{10... | collective-permute-start | bytes 196616 | tf_op jit(solution)/shard_map/ppermute | solution.py:45
  46.7 7.8 %collective-permute-start.23 = (bf16[2,128,128]{2,1,0:T(8,128)(2,1)S(1)}, bf16[2,128,128]{2,1,0:T(8,128)(2,1)S(1)}, u32[]{:S(2)}, u32[]{:S(2)}) collective-permute-start(bf16[2,128,128]{2,1,0:T(8,128)(2,1)S(1)} %get-tuple-element.72), channel_id=1, source_target_pairs={{0,8},{8,0},{16,24},{24,16},{1,9},{9,1},{17,25},{25,17},{2,10},{10... | collective-permute-start | bytes 196616 | tf_op jit(solution)/shard_map/ppermute | solution.py:45
  46.7 10.3 %collective-permute-start.24 = (bf16[2,128,128]{2,1,0:T(8,128)(2,1)S(1)}, bf16[2,128,128]{2,1,0:T(8,128)(2,1)S(1)}, u32[]{:S(2)}, u32[]{:S(2)}) collective-permute-start(bf16[2,128,128]{2,1,0:T(8,128)(2,1)S(1)} %get-tuple-element.73), channel_id=1, source_target_pairs={{0,16},{8,24},{16,0},{24,8},{1,17},{9,25},{17,1},{25,9},{2,18},{10... | collective-permute-start | bytes 196616 | tf_op jit(solution)/shard_map/ppermute | solution.py:45
  48.5 8.5 %collective-permute-start.25 = (bf16[2,128,128]{2,1,0:T(8,128)(2,1)S(1)}, bf16[2,128,128]{2,1,0:T(8,128)(2,1)S(1)}, u32[]{:S(2)}, u32[]{:S(2)}) collective-permute-start(bf16[2,128,128]{2,1,0:T(8,128)(2,1)S(1)} %get-tuple-element.74), channel_id=1, source_target_pairs={{0,24},{8,16},{16,8},{24,0},{1,25},{9,17},{17,9},{25,1},{2,26},{10... | collective-permute-start | bytes 196616 | tf_op jit(solution)/shard_map/ppermute | solution.py:45
  52.6 7.2 %collective-permute-start.20 = (bf16[2,128,128]{2,1,0:T(8,128)(2,1)S(1)}, bf16[2,128,128]{2,1,0:T(8,128)(2,1)S(1)}, u32[]{:S(2)}, u32[]{:S(2)}) collective-permute-start(bf16[2,128,128]{2,1,0:T(8,128)(2,1)S(1)} %get-tuple-element.69), channel_id=1, source_target_pairs={{0,8},{8,0},{16,24},{24,16},{1,9},{9,1},{17,25},{25,17},{2,10},{10... | collective-permute-start | bytes 196616 | tf_op jit(solution)/shard_map/ppermute | solution.py:45
  52.7 7.2 %collective-permute-start.21 = (bf16[2,128,128]{2,1,0:T(8,128)(2,1)S(1)}, bf16[2,128,128]{2,1,0:T(8,128)(2,1)S(1)}, u32[]{:S(2)}, u32[]{:S(2)}) collective-permute-start(bf16[2,128,128]{2,1,0:T(8,128)(2,1)S(1)} %get-tuple-element.70), channel_id=1, source_target_pairs={{0,16},{8,24},{16,0},{24,8},{1,17},{9,25},{17,1},{25,9},{2,18},{10... | collective-permute-start | bytes 196616 | tf_op jit(solution)/shard_map/ppermute | solution.py:45
  54.5 6.1 %collective-permute-start.22 = (bf16[2,128,128]{2,1,0:T(8,128)(2,1)S(1)}, bf16[2,128,128]{2,1,0:T(8,128)(2,1)S(1)}, u32[]{:S(2)}, u32[]{:S(2)}) collective-permute-start(bf16[2,128,128]{2,1,0:T(8,128)(2,1)S(1)} %get-tuple-element.71), channel_id=1, source_target_pairs={{0,24},{8,16},{16,8},{24,0},{1,25},{9,17},{17,9},{25,1},{2,26},{10... | collective-permute-start | bytes 196616 | tf_op jit(solution)/shard_map/ppermute | solution.py:45
  57.6 7.2 %collective-permute-start.26 = (bf16[2,2,256,128]{3,2,1,0:T(8,128)(2,1)S(1)}, bf16[2,2,256,128]{3,2,1,0:T(8,128)(2,1)S(1)}, u32[]{:S(2)}, u32[]{:S(2)}) collective-permute-start(bf16[2,2,256,128]{3,2,1,0:T(8,128)(2,1)S(1)} %interface_collect.2.refs_5_.refs_0_.refs_4_.refs_8_), channel_id=1, source_target_pairs={{0,2},{1,3},{2,0},{3,1},{4,6},{5,7},{6,4},{7,5},{8,10},{9,11},{10,... | collective-permute-start | bytes 786440 | tf_op jit(solution)/shard_map/ppermute | solution.py:45
  58.3 7.3 %collective-permute-start.27 = (bf16[2,2,256,128]{3,2,1,0:T(8,128)(2,1)S(1)}, bf16[2,2,256,128]{3,2,1,0:T(8,128)(2,1)S(1)}, u32[]{:S(2)}, u32[]{:S(2)}) collective-permute-start(bf16[2,2,256,128]{3,2,1,0:T(8,128)(2,1)S(1)} %interface_collect.2.refs_5_.refs_0_.refs_4_.refs_8_), channel_id=1, source_target_pairs={{0,4},{1,5},{2,6},{3,7},{4,0},{5,1},{6,2},{7,3},{8,12},{9,13},{10,... | collective-permute-start | bytes 786440 | tf_op jit(solution)/shard_map/ppermute | solution.py:45
  61.1 7.2 %collective-permute-start.30 = (bf16[2,2,256,128]{3,2,1,0:T(8,128)(2,1)S(1)}, bf16[2,2,256,128]{3,2,1,0:T(8,128)(2,1)S(1)}, u32[]{:S(2)}, u32[]{:S(2)}) collective-permute-start(bf16[2,2,256,128]{3,2,1,0:T(8,128)(2,1)S(1)} %interface_collect.3.refs_3_.refs_0_.refs_9_.refs_4_), channel_id=1, source_target_pairs={{0,2},{1,3},{2,0},{3,1},{4,6},{5,7},{6,4},{7,5},{8,10},{9,11},{10,... | collective-permute-start | bytes 786440 | tf_op jit(solution)/shard_map/ppermute | solution.py:45
  61.9 6.5 %collective-permute-start.31 = (bf16[2,2,256,128]{3,2,1,0:T(8,128)(2,1)S(1)}, bf16[2,2,256,128]{3,2,1,0:T(8,128)(2,1)S(1)}, u32[]{:S(2)}, u32[]{:S(2)}) collective-permute-start(bf16[2,2,256,128]{3,2,1,0:T(8,128)(2,1)S(1)} %interface_collect.3.refs_3_.refs_0_.refs_9_.refs_4_), channel_id=1, source_target_pairs={{0,4},{1,5},{2,6},{3,7},{4,0},{5,1},{6,2},{7,3},{8,12},{9,13},{10,... | collective-permute-start | bytes 786440 | tf_op jit(solution)/shard_map/ppermute | solution.py:45
  65.7 4.0 %collective-permute-start.34 = (bf16[3,2,2,256,128]{4,3,2,1,0:T(8,128)(2,1)S(1)}, bf16[3,2,2,256,128]{4,3,2,1,0:T(8,128)(2,1)S(1)}, u32[]{:S(2)}, u32[]{:S(2)}) collective-permute-start(bf16[3,2,2,256,128]{4,3,2,1,0:T(8,128)(2,1)S(1)} %get-tuple-element.79), channel_id=1, source_target_pairs={{0,1},{1,0},{2,3},{3,2},{4,5},{5,4},{6,7},{7,6},{8,9},{9,8},{10,11... | collective-permute-start | bytes 2359304 | tf_op jit(solution)/shard_map/ppermute | solution.py:45
  65.8 8.7 %collective-permute-start.28 = (bf16[1,2,256,128]{3,2,1,0:T(8,128)(2,1)S(1)}, bf16[1,2,256,128]{3,2,1,0:T(8,128)(2,1)S(1)}, u32[]{:S(2)}, u32[]{:S(2)}) collective-permute-start(bf16[1,2,256,128]{3,2,1,0:T(8,128)(2,1)S(1)} %get-tuple-element.75.refs_3_), channel_id=1, source_target_pairs={{0,4},{1,5},{2,6},{3,7},{4,0},{5,1},{6,2},{7,3},{8,12},{9,13},{10,... | collective-permute-start | bytes 393224 | tf_op jit(solution)/shard_map/ppermute | solution.py:45
  66.9 7.5 %collective-permute-start.29 = (bf16[1,2,256,128]{3,2,1,0:T(8,128)(2,1)S(1)}, bf16[1,2,256,128]{3,2,1,0:T(8,128)(2,1)S(1)}, u32[]{:S(2)}, u32[]{:S(2)}) collective-permute-start(bf16[1,2,256,128]{3,2,1,0:T(8,128)(2,1)S(1)} %get-tuple-element.76), channel_id=1, source_target_pairs={{0,2},{1,3},{2,0},{3,1},{4,6},{5,7},{6,4},{7,5},{8,10},{9,11},{10,... | collective-permute-start | bytes 393224 | tf_op jit(solution)/shard_map/ppermute | solution.py:45
  68.5 6.9 %collective-permute-start.36 = (bf16[3,2,2,256,128]{4,3,2,1,0:T(8,128)(2,1)S(1)}, bf16[3,2,2,256,128]{4,3,2,1,0:T(8,128)(2,1)S(1)}, u32[]{:S(2)}, u32[]{:S(2)}) collective-permute-start(bf16[3,2,2,256,128]{4,3,2,1,0:T(8,128)(2,1)S(1)} %get-tuple-element.81), channel_id=1, source_target_pairs={{0,1},{1,0},{2,3},{3,2},{4,5},{5,4},{6,7},{7,6},{8,9},{9,8},{10,11... | collective-permute-start | bytes 2359304 | tf_op jit(solution)/shard_map/ppermute | solution.py:45
  68.6 5.9 %collective-permute-start.32 = (bf16[1,2,256,128]{3,2,1,0:T(8,128)(2,1)S(1)}, bf16[1,2,256,128]{3,2,1,0:T(8,128)(2,1)S(1)}, u32[]{:S(2)}, u32[]{:S(2)}) collective-permute-start(bf16[1,2,256,128]{3,2,1,0:T(8,128)(2,1)S(1)} %get-tuple-element.77.refs_10_), channel_id=1, source_target_pairs={{0,4},{1,5},{2,6},{3,7},{4,0},{5,1},{6,2},{7,3},{8,12},{9,13},{10,... | collective-permute-start | bytes 393224 | tf_op jit(solution)/shard_map/ppermute | solution.py:45
  69.7 5.6 %collective-permute-start.33 = (bf16[1,2,256,128]{3,2,1,0:T(8,128)(2,1)S(1)}, bf16[1,2,256,128]{3,2,1,0:T(8,128)(2,1)S(1)}, u32[]{:S(2)}, u32[]{:S(2)}) collective-permute-start(bf16[1,2,256,128]{3,2,1,0:T(8,128)(2,1)S(1)} %get-tuple-element.78), channel_id=1, source_target_pairs={{0,2},{1,3},{2,0},{3,1},{4,6},{5,7},{6,4},{7,5},{8,10},{9,11},{10,... | collective-permute-start | bytes 393224 | tf_op jit(solution)/shard_map/ppermute | solution.py:45
  75.3 3.3 %collective-permute-start.35 = (bf16[4,2,256,128]{3,2,1,0:T(8,128)(2,1)S(1)}, bf16[4,2,256,128]{3,2,1,0:T(8,128)(2,1)S(1)}, u32[]{:S(2)}, u32[]{:S(2)}) collective-permute-start(bf16[4,2,256,128]{3,2,1,0:T(8,128)(2,1)S(1)} %interface_join.1.refs_4_), channel_id=1, source_target_pairs={{0,1},{1,0},{2,3},{3,2},{4,5},{5,4},{6,7},{7,6},{8,9},{9,8},{10,11... | collective-permute-start | bytes 1572872 | tf_op jit(solution)/shard_map/ppermute | solution.py:45
